TPU v7x, 32 devices: a whole 2x2x4 slice. The times are simulated.
32 devices in a mesh: blk: 4 (over y, core), uly: 2 (over x), dp: 4 (over z).
Axes of the slice: x: 2, y: 2, z: 4, core: 2. Of those that a mesh axis runs over, the one named last changes fastest.
Arguments:
- queries: bfloat16 [4, 1024, 4096], P(None, ('blk', 'uly', 'dp')), may hold values from -16 to 16
- keys: bfloat16 [4, 1024, 512], P(None, ('blk', 'uly', 'dp')), may hold values from -16 to 16
- values: bfloat16 [4, 1024, 512], P(None, ('blk', 'uly', 'dp')), may hold values from -6 to 6
- grad_out: bfloat16 [4, 1024, 4096], P(None, ('blk', 'uly', 'dp')), may hold values from -6 to 6
- segment_ids: int32 [4, 1024], replicated, may hold values from 0 to 7, never falling along the last dimension, each value on 1 to 256 neighbouring positions
- assignment: int32 [4], replicated, may hold values from 0 to 3, each once
Outputs:
- grad_queries: bfloat16 [4, 1024, 32, 128], P('dp', ('blk', 'uly'))
- grad_keys: bfloat16 [4, 1024, 512], P('dp', ('blk', 'uly'))
- grad_values: bfloat16 [4, 1024, 512], P('dp', ('blk', 'uly'))
Inputs may be any that keep to these rules, and one draw needn't show every extreme that they name: `segment_ids`: no document holds more than 256 tokens, and some document holds exactly 256.
All inputs are finite; a program needn't handle non-finite values.
Results may differ from a plain program's by a relative error of at most 0.008.
Values may be sent and summed in bfloat16 or wider, within the bound.
No kernel may reach another device: no remote copies, remote signals or barrier semaphores. Data moves between devices by JAX's collectives and lax.ppermute only.
A program may use at most 64 MiB of HBM per device.

v0:
```python
import jax
import jax.numpy as jnp
from jax import lax
from jax.sharding import PartitionSpec as P

QH = 32
KVH = 4
HD = 128


def shifted(value, axis, by):
    length = lax.axis_size(axis)
    pairs = [(i, i + by) for i in range(length) if 0 <= i + by < length]
    return lax.ppermute(value, axis, pairs)


def attend(query_four, grad_four, key_pad, value_pad, segment_pad, block_rows, rim_rows):
    total_rows = query_four.shape[0]
    head_ratio = query_four.shape[2]
    nblocks = total_rows // block_rows
    softmax_scale = 1.0 / HD**0.5
    row_pos = jnp.arange(block_rows, dtype=jnp.int32) + rim_rows
    col_pos = jnp.arange(rim_rows + block_rows, dtype=jnp.int32)
    query_heads = query_four.transpose(1, 0, 2, 3)
    grad_heads = grad_four.transpose(1, 0, 2, 3)
    key_heads = key_pad.transpose(1, 0, 2)
    value_heads = value_pad.transpose(1, 0, 2)

    def one_head(items):
        query_three, grad_three, key_two, value_two = items

        def block_step(carry, index):
            key_acc, value_acc = carry
            start = index * block_rows
            segment_query = lax.dynamic_slice_in_dim(segment_pad, start + rim_rows, block_rows, 0)
            allowed = (segment_query[:, None] == segment_pad[None, :]) & (
                col_pos[None, :] <= row_pos[:, None]
            )
            scores = (
                jnp.einsum("qrd,kd->rqk", query_three, key_two, preferred_element_type=jnp.float32)
                * softmax_scale
            )
            scores = jnp.where(allowed, scores, -jnp.inf)
            top_score = jnp.max(scores, axis=-1, keepdims=True)
            weights = jnp.where(allowed, jnp.exp(scores - top_score), 0.0)
            probs = weights / jnp.sum(weights, axis=-1, keepdims=True)
            probs_half = probs.astype(jnp.bfloat16)
            grad_value = jnp.einsum(
                "rqk,qrd->kd", probs_half, grad_three, preferred_element_type=jnp.float32
            )
            grad_probs = jnp.einsum(
                "qrd,kd->rqk", grad_three, value_two, preferred_element_type=jnp.float32
            )
            row_delta = jnp.sum(probs * grad_probs, axis=-1, keepdims=True)
            grad_scores = (softmax_scale * probs * (grad_probs - row_delta)).astype(jnp.bfloat16)
            grad_query = jnp.einsum(
                "rqk,kd->qrd", grad_scores, key_two, preferred_element_type=jnp.float32
            ).astype(jnp.bfloat16)
            grad_key = jnp.einsum(
                "rqk,qrd->kd", grad_scores, query_three, preferred_element_type=jnp.float32
            )
            old_key = key_acc
            old_value = value_acc
            key_acc = old_key + grad_key
            value_acc = old_value + grad_value
            return ((key_acc, value_acc), grad_query)

        start_acc = jnp.zeros((rim_rows + total_rows, HD), jnp.float32)
        (key_acc, value_acc), grad_blocks = lax.scan(
            block_step, (start_acc, start_acc), jnp.arange(nblocks, dtype=jnp.int32)
        )
        return (grad_blocks.reshape(total_rows, head_ratio, HD), key_acc, value_acc)

    grad_query, key_acc, value_acc = lax.map(
        one_head, (query_heads, grad_heads, key_heads, value_heads)
    )
    local_kv = query_four.shape[1]
    grad_query = grad_query.transpose(1, 0, 2, 3).reshape(total_rows, local_kv * head_ratio, HD)
    return (grad_query, key_acc.transpose(1, 0, 2), value_acc.transpose(1, 0, 2))


def shards(queries, keys, values, grad_out, segment_ids, assignment):
    n_heads_axis = lax.axis_size("uly")
    group_index = lax.axis_index("dp")
    blk_index = lax.axis_index("blk")
    query_pick = jnp.take(queries, assignment, axis=0)
    key_pick = jnp.take(keys, assignment, axis=0)
    value_pick = jnp.take(values, assignment, axis=0)
    grad_pick = jnp.take(grad_out, assignment, axis=0)
    query_tok, key_tok, value_tok, grad_tok = (
        lax.all_to_all(query_pick, "dp", split_axis=0, concat_axis=1, tiled=True),
        lax.all_to_all(key_pick, "dp", split_axis=0, concat_axis=1, tiled=True),
        lax.all_to_all(value_pick, "dp", split_axis=0, concat_axis=1, tiled=True),
        lax.all_to_all(grad_pick, "dp", split_axis=0, concat_axis=1, tiled=True),
    )
    tok_dev = query_tok.shape[1]
    query_tok = query_tok.reshape(tok_dev, QH, HD)
    grad_tok = grad_tok.reshape(tok_dev, QH, HD)
    key_tok = key_tok.reshape(tok_dev, KVH, HD)
    value_tok = value_tok.reshape(tok_dev, KVH, HD)
    segment_row = jnp.take(segment_ids, assignment[group_index], axis=0)
    doc_most = min(512, tok_dev * n_heads_axis)
    piece_rows = min(doc_most, tok_dev)
    hops = doc_most // piece_rows
    tail = (key_tok, value_tok)

    def carry_forward(carry, unused):
        moved = shifted((carry[0], carry[1]), ("blk", "uly"), 1)
        return (moved, moved)

    unused_last, (near_key, near_value) = lax.scan(carry_forward, tail, None, length=hops)
    halo_key = near_key[::-1].reshape(doc_most, KVH, HD)
    halo_value = near_value[::-1].reshape(doc_most, KVH, HD)
    key_pad = jnp.concatenate([halo_key, key_tok], axis=0)
    value_pad = jnp.concatenate([halo_value, value_tok], axis=0)
    place = blk_index * n_heads_axis + lax.axis_index("uly")
    start_tok = place * tok_dev
    positions = start_tok - doc_most + jnp.arange(doc_most + tok_dev, dtype=jnp.int32)
    segment_pad = jnp.where(positions >= 0, jnp.take(segment_row, jnp.maximum(positions, 0)), -1)
    head_ratio = QH // KVH
    query_four = query_tok.reshape(tok_dev, KVH, head_ratio, HD)
    grad_four = grad_tok.reshape(tok_dev, KVH, head_ratio, HD)
    block_rows = min(512, tok_dev)
    grad_query, key_acc, value_acc = attend(
        query_four, grad_four, key_pad, value_pad, segment_pad, block_rows, doc_most
    )
    far_key = key_acc[:doc_most].reshape(hops, piece_rows, KVH, HD)
    far_value = value_acc[:doc_most].reshape(hops, piece_rows, KVH, HD)

    def carry_back(carry, pieces):
        total = (carry[0] + pieces[0], carry[1] + pieces[1])
        moved = shifted((total[0], total[1]), ("blk", "uly"), -1)
        return (moved, None)

    zero_piece = jnp.zeros((piece_rows, KVH, HD), jnp.float32)
    (back_key, back_value), unused_out = lax.scan(
        carry_back, (zero_piece, zero_piece), (far_key, far_value)
    )
    key_own = key_acc[doc_most:].at[tok_dev - piece_rows :].add(back_key)
    value_own = value_acc[doc_most:].at[tok_dev - piece_rows :].add(back_value)
    grad_keys = key_own.astype(jnp.bfloat16).reshape(1, tok_dev, KVH * HD)
    grad_values = value_own.astype(jnp.bfloat16).reshape(1, tok_dev, KVH * HD)
    grad_queries = grad_query.reshape(1, tok_dev, QH, HD)
    return (grad_queries, grad_keys, grad_values)


def solution(mesh):
    in_specs = (
        P(None, ("blk", "uly", "dp"), None),
        P(None, ("blk", "uly", "dp"), None),
        P(None, ("blk", "uly", "dp"), None),
        P(None, ("blk", "uly", "dp"), None),
        P(),
        P(),
    )
    out_specs = (
        P("dp", ("blk", "uly"), None, None),
        P("dp", ("blk", "uly"), None),
        P("dp", ("blk", "uly"), None),
    )
    return jax.shard_map(shards, mesh=mesh, in_specs=in_specs, out_specs=out_specs, check_vma=False)
```

profile of v0, /device:TPU:1, one launch (start us, length us, event | category | flops | bytes accessed | tf_op | source)
XLA Modules:
  0.0 170.5 jit_solution(13482333626065000840)
XLA Ops:
  5.8 5.4 %all-to-all-start = ((bf16[4,32,512]{2,1,0:T(8,128)(2,1)}), bf16[4,32,512]{2,1,0:T(8,128)(2,1)S(1)}, u32[]{:S(2)}, u32[]{:S(2)}) async-start(bf16[4,32,512]{2,1,0:T(8,128)(2,1)} %get-tuple-element.425), calls=%async_computation | async-start | bytes 262144 | tf_op jit(solution)/shard_map/all_to_all | solution.py:92
  13.7 2.3 %all-to-all-done = bf16[4,32,512]{2,1,0:T(8,128)(2,1)S(1)} async-done(((bf16[4,32,512]{2,1,0:T(8,128)(2,1)}), bf16[4,32,512]{2,1,0:T(8,128)(2,1)S(1)}, u32[]{:S(2)}, u32[]{:S(2)}) %all-to-all-start) | async-done | bytes 131104 | tf_op jit(solution)/shard_map/all_to_all | solution.py:92
  16.0 3.4 %all-to-all-start.1 = ((bf16[4,32,512]{2,1,0:T(8,128)(2,1)}), bf16[4,32,512]{2,1,0:T(8,128)(2,1)S(1)}, u32[]{:S(2)}, u32[]{:S(2)}) async-start(bf16[4,32,512]{2,1,0:T(8,128)(2,1)} %get-tuple-element.424), calls=%async_computation.1 | async-start | bytes 262144 | tf_op jit(solution)/shard_map/all_to_all | solution.py:93
  21.0 3.2 %all-to-all-done.1 = bf16[4,32,512]{2,1,0:T(8,128)(2,1)S(1)} async-done(((bf16[4,32,512]{2,1,0:T(8,128)(2,1)}), bf16[4,32,512]{2,1,0:T(8,128)(2,1)S(1)}, u32[]{:S(2)}, u32[]{:S(2)}) %all-to-all-start.1) | async-done | bytes 131104 | tf_op jit(solution)/shard_map/all_to_all | solution.py:93
  24.2 27.6 %all_to_all.16 = bf16[4,32,4096]{2,1,0:T(8,128)(2,1)S(1)} all-to-all(bf16[4,32,4096]{2,1,0:T(8,128)(2,1)} %get-tuple-element.422), channel_id=1, replica_groups=mesh['blk'=4,'uly'=2,'dp'=4] {'dp'}, dimensions={0} | all-to-all | bytes 2097152 | tf_op jit(solution)/shard_map/all_to_all | solution.py:94
  51.8 3.6 %all-to-all-start.2 = ((bf16[4,32,4096]{2,1,0:T(8,128)(2,1)}), bf16[4,32,4096]{2,1,0:T(8,128)(2,1)S(1)}, u32[]{:S(2)}, u32[]{:S(2)}) async-start(bf16[4,32,4096]{2,1,0:T(8,128)(2,1)} %get-tuple-element.423), calls=%async_computation.2 | async-start | bytes 2097152 | tf_op jit(solution)/shard_map/all_to_all | solution.py:91
  65.5 26.1 %while.57 = (s32[]{:T(128)}, bf16[128,4,128]{2,1,0:T(4,128)(2,1)}, bf16[128,4,128]{2,1,0:T(4,128)(2,1)}, bf16[2,128,4,128]{3,2,1,0:T(4,128)(2,1)}, bf16[2,128,4,128]{3,2,1,0:T(4,128)(2,1)}, /*index=5*/s32[]{:T(128)}) while((s32[]{:T(128)}, bf16[128,4,128]{2,1,0:T(4,128)(2,1)}, bf16[128,4,128]{2,1,0:T(4,128)(2,1)}, ...), condition=%wide.region_1.0_spmd, body=%wide.region_0.3_spmd.sunk | while | flops 2 | bytes 2097317 | solution.py:111
  65.5 3.1 %collective-permute-start = (bf16[128,4,128]{2,1,0:T(4,128)(2,1)}, bf16[128,4,128]{2,1,0:T(4,128)(2,1)S(1)}, u32[]{:S(2)}, u32[]{:S(2)}) collective-permute-start(bf16[128,4,128]{2,1,0:T(4,128)(2,1)} %get-tuple-element.570), channel_id=1, source_target_pairs={{0,4},{4,8},{8,12},{12,16},{16,20},{20,24},{24,28},{1,5},{5,9},{9,... | collective-permute-start | bytes 393224 | tf_op jit(solution)/shard_map/while/body/eval_jaxpr/ppermute | solution.py:14
  68.6 5.6 %collective-permute-start.1 = (bf16[128,4,128]{2,1,0:T(4,128)(2,1)}, bf16[128,4,128]{2,1,0:T(4,128)(2,1)S(1)}, u32[]{:S(2)}, u32[]{:S(2)}) collective-permute-start(bf16[128,4,128]{2,1,0:T(4,128)(2,1)} %get-tuple-element.571), channel_id=1, source_target_pairs={{0,4},{4,8},{8,12},{12,16},{16,20},{20,24},{24,28},{1,5},{5,9},{9,... | collective-permute-start | bytes 393224 | tf_op jit(solution)/shard_map/while/body/eval_jaxpr/ppermute | solution.py:14
  78.5 4.0 %collective-permute-start = (bf16[128,4,128]{2,1,0:T(4,128)(2,1)}, bf16[128,4,128]{2,1,0:T(4,128)(2,1)S(1)}, u32[]{:S(2)}, u32[]{:S(2)}) collective-permute-start(bf16[128,4,128]{2,1,0:T(4,128)(2,1)} %get-tuple-element.570), channel_id=1, source_target_pairs={{0,4},{4,8},{8,12},{12,16},{16,20},{20,24},{24,28},{1,5},{5,9},{9,... | collective-permute-start | bytes 393224 | tf_op jit(solution)/shard_map/while/body/eval_jaxpr/ppermute | solution.py:14
  82.5 3.8 %collective-permute-start.1 = (bf16[128,4,128]{2,1,0:T(4,128)(2,1)}, bf16[128,4,128]{2,1,0:T(4,128)(2,1)S(1)}, u32[]{:S(2)}, u32[]{:S(2)}) collective-permute-start(bf16[128,4,128]{2,1,0:T(4,128)(2,1)} %get-tuple-element.571), channel_id=1, source_target_pairs={{0,4},{4,8},{8,12},{12,16},{16,20},{20,24},{24,28},{1,5},{5,9},{9,... | collective-permute-start | bytes 393224 | tf_op jit(solution)/shard_map/while/body/eval_jaxpr/ppermute | solution.py:14
  87.7 2.6 %collective-permute-done.1 = bf16[128,4,128]{2,1,0:T(4,128)(2,1)S(1)} collective-permute-done((bf16[128,4,128]{2,1,0:T(4,128)(2,1)}, bf16[128,4,128]{2,1,0:T(4,128)(2,1)S(1)}, u32[]{:S(2)}, u32[]{:S(2)}) %collective-permute-start.1) | collective-permute-done | bytes 131104 | tf_op jit(solution)/shard_map/while/body/eval_jaxpr/ppermute | solution.py:14
  94.5 2.0 %maximum_bitcast_fusion = (bf16[4,384,128]{2,1,0:T(8,128)(2,1)}, bf16[4,384,128]{2,1,0:T(8,128)(2,1)}) fusion(bf16[128,4,128]{2,0,1:T(8,128)(2,1)S(1)} %copy.25, bf16[256,4,128]{2,0,1:T(8,128)(2,1)} %bitcast.154, bf16[128,4,128]{2,0,1:T(8,128)(2,1)} %copy.27, bf16[256,4,128]{2,0,1:T(8,128)(2,1)S(1)} %bitcast.155), kind=kLoop, calls=%fused_computation.58 | loop fusion | flops 1572864 | bytes 1572864 | tf_op jit(solution)/shard_map/transpose | solution.py:26
  98.9 32.6 %while.59 = (s32[]{:T(128)}, bf16[4,128,8,128]{1,3,2,0:T(8,128)(2,1)}, f32[4,384,128]{2,1,0:T(8,128)}, f32[4,384,128]{2,1,0:T(8,128)}, bf16[4,384,128]{2,1,0:T(8...) while((s32[]{:T(128)}, ...), condition=%wide.region_6.9_spmd.clone, body=%wide.region_2.8_spmd.clone.sunk | while | flops 509492736 | bytes 15022193 | solution.py:74
  133.8 30.5 %while.58 = (s32[]{:T(128)}, f32[128,4,128]{2,1,0:T(4,128)S(1)}, f32[128,4,128]{2,1,0:T(4,128)S(1)}, f32[2,128,4,128]{3,1,0,2:T(8,128)S(1)}, f32[2,128,4,128]{3,1,0,2:T(8,128)S(1)}, /*index=5*/s32[]{:T(128)}) while((s32[]{:T(128)}, f32[128,4,128]{2,1,0:T(4,128)S(1)}, f32[128,4,128]{2,1,0:T(4,128)S(1)}, f32[2,128,4,128]{3,1,0,2:T(8,128)S(1)}, ...), condition=%wide.region_8.11_spmd, body=%wide.region_7.10_spmd.sunk | while | flops 131074 | bytes 4718749 | solution.py:136
  134.0 1.9 %collective-permute-start.2 = (f32[128,4,128]{2,1,0:T(4,128)S(1)}, f32[128,4,128]{2,1,0:T(4,128)S(1)}, u32[]{:S(2)}, u32[]{:S(2)}) collective-permute-start(f32[128,4,128]{2,1,0:T(4,128)S(1)} %fusion.60), channel_id=1, source_target_pairs={{4,0},{8,4},{12,8},{16,12},{20,16},{24,20},{28,24},{5,1},{9,5},{13... | collective-permute-start | bytes 786440 | tf_op jit(solution)/shard_map/while/body/eval_jaxpr/ppermute | solution.py:14
  136.2 1.9 %collective-permute-start.3 = (f32[128,4,128]{2,1,0:T(4,128)S(1)}, f32[128,4,128]{2,1,0:T(4,128)S(1)}, u32[]{:S(2)}, u32[]{:S(2)}) collective-permute-start(f32[128,4,128]{2,1,0:T(4,128)S(1)} %fusion.61), channel_id=1, source_target_pairs={{4,0},{8,4},{12,8},{16,12},{20,16},{24,20},{28,24},{5,1},{9,5},{13... | collective-permute-start | bytes 786440 | tf_op jit(solution)/shard_map/while/body/eval_jaxpr/ppermute | solution.py:14
  138.1 6.1 %collective-permute-done.2 = f32[128,4,128]{2,1,0:T(4,128)S(1)} collective-permute-done((f32[128,4,128]{2,1,0:T(4,128)S(1)}, f32[128,4,128]{2,1,0:T(4,128)S(1)}, u32[]{:S(2)}, u32[]{:S(2)}) %collective-permute-start.2) | collective-permute-done | bytes 262176 | tf_op jit(solution)/shard_map/while/body/eval_jaxpr/ppermute | solution.py:14
  144.3 4.1 %collective-permute-done.3 = f32[128,4,128]{2,1,0:T(4,128)S(1)} collective-permute-done((f32[128,4,128]{2,1,0:T(4,128)S(1)}, f32[128,4,128]{2,1,0:T(4,128)S(1)}, u32[]{:S(2)}, u32[]{:S(2)}) %collective-permute-start.3) | collective-permute-done | bytes 262176 | tf_op jit(solution)/shard_map/while/body/eval_jaxpr/ppermute | solution.py:14
  148.6 1.9 %collective-permute-start.2 = (f32[128,4,128]{2,1,0:T(4,128)S(1)}, f32[128,4,128]{2,1,0:T(4,128)S(1)}, u32[]{:S(2)}, u32[]{:S(2)}) collective-permute-start(f32[128,4,128]{2,1,0:T(4,128)S(1)} %fusion.60), channel_id=1, source_target_pairs={{4,0},{8,4},{12,8},{16,12},{20,16},{24,20},{28,24},{5,1},{9,5},{13... | collective-permute-start | bytes 786440 | tf_op jit(solution)/shard_map/while/body/eval_jaxpr/ppermute | solution.py:14
  150.8 3.0 %collective-permute-start.3 = (f32[128,4,128]{2,1,0:T(4,128)S(1)}, f32[128,4,128]{2,1,0:T(4,128)S(1)}, u32[]{:S(2)}, u32[]{:S(2)}) collective-permute-start(f32[128,4,128]{2,1,0:T(4,128)S(1)} %fusion.61), channel_id=1, source_target_pairs={{4,0},{8,4},{12,8},{16,12},{20,16},{24,20},{28,24},{5,1},{9,5},{13... | collective-permute-start | bytes 786440 | tf_op jit(solution)/shard_map/while/body/eval_jaxpr/ppermute | solution.py:14
  153.8 5.0 %collective-permute-done.2 = f32[128,4,128]{2,1,0:T(4,128)S(1)} collective-permute-done((f32[128,4,128]{2,1,0:T(4,128)S(1)}, f32[128,4,128]{2,1,0:T(4,128)S(1)}, u32[]{:S(2)}, u32[]{:S(2)}) %collective-permute-start.2) | collective-permute-done | bytes 262176 | tf_op jit(solution)/shard_map/while/body/eval_jaxpr/ppermute | solution.py:14
  158.8 5.5 %collective-permute-done.3 = f32[128,4,128]{2,1,0:T(4,128)S(1)} collective-permute-done((f32[128,4,128]{2,1,0:T(4,128)S(1)}, f32[128,4,128]{2,1,0:T(4,128)S(1)}, u32[]{:S(2)}, u32[]{:S(2)}) %collective-permute-start.3) | collective-permute-done | bytes 262176 | tf_op jit(solution)/shard_map/while/body/eval_jaxpr/ppermute | solution.py:14
  167.9 2.6 %copy.30 = bf16[128,4,8,128]{3,2,1,0:T(8,128)(2,1)} copy(bf16[128,4,8,128]{0,3,2,1:T(8,128)(2,1)} %bitcast.12) | data formatting | bytes 2097152 | tf_op jit(solution)/shard_map/transpose | solution.py:78
  (105 shorter events, 68.8 us)
Async XLA Ops:
  0.6 10.6 %copy-start = (bf16[4,32,4096]{2,1,0:T(8,128)(2,1)S(1)}, bf16[4,32,4096]{2,1,0:T(8,128)(2,1)}, u32[]{:S(2)}) copy-start(bf16[4,32,4096]{2,1,0:T(8,128)(2,1)} %param.24) | copy-start | bytes 3145732
  5.8 10.2 %all-to-all-start = ((bf16[4,32,512]{2,1,0:T(8,128)(2,1)}), bf16[4,32,512]{2,1,0:T(8,128)(2,1)S(1)}, u32[]{:S(2)}, u32[]{:S(2)}) async-start(bf16[4,32,512]{2,1,0:T(8,128)(2,1)} %get-tuple-element.425), calls=%async_computation | async-start | bytes 262144 | tf_op jit(solution)/shard_map/all_to_all | solution.py:92
  16.0 8.2 %all-to-all-start.1 = ((bf16[4,32,512]{2,1,0:T(8,128)(2,1)}), bf16[4,32,512]{2,1,0:T(8,128)(2,1)S(1)}, u32[]{:S(2)}, u32[]{:S(2)}) async-start(bf16[4,32,512]{2,1,0:T(8,128)(2,1)} %get-tuple-element.424), calls=%async_computation.1 | async-start | bytes 262144 | tf_op jit(solution)/shard_map/all_to_all | solution.py:93
  24.2 27.6 %copy-start.2 = (bf16[4,32,512]{2,1,0:T(8,128)(2,1)}, bf16[4,32,512]{2,1,0:T(8,128)(2,1)S(1)}, u32[]{:S(2)}) copy-start(bf16[4,32,512]{2,1,0:T(8,128)(2,1)S(1)} %all-to-all-done.1) | copy-start | bytes 393220
  51.8 3.7 %copy-start.3 = (s32[4]{0:T(128)S(1)}, s32[4]{0:T(128)}, u32[]{:S(2)}) copy-start(s32[4]{0:T(128)} %param.29) | copy-start | bytes 52
  51.8 45.9 %all-to-all-start.2 = ((bf16[4,32,4096]{2,1,0:T(8,128)(2,1)}), bf16[4,32,4096]{2,1,0:T(8,128)(2,1)S(1)}, u32[]{:S(2)}, u32[]{:S(2)}) async-start(bf16[4,32,4096]{2,1,0:T(8,128)(2,1)} %get-tuple-element.423), calls=%async_computation.2 | async-start | bytes 2097152 | tf_op jit(solution)/shard_map/all_to_all | solution.py:91
  65.5 9.0 %collective-permute-start = (bf16[128,4,128]{2,1,0:T(4,128)(2,1)}, bf16[128,4,128]{2,1,0:T(4,128)(2,1)S(1)}, u32[]{:S(2)}, u32[]{:S(2)}) collective-permute-start(bf16[128,4,128]{2,1,0:T(4,128)(2,1)} %get-tuple-element.570), channel_id=1, source_target_pairs={{0,4},{4,8},{8,12},{12,16},{16,20},{20,24},{24,28},{1,5},{5,9},{9,... | collective-permute-start | bytes 393224 | tf_op jit(solution)/shard_map/while/body/eval_jaxpr/ppermute | solution.py:14
  68.6 8.6 %collective-permute-start.1 = (bf16[128,4,128]{2,1,0:T(4,128)(2,1)}, bf16[128,4,128]{2,1,0:T(4,128)(2,1)S(1)}, u32[]{:S(2)}, u32[]{:S(2)}) collective-permute-start(bf16[128,4,128]{2,1,0:T(4,128)(2,1)} %get-tuple-element.571), channel_id=1, source_target_pairs={{0,4},{4,8},{8,12},{12,16},{16,20},{20,24},{24,28},{1,5},{5,9},{9,... | collective-permute-start | bytes 393224 | tf_op jit(solution)/shard_map/while/body/eval_jaxpr/ppermute | solution.py:14
  78.5 7.8 %collective-permute-start = (bf16[128,4,128]{2,1,0:T(4,128)(2,1)}, bf16[128,4,128]{2,1,0:T(4,128)(2,1)S(1)}, u32[]{:S(2)}, u32[]{:S(2)}) collective-permute-start(bf16[128,4,128]{2,1,0:T(4,128)(2,1)} %get-tuple-element.570), channel_id=1, source_target_pairs={{0,4},{4,8},{8,12},{12,16},{16,20},{20,24},{24,28},{1,5},{5,9},{9,... | collective-permute-start | bytes 393224 | tf_op jit(solution)/shard_map/while/body/eval_jaxpr/ppermute | solution.py:14
  82.5 7.8 %collective-permute-start.1 = (bf16[128,4,128]{2,1,0:T(4,128)(2,1)}, bf16[128,4,128]{2,1,0:T(4,128)(2,1)S(1)}, u32[]{:S(2)}, u32[]{:S(2)}) collective-permute-start(bf16[128,4,128]{2,1,0:T(4,128)(2,1)} %get-tuple-element.571), channel_id=1, source_target_pairs={{0,4},{4,8},{8,12},{12,16},{16,20},{20,24},{24,28},{1,5},{5,9},{9,... | collective-permute-start | bytes 393224 | tf_op jit(solution)/shard_map/while/body/eval_jaxpr/ppermute | solution.py:14
  97.7 1.2 copy-start.1
  134.0 10.2 %collective-permute-start.2 = (f32[128,4,128]{2,1,0:T(4,128)S(1)}, f32[128,4,128]{2,1,0:T(4,128)S(1)}, u32[]{:S(2)}, u32[]{:S(2)}) collective-permute-start(f32[128,4,128]{2,1,0:T(4,128)S(1)} %fusion.60), channel_id=1, source_target_pairs={{4,0},{8,4},{12,8},{16,12},{20,16},{24,20},{28,24},{5,1},{9,5},{13... | collective-permute-start | bytes 786440 | tf_op jit(solution)/shard_map/while/body/eval_jaxpr/ppermute | solution.py:14
  136.2 12.2 %collective-permute-start.3 = (f32[128,4,128]{2,1,0:T(4,128)S(1)}, f32[128,4,128]{2,1,0:T(4,128)S(1)}, u32[]{:S(2)}, u32[]{:S(2)}) collective-permute-start(f32[128,4,128]{2,1,0:T(4,128)S(1)} %fusion.61), channel_id=1, source_target_pairs={{4,0},{8,4},{12,8},{16,12},{20,16},{24,20},{28,24},{5,1},{9,5},{13... | collective-permute-start | bytes 786440 | tf_op jit(solution)/shard_map/while/body/eval_jaxpr/ppermute | solution.py:14
  148.6 10.2 %collective-permute-start.2 = (f32[128,4,128]{2,1,0:T(4,128)S(1)}, f32[128,4,128]{2,1,0:T(4,128)S(1)}, u32[]{:S(2)}, u32[]{:S(2)}) collective-permute-start(f32[128,4,128]{2,1,0:T(4,128)S(1)} %fusion.60), channel_id=1, source_target_pairs={{4,0},{8,4},{12,8},{16,12},{20,16},{24,20},{28,24},{5,1},{9,5},{13... | collective-permute-start | bytes 786440 | tf_op jit(solution)/shard_map/while/body/eval_jaxpr/ppermute | solution.py:14
  150.8 13.5 %collective-permute-start.3 = (f32[128,4,128]{2,1,0:T(4,128)S(1)}, f32[128,4,128]{2,1,0:T(4,128)S(1)}, u32[]{:S(2)}, u32[]{:S(2)}) collective-permute-start(f32[128,4,128]{2,1,0:T(4,128)S(1)} %fusion.61), channel_id=1, source_target_pairs={{4,0},{8,4},{12,8},{16,12},{20,16},{24,20},{28,24},{5,1},{9,5},{13... | collective-permute-start | bytes 786440 | tf_op jit(solution)/shard_map/while/body/eval_jaxpr/ppermute | solution.py:14
where the time goes:
time: 172 us; the launch traced here: 171 us
  starting transfers between devices  37.7 us (22%)
  local copies, waits for them, and re-layouts  34.2 us (20%)
  waiting for transfers between devices  30.5 us (18%)
  blocking collectives  27.6 us (16%)
  matrix products  24 us (14%)
  other arithmetic  13.5 us (8%)
  between operations  2.8 us (2%)
    all_to_all x1, blocking collectives, shards(): lax.all_to_all(grad_pick, 'dp', split_axis=0, concat_axis=1, tiled=True)  27.6 us
    ppermute x8, starting transfers between devices, shifted(): return lax.ppermute(value, axis, pairs)  25.2 us
    ppermute x8, waiting for transfers between devices, shifted(): return lax.ppermute(value, axis, pairs)  25 us
    sub x4, matrix products, block_step(): weights = jnp.where(allowed, jnp.exp(scores - top_score), 0.0)  6.43 us
    all_to_all x1, starting transfers between devices, shards(): lax.all_to_all(key_pick, 'dp', split_axis=0, concat_axis=1, tiled=True)  5.42 us
    dot_general x4, matrix products, block_step(): jnp.einsum('qrd,kd->rqk', grad_three, value_two, preferred_element_type=j...  5.09 us
    dynamic_slice x4, local copies, waits for them, and re-layouts, attend(): lax.map(one_head, (query_heads, grad_heads, key_heads, value_heads))  4.29 us
    dot_general x4, matrix products, block_step(): jnp.einsum('rqk,qrd->kd', grad_scores, query_three, preferred_element_typ...  4.2 us
  transfers between devices with their start and end apart: 11, of which 9 were waited for; matrix products, arithmetic and copies ran while one was open for 14% of the time, Pallas kernels for 0%

commit v1 on v0

v1 whole, which is shorter than its diff:
```python
import functools

import jax
import jax.numpy as jnp
from jax import lax
from jax.experimental import pallas as pl
from jax.experimental.pallas import tpu as pltpu
from jax.sharding import PartitionSpec as P

HD = 128
LOG2E = 1.4426950408889634
BIG_NEGATIVE = -1e30
VMEM_BYTES = 32 * 1024 * 1024
HEADS_STEP = 2


def partner(index, step, count):
    if count & (count - 1) == 0:
        return index ^ step, index ^ step
    return (index + step) % count, (index + count - step) % count


def exchanged(value, axis, step):
    count = lax.axis_size(axis)
    return lax.ppermute(value, axis, [(i, partner(i, step, count)[0]) for i in range(count)])


def shifted(value, axis, by):
    length = lax.axis_size(axis)
    pairs = [(i, i + by) for i in range(length) if 0 <= i + by < length]
    return lax.ppermute(value, axis, pairs)


def stage_kv_kernel(assign_ref, key_ref, value_ref, out_ref, sems):
    copies = []
    for group in range(out_ref.shape[0]):
        chosen = assign_ref[group]
        for which, source in enumerate((key_ref, value_ref)):
            copies.append(
                pltpu.make_async_copy(
                    source.at[chosen], out_ref.at[group, which], sems.at[2 * group + which]
                )
            )
    for copy in copies:
        copy.start()
    for copy in copies:
        copy.wait()


def stage_kv(assignment, keys, values):
    count, rows, width = keys.shape
    return pl.pallas_call(
        stage_kv_kernel,
        out_shape=jax.ShapeDtypeStruct((count, 2, rows, width), keys.dtype),
        in_specs=[
            pl.BlockSpec(memory_space=pltpu.SMEM),
            pl.BlockSpec(memory_space=pl.ANY),
            pl.BlockSpec(memory_space=pl.ANY),
        ],
        out_specs=pl.BlockSpec(memory_space=pl.ANY),
        scratch_shapes=[pltpu.SemaphoreType.DMA((2 * count,))],
        name="stage_kv",
    )(assignment, keys, values)


def stage_rows_kernel(picks_ref, query_ref, grad_ref, *refs):
    out_refs, sems = refs[:-1], refs[-1]
    copies = []
    for step, out_ref in enumerate(out_refs):
        chosen = picks_ref[step]
        for which, source in enumerate((query_ref, grad_ref)):
            copies.append(
                pltpu.make_async_copy(
                    source.at[chosen], out_ref.at[which], sems.at[2 * step + which]
                )
            )
    for copy in copies:
        copy.start()
    for copy in copies:
        copy.wait()


def stage_rows(picks, queries, grad_out):
    count, rows, width = queries.shape
    return pl.pallas_call(
        stage_rows_kernel,
        out_shape=[jax.ShapeDtypeStruct((2, rows, width), queries.dtype)] * count,
        in_specs=[
            pl.BlockSpec(memory_space=pltpu.SMEM),
            pl.BlockSpec(memory_space=pl.ANY),
            pl.BlockSpec(memory_space=pl.ANY),
        ],
        out_specs=[pl.BlockSpec(memory_space=pl.ANY)] * count,
        scratch_shapes=[pltpu.SemaphoreType.DMA((2 * count,))],
        name="stage_rows",
    )(picks, queries, grad_out)


def build_bias(meta_ref, segment_ref, bias_ref, rows, tok_dev, ratio):
    source, sequence, line = meta_ref[0], meta_ref[1], meta_ref[2]
    pieces = bias_ref.shape[0] // tok_dev
    lanes = ratio * rows
    eye = lax.broadcasted_iota(jnp.int32, (tok_dev, tok_dev), 0) == lax.broadcasted_iota(
        jnp.int32, (tok_dev, tok_dev), 1
    )
    token = lax.broadcasted_iota(jnp.int32, (tok_dev, lanes), 0)
    place = source * rows + lax.rem(
        lax.broadcasted_iota(jnp.int32, (tok_dev, lanes), 1), jnp.int32(rows)
    )

    def column(back):
        start = pl.multiple_of(jnp.maximum(line - back, 0) * tok_dev, tok_dev)
        every = segment_ref[:, pl.ds(start, tok_dev)].astype(jnp.float32)
        mine = lax.broadcasted_iota(jnp.int32, every.shape, 0) == sequence
        row = jnp.sum(jnp.where(mine, every, 0.0), axis=0, keepdims=True)
        return jnp.sum(jnp.where(eye, row, 0.0), axis=1, keepdims=True)

    own = column(0)
    asked = jnp.sum(jnp.where(token == place, own, 0.0), axis=0, keepdims=True)
    allowed = (own == asked) & (token <= place)
    bias_ref[:tok_dev, :] = jnp.where(allowed, 0.0, BIG_NEGATIVE)
    for back in range(1, pieces):
        held = jnp.where(line >= back, column(back), -1.0)
        bias_ref[back * tok_dev : (back + 1) * tok_dev, :] = jnp.where(
            held == asked, 0.0, BIG_NEGATIVE
        )


def attend_kernel(first, last, pieces, ratio, meta_ref, segment_ref, rows_ref, *refs):
    refs = list(refs)
    kv_refs = [refs.pop(0) for _ in range(pieces)]
    if not first:
        acc_in_ref = refs.pop(0)
        refs.pop(0)
    query_out_ref = refs.pop(0)
    if last:
        own_ref, halo_ref = refs.pop(0), refs.pop(0)
    else:
        acc_out_ref = refs.pop(0)
    bias_ref = refs.pop(0)

    rows = rows_ref.shape[1]
    count = kv_refs[0].shape[0]
    tok_dev = count * rows
    scale = 1.0 / HD**0.5

    @pl.when(pl.program_id(0) == 0)
    def _():
        build_bias(meta_ref, segment_ref, bias_ref, rows, tok_dev, ratio)

    grads = []
    for head in range(HEADS_STEP):
        columns = slice(head * HD, (head + 1) * HD)

        def stacked(which):
            base = head * ratio * HD
            return jnp.concatenate(
                [rows_ref[which, :, base + r * HD : base + (r + 1) * HD] for r in range(ratio)],
                axis=0,
            )

        def window(which):
            return jnp.concatenate(
                [ref[:, which, :, columns].reshape(tok_dev, HD) for ref in kv_refs], axis=0
            )

        query, grad = stacked(0), stacked(1)
        key, value = window(0), window(1)
        turned = (((1,), (1,)), ((), ()))
        scores = lax.dot_general(key, query, turned, preferred_element_type=jnp.float32)
        scores = scores * (scale * LOG2E) + bias_ref[...]
        top = jnp.max(scores, axis=0, keepdims=True)
        weights = jnp.exp2(scores - top)
        probs = weights * (1.0 / jnp.sum(weights, axis=0, keepdims=True))
        grad_probs = lax.dot_general(value, grad, turned, preferred_element_type=jnp.float32)
        product = probs * grad_probs
        delta = jnp.sum(product, axis=0, keepdims=True)
        grad_scores = (product - probs * delta).astype(jnp.bfloat16)
        grad_value = jnp.dot(
            probs.astype(jnp.bfloat16), grad, preferred_element_type=jnp.float32
        )
        grad_key = jnp.dot(grad_scores, query, preferred_element_type=jnp.float32)
        grad_query = lax.dot_general(
            grad_scores, key, (((0,), (0,)), ((), ())), preferred_element_type=jnp.float32
        )
        grads.append((grad_query * scale).reshape(ratio, rows, HD))
        if not first:
            grad_key = grad_key + acc_in_ref[0, :, columns]
            grad_value = grad_value + acc_in_ref[1, :, columns]
        if last:
            grad_key = grad_key * scale
            own_ref[0, :, columns] = grad_key[:tok_dev]
            own_ref[1, :, columns] = grad_value[:tok_dev]
            for back in range(1, pieces):
                span = slice(back * tok_dev, (back + 1) * tok_dev)
                halo_ref[back - 1, 0, :, columns] = grad_key[span].astype(jnp.bfloat16)
                halo_ref[back - 1, 1, :, columns] = grad_value[span].astype(jnp.bfloat16)
        else:
            acc_out_ref[0, :, columns] = grad_key
            acc_out_ref[1, :, columns] = grad_value
    query_out_ref[...] = jnp.swapaxes(jnp.concatenate(grads, axis=0), 0, 1).astype(jnp.bfloat16)


def attend(meta, segments, rows_pair, kv_pieces, carried, last):
    first = carried is None
    rows, width = rows_pair.shape[1:]
    count, _, _, kv_width = kv_pieces[0].shape
    pieces = len(kv_pieces)
    kv_heads, heads = kv_width // HD, width // HD
    ratio = heads // kv_heads
    tok_dev = count * rows
    keys = pieces * tok_dev
    step_heads, step_lanes = HEADS_STEP * ratio, HEADS_STEP * HD
    acc_spec = pl.BlockSpec((2, keys, step_lanes), lambda c, m: (0, 0, c))
    query_spec = pl.BlockSpec((rows, step_heads, HD), lambda c, m: (m[0], c, 0))
    in_specs = [
        pl.BlockSpec(segments.shape, lambda c, m: (0, 0)),
        pl.BlockSpec((2, rows, step_heads * HD), lambda c, m: (0, 0, c)),
    ]
    in_specs += [
        pl.BlockSpec((count, 2, rows, step_lanes), lambda c, m: (0, 0, 0, c)) for _ in kv_pieces
    ]
    query_shape = jax.ShapeDtypeStruct((tok_dev, heads, HD), jnp.bfloat16)
    out_shape, out_specs = [query_shape], [query_spec]
    operands = [meta, segments, rows_pair, *kv_pieces]
    aliases = {}
    if not first:
        acc, query_full = carried
        aliases[len(operands) + 1] = 0
        if not last:
            aliases[len(operands)] = 1
        operands += [acc, query_full]
        in_specs += [acc_spec, pl.BlockSpec(memory_space=pl.ANY)]
    if last:
        out_shape += [
            jax.ShapeDtypeStruct((2, tok_dev, kv_width), jnp.float32),
            jax.ShapeDtypeStruct((pieces - 1, 2, tok_dev, kv_width), jnp.bfloat16),
        ]
        out_specs += [
            pl.BlockSpec((2, tok_dev, step_lanes), lambda c, m: (0, 0, c)),
            pl.BlockSpec((pieces - 1, 2, tok_dev, step_lanes), lambda c, m: (0, 0, 0, c)),
        ]
    else:
        out_shape.append(jax.ShapeDtypeStruct((2, keys, kv_width), jnp.float32))
        out_specs.append(acc_spec)
    flops = 10 * heads * rows * keys * HD
    return pl.pallas_call(
        functools.partial(attend_kernel, first, last, pieces, ratio),
        out_shape=out_shape,
        grid_spec=pltpu.PrefetchScalarGridSpec(
            num_scalar_prefetch=1,
            grid=(kv_heads // HEADS_STEP,),
            in_specs=in_specs,
            out_specs=out_specs,
            scratch_shapes=[pltpu.VMEM((keys, ratio * rows), jnp.float32)],
        ),
        input_output_aliases=aliases,
        compiler_params=pltpu.CompilerParams(
            dimension_semantics=("arbitrary",), vmem_limit_bytes=VMEM_BYTES
        ),
        cost_estimate=pl.CostEstimate(
            flops=flops, bytes_accessed=4 * keys * kv_width * 4, transcendentals=flops // 1280
        ),
        name="attend",
    )(*operands)


def shards(queries, keys, values, grad_out, segment_ids, assignment):
    count = lax.axis_size("dp")
    uly = lax.axis_size("uly")
    group = lax.axis_index("dp")
    line = lax.axis_index("blk") * uly + lax.axis_index("uly")
    tok_dev = count * queries.shape[1]
    doc_most = min(512, tok_dev * uly)
    hops = -(-doc_most // tok_dev)
    targets = [partner(group, step, count)[0] for step in range(count)]
    sources = [partner(group, step, count)[1] for step in range(count)]
    picks = jnp.take(assignment, jnp.stack(targets))
    sequence = picks[0]
    metas = [jnp.stack([source, sequence, line]).astype(jnp.int32) for source in sources]

    kv_out = stage_kv(assignment, keys, values)
    kv_own = lax.all_to_all(kv_out, "dp", split_axis=0, concat_axis=0, tiled=True)
    staged = stage_rows(picks, queries, grad_out)
    order = [0] + sorted(range(1, count), key=lambda step: (step == count - 1, step))
    arrived = {0: staged[0]}
    for step in reversed(order[1:]):
        arrived[step] = exchanged(staged[step], "dp", step)
    pieces = [kv_own]
    for back in range(1, hops + 1):
        pieces.append(shifted(kv_own, ("blk", "uly"), back))

    carried = None
    for step in order[:-1]:
        query_full, acc = attend(metas[step], segment_ids, arrived[step], pieces, carried, False)
        carried = (acc, query_full)
    step = order[-1]
    query_full, own, halo = attend(metas[step], segment_ids, arrived[step], pieces, carried, True)
    total = own
    for back in range(1, hops + 1):
        total = total + shifted(halo[back - 1], ("blk", "uly"), -back).astype(jnp.float32)
    total = total.astype(jnp.bfloat16)
    return query_full[None], total[0][None], total[1][None]


def solution(mesh):
    in_specs = (
        P(None, ("blk", "uly", "dp"), None),
        P(None, ("blk", "uly", "dp"), None),
        P(None, ("blk", "uly", "dp"), None),
        P(None, ("blk", "uly", "dp"), None),
        P(),
        P(),
    )
    out_specs = (
        P("dp", ("blk", "uly"), None, None),
        P("dp", ("blk", "uly"), None),
        P("dp", ("blk", "uly"), None),
    )
    return jax.shard_map(shards, mesh=mesh, in_specs=in_specs, out_specs=out_specs, check_vma=False)
```

time: 172 us -> 154 us (0.90)
  Pallas kernels: 0 us -> 92.6 us
  local copies, waits for them, and re-layouts: 34.2 us -> 3.1 us
  blocking collectives: 27.6 us -> 0 us
  matrix products: 24 us -> 0 us
  starting transfers between devices: 37.7 us -> 24.1 us
  other arithmetic: 13.5 us -> 1.22 us
  between operations: 2.8 us -> 0.71 us
  waiting for transfers between devices: 30.5 us -> 32.4 us
    pallas_call x0 -> x6, Pallas kernels: none -> 92.6 us  [the longest x1 65.5 us: stage_rows(): pl.pallas_call(stage_rows_kernel, out_shape=[jax.ShapeDtypeStruct((2, row...]
    all_to_all x1 -> x0, blocking collectives: 27.6 us -> none  [shards(): lax.all_to_all(grad_pick, 'dp', split_axis=0, concat_axis=1, tiled=True)]
    ppermute x0 -> x3, waiting for transfers between devices: none -> 20.2 us  [exchanged(): lax.ppermute(value, axis, [(i, partner(i, step, count)[0]) for i in range...]
    dot_general x16 -> x0, matrix products: 17.6 us -> none  [the longest x4 5.09 us: block_step(): jnp.einsum('qrd,kd->rqk', grad_three, value_two, preferred_element_type=j...]
    ppermute x8 -> x4, waiting for transfers between devices: 25 us -> 12.3 us  [shifted(): return lax.ppermute(value, axis, pairs)]
    ppermute x8 -> x4, starting transfers between devices: 25.2 us -> 15 us  [shifted(): return lax.ppermute(value, axis, pairs)]
    all_to_all x3 -> x1, starting transfers between devices: 12.5 us -> 5.43 us  [shards(): lax.all_to_all(kv_out, 'dp', split_axis=0, concat_axis=0, tiled=True)]
    sub x4 -> x0, matrix products: 6.43 us -> none  [block_step(): weights = jnp.where(allowed, jnp.exp(scores - top_score), 0.0)]
  transfers between devices with their start and end apart: 11 -> 8, of which waited for: 9 -> 4; matrix products, arithmetic and copies ran while one was open for 14% -> 2% of each run, Pallas kernels for 0% -> 51%
where the time goes in v1:
time: 154 us
  Pallas kernels  92.6 us (60%)
  waiting for transfers between devices  32.4 us (21%)
  starting transfers between devices  24.1 us (16%)
  local copies, waits for them, and re-layouts  3.1 us (2%)
    pallas_call x1, Pallas kernels, stage_rows(): pl.pallas_call(stage_rows_kernel, out_shape=[jax.ShapeDtypeStruct((2, row...  65.5 us
    ppermute x3, waiting for transfers between devices, exchanged(): lax.ppermute(value, axis, [(i, partner(i, step, count)[0]) for i in range...  20.2 us
    pallas_call x4, Pallas kernels, attend(): pl.pallas_call(functools.partial(attend_kernel, first, last, pieces, rati...  17.3 us
    ppermute x4, starting transfers between devices, shifted(): return lax.ppermute(value, axis, pairs)  15 us
    ppermute x4, waiting for transfers between devices, shifted(): return lax.ppermute(value, axis, pairs)  12.3 us
    pallas_call x1, Pallas kernels, stage_kv(): pl.pallas_call(stage_kv_kernel, out_shape=jax.ShapeDtypeStruct((count, 2,...  9.78 us
    all_to_all x1, starting transfers between devices, shards(): lax.all_to_all(kv_out, 'dp', split_axis=0, concat_axis=0, tiled=True)  5.43 us
    ppermute x3, starting transfers between devices, exchanged(): lax.ppermute(value, axis, [(i, partner(i, step, count)[0]) for i in range...  3.61 us
  transfers between devices with their start and end apart: 8, of which 4 were waited for; matrix products, arithmetic and copies ran while one was open for 2% of the time, Pallas kernels for 51%

profile of v1, /device:TPU:1, one launch (start us, length us, event | category | flops | bytes accessed | tf_op | source)
XLA Modules:
  0.0 154.1 jit_solution(251585509459960873)
XLA Ops:
  0.6 9.8 %stage_kv.1 = bf16[4,2,32,512]{3,2,1,0:T(8,128)(2,1)} custom-call(s32[4]{0:T(128)} %assign_ref.1, bf16[4,32,512]{2,1,0:T(8,128)(2,1)} %key_ref.1, bf16[4,32,512]{2,1,0:T(8,128)(2,1)} %value_ref.1), custom_call_target="tpu_custom_call" | custom-call | tf_op jit(solution)/shard_map/stage_kv/pallas_call | solution.py:52
  10.4 5.4 %all-to-all-start = ((bf16[4,2,32,512]{3,2,1,0:T(8,128)(2,1)}), bf16[4,2,32,512]{3,2,1,0:T(8,128)(2,1)S(1)}, u32[]{:S(2)}, u32[]{:S(2)}) async-start(bf16[4,2,32,512]{3,2,1,0:T(8,128)(2,1)} %stage_kv.1), calls=%async_computation | async-start | bytes 524288 | tf_op jit(solution)/shard_map/all_to_all | solution.py:283
  15.9 1.3 gather_fusion
  17.2 0.6 and_select_fusion.picks_ref
  17.8 65.5 %stage_rows.1 = (bf16[2,32,4096]{2,1,0:T(8,128)(2,1)}, bf16[2,32,4096]{2,1,0:T(8,128)(2,1)}, bf16[2,32,4096]{2,1,0:T(8,128)(2,1)}, bf16[2,32,4096]{2,1,0:T(8,128)(2,1)}) custom-call(s32[4]{0:T(128)} %and_select_fusion.picks_ref, bf16[4,32,4096]{2,1,0:T(8,128)(2,1)} %query_ref.1, bf16[4,32,4096]{2,1,0:T(8,128)(2,1)} %grad_ref.1), custom_call_target="tpu_custom_call" | custom-call | tf_op jit(solution)/shard_map/stage_rows/pallas_call | solution.py:85
  83.3 1.5 collective-permute-start.4
  84.9 2.1 %collective-permute-start = (bf16[2,32,4096]{2,1,0:T(8,128)(2,1)}, bf16[2,32,4096]{2,1,0:T(8,128)(2,1)S(1)}, u32[]{:S(2)}, u32[]{:S(2)}) collective-permute-start(bf16[2,32,4096]{2,1,0:T(8,128)(2,1)} %get-tuple-element.16), channel_id=1, source_target_pairs={{0,3},{1,2},{2,1},{3,0},{4,7},{5,6},{6,5},{7,4},{8,11},{9,10},{10,... | collective-permute-start | bytes 1572872 | tf_op jit(solution)/shard_map/ppermute | solution.py:25
  87.1 4.8 %collective-permute-start.2 = (bf16[4,2,32,512]{3,2,1,0:T(8,128)(2,1)S(1)}, bf16[4,2,32,512]{3,2,1,0:T(8,128)(2,1)S(1)}, u32[]{:S(2)}, u32[]{:S(2)}) collective-permute-start(bf16[4,2,32,512]{3,2,1,0:T(8,128)(2,1)S(1)} %all-to-all-done.refs_0_), channel_id=1, source_target_pairs={{0,8},{4,12},{8,16},{12,20},{16,24},{20,28},{1,9},{5,13},{9,17},{1... | collective-permute-start | bytes 786440 | tf_op jit(solution)/shard_map/ppermute | solution.py:31
  91.9 3.1 %collective-permute-start.1 = (bf16[4,2,32,512]{3,2,1,0:T(8,128)(2,1)S(1)}, bf16[4,2,32,512]{3,2,1,0:T(8,128)(2,1)S(1)}, u32[]{:S(2)}, u32[]{:S(2)}) collective-permute-start(bf16[4,2,32,512]{3,2,1,0:T(8,128)(2,1)S(1)} %all-to-all-done.refs_0_), channel_id=1, source_target_pairs={{0,4},{4,8},{8,12},{12,16},{16,20},{20,24},{24,28},{1,5},{5,9},{9,... | collective-permute-start | bytes 786440 | tf_op jit(solution)/shard_map/ppermute | solution.py:31
  95.1 0.1 add_add_fusion.3.meta_ref
  95.2 0.1 add_add_fusion.meta_ref
  95.4 6.5 %collective-permute-done.1.refs_1_ = bf16[4,2,32,512]{3,2,1,0:T(8,128)(2,1)S(1)} collective-permute-done((bf16[4,2,32,512]{3,2,1,0:T(8,128)(2,1)S(1)}, bf16[4,2,32,512]{3,2,1,0:T(8,128)(2,1)S(1)}, u32[]{:S(2)}, u32[]{:S(2)}) %collective-permute-start.1) | collective-permute-done | bytes 262176 | tf_op jit(solution)/shard_map/ppermute | solution.py:31
  101.9 1.0 copy-done.1
  102.9 4.1 %attend.4 = (bf16[128,32,128]{2,1,0:T(8,128)(2,1)}, f32[2,384,512]{2,1,0:T(8,128)S(1)}) custom-call(s32[3]{0:T(128)S(1)} %add_add_fusion.3.meta_ref, s32[4,1024]{1,0:T(4,128)S(1)} %copy-done, bf16[2,32,4096]{2,1,0:T(8,128)(2,1)S(1)} %copy-done.1, bf16[4,2,32,512]{3,2,1,0:T(8,128)(2,1)S(1)} %all-to-all-done.refs_0_, ...), custom_call_target="tpu_custom_call" | custom-call | flops 503316480 | bytes 3145728 | tf_op jit(solution)/shard_map/attend/pallas_call | solution.py:247
  107.0 4.4 %attend.5 = (bf16[128,32,128]{2,1,0:T(8,128)(2,1)}, f32[2,384,512]{2,1,0:T(8,128)S(1)}) custom-call(s32[3]{0:T(128)S(1)} %add_add_fusion.2.meta_ref, s32[4,1024]{1,0:T(4,128)S(1)} %copy-done, bf16[2,32,4096]{2,1,0:T(8,128)(2,1)S(1)} %collective-permute-done.4.rows_ref, ...), custom_call_target="tpu_custom_call", output_to_operand_aliasing={{0}: (7, {}), {1}: (6, {})} | custom-call | flops 503316480 | bytes 3145728 | tf_op jit(solution)/shard_map/attend/pallas_call | solution.py:247
  111.4 20.1 %collective-permute-done.3.rows_ref = bf16[2,32,4096]{2,1,0:T(8,128)(2,1)S(1)} collective-permute-done((bf16[2,32,4096]{2,1,0:T(8,128)(2,1)}, bf16[2,32,4096]{2,1,0:T(8,128)(2,1)S(1)}, u32[]{:S(2)}, u32[]{:S(2)}) %collective-permute-start.3) | collective-permute-done | bytes 524320 | tf_op jit(solution)/shard_map/ppermute | solution.py:25
  131.6 4.4 %attend.6 = (bf16[128,32,128]{2,1,0:T(8,128)(2,1)}, f32[2,384,512]{2,1,0:T(8,128)S(1)}) custom-call(s32[3]{0:T(128)S(1)} %add_add_fusion.1.meta_ref, s32[4,1024]{1,0:T(4,128)S(1)} %copy-done, bf16[2,32,4096]{2,1,0:T(8,128)(2,1)S(1)} %collective-permute-done.3.rows_ref, ...), custom_call_target="tpu_custom_call", output_to_operand_aliasing={{0}: (7, {}), {1}: (6, {})} | custom-call | flops 503316480 | bytes 3145728 | tf_op jit(solution)/shard_map/attend/pallas_call | solution.py:247
  136.0 4.4 %attend.7 = (bf16[128,32,128]{2,1,0:T(8,128)(2,1)}, f32[2,128,512]{2,1,0:T(8,128)S(1)}, bf16[2,2,128,512]{3,2,1,0:T(8,128)(2,1)S(1)}) custom-call(s32[3]{0:T(128)S(1)} %add_add_fusion.meta_ref, s32[4,1024]{1,0:T(4,128)S(1)} %copy-done, bf16[2,32,4096]{2,1,0:T(8,128)(2,1)S(1)} %collective-permute-done.rows_ref, ...), custom_call_target="tpu_custom_call", output_to_operand_aliasing={{0}: (7, {})} | custom-call | flops 503316480 | bytes 3145728 | tf_op jit(solution)/shard_map/attend/pallas_call | solution.py:247
  140.4 5.2 %collective-permute-start.5 = (bf16[2,128,512]{2,1,0:T(8,128)(2,1)S(1)}, bf16[2,128,512]{2,1,0:T(8,128)(2,1)S(1)}, u32[]{:S(2)}, u32[]{:S(2)}) collective-permute-start(bf16[2,128,512]{2,1,0:T(8,128)(2,1)S(1)} %get-tuple-element.29), channel_id=1, source_target_pairs={{4,0},{8,4},{12,8},{16,12},{20,16},{24,20},{28,24},{5,1},{9,5},{13... | collective-permute-start | bytes 786440 | tf_op jit(solution)/shard_map/ppermute | solution.py:31
  145.6 1.9 %collective-permute-start.6 = (bf16[2,128,512]{2,1,0:T(8,128)(2,1)S(1)}, bf16[2,128,512]{2,1,0:T(8,128)(2,1)S(1)}, u32[]{:S(2)}, u32[]{:S(2)}) collective-permute-start(bf16[2,128,512]{2,1,0:T(8,128)(2,1)S(1)} %get-tuple-element.30), channel_id=1, source_target_pairs={{8,0},{12,4},{16,8},{20,12},{24,16},{28,20},{9,1},{13,5},{17,9},{2... | collective-permute-start | bytes 786440 | tf_op jit(solution)/shard_map/ppermute | solution.py:31
  147.5 1.4 collective-permute-done.5
  148.9 4.4 %collective-permute-done.6 = bf16[2,128,512]{2,1,0:T(8,128)(2,1)S(1)} collective-permute-done((bf16[2,128,512]{2,1,0:T(8,128)(2,1)S(1)}, bf16[2,128,512]{2,1,0:T(8,128)(2,1)S(1)}, u32[]{:S(2)}, u32[]{:S(2)}) %collective-permute-start.6) | collective-permute-done | bytes 262176 | tf_op jit(solution)/shard_map/ppermute | solution.py:31
  153.3 0.1 add_convert_fusion
  153.4 0.7 fusion.1
  (15 shorter events, 0.4 us)
Async XLA Ops:
  10.4 91.5 %copy-start = (s32[4,1024]{1,0:T(4,128)S(1)}, s32[4,1024]{1,0:T(4,128)}, u32[]{:S(2)}) copy-start(s32[4,1024]{1,0:T(4,128)} %segment_ref.7) | copy-start | bytes 49156
  10.4 76.6 %all-to-all-start = ((bf16[4,2,32,512]{3,2,1,0:T(8,128)(2,1)}), bf16[4,2,32,512]{3,2,1,0:T(8,128)(2,1)S(1)}, u32[]{:S(2)}, u32[]{:S(2)}) async-start(bf16[4,2,32,512]{3,2,1,0:T(8,128)(2,1)} %stage_kv.1), calls=%async_computation | async-start | bytes 524288 | tf_op jit(solution)/shard_map/all_to_all | solution.py:283
  17.8 69.1 %copy-start.2 = (s32[4]{0:T(128)S(1)}, s32[4]{0:T(128)}, u32[]{:S(2)}) copy-start(s32[4]{0:T(128)} %and_select_fusion.picks_ref) | copy-start | bytes 52
  83.3 23.7 %collective-permute-start.4 = (bf16[2,32,4096]{2,1,0:T(8,128)(2,1)}, bf16[2,32,4096]{2,1,0:T(8,128)(2,1)S(1)}, u32[]{:S(2)}, u32[]{:S(2)}) collective-permute-start(bf16[2,32,4096]{2,1,0:T(8,128)(2,1)} %get-tuple-element.18), channel_id=1, source_target_pairs={{0,1},{1,0},{2,3},{3,2},{4,5},{5,4},{6,7},{7,6},{8,9},{9,8},{10,11... | collective-permute-start | bytes 1572872 | tf_op jit(solution)/shard_map/ppermute | solution.py:25
  84.9 51.1 %collective-permute-start = (bf16[2,32,4096]{2,1,0:T(8,128)(2,1)}, bf16[2,32,4096]{2,1,0:T(8,128)(2,1)S(1)}, u32[]{:S(2)}, u32[]{:S(2)}) collective-permute-start(bf16[2,32,4096]{2,1,0:T(8,128)(2,1)} %get-tuple-element.16), channel_id=1, source_target_pairs={{0,3},{1,2},{2,1},{3,0},{4,7},{5,6},{6,5},{7,4},{8,11},{9,10},{10,... | collective-permute-start | bytes 1572872 | tf_op jit(solution)/shard_map/ppermute | solution.py:25
  87.0 44.6 %collective-permute-start.3 = (bf16[2,32,4096]{2,1,0:T(8,128)(2,1)}, bf16[2,32,4096]{2,1,0:T(8,128)(2,1)S(1)}, u32[]{:S(2)}, u32[]{:S(2)}) collective-permute-start(bf16[2,32,4096]{2,1,0:T(8,128)(2,1)} %get-tuple-element.17), channel_id=1, source_target_pairs={{0,2},{1,3},{2,0},{3,1},{4,6},{5,7},{6,4},{7,5},{8,10},{9,11},{10,... | collective-permute-start | bytes 1572872 | tf_op jit(solution)/shard_map/ppermute | solution.py:25
  87.1 8.3 %collective-permute-start.2 = (bf16[4,2,32,512]{3,2,1,0:T(8,128)(2,1)S(1)}, bf16[4,2,32,512]{3,2,1,0:T(8,128)(2,1)S(1)}, u32[]{:S(2)}, u32[]{:S(2)}) collective-permute-start(bf16[4,2,32,512]{3,2,1,0:T(8,128)(2,1)S(1)} %all-to-all-done.refs_0_), channel_id=1, source_target_pairs={{0,8},{4,12},{8,16},{12,20},{16,24},{20,28},{1,9},{5,13},{9,17},{1... | collective-permute-start | bytes 786440 | tf_op jit(solution)/shard_map/ppermute | solution.py:31
  91.9 10.0 %collective-permute-start.1 = (bf16[4,2,32,512]{3,2,1,0:T(8,128)(2,1)S(1)}, bf16[4,2,32,512]{3,2,1,0:T(8,128)(2,1)S(1)}, u32[]{:S(2)}, u32[]{:S(2)}) collective-permute-start(bf16[4,2,32,512]{3,2,1,0:T(8,128)(2,1)S(1)} %all-to-all-done.refs_0_), channel_id=1, source_target_pairs={{0,4},{4,8},{8,12},{12,16},{16,20},{20,24},{24,28},{1,5},{5,9},{9,... | collective-permute-start | bytes 786440 | tf_op jit(solution)/shard_map/ppermute | solution.py:31
  101.9 1.0 copy-start.1
  140.4 8.5 %collective-permute-start.5 = (bf16[2,128,512]{2,1,0:T(8,128)(2,1)S(1)}, bf16[2,128,512]{2,1,0:T(8,128)(2,1)S(1)}, u32[]{:S(2)}, u32[]{:S(2)}) collective-permute-start(bf16[2,128,512]{2,1,0:T(8,128)(2,1)S(1)} %get-tuple-element.29), channel_id=1, source_target_pairs={{4,0},{8,4},{12,8},{16,12},{20,16},{24,20},{28,24},{5,1},{9,5},{13... | collective-permute-start | bytes 786440 | tf_op jit(solution)/shard_map/ppermute | solution.py:31
  145.6 7.7 %collective-permute-start.6 = (bf16[2,128,512]{2,1,0:T(8,128)(2,1)S(1)}, bf16[2,128,512]{2,1,0:T(8,128)(2,1)S(1)}, u32[]{:S(2)}, u32[]{:S(2)}) collective-permute-start(bf16[2,128,512]{2,1,0:T(8,128)(2,1)S(1)} %get-tuple-element.30), channel_id=1, source_target_pairs={{8,0},{12,4},{16,8},{20,12},{24,16},{28,20},{9,1},{13,5},{17,9},{2... | collective-permute-start | bytes 786440 | tf_op jit(solution)/shard_map/ppermute | solution.py:31

commit v2 on v1

v2 whole, which is shorter than its diff:
```python
import functools

import jax
import jax.numpy as jnp
from jax import lax
from jax.experimental import pallas as pl
from jax.experimental.pallas import tpu as pltpu
from jax.sharding import PartitionSpec as P

HD = 128
LOG2E = 1.4426950408889634
BIG_NEGATIVE = -1e30
VMEM_BYTES = 32 * 1024 * 1024
HEADS_STEP = 2


def partner(index, step, count):
    if count & (count - 1) == 0:
        return index ^ step, index ^ step
    return (index + step) % count, (index + count - step) % count


def exchanged(value, axis, step):
    count = lax.axis_size(axis)
    return lax.ppermute(value, axis, [(i, partner(i, step, count)[0]) for i in range(count)])


def shifted(value, axis, by):
    length = lax.axis_size(axis)
    pairs = [(i, i + by) for i in range(length) if 0 <= i + by < length]
    return lax.ppermute(value, axis, pairs)


def stage_kernel(count, parts, meta_ref, assign_ref, query_ref, grad_ref, key_ref, value_ref, *refs):
    group = meta_ref[0]
    kv_out_ref, row_out_refs = refs[0], refs[1 : 1 + len(parts)]
    kv_held_ref, row_held_refs = refs[1 + len(parts)], refs[2 + len(parts) : 2 + 2 * len(parts)]
    in_sems, out_sems = refs[-2:]
    loads, stores = [], []

    def hop(source, held, target):
        slot = len(loads)
        loads.append(pltpu.make_async_copy(source, held, in_sems.at[slot]))
        stores.append(pltpu.make_async_copy(held, target, out_sems.at[slot]))

    for other in range(count):
        chosen = assign_ref[other]
        for which, source in enumerate((key_ref, value_ref)):
            hop(source.at[chosen], kv_held_ref.at[other, which], kv_out_ref.at[other, which])
    for (step, start, width), out_ref, held_ref in zip(parts, row_out_refs, row_held_refs):
        chosen = assign_ref[partner(group, step, count)[0]]
        for which, source in enumerate((query_ref, grad_ref)):
            hop(
                source.at[chosen, :, start : start + width], held_ref.at[which], out_ref.at[which]
            )
    for load in loads:
        load.start()
    for load, store in zip(loads, stores):
        load.wait()
        store.start()
    for store in stores:
        store.wait()


def stage(meta, assignment, queries, grad_out, keys, values, parts):
    count, rows, _ = queries.shape
    kv_shape = (count, 2, rows, keys.shape[2])
    shapes = [kv_shape] + [(2, rows, width) for _, _, width in parts]
    copies = 2 * count + 2 * len(parts)
    anywhere, scalars = pl.BlockSpec(memory_space=pl.ANY), pl.BlockSpec(memory_space=pltpu.SMEM)
    return pl.pallas_call(
        functools.partial(stage_kernel, count, parts),
        out_shape=[jax.ShapeDtypeStruct(shape, queries.dtype) for shape in shapes],
        in_specs=[scalars] * 2 + [anywhere] * 4,
        out_specs=[anywhere] * len(shapes),
        scratch_shapes=[pltpu.VMEM(shape, queries.dtype) for shape in shapes]
        + [pltpu.SemaphoreType.DMA((copies,))] * 2,
        compiler_params=pltpu.CompilerParams(vmem_limit_bytes=VMEM_BYTES),
        name="stage",
    )(meta, assignment, queries, grad_out, keys, values)


def build_bias(source, sequence, line, segment_ref, bias_ref, rows, tok_dev, ratio):
    pieces = bias_ref.shape[0] // tok_dev
    lanes = ratio * rows
    eye = lax.broadcasted_iota(jnp.int32, (tok_dev, tok_dev), 0) == lax.broadcasted_iota(
        jnp.int32, (tok_dev, tok_dev), 1
    )
    token = lax.broadcasted_iota(jnp.int32, (tok_dev, lanes), 0)
    place = source * rows + lax.rem(
        lax.broadcasted_iota(jnp.int32, (tok_dev, lanes), 1), jnp.int32(rows)
    )

    def column(back):
        start = pl.multiple_of(jnp.maximum(line - back, 0) * tok_dev, tok_dev)
        every = segment_ref[:, pl.ds(start, tok_dev)].astype(jnp.float32)
        mine = lax.broadcasted_iota(jnp.int32, every.shape, 0) == sequence
        row = jnp.sum(jnp.where(mine, every, 0.0), axis=0, keepdims=True)
        return jnp.sum(jnp.where(eye, row, 0.0), axis=1, keepdims=True)

    own = column(0)
    asked = jnp.sum(jnp.where(token == place, own, 0.0), axis=0, keepdims=True)
    allowed = (own == asked) & (token <= place)
    bias_ref[:tok_dev, :] = jnp.where(allowed, 0.0, BIG_NEGATIVE)
    for back in range(1, pieces):
        held = jnp.where(line >= back, column(back), -1.0)
        bias_ref[back * tok_dev : (back + 1) * tok_dev, :] = jnp.where(
            held == asked, 0.0, BIG_NEGATIVE
        )


def attend_kernel(
    step, first, filled, last, pieces, ratio, meta_ref, assign_ref, segment_ref, query_ref, grad_ref, *refs
):
    refs = list(refs)
    kv_refs = [refs.pop(0) for _ in range(pieces)]
    if not first:
        acc_in_ref = refs.pop(0)
    if filled:
        refs.pop(0)
    query_out_ref = refs.pop(0)
    if last:
        own_ref, halo_refs = refs.pop(0), [refs.pop(0) for _ in range(pieces - 1)]
    else:
        acc_out_ref = refs.pop(0)
    bias_ref, held_ref = refs

    rows = query_ref.shape[0]
    count = kv_refs[0].shape[0]
    tok_dev = count * rows
    scale = 1.0 / HD**0.5
    head = pl.program_id(0)

    @pl.when(head == 0)
    def _():
        group = meta_ref[0]
        source = partner(group, step, count)[1]
        build_bias(
            source, assign_ref[group], meta_ref[1], segment_ref, bias_ref, rows, tok_dev, ratio
        )

    def stacked(ref):
        return jnp.concatenate([ref[:, r * HD : (r + 1) * HD] for r in range(ratio)], axis=0)

    def window(which):
        return jnp.concatenate([ref[:, which].reshape(tok_dev, HD) for ref in kv_refs], axis=0)

    query, grad = stacked(query_ref), stacked(grad_ref)
    key, value = window(0), window(1)
    turned = (((1,), (1,)), ((), ()))
    scores = lax.dot_general(key, query, turned, preferred_element_type=jnp.float32)
    scores = scores * (scale * LOG2E) + bias_ref[...]
    top = jnp.max(scores, axis=0, keepdims=True)
    weights = jnp.exp2(scores - top)
    probs = weights * (1.0 / jnp.sum(weights, axis=0, keepdims=True))
    grad_probs = lax.dot_general(value, grad, turned, preferred_element_type=jnp.float32)
    product = probs * grad_probs
    delta = jnp.sum(product, axis=0, keepdims=True)
    grad_scores = (product - probs * delta).astype(jnp.bfloat16)
    grad_value = jnp.dot(probs.astype(jnp.bfloat16), grad, preferred_element_type=jnp.float32)
    grad_key = jnp.dot(grad_scores, query, preferred_element_type=jnp.float32)
    grad_query = lax.dot_general(
        grad_scores, key, (((0,), (0,)), ((), ())), preferred_element_type=jnp.float32
    )
    held_ref[head] = (grad_query * scale).reshape(ratio, rows, HD)
    if not first:
        grad_key = grad_key + acc_in_ref[0]
        grad_value = grad_value + acc_in_ref[1]
    if last:
        grad_key = grad_key * scale
        own_ref[0] = grad_key[:tok_dev]
        own_ref[1] = grad_value[:tok_dev]
        for back, halo_ref in enumerate(halo_refs, 1):
            span = slice(back * tok_dev, (back + 1) * tok_dev)
            halo_ref[0] = grad_key[span].astype(jnp.bfloat16)
            halo_ref[1] = grad_value[span].astype(jnp.bfloat16)
    else:
        acc_out_ref[0] = grad_key
        acc_out_ref[1] = grad_value

    @pl.when(head == HEADS_STEP - 1)
    def _():
        held = held_ref[...].reshape(HEADS_STEP * ratio, rows, HD)
        query_out_ref[...] = jnp.swapaxes(held, 0, 1).astype(jnp.bfloat16)


def attend(step, half, lanes_from, heads, meta, assignment, segments, query, grad, kv_pieces, acc, full, last):
    first, filled = acc is None, full is not None
    rows, (count, _, _, kv_width) = query[0].shape[1], kv_pieces[0].shape
    pieces = len(kv_pieces)
    ratio = heads // (kv_width // HD)
    tok_dev = count * rows
    keys = pieces * tok_dev
    step_lanes = HEADS_STEP * HD
    base = half * HEADS_STEP

    def rows_spec(pick):
        return pl.BlockSpec(
            (None, rows, ratio * HD), lambda c, m, a: (pick(m, a), 0, lanes_from + c)
        )

    acc_spec = pl.BlockSpec((2, keys, HD), lambda c, m, a: (0, 0, c))
    in_specs = [
        pl.BlockSpec(segments.shape, lambda c, m, a: (0, 0)),
        rows_spec(query[1]),
        rows_spec(grad[1]),
    ]
    in_specs += [
        pl.BlockSpec((count, 2, rows, HD), lambda c, m, a: (0, 0, 0, base + c)) for _ in kv_pieces
    ]
    operands = [meta, assignment, segments, query[0], grad[0], *kv_pieces]
    aliases = {}
    if not first:
        if not last:
            aliases[len(operands)] = 1
        operands.append(acc)
        in_specs.append(acc_spec)
    if filled:
        aliases[len(operands)] = 0
        operands.append(full)
        in_specs.append(pl.BlockSpec(memory_space=pl.ANY))
    out_shape = [jax.ShapeDtypeStruct((tok_dev, heads, HD), jnp.bfloat16)]
    out_specs = [
        pl.BlockSpec(
            (rows, HEADS_STEP * ratio, HD),
            lambda c, m, a: (partner(m[0], step, count)[1], half, 0),
        )
    ]
    if last:
        span_spec = pl.BlockSpec((2, tok_dev, HD), lambda c, m, a: (0, 0, c))
        out_shape.append(jax.ShapeDtypeStruct((2, tok_dev, step_lanes), jnp.float32))
        out_shape += [jax.ShapeDtypeStruct((2, tok_dev, step_lanes), jnp.bfloat16)] * (pieces - 1)
        out_specs += [span_spec] * pieces
    else:
        out_shape.append(jax.ShapeDtypeStruct((2, keys, step_lanes), jnp.float32))
        out_specs.append(acc_spec)
    pairs = HEADS_STEP * ratio * rows * keys
    return pl.pallas_call(
        functools.partial(attend_kernel, step, first, filled, last, pieces, ratio),
        out_shape=out_shape,
        grid_spec=pltpu.PrefetchScalarGridSpec(
            num_scalar_prefetch=2,
            grid=(HEADS_STEP,),
            in_specs=in_specs,
            out_specs=out_specs,
            scratch_shapes=[
                pltpu.VMEM((keys, ratio * rows), jnp.float32),
                pltpu.VMEM((HEADS_STEP, ratio, rows, HD), jnp.float32),
            ],
        ),
        input_output_aliases=aliases,
        compiler_params=pltpu.CompilerParams(
            dimension_semantics=("arbitrary",), vmem_limit_bytes=VMEM_BYTES
        ),
        cost_estimate=pl.CostEstimate(
            flops=10 * pairs * HD, bytes_accessed=8 * keys * step_lanes, transcendentals=pairs
        ),
        name="attend",
    )(*operands)


def shards(queries, keys, values, grad_out, segment_ids, assignment):
    count = lax.axis_size("dp")
    uly = lax.axis_size("uly")
    group = lax.axis_index("dp")
    line = lax.axis_index("blk") * uly + lax.axis_index("uly")
    width, kv_width = queries.shape[2], keys.shape[2]
    heads, kv_heads = width // HD, kv_width // HD
    halves = kv_heads // HEADS_STEP
    part = width // halves
    tok_dev = count * queries.shape[1]
    doc_most = min(512, tok_dev * uly)
    hops = -(-doc_most // tok_dev)
    meta = jnp.stack([group, line]).astype(jnp.int32)
    final = count - 1

    parts = [(step, 0, width) for step in range(1, final)]
    parts += [(final, half * part, part) for half in range(halves)]
    kv_out, *staged = stage(meta, assignment, queries, grad_out, keys, values, parts)
    kv_own = lax.all_to_all(kv_out, "dp", split_axis=0, concat_axis=0, tiled=True)
    whole = {step: exchanged(staged[step - 1], "dp", step) for step in range(final - 1, 0, -1)}
    split = [exchanged(staged[final - 1], "dp", final)]
    for half in range(1, halves):
        after, _ = lax.optimization_barrier((staged[final - 1 + half], split[-1]))
        split.append(exchanged(after, "dp", final))
    pieces = [kv_own]
    for back in range(1, hops + 1):
        pieces.append(shifted(kv_own, ("blk", "uly"), back))

    accs, full, own, halos = [None] * halves, None, [None] * halves, [None] * halves

    def visit(step, half, last):
        nonlocal full
        kv_step = HEADS_STEP * half
        if step == 0:
            query = (queries, lambda m, a: a[m[0]])
            grad = (grad_out, lambda m, a: a[m[0]])
        else:
            both = split[half] if step == final else whole[step]
            query, grad = (both, lambda m, a: 0), (both, lambda m, a: 1)
            if step == final:
                kv_step = 0
        full, *rest = attend(
            step, half, kv_step, heads, meta, assignment, segment_ids, query, grad, pieces,
            accs[half], full, last,
        )
        if last:
            own[half], halos[half] = rest[0], rest[1:]
        else:
            accs[half] = rest[0]

    for step in range(final - 1):
        for half in range(halves):
            visit(step, half, False)
    for half in range(halves - 1):
        visit(final, half, False)
        visit(final - 1, half, True)
    visit(final - 1, halves - 1, False)
    visit(final, halves - 1, True)

    totals = []
    for half in range(halves):
        total = own[half]
        for back in range(1, hops + 1):
            total = total + shifted(halos[half][back - 1], ("blk", "uly"), -back).astype(
                jnp.float32
            )
        totals.append(total.astype(jnp.bfloat16))
    total = jnp.concatenate(totals, axis=2)
    return full[None], total[0][None], total[1][None]


def solution(mesh):
    in_specs = (
        P(None, ("blk", "uly", "dp"), None),
        P(None, ("blk", "uly", "dp"), None),
        P(None, ("blk", "uly", "dp"), None),
        P(None, ("blk", "uly", "dp"), None),
        P(),
        P(),
    )
    out_specs = (
        P("dp", ("blk", "uly"), None, None),
        P("dp", ("blk", "uly"), None),
        P("dp", ("blk", "uly"), None),
    )
    return jax.shard_map(shards, mesh=mesh, in_specs=in_specs, out_specs=out_specs, check_vma=False)
```

time: 154 us -> 106 us (0.69)
  the two profiles are of different devices: /device:TPU:1 before, /device:TPU:11 now
where the time goes in v2:
time: 106 us; the launch traced here: 105 us
  waiting for transfers between devices  40.1 us (38%)
  Pallas kernels  28.7 us (27%)
  starting transfers between devices  27 us (25%)
  local copies, waits for them, and re-layouts  7.86 us (7%)
    ppermute x4, waiting for transfers between devices, exchanged(): lax.ppermute(value, axis, [(i, partner(i, step, count)[0]) for i in range...  32.1 us
    pallas_call x8, Pallas kernels, attend(): pl.pallas_call(functools.partial(attend_kernel, step, first, filled, last...  26.5 us
    ppermute x6, starting transfers between devices, shifted(): return lax.ppermute(value, axis, pairs)  18.9 us
    unnamed x24, local copies, waits for them, and re-layouts  7.86 us
    all_to_all x1, starting transfers between devices, shards(): lax.all_to_all(kv_out, 'dp', split_axis=0, concat_axis=0, tiled=True)  4.89 us
    ppermute x6, waiting for transfers between devices, shifted(): return lax.ppermute(value, axis, pairs)  4.63 us
    all_to_all x1, waiting for transfers between devices, shards(): lax.all_to_all(kv_out, 'dp', split_axis=0, concat_axis=0, tiled=True)  3.43 us
    ppermute x4, starting transfers between devices, exchanged(): lax.ppermute(value, axis, [(i, partner(i, step, count)[0]) for i in range...  3.19 us
  transfers between devices with their start and end apart: 11, of which 4 were waited for; matrix products, arithmetic and copies ran while one was open for 0% of the time, Pallas kernels for 22%

profile of v2, /device:TPU:11, one launch (start us, length us, event | category | flops | bytes accessed | tf_op | source)
XLA Modules:
  0.0 105.4 jit_solution(17059338975122441807)
XLA Ops:
  1.3 1.2 %copy-done = bf16[4,32,4096]{2,1,0:T(8,128)(2,1)S(1)} copy-done((bf16[4,32,4096]{2,1,0:T(8,128)(2,1)S(1)}, bf16[4,32,4096]{2,1,0:T(8,128)(2,1)}, u32[]{:S(2)}) %copy-start) | copy-done | bytes 1048600
  2.5 1.2 %copy-done.2 = bf16[4,32,4096]{2,1,0:T(8,128)(2,1)S(1)} copy-done((bf16[4,32,4096]{2,1,0:T(8,128)(2,1)S(1)}, bf16[4,32,4096]{2,1,0:T(8,128)(2,1)}, u32[]{:S(2)}) %copy-start.2) | copy-done | bytes 1048600
  4.7 0.9 copy-done.6
  5.6 2.2 %stage.1 = (bf16[4,2,32,512]{3,2,1,0:T(8,128)(2,1)}, bf16[2,32,4096]{2,1,0:T(8,128)(2,1)S(1)}, bf16[2,32,4096]{2,1,0:T(8,128)(2,1)S(1)}, bf16[2,32,2048]{2,1,0:T(8,128)(2,1)S(1)}, bf16[2,32,2048]{2,1,0:T(8,128)(2,1)S(1)}) custom-call(s32[2]{0:T(128)S(1)} %pad_add_fusion.meta_ref, s32[4]{0:T(128)S(1)} %copy-done.7, bf16[4,32,4096]{2,1,0:T(8,128)(2,1)S(1)} %copy-done, ...), custom_call_target="tpu_custom_call" | custom-call | tf_op jit(solution)/shard_map/stage/pallas_call | solution.py:71
  10.8 4.9 %all-to-all-start = ((bf16[4,2,32,512]{3,2,1,0:T(8,128)(2,1)}), bf16[4,2,32,512]{3,2,1,0:T(8,128)(2,1)S(1)}, u32[]{:S(2)}, u32[]{:S(2)}) async-start(bf16[4,2,32,512]{3,2,1,0:T(8,128)(2,1)} %get-tuple-element.32), calls=%async_computation | async-start | bytes 524288 | tf_op jit(solution)/shard_map/all_to_all | solution.py:280
  15.7 2.3 %collective-permute-start.4 = (bf16[2,32,4096]{2,1,0:T(8,128)(2,1)}, bf16[2,32,4096]{2,1,0:T(8,128)(2,1)S(1)}, u32[]{:S(2)}, u32[]{:S(2)}) collective-permute-start(bf16[2,32,4096]{2,1,0:T(8,128)(2,1)} %copy-done.8), channel_id=1, source_target_pairs={{0,2},{1,3},{2,0},{3,1},{4,6},{5,7},{6,4},{7,5},{8,10},{9,11},{10,... | collective-permute-start | bytes 1572872 | tf_op jit(solution)/shard_map/ppermute | solution.py:25
  18.4 3.4 %all-to-all-done.refs_0_ = bf16[4,2,32,512]{3,2,1,0:T(8,128)(2,1)S(1)} async-done(((bf16[4,2,32,512]{3,2,1,0:T(8,128)(2,1)}), bf16[4,2,32,512]{3,2,1,0:T(8,128)(2,1)S(1)}, u32[]{:S(2)}, u32[]{:S(2)}) %all-to-all-start) | async-done | bytes 262176 | tf_op jit(solution)/shard_map/all_to_all | solution.py:280
  21.8 6.6 %collective-permute-start.3 = (bf16[4,2,32,512]{3,2,1,0:T(8,128)(2,1)S(1)}, bf16[4,2,32,512]{3,2,1,0:T(8,128)(2,1)S(1)}, u32[]{:S(2)}, u32[]{:S(2)}) collective-permute-start(bf16[4,2,32,512]{3,2,1,0:T(8,128)(2,1)S(1)} %all-to-all-done.refs_0_), channel_id=1, source_target_pairs={{0,8},{4,12},{8,16},{12,20},{16,24},{20,28},{1,9},{5,13},{9,17},{1... | collective-permute-start | bytes 786440 | tf_op jit(solution)/shard_map/ppermute | solution.py:31
  28.4 1.9 %collective-permute-start.2 = (bf16[4,2,32,512]{3,2,1,0:T(8,128)(2,1)S(1)}, bf16[4,2,32,512]{3,2,1,0:T(8,128)(2,1)S(1)}, u32[]{:S(2)}, u32[]{:S(2)}) collective-permute-start(bf16[4,2,32,512]{3,2,1,0:T(8,128)(2,1)S(1)} %all-to-all-done.refs_0_), channel_id=1, source_target_pairs={{0,4},{4,8},{8,12},{12,16},{16,20},{20,24},{24,28},{1,5},{5,9},{9,... | collective-permute-start | bytes 786440 | tf_op jit(solution)/shard_map/ppermute | solution.py:31
  30.3 32.1 %collective-permute-done.query_ref.grad_ref = bf16[2,32,2048]{2,1,0:T(8,128)(2,1)} collective-permute-done((bf16[2,32,2048]{2,1,0:T(8,128)(2,1)}, bf16[2,32,2048]{2,1,0:T(8,128)(2,1)}, u32[]{:S(2)}, u32[]{:S(2)}) %collective-permute-start) | collective-permute-done | bytes 262176 | tf_op jit(solution)/shard_map/ppermute | solution.py:25
  62.9 3.1 %attend.8 = (bf16[128,32,128]{2,1,0:T(8,128)(2,1)}, f32[2,384,256]{2,1,0:T(8,128)S(1)}) custom-call(s32[2]{0:T(128)S(1)} %pad_add_fusion.meta_ref, s32[4]{0:T(128)S(1)} %copy-done.7, s32[4,1024]{1,0:T(4,128)S(1)} %copy-done.4, bf16[4,32,4096]{2,1,0:T(8,128)(2,1)S(1)} %copy-done.1, bf16[4,32,4096]{2,1,0:T(8,128)(2,1)S(1)} %copy-done.3, ...), custom_call_target="tpu_custom_call" | custom-call | flops 251658240 | bytes 786432 | tf_op jit(solution)/shard_map/attend/pallas_call | solution.py:238
  66.0 3.1 %attend.9 = (bf16[128,32,128]{2,1,0:T(8,128)(2,1)}, f32[2,384,256]{2,1,0:T(8,128)S(1)}) custom-call(s32[2]{0:T(128)S(1)} %pad_add_fusion.meta_ref, s32[4]{0:T(128)S(1)} %copy-done.7, s32[4,1024]{1,0:T(4,128)S(1)} %copy-done.4, bf16[4,32,4096]{2,1,0:T(8,128)(2,1)S(1)} %copy-done.1, ...), custom_call_target="tpu_custom_call", output_to_operand_aliasing={{0}: (8, {})} | custom-call | flops 251658240 | bytes 786432 | tf_op jit(solution)/shard_map/attend/pallas_call | solution.py:238
  69.2 3.3 %attend.10 = (bf16[128,32,128]{2,1,0:T(8,128)(2,1)}, f32[2,384,256]{2,1,0:T(8,128)S(1)}) custom-call(s32[2]{0:T(128)S(1)} %pad_add_fusion.meta_ref, s32[4]{0:T(128)S(1)} %copy-done.7, s32[4,1024]{1,0:T(4,128)S(1)} %copy-done.4, bf16[2,32,4096]{2,1,0:T(8,128)(2,1)S(1)} %collective-permute-done.5.query_ref.grad_ref, ...), custom_call_target="tpu_custom_call", output_to_operand_aliasing={{1}: (8, {}), {0}: (9, {})} | custom-call | flops 251658240 | bytes 786432 | tf_op jit(solution)/shard_map/attend/pallas_call | solution.py:238
  72.4 3.3 %attend.11 = (bf16[128,32,128]{2,1,0:T(8,128)(2,1)}, f32[2,384,256]{2,1,0:T(8,128)S(1)}) custom-call(s32[2]{0:T(128)S(1)} %pad_add_fusion.meta_ref, s32[4]{0:T(128)S(1)} %copy-done.7, s32[4,1024]{1,0:T(4,128)S(1)} %copy-done.4, bf16[2,32,4096]{2,1,0:T(8,128)(2,1)S(1)} %collective-permute-done.5.query_ref.grad_ref, ...), custom_call_target="tpu_custom_call", output_to_operand_aliasing={{1}: (8, {}), {0}: (9, {})} | custom-call | flops 251658240 | bytes 786432 | tf_op jit(solution)/shard_map/attend/pallas_call | solution.py:238
  75.7 3.9 %attend.12 = (bf16[128,32,128]{2,1,0:T(8,128)(2,1)}, f32[2,384,256]{2,1,0:T(8,128)S(1)}) custom-call(s32[2]{0:T(128)S(1)} %pad_add_fusion.meta_ref, s32[4]{0:T(128)S(1)} %copy-done.7, s32[4,1024]{1,0:T(4,128)S(1)} %copy-done.4, bf16[2,32,2048]{2,1,0:T(8,128)(2,1)} %collective-permute-done.query_ref.grad_ref, ...), custom_call_target="tpu_custom_call", output_to_operand_aliasing={{1}: (8, {}), {0}: (9, {})} | custom-call | flops 251658240 | bytes 786432 | tf_op jit(solution)/shard_map/attend/pallas_call | solution.py:238
  79.6 3.3 %attend.13 = (bf16[128,32,128]{2,1,0:T(8,128)(2,1)}, f32[2,128,256]{2,1,0:T(8,128)S(1)}, bf16[2,128,256]{2,1,0:T(8,128)(2,1)S(1)}, bf16[2,128,256]{2,1,0:T(8,128)(2,1)S(1)}) custom-call(s32[2]{0:T(128)S(1)} %pad_add_fusion.meta_ref, s32[4]{0:T(128)S(1)} %copy-done.7, s32[4,1024]{1,0:T(4,128)S(1)} %copy-done.4, ...), custom_call_target="tpu_custom_call", output_to_operand_aliasing={{0}: (9, {})} | custom-call | flops 251658240 | bytes 786432 | tf_op jit(solution)/shard_map/attend/pallas_call | solution.py:238
  82.9 3.3 %attend.14 = (bf16[128,32,128]{2,1,0:T(8,128)(2,1)}, f32[2,384,256]{2,1,0:T(8,128)S(1)}) custom-call(s32[2]{0:T(128)S(1)} %pad_add_fusion.meta_ref, s32[4]{0:T(128)S(1)} %copy-done.7, s32[4,1024]{1,0:T(4,128)S(1)} %copy-done.4, bf16[2,32,4096]{2,1,0:T(8,128)(2,1)S(1)} %collective-permute-done.4.query_ref.grad_ref, ...), custom_call_target="tpu_custom_call", output_to_operand_aliasing={{1}: (8, {}), {0}: (9, {})} | custom-call | flops 251658240 | bytes 786432 | tf_op jit(solution)/shard_map/attend/pallas_call | solution.py:238
  86.2 3.3 %attend.15 = (bf16[128,32,128]{2,1,0:T(8,128)(2,1)}, f32[2,128,256]{2,1,0:T(8,128)S(1)}, bf16[2,128,256]{2,1,0:T(8,128)(2,1)S(1)}, bf16[2,128,256]{2,1,0:T(8,128)(2,1)S(1)}) custom-call(s32[2]{0:T(128)S(1)} %pad_add_fusion.meta_ref, s32[4]{0:T(128)S(1)} %copy-done.7, s32[4,1024]{1,0:T(4,128)S(1)} %copy-done.4, ...), custom_call_target="tpu_custom_call", output_to_operand_aliasing={{0}: (9, {})} | custom-call | flops 251658240 | bytes 786432 | tf_op jit(solution)/shard_map/attend/pallas_call | solution.py:238
  89.5 2.2 %collective-permute-start.8 = (bf16[2,128,256]{2,1,0:T(8,128)(2,1)S(1)}, bf16[2,128,256]{2,1,0:T(8,128)(2,1)S(1)}, u32[]{:S(2)}, u32[]{:S(2)}) collective-permute-start(bf16[2,128,256]{2,1,0:T(8,128)(2,1)S(1)} %get-tuple-element.53), channel_id=1, source_target_pairs={{4,0},{8,4},{12,8},{16,12},{20,16},{24,20},{28,24},{5,1},{9,5},{13... | collective-permute-start | bytes 393224 | tf_op jit(solution)/shard_map/ppermute | solution.py:31
  91.7 3.6 %collective-permute-start.9 = (bf16[2,128,256]{2,1,0:T(8,128)(2,1)S(1)}, bf16[2,128,256]{2,1,0:T(8,128)(2,1)S(1)}, u32[]{:S(2)}, u32[]{:S(2)}) collective-permute-start(bf16[2,128,256]{2,1,0:T(8,128)(2,1)S(1)} %get-tuple-element.54), channel_id=1, source_target_pairs={{8,0},{12,4},{16,8},{20,12},{24,16},{28,20},{9,1},{13,5},{17,9},{2... | collective-permute-start | bytes 393224 | tf_op jit(solution)/shard_map/ppermute | solution.py:31
  95.3 2.7 %collective-permute-start.6 = (bf16[2,128,256]{2,1,0:T(8,128)(2,1)S(1)}, bf16[2,128,256]{2,1,0:T(8,128)(2,1)S(1)}, u32[]{:S(2)}, u32[]{:S(2)}) collective-permute-start(bf16[2,128,256]{2,1,0:T(8,128)(2,1)S(1)} %get-tuple-element.50), channel_id=1, source_target_pairs={{4,0},{8,4},{12,8},{16,12},{20,16},{24,20},{28,24},{5,1},{9,5},{13... | collective-permute-start | bytes 393224 | tf_op jit(solution)/shard_map/ppermute | solution.py:31
  98.0 1.9 %collective-permute-start.7 = (bf16[2,128,256]{2,1,0:T(8,128)(2,1)S(1)}, bf16[2,128,256]{2,1,0:T(8,128)(2,1)S(1)}, u32[]{:S(2)}, u32[]{:S(2)}) collective-permute-start(bf16[2,128,256]{2,1,0:T(8,128)(2,1)S(1)} %get-tuple-element.51), channel_id=1, source_target_pairs={{8,0},{12,4},{16,8},{20,12},{24,16},{28,20},{9,1},{13,5},{17,9},{2... | collective-permute-start | bytes 393224 | tf_op jit(solution)/shard_map/ppermute | solution.py:31
  100.0 3.2 %collective-permute-done.6 = bf16[2,128,256]{2,1,0:T(8,128)(2,1)S(1)} collective-permute-done((bf16[2,128,256]{2,1,0:T(8,128)(2,1)S(1)}, bf16[2,128,256]{2,1,0:T(8,128)(2,1)S(1)}, u32[]{:S(2)}, u32[]{:S(2)}) %collective-permute-start.6) | collective-permute-done | bytes 131104 | tf_op jit(solution)/shard_map/ppermute | solution.py:31
  103.2 1.4 %collective-permute-done.7 = bf16[2,128,256]{2,1,0:T(8,128)(2,1)S(1)} collective-permute-done((bf16[2,128,256]{2,1,0:T(8,128)(2,1)S(1)}, bf16[2,128,256]{2,1,0:T(8,128)(2,1)S(1)}, u32[]{:S(2)}, u32[]{:S(2)}) %collective-permute-start.7) | collective-permute-done | bytes 131104 | tf_op jit(solution)/shard_map/ppermute | solution.py:31
  (35 shorter events, 6.3 us)
Async XLA Ops:
  0.6 0.7 copy-start.7
  1.3 1.2 %copy-start = (bf16[4,32,4096]{2,1,0:T(8,128)(2,1)S(1)}, bf16[4,32,4096]{2,1,0:T(8,128)(2,1)}, u32[]{:S(2)}) copy-start(bf16[4,32,4096]{2,1,0:T(8,128)(2,1)} %query_ref.5) | copy-start | bytes 3145732
  2.5 1.2 %copy-start.2 = (bf16[4,32,4096]{2,1,0:T(8,128)(2,1)S(1)}, bf16[4,32,4096]{2,1,0:T(8,128)(2,1)}, u32[]{:S(2)}) copy-start(bf16[4,32,4096]{2,1,0:T(8,128)(2,1)} %grad_ref.5) | copy-start | bytes 3145732
  3.7 0.9 copy-start.5
  4.6 0.9 copy-start.6
  5.6 57.4 %copy-start.1 = (bf16[4,32,4096]{2,1,0:T(8,128)(2,1)S(1)}, bf16[4,32,4096]{2,1,0:T(8,128)(2,1)}, u32[]{:S(2)}) copy-start(bf16[4,32,4096]{2,1,0:T(8,128)(2,1)} %query_ref.5) | copy-start | bytes 3145732
  5.6 57.4 %copy-start.3 = (bf16[4,32,4096]{2,1,0:T(8,128)(2,1)S(1)}, bf16[4,32,4096]{2,1,0:T(8,128)(2,1)}, u32[]{:S(2)}) copy-start(bf16[4,32,4096]{2,1,0:T(8,128)(2,1)} %grad_ref.5) | copy-start | bytes 3145732
  7.8 0.8 copy-start.8
  8.6 0.8 copy-start.9
  9.4 0.7 copy-start.10
  10.1 0.7 copy-start.11
  10.8 52.1 %copy-start.4 = (s32[4,1024]{1,0:T(4,128)S(1)}, s32[4,1024]{1,0:T(4,128)}, u32[]{:S(2)}) copy-start(s32[4,1024]{1,0:T(4,128)} %segment_ref.15) | copy-start | bytes 49156
  10.8 11.0 %all-to-all-start = ((bf16[4,2,32,512]{3,2,1,0:T(8,128)(2,1)}), bf16[4,2,32,512]{3,2,1,0:T(8,128)(2,1)S(1)}, u32[]{:S(2)}, u32[]{:S(2)}) async-start(bf16[4,2,32,512]{3,2,1,0:T(8,128)(2,1)} %get-tuple-element.32), calls=%async_computation | async-start | bytes 524288 | tf_op jit(solution)/shard_map/all_to_all | solution.py:280
  15.7 53.4 %collective-permute-start.5 = (bf16[2,32,4096]{2,1,0:T(8,128)(2,1)}, bf16[2,32,4096]{2,1,0:T(8,128)(2,1)S(1)}, u32[]{:S(2)}, u32[]{:S(2)}) collective-permute-start(bf16[2,32,4096]{2,1,0:T(8,128)(2,1)} %copy-done.9), channel_id=1, source_target_pairs={{0,1},{1,0},{2,3},{3,2},{4,5},{5,4},{6,7},{7,6},{8,9},{9,8},{10,11... | collective-permute-start | bytes 1572872 | tf_op jit(solution)/shard_map/ppermute | solution.py:25
  15.7 63.9 %collective-permute-start.4 = (bf16[2,32,4096]{2,1,0:T(8,128)(2,1)}, bf16[2,32,4096]{2,1,0:T(8,128)(2,1)S(1)}, u32[]{:S(2)}, u32[]{:S(2)}) collective-permute-start(bf16[2,32,4096]{2,1,0:T(8,128)(2,1)} %copy-done.8), channel_id=1, source_target_pairs={{0,2},{1,3},{2,0},{3,1},{4,6},{5,7},{6,4},{7,5},{8,10},{9,11},{10,... | collective-permute-start | bytes 1572872 | tf_op jit(solution)/shard_map/ppermute | solution.py:25
  18.1 44.3 %collective-permute-start = (bf16[2,32,2048]{2,1,0:T(8,128)(2,1)}, bf16[2,32,2048]{2,1,0:T(8,128)(2,1)}, u32[]{:S(2)}, u32[]{:S(2)}) collective-permute-start(bf16[2,32,2048]{2,1,0:T(8,128)(2,1)} %copy-done.11), channel_id=1, source_target_pairs={{0,3},{1,2},{2,1},{3,0},{4,7},{5,6},{6,5},{7,4},{8,11},{9,10},{10,... | collective-permute-start | bytes 786440 | tf_op jit(solution)/shard_map/ppermute | solution.py:25
  21.8 41.1 %collective-permute-start.3 = (bf16[4,2,32,512]{3,2,1,0:T(8,128)(2,1)S(1)}, bf16[4,2,32,512]{3,2,1,0:T(8,128)(2,1)S(1)}, u32[]{:S(2)}, u32[]{:S(2)}) collective-permute-start(bf16[4,2,32,512]{3,2,1,0:T(8,128)(2,1)S(1)} %all-to-all-done.refs_0_), channel_id=1, source_target_pairs={{0,8},{4,12},{8,16},{12,20},{16,24},{20,28},{1,9},{5,13},{9,17},{1... | collective-permute-start | bytes 786440 | tf_op jit(solution)/shard_map/ppermute | solution.py:31
  28.4 34.5 %collective-permute-start.2 = (bf16[4,2,32,512]{3,2,1,0:T(8,128)(2,1)S(1)}, bf16[4,2,32,512]{3,2,1,0:T(8,128)(2,1)S(1)}, u32[]{:S(2)}, u32[]{:S(2)}) collective-permute-start(bf16[4,2,32,512]{3,2,1,0:T(8,128)(2,1)S(1)} %all-to-all-done.refs_0_), channel_id=1, source_target_pairs={{0,4},{4,8},{8,12},{12,16},{16,20},{20,24},{24,28},{1,5},{5,9},{9,... | collective-permute-start | bytes 786440 | tf_op jit(solution)/shard_map/ppermute | solution.py:31
  62.4 23.8 %collective-permute-start.1 = (bf16[2,32,2048]{2,1,0:T(8,128)(2,1)}, bf16[2,32,2048]{2,1,0:T(8,128)(2,1)S(1)}, u32[]{:S(2)}, u32[]{:S(2)}) collective-permute-start(bf16[2,32,2048]{2,1,0:T(8,128)(2,1)} %copy-done.10), channel_id=1, source_target_pairs={{0,3},{1,2},{2,1},{3,0},{4,7},{5,6},{6,5},{7,4},{8,11},{9,10},{10,... | collective-permute-start | bytes 786440 | tf_op jit(solution)/shard_map/ppermute | solution.py:25
  89.5 10.5 %collective-permute-start.8 = (bf16[2,128,256]{2,1,0:T(8,128)(2,1)S(1)}, bf16[2,128,256]{2,1,0:T(8,128)(2,1)S(1)}, u32[]{:S(2)}, u32[]{:S(2)}) collective-permute-start(bf16[2,128,256]{2,1,0:T(8,128)(2,1)S(1)} %get-tuple-element.53), channel_id=1, source_target_pairs={{4,0},{8,4},{12,8},{16,12},{20,16},{24,20},{28,24},{5,1},{9,5},{13... | collective-permute-start | bytes 393224 | tf_op jit(solution)/shard_map/ppermute | solution.py:31
  91.7 8.3 %collective-permute-start.9 = (bf16[2,128,256]{2,1,0:T(8,128)(2,1)S(1)}, bf16[2,128,256]{2,1,0:T(8,128)(2,1)S(1)}, u32[]{:S(2)}, u32[]{:S(2)}) collective-permute-start(bf16[2,128,256]{2,1,0:T(8,128)(2,1)S(1)} %get-tuple-element.54), channel_id=1, source_target_pairs={{8,0},{12,4},{16,8},{20,12},{24,16},{28,20},{9,1},{13,5},{17,9},{2... | collective-permute-start | bytes 393224 | tf_op jit(solution)/shard_map/ppermute | solution.py:31
  95.3 8.0 %collective-permute-start.6 = (bf16[2,128,256]{2,1,0:T(8,128)(2,1)S(1)}, bf16[2,128,256]{2,1,0:T(8,128)(2,1)S(1)}, u32[]{:S(2)}, u32[]{:S(2)}) collective-permute-start(bf16[2,128,256]{2,1,0:T(8,128)(2,1)S(1)} %get-tuple-element.50), channel_id=1, source_target_pairs={{4,0},{8,4},{12,8},{16,12},{20,16},{24,20},{28,24},{5,1},{9,5},{13... | collective-permute-start | bytes 393224 | tf_op jit(solution)/shard_map/ppermute | solution.py:31
  98.0 6.6 %collective-permute-start.7 = (bf16[2,128,256]{2,1,0:T(8,128)(2,1)S(1)}, bf16[2,128,256]{2,1,0:T(8,128)(2,1)S(1)}, u32[]{:S(2)}, u32[]{:S(2)}) collective-permute-start(bf16[2,128,256]{2,1,0:T(8,128)(2,1)S(1)} %get-tuple-element.51), channel_id=1, source_target_pairs={{8,0},{12,4},{16,8},{20,12},{24,16},{28,20},{9,1},{13,5},{17,9},{2... | collective-permute-start | bytes 393224 | tf_op jit(solution)/shard_map/ppermute | solution.py:31

commit v3 on v2

--- a/solution.py
+++ b/solution.py
@@ -14,15 +14,17 @@
 HEADS_STEP = 2
 
 
-def partner(index, step, count):
-    if count & (count - 1) == 0:
-        return index ^ step, index ^ step
-    return (index + step) % count, (index + count - step) % count
+def target_of(index, step, count):
+    return lax.rem(index + step, count)
+
+
+def source_of(index, step, count):
+    return lax.rem(index + count - step, count)
 
 
 def exchanged(value, axis, step):
     count = lax.axis_size(axis)
-    return lax.ppermute(value, axis, [(i, partner(i, step, count)[0]) for i in range(count)])
+    return lax.ppermute(value, axis, [(i, (i + step) % count) for i in range(count)])
 
 
 def shifted(value, axis, by):
@@ -48,7 +50,7 @@
         for which, source in enumerate((key_ref, value_ref)):
             hop(source.at[chosen], kv_held_ref.at[other, which], kv_out_ref.at[other, which])
     for (step, start, width), out_ref, held_ref in zip(parts, row_out_refs, row_held_refs):
-        chosen = assign_ref[partner(group, step, count)[0]]
+        chosen = assign_ref[target_of(group, step, count)]
         for which, source in enumerate((query_ref, grad_ref)):
             hop(
                 source.at[chosen, :, start : start + width], held_ref.at[which], out_ref.at[which]
@@ -67,12 +69,12 @@
     kv_shape = (count, 2, rows, keys.shape[2])
     shapes = [kv_shape] + [(2, rows, width) for _, _, width in parts]
     copies = 2 * count + 2 * len(parts)
-    anywhere, scalars = pl.BlockSpec(memory_space=pl.ANY), pl.BlockSpec(memory_space=pltpu.SMEM)
+    far, scalars = pl.BlockSpec(memory_space=pltpu.HBM), pl.BlockSpec(memory_space=pltpu.SMEM)
     return pl.pallas_call(
         functools.partial(stage_kernel, count, parts),
         out_shape=[jax.ShapeDtypeStruct(shape, queries.dtype) for shape in shapes],
-        in_specs=[scalars] * 2 + [anywhere] * 4,
-        out_specs=[anywhere] * len(shapes),
+        in_specs=[scalars] * 2 + [far] * 4,
+        out_specs=[far] * len(shapes),
         scratch_shapes=[pltpu.VMEM(shape, queries.dtype) for shape in shapes]
         + [pltpu.SemaphoreType.DMA((copies,))] * 2,
         compiler_params=pltpu.CompilerParams(vmem_limit_bytes=VMEM_BYTES),
@@ -130,11 +132,12 @@
     tok_dev = count * rows
     scale = 1.0 / HD**0.5
     head = pl.program_id(0)
+    slot = lax.rem(head, HEADS_STEP)
 
     @pl.when(head == 0)
     def _():
         group = meta_ref[0]
-        source = partner(group, step, count)[1]
+        source = source_of(group, step, count)
         build_bias(
             source, assign_ref[group], meta_ref[1], segment_ref, bias_ref, rows, tok_dev, ratio
         )
@@ -162,7 +165,7 @@
     grad_query = lax.dot_general(
         grad_scores, key, (((0,), (0,)), ((), ())), preferred_element_type=jnp.float32
     )
-    held_ref[head] = (grad_query * scale).reshape(ratio, rows, HD)
+    held_ref[slot] = (grad_query * scale).reshape(ratio, rows, HD)
     if not first:
         grad_key = grad_key + acc_in_ref[0]
         grad_value = grad_value + acc_in_ref[1]
@@ -178,38 +181,35 @@
         acc_out_ref[0] = grad_key
         acc_out_ref[1] = grad_value
 
-    @pl.when(head == HEADS_STEP - 1)
+    @pl.when(slot == HEADS_STEP - 1)
     def _():
         held = held_ref[...].reshape(HEADS_STEP * ratio, rows, HD)
         query_out_ref[...] = jnp.swapaxes(held, 0, 1).astype(jnp.bfloat16)
 
 
-def attend(step, half, lanes_from, heads, meta, assignment, segments, query, grad, kv_pieces, acc, full, last):
+def attend(step, base, span, heads, meta, assignment, segments, query, grad, kv_pieces, acc, full, last):
     first, filled = acc is None, full is not None
     rows, (count, _, _, kv_width) = query[0].shape[1], kv_pieces[0].shape
     pieces = len(kv_pieces)
     ratio = heads // (kv_width // HD)
     tok_dev = count * rows
     keys = pieces * tok_dev
-    step_lanes = HEADS_STEP * HD
-    base = half * HEADS_STEP
-
-    def rows_spec(pick):
-        return pl.BlockSpec(
-            (None, rows, ratio * HD), lambda c, m, a: (pick(m, a), 0, lanes_from + c)
-        )
-
-    acc_spec = pl.BlockSpec((2, keys, HD), lambda c, m, a: (0, 0, c))
+
+    def rows_spec(array, pick):
+        start = base if array.shape[2] == heads * HD else 0
+        return pl.BlockSpec((None, rows, ratio * HD), lambda c, m, a: (pick(m, a), 0, start + c))
+
     in_specs = [
         pl.BlockSpec(segments.shape, lambda c, m, a: (0, 0)),
-        rows_spec(query[1]),
-        rows_spec(grad[1]),
+        rows_spec(*query),
+        rows_spec(*grad),
     ]
     in_specs += [
         pl.BlockSpec((count, 2, rows, HD), lambda c, m, a: (0, 0, 0, base + c)) for _ in kv_pieces
     ]
     operands = [meta, assignment, segments, query[0], grad[0], *kv_pieces]
     aliases = {}
+    acc_spec = pl.BlockSpec((2, keys, HD), lambda c, m, a: (0, 0, base + c))
     if not first:
         if not last:
             aliases[len(operands)] = 1
@@ -223,24 +223,24 @@
     out_specs = [
         pl.BlockSpec(
             (rows, HEADS_STEP * ratio, HD),
-            lambda c, m, a: (partner(m[0], step, count)[1], half, 0),
+            lambda c, m, a: (source_of(m[0], step, count), (base + c) // HEADS_STEP, 0),
         )
     ]
     if last:
         span_spec = pl.BlockSpec((2, tok_dev, HD), lambda c, m, a: (0, 0, c))
-        out_shape.append(jax.ShapeDtypeStruct((2, tok_dev, step_lanes), jnp.float32))
-        out_shape += [jax.ShapeDtypeStruct((2, tok_dev, step_lanes), jnp.bfloat16)] * (pieces - 1)
+        out_shape.append(jax.ShapeDtypeStruct((2, tok_dev, span * HD), jnp.float32))
+        out_shape += [jax.ShapeDtypeStruct((2, tok_dev, span * HD), jnp.bfloat16)] * (pieces - 1)
         out_specs += [span_spec] * pieces
     else:
-        out_shape.append(jax.ShapeDtypeStruct((2, keys, step_lanes), jnp.float32))
+        out_shape.append(jax.ShapeDtypeStruct((2, keys, kv_width), jnp.float32))
         out_specs.append(acc_spec)
-    pairs = HEADS_STEP * ratio * rows * keys
+    pairs = span * ratio * rows * keys
     return pl.pallas_call(
         functools.partial(attend_kernel, step, first, filled, last, pieces, ratio),
         out_shape=out_shape,
         grid_spec=pltpu.PrefetchScalarGridSpec(
             num_scalar_prefetch=2,
-            grid=(HEADS_STEP,),
+            grid=(span,),
             in_specs=in_specs,
             out_specs=out_specs,
             scratch_shapes=[
@@ -253,7 +253,7 @@
             dimension_semantics=("arbitrary",), vmem_limit_bytes=VMEM_BYTES
         ),
         cost_estimate=pl.CostEstimate(
-            flops=10 * pairs * HD, bytes_accessed=8 * keys * step_lanes, transcendentals=pairs
+            flops=100 * pairs * HD, bytes_accessed=8 * keys * span * HD, transcendentals=pairs
         ),
         name="attend",
     )(*operands)
@@ -278,54 +278,27 @@
     parts += [(final, half * part, part) for half in range(halves)]
     kv_out, *staged = stage(meta, assignment, queries, grad_out, keys, values, parts)
     kv_own = lax.all_to_all(kv_out, "dp", split_axis=0, concat_axis=0, tiled=True)
-    whole = {step: exchanged(staged[step - 1], "dp", step) for step in range(final - 1, 0, -1)}
-    split = [exchanged(staged[final - 1], "dp", final)]
-    for half in range(1, halves):
-        after, _ = lax.optimization_barrier((staged[final - 1 + half], split[-1]))
-        split.append(exchanged(after, "dp", final))
+    arrived = [exchanged(rows, "dp", step) for rows, (step, _, _) in zip(staged, parts)]
     pieces = [kv_own]
     for back in range(1, hops + 1):
         pieces.append(shifted(kv_own, ("blk", "uly"), back))
 
-    accs, full, own, halos = [None] * halves, None, [None] * halves, [None] * halves
-
-    def visit(step, half, last):
-        nonlocal full
-        kv_step = HEADS_STEP * half
-        if step == 0:
-            query = (queries, lambda m, a: a[m[0]])
-            grad = (grad_out, lambda m, a: a[m[0]])
-        else:
-            both = split[half] if step == final else whole[step]
-            query, grad = (both, lambda m, a: 0), (both, lambda m, a: 1)
-            if step == final:
-                kv_step = 0
-        full, *rest = attend(
-            step, half, kv_step, heads, meta, assignment, segment_ids, query, grad, pieces,
-            accs[half], full, last,
+    fixed = (heads, meta, assignment, segment_ids)
+    query, grad = (queries, lambda m, a: a[m[0]]), (grad_out, lambda m, a: a[m[0]])
+    full, acc = attend(0, 0, kv_heads, *fixed, query, grad, pieces, None, None, False)
+    for both, (step, _, _) in zip(arrived[:-halves], parts):
+        query, grad = (both, lambda m, a: 0), (both, lambda m, a: 1)
+        full, acc = attend(step, 0, kv_heads, *fixed, query, grad, pieces, acc, full, False)
+    totals = []
+    for half, both in enumerate(arrived[-halves:]):
+        query, grad = (both, lambda m, a: 0), (both, lambda m, a: 1)
+        base = half * HEADS_STEP
+        full, own, *halos = attend(
+            final, base, HEADS_STEP, *fixed, query, grad, pieces, acc, full, True
         )
-        if last:
-            own[half], halos[half] = rest[0], rest[1:]
-        else:
-            accs[half] = rest[0]
-
-    for step in range(final - 1):
-        for half in range(halves):
-            visit(step, half, False)
-    for half in range(halves - 1):
-        visit(final, half, False)
-        visit(final - 1, half, True)
-    visit(final - 1, halves - 1, False)
-    visit(final, halves - 1, True)
-
-    totals = []
-    for half in range(halves):
-        total = own[half]
-        for back in range(1, hops + 1):
-            total = total + shifted(halos[half][back - 1], ("blk", "uly"), -back).astype(
-                jnp.float32
-            )
-        totals.append(total.astype(jnp.bfloat16))
+        for back, halo in enumerate(halos, 1):
+            own = own + shifted(halo, ("blk", "uly"), -back).astype(jnp.float32)
+        totals.append(own.astype(jnp.bfloat16))
     total = jnp.concatenate(totals, axis=2)
     return full[None], total[0][None], total[1][None]
 

time: 106 us -> 103 us (0.972)
  the two profiles are of different devices: /device:TPU:11 before, /device:TPU:1 now
where the time goes in v3:
time: 103 us
  waiting for transfers between devices  37.1 us (36%)
  Pallas kernels  25.4 us (25%)
  starting transfers between devices  21.4 us (21%)
  blocking collectives  12.1 us (12%)
  local copies, waits for them, and re-layouts  4.92 us (5%)
    ppermute x4, waiting for transfers between devices, exchanged(): lax.ppermute(value, axis, [(i, (i + step) % count) for i in range(count)])  29.3 us
    pallas_call x5, Pallas kernels, attend(): pl.pallas_call(functools.partial(attend_kernel, step, first, filled, last...  22.9 us
    ppermute x6, starting transfers between devices, shifted(): return lax.ppermute(value, axis, pairs)  18.1 us
    all_to_all x1, blocking collectives, shards(): lax.all_to_all(kv_out, 'dp', split_axis=0, concat_axis=0, tiled=True)  12.1 us
    ppermute x6, waiting for transfers between devices, shifted(): return lax.ppermute(value, axis, pairs)  7.85 us
    unnamed x12, local copies, waits for them, and re-layouts  4.92 us
    ppermute x4, starting transfers between devices, exchanged(): lax.ppermute(value, axis, [(i, (i + step) % count) for i in range(count)])  3.34 us
    pallas_call x1, Pallas kernels, stage(): pl.pallas_call(functools.partial(stage_kernel, count, parts), out_shape=[...  2.55 us
  transfers between devices with their start and end apart: 10, of which 6 were waited for; matrix products, arithmetic and copies ran while one was open for 0% of the time, Pallas kernels for 19%

profile of v3, /device:TPU:1, one launch (start us, length us, event | category | flops | bytes accessed | tf_op | source)
XLA Modules:
  0.0 102.6 jit_solution(12869687801666095511)
XLA Ops:
  0.7 1.2 %copy-done = bf16[4,32,4096]{2,1,0:T(8,128)(2,1)S(1)} copy-done((bf16[4,32,4096]{2,1,0:T(8,128)(2,1)S(1)}, bf16[4,32,4096]{2,1,0:T(8,128)(2,1)}, u32[]{:S(2)}) %copy-start) | copy-done | bytes 1048600
  2.0 1.2 %copy-done.1 = bf16[4,32,4096]{2,1,0:T(8,128)(2,1)S(1)} copy-done((bf16[4,32,4096]{2,1,0:T(8,128)(2,1)S(1)}, bf16[4,32,4096]{2,1,0:T(8,128)(2,1)}, u32[]{:S(2)}) %copy-start.1) | copy-done | bytes 1048600
  3.2 0.9 copy-done.2
  4.1 0.9 copy-done.3
  5.6 2.6 %stage.1 = (bf16[4,2,32,512]{3,2,1,0:T(8,128)(2,1)S(1)}, bf16[2,32,4096]{2,1,0:T(8,128)(2,1)S(1)}, bf16[2,32,4096]{2,1,0:T(8,128)(2,1)S(1)}, bf16[2,32,2048]{2,1,0:T(8,128)(2,1)S(1)}, bf16[2,32,2048]{2,1,0:T(8,128)(2,1)S(1)}) custom-call(s32[2]{0:T(128)S(1)} %pad_add_fusion.meta_ref, s32[4]{0:T(128)S(1)} %copy-done.4, bf16[4,32,4096]{2,1,0:T(8,128)(2,1)S(1)} %copy-done, ...), custom_call_target="tpu_custom_call" | custom-call | tf_op jit(solution)/shard_map/stage/pallas_call | solution.py:73
  8.2 12.1 %all_to_all.5.refs_0_ = bf16[4,2,32,512]{3,2,1,0:T(8,128)(2,1)S(1)} all-to-all(bf16[4,2,32,512]{3,2,1,0:T(8,128)(2,1)S(1)} %get-tuple-element.23), channel_id=1, replica_groups=mesh['blk'=4,'uly'=2,'dp'=4] {'dp'}, dimensions={0} | all-to-all | bytes 524288 | tf_op jit(solution)/shard_map/all_to_all | solution.py:280
  20.3 6.0 %collective-permute-start.2 = (bf16[4,2,32,512]{3,2,1,0:T(8,128)(2,1)S(1)}, bf16[4,2,32,512]{3,2,1,0:T(8,128)(2,1)S(1)}, u32[]{:S(2)}, u32[]{:S(2)}) collective-permute-start(bf16[4,2,32,512]{3,2,1,0:T(8,128)(2,1)S(1)} %all_to_all.5.refs_0_), channel_id=1, source_target_pairs={{0,8},{4,12},{8,16},{12,20},{16,24},{20,28},{1,9},{5,13},{9,17},{1... | collective-permute-start | bytes 786440 | tf_op jit(solution)/shard_map/ppermute | solution.py:33
  26.3 3.1 %collective-permute-start.1 = (bf16[4,2,32,512]{3,2,1,0:T(8,128)(2,1)S(1)}, bf16[4,2,32,512]{3,2,1,0:T(8,128)(2,1)S(1)}, u32[]{:S(2)}, u32[]{:S(2)}) collective-permute-start(bf16[4,2,32,512]{3,2,1,0:T(8,128)(2,1)S(1)} %all_to_all.5.refs_0_), channel_id=1, source_target_pairs={{0,4},{4,8},{8,12},{12,16},{16,20},{20,24},{24,28},{1,5},{5,9},{9,... | collective-permute-start | bytes 786440 | tf_op jit(solution)/shard_map/ppermute | solution.py:33
  29.5 3.3 %collective-permute-start = (bf16[2,32,2048]{2,1,0:T(8,128)(2,1)S(1)}, bf16[2,32,2048]{2,1,0:T(8,128)(2,1)S(1)}, u32[]{:S(2)}, u32[]{:S(2)}) collective-permute-start(bf16[2,32,2048]{2,1,0:T(8,128)(2,1)S(1)} %get-tuple-element.22), channel_id=1, source_target_pairs={{0,3},{1,0},{2,1},{3,2},{4,7},{5,4},{6,5},{7,6},{8,11},{9,8},{10,9... | collective-permute-start | bytes 786440 | tf_op jit(solution)/shard_map/ppermute | solution.py:27
  32.8 3.5 %collective-permute-done.1.refs_1_ = bf16[4,2,32,512]{3,2,1,0:T(8,128)(2,1)S(1)} collective-permute-done((bf16[4,2,32,512]{3,2,1,0:T(8,128)(2,1)S(1)}, bf16[4,2,32,512]{3,2,1,0:T(8,128)(2,1)S(1)}, u32[]{:S(2)}, u32[]{:S(2)}) %collective-permute-start.1) | collective-permute-done | bytes 262176 | tf_op jit(solution)/shard_map/ppermute | solution.py:33
  36.3 5.0 %attend.5 = (bf16[128,32,128]{2,1,0:T(8,128)(2,1)}, f32[2,384,512]{2,1,0:T(8,128)S(1)}) custom-call(s32[2]{0:T(128)S(1)} %pad_add_fusion.meta_ref, s32[4]{0:T(128)S(1)} %copy-done.4, s32[4,1024]{1,0:T(4,128)S(1)} %copy-done.5, bf16[4,32,4096]{2,1,0:T(8,128)(2,1)S(1)} %copy-done, bf16[4,32,4096]{2,1,0:T(8,128)(2,1)S(1)} %copy-done.1, ...), custom_call_target="tpu_custom_call" | custom-call | flops 5033164800 | bytes 1572864 | tf_op jit(solution)/shard_map/attend/pallas_call | solution.py:238
  41.3 3.6 %collective-permute-done.4.query_ref.grad_ref = bf16[2,32,4096]{2,1,0:T(8,128)(2,1)S(1)} collective-permute-done((bf16[2,32,4096]{2,1,0:T(8,128)(2,1)S(1)}, bf16[2,32,4096]{2,1,0:T(8,128)(2,1)S(1)}, u32[]{:S(2)}, u32[]{:S(2)}) %collective-permute-start.4) | collective-permute-done | bytes 524320 | tf_op jit(solution)/shard_map/ppermute | solution.py:27
  44.9 5.5 %attend.6 = (bf16[128,32,128]{2,1,0:T(8,128)(2,1)}, f32[2,384,512]{2,1,0:T(8,128)S(1)}) custom-call(s32[2]{0:T(128)S(1)} %pad_add_fusion.meta_ref, s32[4]{0:T(128)S(1)} %copy-done.4, s32[4,1024]{1,0:T(4,128)S(1)} %copy-done.5, bf16[2,32,4096]{2,1,0:T(8,128)(2,1)S(1)} %collective-permute-done.4.query_ref.grad_ref, ...), custom_call_target="tpu_custom_call", output_to_operand_aliasing={{1}: (8, {}), {0}: (9, {})} | custom-call | flops 5033164800 | bytes 1572864 | tf_op jit(solution)/shard_map/attend/pallas_call | solution.py:238
  50.4 25.6 %collective-permute-done.3.query_ref.grad_ref = bf16[2,32,4096]{2,1,0:T(8,128)(2,1)S(1)} collective-permute-done((bf16[2,32,4096]{2,1,0:T(8,128)(2,1)S(1)}, bf16[2,32,4096]{2,1,0:T(8,128)(2,1)S(1)}, u32[]{:S(2)}, u32[]{:S(2)}) %collective-permute-start.3) | collective-permute-done | bytes 524320 | tf_op jit(solution)/shard_map/ppermute | solution.py:27
  76.0 5.5 %attend.7 = (bf16[128,32,128]{2,1,0:T(8,128)(2,1)}, f32[2,384,512]{2,1,0:T(8,128)S(1)}) custom-call(s32[2]{0:T(128)S(1)} %pad_add_fusion.meta_ref, s32[4]{0:T(128)S(1)} %copy-done.4, s32[4,1024]{1,0:T(4,128)S(1)} %copy-done.5, bf16[2,32,4096]{2,1,0:T(8,128)(2,1)S(1)} %collective-permute-done.3.query_ref.grad_ref, ...), custom_call_target="tpu_custom_call", output_to_operand_aliasing={{1}: (8, {}), {0}: (9, {})} | custom-call | flops 5033164800 | bytes 1572864 | tf_op jit(solution)/shard_map/attend/pallas_call | solution.py:238
  81.5 3.4 %attend.8 = (bf16[128,32,128]{2,1,0:T(8,128)(2,1)}, f32[2,128,256]{2,1,0:T(8,128)S(1)}, bf16[2,128,256]{2,1,0:T(8,128)(2,1)S(1)}, bf16[2,128,256]{2,1,0:T(8,128)(2,1)S(1)}) custom-call(s32[2]{0:T(128)S(1)} %pad_add_fusion.meta_ref, s32[4]{0:T(128)S(1)} %copy-done.4, s32[4,1024]{1,0:T(4,128)S(1)} %copy-done.5, ...), custom_call_target="tpu_custom_call", output_to_operand_aliasing={{0}: (9, {})} | custom-call | flops 2516582400 | bytes 786432 | tf_op jit(solution)/shard_map/attend/pallas_call | solution.py:238
  85.0 3.4 %attend.9 = (bf16[128,32,128]{2,1,0:T(8,128)(2,1)}, f32[2,128,256]{2,1,0:T(8,128)S(1)}, bf16[2,128,256]{2,1,0:T(8,128)(2,1)S(1)}, bf16[2,128,256]{2,1,0:T(8,128)(2,1)S(1)}) custom-call(s32[2]{0:T(128)S(1)} %pad_add_fusion.meta_ref, s32[4]{0:T(128)S(1)} %copy-done.4, s32[4,1024]{1,0:T(4,128)S(1)} %copy-done.5, ...), custom_call_target="tpu_custom_call", output_to_operand_aliasing={{0}: (9, {})} | custom-call | flops 2516582400 | bytes 786432 | tf_op jit(solution)/shard_map/attend/pallas_call | solution.py:238
  88.4 3.2 %collective-permute-start.8 = (bf16[2,128,256]{2,1,0:T(8,128)(2,1)S(1)}, bf16[2,128,256]{2,1,0:T(8,128)(2,1)S(1)}, u32[]{:S(2)}, u32[]{:S(2)}) collective-permute-start(bf16[2,128,256]{2,1,0:T(8,128)(2,1)S(1)} %get-tuple-element.39), channel_id=1, source_target_pairs={{4,0},{8,4},{12,8},{16,12},{20,16},{24,20},{28,24},{5,1},{9,5},{13... | collective-permute-start | bytes 393224 | tf_op jit(solution)/shard_map/ppermute | solution.py:33
  91.6 1.9 %collective-permute-start.9 = (bf16[2,128,256]{2,1,0:T(8,128)(2,1)S(1)}, bf16[2,128,256]{2,1,0:T(8,128)(2,1)S(1)}, u32[]{:S(2)}, u32[]{:S(2)}) collective-permute-start(bf16[2,128,256]{2,1,0:T(8,128)(2,1)S(1)} %get-tuple-element.40), channel_id=1, source_target_pairs={{8,0},{12,4},{16,8},{20,12},{24,16},{28,20},{9,1},{13,5},{17,9},{2... | collective-permute-start | bytes 393224 | tf_op jit(solution)/shard_map/ppermute | solution.py:33
  93.6 1.9 %collective-permute-start.6 = (bf16[2,128,256]{2,1,0:T(8,128)(2,1)S(1)}, bf16[2,128,256]{2,1,0:T(8,128)(2,1)S(1)}, u32[]{:S(2)}, u32[]{:S(2)}) collective-permute-start(bf16[2,128,256]{2,1,0:T(8,128)(2,1)S(1)} %get-tuple-element.36), channel_id=1, source_target_pairs={{4,0},{8,4},{12,8},{16,12},{20,16},{24,20},{28,24},{5,1},{9,5},{13... | collective-permute-start | bytes 393224 | tf_op jit(solution)/shard_map/ppermute | solution.py:33
  95.5 1.9 %collective-permute-start.7 = (bf16[2,128,256]{2,1,0:T(8,128)(2,1)S(1)}, bf16[2,128,256]{2,1,0:T(8,128)(2,1)S(1)}, u32[]{:S(2)}, u32[]{:S(2)}) collective-permute-start(bf16[2,128,256]{2,1,0:T(8,128)(2,1)S(1)} %get-tuple-element.37), channel_id=1, source_target_pairs={{8,0},{12,4},{16,8},{20,12},{24,16},{28,20},{9,1},{13,5},{17,9},{2... | collective-permute-start | bytes 393224 | tf_op jit(solution)/shard_map/ppermute | solution.py:33
  98.1 1.2 %collective-permute-done.6 = bf16[2,128,256]{2,1,0:T(8,128)(2,1)S(1)} collective-permute-done((bf16[2,128,256]{2,1,0:T(8,128)(2,1)S(1)}, bf16[2,128,256]{2,1,0:T(8,128)(2,1)S(1)}, u32[]{:S(2)}, u32[]{:S(2)}) %collective-permute-start.6) | collective-permute-done | bytes 131104 | tf_op jit(solution)/shard_map/ppermute | solution.py:33
  99.3 2.6 %collective-permute-done.7 = bf16[2,128,256]{2,1,0:T(8,128)(2,1)S(1)} collective-permute-done((bf16[2,128,256]{2,1,0:T(8,128)(2,1)S(1)}, bf16[2,128,256]{2,1,0:T(8,128)(2,1)S(1)}, u32[]{:S(2)}, u32[]{:S(2)}) %collective-permute-start.7) | collective-permute-done | bytes 131104 | tf_op jit(solution)/shard_map/ppermute | solution.py:33
  101.9 0.7 pad_maximum_fusion
  (19 shorter events, 1.5 us)
Async XLA Ops:
  0.6 35.6 %copy-start.5 = (s32[4,1024]{1,0:T(4,128)S(1)}, s32[4,1024]{1,0:T(4,128)}, u32[]{:S(2)}) copy-start(s32[4,1024]{1,0:T(4,128)} %segment_ref.9) | copy-start | bytes 49156
  0.7 1.2 %copy-start = (bf16[4,32,4096]{2,1,0:T(8,128)(2,1)S(1)}, bf16[4,32,4096]{2,1,0:T(8,128)(2,1)}, u32[]{:S(2)}) copy-start(bf16[4,32,4096]{2,1,0:T(8,128)(2,1)} %query_ref.3) | copy-start | bytes 3145732
  1.9 1.2 %copy-start.1 = (bf16[4,32,4096]{2,1,0:T(8,128)(2,1)S(1)}, bf16[4,32,4096]{2,1,0:T(8,128)(2,1)}, u32[]{:S(2)}) copy-start(bf16[4,32,4096]{2,1,0:T(8,128)(2,1)} %grad_ref.3) | copy-start | bytes 3145732
  3.2 0.9 copy-start.2
  4.1 0.9 copy-start.3
  5.0 0.7 copy-start.4
  20.3 12.5 %collective-permute-start.2 = (bf16[4,2,32,512]{3,2,1,0:T(8,128)(2,1)S(1)}, bf16[4,2,32,512]{3,2,1,0:T(8,128)(2,1)S(1)}, u32[]{:S(2)}, u32[]{:S(2)}) collective-permute-start(bf16[4,2,32,512]{3,2,1,0:T(8,128)(2,1)S(1)} %all_to_all.5.refs_0_), channel_id=1, source_target_pairs={{0,8},{4,12},{8,16},{12,20},{16,24},{20,28},{1,9},{5,13},{9,17},{1... | collective-permute-start | bytes 786440 | tf_op jit(solution)/shard_map/ppermute | solution.py:33
  26.3 10.0 %collective-permute-start.1 = (bf16[4,2,32,512]{3,2,1,0:T(8,128)(2,1)S(1)}, bf16[4,2,32,512]{3,2,1,0:T(8,128)(2,1)S(1)}, u32[]{:S(2)}, u32[]{:S(2)}) collective-permute-start(bf16[4,2,32,512]{3,2,1,0:T(8,128)(2,1)S(1)} %all_to_all.5.refs_0_), channel_id=1, source_target_pairs={{0,4},{4,8},{8,12},{12,16},{16,20},{20,24},{24,28},{1,5},{5,9},{9,... | collective-permute-start | bytes 786440 | tf_op jit(solution)/shard_map/ppermute | solution.py:33
  29.4 15.5 %collective-permute-start.4 = (bf16[2,32,4096]{2,1,0:T(8,128)(2,1)S(1)}, bf16[2,32,4096]{2,1,0:T(8,128)(2,1)S(1)}, u32[]{:S(2)}, u32[]{:S(2)}) collective-permute-start(bf16[2,32,4096]{2,1,0:T(8,128)(2,1)S(1)} %get-tuple-element.25), channel_id=1, source_target_pairs={{0,1},{1,2},{2,3},{3,0},{4,5},{5,6},{6,7},{7,4},{8,9},{9,10},{10,1... | collective-permute-start | bytes 1572872 | tf_op jit(solution)/shard_map/ppermute | solution.py:27
  29.5 55.5 %collective-permute-start = (bf16[2,32,2048]{2,1,0:T(8,128)(2,1)S(1)}, bf16[2,32,2048]{2,1,0:T(8,128)(2,1)S(1)}, u32[]{:S(2)}, u32[]{:S(2)}) collective-permute-start(bf16[2,32,2048]{2,1,0:T(8,128)(2,1)S(1)} %get-tuple-element.22), channel_id=1, source_target_pairs={{0,3},{1,0},{2,1},{3,2},{4,7},{5,4},{6,5},{7,6},{8,11},{9,8},{10,9... | collective-permute-start | bytes 786440 | tf_op jit(solution)/shard_map/ppermute | solution.py:27
  32.7 48.8 %collective-permute-start.5 = (bf16[2,32,2048]{2,1,0:T(8,128)(2,1)S(1)}, bf16[2,32,2048]{2,1,0:T(8,128)(2,1)S(1)}, u32[]{:S(2)}, u32[]{:S(2)}) collective-permute-start(bf16[2,32,2048]{2,1,0:T(8,128)(2,1)S(1)} %get-tuple-element.31), channel_id=1, source_target_pairs={{0,3},{1,0},{2,1},{3,2},{4,7},{5,4},{6,5},{7,6},{8,11},{9,8},{10,9... | collective-permute-start | bytes 786440 | tf_op jit(solution)/shard_map/ppermute | solution.py:27
  32.8 43.3 %collective-permute-start.3 = (bf16[2,32,4096]{2,1,0:T(8,128)(2,1)S(1)}, bf16[2,32,4096]{2,1,0:T(8,128)(2,1)S(1)}, u32[]{:S(2)}, u32[]{:S(2)}) collective-permute-start(bf16[2,32,4096]{2,1,0:T(8,128)(2,1)S(1)} %get-tuple-element.24), channel_id=1, source_target_pairs={{0,2},{1,3},{2,0},{3,1},{4,6},{5,7},{6,4},{7,5},{8,10},{9,11},{10,... | collective-permute-start | bytes 1572872 | tf_op jit(solution)/shard_map/ppermute | solution.py:27
  88.4 9.0 %collective-permute-start.8 = (bf16[2,128,256]{2,1,0:T(8,128)(2,1)S(1)}, bf16[2,128,256]{2,1,0:T(8,128)(2,1)S(1)}, u32[]{:S(2)}, u32[]{:S(2)}) collective-permute-start(bf16[2,128,256]{2,1,0:T(8,128)(2,1)S(1)} %get-tuple-element.39), channel_id=1, source_target_pairs={{4,0},{8,4},{12,8},{16,12},{20,16},{24,20},{28,24},{5,1},{9,5},{13... | collective-permute-start | bytes 393224 | tf_op jit(solution)/shard_map/ppermute | solution.py:33
  91.6 6.4 %collective-permute-start.9 = (bf16[2,128,256]{2,1,0:T(8,128)(2,1)S(1)}, bf16[2,128,256]{2,1,0:T(8,128)(2,1)S(1)}, u32[]{:S(2)}, u32[]{:S(2)}) collective-permute-start(bf16[2,128,256]{2,1,0:T(8,128)(2,1)S(1)} %get-tuple-element.40), channel_id=1, source_target_pairs={{8,0},{12,4},{16,8},{20,12},{24,16},{28,20},{9,1},{13,5},{17,9},{2... | collective-permute-start | bytes 393224 | tf_op jit(solution)/shard_map/ppermute | solution.py:33
  93.6 5.7 %collective-permute-start.6 = (bf16[2,128,256]{2,1,0:T(8,128)(2,1)S(1)}, bf16[2,128,256]{2,1,0:T(8,128)(2,1)S(1)}, u32[]{:S(2)}, u32[]{:S(2)}) collective-permute-start(bf16[2,128,256]{2,1,0:T(8,128)(2,1)S(1)} %get-tuple-element.36), channel_id=1, source_target_pairs={{4,0},{8,4},{12,8},{16,12},{20,16},{24,20},{28,24},{5,1},{9,5},{13... | collective-permute-start | bytes 393224 | tf_op jit(solution)/shard_map/ppermute | solution.py:33
  95.5 6.3 %collective-permute-start.7 = (bf16[2,128,256]{2,1,0:T(8,128)(2,1)S(1)}, bf16[2,128,256]{2,1,0:T(8,128)(2,1)S(1)}, u32[]{:S(2)}, u32[]{:S(2)}) collective-permute-start(bf16[2,128,256]{2,1,0:T(8,128)(2,1)S(1)} %get-tuple-element.37), channel_id=1, source_target_pairs={{8,0},{12,4},{16,8},{20,12},{24,16},{28,20},{9,1},{13,5},{17,9},{2... | collective-permute-start | bytes 393224 | tf_op jit(solution)/shard_map/ppermute | solution.py:33

commit v4 on v3

v4 whole, which is shorter than its diff:
```python
import functools

import jax
import jax.numpy as jnp
from jax import lax
from jax.experimental import pallas as pl
from jax.experimental.pallas import tpu as pltpu
from jax.sharding import PartitionSpec as P

HD = 128
LOG2E = 1.4426950408889634
BIG_NEGATIVE = -1e30
VMEM_BYTES = 32 * 1024 * 1024
HEADS_STEP = 2


def target_of(index, step, count):
    return lax.rem(index + step, count)


def source_of(index, step, count):
    return lax.rem(index + count - step, count)


def exchanged(value, axis, step):
    count = lax.axis_size(axis)
    return lax.ppermute(value, axis, [(i, (i + step) % count) for i in range(count)])


def shifted(value, axis, by):
    length = lax.axis_size(axis)
    pairs = [(i, i + by) for i in range(length) if 0 <= i + by < length]
    return lax.ppermute(value, axis, pairs)


def stage_kernel(count, parts, copies, meta_ref, assign_ref, *refs):
    group = meta_ref[0]
    sources = refs[:2]
    out_refs, held_refs = refs[-2 - 2 * len(parts) : -2 - len(parts)], refs[-2 - len(parts) : -2]
    in_sems, out_sems = refs[-2:]
    loads, stores = [], []
    for (step, start, width), out_ref, held_ref in zip(parts, out_refs, held_refs):
        chosen = assign_ref[target_of(group, step, count)]
        for which, source in enumerate(sources):
            slot = len(loads)
            loads.append(
                pltpu.make_async_copy(
                    source.at[chosen, :, start : start + width],
                    held_ref.at[which],
                    in_sems.at[slot],
                )
            )
            stores.append(
                pltpu.make_async_copy(held_ref.at[which], out_ref.at[which], out_sems.at[slot])
            )
    for load in loads:
        load.start()
    for load, store in zip(loads, stores):
        load.wait()
        store.start()
    for store in stores:
        store.wait()


def stage_kv_kernel(assign_ref, key_ref, value_ref, out_ref, held_ref, in_sems, out_sems):
    loads, stores = [], []
    for group in range(out_ref.shape[0]):
        chosen = assign_ref[group]
        for which, source in enumerate((key_ref, value_ref)):
            slot = len(loads)
            held = held_ref.at[group, which]
            loads.append(pltpu.make_async_copy(source.at[chosen], held, in_sems.at[slot]))
            stores.append(
                pltpu.make_async_copy(held, out_ref.at[group, which], out_sems.at[slot])
            )
    for load in loads:
        load.start()
    for load, store in zip(loads, stores):
        load.wait()
        store.start()
    for store in stores:
        store.wait()


def stage_kv(assignment, keys, values):
    count, rows, width = keys.shape
    shape = (count, 2, rows, width)
    far = pl.BlockSpec(memory_space=pltpu.HBM)
    return pl.pallas_call(
        stage_kv_kernel,
        out_shape=jax.ShapeDtypeStruct(shape, keys.dtype),
        in_specs=[pl.BlockSpec(memory_space=pltpu.SMEM), far, far],
        out_specs=far,
        scratch_shapes=[pltpu.VMEM(shape, keys.dtype)]
        + [pltpu.SemaphoreType.DMA((2 * count,))] * 2,
        name="stage_kv",
    )(assignment, keys, values)


def stage(meta, assignment, first, second, parts, after=()):
    count, rows, _ = first.shape
    shapes = [(2, rows, width) for _, _, width in parts]
    copies = 2 * len(parts)
    far, scalars = pl.BlockSpec(memory_space=pltpu.HBM), pl.BlockSpec(memory_space=pltpu.SMEM)
    return pl.pallas_call(
        functools.partial(stage_kernel, count, parts, copies),
        out_shape=[jax.ShapeDtypeStruct(shape, first.dtype) for shape in shapes],
        in_specs=[scalars] * 2 + [far] * 2 + [pl.BlockSpec(memory_space=pl.ANY)] * len(after),
        out_specs=[far] * len(shapes),
        scratch_shapes=[pltpu.VMEM(shape, first.dtype) for shape in shapes]
        + [pltpu.SemaphoreType.DMA((copies,))] * 2,
        name="stage",
    )(meta, assignment, first, second, *after)


def build_bias(source, sequence, line, segment_ref, bias_ref, rows, tok_dev, ratio):
    pieces = bias_ref.shape[0] // tok_dev
    lanes = ratio * rows
    eye = lax.broadcasted_iota(jnp.int32, (tok_dev, tok_dev), 0) == lax.broadcasted_iota(
        jnp.int32, (tok_dev, tok_dev), 1
    )
    token = lax.broadcasted_iota(jnp.int32, (tok_dev, lanes), 0)
    place = source * rows + lax.rem(
        lax.broadcasted_iota(jnp.int32, (tok_dev, lanes), 1), jnp.int32(rows)
    )

    def column(back):
        start = pl.multiple_of(jnp.maximum(line - back, 0) * tok_dev, tok_dev)
        every = segment_ref[:, pl.ds(start, tok_dev)].astype(jnp.float32)
        mine = lax.broadcasted_iota(jnp.int32, every.shape, 0) == sequence
        row = jnp.sum(jnp.where(mine, every, 0.0), axis=0, keepdims=True)
        return jnp.sum(jnp.where(eye, row, 0.0), axis=1, keepdims=True)

    own = column(0)
    asked = jnp.sum(jnp.where(token == place, own, 0.0), axis=0, keepdims=True)
    allowed = (own == asked) & (token <= place)
    bias_ref[:tok_dev, :] = jnp.where(allowed, 0.0, BIG_NEGATIVE)
    for back in range(1, pieces):
        held = jnp.where(line >= back, column(back), -1.0)
        bias_ref[back * tok_dev : (back + 1) * tok_dev, :] = jnp.where(
            held == asked, 0.0, BIG_NEGATIVE
        )


def attend_kernel(
    step, first, filled, last, pieces, ratio, meta_ref, assign_ref, segment_ref, query_ref, grad_ref, *refs
):
    refs = list(refs)
    kv_refs = [refs.pop(0) for _ in range(pieces)]
    if not first:
        acc_in_ref = refs.pop(0)
    if filled:
        refs.pop(0)
    query_out_ref = refs.pop(0)
    if last:
        own_ref, halo_refs = refs.pop(0), [refs.pop(0) for _ in range(pieces - 1)]
    else:
        acc_out_ref = refs.pop(0)
    (bias_ref,) = refs

    rows = query_ref.shape[0]
    count = kv_refs[0].shape[0]
    tok_dev = count * rows
    scale = 1.0 / HD**0.5

    group = meta_ref[0]

    @pl.when(pl.program_id(0) == 0)
    def _():
        source = source_of(group, step, count)
        build_bias(
            source, assign_ref[group], meta_ref[1], segment_ref, bias_ref, rows, tok_dev, ratio
        )

    turned = (((1,), (1,)), ((), ()))
    grads = []
    for head in range(HEADS_STEP):
        lanes = slice(head * HD, (head + 1) * HD)

        def stacked(ref):
            start = head * ratio
            return jnp.concatenate(
                [ref[:, r * HD : (r + 1) * HD] for r in range(start, start + ratio)], axis=0
            )

        def window(which):
            return jnp.concatenate(
                [
                    ref[place, which, :, lanes]
                    for ref in kv_refs
                    for place in range(count)
                ],
                axis=0,
            )

        query, grad = stacked(query_ref), stacked(grad_ref)
        key, value = window(0), window(1)
        scores = lax.dot_general(key, query, turned, preferred_element_type=jnp.float32)
        scores = scores * (scale * LOG2E) + bias_ref[...]
        top = jnp.max(scores, axis=0, keepdims=True)
        weights = jnp.exp2(scores - top)
        probs = weights * (1.0 / jnp.sum(weights, axis=0, keepdims=True))
        grad_probs = lax.dot_general(value, grad, turned, preferred_element_type=jnp.float32)
        product = probs * grad_probs
        delta = jnp.sum(product, axis=0, keepdims=True)
        grad_scores = (product - probs * delta).astype(jnp.bfloat16)
        grad_value = jnp.dot(
            probs.astype(jnp.bfloat16), grad, preferred_element_type=jnp.float32
        )
        grad_key = jnp.dot(grad_scores, query, preferred_element_type=jnp.float32)
        grad_query = lax.dot_general(
            grad_scores, key, (((0,), (0,)), ((), ())), preferred_element_type=jnp.float32
        )
        grads.append((grad_query * scale).reshape(ratio, rows, HD))
        if not first:
            grad_key = grad_key + acc_in_ref[0, :, lanes]
            grad_value = grad_value + acc_in_ref[1, :, lanes]
        if last:
            grad_key = grad_key * scale
            own_ref[0, :, lanes] = grad_key[:tok_dev]
            own_ref[1, :, lanes] = grad_value[:tok_dev]
            for back, halo_ref in enumerate(halo_refs, 1):
                span = slice(back * tok_dev, (back + 1) * tok_dev)
                halo_ref[0, :, lanes] = grad_key[span].astype(jnp.bfloat16)
                halo_ref[1, :, lanes] = grad_value[span].astype(jnp.bfloat16)
        else:
            acc_out_ref[0, :, lanes] = grad_key
            acc_out_ref[1, :, lanes] = grad_value
    query_out_ref[...] = jnp.swapaxes(jnp.concatenate(grads, axis=0), 0, 1).astype(jnp.bfloat16)


def attend(step, base, span, cost, heads, meta, assignment, segments, query, grad, kv_pieces, acc, full, last):
    first, filled = acc is None, full is not None
    rows, (count, _, _, kv_width) = query[0].shape[1], kv_pieces[0].shape
    pieces = len(kv_pieces)
    ratio = heads // (kv_width // HD)
    tok_dev = count * rows
    keys = pieces * tok_dev
    lanes, place = HEADS_STEP * HD, base // HEADS_STEP

    def rows_spec(array, pick):
        start = place if array.shape[2] == heads * HD else 0
        return pl.BlockSpec(
            (None, rows, HEADS_STEP * ratio * HD), lambda c, m, a: (pick(m, a), 0, start + c)
        )

    in_specs = [
        pl.BlockSpec(segments.shape, lambda c, m, a: (0, 0)),
        rows_spec(*query),
        rows_spec(*grad),
    ]
    in_specs += [
        pl.BlockSpec((count, 2, rows, lanes), lambda c, m, a: (0, 0, 0, place + c))
        for _ in kv_pieces
    ]
    operands = [meta, assignment, segments, query[0], grad[0], *kv_pieces]
    aliases = {}
    acc_spec = pl.BlockSpec((2, keys, lanes), lambda c, m, a: (0, 0, place + c))
    if not first:
        if not last:
            aliases[len(operands)] = 1
        operands.append(acc)
        in_specs.append(acc_spec)
    if filled:
        aliases[len(operands)] = 0
        operands.append(full)
        in_specs.append(pl.BlockSpec(memory_space=pl.ANY))
    out_shape = [jax.ShapeDtypeStruct((tok_dev, heads, HD), jnp.bfloat16)]
    out_specs = [
        pl.BlockSpec(
            (rows, HEADS_STEP * ratio, HD),
            lambda c, m, a: (source_of(m[0], step, count), place + c, 0),
        )
    ]
    if last:
        span_spec = pl.BlockSpec((2, tok_dev, lanes), lambda c, m, a: (0, 0, c))
        out_shape.append(jax.ShapeDtypeStruct((2, tok_dev, span * HD), jnp.float32))
        out_shape += [jax.ShapeDtypeStruct((2, tok_dev, span * HD), jnp.bfloat16)] * (pieces - 1)
        out_specs += [span_spec] * pieces
    else:
        out_shape.append(jax.ShapeDtypeStruct((2, keys, kv_width), jnp.float32))
        out_specs.append(acc_spec)
    pairs = span * ratio * rows * keys
    return pl.pallas_call(
        functools.partial(attend_kernel, step, first, filled, last, pieces, ratio),
        out_shape=out_shape,
        grid_spec=pltpu.PrefetchScalarGridSpec(
            num_scalar_prefetch=2,
            grid=(span // HEADS_STEP,),
            in_specs=in_specs,
            out_specs=out_specs,
            scratch_shapes=[
                pltpu.VMEM((keys, ratio * rows), jnp.float32),
            ],
        ),
        input_output_aliases=aliases,
        compiler_params=pltpu.CompilerParams(
            dimension_semantics=("arbitrary",), vmem_limit_bytes=VMEM_BYTES
        ),
        cost_estimate=pl.CostEstimate(
            flops=cost * pairs * HD, bytes_accessed=cost * pairs, transcendentals=0
        ),
        name="attend",
    )(*operands)


def shards(queries, keys, values, grad_out, segment_ids, assignment):
    count = lax.axis_size("dp")
    uly = lax.axis_size("uly")
    group = lax.axis_index("dp")
    line = lax.axis_index("blk") * uly + lax.axis_index("uly")
    width, kv_width = queries.shape[2], keys.shape[2]
    heads, kv_heads = width // HD, kv_width // HD
    tok_dev = count * queries.shape[1]
    doc_most = min(512, tok_dev * uly)
    hops = -(-doc_most // tok_dev)
    meta = jnp.stack([group, line]).astype(jnp.int32)
    final = count - 1

    kv_out = stage_kv(assignment, keys, values)
    parts = [(step, 0, width) for step in range(1, count)]
    staged = stage(meta, assignment, queries, grad_out, parts, after=(kv_out,))
    kv_own = lax.all_to_all(kv_out, "dp", split_axis=0, concat_axis=0, tiled=True)
    arrived = [exchanged(rows, "dp", step) for rows, (step, _, _) in zip(staged, parts)]
    pieces = [kv_own]
    for back in range(1, hops + 1):
        pieces.append(shifted(kv_own, ("blk", "uly"), back))

    fixed = (heads, meta, assignment, segment_ids)
    query, grad = (queries, lambda m, a: a[m[0]]), (grad_out, lambda m, a: a[m[0]])
    full, acc = attend(0, 0, kv_heads, 1, *fixed, query, grad, pieces, None, None, False)
    for both, (step, _, _) in zip(arrived, parts):
        query, grad = (both, lambda m, a: 0), (both, lambda m, a: 1)
        full, acc, *halos = attend(
            step, 0, kv_heads, 1, *fixed, query, grad, pieces, acc, full, step == final
        )
    total = acc
    for back, halo in enumerate(halos, 1):
        total = total + shifted(halo, ("blk", "uly"), -back).astype(jnp.float32)
    total = total.astype(jnp.bfloat16)
    return full[None], total[0][None], total[1][None]


def solution(mesh):
    in_specs = (
        P(None, ("blk", "uly", "dp"), None),
        P(None, ("blk", "uly", "dp"), None),
        P(None, ("blk", "uly", "dp"), None),
        P(None, ("blk", "uly", "dp"), None),
        P(),
        P(),
    )
    out_specs = (
        P("dp", ("blk", "uly"), None, None),
        P("dp", ("blk", "uly"), None),
        P("dp", ("blk", "uly"), None),
    )
    return jax.shard_map(shards, mesh=mesh, in_specs=in_specs, out_specs=out_specs, check_vma=False)
```

time: 103 us -> 83.4 us (0.81)
  waiting for transfers between devices: 37.1 us -> 12.3 us
  starting transfers between devices: 21.4 us -> 44.4 us
  blocking collectives: 12.1 us -> 0 us
  local copies, waits for them, and re-layouts: 4.92 us -> 0.75 us
  Pallas kernels: 25.4 us -> 23.4 us
    ppermute x4 -> x3, waiting for transfers between devices: 29.3 us -> 0.01 us  [exchanged(): lax.ppermute(value, axis, [(i, (i + step) % count) for i in range(count)])]
    ppermute x6 -> x4, starting transfers between devices: 18.1 us -> 34 us  [shifted(): return lax.ppermute(value, axis, pairs)]
    all_to_all x1 -> x0, blocking collectives: 12.1 us -> none  [shards(): lax.all_to_all(kv_out, 'dp', split_axis=0, concat_axis=0, tiled=True)]
    all_to_all x0 -> x1, starting transfers between devices: none -> 5.56 us  [shards(): lax.all_to_all(kv_out, 'dp', split_axis=0, concat_axis=0, tiled=True)]
    unnamed x12 -> x10, local copies, waits for them, and re-layouts: 4.92 us -> 0.03 us
    pallas_call x5 -> x4, Pallas kernels: 22.9 us -> 18.1 us  [attend(): pl.pallas_call(functools.partial(attend_kernel, step, first, filled, last...]
    ppermute x6 -> x4, waiting for transfers between devices: 7.85 us -> 12.3 us  [shifted(): return lax.ppermute(value, axis, pairs)]
    pallas_call x1 -> x2, Pallas kernels: 2.55 us -> 5.32 us  [the longest x1 3.03 us: stage(): pl.pallas_call(functools.partial(stage_kernel, count, parts, copies), out...]
  transfers between devices with their start and end apart: 10 -> 8, of which waited for: 6 -> 4; matrix products, arithmetic and copies ran while one was open for 0% -> 1% of each run, Pallas kernels for 19% -> 20%
where the time goes in v4:
time: 83.4 us; the launch traced here: 82.4 us
  starting transfers between devices  44.4 us (53%)
  Pallas kernels  23.4 us (28%)
  waiting for transfers between devices  12.3 us (15%)
    ppermute x4, starting transfers between devices, shifted(): return lax.ppermute(value, axis, pairs)  34 us
    pallas_call x4, Pallas kernels, attend(): pl.pallas_call(functools.partial(attend_kernel, step, first, filled, last...  18.1 us
    ppermute x4, waiting for transfers between devices, shifted(): return lax.ppermute(value, axis, pairs)  12.3 us
    all_to_all x1, starting transfers between devices, shards(): lax.all_to_all(kv_out, 'dp', split_axis=0, concat_axis=0, tiled=True)  5.56 us
    ppermute x3, starting transfers between devices, exchanged(): lax.ppermute(value, axis, [(i, (i + step) % count) for i in range(count)])  4.78 us
    pallas_call x1, Pallas kernels, stage(): pl.pallas_call(functools.partial(stage_kernel, count, parts, copies), out...  3.03 us
    pallas_call x1, Pallas kernels, stage_kv(): pl.pallas_call(stage_kv_kernel, out_shape=jax.ShapeDtypeStruct(shape, key...  2.29 us
  transfers between devices with their start and end apart: 8, of which 4 were waited for; matrix products, arithmetic and copies ran while one was open for 1% of the time, Pallas kernels for 20%

profile of v4, /device:TPU:1, one launch (start us, length us, event | category | flops | bytes accessed | tf_op | source)
XLA Modules:
  0.0 82.4 jit_solution(1485133111384548914)
XLA Ops:
  0.6 2.3 %stage_kv.1.refs_2_ = bf16[4,2,32,512]{3,2,1,0:T(8,128)(2,1)} custom-call(s32[4]{0:T(128)} %assign_ref.11, bf16[4,32,512]{2,1,0:T(8,128)(2,1)} %key_ref.1, bf16[4,32,512]{2,1,0:T(8,128)(2,1)} %value_ref.1), custom_call_target="tpu_custom_call" | custom-call | tf_op jit(solution)/shard_map/stage_kv/pallas_call | solution.py:89
  2.9 0.0 copy-start
  2.9 0.0 copy-start.1
  3.0 0.0 copy-start.2
  3.0 5.6 %all-to-all-start = ((bf16[4,2,32,512]{3,2,1,0:T(8,128)(2,1)}), bf16[4,2,32,512]{3,2,1,0:T(8,128)(2,1)S(1)}, u32[]{:S(2)}, u32[]{:S(2)}) async-start(bf16[4,2,32,512]{3,2,1,0:T(8,128)(2,1)} %stage_kv.1.refs_2_), calls=%async_computation | async-start | bytes 524288 | tf_op jit(solution)/shard_map/all_to_all | solution.py:323
  8.5 0.7 pad_add_fusion.meta_ref
  9.2 3.0 %stage.1 = (bf16[2,32,4096]{2,1,0:T(8,128)(2,1)}, bf16[2,32,4096]{2,1,0:T(8,128)(2,1)}, bf16[2,32,4096]{2,1,0:T(8,128)(2,1)}) custom-call(s32[2]{0:T(128)} %pad_add_fusion.meta_ref, s32[4]{0:T(128)} %assign_ref.11, bf16[4,32,4096]{2,1,0:T(8,128)(2,1)} %query_ref.1, bf16[4,32,4096]{2,1,0:T(8,128)(2,1)} %grad_ref.1, bf16[4,2,32,512]{3,2,1,0:T(8,128)(2,1)} %stage_kv.1.refs_2_), custom_call_target="tpu_custom_call" | custom-call | tf_op jit(solution)/shard_map/stage/pallas_call | solution.py:105
  12.2 1.5 %collective-permute-start.4 = (bf16[2,32,4096]{2,1,0:T(8,128)(2,1)}, bf16[2,32,4096]{2,1,0:T(8,128)(2,1)}, u32[]{:S(2)}, u32[]{:S(2)}) collective-permute-start(bf16[2,32,4096]{2,1,0:T(8,128)(2,1)} %get-tuple-element.18), channel_id=1, source_target_pairs={{0,1},{1,2},{2,3},{3,0},{4,5},{5,6},{6,7},{7,4},{8,9},{9,10},{10,1... | collective-permute-start | bytes 1572872 | tf_op jit(solution)/shard_map/ppermute | solution.py:27
  13.8 2.1 %collective-permute-start.3 = (bf16[2,32,4096]{2,1,0:T(8,128)(2,1)}, bf16[2,32,4096]{2,1,0:T(8,128)(2,1)S(1)}, u32[]{:S(2)}, u32[]{:S(2)}) collective-permute-start(bf16[2,32,4096]{2,1,0:T(8,128)(2,1)} %get-tuple-element.17), channel_id=1, source_target_pairs={{0,2},{1,3},{2,0},{3,1},{4,6},{5,7},{6,4},{7,5},{8,10},{9,11},{10,... | collective-permute-start | bytes 1572872 | tf_op jit(solution)/shard_map/ppermute | solution.py:27
  15.8 1.2 %collective-permute-start = (bf16[2,32,4096]{2,1,0:T(8,128)(2,1)}, bf16[2,32,4096]{2,1,0:T(8,128)(2,1)S(1)}, u32[]{:S(2)}, u32[]{:S(2)}) collective-permute-start(bf16[2,32,4096]{2,1,0:T(8,128)(2,1)} %get-tuple-element.16), channel_id=1, source_target_pairs={{0,3},{1,0},{2,1},{3,2},{4,7},{5,4},{6,5},{7,6},{8,11},{9,8},{10,9... | collective-permute-start | bytes 1572872 | tf_op jit(solution)/shard_map/ppermute | solution.py:27
  17.0 27.1 %collective-permute-start.2 = (bf16[4,2,32,512]{3,2,1,0:T(8,128)(2,1)S(1)}, bf16[4,2,32,512]{3,2,1,0:T(8,128)(2,1)S(1)}, u32[]{:S(2)}, u32[]{:S(2)}) collective-permute-start(bf16[4,2,32,512]{3,2,1,0:T(8,128)(2,1)S(1)} %all-to-all-done.refs_0_), channel_id=1, source_target_pairs={{0,8},{4,12},{8,16},{12,20},{16,24},{20,28},{1,9},{5,13},{9,17},{1... | collective-permute-start | bytes 786440 | tf_op jit(solution)/shard_map/ppermute | solution.py:33
  44.1 3.1 %collective-permute-start.1 = (bf16[4,2,32,512]{3,2,1,0:T(8,128)(2,1)S(1)}, bf16[4,2,32,512]{3,2,1,0:T(8,128)(2,1)S(1)}, u32[]{:S(2)}, u32[]{:S(2)}) collective-permute-start(bf16[4,2,32,512]{3,2,1,0:T(8,128)(2,1)S(1)} %all-to-all-done.refs_0_), channel_id=1, source_target_pairs={{0,4},{4,8},{8,12},{12,16},{16,20},{20,24},{24,28},{1,5},{5,9},{9,... | collective-permute-start | bytes 786440 | tf_op jit(solution)/shard_map/ppermute | solution.py:33
  47.3 0.2 collective-permute-done.2.refs_2_
  47.4 6.4 %collective-permute-done.1.refs_1_ = bf16[4,2,32,512]{3,2,1,0:T(8,128)(2,1)S(1)} collective-permute-done((bf16[4,2,32,512]{3,2,1,0:T(8,128)(2,1)S(1)}, bf16[4,2,32,512]{3,2,1,0:T(8,128)(2,1)S(1)}, u32[]{:S(2)}, u32[]{:S(2)}) %collective-permute-start.1) | collective-permute-done | bytes 262176 | tf_op jit(solution)/shard_map/ppermute | solution.py:33
  53.8 4.2 %attend.4 = (bf16[128,32,128]{2,1,0:T(8,128)(2,1)}, f32[2,384,512]{2,1,0:T(8,128)S(1)}) custom-call(s32[2]{0:T(128)S(1)} %copy-done.4, s32[4]{0:T(128)S(1)} %copy-done.3, s32[4,1024]{1,0:T(4,128)S(1)} %copy-done.2, bf16[4,32,4096]{2,1,0:T(8,128)(2,1)S(1)} %copy-done, bf16[4,32,4096]{2,1,0:T(8,128)(2,1)S(1)} %copy-done.1, ...), custom_call_target="tpu_custom_call" | custom-call | flops 50331648 | bytes 393216 | tf_op jit(solution)/shard_map/attend/pallas_call | solution.py:284
  58.0 5.1 %attend.5 = (bf16[128,32,128]{2,1,0:T(8,128)(2,1)}, f32[2,384,512]{2,1,0:T(8,128)S(1)}) custom-call(s32[2]{0:T(128)S(1)} %copy-done.4, s32[4]{0:T(128)S(1)} %copy-done.3, s32[4,1024]{1,0:T(4,128)S(1)} %copy-done.2, bf16[2,32,4096]{2,1,0:T(8,128)(2,1)} %collective-permute-done.4.query_ref.grad_ref, ...), custom_call_target="tpu_custom_call", output_to_operand_aliasing={{1}: (8, {}), {0}: (9, {})} | custom-call | flops 50331648 | bytes 393216 | tf_op jit(solution)/shard_map/attend/pallas_call | solution.py:284
  63.1 4.4 %attend.6 = (bf16[128,32,128]{2,1,0:T(8,128)(2,1)}, f32[2,384,512]{2,1,0:T(8,128)S(1)}) custom-call(s32[2]{0:T(128)S(1)} %copy-done.4, s32[4]{0:T(128)S(1)} %copy-done.3, s32[4,1024]{1,0:T(4,128)S(1)} %copy-done.2, bf16[2,32,4096]{2,1,0:T(8,128)(2,1)S(1)} %collective-permute-done.3.query_ref.grad_ref, ...), custom_call_target="tpu_custom_call", output_to_operand_aliasing={{1}: (8, {}), {0}: (9, {})} | custom-call | flops 50331648 | bytes 393216 | tf_op jit(solution)/shard_map/attend/pallas_call | solution.py:284
  67.6 4.4 %attend.7 = (bf16[128,32,128]{2,1,0:T(8,128)(2,1)}, f32[2,128,512]{2,1,0:T(8,128)S(1)}, bf16[2,128,512]{2,1,0:T(8,128)(2,1)S(1)}, bf16[2,128,512]{2,1,0:T(8,128)(2,1)S(1)}) custom-call(s32[2]{0:T(128)S(1)} %copy-done.4, s32[4]{0:T(128)S(1)} %copy-done.3, s32[4,1024]{1,0:T(4,128)S(1)} %copy-done.2, ...), custom_call_target="tpu_custom_call", output_to_operand_aliasing={{0}: (9, {})} | custom-call | flops 50331648 | bytes 393216 | tf_op jit(solution)/shard_map/attend/pallas_call | solution.py:284
  72.0 1.9 %collective-permute-start.5 = (bf16[2,128,512]{2,1,0:T(8,128)(2,1)S(1)}, bf16[2,128,512]{2,1,0:T(8,128)(2,1)S(1)}, u32[]{:S(2)}, u32[]{:S(2)}) collective-permute-start(bf16[2,128,512]{2,1,0:T(8,128)(2,1)S(1)} %get-tuple-element.27), channel_id=1, source_target_pairs={{4,0},{8,4},{12,8},{16,12},{20,16},{24,20},{28,24},{5,1},{9,5},{13... | collective-permute-start | bytes 786440 | tf_op jit(solution)/shard_map/ppermute | solution.py:33
  73.9 1.9 %collective-permute-start.6 = (bf16[2,128,512]{2,1,0:T(8,128)(2,1)S(1)}, bf16[2,128,512]{2,1,0:T(8,128)(2,1)S(1)}, u32[]{:S(2)}, u32[]{:S(2)}) collective-permute-start(bf16[2,128,512]{2,1,0:T(8,128)(2,1)S(1)} %get-tuple-element.28), channel_id=1, source_target_pairs={{8,0},{12,4},{16,8},{20,12},{24,16},{28,20},{9,1},{13,5},{17,9},{2... | collective-permute-start | bytes 786440 | tf_op jit(solution)/shard_map/ppermute | solution.py:33
  75.8 4.7 %collective-permute-done.5 = bf16[2,128,512]{2,1,0:T(8,128)(2,1)S(1)} collective-permute-done((bf16[2,128,512]{2,1,0:T(8,128)(2,1)S(1)}, bf16[2,128,512]{2,1,0:T(8,128)(2,1)S(1)}, u32[]{:S(2)}, u32[]{:S(2)}) %collective-permute-start.5) | collective-permute-done | bytes 262176 | tf_op jit(solution)/shard_map/ppermute | solution.py:33
  80.6 1.0 %collective-permute-done.6 = bf16[2,128,512]{2,1,0:T(8,128)(2,1)S(1)} collective-permute-done((bf16[2,128,512]{2,1,0:T(8,128)(2,1)S(1)}, bf16[2,128,512]{2,1,0:T(8,128)(2,1)S(1)}, u32[]{:S(2)}, u32[]{:S(2)}) %collective-permute-start.6) | collective-permute-done | bytes 262176 | tf_op jit(solution)/shard_map/ppermute | solution.py:33
  81.6 0.1 add_convert_fusion
  81.7 0.7 fusion
  (11 shorter events, 0.0 us)
Async XLA Ops:
  2.9 50.9 %copy-start = (bf16[4,32,4096]{2,1,0:T(8,128)(2,1)S(1)}, bf16[4,32,4096]{2,1,0:T(8,128)(2,1)}, u32[]{:S(2)}) copy-start(bf16[4,32,4096]{2,1,0:T(8,128)(2,1)} %query_ref.1) | copy-start | bytes 3145732
  2.9 50.9 %copy-start.1 = (bf16[4,32,4096]{2,1,0:T(8,128)(2,1)S(1)}, bf16[4,32,4096]{2,1,0:T(8,128)(2,1)}, u32[]{:S(2)}) copy-start(bf16[4,32,4096]{2,1,0:T(8,128)(2,1)} %grad_ref.1) | copy-start | bytes 3145732
  3.0 50.9 %copy-start.2 = (s32[4,1024]{1,0:T(4,128)S(1)}, s32[4,1024]{1,0:T(4,128)}, u32[]{:S(2)}) copy-start(s32[4,1024]{1,0:T(4,128)} %segment_ref.7) | copy-start | bytes 49156
  3.0 50.9 %copy-start.3 = (s32[4]{0:T(128)S(1)}, s32[4]{0:T(128)}, u32[]{:S(2)}) copy-start(s32[4]{0:T(128)} %assign_ref.11) | copy-start | bytes 52
  3.0 14.0 %all-to-all-start = ((bf16[4,2,32,512]{3,2,1,0:T(8,128)(2,1)}), bf16[4,2,32,512]{3,2,1,0:T(8,128)(2,1)S(1)}, u32[]{:S(2)}, u32[]{:S(2)}) async-start(bf16[4,2,32,512]{3,2,1,0:T(8,128)(2,1)} %stage_kv.1.refs_2_), calls=%async_computation | async-start | bytes 524288 | tf_op jit(solution)/shard_map/all_to_all | solution.py:323
  9.2 44.6 %copy-start.4 = (s32[2]{0:T(128)S(1)}, s32[2]{0:T(128)}, u32[]{:S(2)}) copy-start(s32[2]{0:T(128)} %pad_add_fusion.meta_ref) | copy-start | bytes 28
  12.2 45.8 %collective-permute-start.4 = (bf16[2,32,4096]{2,1,0:T(8,128)(2,1)}, bf16[2,32,4096]{2,1,0:T(8,128)(2,1)}, u32[]{:S(2)}, u32[]{:S(2)}) collective-permute-start(bf16[2,32,4096]{2,1,0:T(8,128)(2,1)} %get-tuple-element.18), channel_id=1, source_target_pairs={{0,1},{1,2},{2,3},{3,0},{4,5},{5,6},{6,7},{7,4},{8,9},{9,10},{10,1... | collective-permute-start | bytes 1572872 | tf_op jit(solution)/shard_map/ppermute | solution.py:27
  13.8 49.4 %collective-permute-start.3 = (bf16[2,32,4096]{2,1,0:T(8,128)(2,1)}, bf16[2,32,4096]{2,1,0:T(8,128)(2,1)S(1)}, u32[]{:S(2)}, u32[]{:S(2)}) collective-permute-start(bf16[2,32,4096]{2,1,0:T(8,128)(2,1)} %get-tuple-element.17), channel_id=1, source_target_pairs={{0,2},{1,3},{2,0},{3,1},{4,6},{5,7},{6,4},{7,5},{8,10},{9,11},{10,... | collective-permute-start | bytes 1572872 | tf_op jit(solution)/shard_map/ppermute | solution.py:27
  15.8 51.7 %collective-permute-start = (bf16[2,32,4096]{2,1,0:T(8,128)(2,1)}, bf16[2,32,4096]{2,1,0:T(8,128)(2,1)S(1)}, u32[]{:S(2)}, u32[]{:S(2)}) collective-permute-start(bf16[2,32,4096]{2,1,0:T(8,128)(2,1)} %get-tuple-element.16), channel_id=1, source_target_pairs={{0,3},{1,0},{2,1},{3,2},{4,7},{5,4},{6,5},{7,6},{8,11},{9,8},{10,9... | collective-permute-start | bytes 1572872 | tf_op jit(solution)/shard_map/ppermute | solution.py:27
  17.0 30.4 %collective-permute-start.2 = (bf16[4,2,32,512]{3,2,1,0:T(8,128)(2,1)S(1)}, bf16[4,2,32,512]{3,2,1,0:T(8,128)(2,1)S(1)}, u32[]{:S(2)}, u32[]{:S(2)}) collective-permute-start(bf16[4,2,32,512]{3,2,1,0:T(8,128)(2,1)S(1)} %all-to-all-done.refs_0_), channel_id=1, source_target_pairs={{0,8},{4,12},{8,16},{12,20},{16,24},{20,28},{1,9},{5,13},{9,17},{1... | collective-permute-start | bytes 786440 | tf_op jit(solution)/shard_map/ppermute | solution.py:33
  44.1 9.7 %collective-permute-start.1 = (bf16[4,2,32,512]{3,2,1,0:T(8,128)(2,1)S(1)}, bf16[4,2,32,512]{3,2,1,0:T(8,128)(2,1)S(1)}, u32[]{:S(2)}, u32[]{:S(2)}) collective-permute-start(bf16[4,2,32,512]{3,2,1,0:T(8,128)(2,1)S(1)} %all-to-all-done.refs_0_), channel_id=1, source_target_pairs={{0,4},{4,8},{8,12},{12,16},{16,20},{20,24},{24,28},{1,5},{5,9},{9,... | collective-permute-start | bytes 786440 | tf_op jit(solution)/shard_map/ppermute | solution.py:33
  72.0 8.6 %collective-permute-start.5 = (bf16[2,128,512]{2,1,0:T(8,128)(2,1)S(1)}, bf16[2,128,512]{2,1,0:T(8,128)(2,1)S(1)}, u32[]{:S(2)}, u32[]{:S(2)}) collective-permute-start(bf16[2,128,512]{2,1,0:T(8,128)(2,1)S(1)} %get-tuple-element.27), channel_id=1, source_target_pairs={{4,0},{8,4},{12,8},{16,12},{20,16},{24,20},{28,24},{5,1},{9,5},{13... | collective-permute-start | bytes 786440 | tf_op jit(solution)/shard_map/ppermute | solution.py:33
  73.9 7.7 %collective-permute-start.6 = (bf16[2,128,512]{2,1,0:T(8,128)(2,1)S(1)}, bf16[2,128,512]{2,1,0:T(8,128)(2,1)S(1)}, u32[]{:S(2)}, u32[]{:S(2)}) collective-permute-start(bf16[2,128,512]{2,1,0:T(8,128)(2,1)S(1)} %get-tuple-element.28), channel_id=1, source_target_pairs={{8,0},{12,4},{16,8},{20,12},{24,16},{28,20},{9,1},{13,5},{17,9},{2... | collective-permute-start | bytes 786440 | tf_op jit(solution)/shard_map/ppermute | solution.py:33

commit v5 on v4

--- a/solution.py
+++ b/solution.py
@@ -33,26 +33,17 @@
     return lax.ppermute(value, axis, pairs)
 
 
-def stage_kernel(count, parts, copies, meta_ref, assign_ref, *refs):
+def stage_kernel(count, jobs, outs, meta_ref, assign_ref, *refs):
     group = meta_ref[0]
-    sources = refs[:2]
-    out_refs, held_refs = refs[-2 - 2 * len(parts) : -2 - len(parts)], refs[-2 - len(parts) : -2]
-    in_sems, out_sems = refs[-2:]
+    sources, refs = refs[:4], refs[len(refs) - 2 * outs - 2 :]
+    out_refs, held_refs, (in_sems, out_sems) = refs[:outs], refs[outs : 2 * outs], refs[-2:]
     loads, stores = [], []
-    for (step, start, width), out_ref, held_ref in zip(parts, out_refs, held_refs):
-        chosen = assign_ref[target_of(group, step, count)]
-        for which, source in enumerate(sources):
-            slot = len(loads)
-            loads.append(
-                pltpu.make_async_copy(
-                    source.at[chosen, :, start : start + width],
-                    held_ref.at[which],
-                    in_sems.at[slot],
-                )
-            )
-            stores.append(
-                pltpu.make_async_copy(held_ref.at[which], out_ref.at[which], out_sems.at[slot])
-            )
+    for slot, (source, step, start, width, out, place) in enumerate(jobs):
+        other = step if len(place) > 1 else target_of(group, step, count)
+        origin = sources[source].at[assign_ref[other], :, start : start + width]
+        held, goal = held_refs[out].at[place], out_refs[out].at[place]
+        loads.append(pltpu.make_async_copy(origin, held, in_sems.at[slot]))
+        stores.append(pltpu.make_async_copy(held, goal, out_sems.at[slot]))
     for load in loads:
         load.start()
     for load, store in zip(loads, stores):
@@ -62,55 +53,27 @@
         store.wait()
 
 
-def stage_kv_kernel(assign_ref, key_ref, value_ref, out_ref, held_ref, in_sems, out_sems):
-    loads, stores = [], []
-    for group in range(out_ref.shape[0]):
-        chosen = assign_ref[group]
-        for which, source in enumerate((key_ref, value_ref)):
-            slot = len(loads)
-            held = held_ref.at[group, which]
-            loads.append(pltpu.make_async_copy(source.at[chosen], held, in_sems.at[slot]))
-            stores.append(
-                pltpu.make_async_copy(held, out_ref.at[group, which], out_sems.at[slot])
-            )
-    for load in loads:
-        load.start()
-    for load, store in zip(loads, stores):
-        load.wait()
-        store.start()
-    for store in stores:
-        store.wait()
-
-
-def stage_kv(assignment, keys, values):
-    count, rows, width = keys.shape
-    shape = (count, 2, rows, width)
-    far = pl.BlockSpec(memory_space=pltpu.HBM)
-    return pl.pallas_call(
-        stage_kv_kernel,
-        out_shape=jax.ShapeDtypeStruct(shape, keys.dtype),
-        in_specs=[pl.BlockSpec(memory_space=pltpu.SMEM), far, far],
-        out_specs=far,
-        scratch_shapes=[pltpu.VMEM(shape, keys.dtype)]
-        + [pltpu.SemaphoreType.DMA((2 * count,))] * 2,
-        name="stage_kv",
-    )(assignment, keys, values)
-
-
-def stage(meta, assignment, first, second, parts, after=()):
-    count, rows, _ = first.shape
-    shapes = [(2, rows, width) for _, _, width in parts]
-    copies = 2 * len(parts)
+def stage(meta, assignment, arrays, parts, with_kv, after=()):
+    count, rows, _ = arrays[0].shape
+    kv_width = arrays[2].shape[2]
+    shapes, jobs = [], []
+    if with_kv:
+        shapes.append((count, 2, rows, kv_width))
+        for other in range(count):
+            jobs += [(2 + which, other, 0, kv_width, 0, (other, which)) for which in range(2)]
+    for step, start, width in parts:
+        jobs += [(which, step, start, width, len(shapes), (which,)) for which in range(2)]
+        shapes.append((2, rows, width))
     far, scalars = pl.BlockSpec(memory_space=pltpu.HBM), pl.BlockSpec(memory_space=pltpu.SMEM)
     return pl.pallas_call(
-        functools.partial(stage_kernel, count, parts, copies),
-        out_shape=[jax.ShapeDtypeStruct(shape, first.dtype) for shape in shapes],
-        in_specs=[scalars] * 2 + [far] * 2 + [pl.BlockSpec(memory_space=pl.ANY)] * len(after),
+        functools.partial(stage_kernel, count, jobs, len(shapes)),
+        out_shape=[jax.ShapeDtypeStruct(shape, arrays[0].dtype) for shape in shapes],
+        in_specs=[scalars] * 2 + [far] * 4 + [pl.BlockSpec(memory_space=pl.ANY)] * len(after),
         out_specs=[far] * len(shapes),
-        scratch_shapes=[pltpu.VMEM(shape, first.dtype) for shape in shapes]
-        + [pltpu.SemaphoreType.DMA((copies,))] * 2,
+        scratch_shapes=[pltpu.VMEM(shape, arrays[0].dtype) for shape in shapes]
+        + [pltpu.SemaphoreType.DMA((len(jobs),))] * 2,
         name="stage",
-    )(meta, assignment, first, second, *after)
+    )(meta, assignment, *arrays, *after)
 
 
 def build_bias(source, sequence, line, segment_ref, bias_ref, rows, tok_dev, ratio):
@@ -315,13 +278,19 @@
     doc_most = min(512, tok_dev * uly)
     hops = -(-doc_most // tok_dev)
     meta = jnp.stack([group, line]).astype(jnp.int32)
-    final = count - 1
-
-    kv_out = stage_kv(assignment, keys, values)
-    parts = [(step, 0, width) for step in range(1, count)]
-    staged = stage(meta, assignment, queries, grad_out, parts, after=(kv_out,))
+    halves = kv_heads // HEADS_STEP
+    part = width // halves
+    final = count // 2
+    others = [step for step in range(1, count) if step != final]
+
+    arrays = (queries, grad_out, keys, values)
+    parts = [(step, 0, width) for step in others]
+    parts += [(final, half * part, part) for half in range(halves)]
+    ahead = stage(meta, assignment, arrays, parts[:1], False)
+    kv_out, *behind = stage(meta, assignment, arrays, parts[1:], True, after=ahead)
     kv_own = lax.all_to_all(kv_out, "dp", split_axis=0, concat_axis=0, tiled=True)
-    arrived = [exchanged(rows, "dp", step) for rows, (step, _, _) in zip(staged, parts)]
+    early, late = [*ahead, *behind][: len(others) + 1], behind[len(others) :]
+    arrived = [exchanged(rows, "dp", step) for rows, (step, _, _) in zip(early, parts)]
     pieces = [kv_own]
     for back in range(1, hops + 1):
         pieces.append(shifted(kv_own, ("blk", "uly"), back))
@@ -329,15 +298,24 @@
     fixed = (heads, meta, assignment, segment_ids)
     query, grad = (queries, lambda m, a: a[m[0]]), (grad_out, lambda m, a: a[m[0]])
     full, acc = attend(0, 0, kv_heads, 1, *fixed, query, grad, pieces, None, None, False)
-    for both, (step, _, _) in zip(arrived, parts):
+    late, acc = lax.optimization_barrier((late, acc))
+    arrived += [exchanged(rows, "dp", final) for rows in late]
+    for both, step in zip(arrived, others):
         query, grad = (both, lambda m, a: 0), (both, lambda m, a: 1)
-        full, acc, *halos = attend(
-            step, 0, kv_heads, 1, *fixed, query, grad, pieces, acc, full, step == final
-        )
-    total = acc
-    for back, halo in enumerate(halos, 1):
-        total = total + shifted(halo, ("blk", "uly"), -back).astype(jnp.float32)
-    total = total.astype(jnp.bfloat16)
+        full, acc = attend(step, 0, kv_heads, 1, *fixed, query, grad, pieces, acc, full, False)
+    totals, returned = [], []
+    for half, both in enumerate(arrived[len(others) :]):
+        if half:
+            both, returned = lax.optimization_barrier((both, returned))
+        query, grad = (both, lambda m, a: 0), (both, lambda m, a: 1)
+        full, total, *halos = attend(
+            final, half * HEADS_STEP, HEADS_STEP, 1, *fixed, query, grad, pieces, acc, full, True
+        )
+        returned = [shifted(halo, ("blk", "uly"), -back) for back, halo in enumerate(halos, 1)]
+        for halo in returned:
+            total = total + halo.astype(jnp.float32)
+        totals.append(total.astype(jnp.bfloat16))
+    total = jnp.concatenate(totals, axis=2)
     return full[None], total[0][None], total[1][None]
 
 

time: 83.4 us -> 86.4 us (1.036)
  waiting for transfers between devices: 12.3 us -> 19.5 us
  starting transfers between devices: 44.4 us -> 40.5 us
    all_to_all x1, waiting for transfers between devices: 0.01 us -> 4.35 us  [shards(): lax.all_to_all(kv_out, 'dp', split_axis=0, concat_axis=0, tiled=True)]
    ppermute x4 -> x6, waiting for transfers between devices: 12.3 us -> 15.1 us  [shifted(): return lax.ppermute(value, axis, pairs)]
    ppermute x4 -> x6, starting transfers between devices: 34 us -> 31.7 us  [shifted(): return lax.ppermute(value, axis, pairs)]
    ppermute x3 -> x4, starting transfers between devices: 4.78 us -> 3.37 us  [exchanged(): lax.ppermute(value, axis, [(i, (i + step) % count) for i in range(count)])]
    pallas_call x4 -> x5, Pallas kernels: 18.1 us -> 18.2 us  [attend(): pl.pallas_call(functools.partial(attend_kernel, step, first, filled, last...]
  transfers between devices with their start and end apart: 8 -> 11, of which waited for: 4 -> 6; matrix products, arithmetic and copies ran while one was open for 1% -> 0% of each run, Pallas kernels for 20% -> 18%
where the time goes in v5:
time: 86.4 us; the launch traced here: 86 us
  starting transfers between devices  40.5 us (47%)
  Pallas kernels  23.7 us (27%)
  waiting for transfers between devices  19.5 us (23%)
  other arithmetic  1.46 us (2%)
    ppermute x6, starting transfers between devices, shifted(): return lax.ppermute(value, axis, pairs)  31.7 us
    pallas_call x5, Pallas kernels, attend(): pl.pallas_call(functools.partial(attend_kernel, step, first, filled, last...  18.2 us
    ppermute x6, waiting for transfers between devices, shifted(): return lax.ppermute(value, axis, pairs)  15.1 us
    pallas_call x2, Pallas kernels, stage(): pl.pallas_call(functools.partial(stage_kernel, count, jobs, len(shapes)),...  5.58 us
    all_to_all x1, starting transfers between devices, shards(): lax.all_to_all(kv_out, 'dp', split_axis=0, concat_axis=0, tiled=True)  5.43 us
    all_to_all x1, waiting for transfers between devices, shards(): lax.all_to_all(kv_out, 'dp', split_axis=0, concat_axis=0, tiled=True)  4.35 us
    ppermute x4, starting transfers between devices, exchanged(): lax.ppermute(value, axis, [(i, (i + step) % count) for i in range(count)])  3.37 us
  transfers between devices with their start and end apart: 11, of which 6 were waited for; matrix products, arithmetic and copies ran while one was open for 0% of the time, Pallas kernels for 18%

profile of v5, /device:TPU:1, one launch (start us, length us, event | category | flops | bytes accessed | tf_op | source)
XLA Modules:
  0.0 86.0 jit_solution(17201099811373388869)
XLA Ops:
  0.6 0.6 pad_add_fusion.meta_ref
  1.3 2.5 %stage.2.refs_4_ = bf16[2,32,4096]{2,1,0:T(8,128)(2,1)} custom-call(s32[2]{0:T(128)} %pad_add_fusion.meta_ref, s32[4]{0:T(128)} %assign_ref.13, bf16[4,32,4096]{2,1,0:T(8,128)(2,1)} %query_ref.1, bf16[4,32,4096]{2,1,0:T(8,128)(2,1)} %grad_ref.1, bf16[4,32,512]{2,1,0:T(8,128)(2,1)} %refs_2_.3, bf16[4,32,512]{2,1,0:T(8,128)(2,1)} %refs_3_.3), custom_call_target="tpu_custom_call" | custom-call | tf_op jit(solution)/shard_map/stage/pallas_call | solution.py:68
  3.8 3.1 %stage.3 = (bf16[4,2,32,512]{3,2,1,0:T(8,128)(2,1)}, bf16[2,32,4096]{2,1,0:T(8,128)(2,1)}, bf16[2,32,2048]{2,1,0:T(8,128)(2,1)}, bf16[2,32,2048]{2,1,0:T(8,128)(2,1)}) custom-call(s32[2]{0:T(128)} %pad_add_fusion.meta_ref, s32[4]{0:T(128)} %assign_ref.13, bf16[4,32,4096]{2,1,0:T(8,128)(2,1)} %query_ref.1, bf16[4,32,4096]{2,1,0:T(8,128)(2,1)} %grad_ref.1, ...), custom_call_target="tpu_custom_call" | custom-call | tf_op jit(solution)/shard_map/stage/pallas_call | solution.py:68
  6.9 5.4 %all-to-all-start = ((bf16[4,2,32,512]{3,2,1,0:T(8,128)(2,1)}), bf16[4,2,32,512]{3,2,1,0:T(8,128)(2,1)S(1)}, u32[]{:S(2)}, u32[]{:S(2)}) async-start(bf16[4,2,32,512]{3,2,1,0:T(8,128)(2,1)} %get-tuple-element.25), calls=%async_computation | async-start | bytes 524288 | tf_op jit(solution)/shard_map/all_to_all | solution.py:291
  12.4 1.5 %collective-permute-start.5 = (bf16[2,32,4096]{2,1,0:T(8,128)(2,1)}, bf16[2,32,4096]{2,1,0:T(8,128)(2,1)S(1)}, u32[]{:S(2)}, u32[]{:S(2)}) collective-permute-start(bf16[2,32,4096]{2,1,0:T(8,128)(2,1)} %stage.2.refs_4_), channel_id=1, source_target_pairs={{0,1},{1,2},{2,3},{3,0},{4,5},{5,6},{6,7},{7,4},{8,9},{9,10},{10,1... | collective-permute-start | bytes 1572872 | tf_op jit(solution)/shard_map/ppermute | solution.py:27
  13.8 1.8 %collective-permute-start.4 = (bf16[2,32,4096]{2,1,0:T(8,128)(2,1)}, bf16[2,32,4096]{2,1,0:T(8,128)(2,1)S(1)}, u32[]{:S(2)}, u32[]{:S(2)}) collective-permute-start(bf16[2,32,4096]{2,1,0:T(8,128)(2,1)} %get-tuple-element.29), channel_id=1, source_target_pairs={{0,3},{1,0},{2,1},{3,2},{4,7},{5,4},{6,5},{7,6},{8,11},{9,8},{10,9... | collective-permute-start | bytes 1572872 | tf_op jit(solution)/shard_map/ppermute | solution.py:27
  15.7 4.3 %all-to-all-done.refs_0_ = bf16[4,2,32,512]{3,2,1,0:T(8,128)(2,1)S(1)} async-done(((bf16[4,2,32,512]{3,2,1,0:T(8,128)(2,1)}), bf16[4,2,32,512]{3,2,1,0:T(8,128)(2,1)S(1)}, u32[]{:S(2)}, u32[]{:S(2)}) %all-to-all-start) | async-done | bytes 262176 | tf_op jit(solution)/shard_map/all_to_all | solution.py:291
  20.0 17.7 %collective-permute-start.1 = (bf16[4,2,32,512]{3,2,1,0:T(8,128)(2,1)S(1)}, bf16[4,2,32,512]{3,2,1,0:T(8,128)(2,1)S(1)}, u32[]{:S(2)}, u32[]{:S(2)}) collective-permute-start(bf16[4,2,32,512]{3,2,1,0:T(8,128)(2,1)S(1)} %all-to-all-done.refs_0_), channel_id=1, source_target_pairs={{0,8},{4,12},{8,16},{12,20},{16,24},{20,28},{1,9},{5,13},{9,17},{1... | collective-permute-start | bytes 786440 | tf_op jit(solution)/shard_map/ppermute | solution.py:33
  37.7 3.1 %collective-permute-start = (bf16[4,2,32,512]{3,2,1,0:T(8,128)(2,1)S(1)}, bf16[4,2,32,512]{3,2,1,0:T(8,128)(2,1)S(1)}, u32[]{:S(2)}, u32[]{:S(2)}) collective-permute-start(bf16[4,2,32,512]{3,2,1,0:T(8,128)(2,1)S(1)} %all-to-all-done.refs_0_), channel_id=1, source_target_pairs={{0,4},{4,8},{8,12},{12,16},{16,20},{20,24},{24,28},{1,5},{5,9},{9,... | collective-permute-start | bytes 786440 | tf_op jit(solution)/shard_map/ppermute | solution.py:33
  40.9 0.1 collective-permute-done.1.refs_2_
  41.0 6.4 %collective-permute-done.refs_1_ = bf16[4,2,32,512]{3,2,1,0:T(8,128)(2,1)S(1)} collective-permute-done((bf16[4,2,32,512]{3,2,1,0:T(8,128)(2,1)S(1)}, bf16[4,2,32,512]{3,2,1,0:T(8,128)(2,1)S(1)}, u32[]{:S(2)}, u32[]{:S(2)}) %collective-permute-start) | collective-permute-done | bytes 262176 | tf_op jit(solution)/shard_map/ppermute | solution.py:33
  47.4 4.2 %attend.5 = (bf16[128,32,128]{2,1,0:T(8,128)(2,1)}, f32[2,384,512]{2,1,0:T(8,128)S(1)}) custom-call(s32[2]{0:T(128)S(1)} %copy-done.4, s32[4]{0:T(128)S(1)} %copy-done.3, s32[4,1024]{1,0:T(4,128)S(1)} %copy-done.2, bf16[4,32,4096]{2,1,0:T(8,128)(2,1)S(1)} %copy-done, bf16[4,32,4096]{2,1,0:T(8,128)(2,1)S(1)} %copy-done.1, ...), custom_call_target="tpu_custom_call" | custom-call | flops 50331648 | bytes 393216 | tf_op jit(solution)/shard_map/attend/pallas_call | solution.py:247
  51.6 4.4 %attend.6 = (bf16[128,32,128]{2,1,0:T(8,128)(2,1)}, f32[2,384,512]{2,1,0:T(8,128)S(1)}) custom-call(s32[2]{0:T(128)S(1)} %copy-done.4, s32[4]{0:T(128)S(1)} %copy-done.3, s32[4,1024]{1,0:T(4,128)S(1)} %copy-done.2, bf16[2,32,4096]{2,1,0:T(8,128)(2,1)S(1)} %collective-permute-done.5.query_ref.grad_ref, ...), custom_call_target="tpu_custom_call", output_to_operand_aliasing={{1}: (8, {}), {0}: (9, {})} | custom-call | flops 50331648 | bytes 393216 | tf_op jit(solution)/shard_map/attend/pallas_call | solution.py:247
  56.0 4.4 %attend.7 = (bf16[128,32,128]{2,1,0:T(8,128)(2,1)}, f32[2,384,512]{2,1,0:T(8,128)S(1)}) custom-call(s32[2]{0:T(128)S(1)} %copy-done.4, s32[4]{0:T(128)S(1)} %copy-done.3, s32[4,1024]{1,0:T(4,128)S(1)} %copy-done.2, bf16[2,32,4096]{2,1,0:T(8,128)(2,1)S(1)} %collective-permute-done.4.query_ref.grad_ref, ...), custom_call_target="tpu_custom_call", output_to_operand_aliasing={{1}: (8, {}), {0}: (9, {})} | custom-call | flops 50331648 | bytes 393216 | tf_op jit(solution)/shard_map/attend/pallas_call | solution.py:247
  60.4 2.6 %attend.8 = (bf16[128,32,128]{2,1,0:T(8,128)(2,1)}, f32[2,128,256]{2,1,0:T(8,128)S(1)}, bf16[2,128,256]{2,1,0:T(8,128)(2,1)S(1)}, bf16[2,128,256]{2,1,0:T(8,128)(2,1)S(1)}) custom-call(s32[2]{0:T(128)S(1)} %copy-done.4, s32[4]{0:T(128)S(1)} %copy-done.3, s32[4,1024]{1,0:T(4,128)S(1)} %copy-done.2, ...), custom_call_target="tpu_custom_call", output_to_operand_aliasing={{0}: (9, {})} | custom-call | flops 25165824 | bytes 196608 | tf_op jit(solution)/shard_map/attend/pallas_call | solution.py:247
  63.0 5.2 %collective-permute-start.6 = (bf16[2,128,256]{2,1,0:T(8,128)(2,1)S(1)}, bf16[2,128,256]{2,1,0:T(8,128)(2,1)S(1)}, u32[]{:S(2)}, u32[]{:S(2)}) collective-permute-start(bf16[2,128,256]{2,1,0:T(8,128)(2,1)S(1)} %get-tuple-element.36), channel_id=1, source_target_pairs={{4,0},{8,4},{12,8},{16,12},{20,16},{24,20},{28,24},{5,1},{9,5},{13... | collective-permute-start | bytes 393224 | tf_op jit(solution)/shard_map/ppermute | solution.py:33
  68.2 1.9 %collective-permute-start.7 = (bf16[2,128,256]{2,1,0:T(8,128)(2,1)S(1)}, bf16[2,128,256]{2,1,0:T(8,128)(2,1)S(1)}, u32[]{:S(2)}, u32[]{:S(2)}) collective-permute-start(bf16[2,128,256]{2,1,0:T(8,128)(2,1)S(1)} %get-tuple-element.37), channel_id=1, source_target_pairs={{8,0},{12,4},{16,8},{20,12},{24,16},{28,20},{9,1},{13,5},{17,9},{2... | collective-permute-start | bytes 393224 | tf_op jit(solution)/shard_map/ppermute | solution.py:33
  70.1 4.3 %collective-permute-done.7 = bf16[2,128,256]{2,1,0:T(8,128)(2,1)S(1)} collective-permute-done((bf16[2,128,256]{2,1,0:T(8,128)(2,1)S(1)}, bf16[2,128,256]{2,1,0:T(8,128)(2,1)S(1)}, u32[]{:S(2)}, u32[]{:S(2)}) %collective-permute-start.7) | collective-permute-done | bytes 131104 | tf_op jit(solution)/shard_map/ppermute | solution.py:33
  74.5 2.6 %attend.9 = (bf16[128,32,128]{2,1,0:T(8,128)(2,1)}, f32[2,128,256]{2,1,0:T(8,128)S(1)}, bf16[2,128,256]{2,1,0:T(8,128)(2,1)S(1)}, bf16[2,128,256]{2,1,0:T(8,128)(2,1)S(1)}) custom-call(s32[2]{0:T(128)S(1)} %copy-done.4, s32[4]{0:T(128)S(1)} %copy-done.3, s32[4,1024]{1,0:T(4,128)S(1)} %copy-done.2, ...), custom_call_target="tpu_custom_call", output_to_operand_aliasing={{0}: (9, {})} | custom-call | flops 25165824 | bytes 196608 | tf_op jit(solution)/shard_map/attend/pallas_call | solution.py:247
  77.0 1.9 %collective-permute-start.8 = (bf16[2,128,256]{2,1,0:T(8,128)(2,1)S(1)}, bf16[2,128,256]{2,1,0:T(8,128)(2,1)S(1)}, u32[]{:S(2)}, u32[]{:S(2)}) collective-permute-start(bf16[2,128,256]{2,1,0:T(8,128)(2,1)S(1)} %get-tuple-element.43), channel_id=1, source_target_pairs={{4,0},{8,4},{12,8},{16,12},{20,16},{24,20},{28,24},{5,1},{9,5},{13... | collective-permute-start | bytes 393224 | tf_op jit(solution)/shard_map/ppermute | solution.py:33
  79.0 1.9 %collective-permute-start.9 = (bf16[2,128,256]{2,1,0:T(8,128)(2,1)S(1)}, bf16[2,128,256]{2,1,0:T(8,128)(2,1)S(1)}, u32[]{:S(2)}, u32[]{:S(2)}) collective-permute-start(bf16[2,128,256]{2,1,0:T(8,128)(2,1)S(1)} %get-tuple-element.44), channel_id=1, source_target_pairs={{8,0},{12,4},{16,8},{20,12},{24,16},{28,20},{9,1},{13,5},{17,9},{2... | collective-permute-start | bytes 393224 | tf_op jit(solution)/shard_map/ppermute | solution.py:33
  80.9 1.8 %collective-permute-done.8 = bf16[2,128,256]{2,1,0:T(8,128)(2,1)S(1)} collective-permute-done((bf16[2,128,256]{2,1,0:T(8,128)(2,1)S(1)}, bf16[2,128,256]{2,1,0:T(8,128)(2,1)S(1)}, u32[]{:S(2)}, u32[]{:S(2)}) %collective-permute-start.8) | collective-permute-done | bytes 131104 | tf_op jit(solution)/shard_map/ppermute | solution.py:33
  82.7 2.5 %collective-permute-done.9 = bf16[2,128,256]{2,1,0:T(8,128)(2,1)S(1)} collective-permute-done((bf16[2,128,256]{2,1,0:T(8,128)(2,1)S(1)}, bf16[2,128,256]{2,1,0:T(8,128)(2,1)S(1)}, u32[]{:S(2)}, u32[]{:S(2)}) %collective-permute-start.9) | collective-permute-done | bytes 131104 | tf_op jit(solution)/shard_map/ppermute | solution.py:33
  85.3 0.7 pad_maximum_fusion
  (21 shorter events, 0.2 us)
Async XLA Ops:
  3.8 43.6 %copy-start = (bf16[4,32,4096]{2,1,0:T(8,128)(2,1)S(1)}, bf16[4,32,4096]{2,1,0:T(8,128)(2,1)}, u32[]{:S(2)}) copy-start(bf16[4,32,4096]{2,1,0:T(8,128)(2,1)} %query_ref.1) | copy-start | bytes 3145732
  3.8 43.6 %copy-start.1 = (bf16[4,32,4096]{2,1,0:T(8,128)(2,1)S(1)}, bf16[4,32,4096]{2,1,0:T(8,128)(2,1)}, u32[]{:S(2)}) copy-start(bf16[4,32,4096]{2,1,0:T(8,128)(2,1)} %grad_ref.1) | copy-start | bytes 3145732
  3.8 43.6 %copy-start.2 = (s32[4,1024]{1,0:T(4,128)S(1)}, s32[4,1024]{1,0:T(4,128)}, u32[]{:S(2)}) copy-start(s32[4,1024]{1,0:T(4,128)} %segment_ref.9) | copy-start | bytes 49156
  3.8 43.6 %copy-start.3 = (s32[4]{0:T(128)S(1)}, s32[4]{0:T(128)}, u32[]{:S(2)}) copy-start(s32[4]{0:T(128)} %assign_ref.13) | copy-start | bytes 52
  3.8 43.6 %copy-start.4 = (s32[2]{0:T(128)S(1)}, s32[2]{0:T(128)}, u32[]{:S(2)}) copy-start(s32[2]{0:T(128)} %pad_add_fusion.meta_ref) | copy-start | bytes 28
  6.9 13.1 %all-to-all-start = ((bf16[4,2,32,512]{3,2,1,0:T(8,128)(2,1)}), bf16[4,2,32,512]{3,2,1,0:T(8,128)(2,1)S(1)}, u32[]{:S(2)}, u32[]{:S(2)}) async-start(bf16[4,2,32,512]{3,2,1,0:T(8,128)(2,1)} %get-tuple-element.25), calls=%async_computation | async-start | bytes 524288 | tf_op jit(solution)/shard_map/all_to_all | solution.py:291
  12.4 39.2 %collective-permute-start.5 = (bf16[2,32,4096]{2,1,0:T(8,128)(2,1)}, bf16[2,32,4096]{2,1,0:T(8,128)(2,1)S(1)}, u32[]{:S(2)}, u32[]{:S(2)}) collective-permute-start(bf16[2,32,4096]{2,1,0:T(8,128)(2,1)} %stage.2.refs_4_), channel_id=1, source_target_pairs={{0,1},{1,2},{2,3},{3,0},{4,5},{5,6},{6,7},{7,4},{8,9},{9,10},{10,1... | collective-permute-start | bytes 1572872 | tf_op jit(solution)/shard_map/ppermute | solution.py:27
  13.8 42.2 %collective-permute-start.4 = (bf16[2,32,4096]{2,1,0:T(8,128)(2,1)}, bf16[2,32,4096]{2,1,0:T(8,128)(2,1)S(1)}, u32[]{:S(2)}, u32[]{:S(2)}) collective-permute-start(bf16[2,32,4096]{2,1,0:T(8,128)(2,1)} %get-tuple-element.29), channel_id=1, source_target_pairs={{0,3},{1,0},{2,1},{3,2},{4,7},{5,4},{6,5},{7,6},{8,11},{9,8},{10,9... | collective-permute-start | bytes 1572872 | tf_op jit(solution)/shard_map/ppermute | solution.py:27
  20.0 31.6 %copy-start.5 = (bf16[2,32,2048]{2,1,0:T(8,128)(2,1)S(1)}, bf16[2,32,2048]{2,1,0:T(8,128)(2,1)}, u32[]{:S(2)}) copy-start(bf16[2,32,2048]{2,1,0:T(8,128)(2,1)} %get-tuple-element.27) | copy-start | bytes 786436
  20.0 21.0 %collective-permute-start.1 = (bf16[4,2,32,512]{3,2,1,0:T(8,128)(2,1)S(1)}, bf16[4,2,32,512]{3,2,1,0:T(8,128)(2,1)S(1)}, u32[]{:S(2)}, u32[]{:S(2)}) collective-permute-start(bf16[4,2,32,512]{3,2,1,0:T(8,128)(2,1)S(1)} %all-to-all-done.refs_0_), channel_id=1, source_target_pairs={{0,8},{4,12},{8,16},{12,20},{16,24},{20,28},{1,9},{5,13},{9,17},{1... | collective-permute-start | bytes 786440 | tf_op jit(solution)/shard_map/ppermute | solution.py:33
  37.7 9.7 %collective-permute-start = (bf16[4,2,32,512]{3,2,1,0:T(8,128)(2,1)S(1)}, bf16[4,2,32,512]{3,2,1,0:T(8,128)(2,1)S(1)}, u32[]{:S(2)}, u32[]{:S(2)}) collective-permute-start(bf16[4,2,32,512]{3,2,1,0:T(8,128)(2,1)S(1)} %all-to-all-done.refs_0_), channel_id=1, source_target_pairs={{0,4},{4,8},{8,12},{12,16},{16,20},{20,24},{24,28},{1,5},{5,9},{9,... | collective-permute-start | bytes 786440 | tf_op jit(solution)/shard_map/ppermute | solution.py:33
  40.8 19.6 %collective-permute-start.3 = (bf16[2,32,2048]{2,1,0:T(8,128)(2,1)}, bf16[2,32,2048]{2,1,0:T(8,128)(2,1)S(1)}, u32[]{:S(2)}, u32[]{:S(2)}) collective-permute-start(bf16[2,32,2048]{2,1,0:T(8,128)(2,1)} %get-tuple-element.28), channel_id=1, source_target_pairs={{0,2},{1,3},{2,0},{3,1},{4,6},{5,7},{6,4},{7,5},{8,10},{9,11},{10,... | collective-permute-start | bytes 786440 | tf_op jit(solution)/shard_map/ppermute | solution.py:27
  51.6 22.9 %collective-permute-start.2 = (bf16[2,32,2048]{2,1,0:T(8,128)(2,1)S(1)}, bf16[2,32,2048]{2,1,0:T(8,128)(2,1)S(1)}, u32[]{:S(2)}, u32[]{:S(2)}) collective-permute-start(bf16[2,32,2048]{2,1,0:T(8,128)(2,1)S(1)} %copy-done.5), channel_id=1, source_target_pairs={{0,2},{1,3},{2,0},{3,1},{4,6},{5,7},{6,4},{7,5},{8,10},{9,11},{10,... | collective-permute-start | bytes 786440 | tf_op jit(solution)/shard_map/ppermute | solution.py:27
  63.0 7.1 %collective-permute-start.6 = (bf16[2,128,256]{2,1,0:T(8,128)(2,1)S(1)}, bf16[2,128,256]{2,1,0:T(8,128)(2,1)S(1)}, u32[]{:S(2)}, u32[]{:S(2)}) collective-permute-start(bf16[2,128,256]{2,1,0:T(8,128)(2,1)S(1)} %get-tuple-element.36), channel_id=1, source_target_pairs={{4,0},{8,4},{12,8},{16,12},{20,16},{24,20},{28,24},{5,1},{9,5},{13... | collective-permute-start | bytes 393224 | tf_op jit(solution)/shard_map/ppermute | solution.py:33
  68.2 6.3 %collective-permute-start.7 = (bf16[2,128,256]{2,1,0:T(8,128)(2,1)S(1)}, bf16[2,128,256]{2,1,0:T(8,128)(2,1)S(1)}, u32[]{:S(2)}, u32[]{:S(2)}) collective-permute-start(bf16[2,128,256]{2,1,0:T(8,128)(2,1)S(1)} %get-tuple-element.37), channel_id=1, source_target_pairs={{8,0},{12,4},{16,8},{20,12},{24,16},{28,20},{9,1},{13,5},{17,9},{2... | collective-permute-start | bytes 393224 | tf_op jit(solution)/shard_map/ppermute | solution.py:33
  77.0 5.7 %collective-permute-start.8 = (bf16[2,128,256]{2,1,0:T(8,128)(2,1)S(1)}, bf16[2,128,256]{2,1,0:T(8,128)(2,1)S(1)}, u32[]{:S(2)}, u32[]{:S(2)}) collective-permute-start(bf16[2,128,256]{2,1,0:T(8,128)(2,1)S(1)} %get-tuple-element.43), channel_id=1, source_target_pairs={{4,0},{8,4},{12,8},{16,12},{20,16},{24,20},{28,24},{5,1},{9,5},{13... | collective-permute-start | bytes 393224 | tf_op jit(solution)/shard_map/ppermute | solution.py:33
  79.0 6.3 %collective-permute-start.9 = (bf16[2,128,256]{2,1,0:T(8,128)(2,1)S(1)}, bf16[2,128,256]{2,1,0:T(8,128)(2,1)S(1)}, u32[]{:S(2)}, u32[]{:S(2)}) collective-permute-start(bf16[2,128,256]{2,1,0:T(8,128)(2,1)S(1)} %get-tuple-element.44), channel_id=1, source_target_pairs={{8,0},{12,4},{16,8},{20,12},{24,16},{28,20},{9,1},{13,5},{17,9},{2... | collective-permute-start | bytes 393224 | tf_op jit(solution)/shard_map/ppermute | solution.py:33

commit v6 on v5

v6 whole, which is shorter than its diff:
```python
import functools

import jax
import jax.numpy as jnp
from jax import lax
from jax.experimental import pallas as pl
from jax.experimental.pallas import tpu as pltpu
from jax.sharding import PartitionSpec as P

HD = 128
LOG2E = 1.4426950408889634
BIG_NEGATIVE = -1e30
VMEM_BYTES = 32 * 1024 * 1024
HEADS_STEP = 2
STAGE_COST = 30_000_000_000


def target_of(index, step, count):
    return lax.rem(index + step, count)


def source_of(index, step, count):
    return lax.rem(index + count - step, count)


def exchanged(value, axis, step):
    count = lax.axis_size(axis)
    return lax.ppermute(value, axis, [(i, (i + step) % count) for i in range(count)])


def shifted(value, axis, by):
    length = lax.axis_size(axis)
    pairs = [(i, i + by) for i in range(length) if 0 <= i + by < length]
    return lax.ppermute(value, axis, pairs)


def stage_kernel(count, jobs, outs, meta_ref, assign_ref, *refs):
    group = meta_ref[0]
    sources, refs = refs[:4], refs[len(refs) - 2 * outs - 2 :]
    out_refs, held_refs, (in_sems, out_sems) = refs[:outs], refs[outs : 2 * outs], refs[-2:]
    loads, stores = [], []
    for slot, (source, step, start, width, out, place) in enumerate(jobs):
        other = step if len(place) > 1 else target_of(group, step, count)
        origin = sources[source].at[assign_ref[other], :, start : start + width]
        held, goal = held_refs[out].at[place], out_refs[out].at[place]
        loads.append(pltpu.make_async_copy(origin, held, in_sems.at[slot]))
        stores.append(pltpu.make_async_copy(held, goal, out_sems.at[slot]))
    for load in loads:
        load.start()
    for load, store in zip(loads, stores):
        load.wait()
        store.start()
    for store in stores:
        store.wait()


def stage(meta, assignment, arrays, parts, with_kv, cost, after=()):
    count, rows, _ = arrays[0].shape
    kv_width = arrays[2].shape[2]
    shapes, jobs = [], []
    if with_kv:
        shapes.append((count, 2, rows, kv_width))
        for other in range(count):
            jobs += [(2 + which, other, 0, kv_width, 0, (other, which)) for which in range(2)]
    for step, start, width in parts:
        jobs += [(which, step, start, width, len(shapes), (which,)) for which in range(2)]
        shapes.append((2, rows, width))
    far, scalars = pl.BlockSpec(memory_space=pltpu.HBM), pl.BlockSpec(memory_space=pltpu.SMEM)
    return pl.pallas_call(
        functools.partial(stage_kernel, count, jobs, len(shapes)),
        out_shape=[jax.ShapeDtypeStruct(shape, arrays[0].dtype) for shape in shapes],
        in_specs=[scalars] * 2 + [far] * 4 + [pl.BlockSpec(memory_space=pl.ANY)] * len(after),
        out_specs=[far] * len(shapes),
        scratch_shapes=[pltpu.VMEM(shape, arrays[0].dtype) for shape in shapes]
        + [pltpu.SemaphoreType.DMA((len(jobs),))] * 2,
        cost_estimate=pl.CostEstimate(flops=cost, bytes_accessed=cost, transcendentals=0),
        name="stage",
    )(meta, assignment, *arrays, *after)


def build_bias(source, sequence, line, segment_ref, column_ref, bias_ref, rows, tok_dev, reach):
    keys, lanes = column_ref.shape
    pieces = keys // tok_dev
    window = bias_ref.shape[0]
    eye = lax.broadcasted_iota(jnp.int32, (tok_dev, tok_dev), 0) == lax.broadcasted_iota(
        jnp.int32, (tok_dev, tok_dev), 1
    )
    for place in range(pieces):
        back = pieces - 1 - place
        start = pl.multiple_of(jnp.maximum(line - back, 0) * tok_dev, tok_dev)
        every = segment_ref[:, pl.ds(start, tok_dev)].astype(jnp.float32)
        mine = lax.broadcasted_iota(jnp.int32, every.shape, 0) == sequence
        row = jnp.sum(jnp.where(mine, every, 0.0), axis=0, keepdims=True)
        column = jnp.sum(jnp.where(eye, row, 0.0), axis=1, keepdims=True)
        column = jnp.where(line >= back, column, -1.0)
        column_ref[place * tok_dev : (place + 1) * tok_dev, :] = jnp.broadcast_to(
            column, (tok_dev, lanes)
        )

    def token(shape):
        return lax.rem(lax.broadcasted_iota(jnp.int32, shape, 1), jnp.int32(rows))

    here = pl.multiple_of(keys - tok_dev + source * rows, rows)
    asked_rows = column_ref[pl.ds(here, rows), :]
    same = lax.broadcasted_iota(jnp.int32, (rows, lanes), 0) == token((rows, lanes))
    asked = jnp.sum(jnp.where(same, asked_rows, 0.0), axis=0, keepdims=True)
    held = column_ref[pl.ds(pl.multiple_of(here - reach, rows), window), :]
    place = lax.broadcasted_iota(jnp.int32, (window, lanes), 0)
    allowed = (held == asked) & (place <= token((window, lanes)) + reach)
    bias_ref[...] = jnp.where(allowed, 0.0, BIG_NEGATIVE)


def attend_kernel(
    step, first, filled, last, tok_dev, reach, ratio,
    meta_ref, assign_ref, segment_ref, query_ref, grad_ref, kv_ref, *refs,
):
    refs = list(refs)
    if not first:
        acc_in_ref = refs.pop(0)
    if filled:
        refs.pop(0)
    query_out_ref = refs.pop(0)
    column_ref, bias_ref = refs[-2 - last], refs[-1 - last]
    if last:
        own_ref, halo_refs, acc_ref = refs[0], refs[1:-3], refs[-1]
    else:
        acc_ref = refs[0]

    rows = query_ref.shape[0]
    window = bias_ref.shape[0]
    keys = column_ref.shape[0]
    scale = 1.0 / HD**0.5
    group = meta_ref[0]
    source = source_of(group, step, tok_dev // rows)
    block = (keys - tok_dev - reach) // rows + source
    span = pl.ds(pl.multiple_of(block * rows, rows), window)

    @pl.when(pl.program_id(0) == 0)
    def _():
        build_bias(
            source, assign_ref[group], meta_ref[1], segment_ref, column_ref, bias_ref, rows, tok_dev, reach
        )

    acc_ref[...] = jnp.zeros_like(acc_ref) if first else acc_in_ref[...]
    turned = (((1,), (1,)), ((), ()))
    grads = []
    for head in range(HEADS_STEP):
        lanes = slice(head * HD, (head + 1) * HD)

        def stacked(ref):
            start = head * ratio
            return jnp.concatenate(
                [ref[:, r * HD : (r + 1) * HD] for r in range(start, start + ratio)], axis=0
            )

        def windowed(which):
            return kv_ref[pl.ds(block, window // rows), which, :, lanes].reshape(window, HD)

        query, grad = stacked(query_ref), stacked(grad_ref)
        key, value = windowed(0), windowed(1)
        scores = lax.dot_general(key, query, turned, preferred_element_type=jnp.float32)
        scores = scores * (scale * LOG2E) + bias_ref[...]
        top = jnp.max(scores, axis=0, keepdims=True)
        weights = jnp.exp2(scores - top)
        probs = weights * (1.0 / jnp.sum(weights, axis=0, keepdims=True))
        grad_probs = lax.dot_general(value, grad, turned, preferred_element_type=jnp.float32)
        product = probs * grad_probs
        delta = jnp.sum(product, axis=0, keepdims=True)
        grad_scores = (product - probs * delta).astype(jnp.bfloat16)
        grad_value = jnp.dot(
            probs.astype(jnp.bfloat16), grad, preferred_element_type=jnp.float32
        )
        grad_key = jnp.dot(grad_scores, query, preferred_element_type=jnp.float32)
        grad_query = lax.dot_general(
            grad_scores, key, (((0,), (0,)), ((), ())), preferred_element_type=jnp.float32
        )
        grads.append((grad_query * scale).reshape(ratio, rows, HD))
        acc_ref[0, span, lanes] += grad_key
        acc_ref[1, span, lanes] += grad_value
    if last:
        own_ref[0] = acc_ref[0, keys - tok_dev :] * scale
        own_ref[1] = acc_ref[1, keys - tok_dev :]
        for back, halo_ref in enumerate(halo_refs, 1):
            part = slice(keys - (back + 1) * tok_dev, keys - back * tok_dev)
            halo_ref[0] = (acc_ref[0, part] * scale).astype(jnp.bfloat16)
            halo_ref[1] = acc_ref[1, part].astype(jnp.bfloat16)
    query_out_ref[...] = jnp.swapaxes(jnp.concatenate(grads, axis=0), 0, 1).astype(jnp.bfloat16)


def attend(step, base, span, reach, heads, meta, assignment, segments, query, grad, kv, acc, full, last):
    first, filled = acc is None, full is not None
    rows, (blocks, _, _, kv_width) = query[0].shape[1], kv.shape
    ratio = heads // (kv_width // HD)
    keys, tok_dev = blocks * rows, query[0].shape[1] * lax.axis_size("dp")
    pieces, window = keys // tok_dev, reach + rows
    lanes, place = HEADS_STEP * HD, base // HEADS_STEP

    def rows_spec(array, pick):
        start = place if array.shape[2] == heads * HD else 0
        return pl.BlockSpec(
            (None, rows, HEADS_STEP * ratio * HD), lambda c, m, a: (pick(m, a), 0, start + c)
        )

    in_specs = [
        pl.BlockSpec(segments.shape, lambda c, m, a: (0, 0)),
        rows_spec(*query),
        rows_spec(*grad),
    ]
    in_specs.append(pl.BlockSpec((blocks, 2, rows, lanes), lambda c, m, a: (0, 0, 0, place + c)))
    operands = [meta, assignment, segments, query[0], grad[0], kv]
    aliases = {}
    acc_spec = pl.BlockSpec((2, keys, lanes), lambda c, m, a: (0, 0, place + c))
    if not first:
        if not last:
            aliases[len(operands)] = 1
        operands.append(acc)
        in_specs.append(acc_spec)
    if filled:
        aliases[len(operands)] = 0
        operands.append(full)
        in_specs.append(pl.BlockSpec(memory_space=pl.ANY))
    out_shape = [jax.ShapeDtypeStruct((tok_dev, heads, HD), jnp.bfloat16)]
    out_specs = [
        pl.BlockSpec(
            (rows, HEADS_STEP * ratio, HD),
            lambda c, m, a: (source_of(m[0], step, tok_dev // rows), place + c, 0),
        )
    ]
    if last:
        span_spec = pl.BlockSpec((2, tok_dev, lanes), lambda c, m, a: (0, 0, c))
        out_shape.append(jax.ShapeDtypeStruct((2, tok_dev, span * HD), jnp.float32))
        out_shape += [jax.ShapeDtypeStruct((2, tok_dev, span * HD), jnp.bfloat16)] * (pieces - 1)
        out_specs += [span_spec] * pieces
    else:
        out_shape.append(jax.ShapeDtypeStruct((2, keys, kv_width), jnp.float32))
        out_specs.append(acc_spec)
    pairs = span * ratio * rows * window
    held = (keys, ratio * rows), (window, ratio * rows)
    held += ((2, keys, lanes),) * last
    return pl.pallas_call(
        functools.partial(attend_kernel, step, first, filled, last, tok_dev, reach, ratio),
        out_shape=out_shape,
        grid_spec=pltpu.PrefetchScalarGridSpec(
            num_scalar_prefetch=2,
            grid=(span // HEADS_STEP,),
            in_specs=in_specs,
            out_specs=out_specs,
            scratch_shapes=[pltpu.VMEM(shape, jnp.float32) for shape in held],
        ),
        input_output_aliases=aliases,
        compiler_params=pltpu.CompilerParams(
            dimension_semantics=("arbitrary",), vmem_limit_bytes=VMEM_BYTES
        ),
        cost_estimate=pl.CostEstimate(
            flops=pairs * HD, bytes_accessed=pairs, transcendentals=0
        ),
        name="attend",
    )(*operands)


def shards(queries, keys, values, grad_out, segment_ids, assignment):
    count = lax.axis_size("dp")
    uly = lax.axis_size("uly")
    group = lax.axis_index("dp")
    line = lax.axis_index("blk") * uly + lax.axis_index("uly")
    width, kv_width = queries.shape[2], keys.shape[2]
    heads, kv_heads = width // HD, kv_width // HD
    tok_dev = count * queries.shape[1]
    doc_most = min(512, tok_dev * uly)
    hops = -(-doc_most // tok_dev)
    meta = jnp.stack([group, line]).astype(jnp.int32)

    arrays = (queries, grad_out, keys, values)
    parts = [(step, 0, width) for step in range(1, count)]
    ahead = stage(meta, assignment, arrays, parts[:1], False, 1)
    kv_out, *behind = stage(meta, assignment, arrays, parts[1:], True, STAGE_COST, after=ahead)
    arrived = [exchanged(ahead[0], "dp", 1)]
    kv_own = lax.all_to_all(kv_out, "dp", split_axis=0, concat_axis=0, tiled=True)
    behind, kv_own = lax.optimization_barrier((behind, kv_own))
    arrived += [exchanged(rows, "dp", step) for rows, (step, _, _) in zip(behind, parts[1:])]
    halos = [shifted(kv_own, ("blk", "uly"), back) for back in range(hops, 0, -1)]
    kv = jnp.concatenate([*halos, kv_own], axis=0)

    fixed = (doc_most, heads, meta, assignment, segment_ids)
    query, grad = (queries, lambda m, a: a[m[0]]), (grad_out, lambda m, a: a[m[0]])
    full, acc = attend(0, 0, kv_heads, *fixed, query, grad, kv, None, None, False)
    for both, (step, _, _) in zip(arrived, parts):
        query, grad = (both, lambda m, a: 0), (both, lambda m, a: 1)
        full, acc, *returned = attend(
            step, 0, kv_heads, *fixed, query, grad, kv, acc, full, step == count - 1
        )
    for back, halo in enumerate(returned, 1):
        acc = acc + shifted(halo, ("blk", "uly"), -back).astype(jnp.float32)
    total = acc.astype(jnp.bfloat16)
    return full[None], total[0][None], total[1][None]


def solution(mesh):
    in_specs = (
        P(None, ("blk", "uly", "dp"), None),
        P(None, ("blk", "uly", "dp"), None),
        P(None, ("blk", "uly", "dp"), None),
        P(None, ("blk", "uly", "dp"), None),
        P(),
        P(),
    )
    out_specs = (
        P("dp", ("blk", "uly"), None, None),
        P("dp", ("blk", "uly"), None),
        P("dp", ("blk", "uly"), None),
    )
    return jax.shard_map(shards, mesh=mesh, in_specs=in_specs, out_specs=out_specs, check_vma=False)
```

time: 86.4 us -> 89.5 us (1.036)
  the two profiles are of different devices: /device:TPU:1 before, /device:TPU:27 now
where the time goes in v6:
time: 89.5 us; the launch traced here: 89.1 us
  waiting for transfers between devices  40.7 us (45%)
  Pallas kernels  21.5 us (24%)
  starting transfers between devices  13.3 us (15%)
  blocking collectives  11.3 us (13%)
    ppermute x3, waiting for transfers between devices, exchanged(): lax.ppermute(value, axis, [(i, (i + step) % count) for i in range(count)])  25.7 us
    pallas_call x4, Pallas kernels, attend(): pl.pallas_call(functools.partial(attend_kernel, step, first, filled, last...  15.9 us
    ppermute x4, waiting for transfers between devices, shifted(): return lax.ppermute(value, axis, pairs)  15 us
    all_to_all x1, blocking collectives, shards(): lax.all_to_all(kv_out, 'dp', split_axis=0, concat_axis=0, tiled=True)  11.3 us
    ppermute x4, starting transfers between devices, shifted(): return lax.ppermute(value, axis, pairs)  10.8 us
    pallas_call x2, Pallas kernels, stage(): pl.pallas_call(functools.partial(stage_kernel, count, jobs, len(shapes)),...  5.56 us
    ppermute x3, starting transfers between devices, exchanged(): lax.ppermute(value, axis, [(i, (i + step) % count) for i in range(count)])  2.5 us
  transfers between devices with their start and end apart: 7, of which 4 were waited for; matrix products, arithmetic and copies ran while one was open for 0% of the time, Pallas kernels for 13%

profile of v6, /device:TPU:27, one launch (start us, length us, event | category | flops | bytes accessed | tf_op | source)
XLA Modules:
  0.0 89.1 jit_solution(8280347287461577623)
XLA Ops:
  0.6 0.6 pad_add_fusion.meta_ref
  1.3 2.5 %stage.2.refs_4_ = bf16[2,32,4096]{2,1,0:T(8,128)(2,1)} custom-call(s32[2]{0:T(128)} %pad_add_fusion.meta_ref, s32[4]{0:T(128)} %assign_ref.11, bf16[4,32,4096]{2,1,0:T(8,128)(2,1)} %query_ref.1, bf16[4,32,4096]{2,1,0:T(8,128)(2,1)} %grad_ref.1, bf16[4,32,512]{2,1,0:T(8,128)(2,1)} %refs_2_.3, bf16[4,32,512]{2,1,0:T(8,128)(2,1)} %refs_3_.3), custom_call_target="tpu_custom_call" | custom-call | flops 1 | bytes 1 | tf_op jit(solution)/shard_map/stage/pallas_call | solution.py:69
  3.7 0.0 copy-start.5
  3.8 0.0 copy-start.2
  3.8 3.1 %stage.3 = (bf16[4,2,32,512]{3,2,1,0:T(8,128)(2,1)}, bf16[2,32,4096]{2,1,0:T(8,128)(2,1)}, bf16[2,32,4096]{2,1,0:T(8,128)(2,1)}) custom-call(s32[2]{0:T(128)} %pad_add_fusion.meta_ref, s32[4]{0:T(128)} %assign_ref.11, bf16[4,32,4096]{2,1,0:T(8,128)(2,1)} %query_ref.1, bf16[4,32,4096]{2,1,0:T(8,128)(2,1)} %grad_ref.1, bf16[4,32,512]{2,1,0:T(8,128)(2,1)} %refs_2_.3, ...), custom_call_target="tpu_custom_call" | custom-call | flops 30000001024 | bytes 30000001024 | tf_op jit(solution)/shard_map/stage/pallas_call | solution.py:69
  6.9 0.0 copy-start
  6.9 0.0 copy-start.1
  6.9 11.3 %all_to_all.5 = bf16[4,2,32,512]{3,2,1,0:T(8,128)(2,1)S(1)} all-to-all(bf16[4,2,32,512]{3,2,1,0:T(8,128)(2,1)} %get-tuple-element.21), channel_id=1, replica_groups=mesh['blk'=4,'uly'=2,'dp'=4] {'dp'}, dimensions={0} | all-to-all | bytes 524288 | tf_op jit(solution)/shard_map/all_to_all | solution.py:278
  18.2 4.2 %collective-permute-start.1 = (bf16[4,2,32,512]{3,2,1,0:T(8,128)(2,1)S(1)}, bf16[4,2,32,512]{3,2,1,0:T(8,128)(2,1)S(1)}, u32[]{:S(2)}, u32[]{:S(2)}) collective-permute-start(bf16[4,2,32,512]{3,2,1,0:T(8,128)(2,1)S(1)} %all_to_all.5), channel_id=1, source_target_pairs={{0,8},{4,12},{8,16},{12,20},{16,24},{20,28},{1,9},{5,13},{9,17},{1... | collective-permute-start | bytes 786440 | tf_op jit(solution)/shard_map/ppermute | solution.py:34
  22.4 2.1 %collective-permute-start.4 = (bf16[2,32,4096]{2,1,0:T(8,128)(2,1)S(1)}, bf16[2,32,4096]{2,1,0:T(8,128)(2,1)S(1)}, u32[]{:S(2)}, u32[]{:S(2)}) collective-permute-start(bf16[2,32,4096]{2,1,0:T(8,128)(2,1)S(1)} %copy-done.5), channel_id=1, source_target_pairs={{0,1},{1,2},{2,3},{3,0},{4,5},{5,6},{6,7},{7,4},{8,9},{9,10},{10,1... | collective-permute-start | bytes 1572872 | tf_op jit(solution)/shard_map/ppermute | solution.py:28
  24.5 0.4 collective-permute-start
  24.9 2.6 %collective-permute-start.2 = (bf16[4,2,32,512]{3,2,1,0:T(8,128)(2,1)S(1)}, bf16[4,2,32,512]{3,2,1,0:T(8,128)(2,1)S(1)}, u32[]{:S(2)}, u32[]{:S(2)}) collective-permute-start(bf16[4,2,32,512]{3,2,1,0:T(8,128)(2,1)S(1)} %all_to_all.5), channel_id=1, source_target_pairs={{0,4},{4,8},{8,12},{12,16},{16,20},{20,24},{24,28},{1,5},{5,9},{9,... | collective-permute-start | bytes 786440 | tf_op jit(solution)/shard_map/ppermute | solution.py:34
  27.5 7.0 %collective-permute-done.2 = bf16[4,2,32,512]{3,2,1,0:T(8,128)(2,1)S(1)} collective-permute-done((bf16[4,2,32,512]{3,2,1,0:T(8,128)(2,1)S(1)}, bf16[4,2,32,512]{3,2,1,0:T(8,128)(2,1)S(1)}, u32[]{:S(2)}, u32[]{:S(2)}) %collective-permute-start.2) | collective-permute-done | bytes 262176 | tf_op jit(solution)/shard_map/ppermute | solution.py:34
  34.6 3.9 %attend.4 = (bf16[128,32,128]{2,1,0:T(8,128)(2,1)}, f32[2,384,512]{2,1,0:T(8,128)S(1)}) custom-call(s32[2]{0:T(128)S(1)} %copy-done.4, s32[4]{0:T(128)S(1)} %copy-done.3, s32[4,1024]{1,0:T(4,128)S(1)} %copy-done.2, bf16[4,32,4096]{2,1,0:T(8,128)(2,1)S(1)} %copy-done, bf16[4,32,4096]{2,1,0:T(8,128)(2,1)S(1)} %copy-done.1, ...), custom_call_target="tpu_custom_call" | custom-call | flops 37748736 | bytes 294912 | tf_op jit(solution)/shard_map/attend/pallas_call | solution.py:240
  38.6 3.9 %attend.5 = (bf16[128,32,128]{2,1,0:T(8,128)(2,1)}, f32[2,384,512]{2,1,0:T(8,128)S(1)}) custom-call(s32[2]{0:T(128)S(1)} %copy-done.4, s32[4]{0:T(128)S(1)} %copy-done.3, s32[4,1024]{1,0:T(4,128)S(1)} %copy-done.2, bf16[2,32,4096]{2,1,0:T(8,128)(2,1)S(1)} %collective-permute-done.4.query_ref.grad_ref, ...), custom_call_target="tpu_custom_call", output_to_operand_aliasing={{1}: (6, {}), {0}: (7, {})} | custom-call | flops 37748736 | bytes 294912 | tf_op jit(solution)/shard_map/attend/pallas_call | solution.py:240
  42.5 25.7 %collective-permute-done.3.query_ref.grad_ref = bf16[2,32,4096]{2,1,0:T(8,128)(2,1)S(1)} collective-permute-done((bf16[2,32,4096]{2,1,0:T(8,128)(2,1)}, bf16[2,32,4096]{2,1,0:T(8,128)(2,1)S(1)}, u32[]{:S(2)}, u32[]{:S(2)}) %collective-permute-start.3) | collective-permute-done | bytes 524320 | tf_op jit(solution)/shard_map/ppermute | solution.py:28
  68.2 3.9 %attend.6 = (bf16[128,32,128]{2,1,0:T(8,128)(2,1)}, f32[2,384,512]{2,1,0:T(8,128)S(1)}) custom-call(s32[2]{0:T(128)S(1)} %copy-done.4, s32[4]{0:T(128)S(1)} %copy-done.3, s32[4,1024]{1,0:T(4,128)S(1)} %copy-done.2, bf16[2,32,4096]{2,1,0:T(8,128)(2,1)S(1)} %collective-permute-done.3.query_ref.grad_ref, ...), custom_call_target="tpu_custom_call", output_to_operand_aliasing={{1}: (6, {}), {0}: (7, {})} | custom-call | flops 37748736 | bytes 294912 | tf_op jit(solution)/shard_map/attend/pallas_call | solution.py:240
  72.1 4.1 %attend.7 = (bf16[128,32,128]{2,1,0:T(8,128)(2,1)}, f32[2,128,512]{2,1,0:T(8,128)S(1)}, bf16[2,128,512]{2,1,0:T(8,128)(2,1)S(1)}, bf16[2,128,512]{2,1,0:T(8,128)(2,1)S(1)}) custom-call(s32[2]{0:T(128)S(1)} %copy-done.4, s32[4]{0:T(128)S(1)} %copy-done.3, s32[4,1024]{1,0:T(4,128)S(1)} %copy-done.2, ...), custom_call_target="tpu_custom_call", output_to_operand_aliasing={{0}: (7, {})} | custom-call | flops 37748736 | bytes 294912 | tf_op jit(solution)/shard_map/attend/pallas_call | solution.py:240
  76.2 2.2 %collective-permute-start.5 = (bf16[2,128,512]{2,1,0:T(8,128)(2,1)S(1)}, bf16[2,128,512]{2,1,0:T(8,128)(2,1)S(1)}, u32[]{:S(2)}, u32[]{:S(2)}) collective-permute-start(bf16[2,128,512]{2,1,0:T(8,128)(2,1)S(1)} %get-tuple-element.33), channel_id=1, source_target_pairs={{4,0},{8,4},{12,8},{16,12},{20,16},{24,20},{28,24},{5,1},{9,5},{13... | collective-permute-start | bytes 786440 | tf_op jit(solution)/shard_map/ppermute | solution.py:34
  78.4 1.9 %collective-permute-start.6 = (bf16[2,128,512]{2,1,0:T(8,128)(2,1)S(1)}, bf16[2,128,512]{2,1,0:T(8,128)(2,1)S(1)}, u32[]{:S(2)}, u32[]{:S(2)}) collective-permute-start(bf16[2,128,512]{2,1,0:T(8,128)(2,1)S(1)} %get-tuple-element.34), channel_id=1, source_target_pairs={{8,0},{12,4},{16,8},{20,12},{24,16},{28,20},{9,1},{13,5},{17,9},{2... | collective-permute-start | bytes 786440 | tf_op jit(solution)/shard_map/ppermute | solution.py:34
  80.3 5.5 %collective-permute-done.5 = bf16[2,128,512]{2,1,0:T(8,128)(2,1)S(1)} collective-permute-done((bf16[2,128,512]{2,1,0:T(8,128)(2,1)S(1)}, bf16[2,128,512]{2,1,0:T(8,128)(2,1)S(1)}, u32[]{:S(2)}, u32[]{:S(2)}) %collective-permute-start.5) | collective-permute-done | bytes 262176 | tf_op jit(solution)/shard_map/ppermute | solution.py:34
  85.8 2.5 %collective-permute-done.6 = bf16[2,128,512]{2,1,0:T(8,128)(2,1)S(1)} collective-permute-done((bf16[2,128,512]{2,1,0:T(8,128)(2,1)S(1)}, bf16[2,128,512]{2,1,0:T(8,128)(2,1)S(1)}, u32[]{:S(2)}, u32[]{:S(2)}) %collective-permute-start.6) | collective-permute-done | bytes 262176 | tf_op jit(solution)/shard_map/ppermute | solution.py:34
  88.3 0.1 add_convert_fusion
  88.4 0.7 fusion
  (15 shorter events, 0.1 us)
Async XLA Ops:
  3.7 18.6 %copy-start.5 = (bf16[2,32,4096]{2,1,0:T(8,128)(2,1)S(1)}, bf16[2,32,4096]{2,1,0:T(8,128)(2,1)}, u32[]{:S(2)}) copy-start(bf16[2,32,4096]{2,1,0:T(8,128)(2,1)} %stage.2.refs_4_) | copy-start | bytes 1572868
  3.8 30.8 %copy-start.2 = (s32[4,1024]{1,0:T(4,128)S(1)}, s32[4,1024]{1,0:T(4,128)}, u32[]{:S(2)}) copy-start(s32[4,1024]{1,0:T(4,128)} %segment_ref.7) | copy-start | bytes 49156
  6.9 27.7 %copy-start = (bf16[4,32,4096]{2,1,0:T(8,128)(2,1)S(1)}, bf16[4,32,4096]{2,1,0:T(8,128)(2,1)}, u32[]{:S(2)}) copy-start(bf16[4,32,4096]{2,1,0:T(8,128)(2,1)} %query_ref.1) | copy-start | bytes 3145732
  6.9 27.7 %copy-start.1 = (bf16[4,32,4096]{2,1,0:T(8,128)(2,1)S(1)}, bf16[4,32,4096]{2,1,0:T(8,128)(2,1)}, u32[]{:S(2)}) copy-start(bf16[4,32,4096]{2,1,0:T(8,128)(2,1)} %grad_ref.1) | copy-start | bytes 3145732
  6.9 27.7 %copy-start.3 = (s32[4]{0:T(128)S(1)}, s32[4]{0:T(128)}, u32[]{:S(2)}) copy-start(s32[4]{0:T(128)} %assign_ref.11) | copy-start | bytes 52
  6.9 27.7 %copy-start.4 = (s32[2]{0:T(128)S(1)}, s32[2]{0:T(128)}, u32[]{:S(2)}) copy-start(s32[2]{0:T(128)} %pad_add_fusion.meta_ref) | copy-start | bytes 28
  18.2 9.3 %collective-permute-start.1 = (bf16[4,2,32,512]{3,2,1,0:T(8,128)(2,1)S(1)}, bf16[4,2,32,512]{3,2,1,0:T(8,128)(2,1)S(1)}, u32[]{:S(2)}, u32[]{:S(2)}) collective-permute-start(bf16[4,2,32,512]{3,2,1,0:T(8,128)(2,1)S(1)} %all_to_all.5), channel_id=1, source_target_pairs={{0,8},{4,12},{8,16},{12,20},{16,24},{20,28},{1,9},{5,13},{9,17},{1... | collective-permute-start | bytes 786440 | tf_op jit(solution)/shard_map/ppermute | solution.py:34
  22.4 16.2 %collective-permute-start.4 = (bf16[2,32,4096]{2,1,0:T(8,128)(2,1)S(1)}, bf16[2,32,4096]{2,1,0:T(8,128)(2,1)S(1)}, u32[]{:S(2)}, u32[]{:S(2)}) collective-permute-start(bf16[2,32,4096]{2,1,0:T(8,128)(2,1)S(1)} %copy-done.5), channel_id=1, source_target_pairs={{0,1},{1,2},{2,3},{3,0},{4,5},{5,6},{6,7},{7,4},{8,9},{9,10},{10,1... | collective-permute-start | bytes 1572872 | tf_op jit(solution)/shard_map/ppermute | solution.py:28
  24.5 43.7 %collective-permute-start.3 = (bf16[2,32,4096]{2,1,0:T(8,128)(2,1)}, bf16[2,32,4096]{2,1,0:T(8,128)(2,1)S(1)}, u32[]{:S(2)}, u32[]{:S(2)}) collective-permute-start(bf16[2,32,4096]{2,1,0:T(8,128)(2,1)} %get-tuple-element.24), channel_id=1, source_target_pairs={{0,2},{1,3},{2,0},{3,1},{4,6},{5,7},{6,4},{7,5},{8,10},{9,11},{10,... | collective-permute-start | bytes 1572872 | tf_op jit(solution)/shard_map/ppermute | solution.py:28
  24.5 47.6 %collective-permute-start = (bf16[2,32,4096]{2,1,0:T(8,128)(2,1)}, bf16[2,32,4096]{2,1,0:T(8,128)(2,1)S(1)}, u32[]{:S(2)}, u32[]{:S(2)}) collective-permute-start(bf16[2,32,4096]{2,1,0:T(8,128)(2,1)} %get-tuple-element.22), channel_id=1, source_target_pairs={{0,3},{1,0},{2,1},{3,2},{4,7},{5,4},{6,5},{7,6},{8,11},{9,8},{10,9... | collective-permute-start | bytes 1572872 | tf_op jit(solution)/shard_map/ppermute | solution.py:28
  24.9 9.6 %collective-permute-start.2 = (bf16[4,2,32,512]{3,2,1,0:T(8,128)(2,1)S(1)}, bf16[4,2,32,512]{3,2,1,0:T(8,128)(2,1)S(1)}, u32[]{:S(2)}, u32[]{:S(2)}) collective-permute-start(bf16[4,2,32,512]{3,2,1,0:T(8,128)(2,1)S(1)} %all_to_all.5), channel_id=1, source_target_pairs={{0,4},{4,8},{8,12},{12,16},{16,20},{20,24},{24,28},{1,5},{5,9},{9,... | collective-permute-start | bytes 786440 | tf_op jit(solution)/shard_map/ppermute | solution.py:34
  76.2 9.6 %collective-permute-start.5 = (bf16[2,128,512]{2,1,0:T(8,128)(2,1)S(1)}, bf16[2,128,512]{2,1,0:T(8,128)(2,1)S(1)}, u32[]{:S(2)}, u32[]{:S(2)}) collective-permute-start(bf16[2,128,512]{2,1,0:T(8,128)(2,1)S(1)} %get-tuple-element.33), channel_id=1, source_target_pairs={{4,0},{8,4},{12,8},{16,12},{20,16},{24,20},{28,24},{5,1},{9,5},{13... | collective-permute-start | bytes 786440 | tf_op jit(solution)/shard_map/ppermute | solution.py:34
  78.4 9.9 %collective-permute-start.6 = (bf16[2,128,512]{2,1,0:T(8,128)(2,1)S(1)}, bf16[2,128,512]{2,1,0:T(8,128)(2,1)S(1)}, u32[]{:S(2)}, u32[]{:S(2)}) collective-permute-start(bf16[2,128,512]{2,1,0:T(8,128)(2,1)S(1)} %get-tuple-element.34), channel_id=1, source_target_pairs={{8,0},{12,4},{16,8},{20,12},{24,16},{28,20},{9,1},{13,5},{17,9},{2... | collective-permute-start | bytes 786440 | tf_op jit(solution)/shard_map/ppermute | solution.py:34

commit v7 on v6

--- a/solution.py
+++ b/solution.py
@@ -12,7 +12,6 @@
 BIG_NEGATIVE = -1e30
 VMEM_BYTES = 32 * 1024 * 1024
 HEADS_STEP = 2
-STAGE_COST = 30_000_000_000
 
 
 def target_of(index, step, count):
@@ -36,13 +35,12 @@
 
 def stage_kernel(count, jobs, outs, meta_ref, assign_ref, *refs):
     group = meta_ref[0]
-    sources, refs = refs[:4], refs[len(refs) - 2 * outs - 2 :]
+    sources, refs = refs[:4], refs[4:]
     out_refs, held_refs, (in_sems, out_sems) = refs[:outs], refs[outs : 2 * outs], refs[-2:]
     loads, stores = [], []
-    for slot, (source, step, start, width, out, place) in enumerate(jobs):
-        other = step if len(place) > 1 else target_of(group, step, count)
-        origin = sources[source].at[assign_ref[other], :, start : start + width]
-        held, goal = held_refs[out].at[place], out_refs[out].at[place]
+    for slot, (source, step, out, which) in enumerate(jobs):
+        origin = sources[source].at[assign_ref[target_of(group, step, count)]]
+        held, goal = held_refs[out].at[which], out_refs[out].at[which]
         loads.append(pltpu.make_async_copy(origin, held, in_sems.at[slot]))
         stores.append(pltpu.make_async_copy(held, goal, out_sems.at[slot]))
     for load in loads:
@@ -54,28 +52,25 @@
         store.wait()
 
 
-def stage(meta, assignment, arrays, parts, with_kv, cost, after=()):
-    count, rows, _ = arrays[0].shape
-    kv_width = arrays[2].shape[2]
+def stage(meta, assignment, queries, grad_out, keys, values):
+    count, rows, _ = queries.shape
     shapes, jobs = [], []
-    if with_kv:
-        shapes.append((count, 2, rows, kv_width))
-        for other in range(count):
-            jobs += [(2 + which, other, 0, kv_width, 0, (other, which)) for which in range(2)]
-    for step, start, width in parts:
-        jobs += [(which, step, start, width, len(shapes), (which,)) for which in range(2)]
-        shapes.append((2, rows, width))
+    for first, steps in ((2, range(count)), (0, range(1, count))):
+        width = (queries, grad_out, keys, values)[first].shape[2]
+        for step in steps:
+            jobs += [(first + which, step, len(shapes), which) for which in range(2)]
+            shapes.append((2, rows, width))
     far, scalars = pl.BlockSpec(memory_space=pltpu.HBM), pl.BlockSpec(memory_space=pltpu.SMEM)
-    return pl.pallas_call(
+    staged = pl.pallas_call(
         functools.partial(stage_kernel, count, jobs, len(shapes)),
-        out_shape=[jax.ShapeDtypeStruct(shape, arrays[0].dtype) for shape in shapes],
-        in_specs=[scalars] * 2 + [far] * 4 + [pl.BlockSpec(memory_space=pl.ANY)] * len(after),
+        out_shape=[jax.ShapeDtypeStruct(shape, queries.dtype) for shape in shapes],
+        in_specs=[scalars] * 2 + [far] * 4,
         out_specs=[far] * len(shapes),
-        scratch_shapes=[pltpu.VMEM(shape, arrays[0].dtype) for shape in shapes]
+        scratch_shapes=[pltpu.VMEM(shape, queries.dtype) for shape in shapes]
         + [pltpu.SemaphoreType.DMA((len(jobs),))] * 2,
-        cost_estimate=pl.CostEstimate(flops=cost, bytes_accessed=cost, transcendentals=0),
         name="stage",
-    )(meta, assignment, *arrays, *after)
+    )(meta, assignment, queries, grad_out, keys, values)
+    return staged[:count], staged[count:]
 
 
 def build_bias(source, sequence, line, segment_ref, column_ref, bias_ref, rows, tok_dev, reach):
@@ -270,21 +265,22 @@
     hops = -(-doc_most // tok_dev)
     meta = jnp.stack([group, line]).astype(jnp.int32)
 
-    arrays = (queries, grad_out, keys, values)
-    parts = [(step, 0, width) for step in range(1, count)]
-    ahead = stage(meta, assignment, arrays, parts[:1], False, 1)
-    kv_out, *behind = stage(meta, assignment, arrays, parts[1:], True, STAGE_COST, after=ahead)
-    arrived = [exchanged(ahead[0], "dp", 1)]
-    kv_own = lax.all_to_all(kv_out, "dp", split_axis=0, concat_axis=0, tiled=True)
-    behind, kv_own = lax.optimization_barrier((behind, kv_own))
-    arrived += [exchanged(rows, "dp", step) for rows, (step, _, _) in zip(behind, parts[1:])]
+    kv_staged, staged = stage(meta, assignment, queries, grad_out, keys, values)
+    kv_arrived = [exchanged(kv_staged[step], "dp", step) for step in range(1, count)]
+    staged, kv_arrived = lax.optimization_barrier((staged, kv_arrived))
+    arrived = [exchanged(rows, "dp", step) for step, rows in enumerate(staged, 1)]
+    kv_own = jnp.zeros((count, *kv_staged[0].shape), keys.dtype)
+    for step, piece in enumerate([kv_staged[0], *kv_arrived]):
+        kv_own = lax.dynamic_update_index_in_dim(
+            kv_own, piece, source_of(group, step, count), 0
+        )
     halos = [shifted(kv_own, ("blk", "uly"), back) for back in range(hops, 0, -1)]
     kv = jnp.concatenate([*halos, kv_own], axis=0)
 
     fixed = (doc_most, heads, meta, assignment, segment_ids)
     query, grad = (queries, lambda m, a: a[m[0]]), (grad_out, lambda m, a: a[m[0]])
     full, acc = attend(0, 0, kv_heads, *fixed, query, grad, kv, None, None, False)
-    for both, (step, _, _) in zip(arrived, parts):
+    for step, both in enumerate(arrived, 1):
         query, grad = (both, lambda m, a: 0), (both, lambda m, a: 1)
         full, acc, *returned = attend(
             step, 0, kv_heads, *fixed, query, grad, kv, acc, full, step == count - 1

time: 89.5 us -> 85.2 us (0.952)
  the two profiles are of different devices: /device:TPU:27 before, /device:TPU:19 now
where the time goes in v7:
time: 85.2 us; the launch traced here: 84.9 us
  waiting for transfers between devices  43.1 us (51%)
  starting transfers between devices  19.5 us (23%)
  Pallas kernels  19.1 us (22%)
  local copies, waits for them, and re-layouts  1.65 us (2%)
    ppermute x6, waiting for transfers between devices, exchanged(): lax.ppermute(value, axis, [(i, (i + step) % count) for i in range(count)])  33.4 us
    pallas_call x4, Pallas kernels, attend(): pl.pallas_call(functools.partial(attend_kernel, step, first, filled, last...  15.9 us
    ppermute x4, starting transfers between devices, shifted(): return lax.ppermute(value, axis, pairs)  13.6 us
    ppermute x4, waiting for transfers between devices, shifted(): return lax.ppermute(value, axis, pairs)  9.68 us
    ppermute x6, starting transfers between devices, exchanged(): lax.ppermute(value, axis, [(i, (i + step) % count) for i in range(count)])  5.89 us
    pallas_call x1, Pallas kernels, stage(): pl.pallas_call(functools.partial(stage_kernel, count, jobs, len(shapes)),...  3.17 us
  transfers between devices with their start and end apart: 10, of which 7 were waited for; matrix products, arithmetic and copies ran while one was open for 1% of the time, Pallas kernels for 14%

profile of v7, /device:TPU:19, one launch (start us, length us, event | category | flops | bytes accessed | tf_op | source)
XLA Modules:
  0.0 84.9 jit_solution(8505336301849463086)
XLA Ops:
  0.6 0.7 pad_add_fusion.meta_ref
  1.3 3.2 %stage.1 = (bf16[2,32,512]{2,1,0:T(8,128)(2,1)}, bf16[2,32,512]{2,1,0:T(8,128)(2,1)}, bf16[2,32,512]{2,1,0:T(8,128)(2,1)}, bf16[2,32,512]{2,1,0:T(8,128)(2,1)}, ...) custom-call(s32[2]{0:T(128)} %pad_add_fusion.meta_ref, s32[4]{0:T(128)} %assign_ref.9, ...), custom_call_target="tpu_custom_call" | custom-call | tf_op jit(solution)/shard_map/stage/pallas_call | solution.py:64
  4.5 1.3 %collective-permute-start = (bf16[2,32,512]{2,1,0:T(8,128)(2,1)}, bf16[2,32,512]{2,1,0:T(8,128)(2,1)S(1)}, u32[]{:S(2)}, u32[]{:S(2)}) collective-permute-start(bf16[2,32,512]{2,1,0:T(8,128)(2,1)} %get-tuple-element.29), channel_id=1, source_target_pairs={{0,1},{1,2},{2,3},{3,0},{4,5},{5,6},{6,7},{7,4},{8,9},{9,10},{10,1... | collective-permute-start | bytes 196616 | tf_op jit(solution)/shard_map/ppermute | solution.py:27
  5.9 1.2 %collective-permute-start.2 = (bf16[2,32,512]{2,1,0:T(8,128)(2,1)}, bf16[2,32,512]{2,1,0:T(8,128)(2,1)S(1)}, u32[]{:S(2)}, u32[]{:S(2)}) collective-permute-start(bf16[2,32,512]{2,1,0:T(8,128)(2,1)} %get-tuple-element.31), channel_id=1, source_target_pairs={{0,3},{1,0},{2,1},{3,2},{4,7},{5,4},{6,5},{7,6},{8,11},{9,8},{10,9... | collective-permute-start | bytes 196616 | tf_op jit(solution)/shard_map/ppermute | solution.py:27
  7.2 0.9 %bitcast_dynamic-update-slice_fusion.3 = bf16[4,2,32,512]{3,2,1,0:T(8,128)(2,1)S(1)} fusion(bf16[4,2,32,512]{3,2,1,0:T(8,128)(2,1)S(1)} %broadcast_in_dim.19, s32[]{:T(128)S(6)} %select_n.13, bf16[2,32,512]{2,1,0:T(8,128)(2,1)} %get-tuple-element.33), kind=kLoop, calls=%fused_computation.5 | loop fusion | bytes 131076 | tf_op jit(solution)/shard_map/jit(dynamic_update_index_in_dim)/dynamic_update_slice | solution.py:274
  8.0 2.2 %collective-permute-done.1 = bf16[2,32,512]{2,1,0:T(8,128)(2,1)S(1)} collective-permute-done((bf16[2,32,512]{2,1,0:T(8,128)(2,1)}, bf16[2,32,512]{2,1,0:T(8,128)(2,1)S(1)}, u32[]{:S(2)}, u32[]{:S(2)}) %collective-permute-start.1) | collective-permute-done | bytes 65568 | tf_op jit(solution)/shard_map/ppermute | solution.py:27
  10.2 1.4 %collective-permute-done.2 = bf16[2,32,512]{2,1,0:T(8,128)(2,1)S(1)} collective-permute-done((bf16[2,32,512]{2,1,0:T(8,128)(2,1)}, bf16[2,32,512]{2,1,0:T(8,128)(2,1)S(1)}, u32[]{:S(2)}, u32[]{:S(2)}) %collective-permute-start.2) | collective-permute-done | bytes 65568 | tf_op jit(solution)/shard_map/ppermute | solution.py:27
  11.6 2.1 %collective-permute-start.3 = (bf16[2,32,4096]{2,1,0:T(8,128)(2,1)}, bf16[2,32,4096]{2,1,0:T(8,128)(2,1)S(1)}, u32[]{:S(2)}, u32[]{:S(2)}) collective-permute-start(bf16[2,32,4096]{2,1,0:T(8,128)(2,1)} %get-tuple-element.32), channel_id=1, source_target_pairs={{0,3},{1,0},{2,1},{3,2},{4,7},{5,4},{6,5},{7,6},{8,11},{9,8},{10,9... | collective-permute-start | bytes 1572872 | tf_op jit(solution)/shard_map/ppermute | solution.py:27
  13.7 1.2 %collective-permute-start.6 = (bf16[2,32,4096]{2,1,0:T(8,128)(2,1)}, bf16[2,32,4096]{2,1,0:T(8,128)(2,1)S(1)}, u32[]{:S(2)}, u32[]{:S(2)}) collective-permute-start(bf16[2,32,4096]{2,1,0:T(8,128)(2,1)} %get-tuple-element.37), channel_id=1, source_target_pairs={{0,2},{1,3},{2,0},{3,1},{4,6},{5,7},{6,4},{7,5},{8,10},{9,11},{10,... | collective-permute-start | bytes 1572872 | tf_op jit(solution)/shard_map/ppermute | solution.py:27
  14.9 5.8 %collective-permute-start.5 = (bf16[4,2,32,512]{3,2,1,0:T(8,128)(2,1)S(1)}, bf16[4,2,32,512]{3,2,1,0:T(8,128)(2,1)S(1)}, u32[]{:S(2)}, u32[]{:S(2)}) collective-permute-start(bf16[4,2,32,512]{3,2,1,0:T(8,128)(2,1)S(1)} %bitcast_dynamic-update-slice_fusion), channel_id=1, source_target_pairs={{0,4},{4,8},{8,12},{12,16},{16,20},{20,24},{24,28},{1,5},{5,9},{9,... | collective-permute-start | bytes 786440 | tf_op jit(solution)/shard_map/ppermute | solution.py:33
  20.8 1.9 %collective-permute-start.4 = (bf16[4,2,32,512]{3,2,1,0:T(8,128)(2,1)S(1)}, bf16[4,2,32,512]{3,2,1,0:T(8,128)(2,1)S(1)}, u32[]{:S(2)}, u32[]{:S(2)}) collective-permute-start(bf16[4,2,32,512]{3,2,1,0:T(8,128)(2,1)S(1)} %bitcast_dynamic-update-slice_fusion), channel_id=1, source_target_pairs={{0,8},{4,12},{8,16},{12,20},{16,24},{20,28},{1,9},{5,13},{9,17},{1... | collective-permute-start | bytes 786440 | tf_op jit(solution)/shard_map/ppermute | solution.py:33
  22.7 3.2 %collective-permute-done.5 = bf16[4,2,32,512]{3,2,1,0:T(8,128)(2,1)S(1)} collective-permute-done((bf16[4,2,32,512]{3,2,1,0:T(8,128)(2,1)S(1)}, bf16[4,2,32,512]{3,2,1,0:T(8,128)(2,1)S(1)}, u32[]{:S(2)}, u32[]{:S(2)}) %collective-permute-start.5) | collective-permute-done | bytes 262176 | tf_op jit(solution)/shard_map/ppermute | solution.py:33
  26.0 0.1 pad_maximum_fusion.kv_ref
  26.2 3.9 %attend.4 = (bf16[128,32,128]{2,1,0:T(8,128)(2,1)}, f32[2,384,512]{2,1,0:T(8,128)S(1)}) custom-call(s32[2]{0:T(128)S(1)} %copy-done.4, s32[4]{0:T(128)S(1)} %copy-done.3, s32[4,1024]{1,0:T(4,128)S(1)} %copy-done.2, bf16[4,32,4096]{2,1,0:T(8,128)(2,1)S(1)} %copy-done, bf16[4,32,4096]{2,1,0:T(8,128)(2,1)S(1)} %copy-done.1, ...), custom_call_target="tpu_custom_call" | custom-call | flops 37748736 | bytes 294912 | tf_op jit(solution)/shard_map/attend/pallas_call | solution.py:235
  30.1 29.8 %collective-permute-done.7.query_ref.grad_ref = bf16[2,32,4096]{2,1,0:T(8,128)(2,1)S(1)} collective-permute-done((bf16[2,32,4096]{2,1,0:T(8,128)(2,1)}, bf16[2,32,4096]{2,1,0:T(8,128)(2,1)S(1)}, u32[]{:S(2)}, u32[]{:S(2)}) %collective-permute-start.7) | collective-permute-done | bytes 524320 | tf_op jit(solution)/shard_map/ppermute | solution.py:27
  59.9 3.9 %attend.5 = (bf16[128,32,128]{2,1,0:T(8,128)(2,1)}, f32[2,384,512]{2,1,0:T(8,128)S(1)}) custom-call(s32[2]{0:T(128)S(1)} %copy-done.4, s32[4]{0:T(128)S(1)} %copy-done.3, s32[4,1024]{1,0:T(4,128)S(1)} %copy-done.2, bf16[2,32,4096]{2,1,0:T(8,128)(2,1)S(1)} %collective-permute-done.7.query_ref.grad_ref, ...), custom_call_target="tpu_custom_call", output_to_operand_aliasing={{1}: (6, {}), {0}: (7, {})} | custom-call | flops 37748736 | bytes 294912 | tf_op jit(solution)/shard_map/attend/pallas_call | solution.py:235
  63.8 3.9 %attend.6 = (bf16[128,32,128]{2,1,0:T(8,128)(2,1)}, f32[2,384,512]{2,1,0:T(8,128)S(1)}) custom-call(s32[2]{0:T(128)S(1)} %copy-done.4, s32[4]{0:T(128)S(1)} %copy-done.3, s32[4,1024]{1,0:T(4,128)S(1)} %copy-done.2, bf16[2,32,4096]{2,1,0:T(8,128)(2,1)S(1)} %collective-permute-done.6.query_ref.grad_ref, ...), custom_call_target="tpu_custom_call", output_to_operand_aliasing={{1}: (6, {}), {0}: (7, {})} | custom-call | flops 37748736 | bytes 294912 | tf_op jit(solution)/shard_map/attend/pallas_call | solution.py:235
  67.8 4.1 %attend.7 = (bf16[128,32,128]{2,1,0:T(8,128)(2,1)}, f32[2,128,512]{2,1,0:T(8,128)S(1)}, bf16[2,128,512]{2,1,0:T(8,128)(2,1)S(1)}, bf16[2,128,512]{2,1,0:T(8,128)(2,1)S(1)}) custom-call(s32[2]{0:T(128)S(1)} %copy-done.4, s32[4]{0:T(128)S(1)} %copy-done.3, s32[4,1024]{1,0:T(4,128)S(1)} %copy-done.2, ...), custom_call_target="tpu_custom_call", output_to_operand_aliasing={{0}: (7, {})} | custom-call | flops 37748736 | bytes 294912 | tf_op jit(solution)/shard_map/attend/pallas_call | solution.py:235
  71.9 2.7 %collective-permute-start.8 = (bf16[2,128,512]{2,1,0:T(8,128)(2,1)S(1)}, bf16[2,128,512]{2,1,0:T(8,128)(2,1)S(1)}, u32[]{:S(2)}, u32[]{:S(2)}) collective-permute-start(bf16[2,128,512]{2,1,0:T(8,128)(2,1)S(1)} %get-tuple-element.47), channel_id=1, source_target_pairs={{4,0},{8,4},{12,8},{16,12},{20,16},{24,20},{28,24},{5,1},{9,5},{13... | collective-permute-start | bytes 786440 | tf_op jit(solution)/shard_map/ppermute | solution.py:33
  74.6 3.1 %collective-permute-start.9 = (bf16[2,128,512]{2,1,0:T(8,128)(2,1)S(1)}, bf16[2,128,512]{2,1,0:T(8,128)(2,1)S(1)}, u32[]{:S(2)}, u32[]{:S(2)}) collective-permute-start(bf16[2,128,512]{2,1,0:T(8,128)(2,1)S(1)} %get-tuple-element.48), channel_id=1, source_target_pairs={{8,0},{12,4},{16,8},{20,12},{24,16},{28,20},{9,1},{13,5},{17,9},{2... | collective-permute-start | bytes 786440 | tf_op jit(solution)/shard_map/ppermute | solution.py:33
  77.7 5.1 %collective-permute-done.8 = bf16[2,128,512]{2,1,0:T(8,128)(2,1)S(1)} collective-permute-done((bf16[2,128,512]{2,1,0:T(8,128)(2,1)S(1)}, bf16[2,128,512]{2,1,0:T(8,128)(2,1)S(1)}, u32[]{:S(2)}, u32[]{:S(2)}) %collective-permute-start.8) | collective-permute-done | bytes 262176 | tf_op jit(solution)/shard_map/ppermute | solution.py:33
  82.8 1.3 %collective-permute-done.9 = bf16[2,128,512]{2,1,0:T(8,128)(2,1)S(1)} collective-permute-done((bf16[2,128,512]{2,1,0:T(8,128)(2,1)S(1)}, bf16[2,128,512]{2,1,0:T(8,128)(2,1)S(1)}, u32[]{:S(2)}, u32[]{:S(2)}) %collective-permute-start.9) | collective-permute-done | bytes 262176 | tf_op jit(solution)/shard_map/ppermute | solution.py:33
  84.1 0.1 add_convert_fusion
  84.2 0.7 fusion
  (20 shorter events, 0.2 us)
Async XLA Ops:
  4.5 21.7 %copy-start = (bf16[4,32,4096]{2,1,0:T(8,128)(2,1)S(1)}, bf16[4,32,4096]{2,1,0:T(8,128)(2,1)}, u32[]{:S(2)}) copy-start(bf16[4,32,4096]{2,1,0:T(8,128)(2,1)} %query_ref.1) | copy-start | bytes 3145732
  4.5 21.7 %copy-start.1 = (bf16[4,32,4096]{2,1,0:T(8,128)(2,1)S(1)}, bf16[4,32,4096]{2,1,0:T(8,128)(2,1)}, u32[]{:S(2)}) copy-start(bf16[4,32,4096]{2,1,0:T(8,128)(2,1)} %grad_ref.1) | copy-start | bytes 3145732
  4.5 21.7 %copy-start.2 = (s32[4,1024]{1,0:T(4,128)S(1)}, s32[4,1024]{1,0:T(4,128)}, u32[]{:S(2)}) copy-start(s32[4,1024]{1,0:T(4,128)} %segment_ref.7) | copy-start | bytes 49156
  4.5 21.7 %copy-start.3 = (s32[4]{0:T(128)S(1)}, s32[4]{0:T(128)}, u32[]{:S(2)}) copy-start(s32[4]{0:T(128)} %assign_ref.9) | copy-start | bytes 52
  4.5 21.7 %copy-start.4 = (s32[2]{0:T(128)S(1)}, s32[2]{0:T(128)}, u32[]{:S(2)}) copy-start(s32[2]{0:T(128)} %pad_add_fusion.meta_ref) | copy-start | bytes 28
  4.5 3.5 %collective-permute-start = (bf16[2,32,512]{2,1,0:T(8,128)(2,1)}, bf16[2,32,512]{2,1,0:T(8,128)(2,1)S(1)}, u32[]{:S(2)}, u32[]{:S(2)}) collective-permute-start(bf16[2,32,512]{2,1,0:T(8,128)(2,1)} %get-tuple-element.29), channel_id=1, source_target_pairs={{0,1},{1,2},{2,3},{3,0},{4,5},{5,6},{6,7},{7,4},{8,9},{9,10},{10,1... | collective-permute-start | bytes 196616 | tf_op jit(solution)/shard_map/ppermute | solution.py:27
  5.9 4.3 %collective-permute-start.1 = (bf16[2,32,512]{2,1,0:T(8,128)(2,1)}, bf16[2,32,512]{2,1,0:T(8,128)(2,1)S(1)}, u32[]{:S(2)}, u32[]{:S(2)}) collective-permute-start(bf16[2,32,512]{2,1,0:T(8,128)(2,1)} %get-tuple-element.30), channel_id=1, source_target_pairs={{0,2},{1,3},{2,0},{3,1},{4,6},{5,7},{6,4},{7,5},{8,10},{9,11},{10,... | collective-permute-start | bytes 196616 | tf_op jit(solution)/shard_map/ppermute | solution.py:27
  5.9 5.7 %collective-permute-start.2 = (bf16[2,32,512]{2,1,0:T(8,128)(2,1)}, bf16[2,32,512]{2,1,0:T(8,128)(2,1)S(1)}, u32[]{:S(2)}, u32[]{:S(2)}) collective-permute-start(bf16[2,32,512]{2,1,0:T(8,128)(2,1)} %get-tuple-element.31), channel_id=1, source_target_pairs={{0,3},{1,0},{2,1},{3,2},{4,7},{5,4},{6,5},{7,6},{8,11},{9,8},{10,9... | collective-permute-start | bytes 196616 | tf_op jit(solution)/shard_map/ppermute | solution.py:27
  11.6 56.2 %collective-permute-start.3 = (bf16[2,32,4096]{2,1,0:T(8,128)(2,1)}, bf16[2,32,4096]{2,1,0:T(8,128)(2,1)S(1)}, u32[]{:S(2)}, u32[]{:S(2)}) collective-permute-start(bf16[2,32,4096]{2,1,0:T(8,128)(2,1)} %get-tuple-element.32), channel_id=1, source_target_pairs={{0,3},{1,0},{2,1},{3,2},{4,7},{5,4},{6,5},{7,6},{8,11},{9,8},{10,9... | collective-permute-start | bytes 1572872 | tf_op jit(solution)/shard_map/ppermute | solution.py:27
  13.7 50.1 %collective-permute-start.6 = (bf16[2,32,4096]{2,1,0:T(8,128)(2,1)}, bf16[2,32,4096]{2,1,0:T(8,128)(2,1)S(1)}, u32[]{:S(2)}, u32[]{:S(2)}) collective-permute-start(bf16[2,32,4096]{2,1,0:T(8,128)(2,1)} %get-tuple-element.37), channel_id=1, source_target_pairs={{0,2},{1,3},{2,0},{3,1},{4,6},{5,7},{6,4},{7,5},{8,10},{9,11},{10,... | collective-permute-start | bytes 1572872 | tf_op jit(solution)/shard_map/ppermute | solution.py:27
  14.9 45.0 %collective-permute-start.7 = (bf16[2,32,4096]{2,1,0:T(8,128)(2,1)}, bf16[2,32,4096]{2,1,0:T(8,128)(2,1)S(1)}, u32[]{:S(2)}, u32[]{:S(2)}) collective-permute-start(bf16[2,32,4096]{2,1,0:T(8,128)(2,1)} %get-tuple-element.38), channel_id=1, source_target_pairs={{0,1},{1,2},{2,3},{3,0},{4,5},{5,6},{6,7},{7,4},{8,9},{9,10},{10,1... | collective-permute-start | bytes 1572872 | tf_op jit(solution)/shard_map/ppermute | solution.py:27
  14.9 11.1 %collective-permute-start.5 = (bf16[4,2,32,512]{3,2,1,0:T(8,128)(2,1)S(1)}, bf16[4,2,32,512]{3,2,1,0:T(8,128)(2,1)S(1)}, u32[]{:S(2)}, u32[]{:S(2)}) collective-permute-start(bf16[4,2,32,512]{3,2,1,0:T(8,128)(2,1)S(1)} %bitcast_dynamic-update-slice_fusion), channel_id=1, source_target_pairs={{0,4},{4,8},{8,12},{12,16},{16,20},{20,24},{24,28},{1,5},{5,9},{9,... | collective-permute-start | bytes 786440 | tf_op jit(solution)/shard_map/ppermute | solution.py:33
  20.8 5.3 %collective-permute-start.4 = (bf16[4,2,32,512]{3,2,1,0:T(8,128)(2,1)S(1)}, bf16[4,2,32,512]{3,2,1,0:T(8,128)(2,1)S(1)}, u32[]{:S(2)}, u32[]{:S(2)}) collective-permute-start(bf16[4,2,32,512]{3,2,1,0:T(8,128)(2,1)S(1)} %bitcast_dynamic-update-slice_fusion), channel_id=1, source_target_pairs={{0,8},{4,12},{8,16},{12,20},{16,24},{20,28},{1,9},{5,13},{9,17},{1... | collective-permute-start | bytes 786440 | tf_op jit(solution)/shard_map/ppermute | solution.py:33
  71.9 10.9 %collective-permute-start.8 = (bf16[2,128,512]{2,1,0:T(8,128)(2,1)S(1)}, bf16[2,128,512]{2,1,0:T(8,128)(2,1)S(1)}, u32[]{:S(2)}, u32[]{:S(2)}) collective-permute-start(bf16[2,128,512]{2,1,0:T(8,128)(2,1)S(1)} %get-tuple-element.47), channel_id=1, source_target_pairs={{4,0},{8,4},{12,8},{16,12},{20,16},{24,20},{28,24},{5,1},{9,5},{13... | collective-permute-start | bytes 786440 | tf_op jit(solution)/shard_map/ppermute | solution.py:33
  74.6 9.5 %collective-permute-start.9 = (bf16[2,128,512]{2,1,0:T(8,128)(2,1)S(1)}, bf16[2,128,512]{2,1,0:T(8,128)(2,1)S(1)}, u32[]{:S(2)}, u32[]{:S(2)}) collective-permute-start(bf16[2,128,512]{2,1,0:T(8,128)(2,1)S(1)} %get-tuple-element.48), channel_id=1, source_target_pairs={{8,0},{12,4},{16,8},{20,12},{24,16},{28,20},{9,1},{13,5},{17,9},{2... | collective-permute-start | bytes 786440 | tf_op jit(solution)/shard_map/ppermute | solution.py:33

commit v8 on v7

--- a/solution.py
+++ b/solution.py
@@ -33,16 +33,17 @@
     return lax.ppermute(value, axis, pairs)
 
 
-def stage_kernel(count, jobs, outs, meta_ref, assign_ref, *refs):
+def stage_kernel(count, jobs, outs, meta_ref, assign_ref, first_ref, second_ref, *refs):
     group = meta_ref[0]
-    sources, refs = refs[:4], refs[4:]
-    out_refs, held_refs, (in_sems, out_sems) = refs[:outs], refs[outs : 2 * outs], refs[-2:]
+    out_refs, held_refs, (in_sems, out_sems) = refs[-2 - 2 * outs : -2 - outs], refs[-2 - outs : -2], refs[-2:]
     loads, stores = [], []
-    for slot, (source, step, out, which) in enumerate(jobs):
-        origin = sources[source].at[assign_ref[target_of(group, step, count)]]
-        held, goal = held_refs[out].at[which], out_refs[out].at[which]
-        loads.append(pltpu.make_async_copy(origin, held, in_sems.at[slot]))
-        stores.append(pltpu.make_async_copy(held, goal, out_sems.at[slot]))
+    for out, (step, start, width) in enumerate(jobs):
+        chosen = assign_ref[target_of(group, step, count)]
+        for which, source in enumerate((first_ref, second_ref)):
+            origin = source.at[chosen, :, start : start + width]
+            held, goal, slot = held_refs[out].at[which], out_refs[out].at[which], 2 * out + which
+            loads.append(pltpu.make_async_copy(origin, held, in_sems.at[slot]))
+            stores.append(pltpu.make_async_copy(held, goal, out_sems.at[slot]))
     for load in loads:
         load.start()
     for load, store in zip(loads, stores):
@@ -52,25 +53,19 @@
         store.wait()
 
 
-def stage(meta, assignment, queries, grad_out, keys, values):
-    count, rows, _ = queries.shape
-    shapes, jobs = [], []
-    for first, steps in ((2, range(count)), (0, range(1, count))):
-        width = (queries, grad_out, keys, values)[first].shape[2]
-        for step in steps:
-            jobs += [(first + which, step, len(shapes), which) for which in range(2)]
-            shapes.append((2, rows, width))
+def stage(meta, assignment, first, second, jobs, after=()):
+    count, rows, _ = first.shape
+    shapes = [(2, rows, width) for _, _, width in jobs]
     far, scalars = pl.BlockSpec(memory_space=pltpu.HBM), pl.BlockSpec(memory_space=pltpu.SMEM)
-    staged = pl.pallas_call(
+    return pl.pallas_call(
         functools.partial(stage_kernel, count, jobs, len(shapes)),
-        out_shape=[jax.ShapeDtypeStruct(shape, queries.dtype) for shape in shapes],
-        in_specs=[scalars] * 2 + [far] * 4,
+        out_shape=[jax.ShapeDtypeStruct(shape, first.dtype) for shape in shapes],
+        in_specs=[scalars] * 2 + [far] * 2 + [pl.BlockSpec(memory_space=pl.ANY)] * len(after),
         out_specs=[far] * len(shapes),
-        scratch_shapes=[pltpu.VMEM(shape, queries.dtype) for shape in shapes]
-        + [pltpu.SemaphoreType.DMA((len(jobs),))] * 2,
+        scratch_shapes=[pltpu.VMEM(shape, first.dtype) for shape in shapes]
+        + [pltpu.SemaphoreType.DMA((2 * len(shapes),))] * 2,
         name="stage",
-    )(meta, assignment, queries, grad_out, keys, values)
-    return staged[:count], staged[count:]
+    )(meta, assignment, first, second, *after)
 
 
 def build_bias(source, sequence, line, segment_ref, column_ref, bias_ref, rows, tok_dev, reach):
@@ -265,10 +260,17 @@
     hops = -(-doc_most // tok_dev)
     meta = jnp.stack([group, line]).astype(jnp.int32)
 
-    kv_staged, staged = stage(meta, assignment, queries, grad_out, keys, values)
+    final, halves = count - 1, kv_heads // HEADS_STEP
+    part = width // halves
+    kv_jobs = [(step, 0, kv_width) for step in range(count)]
+    kv_staged = stage(meta, assignment, keys, values, kv_jobs)
+    jobs = [(step, 0, width) for step in range(1, final)]
+    jobs += [(final, half * part, part) for half in range(halves)]
+    staged = stage(meta, assignment, queries, grad_out, jobs, after=kv_staged[:1])
     kv_arrived = [exchanged(kv_staged[step], "dp", step) for step in range(1, count)]
     staged, kv_arrived = lax.optimization_barrier((staged, kv_arrived))
-    arrived = [exchanged(rows, "dp", step) for step, rows in enumerate(staged, 1)]
+    arrived = [exchanged(staged[step - 1], "dp", step) for step in range(1, final)]
+    split = [exchanged(staged[final - 1], "dp", final)]
     kv_own = jnp.zeros((count, *kv_staged[0].shape), keys.dtype)
     for step, piece in enumerate([kv_staged[0], *kv_arrived]):
         kv_own = lax.dynamic_update_index_in_dim(
@@ -280,14 +282,25 @@
     fixed = (doc_most, heads, meta, assignment, segment_ids)
     query, grad = (queries, lambda m, a: a[m[0]]), (grad_out, lambda m, a: a[m[0]])
     full, acc = attend(0, 0, kv_heads, *fixed, query, grad, kv, None, None, False)
-    for step, both in enumerate(arrived, 1):
+    rows, acc = lax.optimization_barrier((staged[final], acc))
+    split.append(exchanged(rows, "dp", final))
+    for step in range(1, final):
+        both = arrived[step - 1]
         query, grad = (both, lambda m, a: 0), (both, lambda m, a: 1)
-        full, acc, *returned = attend(
-            step, 0, kv_heads, *fixed, query, grad, kv, acc, full, step == count - 1
-        )
-    for back, halo in enumerate(returned, 1):
-        acc = acc + shifted(halo, ("blk", "uly"), -back).astype(jnp.float32)
-    total = acc.astype(jnp.bfloat16)
+        full, acc = attend(step, 0, kv_heads, *fixed, query, grad, kv, acc, full, False)
+    totals, returned = [], []
+    for half, both in enumerate(split):
+        query, grad = (both, lambda m, a: 0), (both, lambda m, a: 1)
+        full, total, *halos = attend(
+            final, half * HEADS_STEP, HEADS_STEP, *fixed, query, grad, kv, acc, full, True
+        )
+        if half:
+            halos, returned = lax.optimization_barrier((halos, returned))
+        returned = [shifted(halo, ("blk", "uly"), -back) for back, halo in enumerate(halos, 1)]
+        for halo in returned:
+            total = total + halo.astype(jnp.float32)
+        totals.append(total.astype(jnp.bfloat16))
+    total = jnp.concatenate(totals, axis=2)
     return full[None], total[0][None], total[1][None]
 
 

time: 85.2 us -> 84.6 us (level)
  the two profiles are of different devices: /device:TPU:19 before, /device:TPU:27 now
where the time goes in v8:
time: 84.6 us; the launch traced here: 84.2 us
  waiting for transfers between devices  36 us (43%)
  starting transfers between devices  23 us (27%)
  Pallas kernels  22 us (26%)
  other arithmetic  1.48 us (2%)
  local copies, waits for them, and re-layouts  0.93 us (1%)
  between operations  0.85 us (1%)
    ppermute x7, waiting for transfers between devices, exchanged(): lax.ppermute(value, axis, [(i, (i + step) % count) for i in range(count)])  28.4 us
    ppermute x6, starting transfers between devices, shifted(): return lax.ppermute(value, axis, pairs)  18.1 us
    pallas_call x5, Pallas kernels, attend(): pl.pallas_call(functools.partial(attend_kernel, step, first, filled, last...  16.6 us
    ppermute x6, waiting for transfers between devices, shifted(): return lax.ppermute(value, axis, pairs)  7.56 us
    pallas_call x2, Pallas kernels, stage(): pl.pallas_call(functools.partial(stage_kernel, count, jobs, len(shapes)),...  5.4 us
    ppermute x7, starting transfers between devices, exchanged(): lax.ppermute(value, axis, [(i, (i + step) % count) for i in range(count)])  4.93 us
  transfers between devices with their start and end apart: 13, of which 8 were waited for; matrix products, arithmetic and copies ran while one was open for 1% of the time, Pallas kernels for 23%

profile of v8, /device:TPU:27, one launch (start us, length us, event | category | flops | bytes accessed | tf_op | source)
XLA Modules:
  0.0 84.2 jit_solution(6441401351953012113)
XLA Ops:
  1.2 2.3 %stage.2 = (bf16[2,32,512]{2,1,0:T(8,128)(2,1)}, bf16[2,32,512]{2,1,0:T(8,128)(2,1)}, bf16[2,32,512]{2,1,0:T(8,128)(2,1)}, bf16[2,32,512]{2,1,0:T(8,128)(2,1)}) custom-call(s32[2]{0:T(128)} %pad_add_fusion.meta_ref, s32[4]{0:T(128)} %assign_ref.13, bf16[4,32,512]{2,1,0:T(8,128)(2,1)} %first_ref.2, bf16[4,32,512]{2,1,0:T(8,128)(2,1)} %second_ref.2), custom_call_target="tpu_custom_call" | custom-call | tf_op jit(solution)/shard_map/stage/pallas_call | solution.py:60
  3.6 1.3 %collective-permute-start.1 = (bf16[2,32,512]{2,1,0:T(8,128)(2,1)}, bf16[2,32,512]{2,1,0:T(8,128)(2,1)S(1)}, u32[]{:S(2)}, u32[]{:S(2)}) collective-permute-start(bf16[2,32,512]{2,1,0:T(8,128)(2,1)} %get-tuple-element.42), channel_id=1, source_target_pairs={{0,2},{1,3},{2,0},{3,1},{4,6},{5,7},{6,4},{7,5},{8,10},{9,11},{10,... | collective-permute-start | bytes 196616 | tf_op jit(solution)/shard_map/ppermute | solution.py:27
  5.1 0.9 %bitcast_dynamic-update-slice_fusion.3 = bf16[4,2,32,512]{3,2,1,0:T(8,128)(2,1)S(1)} fusion(bf16[4,2,32,512]{3,2,1,0:T(8,128)(2,1)S(1)} %broadcast_in_dim.19, s32[]{:T(128)S(6)} %select_n.13, bf16[2,32,512]{2,1,0:T(8,128)(2,1)} %get-tuple-element.36.refs_0_), kind=kLoop, calls=%fused_computation.10 | loop fusion | bytes 131076 | tf_op jit(solution)/shard_map/jit(dynamic_update_index_in_dim)/dynamic_update_slice | solution.py:276
  6.0 3.1 %stage.3 = (bf16[2,32,4096]{2,1,0:T(8,128)(2,1)}, bf16[2,32,4096]{2,1,0:T(8,128)(2,1)}, bf16[2,32,2048]{2,1,0:T(8,128)(2,1)}, bf16[2,32,2048]{2,1,0:T(8,128)(2,1)}) custom-call(s32[2]{0:T(128)} %pad_add_fusion.meta_ref, s32[4]{0:T(128)} %assign_ref.13, bf16[4,32,4096]{2,1,0:T(8,128)(2,1)} %query_ref.1, bf16[4,32,4096]{2,1,0:T(8,128)(2,1)} %grad_ref.1, ...), custom_call_target="tpu_custom_call" | custom-call | tf_op jit(solution)/shard_map/stage/pallas_call | solution.py:60
  9.2 1.3 %collective-permute-done.2 = bf16[2,32,512]{2,1,0:T(8,128)(2,1)S(1)} collective-permute-done((bf16[2,32,512]{2,1,0:T(8,128)(2,1)}, bf16[2,32,512]{2,1,0:T(8,128)(2,1)S(1)}, u32[]{:S(2)}, u32[]{:S(2)}) %collective-permute-start.2) | collective-permute-done | bytes 65568 | tf_op jit(solution)/shard_map/ppermute | solution.py:27
  10.5 1.8 %collective-permute-start.7 = (bf16[2,32,4096]{2,1,0:T(8,128)(2,1)}, bf16[2,32,4096]{2,1,0:T(8,128)(2,1)S(1)}, u32[]{:S(2)}, u32[]{:S(2)}) collective-permute-start(bf16[2,32,4096]{2,1,0:T(8,128)(2,1)} %get-tuple-element.51), channel_id=1, source_target_pairs={{0,1},{1,2},{2,3},{3,0},{4,5},{5,6},{6,7},{7,4},{8,9},{9,10},{10,1... | collective-permute-start | bytes 1572872 | tf_op jit(solution)/shard_map/ppermute | solution.py:27
  12.4 4.8 %collective-permute-start.4 = (bf16[4,2,32,512]{3,2,1,0:T(8,128)(2,1)S(1)}, bf16[4,2,32,512]{3,2,1,0:T(8,128)(2,1)S(1)}, u32[]{:S(2)}, u32[]{:S(2)}) collective-permute-start(bf16[4,2,32,512]{3,2,1,0:T(8,128)(2,1)S(1)} %bitcast_dynamic-update-slice_fusion), channel_id=1, source_target_pairs={{0,4},{4,8},{8,12},{12,16},{16,20},{20,24},{24,28},{1,5},{5,9},{9,... | collective-permute-start | bytes 786440 | tf_op jit(solution)/shard_map/ppermute | solution.py:33
  17.2 1.9 %collective-permute-start.3 = (bf16[4,2,32,512]{3,2,1,0:T(8,128)(2,1)S(1)}, bf16[4,2,32,512]{3,2,1,0:T(8,128)(2,1)S(1)}, u32[]{:S(2)}, u32[]{:S(2)}) collective-permute-start(bf16[4,2,32,512]{3,2,1,0:T(8,128)(2,1)S(1)} %bitcast_dynamic-update-slice_fusion), channel_id=1, source_target_pairs={{0,8},{4,12},{8,16},{12,20},{16,24},{20,28},{1,9},{5,13},{9,17},{1... | collective-permute-start | bytes 786440 | tf_op jit(solution)/shard_map/ppermute | solution.py:33
  19.2 1.1 %collective-permute-start.8 = (bf16[2,32,2048]{2,1,0:T(8,128)(2,1)}, bf16[2,32,2048]{2,1,0:T(8,128)(2,1)S(1)}, u32[]{:S(2)}, u32[]{:S(2)}) collective-permute-start(bf16[2,32,2048]{2,1,0:T(8,128)(2,1)} %get-tuple-element.57), channel_id=1, source_target_pairs={{0,3},{1,0},{2,1},{3,2},{4,7},{5,4},{6,5},{7,6},{8,11},{9,8},{10,9... | collective-permute-start | bytes 786440 | tf_op jit(solution)/shard_map/ppermute | solution.py:27
  20.3 2.1 %collective-permute-done.4 = bf16[4,2,32,512]{3,2,1,0:T(8,128)(2,1)S(1)} collective-permute-done((bf16[4,2,32,512]{3,2,1,0:T(8,128)(2,1)S(1)}, bf16[4,2,32,512]{3,2,1,0:T(8,128)(2,1)S(1)}, u32[]{:S(2)}, u32[]{:S(2)}) %collective-permute-start.4) | collective-permute-done | bytes 262176 | tf_op jit(solution)/shard_map/ppermute | solution.py:33
  22.6 3.9 %attend.5 = (bf16[128,32,128]{2,1,0:T(8,128)(2,1)}, f32[2,384,512]{2,1,0:T(8,128)S(1)}) custom-call(s32[2]{0:T(128)S(1)} %copy-done.4, s32[4]{0:T(128)S(1)} %copy-done.3, s32[4,1024]{1,0:T(4,128)S(1)} %copy-done.2, bf16[4,32,4096]{2,1,0:T(8,128)(2,1)S(1)} %copy-done, bf16[4,32,4096]{2,1,0:T(8,128)(2,1)S(1)} %copy-done.1, ...), custom_call_target="tpu_custom_call" | custom-call | flops 37748736 | bytes 294912 | tf_op jit(solution)/shard_map/attend/pallas_call | solution.py:230
  27.0 3.9 %attend.6 = (bf16[128,32,128]{2,1,0:T(8,128)(2,1)}, f32[2,384,512]{2,1,0:T(8,128)S(1)}) custom-call(s32[2]{0:T(128)S(1)} %copy-done.4, s32[4]{0:T(128)S(1)} %copy-done.3, s32[4,1024]{1,0:T(4,128)S(1)} %copy-done.2, bf16[2,32,4096]{2,1,0:T(8,128)(2,1)S(1)} %collective-permute-done.7.query_ref.grad_ref, ...), custom_call_target="tpu_custom_call", output_to_operand_aliasing={{1}: (6, {}), {0}: (7, {})} | custom-call | flops 37748736 | bytes 294912 | tf_op jit(solution)/shard_map/attend/pallas_call | solution.py:230
  30.9 27.1 %collective-permute-done.6.query_ref.grad_ref = bf16[2,32,4096]{2,1,0:T(8,128)(2,1)S(1)} collective-permute-done((bf16[2,32,4096]{2,1,0:T(8,128)(2,1)}, bf16[2,32,4096]{2,1,0:T(8,128)(2,1)S(1)}, u32[]{:S(2)}, u32[]{:S(2)}) %collective-permute-start.6) | collective-permute-done | bytes 524320 | tf_op jit(solution)/shard_map/ppermute | solution.py:27
  57.9 3.9 %attend.7 = (bf16[128,32,128]{2,1,0:T(8,128)(2,1)}, f32[2,384,512]{2,1,0:T(8,128)S(1)}) custom-call(s32[2]{0:T(128)S(1)} %copy-done.4, s32[4]{0:T(128)S(1)} %copy-done.3, s32[4,1024]{1,0:T(4,128)S(1)} %copy-done.2, bf16[2,32,4096]{2,1,0:T(8,128)(2,1)S(1)} %collective-permute-done.6.query_ref.grad_ref, ...), custom_call_target="tpu_custom_call", output_to_operand_aliasing={{1}: (6, {}), {0}: (7, {})} | custom-call | flops 37748736 | bytes 294912 | tf_op jit(solution)/shard_map/attend/pallas_call | solution.py:230
  61.9 2.4 %attend.8 = (bf16[128,32,128]{2,1,0:T(8,128)(2,1)}, f32[2,128,256]{2,1,0:T(8,128)S(1)}, bf16[2,128,256]{2,1,0:T(8,128)(2,1)S(1)}, bf16[2,128,256]{2,1,0:T(8,128)(2,1)S(1)}) custom-call(s32[2]{0:T(128)S(1)} %copy-done.4, s32[4]{0:T(128)S(1)} %copy-done.3, s32[4,1024]{1,0:T(4,128)S(1)} %copy-done.2, ...), custom_call_target="tpu_custom_call", output_to_operand_aliasing={{0}: (7, {})} | custom-call | flops 18874368 | bytes 147456 | tf_op jit(solution)/shard_map/attend/pallas_call | solution.py:230
  64.3 2.8 %collective-permute-start.9 = (bf16[2,128,256]{2,1,0:T(8,128)(2,1)S(1)}, bf16[2,128,256]{2,1,0:T(8,128)(2,1)S(1)}, u32[]{:S(2)}, u32[]{:S(2)}) collective-permute-start(bf16[2,128,256]{2,1,0:T(8,128)(2,1)S(1)} %get-tuple-element.62), channel_id=1, source_target_pairs={{4,0},{8,4},{12,8},{16,12},{20,16},{24,20},{28,24},{5,1},{9,5},{13... | collective-permute-start | bytes 393224 | tf_op jit(solution)/shard_map/ppermute | solution.py:33
  67.1 3.3 %collective-permute-start.10 = (bf16[2,128,256]{2,1,0:T(8,128)(2,1)S(1)}, bf16[2,128,256]{2,1,0:T(8,128)(2,1)S(1)}, u32[]{:S(2)}, u32[]{:S(2)}) collective-permute-start(bf16[2,128,256]{2,1,0:T(8,128)(2,1)S(1)} %get-tuple-element.63), channel_id=1, source_target_pairs={{8,0},{12,4},{16,8},{20,12},{24,16},{28,20},{9,1},{13,5},{17,9},{2... | collective-permute-start | bytes 393224 | tf_op jit(solution)/shard_map/ppermute | solution.py:33
  70.3 2.4 %attend.9 = (bf16[128,32,128]{2,1,0:T(8,128)(2,1)}, f32[2,128,256]{2,1,0:T(8,128)S(1)}, bf16[2,128,256]{2,1,0:T(8,128)(2,1)S(1)}, bf16[2,128,256]{2,1,0:T(8,128)(2,1)S(1)}) custom-call(s32[2]{0:T(128)S(1)} %copy-done.4, s32[4]{0:T(128)S(1)} %copy-done.3, s32[4,1024]{1,0:T(4,128)S(1)} %copy-done.2, ...), custom_call_target="tpu_custom_call", output_to_operand_aliasing={{0}: (7, {})} | custom-call | flops 18874368 | bytes 147456 | tf_op jit(solution)/shard_map/attend/pallas_call | solution.py:230
  72.7 1.1 %collective-permute-done.10 = bf16[2,128,256]{2,1,0:T(8,128)(2,1)S(1)} collective-permute-done((bf16[2,128,256]{2,1,0:T(8,128)(2,1)S(1)}, bf16[2,128,256]{2,1,0:T(8,128)(2,1)S(1)}, u32[]{:S(2)}, u32[]{:S(2)}) %collective-permute-start.10) | collective-permute-done | bytes 131104 | tf_op jit(solution)/shard_map/ppermute | solution.py:33
  73.8 3.3 %collective-permute-start.11 = (bf16[2,128,256]{2,1,0:T(8,128)(2,1)S(1)}, bf16[2,128,256]{2,1,0:T(8,128)(2,1)S(1)}, u32[]{:S(2)}, u32[]{:S(2)}) collective-permute-start(bf16[2,128,256]{2,1,0:T(8,128)(2,1)S(1)} %get-tuple-element.67), channel_id=1, source_target_pairs={{4,0},{8,4},{12,8},{16,12},{20,16},{24,20},{28,24},{5,1},{9,5},{13... | collective-permute-start | bytes 393224 | tf_op jit(solution)/shard_map/ppermute | solution.py:33
  77.2 1.9 %collective-permute-start.12 = (bf16[2,128,256]{2,1,0:T(8,128)(2,1)S(1)}, bf16[2,128,256]{2,1,0:T(8,128)(2,1)S(1)}, u32[]{:S(2)}, u32[]{:S(2)}) collective-permute-start(bf16[2,128,256]{2,1,0:T(8,128)(2,1)S(1)} %get-tuple-element.68), channel_id=1, source_target_pairs={{8,0},{12,4},{16,8},{20,12},{24,16},{28,20},{9,1},{13,5},{17,9},{2... | collective-permute-start | bytes 393224 | tf_op jit(solution)/shard_map/ppermute | solution.py:33
  79.1 1.9 %collective-permute-done.11 = bf16[2,128,256]{2,1,0:T(8,128)(2,1)S(1)} collective-permute-done((bf16[2,128,256]{2,1,0:T(8,128)(2,1)S(1)}, bf16[2,128,256]{2,1,0:T(8,128)(2,1)S(1)}, u32[]{:S(2)}, u32[]{:S(2)}) %collective-permute-start.11) | collective-permute-done | bytes 131104 | tf_op jit(solution)/shard_map/ppermute | solution.py:33
  81.0 2.4 %collective-permute-done.12 = bf16[2,128,256]{2,1,0:T(8,128)(2,1)S(1)} collective-permute-done((bf16[2,128,256]{2,1,0:T(8,128)(2,1)S(1)}, bf16[2,128,256]{2,1,0:T(8,128)(2,1)S(1)}, u32[]{:S(2)}, u32[]{:S(2)}) %collective-permute-start.12) | collective-permute-done | bytes 131104 | tf_op jit(solution)/shard_map/ppermute | solution.py:33
  83.5 0.7 pad_maximum_fusion.1
  (31 shorter events, 1.8 us)
Async XLA Ops:
  3.5 5.6 %collective-permute-start = (bf16[2,32,512]{2,1,0:T(8,128)(2,1)}, bf16[2,32,512]{2,1,0:T(8,128)(2,1)S(1)}, u32[]{:S(2)}, u32[]{:S(2)}) collective-permute-start(bf16[2,32,512]{2,1,0:T(8,128)(2,1)} %get-tuple-element.41), channel_id=1, source_target_pairs={{0,1},{1,2},{2,3},{3,0},{4,5},{5,6},{6,7},{7,4},{8,9},{9,10},{10,1... | collective-permute-start | bytes 196616 | tf_op jit(solution)/shard_map/ppermute | solution.py:27
  3.6 5.6 %collective-permute-start.1 = (bf16[2,32,512]{2,1,0:T(8,128)(2,1)}, bf16[2,32,512]{2,1,0:T(8,128)(2,1)S(1)}, u32[]{:S(2)}, u32[]{:S(2)}) collective-permute-start(bf16[2,32,512]{2,1,0:T(8,128)(2,1)} %get-tuple-element.42), channel_id=1, source_target_pairs={{0,2},{1,3},{2,0},{3,1},{4,6},{5,7},{6,4},{7,5},{8,10},{9,11},{10,... | collective-permute-start | bytes 196616 | tf_op jit(solution)/shard_map/ppermute | solution.py:27
  4.9 5.6 %collective-permute-start.2 = (bf16[2,32,512]{2,1,0:T(8,128)(2,1)}, bf16[2,32,512]{2,1,0:T(8,128)(2,1)S(1)}, u32[]{:S(2)}, u32[]{:S(2)}) collective-permute-start(bf16[2,32,512]{2,1,0:T(8,128)(2,1)} %get-tuple-element.43), channel_id=1, source_target_pairs={{0,3},{1,0},{2,1},{3,2},{4,7},{5,4},{6,5},{7,6},{8,11},{9,8},{10,9... | collective-permute-start | bytes 196616 | tf_op jit(solution)/shard_map/ppermute | solution.py:27
  6.0 16.5 %copy-start = (bf16[4,32,4096]{2,1,0:T(8,128)(2,1)S(1)}, bf16[4,32,4096]{2,1,0:T(8,128)(2,1)}, u32[]{:S(2)}) copy-start(bf16[4,32,4096]{2,1,0:T(8,128)(2,1)} %query_ref.1) | copy-start | bytes 3145732
  6.0 16.5 %copy-start.1 = (bf16[4,32,4096]{2,1,0:T(8,128)(2,1)S(1)}, bf16[4,32,4096]{2,1,0:T(8,128)(2,1)}, u32[]{:S(2)}) copy-start(bf16[4,32,4096]{2,1,0:T(8,128)(2,1)} %grad_ref.1) | copy-start | bytes 3145732
  6.0 16.5 %copy-start.2 = (s32[4,1024]{1,0:T(4,128)S(1)}, s32[4,1024]{1,0:T(4,128)}, u32[]{:S(2)}) copy-start(s32[4,1024]{1,0:T(4,128)} %segment_ref.9) | copy-start | bytes 49156
  6.0 16.5 %copy-start.3 = (s32[4]{0:T(128)S(1)}, s32[4]{0:T(128)}, u32[]{:S(2)}) copy-start(s32[4]{0:T(128)} %assign_ref.13) | copy-start | bytes 52
  6.0 16.5 %copy-start.4 = (s32[2]{0:T(128)S(1)}, s32[2]{0:T(128)}, u32[]{:S(2)}) copy-start(s32[2]{0:T(128)} %pad_add_fusion.meta_ref) | copy-start | bytes 28
  10.5 16.4 %collective-permute-start.7 = (bf16[2,32,4096]{2,1,0:T(8,128)(2,1)}, bf16[2,32,4096]{2,1,0:T(8,128)(2,1)S(1)}, u32[]{:S(2)}, u32[]{:S(2)}) collective-permute-start(bf16[2,32,4096]{2,1,0:T(8,128)(2,1)} %get-tuple-element.51), channel_id=1, source_target_pairs={{0,1},{1,2},{2,3},{3,0},{4,5},{5,6},{6,7},{7,4},{8,9},{9,10},{10,1... | collective-permute-start | bytes 1572872 | tf_op jit(solution)/shard_map/ppermute | solution.py:27
  12.4 10.0 %collective-permute-start.4 = (bf16[4,2,32,512]{3,2,1,0:T(8,128)(2,1)S(1)}, bf16[4,2,32,512]{3,2,1,0:T(8,128)(2,1)S(1)}, u32[]{:S(2)}, u32[]{:S(2)}) collective-permute-start(bf16[4,2,32,512]{3,2,1,0:T(8,128)(2,1)S(1)} %bitcast_dynamic-update-slice_fusion), channel_id=1, source_target_pairs={{0,4},{4,8},{8,12},{12,16},{16,20},{20,24},{24,28},{1,5},{5,9},{9,... | collective-permute-start | bytes 786440 | tf_op jit(solution)/shard_map/ppermute | solution.py:33
  17.2 5.3 %collective-permute-start.3 = (bf16[4,2,32,512]{3,2,1,0:T(8,128)(2,1)S(1)}, bf16[4,2,32,512]{3,2,1,0:T(8,128)(2,1)S(1)}, u32[]{:S(2)}, u32[]{:S(2)}) collective-permute-start(bf16[4,2,32,512]{3,2,1,0:T(8,128)(2,1)S(1)} %bitcast_dynamic-update-slice_fusion), channel_id=1, source_target_pairs={{0,8},{4,12},{8,16},{12,20},{16,24},{20,28},{1,9},{5,13},{9,17},{1... | collective-permute-start | bytes 786440 | tf_op jit(solution)/shard_map/ppermute | solution.py:33
  19.1 38.8 %collective-permute-start.6 = (bf16[2,32,4096]{2,1,0:T(8,128)(2,1)}, bf16[2,32,4096]{2,1,0:T(8,128)(2,1)S(1)}, u32[]{:S(2)}, u32[]{:S(2)}) collective-permute-start(bf16[2,32,4096]{2,1,0:T(8,128)(2,1)} %get-tuple-element.50), channel_id=1, source_target_pairs={{0,2},{1,3},{2,0},{3,1},{4,6},{5,7},{6,4},{7,5},{8,10},{9,11},{10,... | collective-permute-start | bytes 1572872 | tf_op jit(solution)/shard_map/ppermute | solution.py:27
  19.2 42.7 %collective-permute-start.8 = (bf16[2,32,2048]{2,1,0:T(8,128)(2,1)}, bf16[2,32,2048]{2,1,0:T(8,128)(2,1)S(1)}, u32[]{:S(2)}, u32[]{:S(2)}) collective-permute-start(bf16[2,32,2048]{2,1,0:T(8,128)(2,1)} %get-tuple-element.57), channel_id=1, source_target_pairs={{0,3},{1,0},{2,1},{3,2},{4,7},{5,4},{6,5},{7,6},{8,11},{9,8},{10,9... | collective-permute-start | bytes 786440 | tf_op jit(solution)/shard_map/ppermute | solution.py:27
  22.6 3.9 %copy-start.5 = (bf16[2,32,2048]{2,1,0:T(8,128)(2,1)S(1)}, bf16[2,32,2048]{2,1,0:T(8,128)(2,1)}, u32[]{:S(2)}) copy-start(bf16[2,32,2048]{2,1,0:T(8,128)(2,1)} %get-tuple-element.49) | copy-start | bytes 786436
  26.5 43.8 %collective-permute-start.5 = (bf16[2,32,2048]{2,1,0:T(8,128)(2,1)S(1)}, bf16[2,32,2048]{2,1,0:T(8,128)(2,1)S(1)}, u32[]{:S(2)}, u32[]{:S(2)}) collective-permute-start(bf16[2,32,2048]{2,1,0:T(8,128)(2,1)S(1)} %copy-done.5), channel_id=1, source_target_pairs={{0,3},{1,0},{2,1},{3,2},{4,7},{5,4},{6,5},{7,6},{8,11},{9,8},{10,9... | collective-permute-start | bytes 786440 | tf_op jit(solution)/shard_map/ppermute | solution.py:27
  64.3 8.5 %collective-permute-start.9 = (bf16[2,128,256]{2,1,0:T(8,128)(2,1)S(1)}, bf16[2,128,256]{2,1,0:T(8,128)(2,1)S(1)}, u32[]{:S(2)}, u32[]{:S(2)}) collective-permute-start(bf16[2,128,256]{2,1,0:T(8,128)(2,1)S(1)} %get-tuple-element.62), channel_id=1, source_target_pairs={{4,0},{8,4},{12,8},{16,12},{20,16},{24,20},{28,24},{5,1},{9,5},{13... | collective-permute-start | bytes 393224 | tf_op jit(solution)/shard_map/ppermute | solution.py:33
  67.1 6.8 %collective-permute-start.10 = (bf16[2,128,256]{2,1,0:T(8,128)(2,1)S(1)}, bf16[2,128,256]{2,1,0:T(8,128)(2,1)S(1)}, u32[]{:S(2)}, u32[]{:S(2)}) collective-permute-start(bf16[2,128,256]{2,1,0:T(8,128)(2,1)S(1)} %get-tuple-element.63), channel_id=1, source_target_pairs={{8,0},{12,4},{16,8},{20,12},{24,16},{28,20},{9,1},{13,5},{17,9},{2... | collective-permute-start | bytes 393224 | tf_op jit(solution)/shard_map/ppermute | solution.py:33
  73.8 7.2 %collective-permute-start.11 = (bf16[2,128,256]{2,1,0:T(8,128)(2,1)S(1)}, bf16[2,128,256]{2,1,0:T(8,128)(2,1)S(1)}, u32[]{:S(2)}, u32[]{:S(2)}) collective-permute-start(bf16[2,128,256]{2,1,0:T(8,128)(2,1)S(1)} %get-tuple-element.67), channel_id=1, source_target_pairs={{4,0},{8,4},{12,8},{16,12},{20,16},{24,20},{28,24},{5,1},{9,5},{13... | collective-permute-start | bytes 393224 | tf_op jit(solution)/shard_map/ppermute | solution.py:33
  77.2 6.3 %collective-permute-start.12 = (bf16[2,128,256]{2,1,0:T(8,128)(2,1)S(1)}, bf16[2,128,256]{2,1,0:T(8,128)(2,1)S(1)}, u32[]{:S(2)}, u32[]{:S(2)}) collective-permute-start(bf16[2,128,256]{2,1,0:T(8,128)(2,1)S(1)} %get-tuple-element.68), channel_id=1, source_target_pairs={{8,0},{12,4},{16,8},{20,12},{24,16},{28,20},{9,1},{13,5},{17,9},{2... | collective-permute-start | bytes 393224 | tf_op jit(solution)/shard_map/ppermute | solution.py:33

commit v9 on v8

--- a/solution.py
+++ b/solution.py
@@ -260,17 +260,18 @@
     hops = -(-doc_most // tok_dev)
     meta = jnp.stack([group, line]).astype(jnp.int32)
 
-    final, halves = count - 1, kv_heads // HEADS_STEP
+    final, halves = count // 2, kv_heads // HEADS_STEP
     part = width // halves
+    others = [step for step in range(1, count) if step != final]
     kv_jobs = [(step, 0, kv_width) for step in range(count)]
     kv_staged = stage(meta, assignment, keys, values, kv_jobs)
-    jobs = [(step, 0, width) for step in range(1, final)]
+    jobs = [(step, 0, width) for step in others]
     jobs += [(final, half * part, part) for half in range(halves)]
     staged = stage(meta, assignment, queries, grad_out, jobs, after=kv_staged[:1])
     kv_arrived = [exchanged(kv_staged[step], "dp", step) for step in range(1, count)]
     staged, kv_arrived = lax.optimization_barrier((staged, kv_arrived))
-    arrived = [exchanged(staged[step - 1], "dp", step) for step in range(1, final)]
-    split = [exchanged(staged[final - 1], "dp", final)]
+    arrived = [exchanged(rows, "dp", step) for rows, step in zip(staged, others)]
+    held = staged[len(others) :]
     kv_own = jnp.zeros((count, *kv_staged[0].shape), keys.dtype)
     for step, piece in enumerate([kv_staged[0], *kv_arrived]):
         kv_own = lax.dynamic_update_index_in_dim(
@@ -282,12 +283,14 @@
     fixed = (doc_most, heads, meta, assignment, segment_ids)
     query, grad = (queries, lambda m, a: a[m[0]]), (grad_out, lambda m, a: a[m[0]])
     full, acc = attend(0, 0, kv_heads, *fixed, query, grad, kv, None, None, False)
-    rows, acc = lax.optimization_barrier((staged[final], acc))
-    split.append(exchanged(rows, "dp", final))
-    for step in range(1, final):
-        both = arrived[step - 1]
+    rows, acc = lax.optimization_barrier((held[0], acc))
+    split = [exchanged(rows, "dp", final)]
+    for step, both in zip(others, arrived):
         query, grad = (both, lambda m, a: 0), (both, lambda m, a: 1)
         full, acc = attend(step, 0, kv_heads, *fixed, query, grad, kv, acc, full, False)
+    for rows in held[1:]:
+        rows, acc = lax.optimization_barrier((rows, acc))
+        split.append(exchanged(rows, "dp", final))
     totals, returned = [], []
     for half, both in enumerate(split):
         query, grad = (both, lambda m, a: 0), (both, lambda m, a: 1)

time: 84.6 us -> 79.2 us (0.936)
  the two profiles are of different devices: /device:TPU:27 before, /device:TPU:1 now
where the time goes in v9:
time: 79.2 us; the launch traced here: 78.8 us
  starting transfers between devices  29.1 us (37%)
  waiting for transfers between devices  24.5 us (31%)
  Pallas kernels  21.9 us (28%)
  other arithmetic  1.5 us (2%)
  local copies, waits for them, and re-layouts  0.93 us (1%)
  between operations  0.84 us (1%)
    pallas_call x5, Pallas kernels, attend(): pl.pallas_call(functools.partial(attend_kernel, step, first, filled, last...  16.5 us
    ppermute x6, starting transfers between devices, shifted(): return lax.ppermute(value, axis, pairs)  16.3 us
    ppermute x7, waiting for transfers between devices, exchanged(): lax.ppermute(value, axis, [(i, (i + step) % count) for i in range(count)])  15.5 us
    ppermute x7, starting transfers between devices, exchanged(): lax.ppermute(value, axis, [(i, (i + step) % count) for i in range(count)])  12.8 us
    ppermute x6, waiting for transfers between devices, shifted(): return lax.ppermute(value, axis, pairs)  9.04 us
    pallas_call x2, Pallas kernels, stage(): pl.pallas_call(functools.partial(stage_kernel, count, jobs, len(shapes)),...  5.38 us
  transfers between devices with their start and end apart: 13, of which 8 were waited for; matrix products, arithmetic and copies ran while one was open for 1% of the time, Pallas kernels for 25%

profile of v9, /device:TPU:1, one launch (start us, length us, event | category | flops | bytes accessed | tf_op | source)
XLA Modules:
  0.0 78.8 jit_solution(13895729663592517708)
XLA Ops:
  1.2 2.3 %stage.2 = (bf16[2,32,512]{2,1,0:T(8,128)(2,1)}, bf16[2,32,512]{2,1,0:T(8,128)(2,1)}, bf16[2,32,512]{2,1,0:T(8,128)(2,1)}, bf16[2,32,512]{2,1,0:T(8,128)(2,1)}) custom-call(s32[2]{0:T(128)} %pad_add_fusion.meta_ref, s32[4]{0:T(128)} %assign_ref.13, bf16[4,32,512]{2,1,0:T(8,128)(2,1)} %first_ref.2, bf16[4,32,512]{2,1,0:T(8,128)(2,1)} %second_ref.2), custom_call_target="tpu_custom_call" | custom-call | tf_op jit(solution)/shard_map/stage/pallas_call | solution.py:60
  3.5 2.2 %collective-permute-start = (bf16[2,32,512]{2,1,0:T(8,128)(2,1)}, bf16[2,32,512]{2,1,0:T(8,128)(2,1)S(1)}, u32[]{:S(2)}, u32[]{:S(2)}) collective-permute-start(bf16[2,32,512]{2,1,0:T(8,128)(2,1)} %get-tuple-element.43), channel_id=1, source_target_pairs={{0,1},{1,2},{2,3},{3,0},{4,5},{5,6},{6,7},{7,4},{8,9},{9,10},{10,1... | collective-permute-start | bytes 196616 | tf_op jit(solution)/shard_map/ppermute | solution.py:27
  5.7 2.3 %collective-permute-start.1 = (bf16[2,32,512]{2,1,0:T(8,128)(2,1)}, bf16[2,32,512]{2,1,0:T(8,128)(2,1)S(1)}, u32[]{:S(2)}, u32[]{:S(2)}) collective-permute-start(bf16[2,32,512]{2,1,0:T(8,128)(2,1)} %get-tuple-element.44), channel_id=1, source_target_pairs={{0,2},{1,3},{2,0},{3,1},{4,6},{5,7},{6,4},{7,5},{8,10},{9,11},{10,... | collective-permute-start | bytes 196616 | tf_op jit(solution)/shard_map/ppermute | solution.py:27
  10.0 3.1 %stage.3 = (bf16[2,32,4096]{2,1,0:T(8,128)(2,1)}, bf16[2,32,4096]{2,1,0:T(8,128)(2,1)}, bf16[2,32,2048]{2,1,0:T(8,128)(2,1)}, bf16[2,32,2048]{2,1,0:T(8,128)(2,1)}) custom-call(s32[2]{0:T(128)} %pad_add_fusion.meta_ref, s32[4]{0:T(128)} %assign_ref.13, bf16[4,32,4096]{2,1,0:T(8,128)(2,1)} %query_ref.1, bf16[4,32,4096]{2,1,0:T(8,128)(2,1)} %grad_ref.1, ...), custom_call_target="tpu_custom_call" | custom-call | tf_op jit(solution)/shard_map/stage/pallas_call | solution.py:60
  13.3 1.7 %collective-permute-start.6 = (bf16[2,32,4096]{2,1,0:T(8,128)(2,1)}, bf16[2,32,4096]{2,1,0:T(8,128)(2,1)S(1)}, u32[]{:S(2)}, u32[]{:S(2)}) collective-permute-start(bf16[2,32,4096]{2,1,0:T(8,128)(2,1)} %get-tuple-element.51), channel_id=1, source_target_pairs={{0,1},{1,2},{2,3},{3,0},{4,5},{5,6},{6,7},{7,4},{8,9},{9,10},{10,1... | collective-permute-start | bytes 1572872 | tf_op jit(solution)/shard_map/ppermute | solution.py:27
  15.0 2.8 %collective-permute-start.5 = (bf16[4,2,32,512]{3,2,1,0:T(8,128)(2,1)S(1)}, bf16[4,2,32,512]{3,2,1,0:T(8,128)(2,1)S(1)}, u32[]{:S(2)}, u32[]{:S(2)}) collective-permute-start(bf16[4,2,32,512]{3,2,1,0:T(8,128)(2,1)S(1)} %bitcast_dynamic-update-slice_fusion), channel_id=1, source_target_pairs={{0,4},{4,8},{8,12},{12,16},{16,20},{20,24},{24,28},{1,5},{5,9},{9,... | collective-permute-start | bytes 786440 | tf_op jit(solution)/shard_map/ppermute | solution.py:33
  17.9 4.4 %collective-permute-start.4 = (bf16[4,2,32,512]{3,2,1,0:T(8,128)(2,1)S(1)}, bf16[4,2,32,512]{3,2,1,0:T(8,128)(2,1)S(1)}, u32[]{:S(2)}, u32[]{:S(2)}) collective-permute-start(bf16[4,2,32,512]{3,2,1,0:T(8,128)(2,1)S(1)} %bitcast_dynamic-update-slice_fusion), channel_id=1, source_target_pairs={{0,8},{4,12},{8,16},{12,20},{16,24},{20,28},{1,9},{5,13},{9,17},{1... | collective-permute-start | bytes 786440 | tf_op jit(solution)/shard_map/ppermute | solution.py:33
  22.3 2.5 %collective-permute-start.3 = (bf16[2,32,4096]{2,1,0:T(8,128)(2,1)}, bf16[2,32,4096]{2,1,0:T(8,128)(2,1)S(1)}, u32[]{:S(2)}, u32[]{:S(2)}) collective-permute-start(bf16[2,32,4096]{2,1,0:T(8,128)(2,1)} %get-tuple-element.47), channel_id=1, source_target_pairs={{0,3},{1,0},{2,1},{3,2},{4,7},{5,4},{6,5},{7,6},{8,11},{9,8},{10,9... | collective-permute-start | bytes 1572872 | tf_op jit(solution)/shard_map/ppermute | solution.py:27
  25.1 2.0 %collective-permute-done.4 = bf16[4,2,32,512]{3,2,1,0:T(8,128)(2,1)S(1)} collective-permute-done((bf16[4,2,32,512]{3,2,1,0:T(8,128)(2,1)S(1)}, bf16[4,2,32,512]{3,2,1,0:T(8,128)(2,1)S(1)}, u32[]{:S(2)}, u32[]{:S(2)}) %collective-permute-start.4) | collective-permute-done | bytes 262176 | tf_op jit(solution)/shard_map/ppermute | solution.py:33
  27.3 3.9 %attend.5 = (bf16[128,32,128]{2,1,0:T(8,128)(2,1)}, f32[2,384,512]{2,1,0:T(8,128)S(1)}) custom-call(s32[2]{0:T(128)S(1)} %copy-done.4, s32[4]{0:T(128)S(1)} %copy-done.3, s32[4,1024]{1,0:T(4,128)S(1)} %copy-done.2, bf16[4,32,4096]{2,1,0:T(8,128)(2,1)S(1)} %copy-done, bf16[4,32,4096]{2,1,0:T(8,128)(2,1)S(1)} %copy-done.1, ...), custom_call_target="tpu_custom_call" | custom-call | flops 37748736 | bytes 294912 | tf_op jit(solution)/shard_map/attend/pallas_call | solution.py:230
  31.2 1.7 %collective-permute-start.8 = (bf16[2,32,2048]{2,1,0:T(8,128)(2,1)S(1)}, bf16[2,32,2048]{2,1,0:T(8,128)(2,1)S(1)}, u32[]{:S(2)}, u32[]{:S(2)}) collective-permute-start(bf16[2,32,2048]{2,1,0:T(8,128)(2,1)S(1)} %copy-done.6), channel_id=1, source_target_pairs={{0,2},{1,3},{2,0},{3,1},{4,6},{5,7},{6,4},{7,5},{8,10},{9,11},{10,... | collective-permute-start | bytes 786440 | tf_op jit(solution)/shard_map/ppermute | solution.py:27
  33.0 3.9 %attend.6 = (bf16[128,32,128]{2,1,0:T(8,128)(2,1)}, f32[2,384,512]{2,1,0:T(8,128)S(1)}) custom-call(s32[2]{0:T(128)S(1)} %copy-done.4, s32[4]{0:T(128)S(1)} %copy-done.3, s32[4,1024]{1,0:T(4,128)S(1)} %copy-done.2, bf16[2,32,4096]{2,1,0:T(8,128)(2,1)S(1)} %collective-permute-done.6.query_ref.grad_ref, ...), custom_call_target="tpu_custom_call", output_to_operand_aliasing={{1}: (6, {}), {0}: (7, {})} | custom-call | flops 37748736 | bytes 294912 | tf_op jit(solution)/shard_map/attend/pallas_call | solution.py:230
  36.9 3.5 %collective-permute-done.3.query_ref.grad_ref = bf16[2,32,4096]{2,1,0:T(8,128)(2,1)S(1)} collective-permute-done((bf16[2,32,4096]{2,1,0:T(8,128)(2,1)}, bf16[2,32,4096]{2,1,0:T(8,128)(2,1)S(1)}, u32[]{:S(2)}, u32[]{:S(2)}) %collective-permute-start.3) | collective-permute-done | bytes 524320 | tf_op jit(solution)/shard_map/ppermute | solution.py:27
  40.3 3.9 %attend.7 = (bf16[128,32,128]{2,1,0:T(8,128)(2,1)}, f32[2,384,512]{2,1,0:T(8,128)S(1)}) custom-call(s32[2]{0:T(128)S(1)} %copy-done.4, s32[4]{0:T(128)S(1)} %copy-done.3, s32[4,1024]{1,0:T(4,128)S(1)} %copy-done.2, bf16[2,32,4096]{2,1,0:T(8,128)(2,1)S(1)} %collective-permute-done.3.query_ref.grad_ref, ...), custom_call_target="tpu_custom_call", output_to_operand_aliasing={{1}: (6, {}), {0}: (7, {})} | custom-call | flops 37748736 | bytes 294912 | tf_op jit(solution)/shard_map/attend/pallas_call | solution.py:230
  45.5 11.9 %collective-permute-done.8.query_ref.grad_ref = bf16[2,32,2048]{2,1,0:T(8,128)(2,1)S(1)} collective-permute-done((bf16[2,32,2048]{2,1,0:T(8,128)(2,1)S(1)}, bf16[2,32,2048]{2,1,0:T(8,128)(2,1)S(1)}, u32[]{:S(2)}, u32[]{:S(2)}) %collective-permute-start.8) | collective-permute-done | bytes 262176 | tf_op jit(solution)/shard_map/ppermute | solution.py:27
  57.4 2.4 %attend.8 = (bf16[128,32,128]{2,1,0:T(8,128)(2,1)}, f32[2,128,256]{2,1,0:T(8,128)S(1)}, bf16[2,128,256]{2,1,0:T(8,128)(2,1)S(1)}, bf16[2,128,256]{2,1,0:T(8,128)(2,1)S(1)}) custom-call(s32[2]{0:T(128)S(1)} %copy-done.4, s32[4]{0:T(128)S(1)} %copy-done.3, s32[4,1024]{1,0:T(4,128)S(1)} %copy-done.2, ...), custom_call_target="tpu_custom_call", output_to_operand_aliasing={{0}: (7, {})} | custom-call | flops 18874368 | bytes 147456 | tf_op jit(solution)/shard_map/attend/pallas_call | solution.py:230
  59.8 3.3 %collective-permute-start.9 = (bf16[2,128,256]{2,1,0:T(8,128)(2,1)S(1)}, bf16[2,128,256]{2,1,0:T(8,128)(2,1)S(1)}, u32[]{:S(2)}, u32[]{:S(2)}) collective-permute-start(bf16[2,128,256]{2,1,0:T(8,128)(2,1)S(1)} %get-tuple-element.66), channel_id=1, source_target_pairs={{4,0},{8,4},{12,8},{16,12},{20,16},{24,20},{28,24},{5,1},{9,5},{13... | collective-permute-start | bytes 393224 | tf_op jit(solution)/shard_map/ppermute | solution.py:33
  63.1 1.9 %collective-permute-start.10 = (bf16[2,128,256]{2,1,0:T(8,128)(2,1)S(1)}, bf16[2,128,256]{2,1,0:T(8,128)(2,1)S(1)}, u32[]{:S(2)}, u32[]{:S(2)}) collective-permute-start(bf16[2,128,256]{2,1,0:T(8,128)(2,1)S(1)} %get-tuple-element.67), channel_id=1, source_target_pairs={{8,0},{12,4},{16,8},{20,12},{24,16},{28,20},{9,1},{13,5},{17,9},{2... | collective-permute-start | bytes 393224 | tf_op jit(solution)/shard_map/ppermute | solution.py:33
  65.0 2.4 %attend.9 = (bf16[128,32,128]{2,1,0:T(8,128)(2,1)}, f32[2,128,256]{2,1,0:T(8,128)S(1)}, bf16[2,128,256]{2,1,0:T(8,128)(2,1)S(1)}, bf16[2,128,256]{2,1,0:T(8,128)(2,1)S(1)}) custom-call(s32[2]{0:T(128)S(1)} %copy-done.4, s32[4]{0:T(128)S(1)} %copy-done.3, s32[4,1024]{1,0:T(4,128)S(1)} %copy-done.2, ...), custom_call_target="tpu_custom_call", output_to_operand_aliasing={{0}: (7, {})} | custom-call | flops 18874368 | bytes 147456 | tf_op jit(solution)/shard_map/attend/pallas_call | solution.py:230
  67.4 2.0 %collective-permute-done.10 = bf16[2,128,256]{2,1,0:T(8,128)(2,1)S(1)} collective-permute-done((bf16[2,128,256]{2,1,0:T(8,128)(2,1)S(1)}, bf16[2,128,256]{2,1,0:T(8,128)(2,1)S(1)}, u32[]{:S(2)}, u32[]{:S(2)}) %collective-permute-start.10) | collective-permute-done | bytes 131104 | tf_op jit(solution)/shard_map/ppermute | solution.py:33
  69.3 1.9 %collective-permute-start.11 = (bf16[2,128,256]{2,1,0:T(8,128)(2,1)S(1)}, bf16[2,128,256]{2,1,0:T(8,128)(2,1)S(1)}, u32[]{:S(2)}, u32[]{:S(2)}) collective-permute-start(bf16[2,128,256]{2,1,0:T(8,128)(2,1)S(1)} %get-tuple-element.71), channel_id=1, source_target_pairs={{4,0},{8,4},{12,8},{16,12},{20,16},{24,20},{28,24},{5,1},{9,5},{13... | collective-permute-start | bytes 393224 | tf_op jit(solution)/shard_map/ppermute | solution.py:33
  71.3 1.9 %collective-permute-start.12 = (bf16[2,128,256]{2,1,0:T(8,128)(2,1)S(1)}, bf16[2,128,256]{2,1,0:T(8,128)(2,1)S(1)}, u32[]{:S(2)}, u32[]{:S(2)}) collective-permute-start(bf16[2,128,256]{2,1,0:T(8,128)(2,1)S(1)} %get-tuple-element.72), channel_id=1, source_target_pairs={{8,0},{12,4},{16,8},{20,12},{24,16},{28,20},{9,1},{13,5},{17,9},{2... | collective-permute-start | bytes 393224 | tf_op jit(solution)/shard_map/ppermute | solution.py:33
  73.2 1.9 %collective-permute-done.11 = bf16[2,128,256]{2,1,0:T(8,128)(2,1)S(1)} collective-permute-done((bf16[2,128,256]{2,1,0:T(8,128)(2,1)S(1)}, bf16[2,128,256]{2,1,0:T(8,128)(2,1)S(1)}, u32[]{:S(2)}, u32[]{:S(2)}) %collective-permute-start.11) | collective-permute-done | bytes 131104 | tf_op jit(solution)/shard_map/ppermute | solution.py:33
  75.1 2.9 %collective-permute-done.12 = bf16[2,128,256]{2,1,0:T(8,128)(2,1)S(1)} collective-permute-done((bf16[2,128,256]{2,1,0:T(8,128)(2,1)S(1)}, bf16[2,128,256]{2,1,0:T(8,128)(2,1)S(1)}, u32[]{:S(2)}, u32[]{:S(2)}) %collective-permute-start.12) | collective-permute-done | bytes 131104 | tf_op jit(solution)/shard_map/ppermute | solution.py:33
  (33 shorter events, 5.2 us)
Async XLA Ops:
  3.5 9.6 %collective-permute-start = (bf16[2,32,512]{2,1,0:T(8,128)(2,1)}, bf16[2,32,512]{2,1,0:T(8,128)(2,1)S(1)}, u32[]{:S(2)}, u32[]{:S(2)}) collective-permute-start(bf16[2,32,512]{2,1,0:T(8,128)(2,1)} %get-tuple-element.43), channel_id=1, source_target_pairs={{0,1},{1,2},{2,3},{3,0},{4,5},{5,6},{6,7},{7,4},{8,9},{9,10},{10,1... | collective-permute-start | bytes 196616 | tf_op jit(solution)/shard_map/ppermute | solution.py:27
  5.7 7.5 %collective-permute-start.1 = (bf16[2,32,512]{2,1,0:T(8,128)(2,1)}, bf16[2,32,512]{2,1,0:T(8,128)(2,1)S(1)}, u32[]{:S(2)}, u32[]{:S(2)}) collective-permute-start(bf16[2,32,512]{2,1,0:T(8,128)(2,1)} %get-tuple-element.44), channel_id=1, source_target_pairs={{0,2},{1,3},{2,0},{3,1},{4,6},{5,7},{6,4},{7,5},{8,10},{9,11},{10,... | collective-permute-start | bytes 196616 | tf_op jit(solution)/shard_map/ppermute | solution.py:27
  8.0 5.2 %collective-permute-start.2 = (bf16[2,32,512]{2,1,0:T(8,128)(2,1)}, bf16[2,32,512]{2,1,0:T(8,128)(2,1)S(1)}, u32[]{:S(2)}, u32[]{:S(2)}) collective-permute-start(bf16[2,32,512]{2,1,0:T(8,128)(2,1)} %get-tuple-element.45), channel_id=1, source_target_pairs={{0,3},{1,0},{2,1},{3,2},{4,7},{5,4},{6,5},{7,6},{8,11},{9,8},{10,9... | collective-permute-start | bytes 196616 | tf_op jit(solution)/shard_map/ppermute | solution.py:27
  10.0 17.2 %copy-start = (bf16[4,32,4096]{2,1,0:T(8,128)(2,1)S(1)}, bf16[4,32,4096]{2,1,0:T(8,128)(2,1)}, u32[]{:S(2)}) copy-start(bf16[4,32,4096]{2,1,0:T(8,128)(2,1)} %query_ref.1) | copy-start | bytes 3145732
  10.0 17.2 %copy-start.1 = (bf16[4,32,4096]{2,1,0:T(8,128)(2,1)S(1)}, bf16[4,32,4096]{2,1,0:T(8,128)(2,1)}, u32[]{:S(2)}) copy-start(bf16[4,32,4096]{2,1,0:T(8,128)(2,1)} %grad_ref.1) | copy-start | bytes 3145732
  10.0 17.3 %copy-start.2 = (s32[4,1024]{1,0:T(4,128)S(1)}, s32[4,1024]{1,0:T(4,128)}, u32[]{:S(2)}) copy-start(s32[4,1024]{1,0:T(4,128)} %segment_ref.9) | copy-start | bytes 49156
  10.0 17.2 %copy-start.3 = (s32[4]{0:T(128)S(1)}, s32[4]{0:T(128)}, u32[]{:S(2)}) copy-start(s32[4]{0:T(128)} %assign_ref.13) | copy-start | bytes 52
  10.0 17.2 %copy-start.4 = (s32[2]{0:T(128)S(1)}, s32[2]{0:T(128)}, u32[]{:S(2)}) copy-start(s32[2]{0:T(128)} %pad_add_fusion.meta_ref) | copy-start | bytes 28
  13.3 19.7 %collective-permute-start.6 = (bf16[2,32,4096]{2,1,0:T(8,128)(2,1)}, bf16[2,32,4096]{2,1,0:T(8,128)(2,1)S(1)}, u32[]{:S(2)}, u32[]{:S(2)}) collective-permute-start(bf16[2,32,4096]{2,1,0:T(8,128)(2,1)} %get-tuple-element.51), channel_id=1, source_target_pairs={{0,1},{1,2},{2,3},{3,0},{4,5},{5,6},{6,7},{7,4},{8,9},{9,10},{10,1... | collective-permute-start | bytes 1572872 | tf_op jit(solution)/shard_map/ppermute | solution.py:27
  15.0 10.1 %collective-permute-start.5 = (bf16[4,2,32,512]{3,2,1,0:T(8,128)(2,1)S(1)}, bf16[4,2,32,512]{3,2,1,0:T(8,128)(2,1)S(1)}, u32[]{:S(2)}, u32[]{:S(2)}) collective-permute-start(bf16[4,2,32,512]{3,2,1,0:T(8,128)(2,1)S(1)} %bitcast_dynamic-update-slice_fusion), channel_id=1, source_target_pairs={{0,4},{4,8},{8,12},{12,16},{16,20},{20,24},{24,28},{1,5},{5,9},{9,... | collective-permute-start | bytes 786440 | tf_op jit(solution)/shard_map/ppermute | solution.py:33
  17.9 9.3 %collective-permute-start.4 = (bf16[4,2,32,512]{3,2,1,0:T(8,128)(2,1)S(1)}, bf16[4,2,32,512]{3,2,1,0:T(8,128)(2,1)S(1)}, u32[]{:S(2)}, u32[]{:S(2)}) collective-permute-start(bf16[4,2,32,512]{3,2,1,0:T(8,128)(2,1)S(1)} %bitcast_dynamic-update-slice_fusion), channel_id=1, source_target_pairs={{0,8},{4,12},{8,16},{12,20},{16,24},{20,28},{1,9},{5,13},{9,17},{1... | collective-permute-start | bytes 786440 | tf_op jit(solution)/shard_map/ppermute | solution.py:33
  22.3 18.1 %collective-permute-start.3 = (bf16[2,32,4096]{2,1,0:T(8,128)(2,1)}, bf16[2,32,4096]{2,1,0:T(8,128)(2,1)S(1)}, u32[]{:S(2)}, u32[]{:S(2)}) collective-permute-start(bf16[2,32,4096]{2,1,0:T(8,128)(2,1)} %get-tuple-element.47), channel_id=1, source_target_pairs={{0,3},{1,0},{2,1},{3,2},{4,7},{5,4},{6,5},{7,6},{8,11},{9,8},{10,9... | collective-permute-start | bytes 1572872 | tf_op jit(solution)/shard_map/ppermute | solution.py:27
  27.3 3.9 %copy-start.6 = (bf16[2,32,2048]{2,1,0:T(8,128)(2,1)S(1)}, bf16[2,32,2048]{2,1,0:T(8,128)(2,1)}, u32[]{:S(2)}) copy-start(bf16[2,32,2048]{2,1,0:T(8,128)(2,1)} %get-tuple-element.61) | copy-start | bytes 786436
  31.2 26.2 %collective-permute-start.8 = (bf16[2,32,2048]{2,1,0:T(8,128)(2,1)S(1)}, bf16[2,32,2048]{2,1,0:T(8,128)(2,1)S(1)}, u32[]{:S(2)}, u32[]{:S(2)}) collective-permute-start(bf16[2,32,2048]{2,1,0:T(8,128)(2,1)S(1)} %copy-done.6), channel_id=1, source_target_pairs={{0,2},{1,3},{2,0},{3,1},{4,6},{5,7},{6,4},{7,5},{8,10},{9,11},{10,... | collective-permute-start | bytes 786440 | tf_op jit(solution)/shard_map/ppermute | solution.py:27
  40.3 3.9 %copy-start.5 = (bf16[2,32,2048]{2,1,0:T(8,128)(2,1)S(1)}, bf16[2,32,2048]{2,1,0:T(8,128)(2,1)}, u32[]{:S(2)}) copy-start(bf16[2,32,2048]{2,1,0:T(8,128)(2,1)} %get-tuple-element.59) | copy-start | bytes 786436
  44.3 20.7 %collective-permute-start.7 = (bf16[2,32,2048]{2,1,0:T(8,128)(2,1)S(1)}, bf16[2,32,2048]{2,1,0:T(8,128)(2,1)S(1)}, u32[]{:S(2)}, u32[]{:S(2)}) collective-permute-start(bf16[2,32,2048]{2,1,0:T(8,128)(2,1)S(1)} %copy-done.5), channel_id=1, source_target_pairs={{0,2},{1,3},{2,0},{3,1},{4,6},{5,7},{6,4},{7,5},{8,10},{9,11},{10,... | collective-permute-start | bytes 786440 | tf_op jit(solution)/shard_map/ppermute | solution.py:27
  59.8 7.6 %collective-permute-start.9 = (bf16[2,128,256]{2,1,0:T(8,128)(2,1)S(1)}, bf16[2,128,256]{2,1,0:T(8,128)(2,1)S(1)}, u32[]{:S(2)}, u32[]{:S(2)}) collective-permute-start(bf16[2,128,256]{2,1,0:T(8,128)(2,1)S(1)} %get-tuple-element.66), channel_id=1, source_target_pairs={{4,0},{8,4},{12,8},{16,12},{20,16},{24,20},{28,24},{5,1},{9,5},{13... | collective-permute-start | bytes 393224 | tf_op jit(solution)/shard_map/ppermute | solution.py:33
  63.1 6.3 %collective-permute-start.10 = (bf16[2,128,256]{2,1,0:T(8,128)(2,1)S(1)}, bf16[2,128,256]{2,1,0:T(8,128)(2,1)S(1)}, u32[]{:S(2)}, u32[]{:S(2)}) collective-permute-start(bf16[2,128,256]{2,1,0:T(8,128)(2,1)S(1)} %get-tuple-element.67), channel_id=1, source_target_pairs={{8,0},{12,4},{16,8},{20,12},{24,16},{28,20},{9,1},{13,5},{17,9},{2... | collective-permute-start | bytes 393224 | tf_op jit(solution)/shard_map/ppermute | solution.py:33
  69.3 5.8 %collective-permute-start.11 = (bf16[2,128,256]{2,1,0:T(8,128)(2,1)S(1)}, bf16[2,128,256]{2,1,0:T(8,128)(2,1)S(1)}, u32[]{:S(2)}, u32[]{:S(2)}) collective-permute-start(bf16[2,128,256]{2,1,0:T(8,128)(2,1)S(1)} %get-tuple-element.71), channel_id=1, source_target_pairs={{4,0},{8,4},{12,8},{16,12},{20,16},{24,20},{28,24},{5,1},{9,5},{13... | collective-permute-start | bytes 393224 | tf_op jit(solution)/shard_map/ppermute | solution.py:33
  71.3 6.7 %collective-permute-start.12 = (bf16[2,128,256]{2,1,0:T(8,128)(2,1)S(1)}, bf16[2,128,256]{2,1,0:T(8,128)(2,1)S(1)}, u32[]{:S(2)}, u32[]{:S(2)}) collective-permute-start(bf16[2,128,256]{2,1,0:T(8,128)(2,1)S(1)} %get-tuple-element.72), channel_id=1, source_target_pairs={{8,0},{12,4},{16,8},{20,12},{24,16},{28,20},{9,1},{13,5},{17,9},{2... | collective-permute-start | bytes 393224 | tf_op jit(solution)/shard_map/ppermute | solution.py:33

commit v10 on v9

--- a/solution.py
+++ b/solution.py
@@ -33,17 +33,19 @@
     return lax.ppermute(value, axis, pairs)
 
 
-def stage_kernel(count, jobs, outs, meta_ref, assign_ref, first_ref, second_ref, *refs):
-    group = meta_ref[0]
-    out_refs, held_refs, (in_sems, out_sems) = refs[-2 - 2 * outs : -2 - outs], refs[-2 - outs : -2], refs[-2:]
+def stage_kernel(count, jobs, outs, assign_ref, *refs):
+    group = lax.axis_index("dp")
+    sources, refs = refs[:4], refs[4:]
+    out_refs, held_refs, (in_sems, out_sems) = refs[:outs], refs[outs : 2 * outs], refs[-2:]
     loads, stores = [], []
-    for out, (step, start, width) in enumerate(jobs):
+    for out, (first, step, start, width) in enumerate(jobs):
         chosen = assign_ref[target_of(group, step, count)]
-        for which, source in enumerate((first_ref, second_ref)):
-            origin = source.at[chosen, :, start : start + width]
-            held, goal, slot = held_refs[out].at[which], out_refs[out].at[which], 2 * out + which
+        goal = out_refs[out] if step else out_refs[out].at[group]
+        for which in range(2):
+            origin = sources[first + which].at[chosen, :, start : start + width]
+            held, slot = held_refs[out].at[which], 2 * out + which
             loads.append(pltpu.make_async_copy(origin, held, in_sems.at[slot]))
-            stores.append(pltpu.make_async_copy(held, goal, out_sems.at[slot]))
+            stores.append(pltpu.make_async_copy(held, goal.at[which], out_sems.at[slot]))
     for load in loads:
         load.start()
     for load, store in zip(loads, stores):
@@ -53,19 +55,21 @@
         store.wait()
 
 
-def stage(meta, assignment, first, second, jobs, after=()):
-    count, rows, _ = first.shape
-    shapes = [(2, rows, width) for _, _, width in jobs]
-    far, scalars = pl.BlockSpec(memory_space=pltpu.HBM), pl.BlockSpec(memory_space=pltpu.SMEM)
+def stage(assignment, arrays, jobs):
+    count, rows, _ = arrays[0].shape
+    held = [(2, rows, width) for _, _, _, width in jobs]
+    shapes = [shape if job[1] else (count, *shape) for shape, job in zip(held, jobs)]
+    kind = arrays[0].dtype
+    far = pl.BlockSpec(memory_space=pltpu.HBM)
     return pl.pallas_call(
-        functools.partial(stage_kernel, count, jobs, len(shapes)),
-        out_shape=[jax.ShapeDtypeStruct(shape, first.dtype) for shape in shapes],
-        in_specs=[scalars] * 2 + [far] * 2 + [pl.BlockSpec(memory_space=pl.ANY)] * len(after),
-        out_specs=[far] * len(shapes),
-        scratch_shapes=[pltpu.VMEM(shape, first.dtype) for shape in shapes]
-        + [pltpu.SemaphoreType.DMA((2 * len(shapes),))] * 2,
+        functools.partial(stage_kernel, count, jobs, len(jobs)),
+        out_shape=[jax.ShapeDtypeStruct(shape, kind) for shape in shapes],
+        in_specs=[pl.BlockSpec(memory_space=pltpu.SMEM)] + [far] * len(arrays),
+        out_specs=[far] * len(jobs),
+        scratch_shapes=[pltpu.VMEM(shape, kind) for shape in held]
+        + [pltpu.SemaphoreType.DMA((2 * len(jobs),))] * 2,
         name="stage",
-    )(meta, assignment, first, second, *after)
+    )(assignment, *arrays)
 
 
 def build_bias(source, sequence, line, segment_ref, column_ref, bias_ref, rows, tok_dev, reach):
@@ -199,7 +203,7 @@
     in_specs.append(pl.BlockSpec((blocks, 2, rows, lanes), lambda c, m, a: (0, 0, 0, place + c)))
     operands = [meta, assignment, segments, query[0], grad[0], kv]
     aliases = {}
-    acc_spec = pl.BlockSpec((2, keys, lanes), lambda c, m, a: (0, 0, place + c))
+    acc_spec = pl.BlockSpec((2, keys, lanes), lambda c, m, a: (0, 0, c))
     if not first:
         if not last:
             aliases[len(operands)] = 1
@@ -222,7 +226,7 @@
         out_shape += [jax.ShapeDtypeStruct((2, tok_dev, span * HD), jnp.bfloat16)] * (pieces - 1)
         out_specs += [span_spec] * pieces
     else:
-        out_shape.append(jax.ShapeDtypeStruct((2, keys, kv_width), jnp.float32))
+        out_shape.append(jax.ShapeDtypeStruct((2, keys, span * HD), jnp.float32))
         out_specs.append(acc_spec)
     pairs = span * ratio * rows * window
     held = (keys, ratio * rows), (window, ratio * rows)
@@ -263,17 +267,17 @@
     final, halves = count // 2, kv_heads // HEADS_STEP
     part = width // halves
     others = [step for step in range(1, count) if step != final]
-    kv_jobs = [(step, 0, kv_width) for step in range(count)]
-    kv_staged = stage(meta, assignment, keys, values, kv_jobs)
-    jobs = [(step, 0, width) for step in others]
-    jobs += [(final, half * part, part) for half in range(halves)]
-    staged = stage(meta, assignment, queries, grad_out, jobs, after=kv_staged[:1])
-    kv_arrived = [exchanged(kv_staged[step], "dp", step) for step in range(1, count)]
-    staged, kv_arrived = lax.optimization_barrier((staged, kv_arrived))
-    arrived = [exchanged(rows, "dp", step) for rows, step in zip(staged, others)]
-    held = staged[len(others) :]
-    kv_own = jnp.zeros((count, *kv_staged[0].shape), keys.dtype)
-    for step, piece in enumerate([kv_staged[0], *kv_arrived]):
+    jobs = [(2, step, 0, kv_width) for step in range(count)]
+    order = [*others[1:], final]
+    jobs.append((0, others[0], 0, width))
+    jobs += [(0, step, half * part, part) for half in range(halves) for step in order]
+    kv_own, *staged = stage(assignment, (queries, grad_out, keys, values), jobs)
+    kv_arrived = [exchanged(staged[step - 1], "dp", step) for step in range(1, count)]
+    ahead, behind = staged[count - 1 : count + len(order)], staged[count + len(order) :]
+    ahead, kv_arrived = lax.optimization_barrier((ahead, kv_arrived))
+    whole = exchanged(ahead[0], "dp", others[0])
+    arrived = [[exchanged(rows, "dp", step) for rows, step in zip(ahead[1:], order)]]
+    for step, piece in enumerate(kv_arrived, 1):
         kv_own = lax.dynamic_update_index_in_dim(
             kv_own, piece, source_of(group, step, count), 0
         )
@@ -281,25 +285,37 @@
     kv = jnp.concatenate([*halos, kv_own], axis=0)
 
     fixed = (doc_most, heads, meta, assignment, segment_ids)
-    query, grad = (queries, lambda m, a: a[m[0]]), (grad_out, lambda m, a: a[m[0]])
-    full, acc = attend(0, 0, kv_heads, *fixed, query, grad, kv, None, None, False)
-    rows, acc = lax.optimization_barrier((held[0], acc))
-    split = [exchanged(rows, "dp", final)]
-    for step, both in zip(others, arrived):
-        query, grad = (both, lambda m, a: 0), (both, lambda m, a: 1)
-        full, acc = attend(step, 0, kv_heads, *fixed, query, grad, kv, acc, full, False)
-    for rows in held[1:]:
-        rows, acc = lax.optimization_barrier((rows, acc))
-        split.append(exchanged(rows, "dp", final))
-    totals, returned = [], []
-    for half, both in enumerate(split):
-        query, grad = (both, lambda m, a: 0), (both, lambda m, a: 1)
-        full, total, *halos = attend(
-            final, half * HEADS_STEP, HEADS_STEP, *fixed, query, grad, kv, acc, full, True
-        )
+    own = (queries, lambda m, a: a[m[0]]), (grad_out, lambda m, a: a[m[0]])
+    first = (whole, lambda m, a: 0), (whole, lambda m, a: 1)
+    accs, full, totals, returned = [], None, [], []
+    for half in range(halves):
+        base = half * HEADS_STEP
+        full, acc = attend(0, base, HEADS_STEP, *fixed, *own, kv, None, full, False)
+        if not half:
+            behind, acc = lax.optimization_barrier((behind, acc))
+        accs.append(acc)
+    for half in range(halves):
+        base = half * HEADS_STEP
+        full, accs[half] = attend(
+            others[0], base, HEADS_STEP, *fixed, *first, kv, accs[half], full, False
+        )
+    for half in range(halves):
+        base = half * HEADS_STEP
+        if half:
+            rows, full = lax.optimization_barrier((behind[half * len(order) - 1], full))
+            arrived[half].append(exchanged(rows, "dp", final))
+        if half + 1 < halves:
+            rows = behind[half * len(order) : (half + 1) * len(order) - 1]
+            arrived.append([exchanged(piece, "dp", step) for piece, step in zip(rows, order)])
+        for both, step in zip(arrived[half], order):
+            pair = (both, lambda m, a: 0), (both, lambda m, a: 1)
+            full, accs[half], *halos = attend(
+                step, base, HEADS_STEP, *fixed, *pair, kv, accs[half], full, step == final
+            )
         if half:
             halos, returned = lax.optimization_barrier((halos, returned))
         returned = [shifted(halo, ("blk", "uly"), -back) for back, halo in enumerate(halos, 1)]
+        total = accs[half]
         for halo in returned:
             total = total + halo.astype(jnp.float32)
         totals.append(total.astype(jnp.bfloat16))

time: 79.2 us -> 78.6 us (level)
  the two profiles are of different devices: /device:TPU:1 before, /device:TPU:11 now
where the time goes in v10:
time: 78.6 us; the launch traced here: 78.3 us
  starting transfers between devices  33.2 us (42%)
  Pallas kernels  22.5 us (29%)
  waiting for transfers between devices  17.9 us (23%)
  other arithmetic  2 us (3%)
  local copies, waits for them, and re-layouts  1.93 us (2%)
    ppermute x6, starting transfers between devices, shifted(): return lax.ppermute(value, axis, pairs)  21.1 us
    pallas_call x8, Pallas kernels, attend(): pl.pallas_call(functools.partial(attend_kernel, step, first, filled, last...  19.2 us
    ppermute x8, waiting for transfers between devices, exchanged(): lax.ppermute(value, axis, [(i, (i + step) % count) for i in range(count)])  12.5 us
    ppermute x8, starting transfers between devices, exchanged(): lax.ppermute(value, axis, [(i, (i + step) % count) for i in range(count)])  12.1 us
    ppermute x6, waiting for transfers between devices, shifted(): return lax.ppermute(value, axis, pairs)  5.37 us
    pallas_call x1, Pallas kernels, stage(): pl.pallas_call(functools.partial(stage_kernel, count, jobs, len(jobs)), o...  3.36 us
    dynamic_update_slice x3, local copies, waits for them, and re-layouts, shards(): lax.dynamic_update_index_in_dim(kv_own, piece, source_of(group, step, cou...  1.9 us
  transfers between devices with their start and end apart: 14, of which 5 were waited for; matrix products, arithmetic and copies ran while one was open for 4% of the time, Pallas kernels for 24%

profile of v10, /device:TPU:11, one launch (start us, length us, event | category | flops | bytes accessed | tf_op | source)
XLA Modules:
  0.0 78.3 jit_solution(9444441845203509884)
XLA Ops:
  0.6 3.4 %stage.1 = (bf16[4,2,32,512]{3,2,1,0:T(8,128)(2,1)}, bf16[2,32,512]{2,1,0:T(8,128)(2,1)}, bf16[2,32,512]{2,1,0:T(8,128)(2,1)}, bf16[2,32,512]{2,1,0:T(8,128)(2,1...) custom-call(s32[4]{0:T(128)} %assign_ref.17, ...), custom_call_target="tpu_custom_call" | custom-call | tf_op jit(solution)/shard_map/stage/pallas_call | solution.py:64
  6.5 1.4 %collective-permute-start.2 = (bf16[2,32,512]{2,1,0:T(8,128)(2,1)}, bf16[2,32,512]{2,1,0:T(8,128)(2,1)S(1)}, u32[]{:S(2)}, u32[]{:S(2)}) collective-permute-start(bf16[2,32,512]{2,1,0:T(8,128)(2,1)} %get-tuple-element.53), channel_id=1, source_target_pairs={{0,3},{1,0},{2,1},{3,2},{4,7},{5,4},{6,5},{7,6},{8,11},{9,8},{10,9... | collective-permute-start | bytes 196616 | tf_op jit(solution)/shard_map/ppermute | solution.py:27
  7.9 2.2 %collective-permute-done.1 = bf16[2,32,512]{2,1,0:T(8,128)(2,1)S(1)} collective-permute-done((bf16[2,32,512]{2,1,0:T(8,128)(2,1)}, bf16[2,32,512]{2,1,0:T(8,128)(2,1)S(1)}, u32[]{:S(2)}, u32[]{:S(2)}) %collective-permute-start.1) | collective-permute-done | bytes 65568 | tf_op jit(solution)/shard_map/ppermute | solution.py:27
  10.0 3.0 %collective-permute-done.2 = bf16[2,32,512]{2,1,0:T(8,128)(2,1)S(1)} collective-permute-done((bf16[2,32,512]{2,1,0:T(8,128)(2,1)}, bf16[2,32,512]{2,1,0:T(8,128)(2,1)S(1)}, u32[]{:S(2)}, u32[]{:S(2)}) %collective-permute-start.2) | collective-permute-done | bytes 65568 | tf_op jit(solution)/shard_map/ppermute | solution.py:27
  14.9 3.8 %collective-permute-start.4 = (bf16[4,2,32,512]{3,2,1,0:T(8,128)(2,1)}, bf16[4,2,32,512]{3,2,1,0:T(8,128)(2,1)S(1)}, u32[]{:S(2)}, u32[]{:S(2)}) collective-permute-start(bf16[4,2,32,512]{3,2,1,0:T(8,128)(2,1)} %bitcast_dynamic-update-slice_fusion), channel_id=1, source_target_pairs={{0,4},{4,8},{8,12},{12,16},{16,20},{20,24},{24,28},{1,5},{5,9},{9,... | collective-permute-start | bytes 786440 | tf_op jit(solution)/shard_map/ppermute | solution.py:33
  18.8 2.0 %collective-permute-start.3 = (bf16[4,2,32,512]{3,2,1,0:T(8,128)(2,1)}, bf16[4,2,32,512]{3,2,1,0:T(8,128)(2,1)}, u32[]{:S(2)}, u32[]{:S(2)}) collective-permute-start(bf16[4,2,32,512]{3,2,1,0:T(8,128)(2,1)} %bitcast_dynamic-update-slice_fusion), channel_id=1, source_target_pairs={{0,8},{4,12},{8,16},{12,20},{16,24},{20,28},{1,9},{5,13},{9,17},{1... | collective-permute-start | bytes 786440 | tf_op jit(solution)/shard_map/ppermute | solution.py:33
  20.7 1.8 %collective-permute-start.6 = (bf16[2,32,2048]{2,1,0:T(8,128)(2,1)}, bf16[2,32,2048]{2,1,0:T(8,128)(2,1)S(1)}, u32[]{:S(2)}, u32[]{:S(2)}) collective-permute-start(bf16[2,32,2048]{2,1,0:T(8,128)(2,1)} %get-tuple-element.60), channel_id=1, source_target_pairs={{0,3},{1,0},{2,1},{3,2},{4,7},{5,4},{6,5},{7,6},{8,11},{9,8},{10,9... | collective-permute-start | bytes 786440 | tf_op jit(solution)/shard_map/ppermute | solution.py:27
  22.5 1.7 %collective-permute-start.5 = (bf16[2,32,2048]{2,1,0:T(8,128)(2,1)}, bf16[2,32,2048]{2,1,0:T(8,128)(2,1)S(1)}, u32[]{:S(2)}, u32[]{:S(2)}) collective-permute-start(bf16[2,32,2048]{2,1,0:T(8,128)(2,1)} %get-tuple-element.59), channel_id=1, source_target_pairs={{0,2},{1,3},{2,0},{3,1},{4,6},{5,7},{6,4},{7,5},{8,10},{9,11},{10,... | collective-permute-start | bytes 786440 | tf_op jit(solution)/shard_map/ppermute | solution.py:27
  25.5 2.3 %attend.8 = (bf16[128,32,128]{2,1,0:T(8,128)(2,1)}, f32[2,384,256]{2,1,0:T(8,128)S(1)}) custom-call(s32[2]{0:T(128)S(1)} %pad_add_fusion.meta_ref, s32[4]{0:T(128)S(1)} %copy-done.3, s32[4,1024]{1,0:T(4,128)S(1)} %copy-done.2, bf16[4,32,4096]{2,1,0:T(8,128)(2,1)S(1)} %copy-done, bf16[4,32,4096]{2,1,0:T(8,128)(2,1)S(1)} %copy-done.1, ...), custom_call_target="tpu_custom_call" | custom-call | flops 18874368 | bytes 147456 | tf_op jit(solution)/shard_map/attend/pallas_call | solution.py:234
  27.9 1.7 %collective-permute-start.9 = (bf16[2,32,2048]{2,1,0:T(8,128)(2,1)S(1)}, bf16[2,32,2048]{2,1,0:T(8,128)(2,1)S(1)}, u32[]{:S(2)}, u32[]{:S(2)}) collective-permute-start(bf16[2,32,2048]{2,1,0:T(8,128)(2,1)S(1)} %copy-done.5), channel_id=1, source_target_pairs={{0,3},{1,0},{2,1},{3,2},{4,7},{5,4},{6,5},{7,6},{8,11},{9,8},{10,9... | collective-permute-start | bytes 786440 | tf_op jit(solution)/shard_map/ppermute | solution.py:27
  29.6 2.3 %attend.9 = (bf16[128,32,128]{2,1,0:T(8,128)(2,1)}, f32[2,384,256]{2,1,0:T(8,128)S(1)}) custom-call(s32[2]{0:T(128)S(1)} %pad_add_fusion.meta_ref, s32[4]{0:T(128)S(1)} %copy-done.3, s32[4,1024]{1,0:T(4,128)S(1)} %copy-done.2, bf16[4,32,4096]{2,1,0:T(8,128)(2,1)S(1)} %copy-done, bf16[4,32,4096]{2,1,0:T(8,128)(2,1)S(1)} %copy-done.1, ...), custom_call_target="tpu_custom_call", output_to_operand_aliasing={{0}: (6, {})} | custom-call | flops 18874368 | bytes 147456 | tf_op jit(solution)/shard_map/attend/pallas_call | solution.py:234
  31.9 2.5 %attend.10 = (bf16[128,32,128]{2,1,0:T(8,128)(2,1)}, f32[2,384,256]{2,1,0:T(8,128)S(1)}) custom-call(s32[2]{0:T(128)S(1)} %pad_add_fusion.meta_ref, s32[4]{0:T(128)S(1)} %copy-done.3, s32[4,1024]{1,0:T(4,128)S(1)} %copy-done.2, bf16[2,32,4096]{2,1,0:T(8,128)(2,1)S(1)} %collective-permute-done.7.query_ref.grad_ref, ...), custom_call_target="tpu_custom_call", output_to_operand_aliasing={{1}: (6, {}), {0}: (7, {})} | custom-call | flops 18874368 | bytes 147456 | tf_op jit(solution)/shard_map/attend/pallas_call | solution.py:234
  34.3 2.5 %attend.11 = (bf16[128,32,128]{2,1,0:T(8,128)(2,1)}, f32[2,384,256]{2,1,0:T(8,128)S(1)}) custom-call(s32[2]{0:T(128)S(1)} %pad_add_fusion.meta_ref, s32[4]{0:T(128)S(1)} %copy-done.3, s32[4,1024]{1,0:T(4,128)S(1)} %copy-done.2, bf16[2,32,4096]{2,1,0:T(8,128)(2,1)S(1)} %collective-permute-done.7.query_ref.grad_ref, ...), custom_call_target="tpu_custom_call", output_to_operand_aliasing={{1}: (6, {}), {0}: (7, {})} | custom-call | flops 18874368 | bytes 147456 | tf_op jit(solution)/shard_map/attend/pallas_call | solution.py:234
  36.8 2.4 %attend.12 = (bf16[128,32,128]{2,1,0:T(8,128)(2,1)}, f32[2,384,256]{2,1,0:T(8,128)S(1)}) custom-call(s32[2]{0:T(128)S(1)} %pad_add_fusion.meta_ref, s32[4]{0:T(128)S(1)} %copy-done.3, s32[4,1024]{1,0:T(4,128)S(1)} %copy-done.2, bf16[2,32,2048]{2,1,0:T(8,128)(2,1)S(1)} %collective-permute-done.6.query_ref.grad_ref, ...), custom_call_target="tpu_custom_call", output_to_operand_aliasing={{1}: (6, {}), {0}: (7, {})} | custom-call | flops 18874368 | bytes 147456 | tf_op jit(solution)/shard_map/attend/pallas_call | solution.py:234
  39.2 7.4 %collective-permute-done.5.query_ref.grad_ref = bf16[2,32,2048]{2,1,0:T(8,128)(2,1)S(1)} collective-permute-done((bf16[2,32,2048]{2,1,0:T(8,128)(2,1)}, bf16[2,32,2048]{2,1,0:T(8,128)(2,1)S(1)}, u32[]{:S(2)}, u32[]{:S(2)}) %collective-permute-start.5) | collective-permute-done | bytes 262176 | tf_op jit(solution)/shard_map/ppermute | solution.py:27
  46.6 2.4 %attend.13 = (bf16[128,32,128]{2,1,0:T(8,128)(2,1)}, f32[2,128,256]{2,1,0:T(8,128)S(1)}, bf16[2,128,256]{2,1,0:T(8,128)(2,1)S(1)}, bf16[2,128,256]{2,1,0:T(8,128)(2,1)S(1)}) custom-call(s32[2]{0:T(128)S(1)} %pad_add_fusion.meta_ref, s32[4]{0:T(128)S(1)} %copy-done.3, s32[4,1024]{1,0:T(4,128)S(1)} %copy-done.2, ...), custom_call_target="tpu_custom_call", output_to_operand_aliasing={{0}: (7, {})} | custom-call | flops 18874368 | bytes 147456 | tf_op jit(solution)/shard_map/attend/pallas_call | solution.py:234
  49.0 3.0 %collective-permute-start.8 = (bf16[2,32,2048]{2,1,0:T(8,128)(2,1)S(1)}, bf16[2,32,2048]{2,1,0:T(8,128)(2,1)S(1)}, u32[]{:S(2)}, u32[]{:S(2)}) collective-permute-start(bf16[2,32,2048]{2,1,0:T(8,128)(2,1)S(1)} %copy-done.4), channel_id=1, source_target_pairs={{0,2},{1,3},{2,0},{3,1},{4,6},{5,7},{6,4},{7,5},{8,10},{9,11},{10,... | collective-permute-start | bytes 786440 | tf_op jit(solution)/shard_map/ppermute | solution.py:27
  51.9 9.6 %collective-permute-start.10 = (bf16[2,128,256]{2,1,0:T(8,128)(2,1)S(1)}, bf16[2,128,256]{2,1,0:T(8,128)(2,1)S(1)}, u32[]{:S(2)}, u32[]{:S(2)}) collective-permute-start(bf16[2,128,256]{2,1,0:T(8,128)(2,1)S(1)} %get-tuple-element.80), channel_id=1, source_target_pairs={{4,0},{8,4},{12,8},{16,12},{20,16},{24,20},{28,24},{5,1},{9,5},{13... | collective-permute-start | bytes 393224 | tf_op jit(solution)/shard_map/ppermute | solution.py:33
  61.6 1.9 %collective-permute-start.11 = (bf16[2,128,256]{2,1,0:T(8,128)(2,1)S(1)}, bf16[2,128,256]{2,1,0:T(8,128)(2,1)S(1)}, u32[]{:S(2)}, u32[]{:S(2)}) collective-permute-start(bf16[2,128,256]{2,1,0:T(8,128)(2,1)S(1)} %get-tuple-element.81), channel_id=1, source_target_pairs={{8,0},{12,4},{16,8},{20,12},{24,16},{28,20},{9,1},{13,5},{17,9},{2... | collective-permute-start | bytes 393224 | tf_op jit(solution)/shard_map/ppermute | solution.py:33
  63.5 2.4 %attend.14 = (bf16[128,32,128]{2,1,0:T(8,128)(2,1)}, f32[2,384,256]{2,1,0:T(8,128)S(1)}) custom-call(s32[2]{0:T(128)S(1)} %pad_add_fusion.meta_ref, s32[4]{0:T(128)S(1)} %copy-done.3, s32[4,1024]{1,0:T(4,128)S(1)} %copy-done.2, bf16[2,32,2048]{2,1,0:T(8,128)(2,1)S(1)} %collective-permute-done.9.query_ref.grad_ref, ...), custom_call_target="tpu_custom_call", output_to_operand_aliasing={{1}: (6, {}), {0}: (7, {})} | custom-call | flops 18874368 | bytes 147456 | tf_op jit(solution)/shard_map/attend/pallas_call | solution.py:234
  65.9 2.4 %attend.15 = (bf16[128,32,128]{2,1,0:T(8,128)(2,1)}, f32[2,128,256]{2,1,0:T(8,128)S(1)}, bf16[2,128,256]{2,1,0:T(8,128)(2,1)S(1)}, bf16[2,128,256]{2,1,0:T(8,128)(2,1)S(1)}) custom-call(s32[2]{0:T(128)S(1)} %pad_add_fusion.meta_ref, s32[4]{0:T(128)S(1)} %copy-done.3, s32[4,1024]{1,0:T(4,128)S(1)} %copy-done.2, ...), custom_call_target="tpu_custom_call", output_to_operand_aliasing={{0}: (7, {})} | custom-call | flops 18874368 | bytes 147456 | tf_op jit(solution)/shard_map/attend/pallas_call | solution.py:234
  68.3 1.9 %collective-permute-start.12 = (bf16[2,128,256]{2,1,0:T(8,128)(2,1)S(1)}, bf16[2,128,256]{2,1,0:T(8,128)(2,1)S(1)}, u32[]{:S(2)}, u32[]{:S(2)}) collective-permute-start(bf16[2,128,256]{2,1,0:T(8,128)(2,1)S(1)} %get-tuple-element.85), channel_id=1, source_target_pairs={{4,0},{8,4},{12,8},{16,12},{20,16},{24,20},{28,24},{5,1},{9,5},{13... | collective-permute-start | bytes 393224 | tf_op jit(solution)/shard_map/ppermute | solution.py:33
  70.3 1.9 %collective-permute-start.13 = (bf16[2,128,256]{2,1,0:T(8,128)(2,1)S(1)}, bf16[2,128,256]{2,1,0:T(8,128)(2,1)S(1)}, u32[]{:S(2)}, u32[]{:S(2)}) collective-permute-start(bf16[2,128,256]{2,1,0:T(8,128)(2,1)S(1)} %get-tuple-element.86), channel_id=1, source_target_pairs={{8,0},{12,4},{16,8},{20,12},{24,16},{28,20},{9,1},{13,5},{17,9},{2... | collective-permute-start | bytes 393224 | tf_op jit(solution)/shard_map/ppermute | solution.py:33
  72.2 4.8 %collective-permute-done.12 = bf16[2,128,256]{2,1,0:T(8,128)(2,1)S(1)} collective-permute-done((bf16[2,128,256]{2,1,0:T(8,128)(2,1)S(1)}, bf16[2,128,256]{2,1,0:T(8,128)(2,1)S(1)}, u32[]{:S(2)}, u32[]{:S(2)}) %collective-permute-start.12) | collective-permute-done | bytes 131104 | tf_op jit(solution)/shard_map/ppermute | solution.py:33
  (33 shorter events, 7.0 us)
Async XLA Ops:
  0.6 24.9 %copy-start.1 = (bf16[4,32,4096]{2,1,0:T(8,128)(2,1)S(1)}, bf16[4,32,4096]{2,1,0:T(8,128)(2,1)}, u32[]{:S(2)}) copy-start(bf16[4,32,4096]{2,1,0:T(8,128)(2,1)} %grad_ref.3) | copy-start | bytes 3145732
  4.0 21.5 %copy-start = (bf16[4,32,4096]{2,1,0:T(8,128)(2,1)S(1)}, bf16[4,32,4096]{2,1,0:T(8,128)(2,1)}, u32[]{:S(2)}) copy-start(bf16[4,32,4096]{2,1,0:T(8,128)(2,1)} %query_ref.3) | copy-start | bytes 3145732
  4.0 3.8 %collective-permute-start = (bf16[2,32,512]{2,1,0:T(8,128)(2,1)}, bf16[2,32,512]{2,1,0:T(8,128)(2,1)S(1)}, u32[]{:S(2)}, u32[]{:S(2)}) collective-permute-start(bf16[2,32,512]{2,1,0:T(8,128)(2,1)} %get-tuple-element.51), channel_id=1, source_target_pairs={{0,1},{1,2},{2,3},{3,0},{4,5},{5,6},{6,7},{7,4},{8,9},{9,10},{10,1... | collective-permute-start | bytes 196616 | tf_op jit(solution)/shard_map/ppermute | solution.py:27
  5.4 4.7 %collective-permute-start.1 = (bf16[2,32,512]{2,1,0:T(8,128)(2,1)}, bf16[2,32,512]{2,1,0:T(8,128)(2,1)S(1)}, u32[]{:S(2)}, u32[]{:S(2)}) collective-permute-start(bf16[2,32,512]{2,1,0:T(8,128)(2,1)} %get-tuple-element.52), channel_id=1, source_target_pairs={{0,2},{1,3},{2,0},{3,1},{4,6},{5,7},{6,4},{7,5},{8,10},{9,11},{10,... | collective-permute-start | bytes 196616 | tf_op jit(solution)/shard_map/ppermute | solution.py:27
  6.5 6.6 %collective-permute-start.2 = (bf16[2,32,512]{2,1,0:T(8,128)(2,1)}, bf16[2,32,512]{2,1,0:T(8,128)(2,1)S(1)}, u32[]{:S(2)}, u32[]{:S(2)}) collective-permute-start(bf16[2,32,512]{2,1,0:T(8,128)(2,1)} %get-tuple-element.53), channel_id=1, source_target_pairs={{0,3},{1,0},{2,1},{3,2},{4,7},{5,4},{6,5},{7,6},{8,11},{9,8},{10,9... | collective-permute-start | bytes 196616 | tf_op jit(solution)/shard_map/ppermute | solution.py:27
  13.0 18.8 %collective-permute-start.7 = (bf16[2,32,4096]{2,1,0:T(8,128)(2,1)}, bf16[2,32,4096]{2,1,0:T(8,128)(2,1)S(1)}, u32[]{:S(2)}, u32[]{:S(2)}) collective-permute-start(bf16[2,32,4096]{2,1,0:T(8,128)(2,1)} %get-tuple-element.61), channel_id=1, source_target_pairs={{0,1},{1,2},{2,3},{3,0},{4,5},{5,6},{6,7},{7,4},{8,9},{9,10},{10,1... | collective-permute-start | bytes 1572872 | tf_op jit(solution)/shard_map/ppermute | solution.py:27
  14.9 9.4 %collective-permute-start.4 = (bf16[4,2,32,512]{3,2,1,0:T(8,128)(2,1)}, bf16[4,2,32,512]{3,2,1,0:T(8,128)(2,1)S(1)}, u32[]{:S(2)}, u32[]{:S(2)}) collective-permute-start(bf16[4,2,32,512]{3,2,1,0:T(8,128)(2,1)} %bitcast_dynamic-update-slice_fusion), channel_id=1, source_target_pairs={{0,4},{4,8},{8,12},{12,16},{16,20},{20,24},{24,28},{1,5},{5,9},{9,... | collective-permute-start | bytes 786440 | tf_op jit(solution)/shard_map/ppermute | solution.py:33
  18.8 5.6 %collective-permute-start.3 = (bf16[4,2,32,512]{3,2,1,0:T(8,128)(2,1)}, bf16[4,2,32,512]{3,2,1,0:T(8,128)(2,1)}, u32[]{:S(2)}, u32[]{:S(2)}) collective-permute-start(bf16[4,2,32,512]{3,2,1,0:T(8,128)(2,1)} %bitcast_dynamic-update-slice_fusion), channel_id=1, source_target_pairs={{0,8},{4,12},{8,16},{12,20},{16,24},{20,28},{1,9},{5,13},{9,17},{1... | collective-permute-start | bytes 786440 | tf_op jit(solution)/shard_map/ppermute | solution.py:33
  20.7 16.1 %collective-permute-start.6 = (bf16[2,32,2048]{2,1,0:T(8,128)(2,1)}, bf16[2,32,2048]{2,1,0:T(8,128)(2,1)S(1)}, u32[]{:S(2)}, u32[]{:S(2)}) collective-permute-start(bf16[2,32,2048]{2,1,0:T(8,128)(2,1)} %get-tuple-element.60), channel_id=1, source_target_pairs={{0,3},{1,0},{2,1},{3,2},{4,7},{5,4},{6,5},{7,6},{8,11},{9,8},{10,9... | collective-permute-start | bytes 786440 | tf_op jit(solution)/shard_map/ppermute | solution.py:27
  22.5 24.0 %collective-permute-start.5 = (bf16[2,32,2048]{2,1,0:T(8,128)(2,1)}, bf16[2,32,2048]{2,1,0:T(8,128)(2,1)S(1)}, u32[]{:S(2)}, u32[]{:S(2)}) collective-permute-start(bf16[2,32,2048]{2,1,0:T(8,128)(2,1)} %get-tuple-element.59), channel_id=1, source_target_pairs={{0,2},{1,3},{2,0},{3,1},{4,6},{5,7},{6,4},{7,5},{8,10},{9,11},{10,... | collective-permute-start | bytes 786440 | tf_op jit(solution)/shard_map/ppermute | solution.py:27
  24.3 1.2 %copy-start.2 = (s32[4,1024]{1,0:T(4,128)S(1)}, s32[4,1024]{1,0:T(4,128)}, u32[]{:S(2)}) copy-start(s32[4,1024]{1,0:T(4,128)} %segment_ref.15) | copy-start | bytes 49156
  24.3 1.2 %copy-start.3 = (s32[4]{0:T(128)S(1)}, s32[4]{0:T(128)}, u32[]{:S(2)}) copy-start(s32[4]{0:T(128)} %assign_ref.17) | copy-start | bytes 52
  25.5 2.3 %copy-start.5 = (bf16[2,32,2048]{2,1,0:T(8,128)(2,1)S(1)}, bf16[2,32,2048]{2,1,0:T(8,128)(2,1)}, u32[]{:S(2)}) copy-start(bf16[2,32,2048]{2,1,0:T(8,128)(2,1)} %get-tuple-element.73) | copy-start | bytes 786436
  27.9 35.7 %collective-permute-start.9 = (bf16[2,32,2048]{2,1,0:T(8,128)(2,1)S(1)}, bf16[2,32,2048]{2,1,0:T(8,128)(2,1)S(1)}, u32[]{:S(2)}, u32[]{:S(2)}) collective-permute-start(bf16[2,32,2048]{2,1,0:T(8,128)(2,1)S(1)} %copy-done.5), channel_id=1, source_target_pairs={{0,3},{1,0},{2,1},{3,2},{4,7},{5,4},{6,5},{7,6},{8,11},{9,8},{10,9... | collective-permute-start | bytes 786440 | tf_op jit(solution)/shard_map/ppermute | solution.py:27
  46.6 2.4 %copy-start.4 = (bf16[2,32,2048]{2,1,0:T(8,128)(2,1)S(1)}, bf16[2,32,2048]{2,1,0:T(8,128)(2,1)}, u32[]{:S(2)}) copy-start(bf16[2,32,2048]{2,1,0:T(8,128)(2,1)} %get-tuple-element.72) | copy-start | bytes 786436
  49.0 17.0 %collective-permute-start.8 = (bf16[2,32,2048]{2,1,0:T(8,128)(2,1)S(1)}, bf16[2,32,2048]{2,1,0:T(8,128)(2,1)S(1)}, u32[]{:S(2)}, u32[]{:S(2)}) collective-permute-start(bf16[2,32,2048]{2,1,0:T(8,128)(2,1)S(1)} %copy-done.4), channel_id=1, source_target_pairs={{0,2},{1,3},{2,0},{3,1},{4,6},{5,7},{6,4},{7,5},{8,10},{9,11},{10,... | collective-permute-start | bytes 786440 | tf_op jit(solution)/shard_map/ppermute | solution.py:27
  51.9 16.4 %collective-permute-start.10 = (bf16[2,128,256]{2,1,0:T(8,128)(2,1)S(1)}, bf16[2,128,256]{2,1,0:T(8,128)(2,1)S(1)}, u32[]{:S(2)}, u32[]{:S(2)}) collective-permute-start(bf16[2,128,256]{2,1,0:T(8,128)(2,1)S(1)} %get-tuple-element.80), channel_id=1, source_target_pairs={{4,0},{8,4},{12,8},{16,12},{20,16},{24,20},{28,24},{5,1},{9,5},{13... | collective-permute-start | bytes 393224 | tf_op jit(solution)/shard_map/ppermute | solution.py:33
  61.6 6.8 %collective-permute-start.11 = (bf16[2,128,256]{2,1,0:T(8,128)(2,1)S(1)}, bf16[2,128,256]{2,1,0:T(8,128)(2,1)S(1)}, u32[]{:S(2)}, u32[]{:S(2)}) collective-permute-start(bf16[2,128,256]{2,1,0:T(8,128)(2,1)S(1)} %get-tuple-element.81), channel_id=1, source_target_pairs={{8,0},{12,4},{16,8},{20,12},{24,16},{28,20},{9,1},{13,5},{17,9},{2... | collective-permute-start | bytes 393224 | tf_op jit(solution)/shard_map/ppermute | solution.py:33
  68.3 8.7 %collective-permute-start.12 = (bf16[2,128,256]{2,1,0:T(8,128)(2,1)S(1)}, bf16[2,128,256]{2,1,0:T(8,128)(2,1)S(1)}, u32[]{:S(2)}, u32[]{:S(2)}) collective-permute-start(bf16[2,128,256]{2,1,0:T(8,128)(2,1)S(1)} %get-tuple-element.85), channel_id=1, source_target_pairs={{4,0},{8,4},{12,8},{16,12},{20,16},{24,20},{28,24},{5,1},{9,5},{13... | collective-permute-start | bytes 393224 | tf_op jit(solution)/shard_map/ppermute | solution.py:33
  70.3 7.3 %collective-permute-start.13 = (bf16[2,128,256]{2,1,0:T(8,128)(2,1)S(1)}, bf16[2,128,256]{2,1,0:T(8,128)(2,1)S(1)}, u32[]{:S(2)}, u32[]{:S(2)}) collective-permute-start(bf16[2,128,256]{2,1,0:T(8,128)(2,1)S(1)} %get-tuple-element.86), channel_id=1, source_target_pairs={{8,0},{12,4},{16,8},{20,12},{24,16},{28,20},{9,1},{13,5},{17,9},{2... | collective-permute-start | bytes 393224 | tf_op jit(solution)/shard_map/ppermute | solution.py:33

commit v11 on v9

--- a/solution.py
+++ b/solution.py
@@ -33,17 +33,18 @@
     return lax.ppermute(value, axis, pairs)
 
 
-def stage_kernel(count, jobs, outs, meta_ref, assign_ref, first_ref, second_ref, *refs):
-    group = meta_ref[0]
-    out_refs, held_refs, (in_sems, out_sems) = refs[-2 - 2 * outs : -2 - outs], refs[-2 - outs : -2], refs[-2:]
+def stage_kernel(count, jobs, outs, assign_ref, *refs):
+    group = lax.axis_index("dp")
+    sources, refs = refs[:4], refs[4:]
+    out_refs, held_refs, (in_sems, out_sems) = refs[:outs], refs[outs : 2 * outs], refs[-2:]
     loads, stores = [], []
-    for out, (step, start, width) in enumerate(jobs):
+    for out, (first, step, start, width) in enumerate(jobs):
         chosen = assign_ref[target_of(group, step, count)]
-        for which, source in enumerate((first_ref, second_ref)):
-            origin = source.at[chosen, :, start : start + width]
-            held, goal, slot = held_refs[out].at[which], out_refs[out].at[which], 2 * out + which
+        for which in range(2):
+            origin = sources[first + which].at[chosen, :, start : start + width]
+            held, slot = held_refs[out].at[which], 2 * out + which
             loads.append(pltpu.make_async_copy(origin, held, in_sems.at[slot]))
-            stores.append(pltpu.make_async_copy(held, goal, out_sems.at[slot]))
+            stores.append(pltpu.make_async_copy(held, out_refs[out].at[which], out_sems.at[slot]))
     for load in loads:
         load.start()
     for load, store in zip(loads, stores):
@@ -53,19 +54,20 @@
         store.wait()
 
 
-def stage(meta, assignment, first, second, jobs, after=()):
-    count, rows, _ = first.shape
-    shapes = [(2, rows, width) for _, _, width in jobs]
-    far, scalars = pl.BlockSpec(memory_space=pltpu.HBM), pl.BlockSpec(memory_space=pltpu.SMEM)
+def stage(assignment, arrays, jobs):
+    count, rows, _ = arrays[0].shape
+    shapes = [(2, rows, width) for _, _, _, width in jobs]
+    kind = arrays[0].dtype
+    far = pl.BlockSpec(memory_space=pltpu.HBM)
     return pl.pallas_call(
-        functools.partial(stage_kernel, count, jobs, len(shapes)),
-        out_shape=[jax.ShapeDtypeStruct(shape, first.dtype) for shape in shapes],
-        in_specs=[scalars] * 2 + [far] * 2 + [pl.BlockSpec(memory_space=pl.ANY)] * len(after),
-        out_specs=[far] * len(shapes),
-        scratch_shapes=[pltpu.VMEM(shape, first.dtype) for shape in shapes]
-        + [pltpu.SemaphoreType.DMA((2 * len(shapes),))] * 2,
+        functools.partial(stage_kernel, count, jobs, len(jobs)),
+        out_shape=[jax.ShapeDtypeStruct(shape, kind) for shape in shapes],
+        in_specs=[pl.BlockSpec(memory_space=pltpu.SMEM)] + [far] * len(arrays),
+        out_specs=[far] * len(jobs),
+        scratch_shapes=[pltpu.VMEM(shape, kind) for shape in shapes]
+        + [pltpu.SemaphoreType.DMA((2 * len(jobs),))] * 2,
         name="stage",
-    )(meta, assignment, first, second, *after)
+    )(assignment, *arrays)
 
 
 def build_bias(source, sequence, line, segment_ref, column_ref, bias_ref, rows, tok_dev, reach):
@@ -263,13 +265,13 @@
     final, halves = count // 2, kv_heads // HEADS_STEP
     part = width // halves
     others = [step for step in range(1, count) if step != final]
-    kv_jobs = [(step, 0, kv_width) for step in range(count)]
-    kv_staged = stage(meta, assignment, keys, values, kv_jobs)
-    jobs = [(step, 0, width) for step in others]
-    jobs += [(final, half * part, part) for half in range(halves)]
-    staged = stage(meta, assignment, queries, grad_out, jobs, after=kv_staged[:1])
+    jobs = [(2, step, 0, kv_width) for step in range(count)]
+    jobs += [(0, step, 0, width) for step in others]
+    jobs += [(0, final, half * part, part) for half in range(halves)]
+    staged = stage(assignment, (queries, grad_out, keys, values), jobs)
+    kv_staged, staged = staged[:count], list(staged[count:])
     kv_arrived = [exchanged(kv_staged[step], "dp", step) for step in range(1, count)]
-    staged, kv_arrived = lax.optimization_barrier((staged, kv_arrived))
+    staged, kv_arrived[0] = lax.optimization_barrier((staged, kv_arrived[0]))
     arrived = [exchanged(rows, "dp", step) for rows, step in zip(staged, others)]
     held = staged[len(others) :]
     kv_own = jnp.zeros((count, *kv_staged[0].shape), keys.dtype)
@@ -280,30 +282,28 @@
     halos = [shifted(kv_own, ("blk", "uly"), back) for back in range(hops, 0, -1)]
     kv = jnp.concatenate([*halos, kv_own], axis=0)
 
+    rows, kv = lax.optimization_barrier((held[0], kv))
+    split = [exchanged(rows, "dp", final)]
     fixed = (doc_most, heads, meta, assignment, segment_ids)
     query, grad = (queries, lambda m, a: a[m[0]]), (grad_out, lambda m, a: a[m[0]])
     full, acc = attend(0, 0, kv_heads, *fixed, query, grad, kv, None, None, False)
-    rows, acc = lax.optimization_barrier((held[0], acc))
-    split = [exchanged(rows, "dp", final)]
     for step, both in zip(others, arrived):
         query, grad = (both, lambda m, a: 0), (both, lambda m, a: 1)
         full, acc = attend(step, 0, kv_heads, *fixed, query, grad, kv, acc, full, False)
-    for rows in held[1:]:
-        rows, acc = lax.optimization_barrier((rows, acc))
-        split.append(exchanged(rows, "dp", final))
-    totals, returned = [], []
+        if len(split) < halves:
+            rows, acc = lax.optimization_barrier((held[len(split)], acc))
+            split.append(exchanged(rows, "dp", final))
+    parts = []
     for half, both in enumerate(split):
         query, grad = (both, lambda m, a: 0), (both, lambda m, a: 1)
-        full, total, *halos = attend(
+        full, *part = attend(
             final, half * HEADS_STEP, HEADS_STEP, *fixed, query, grad, kv, acc, full, True
         )
-        if half:
-            halos, returned = lax.optimization_barrier((halos, returned))
-        returned = [shifted(halo, ("blk", "uly"), -back) for back, halo in enumerate(halos, 1)]
-        for halo in returned:
-            total = total + halo.astype(jnp.float32)
-        totals.append(total.astype(jnp.bfloat16))
-    total = jnp.concatenate(totals, axis=2)
+        parts.append(part)
+    total, *halos = [jnp.concatenate(part, axis=2) for part in zip(*parts)]
+    for back, halo in enumerate(halos, 1):
+        total = total + shifted(halo, ("blk", "uly"), -back).astype(jnp.float32)
+    total = total.astype(jnp.bfloat16)
     return full[None], total[0][None], total[1][None]
 
 

time: 79.2 us -> 76.2 us (0.962)
  starting transfers between devices: 29.1 us -> 23.9 us
  waiting for transfers between devices: 24.5 us -> 28.2 us
  Pallas kernels: 21.9 us -> 19.7 us
    ppermute x6 -> x4, starting transfers between devices: 16.3 us -> 12.1 us  [shifted(): return lax.ppermute(value, axis, pairs)]
    ppermute x7, waiting for transfers between devices: 15.5 us -> 19.3 us  [exchanged(): lax.ppermute(value, axis, [(i, (i + step) % count) for i in range(count)])]
    pallas_call x2 -> x1, Pallas kernels: 5.38 us -> 3.19 us  [stage(): pl.pallas_call(functools.partial(stage_kernel, count, jobs, len(jobs)), o...]
    concatenate x1, other arithmetic: 0.09 us -> 1.12 us  [shards(): kv = jnp.concatenate([*halos, kv_own], axis=0)]
    ppermute x7, starting transfers between devices: 12.8 us -> 11.8 us  [exchanged(): lax.ppermute(value, axis, [(i, (i + step) % count) for i in range(count)])]
    ppermute x6 -> x4, waiting for transfers between devices: 9.04 us -> 8.93 us  [shifted(): return lax.ppermute(value, axis, pairs)]
  transfers between devices with their start and end apart: 13 -> 11, of which waited for: 8 -> 7; matrix products, arithmetic and copies ran while one was open for 1% -> 3% of each run, Pallas kernels for 25% -> 19%
where the time goes in v11:
time: 76.2 us; the launch traced here: 75.6 us
  waiting for transfers between devices  28.2 us (37%)
  starting transfers between devices  23.9 us (31%)
  Pallas kernels  19.7 us (26%)
  local copies, waits for them, and re-layouts  1.65 us (2%)
  other arithmetic  1.33 us (2%)
  between operations  0.77 us (1%)
    ppermute x7, waiting for transfers between devices, exchanged(): lax.ppermute(value, axis, [(i, (i + step) % count) for i in range(count)])  19.3 us
    pallas_call x5, Pallas kernels, attend(): pl.pallas_call(functools.partial(attend_kernel, step, first, filled, last...  16.6 us
    ppermute x4, starting transfers between devices, shifted(): return lax.ppermute(value, axis, pairs)  12.1 us
    ppermute x7, starting transfers between devices, exchanged(): lax.ppermute(value, axis, [(i, (i + step) % count) for i in range(count)])  11.8 us
    ppermute x4, waiting for transfers between devices, shifted(): return lax.ppermute(value, axis, pairs)  8.93 us
    pallas_call x1, Pallas kernels, stage(): pl.pallas_call(functools.partial(stage_kernel, count, jobs, len(jobs)), o...  3.19 us
  transfers between devices with their start and end apart: 11, of which 7 were waited for; matrix products, arithmetic and copies ran while one was open for 3% of the time, Pallas kernels for 19%

profile of v11, /device:TPU:1, one launch (start us, length us, event | category | flops | bytes accessed | tf_op | source)
XLA Modules:
  0.0 75.6 jit_solution(7698336991339500598)
XLA Ops:
  0.6 3.2 %stage.1 = (bf16[2,32,512]{2,1,0:T(8,128)(2,1)}, bf16[2,32,512]{2,1,0:T(8,128)(2,1)}, bf16[2,32,512]{2,1,0:T(8,128)(2,1)}, bf16[2,32,512]{2,1,0:T(8,128)(2,1)}, ...) custom-call(s32[4]{0:T(128)} %assign_ref.11, ...), custom_call_target="tpu_custom_call" | custom-call | tf_op jit(solution)/shard_map/stage/pallas_call | solution.py:62
  3.9 2.2 %collective-permute-start = (bf16[2,32,512]{2,1,0:T(8,128)(2,1)}, bf16[2,32,512]{2,1,0:T(8,128)(2,1)S(1)}, u32[]{:S(2)}, u32[]{:S(2)}) collective-permute-start(bf16[2,32,512]{2,1,0:T(8,128)(2,1)} %get-tuple-element.38), channel_id=1, source_target_pairs={{0,1},{1,2},{2,3},{3,0},{4,5},{5,6},{6,7},{7,4},{8,9},{9,10},{10,1... | collective-permute-start | bytes 196616 | tf_op jit(solution)/shard_map/ppermute | solution.py:27
  6.1 2.3 %collective-permute-start.2 = (bf16[2,32,512]{2,1,0:T(8,128)(2,1)}, bf16[2,32,512]{2,1,0:T(8,128)(2,1)S(1)}, u32[]{:S(2)}, u32[]{:S(2)}) collective-permute-start(bf16[2,32,512]{2,1,0:T(8,128)(2,1)} %get-tuple-element.44), channel_id=1, source_target_pairs={{0,2},{1,3},{2,0},{3,1},{4,6},{5,7},{6,4},{7,5},{8,10},{9,11},{10,... | collective-permute-start | bytes 196616 | tf_op jit(solution)/shard_map/ppermute | solution.py:27
  8.4 1.1 %collective-permute-start.3 = (bf16[2,32,512]{2,1,0:T(8,128)(2,1)}, bf16[2,32,512]{2,1,0:T(8,128)(2,1)S(1)}, u32[]{:S(2)}, u32[]{:S(2)}) collective-permute-start(bf16[2,32,512]{2,1,0:T(8,128)(2,1)} %get-tuple-element.45), channel_id=1, source_target_pairs={{0,3},{1,0},{2,1},{3,2},{4,7},{5,4},{6,5},{7,6},{8,11},{9,8},{10,9... | collective-permute-start | bytes 196616 | tf_op jit(solution)/shard_map/ppermute | solution.py:27
  9.5 0.9 %bitcast_dynamic-update-slice_fusion.3 = bf16[4,2,32,512]{3,2,1,0:T(8,128)(2,1)S(1)} fusion(bf16[4,2,32,512]{3,2,1,0:T(8,128)(2,1)S(1)} %broadcast_in_dim.19, s32[]{:T(128)S(6)} %select_n.13, bf16[2,32,512]{2,1,0:T(8,128)(2,1)} %get-tuple-element.42), kind=kLoop, calls=%fused_computation.9 | loop fusion | bytes 131076 | tf_op jit(solution)/shard_map/jit(dynamic_update_index_in_dim)/dynamic_update_slice | solution.py:279
  10.8 2.8 %collective-permute-done.2 = bf16[2,32,512]{2,1,0:T(8,128)(2,1)S(1)} collective-permute-done((bf16[2,32,512]{2,1,0:T(8,128)(2,1)}, bf16[2,32,512]{2,1,0:T(8,128)(2,1)S(1)}, u32[]{:S(2)}, u32[]{:S(2)}) %collective-permute-start.2) | collective-permute-done | bytes 65568 | tf_op jit(solution)/shard_map/ppermute | solution.py:27
  13.6 2.4 %collective-permute-start.5 = (bf16[4,2,32,512]{3,2,1,0:T(8,128)(2,1)S(1)}, bf16[4,2,32,512]{3,2,1,0:T(8,128)(2,1)}, u32[]{:S(2)}, u32[]{:S(2)}) collective-permute-start(bf16[4,2,32,512]{3,2,1,0:T(8,128)(2,1)S(1)} %bitcast_dynamic-update-slice_fusion), channel_id=1, source_target_pairs={{0,4},{4,8},{8,12},{12,16},{16,20},{20,24},{24,28},{1,5},{5,9},{9,... | collective-permute-start | bytes 786440 | tf_op jit(solution)/shard_map/ppermute | solution.py:33
  16.0 5.0 %collective-permute-start.4 = (bf16[4,2,32,512]{3,2,1,0:T(8,128)(2,1)S(1)}, bf16[4,2,32,512]{3,2,1,0:T(8,128)(2,1)}, u32[]{:S(2)}, u32[]{:S(2)}) collective-permute-start(bf16[4,2,32,512]{3,2,1,0:T(8,128)(2,1)S(1)} %bitcast_dynamic-update-slice_fusion), channel_id=1, source_target_pairs={{0,8},{4,12},{8,16},{12,20},{16,24},{20,28},{1,9},{5,13},{9,17},{1... | collective-permute-start | bytes 786440 | tf_op jit(solution)/shard_map/ppermute | solution.py:33
  21.1 3.3 %collective-permute-start.7 = (bf16[2,32,4096]{2,1,0:T(8,128)(2,1)}, bf16[2,32,4096]{2,1,0:T(8,128)(2,1)S(1)}, u32[]{:S(2)}, u32[]{:S(2)}) collective-permute-start(bf16[2,32,4096]{2,1,0:T(8,128)(2,1)} %get-tuple-element.51), channel_id=1, source_target_pairs={{0,3},{1,0},{2,1},{3,2},{4,7},{5,4},{6,5},{7,6},{8,11},{9,8},{10,9... | collective-permute-start | bytes 1572872 | tf_op jit(solution)/shard_map/ppermute | solution.py:27
  24.5 1.4 %collective-permute-done.4 = bf16[4,2,32,512]{3,2,1,0:T(8,128)(2,1)} collective-permute-done((bf16[4,2,32,512]{3,2,1,0:T(8,128)(2,1)S(1)}, bf16[4,2,32,512]{3,2,1,0:T(8,128)(2,1)}, u32[]{:S(2)}, u32[]{:S(2)}) %collective-permute-start.4) | collective-permute-done | bytes 262176 | tf_op jit(solution)/shard_map/ppermute | solution.py:33
  25.9 1.1 %pad_maximum_fusion.kv_ref = bf16[12,2,32,512]{3,2,1,0:T(8,128)(2,1)S(1)} fusion(bf16[4,2,32,512]{3,2,1,0:T(8,128)(2,1)S(1)} %bitcast_dynamic-update-slice_fusion, bf16[4,2,32,512]{3,2,1,0:T(8,128)(2,1)} %collective-permute-done.5, bf16[4,2,32,512]{3,2,1,0:T(8,128)(2,1)} %collective-permute-done.4), kind=kLoop, calls=%fused_computation | loop fusion | flops 786432 | bytes 1572864 | tf_op jit(solution)/shard_map/concatenate | solution.py:283
  27.7 3.9 %attend.5 = (bf16[128,32,128]{2,1,0:T(8,128)(2,1)}, f32[2,384,512]{2,1,0:T(8,128)S(1)}) custom-call(s32[2]{0:T(128)S(1)} %pad_add_fusion.meta_ref, s32[4]{0:T(128)S(1)} %copy-done.3, s32[4,1024]{1,0:T(4,128)S(1)} %copy-done.2, bf16[4,32,4096]{2,1,0:T(8,128)(2,1)S(1)} %copy-done, bf16[4,32,4096]{2,1,0:T(8,128)(2,1)S(1)} %copy-done.1, ...), custom_call_target="tpu_custom_call" | custom-call | flops 37748736 | bytes 294912 | tf_op jit(solution)/shard_map/attend/pallas_call | solution.py:232
  31.6 3.9 %attend.6 = (bf16[128,32,128]{2,1,0:T(8,128)(2,1)}, f32[2,384,512]{2,1,0:T(8,128)S(1)}) custom-call(s32[2]{0:T(128)S(1)} %pad_add_fusion.meta_ref, s32[4]{0:T(128)S(1)} %copy-done.3, s32[4,1024]{1,0:T(4,128)S(1)} %copy-done.2, bf16[2,32,4096]{2,1,0:T(8,128)(2,1)S(1)} %collective-permute-done.1.query_ref.grad_ref, ...), custom_call_target="tpu_custom_call", output_to_operand_aliasing={{1}: (6, {}), {0}: (7, {})} | custom-call | flops 37748736 | bytes 294912 | tf_op jit(solution)/shard_map/attend/pallas_call | solution.py:232
  35.5 1.8 %collective-permute-start.6 = (bf16[2,32,2048]{2,1,0:T(8,128)(2,1)S(1)}, bf16[2,32,2048]{2,1,0:T(8,128)(2,1)S(1)}, u32[]{:S(2)}, u32[]{:S(2)}) collective-permute-start(bf16[2,32,2048]{2,1,0:T(8,128)(2,1)S(1)} %copy-done.4), channel_id=1, source_target_pairs={{0,2},{1,3},{2,0},{3,1},{4,6},{5,7},{6,4},{7,5},{8,10},{9,11},{10,... | collective-permute-start | bytes 786440 | tf_op jit(solution)/shard_map/ppermute | solution.py:27
  37.6 3.9 %attend.7 = (bf16[128,32,128]{2,1,0:T(8,128)(2,1)}, f32[2,384,512]{2,1,0:T(8,128)S(1)}) custom-call(s32[2]{0:T(128)S(1)} %pad_add_fusion.meta_ref, s32[4]{0:T(128)S(1)} %copy-done.3, s32[4,1024]{1,0:T(4,128)S(1)} %copy-done.2, bf16[2,32,4096]{2,1,0:T(8,128)(2,1)S(1)} %collective-permute-done.7.query_ref.grad_ref, ...), custom_call_target="tpu_custom_call", output_to_operand_aliasing={{1}: (6, {}), {0}: (7, {})} | custom-call | flops 37748736 | bytes 294912 | tf_op jit(solution)/shard_map/attend/pallas_call | solution.py:232
  41.5 12.9 %collective-permute-done.8.query_ref.grad_ref = bf16[2,32,2048]{2,1,0:T(8,128)(2,1)S(1)} collective-permute-done((bf16[2,32,2048]{2,1,0:T(8,128)(2,1)S(1)}, bf16[2,32,2048]{2,1,0:T(8,128)(2,1)S(1)}, u32[]{:S(2)}, u32[]{:S(2)}) %collective-permute-start.8) | collective-permute-done | bytes 262176 | tf_op jit(solution)/shard_map/ppermute | solution.py:27
  54.5 2.4 %attend.8 = (bf16[128,32,128]{2,1,0:T(8,128)(2,1)}, f32[2,128,256]{2,1,0:T(8,128)S(1)}, bf16[2,128,256]{2,1,0:T(8,128)(2,1)S(1)}, bf16[2,128,256]{2,1,0:T(8,128)(2,1)S(1)}) custom-call(s32[2]{0:T(128)S(1)} %pad_add_fusion.meta_ref, s32[4]{0:T(128)S(1)} %copy-done.3, s32[4,1024]{1,0:T(4,128)S(1)} %copy-done.2, ...), custom_call_target="tpu_custom_call", output_to_operand_aliasing={{0}: (7, {})} | custom-call | flops 18874368 | bytes 147456 | tf_op jit(solution)/shard_map/attend/pallas_call | solution.py:232
  56.8 3.2 %collective-permute-done.6.query_ref.grad_ref = bf16[2,32,2048]{2,1,0:T(8,128)(2,1)S(1)} collective-permute-done((bf16[2,32,2048]{2,1,0:T(8,128)(2,1)S(1)}, bf16[2,32,2048]{2,1,0:T(8,128)(2,1)S(1)}, u32[]{:S(2)}, u32[]{:S(2)}) %collective-permute-start.6) | collective-permute-done | bytes 262176 | tf_op jit(solution)/shard_map/ppermute | solution.py:27
  60.1 2.4 %attend.9 = (bf16[128,32,128]{2,1,0:T(8,128)(2,1)}, f32[2,128,256]{2,1,0:T(8,128)S(1)}, bf16[2,128,256]{2,1,0:T(8,128)(2,1)S(1)}, bf16[2,128,256]{2,1,0:T(8,128)(2,1)S(1)}) custom-call(s32[2]{0:T(128)S(1)} %pad_add_fusion.meta_ref, s32[4]{0:T(128)S(1)} %copy-done.3, s32[4,1024]{1,0:T(4,128)S(1)} %copy-done.2, ...), custom_call_target="tpu_custom_call", output_to_operand_aliasing={{0}: (7, {})} | custom-call | flops 18874368 | bytes 147456 | tf_op jit(solution)/shard_map/attend/pallas_call | solution.py:232
  62.5 2.3 %collective-permute-start.10 = (bf16[2,128,512]{2,1,0:T(8,128)(2,1)S(1)}, bf16[2,128,512]{2,1,0:T(8,128)(2,1)S(1)}, u32[]{:S(2)}, u32[]{:S(2)}) collective-permute-start(bf16[2,128,512]{2,1,0:T(8,128)(2,1)S(1)} %pad_maximum_fusion.2), channel_id=1, source_target_pairs={{8,0},{12,4},{16,8},{20,12},{24,16},{28,20},{9,1},{13,5},{17,9},{2... | collective-permute-start | bytes 786440 | tf_op jit(solution)/shard_map/ppermute | solution.py:33
  64.8 2.4 %collective-permute-start.9 = (bf16[2,128,512]{2,1,0:T(8,128)(2,1)S(1)}, bf16[2,128,512]{2,1,0:T(8,128)(2,1)S(1)}, u32[]{:S(2)}, u32[]{:S(2)}) collective-permute-start(bf16[2,128,512]{2,1,0:T(8,128)(2,1)S(1)} %pad_maximum_fusion.1), channel_id=1, source_target_pairs={{4,0},{8,4},{12,8},{16,12},{20,16},{24,20},{28,24},{5,1},{9,5},{13... | collective-permute-start | bytes 786440 | tf_op jit(solution)/shard_map/ppermute | solution.py:33
  67.2 3.3 %collective-permute-done.10 = bf16[2,128,512]{2,1,0:T(8,128)(2,1)S(1)} collective-permute-done((bf16[2,128,512]{2,1,0:T(8,128)(2,1)S(1)}, bf16[2,128,512]{2,1,0:T(8,128)(2,1)S(1)}, u32[]{:S(2)}, u32[]{:S(2)}) %collective-permute-start.10) | collective-permute-done | bytes 262176 | tf_op jit(solution)/shard_map/ppermute | solution.py:33
  70.5 4.3 %collective-permute-done.9 = bf16[2,128,512]{2,1,0:T(8,128)(2,1)S(1)} collective-permute-done((bf16[2,128,512]{2,1,0:T(8,128)(2,1)S(1)}, bf16[2,128,512]{2,1,0:T(8,128)(2,1)S(1)}, u32[]{:S(2)}, u32[]{:S(2)}) %collective-permute-start.9) | collective-permute-done | bytes 262176 | tf_op jit(solution)/shard_map/ppermute | solution.py:33
  74.8 0.7 fusion.2
  (27 shorter events, 1.7 us)
Async XLA Ops:
  3.8 23.8 %copy-start = (bf16[4,32,4096]{2,1,0:T(8,128)(2,1)S(1)}, bf16[4,32,4096]{2,1,0:T(8,128)(2,1)}, u32[]{:S(2)}) copy-start(bf16[4,32,4096]{2,1,0:T(8,128)(2,1)} %query_ref.1) | copy-start | bytes 3145732
  3.8 23.8 %copy-start.1 = (bf16[4,32,4096]{2,1,0:T(8,128)(2,1)S(1)}, bf16[4,32,4096]{2,1,0:T(8,128)(2,1)}, u32[]{:S(2)}) copy-start(bf16[4,32,4096]{2,1,0:T(8,128)(2,1)} %grad_ref.1) | copy-start | bytes 3145732
  3.8 23.8 %copy-start.2 = (s32[4,1024]{1,0:T(4,128)S(1)}, s32[4,1024]{1,0:T(4,128)}, u32[]{:S(2)}) copy-start(s32[4,1024]{1,0:T(4,128)} %segment_ref.9) | copy-start | bytes 49156
  3.9 23.8 %copy-start.3 = (s32[4]{0:T(128)S(1)}, s32[4]{0:T(128)}, u32[]{:S(2)}) copy-start(s32[4]{0:T(128)} %assign_ref.11) | copy-start | bytes 52
  3.9 6.4 %collective-permute-start = (bf16[2,32,512]{2,1,0:T(8,128)(2,1)}, bf16[2,32,512]{2,1,0:T(8,128)(2,1)S(1)}, u32[]{:S(2)}, u32[]{:S(2)}) collective-permute-start(bf16[2,32,512]{2,1,0:T(8,128)(2,1)} %get-tuple-element.38), channel_id=1, source_target_pairs={{0,1},{1,2},{2,3},{3,0},{4,5},{5,6},{6,7},{7,4},{8,9},{9,10},{10,1... | collective-permute-start | bytes 196616 | tf_op jit(solution)/shard_map/ppermute | solution.py:27
  6.1 7.5 %collective-permute-start.2 = (bf16[2,32,512]{2,1,0:T(8,128)(2,1)}, bf16[2,32,512]{2,1,0:T(8,128)(2,1)S(1)}, u32[]{:S(2)}, u32[]{:S(2)}) collective-permute-start(bf16[2,32,512]{2,1,0:T(8,128)(2,1)} %get-tuple-element.44), channel_id=1, source_target_pairs={{0,2},{1,3},{2,0},{3,1},{4,6},{5,7},{6,4},{7,5},{8,10},{9,11},{10,... | collective-permute-start | bytes 196616 | tf_op jit(solution)/shard_map/ppermute | solution.py:27
  8.4 5.2 %collective-permute-start.3 = (bf16[2,32,512]{2,1,0:T(8,128)(2,1)}, bf16[2,32,512]{2,1,0:T(8,128)(2,1)S(1)}, u32[]{:S(2)}, u32[]{:S(2)}) collective-permute-start(bf16[2,32,512]{2,1,0:T(8,128)(2,1)} %get-tuple-element.45), channel_id=1, source_target_pairs={{0,3},{1,0},{2,1},{3,2},{4,7},{5,4},{6,5},{7,6},{8,11},{9,8},{10,9... | collective-permute-start | bytes 196616 | tf_op jit(solution)/shard_map/ppermute | solution.py:27
  10.3 21.3 %collective-permute-start.1 = (bf16[2,32,4096]{2,1,0:T(8,128)(2,1)}, bf16[2,32,4096]{2,1,0:T(8,128)(2,1)S(1)}, u32[]{:S(2)}, u32[]{:S(2)}) collective-permute-start(bf16[2,32,4096]{2,1,0:T(8,128)(2,1)} %get-tuple-element.40), channel_id=1, source_target_pairs={{0,1},{1,2},{2,3},{3,0},{4,5},{5,6},{6,7},{7,4},{8,9},{9,10},{10,1... | collective-permute-start | bytes 1572872 | tf_op jit(solution)/shard_map/ppermute | solution.py:27
  13.6 10.8 %collective-permute-start.5 = (bf16[4,2,32,512]{3,2,1,0:T(8,128)(2,1)S(1)}, bf16[4,2,32,512]{3,2,1,0:T(8,128)(2,1)}, u32[]{:S(2)}, u32[]{:S(2)}) collective-permute-start(bf16[4,2,32,512]{3,2,1,0:T(8,128)(2,1)S(1)} %bitcast_dynamic-update-slice_fusion), channel_id=1, source_target_pairs={{0,4},{4,8},{8,12},{12,16},{16,20},{20,24},{24,28},{1,5},{5,9},{9,... | collective-permute-start | bytes 786440 | tf_op jit(solution)/shard_map/ppermute | solution.py:33
  16.0 9.9 %collective-permute-start.4 = (bf16[4,2,32,512]{3,2,1,0:T(8,128)(2,1)S(1)}, bf16[4,2,32,512]{3,2,1,0:T(8,128)(2,1)}, u32[]{:S(2)}, u32[]{:S(2)}) collective-permute-start(bf16[4,2,32,512]{3,2,1,0:T(8,128)(2,1)S(1)} %bitcast_dynamic-update-slice_fusion), channel_id=1, source_target_pairs={{0,8},{4,12},{8,16},{12,20},{16,24},{20,28},{1,9},{5,13},{9,17},{1... | collective-permute-start | bytes 786440 | tf_op jit(solution)/shard_map/ppermute | solution.py:33
  21.1 16.6 %collective-permute-start.7 = (bf16[2,32,4096]{2,1,0:T(8,128)(2,1)}, bf16[2,32,4096]{2,1,0:T(8,128)(2,1)S(1)}, u32[]{:S(2)}, u32[]{:S(2)}) collective-permute-start(bf16[2,32,4096]{2,1,0:T(8,128)(2,1)} %get-tuple-element.51), channel_id=1, source_target_pairs={{0,3},{1,0},{2,1},{3,2},{4,7},{5,4},{6,5},{7,6},{8,11},{9,8},{10,9... | collective-permute-start | bytes 1572872 | tf_op jit(solution)/shard_map/ppermute | solution.py:27
  24.4 2.6 %copy-start.5 = (bf16[2,32,2048]{2,1,0:T(8,128)(2,1)S(1)}, bf16[2,32,2048]{2,1,0:T(8,128)(2,1)}, u32[]{:S(2)}) copy-start(bf16[2,32,2048]{2,1,0:T(8,128)(2,1)} %get-tuple-element.55) | copy-start | bytes 786436
  27.0 27.4 %collective-permute-start.8 = (bf16[2,32,2048]{2,1,0:T(8,128)(2,1)S(1)}, bf16[2,32,2048]{2,1,0:T(8,128)(2,1)S(1)}, u32[]{:S(2)}, u32[]{:S(2)}) collective-permute-start(bf16[2,32,2048]{2,1,0:T(8,128)(2,1)S(1)} %copy-done.5), channel_id=1, source_target_pairs={{0,2},{1,3},{2,0},{3,1},{4,6},{5,7},{6,4},{7,5},{8,10},{9,11},{10,... | collective-permute-start | bytes 786440 | tf_op jit(solution)/shard_map/ppermute | solution.py:27
  31.6 3.9 %copy-start.4 = (bf16[2,32,2048]{2,1,0:T(8,128)(2,1)S(1)}, bf16[2,32,2048]{2,1,0:T(8,128)(2,1)}, u32[]{:S(2)}) copy-start(bf16[2,32,2048]{2,1,0:T(8,128)(2,1)} %get-tuple-element.50) | copy-start | bytes 786436
  35.5 24.5 %collective-permute-start.6 = (bf16[2,32,2048]{2,1,0:T(8,128)(2,1)S(1)}, bf16[2,32,2048]{2,1,0:T(8,128)(2,1)S(1)}, u32[]{:S(2)}, u32[]{:S(2)}) collective-permute-start(bf16[2,32,2048]{2,1,0:T(8,128)(2,1)S(1)} %copy-done.4), channel_id=1, source_target_pairs={{0,2},{1,3},{2,0},{3,1},{4,6},{5,7},{6,4},{7,5},{8,10},{9,11},{10,... | collective-permute-start | bytes 786440 | tf_op jit(solution)/shard_map/ppermute | solution.py:27
  62.5 8.0 %collective-permute-start.10 = (bf16[2,128,512]{2,1,0:T(8,128)(2,1)S(1)}, bf16[2,128,512]{2,1,0:T(8,128)(2,1)S(1)}, u32[]{:S(2)}, u32[]{:S(2)}) collective-permute-start(bf16[2,128,512]{2,1,0:T(8,128)(2,1)S(1)} %pad_maximum_fusion.2), channel_id=1, source_target_pairs={{8,0},{12,4},{16,8},{20,12},{24,16},{28,20},{9,1},{13,5},{17,9},{2... | collective-permute-start | bytes 786440 | tf_op jit(solution)/shard_map/ppermute | solution.py:33
  64.8 9.9 %collective-permute-start.9 = (bf16[2,128,512]{2,1,0:T(8,128)(2,1)S(1)}, bf16[2,128,512]{2,1,0:T(8,128)(2,1)S(1)}, u32[]{:S(2)}, u32[]{:S(2)}) collective-permute-start(bf16[2,128,512]{2,1,0:T(8,128)(2,1)S(1)} %pad_maximum_fusion.1), channel_id=1, source_target_pairs={{4,0},{8,4},{12,8},{16,12},{20,16},{24,20},{28,24},{5,1},{9,5},{13... | collective-permute-start | bytes 786440 | tf_op jit(solution)/shard_map/ppermute | solution.py:33

commit v12 on v10

--- a/solution.py
+++ b/solution.py
@@ -40,12 +40,11 @@
     loads, stores = [], []
     for out, (first, step, start, width) in enumerate(jobs):
         chosen = assign_ref[target_of(group, step, count)]
-        goal = out_refs[out] if step else out_refs[out].at[group]
         for which in range(2):
             origin = sources[first + which].at[chosen, :, start : start + width]
             held, slot = held_refs[out].at[which], 2 * out + which
             loads.append(pltpu.make_async_copy(origin, held, in_sems.at[slot]))
-            stores.append(pltpu.make_async_copy(held, goal.at[which], out_sems.at[slot]))
+            stores.append(pltpu.make_async_copy(held, out_refs[out].at[which], out_sems.at[slot]))
     for load in loads:
         load.start()
     for load, store in zip(loads, stores):
@@ -57,8 +56,7 @@
 
 def stage(assignment, arrays, jobs):
     count, rows, _ = arrays[0].shape
-    held = [(2, rows, width) for _, _, _, width in jobs]
-    shapes = [shape if job[1] else (count, *shape) for shape, job in zip(held, jobs)]
+    shapes = [(2, rows, width) for _, _, _, width in jobs]
     kind = arrays[0].dtype
     far = pl.BlockSpec(memory_space=pltpu.HBM)
     return pl.pallas_call(
@@ -66,7 +64,7 @@
         out_shape=[jax.ShapeDtypeStruct(shape, kind) for shape in shapes],
         in_specs=[pl.BlockSpec(memory_space=pltpu.SMEM)] + [far] * len(arrays),
         out_specs=[far] * len(jobs),
-        scratch_shapes=[pltpu.VMEM(shape, kind) for shape in held]
+        scratch_shapes=[pltpu.VMEM(shape, kind) for shape in shapes]
         + [pltpu.SemaphoreType.DMA((2 * len(jobs),))] * 2,
         name="stage",
     )(assignment, *arrays)
@@ -271,13 +269,15 @@
     order = [*others[1:], final]
     jobs.append((0, others[0], 0, width))
     jobs += [(0, step, half * part, part) for half in range(halves) for step in order]
-    kv_own, *staged = stage(assignment, (queries, grad_out, keys, values), jobs)
-    kv_arrived = [exchanged(staged[step - 1], "dp", step) for step in range(1, count)]
-    ahead, behind = staged[count - 1 : count + len(order)], staged[count + len(order) :]
-    ahead, kv_arrived = lax.optimization_barrier((ahead, kv_arrived))
-    whole = exchanged(ahead[0], "dp", others[0])
-    arrived = [[exchanged(rows, "dp", step) for rows, step in zip(ahead[1:], order)]]
-    for step, piece in enumerate(kv_arrived, 1):
+    staged = stage(assignment, (queries, grad_out, keys, values), jobs)
+    kv_staged, staged = staged[:count], list(staged[count:])
+    kv_arrived = [exchanged(kv_staged[step], "dp", step) for step in range(1, count)]
+    staged, kv_arrived[0] = lax.optimization_barrier((staged, kv_arrived[0]))
+    whole = exchanged(staged[0], "dp", others[0])
+    arrived = [exchanged(rows, "dp", step) for rows, step in zip(staged[1:], order)]
+    behind = staged[1 + len(order) :]
+    kv_own = jnp.zeros((count, *kv_staged[0].shape), keys.dtype)
+    for step, piece in enumerate([kv_staged[0], *kv_arrived]):
         kv_own = lax.dynamic_update_index_in_dim(
             kv_own, piece, source_of(group, step, count), 0
         )
@@ -291,9 +291,10 @@
     for half in range(halves):
         base = half * HEADS_STEP
         full, acc = attend(0, base, HEADS_STEP, *fixed, *own, kv, None, full, False)
+        accs.append(acc)
         if not half:
-            behind, acc = lax.optimization_barrier((behind, acc))
-        accs.append(acc)
+            behind, full = lax.optimization_barrier((behind, full))
+    arrived += [exchanged(rows, "dp", order[at % len(order)]) for at, rows in enumerate(behind)]
     for half in range(halves):
         base = half * HEADS_STEP
         full, accs[half] = attend(
@@ -301,13 +302,7 @@
         )
     for half in range(halves):
         base = half * HEADS_STEP
-        if half:
-            rows, full = lax.optimization_barrier((behind[half * len(order) - 1], full))
-            arrived[half].append(exchanged(rows, "dp", final))
-        if half + 1 < halves:
-            rows = behind[half * len(order) : (half + 1) * len(order) - 1]
-            arrived.append([exchanged(piece, "dp", step) for piece, step in zip(rows, order)])
-        for both, step in zip(arrived[half], order):
+        for both, step in zip(arrived[half * len(order) :], order):
             pair = (both, lambda m, a: 0), (both, lambda m, a: 1)
             full, accs[half], *halos = attend(
                 step, base, HEADS_STEP, *fixed, *pair, kv, accs[half], full, step == final

time: 78.6 us -> 77.4 us (0.985)
  the two profiles are of different devices: /device:TPU:11 before, /device:TPU:19 now
where the time goes in v12:
time: 77.4 us; the launch traced here: 77 us
  starting transfers between devices  39.2 us (51%)
  Pallas kernels  22.4 us (29%)
  waiting for transfers between devices  12.8 us (17%)
  other arithmetic  0.99 us (1%)
  local copies, waits for them, and re-layouts  0.89 us (1%)
  between operations  0.83 us (1%)
    ppermute x6, starting transfers between devices, shifted(): return lax.ppermute(value, axis, pairs)  27.1 us
    pallas_call x8, Pallas kernels, attend(): pl.pallas_call(functools.partial(attend_kernel, step, first, filled, last...  19.1 us
    ppermute x8, starting transfers between devices, exchanged(): lax.ppermute(value, axis, [(i, (i + step) % count) for i in range(count)])  12.1 us
    ppermute x8, waiting for transfers between devices, exchanged(): lax.ppermute(value, axis, [(i, (i + step) % count) for i in range(count)])  8.11 us
    ppermute x6, waiting for transfers between devices, shifted(): return lax.ppermute(value, axis, pairs)  4.64 us
    pallas_call x1, Pallas kernels, stage(): pl.pallas_call(functools.partial(stage_kernel, count, jobs, len(jobs)), o...  3.25 us
  transfers between devices with their start and end apart: 14, of which 5 were waited for; matrix products, arithmetic and copies ran while one was open for 0% of the time, Pallas kernels for 25%

profile of v12, /device:TPU:19, one launch (start us, length us, event | category | flops | bytes accessed | tf_op | source)
XLA Modules:
  0.0 77.0 jit_solution(2013238805099389330)
XLA Ops:
  0.6 3.2 %stage.1 = (bf16[2,32,512]{2,1,0:T(8,128)(2,1)}, bf16[2,32,512]{2,1,0:T(8,128)(2,1)}, bf16[2,32,512]{2,1,0:T(8,128)(2,1)}, bf16[2,32,512]{2,1,0:T(8,128)(2,1)}, ...) custom-call(s32[4]{0:T(128)} %assign_ref.17, ...), custom_call_target="tpu_custom_call" | custom-call | tf_op jit(solution)/shard_map/stage/pallas_call | solution.py:62
  3.9 1.3 %collective-permute-start = (bf16[2,32,512]{2,1,0:T(8,128)(2,1)}, bf16[2,32,512]{2,1,0:T(8,128)(2,1)S(1)}, u32[]{:S(2)}, u32[]{:S(2)}) collective-permute-start(bf16[2,32,512]{2,1,0:T(8,128)(2,1)} %get-tuple-element.48), channel_id=1, source_target_pairs={{0,1},{1,2},{2,3},{3,0},{4,5},{5,6},{6,7},{7,4},{8,9},{9,10},{10,1... | collective-permute-start | bytes 196616 | tf_op jit(solution)/shard_map/ppermute | solution.py:27
  5.3 1.2 %collective-permute-start.2 = (bf16[2,32,512]{2,1,0:T(8,128)(2,1)}, bf16[2,32,512]{2,1,0:T(8,128)(2,1)S(1)}, u32[]{:S(2)}, u32[]{:S(2)}) collective-permute-start(bf16[2,32,512]{2,1,0:T(8,128)(2,1)} %get-tuple-element.54), channel_id=1, source_target_pairs={{0,3},{1,0},{2,1},{3,2},{4,7},{5,4},{6,5},{7,6},{8,11},{9,8},{10,9... | collective-permute-start | bytes 196616 | tf_op jit(solution)/shard_map/ppermute | solution.py:27
  9.6 1.4 %collective-permute-done.2 = bf16[2,32,512]{2,1,0:T(8,128)(2,1)S(1)} collective-permute-done((bf16[2,32,512]{2,1,0:T(8,128)(2,1)}, bf16[2,32,512]{2,1,0:T(8,128)(2,1)S(1)}, u32[]{:S(2)}, u32[]{:S(2)}) %collective-permute-start.2) | collective-permute-done | bytes 65568 | tf_op jit(solution)/shard_map/ppermute | solution.py:27
  11.0 4.0 %collective-permute-start.4 = (bf16[4,2,32,512]{3,2,1,0:T(8,128)(2,1)S(1)}, bf16[4,2,32,512]{3,2,1,0:T(8,128)(2,1)S(1)}, u32[]{:S(2)}, u32[]{:S(2)}) collective-permute-start(bf16[4,2,32,512]{3,2,1,0:T(8,128)(2,1)S(1)} %bitcast_dynamic-update-slice_fusion), channel_id=1, source_target_pairs={{0,4},{4,8},{8,12},{12,16},{16,20},{20,24},{24,28},{1,5},{5,9},{9,... | collective-permute-start | bytes 786440 | tf_op jit(solution)/shard_map/ppermute | solution.py:33
  15.0 1.9 %collective-permute-start.3 = (bf16[4,2,32,512]{3,2,1,0:T(8,128)(2,1)S(1)}, bf16[4,2,32,512]{3,2,1,0:T(8,128)(2,1)S(1)}, u32[]{:S(2)}, u32[]{:S(2)}) collective-permute-start(bf16[4,2,32,512]{3,2,1,0:T(8,128)(2,1)S(1)} %bitcast_dynamic-update-slice_fusion), channel_id=1, source_target_pairs={{0,8},{4,12},{8,16},{12,20},{16,24},{20,28},{1,9},{5,13},{9,17},{1... | collective-permute-start | bytes 786440 | tf_op jit(solution)/shard_map/ppermute | solution.py:33
  17.1 1.8 %collective-permute-start.8 = (bf16[2,32,2048]{2,1,0:T(8,128)(2,1)}, bf16[2,32,2048]{2,1,0:T(8,128)(2,1)S(1)}, u32[]{:S(2)}, u32[]{:S(2)}) collective-permute-start(bf16[2,32,2048]{2,1,0:T(8,128)(2,1)} %get-tuple-element.65), channel_id=1, source_target_pairs={{0,2},{1,3},{2,0},{3,1},{4,6},{5,7},{6,4},{7,5},{8,10},{9,11},{10,... | collective-permute-start | bytes 786440 | tf_op jit(solution)/shard_map/ppermute | solution.py:27
  18.9 2.4 %collective-permute-start.9 = (bf16[2,32,2048]{2,1,0:T(8,128)(2,1)}, bf16[2,32,2048]{2,1,0:T(8,128)(2,1)S(1)}, u32[]{:S(2)}, u32[]{:S(2)}) collective-permute-start(bf16[2,32,2048]{2,1,0:T(8,128)(2,1)} %get-tuple-element.66), channel_id=1, source_target_pairs={{0,3},{1,0},{2,1},{3,2},{4,7},{5,4},{6,5},{7,6},{8,11},{9,8},{10,9... | collective-permute-start | bytes 786440 | tf_op jit(solution)/shard_map/ppermute | solution.py:27
  21.5 2.3 %attend.8 = (bf16[128,32,128]{2,1,0:T(8,128)(2,1)}, f32[2,384,256]{2,1,0:T(8,128)S(1)}) custom-call(s32[2]{0:T(128)S(1)} %pad_add_fusion.meta_ref, s32[4]{0:T(128)S(1)} %copy-done.3, s32[4,1024]{1,0:T(4,128)S(1)} %copy-done.2, bf16[4,32,4096]{2,1,0:T(8,128)(2,1)S(1)} %copy-done, bf16[4,32,4096]{2,1,0:T(8,128)(2,1)S(1)} %copy-done.1, ...), custom_call_target="tpu_custom_call" | custom-call | flops 18874368 | bytes 147456 | tf_op jit(solution)/shard_map/attend/pallas_call | solution.py:232
  24.7 3.2 %collective-permute-start.5 = (bf16[2,32,2048]{2,1,0:T(8,128)(2,1)S(1)}, bf16[2,32,2048]{2,1,0:T(8,128)(2,1)S(1)}, u32[]{:S(2)}, u32[]{:S(2)}) collective-permute-start(bf16[2,32,2048]{2,1,0:T(8,128)(2,1)S(1)} %copy-done.5), channel_id=1, source_target_pairs={{0,2},{1,3},{2,0},{3,1},{4,6},{5,7},{6,4},{7,5},{8,10},{9,11},{10,... | collective-permute-start | bytes 786440 | tf_op jit(solution)/shard_map/ppermute | solution.py:27
  27.9 2.3 %attend.9 = (bf16[128,32,128]{2,1,0:T(8,128)(2,1)}, f32[2,384,256]{2,1,0:T(8,128)S(1)}) custom-call(s32[2]{0:T(128)S(1)} %pad_add_fusion.meta_ref, s32[4]{0:T(128)S(1)} %copy-done.3, s32[4,1024]{1,0:T(4,128)S(1)} %copy-done.2, bf16[4,32,4096]{2,1,0:T(8,128)(2,1)S(1)} %copy-done, bf16[4,32,4096]{2,1,0:T(8,128)(2,1)S(1)} %copy-done.1, ...), custom_call_target="tpu_custom_call", output_to_operand_aliasing={{0}: (6, {})} | custom-call | flops 18874368 | bytes 147456 | tf_op jit(solution)/shard_map/attend/pallas_call | solution.py:232
  30.2 2.5 %attend.10 = (bf16[128,32,128]{2,1,0:T(8,128)(2,1)}, f32[2,384,256]{2,1,0:T(8,128)S(1)}) custom-call(s32[2]{0:T(128)S(1)} %pad_add_fusion.meta_ref, s32[4]{0:T(128)S(1)} %copy-done.3, s32[4,1024]{1,0:T(4,128)S(1)} %copy-done.2, bf16[2,32,4096]{2,1,0:T(8,128)(2,1)S(1)} %collective-permute-done.7.query_ref.grad_ref, ...), custom_call_target="tpu_custom_call", output_to_operand_aliasing={{1}: (6, {}), {0}: (7, {})} | custom-call | flops 18874368 | bytes 147456 | tf_op jit(solution)/shard_map/attend/pallas_call | solution.py:232
  32.6 2.5 %attend.11 = (bf16[128,32,128]{2,1,0:T(8,128)(2,1)}, f32[2,384,256]{2,1,0:T(8,128)S(1)}) custom-call(s32[2]{0:T(128)S(1)} %pad_add_fusion.meta_ref, s32[4]{0:T(128)S(1)} %copy-done.3, s32[4,1024]{1,0:T(4,128)S(1)} %copy-done.2, bf16[2,32,4096]{2,1,0:T(8,128)(2,1)S(1)} %collective-permute-done.7.query_ref.grad_ref, ...), custom_call_target="tpu_custom_call", output_to_operand_aliasing={{1}: (6, {}), {0}: (7, {})} | custom-call | flops 18874368 | bytes 147456 | tf_op jit(solution)/shard_map/attend/pallas_call | solution.py:232
  35.1 5.7 %collective-permute-done.9.query_ref.grad_ref = bf16[2,32,2048]{2,1,0:T(8,128)(2,1)S(1)} collective-permute-done((bf16[2,32,2048]{2,1,0:T(8,128)(2,1)}, bf16[2,32,2048]{2,1,0:T(8,128)(2,1)S(1)}, u32[]{:S(2)}, u32[]{:S(2)}) %collective-permute-start.9) | collective-permute-done | bytes 262176 | tf_op jit(solution)/shard_map/ppermute | solution.py:27
  40.8 2.4 %attend.12 = (bf16[128,32,128]{2,1,0:T(8,128)(2,1)}, f32[2,384,256]{2,1,0:T(8,128)S(1)}) custom-call(s32[2]{0:T(128)S(1)} %pad_add_fusion.meta_ref, s32[4]{0:T(128)S(1)} %copy-done.3, s32[4,1024]{1,0:T(4,128)S(1)} %copy-done.2, bf16[2,32,2048]{2,1,0:T(8,128)(2,1)S(1)} %collective-permute-done.9.query_ref.grad_ref, ...), custom_call_target="tpu_custom_call", output_to_operand_aliasing={{1}: (6, {}), {0}: (7, {})} | custom-call | flops 18874368 | bytes 147456 | tf_op jit(solution)/shard_map/attend/pallas_call | solution.py:232
  43.2 2.4 %attend.13 = (bf16[128,32,128]{2,1,0:T(8,128)(2,1)}, f32[2,128,256]{2,1,0:T(8,128)S(1)}, bf16[2,128,256]{2,1,0:T(8,128)(2,1)S(1)}, bf16[2,128,256]{2,1,0:T(8,128)(2,1)S(1)}) custom-call(s32[2]{0:T(128)S(1)} %pad_add_fusion.meta_ref, s32[4]{0:T(128)S(1)} %copy-done.3, s32[4,1024]{1,0:T(4,128)S(1)} %copy-done.2, ...), custom_call_target="tpu_custom_call", output_to_operand_aliasing={{0}: (7, {})} | custom-call | flops 18874368 | bytes 147456 | tf_op jit(solution)/shard_map/attend/pallas_call | solution.py:232
  45.6 1.9 %collective-permute-start.10 = (bf16[2,128,256]{2,1,0:T(8,128)(2,1)S(1)}, bf16[2,128,256]{2,1,0:T(8,128)(2,1)S(1)}, u32[]{:S(2)}, u32[]{:S(2)}) collective-permute-start(bf16[2,128,256]{2,1,0:T(8,128)(2,1)S(1)} %get-tuple-element.76), channel_id=1, source_target_pairs={{4,0},{8,4},{12,8},{16,12},{20,16},{24,20},{28,24},{5,1},{9,5},{13... | collective-permute-start | bytes 393224 | tf_op jit(solution)/shard_map/ppermute | solution.py:33
  47.5 14.2 %collective-permute-start.11 = (bf16[2,128,256]{2,1,0:T(8,128)(2,1)S(1)}, bf16[2,128,256]{2,1,0:T(8,128)(2,1)S(1)}, u32[]{:S(2)}, u32[]{:S(2)}) collective-permute-start(bf16[2,128,256]{2,1,0:T(8,128)(2,1)S(1)} %get-tuple-element.77), channel_id=1, source_target_pairs={{8,0},{12,4},{16,8},{20,12},{24,16},{28,20},{9,1},{13,5},{17,9},{2... | collective-permute-start | bytes 393224 | tf_op jit(solution)/shard_map/ppermute | solution.py:33
  61.7 2.4 %attend.14 = (bf16[128,32,128]{2,1,0:T(8,128)(2,1)}, f32[2,384,256]{2,1,0:T(8,128)S(1)}) custom-call(s32[2]{0:T(128)S(1)} %pad_add_fusion.meta_ref, s32[4]{0:T(128)S(1)} %copy-done.3, s32[4,1024]{1,0:T(4,128)S(1)} %copy-done.2, bf16[2,32,2048]{2,1,0:T(8,128)(2,1)S(1)} %collective-permute-done.6.query_ref.grad_ref, ...), custom_call_target="tpu_custom_call", output_to_operand_aliasing={{1}: (6, {}), {0}: (7, {})} | custom-call | flops 18874368 | bytes 147456 | tf_op jit(solution)/shard_map/attend/pallas_call | solution.py:232
  64.2 2.4 %attend.15 = (bf16[128,32,128]{2,1,0:T(8,128)(2,1)}, f32[2,128,256]{2,1,0:T(8,128)S(1)}, bf16[2,128,256]{2,1,0:T(8,128)(2,1)S(1)}, bf16[2,128,256]{2,1,0:T(8,128)(2,1)S(1)}) custom-call(s32[2]{0:T(128)S(1)} %pad_add_fusion.meta_ref, s32[4]{0:T(128)S(1)} %copy-done.3, s32[4,1024]{1,0:T(4,128)S(1)} %copy-done.2, ...), custom_call_target="tpu_custom_call", output_to_operand_aliasing={{0}: (7, {})} | custom-call | flops 18874368 | bytes 147456 | tf_op jit(solution)/shard_map/attend/pallas_call | solution.py:232
  66.6 3.1 %collective-permute-start.12 = (bf16[2,128,256]{2,1,0:T(8,128)(2,1)S(1)}, bf16[2,128,256]{2,1,0:T(8,128)(2,1)S(1)}, u32[]{:S(2)}, u32[]{:S(2)}) collective-permute-start(bf16[2,128,256]{2,1,0:T(8,128)(2,1)S(1)} %get-tuple-element.81), channel_id=1, source_target_pairs={{4,0},{8,4},{12,8},{16,12},{20,16},{24,20},{28,24},{5,1},{9,5},{13... | collective-permute-start | bytes 393224 | tf_op jit(solution)/shard_map/ppermute | solution.py:33
  69.7 1.9 %collective-permute-start.13 = (bf16[2,128,256]{2,1,0:T(8,128)(2,1)S(1)}, bf16[2,128,256]{2,1,0:T(8,128)(2,1)S(1)}, u32[]{:S(2)}, u32[]{:S(2)}) collective-permute-start(bf16[2,128,256]{2,1,0:T(8,128)(2,1)S(1)} %get-tuple-element.82), channel_id=1, source_target_pairs={{8,0},{12,4},{16,8},{20,12},{24,16},{28,20},{9,1},{13,5},{17,9},{2... | collective-permute-start | bytes 393224 | tf_op jit(solution)/shard_map/ppermute | solution.py:33
  71.6 3.2 %collective-permute-done.12 = bf16[2,128,256]{2,1,0:T(8,128)(2,1)S(1)} collective-permute-done((bf16[2,128,256]{2,1,0:T(8,128)(2,1)S(1)}, bf16[2,128,256]{2,1,0:T(8,128)(2,1)S(1)}, u32[]{:S(2)}, u32[]{:S(2)}) %collective-permute-start.12) | collective-permute-done | bytes 131104 | tf_op jit(solution)/shard_map/ppermute | solution.py:33
  74.9 1.4 %collective-permute-done.13 = bf16[2,128,256]{2,1,0:T(8,128)(2,1)S(1)} collective-permute-done((bf16[2,128,256]{2,1,0:T(8,128)(2,1)S(1)}, bf16[2,128,256]{2,1,0:T(8,128)(2,1)S(1)}, u32[]{:S(2)}, u32[]{:S(2)}) %collective-permute-start.13) | collective-permute-done | bytes 131104 | tf_op jit(solution)/shard_map/ppermute | solution.py:33
  (37 shorter events, 5.0 us)
Async XLA Ops:
  3.9 3.5 %collective-permute-start = (bf16[2,32,512]{2,1,0:T(8,128)(2,1)}, bf16[2,32,512]{2,1,0:T(8,128)(2,1)S(1)}, u32[]{:S(2)}, u32[]{:S(2)}) collective-permute-start(bf16[2,32,512]{2,1,0:T(8,128)(2,1)} %get-tuple-element.48), channel_id=1, source_target_pairs={{0,1},{1,2},{2,3},{3,0},{4,5},{5,6},{6,7},{7,4},{8,9},{9,10},{10,1... | collective-permute-start | bytes 196616 | tf_op jit(solution)/shard_map/ppermute | solution.py:27
  5.2 4.3 %collective-permute-start.1 = (bf16[2,32,512]{2,1,0:T(8,128)(2,1)}, bf16[2,32,512]{2,1,0:T(8,128)(2,1)S(1)}, u32[]{:S(2)}, u32[]{:S(2)}) collective-permute-start(bf16[2,32,512]{2,1,0:T(8,128)(2,1)} %get-tuple-element.53), channel_id=1, source_target_pairs={{0,2},{1,3},{2,0},{3,1},{4,6},{5,7},{6,4},{7,5},{8,10},{9,11},{10,... | collective-permute-start | bytes 196616 | tf_op jit(solution)/shard_map/ppermute | solution.py:27
  5.3 5.7 %collective-permute-start.2 = (bf16[2,32,512]{2,1,0:T(8,128)(2,1)}, bf16[2,32,512]{2,1,0:T(8,128)(2,1)S(1)}, u32[]{:S(2)}, u32[]{:S(2)}) collective-permute-start(bf16[2,32,512]{2,1,0:T(8,128)(2,1)} %get-tuple-element.54), channel_id=1, source_target_pairs={{0,3},{1,0},{2,1},{3,2},{4,7},{5,4},{6,5},{7,6},{8,11},{9,8},{10,9... | collective-permute-start | bytes 196616 | tf_op jit(solution)/shard_map/ppermute | solution.py:27
  6.5 0.8 %copy-start.4 = (bf16[2,32,512]{2,1,0:T(8,128)(2,1)S(1)}, bf16[2,32,512]{2,1,0:T(8,128)(2,1)}, u32[]{:S(2)}) copy-start(bf16[2,32,512]{2,1,0:T(8,128)(2,1)} %get-tuple-element.51) | copy-start | bytes 196612
  7.3 14.1 %copy-start.1 = (bf16[4,32,4096]{2,1,0:T(8,128)(2,1)S(1)}, bf16[4,32,4096]{2,1,0:T(8,128)(2,1)}, u32[]{:S(2)}) copy-start(bf16[4,32,4096]{2,1,0:T(8,128)(2,1)} %grad_ref.3) | copy-start | bytes 3145732
  7.3 14.1 %copy-start = (bf16[4,32,4096]{2,1,0:T(8,128)(2,1)S(1)}, bf16[4,32,4096]{2,1,0:T(8,128)(2,1)}, u32[]{:S(2)}) copy-start(bf16[4,32,4096]{2,1,0:T(8,128)(2,1)} %query_ref.3) | copy-start | bytes 3145732
  7.4 22.8 %collective-permute-start.7 = (bf16[2,32,4096]{2,1,0:T(8,128)(2,1)}, bf16[2,32,4096]{2,1,0:T(8,128)(2,1)S(1)}, u32[]{:S(2)}, u32[]{:S(2)}) collective-permute-start(bf16[2,32,4096]{2,1,0:T(8,128)(2,1)} %get-tuple-element.58), channel_id=1, source_target_pairs={{0,1},{1,2},{2,3},{3,0},{4,5},{5,6},{6,7},{7,4},{8,9},{9,10},{10,1... | collective-permute-start | bytes 1572872 | tf_op jit(solution)/shard_map/ppermute | solution.py:27
  11.0 10.3 %collective-permute-start.4 = (bf16[4,2,32,512]{3,2,1,0:T(8,128)(2,1)S(1)}, bf16[4,2,32,512]{3,2,1,0:T(8,128)(2,1)S(1)}, u32[]{:S(2)}, u32[]{:S(2)}) collective-permute-start(bf16[4,2,32,512]{3,2,1,0:T(8,128)(2,1)S(1)} %bitcast_dynamic-update-slice_fusion), channel_id=1, source_target_pairs={{0,4},{4,8},{8,12},{12,16},{16,20},{20,24},{24,28},{1,5},{5,9},{9,... | collective-permute-start | bytes 786440 | tf_op jit(solution)/shard_map/ppermute | solution.py:33
  15.0 6.3 %collective-permute-start.3 = (bf16[4,2,32,512]{3,2,1,0:T(8,128)(2,1)S(1)}, bf16[4,2,32,512]{3,2,1,0:T(8,128)(2,1)S(1)}, u32[]{:S(2)}, u32[]{:S(2)}) collective-permute-start(bf16[4,2,32,512]{3,2,1,0:T(8,128)(2,1)S(1)} %bitcast_dynamic-update-slice_fusion), channel_id=1, source_target_pairs={{0,8},{4,12},{8,16},{12,20},{16,24},{20,28},{1,9},{5,13},{9,17},{1... | collective-permute-start | bytes 786440 | tf_op jit(solution)/shard_map/ppermute | solution.py:33
  17.1 4.4 %copy-start.2 = (s32[4,1024]{1,0:T(4,128)S(1)}, s32[4,1024]{1,0:T(4,128)}, u32[]{:S(2)}) copy-start(s32[4,1024]{1,0:T(4,128)} %segment_ref.15) | copy-start | bytes 49156
  17.1 4.4 %copy-start.3 = (s32[4]{0:T(128)S(1)}, s32[4]{0:T(128)}, u32[]{:S(2)}) copy-start(s32[4]{0:T(128)} %assign_ref.17) | copy-start | bytes 52
  17.1 26.1 %collective-permute-start.8 = (bf16[2,32,2048]{2,1,0:T(8,128)(2,1)}, bf16[2,32,2048]{2,1,0:T(8,128)(2,1)S(1)}, u32[]{:S(2)}, u32[]{:S(2)}) collective-permute-start(bf16[2,32,2048]{2,1,0:T(8,128)(2,1)} %get-tuple-element.65), channel_id=1, source_target_pairs={{0,2},{1,3},{2,0},{3,1},{4,6},{5,7},{6,4},{7,5},{8,10},{9,11},{10,... | collective-permute-start | bytes 786440 | tf_op jit(solution)/shard_map/ppermute | solution.py:27
  18.9 21.9 %collective-permute-start.9 = (bf16[2,32,2048]{2,1,0:T(8,128)(2,1)}, bf16[2,32,2048]{2,1,0:T(8,128)(2,1)S(1)}, u32[]{:S(2)}, u32[]{:S(2)}) collective-permute-start(bf16[2,32,2048]{2,1,0:T(8,128)(2,1)} %get-tuple-element.66), channel_id=1, source_target_pairs={{0,3},{1,0},{2,1},{3,2},{4,7},{5,4},{6,5},{7,6},{8,11},{9,8},{10,9... | collective-permute-start | bytes 786440 | tf_op jit(solution)/shard_map/ppermute | solution.py:27
  21.4 2.3 %copy-start.6 = (bf16[2,32,2048]{2,1,0:T(8,128)(2,1)S(1)}, bf16[2,32,2048]{2,1,0:T(8,128)(2,1)}, u32[]{:S(2)}) copy-start(bf16[2,32,2048]{2,1,0:T(8,128)(2,1)} %get-tuple-element.57) | copy-start | bytes 786436
  21.5 3.2 %copy-start.5 = (bf16[2,32,2048]{2,1,0:T(8,128)(2,1)S(1)}, bf16[2,32,2048]{2,1,0:T(8,128)(2,1)}, u32[]{:S(2)}) copy-start(bf16[2,32,2048]{2,1,0:T(8,128)(2,1)} %get-tuple-element.56) | copy-start | bytes 786436
  23.8 37.9 %collective-permute-start.6 = (bf16[2,32,2048]{2,1,0:T(8,128)(2,1)S(1)}, bf16[2,32,2048]{2,1,0:T(8,128)(2,1)S(1)}, u32[]{:S(2)}, u32[]{:S(2)}) collective-permute-start(bf16[2,32,2048]{2,1,0:T(8,128)(2,1)S(1)} %copy-done.6), channel_id=1, source_target_pairs={{0,3},{1,0},{2,1},{3,2},{4,7},{5,4},{6,5},{7,6},{8,11},{9,8},{10,9... | collective-permute-start | bytes 786440 | tf_op jit(solution)/shard_map/ppermute | solution.py:27
  24.7 39.5 %collective-permute-start.5 = (bf16[2,32,2048]{2,1,0:T(8,128)(2,1)S(1)}, bf16[2,32,2048]{2,1,0:T(8,128)(2,1)S(1)}, u32[]{:S(2)}, u32[]{:S(2)}) collective-permute-start(bf16[2,32,2048]{2,1,0:T(8,128)(2,1)S(1)} %copy-done.5), channel_id=1, source_target_pairs={{0,2},{1,3},{2,0},{3,1},{4,6},{5,7},{6,4},{7,5},{8,10},{9,11},{10,... | collective-permute-start | bytes 786440 | tf_op jit(solution)/shard_map/ppermute | solution.py:27
  45.6 21.0 %collective-permute-start.10 = (bf16[2,128,256]{2,1,0:T(8,128)(2,1)S(1)}, bf16[2,128,256]{2,1,0:T(8,128)(2,1)S(1)}, u32[]{:S(2)}, u32[]{:S(2)}) collective-permute-start(bf16[2,128,256]{2,1,0:T(8,128)(2,1)S(1)} %get-tuple-element.76), channel_id=1, source_target_pairs={{4,0},{8,4},{12,8},{16,12},{20,16},{24,20},{28,24},{5,1},{9,5},{13... | collective-permute-start | bytes 393224 | tf_op jit(solution)/shard_map/ppermute | solution.py:33
  47.5 19.0 %collective-permute-start.11 = (bf16[2,128,256]{2,1,0:T(8,128)(2,1)S(1)}, bf16[2,128,256]{2,1,0:T(8,128)(2,1)S(1)}, u32[]{:S(2)}, u32[]{:S(2)}) collective-permute-start(bf16[2,128,256]{2,1,0:T(8,128)(2,1)S(1)} %get-tuple-element.77), channel_id=1, source_target_pairs={{8,0},{12,4},{16,8},{20,12},{24,16},{28,20},{9,1},{13,5},{17,9},{2... | collective-permute-start | bytes 393224 | tf_op jit(solution)/shard_map/ppermute | solution.py:33
  66.6 8.3 %collective-permute-start.12 = (bf16[2,128,256]{2,1,0:T(8,128)(2,1)S(1)}, bf16[2,128,256]{2,1,0:T(8,128)(2,1)S(1)}, u32[]{:S(2)}, u32[]{:S(2)}) collective-permute-start(bf16[2,128,256]{2,1,0:T(8,128)(2,1)S(1)} %get-tuple-element.81), channel_id=1, source_target_pairs={{4,0},{8,4},{12,8},{16,12},{20,16},{24,20},{28,24},{5,1},{9,5},{13... | collective-permute-start | bytes 393224 | tf_op jit(solution)/shard_map/ppermute | solution.py:33
  69.7 6.6 %collective-permute-start.13 = (bf16[2,128,256]{2,1,0:T(8,128)(2,1)S(1)}, bf16[2,128,256]{2,1,0:T(8,128)(2,1)S(1)}, u32[]{:S(2)}, u32[]{:S(2)}) collective-permute-start(bf16[2,128,256]{2,1,0:T(8,128)(2,1)S(1)} %get-tuple-element.82), channel_id=1, source_target_pairs={{8,0},{12,4},{16,8},{20,12},{24,16},{28,20},{9,1},{13,5},{17,9},{2... | collective-permute-start | bytes 393224 | tf_op jit(solution)/shard_map/ppermute | solution.py:33

commit v13 on v11

--- a/solution.py
+++ b/solution.py
@@ -282,28 +282,30 @@
     halos = [shifted(kv_own, ("blk", "uly"), back) for back in range(hops, 0, -1)]
     kv = jnp.concatenate([*halos, kv_own], axis=0)
 
-    rows, kv = lax.optimization_barrier((held[0], kv))
-    split = [exchanged(rows, "dp", final)]
     fixed = (doc_most, heads, meta, assignment, segment_ids)
     query, grad = (queries, lambda m, a: a[m[0]]), (grad_out, lambda m, a: a[m[0]])
     full, acc = attend(0, 0, kv_heads, *fixed, query, grad, kv, None, None, False)
+    rows, acc = lax.optimization_barrier((held[0], acc))
+    split = [exchanged(rows, "dp", final)]
     for step, both in zip(others, arrived):
         query, grad = (both, lambda m, a: 0), (both, lambda m, a: 1)
         full, acc = attend(step, 0, kv_heads, *fixed, query, grad, kv, acc, full, False)
-        if len(split) < halves:
-            rows, acc = lax.optimization_barrier((held[len(split)], acc))
-            split.append(exchanged(rows, "dp", final))
-    parts = []
+    for rows in held[1:]:
+        rows, acc = lax.optimization_barrier((rows, acc))
+        split.append(exchanged(rows, "dp", final))
+    totals, returned = [], []
     for half, both in enumerate(split):
         query, grad = (both, lambda m, a: 0), (both, lambda m, a: 1)
-        full, *part = attend(
+        full, total, *halos = attend(
             final, half * HEADS_STEP, HEADS_STEP, *fixed, query, grad, kv, acc, full, True
         )
-        parts.append(part)
-    total, *halos = [jnp.concatenate(part, axis=2) for part in zip(*parts)]
-    for back, halo in enumerate(halos, 1):
-        total = total + shifted(halo, ("blk", "uly"), -back).astype(jnp.float32)
-    total = total.astype(jnp.bfloat16)
+        if half:
+            halos, returned = lax.optimization_barrier((halos, returned))
+        returned = [shifted(halo, ("blk", "uly"), -back) for back, halo in enumerate(halos, 1)]
+        for halo in returned:
+            total = total + halo.astype(jnp.float32)
+        totals.append(total.astype(jnp.bfloat16))
+    total = jnp.concatenate(totals, axis=2)
     return full[None], total[0][None], total[1][None]
 
 

time: 76.2 us -> 75.5 us (level)
  waiting for transfers between devices: 28.2 us -> 26.7 us
  starting transfers between devices: 23.9 us -> 25 us
    ppermute x4 -> x6, starting transfers between devices: 12.1 us -> 15.1 us  [shifted(): return lax.ppermute(value, axis, pairs)]
    ppermute x7, starting transfers between devices: 11.8 us -> 9.91 us  [exchanged(): lax.ppermute(value, axis, [(i, (i + step) % count) for i in range(count)])]
    ppermute x7, waiting for transfers between devices: 19.3 us -> 17.9 us  [exchanged(): lax.ppermute(value, axis, [(i, (i + step) % count) for i in range(count)])]
    ppermute x4 -> x6, waiting for transfers between devices: 8.93 us -> 8.86 us  [shifted(): return lax.ppermute(value, axis, pairs)]
  transfers between devices with their start and end apart: 11 -> 13, of which waited for: 7 -> 8; matrix products, arithmetic and copies ran while one was open for 3% -> 3% of each run, Pallas kernels for 19% -> 22%
where the time goes in v13:
time: 75.5 us; the launch traced here: 75.2 us
  waiting for transfers between devices  26.7 us (35%)
  starting transfers between devices  25 us (33%)
  Pallas kernels  19.7 us (26%)
  other arithmetic  2.01 us (3%)
  local copies, waits for them, and re-layouts  0.93 us (1%)
  between operations  0.82 us (1%)
    ppermute x7, waiting for transfers between devices, exchanged(): lax.ppermute(value, axis, [(i, (i + step) % count) for i in range(count)])  17.9 us
    pallas_call x5, Pallas kernels, attend(): pl.pallas_call(functools.partial(attend_kernel, step, first, filled, last...  16.5 us
    ppermute x6, starting transfers between devices, shifted(): return lax.ppermute(value, axis, pairs)  15.1 us
    ppermute x7, starting transfers between devices, exchanged(): lax.ppermute(value, axis, [(i, (i + step) % count) for i in range(count)])  9.91 us
    ppermute x6, waiting for transfers between devices, shifted(): return lax.ppermute(value, axis, pairs)  8.86 us
    pallas_call x1, Pallas kernels, stage(): pl.pallas_call(functools.partial(stage_kernel, count, jobs, len(jobs)), o...  3.19 us
  transfers between devices with their start and end apart: 13, of which 8 were waited for; matrix products, arithmetic and copies ran while one was open for 3% of the time, Pallas kernels for 22%

profile of v13, /device:TPU:1, one launch (start us, length us, event | category | flops | bytes accessed | tf_op | source)
XLA Modules:
  0.0 75.2 jit_solution(10032743769077497894)
XLA Ops:
  0.6 3.2 %stage.1 = (bf16[2,32,512]{2,1,0:T(8,128)(2,1)}, bf16[2,32,512]{2,1,0:T(8,128)(2,1)}, bf16[2,32,512]{2,1,0:T(8,128)(2,1)}, bf16[2,32,512]{2,1,0:T(8,128)(2,1)}, ...) custom-call(s32[4]{0:T(128)} %assign_ref.11, ...), custom_call_target="tpu_custom_call" | custom-call | tf_op jit(solution)/shard_map/stage/pallas_call | solution.py:62
  3.9 2.2 %collective-permute-start = (bf16[2,32,512]{2,1,0:T(8,128)(2,1)}, bf16[2,32,512]{2,1,0:T(8,128)(2,1)S(1)}, u32[]{:S(2)}, u32[]{:S(2)}) collective-permute-start(bf16[2,32,512]{2,1,0:T(8,128)(2,1)} %get-tuple-element.40), channel_id=1, source_target_pairs={{0,1},{1,2},{2,3},{3,0},{4,5},{5,6},{6,7},{7,4},{8,9},{9,10},{10,1... | collective-permute-start | bytes 196616 | tf_op jit(solution)/shard_map/ppermute | solution.py:27
  6.1 2.3 %collective-permute-start.2 = (bf16[2,32,512]{2,1,0:T(8,128)(2,1)}, bf16[2,32,512]{2,1,0:T(8,128)(2,1)S(1)}, u32[]{:S(2)}, u32[]{:S(2)}) collective-permute-start(bf16[2,32,512]{2,1,0:T(8,128)(2,1)} %get-tuple-element.45), channel_id=1, source_target_pairs={{0,2},{1,3},{2,0},{3,1},{4,6},{5,7},{6,4},{7,5},{8,10},{9,11},{10,... | collective-permute-start | bytes 196616 | tf_op jit(solution)/shard_map/ppermute | solution.py:27
  8.4 1.1 %collective-permute-start.3 = (bf16[2,32,512]{2,1,0:T(8,128)(2,1)}, bf16[2,32,512]{2,1,0:T(8,128)(2,1)S(1)}, u32[]{:S(2)}, u32[]{:S(2)}) collective-permute-start(bf16[2,32,512]{2,1,0:T(8,128)(2,1)} %get-tuple-element.46), channel_id=1, source_target_pairs={{0,3},{1,0},{2,1},{3,2},{4,7},{5,4},{6,5},{7,6},{8,11},{9,8},{10,9... | collective-permute-start | bytes 196616 | tf_op jit(solution)/shard_map/ppermute | solution.py:27
  10.8 2.8 %collective-permute-done.2 = bf16[2,32,512]{2,1,0:T(8,128)(2,1)S(1)} collective-permute-done((bf16[2,32,512]{2,1,0:T(8,128)(2,1)}, bf16[2,32,512]{2,1,0:T(8,128)(2,1)S(1)}, u32[]{:S(2)}, u32[]{:S(2)}) %collective-permute-start.2) | collective-permute-done | bytes 65568 | tf_op jit(solution)/shard_map/ppermute | solution.py:27
  13.6 2.4 %collective-permute-start.5 = (bf16[4,2,32,512]{3,2,1,0:T(8,128)(2,1)S(1)}, bf16[4,2,32,512]{3,2,1,0:T(8,128)(2,1)}, u32[]{:S(2)}, u32[]{:S(2)}) collective-permute-start(bf16[4,2,32,512]{3,2,1,0:T(8,128)(2,1)S(1)} %bitcast_dynamic-update-slice_fusion), channel_id=1, source_target_pairs={{0,4},{4,8},{8,12},{12,16},{16,20},{20,24},{24,28},{1,5},{5,9},{9,... | collective-permute-start | bytes 786440 | tf_op jit(solution)/shard_map/ppermute | solution.py:33
  16.0 5.0 %collective-permute-start.4 = (bf16[4,2,32,512]{3,2,1,0:T(8,128)(2,1)S(1)}, bf16[4,2,32,512]{3,2,1,0:T(8,128)(2,1)}, u32[]{:S(2)}, u32[]{:S(2)}) collective-permute-start(bf16[4,2,32,512]{3,2,1,0:T(8,128)(2,1)S(1)} %bitcast_dynamic-update-slice_fusion), channel_id=1, source_target_pairs={{0,8},{4,12},{8,16},{12,20},{16,24},{20,28},{1,9},{5,13},{9,17},{1... | collective-permute-start | bytes 786440 | tf_op jit(solution)/shard_map/ppermute | solution.py:33
  21.1 3.3 %collective-permute-start.1 = (bf16[2,32,4096]{2,1,0:T(8,128)(2,1)}, bf16[2,32,4096]{2,1,0:T(8,128)(2,1)S(1)}, u32[]{:S(2)}, u32[]{:S(2)}) collective-permute-start(bf16[2,32,4096]{2,1,0:T(8,128)(2,1)} %get-tuple-element.42), channel_id=1, source_target_pairs={{0,3},{1,0},{2,1},{3,2},{4,7},{5,4},{6,5},{7,6},{8,11},{9,8},{10,9... | collective-permute-start | bytes 1572872 | tf_op jit(solution)/shard_map/ppermute | solution.py:27
  24.5 1.4 %collective-permute-done.4 = bf16[4,2,32,512]{3,2,1,0:T(8,128)(2,1)} collective-permute-done((bf16[4,2,32,512]{3,2,1,0:T(8,128)(2,1)S(1)}, bf16[4,2,32,512]{3,2,1,0:T(8,128)(2,1)}, u32[]{:S(2)}, u32[]{:S(2)}) %collective-permute-start.4) | collective-permute-done | bytes 262176 | tf_op jit(solution)/shard_map/ppermute | solution.py:33
  25.9 1.1 %pad_maximum_fusion.kv_ref = bf16[12,2,32,512]{3,2,1,0:T(8,128)(2,1)S(1)} fusion(bf16[4,2,32,512]{3,2,1,0:T(8,128)(2,1)S(1)} %bitcast_dynamic-update-slice_fusion, bf16[4,2,32,512]{3,2,1,0:T(8,128)(2,1)} %collective-permute-done.5, bf16[4,2,32,512]{3,2,1,0:T(8,128)(2,1)} %collective-permute-done.4), kind=kLoop, calls=%fused_computation | loop fusion | flops 786432 | bytes 1572864 | tf_op jit(solution)/shard_map/concatenate | solution.py:283
  27.1 3.9 %attend.5 = (bf16[128,32,128]{2,1,0:T(8,128)(2,1)}, f32[2,384,512]{2,1,0:T(8,128)S(1)}) custom-call(s32[2]{0:T(128)S(1)} %pad_add_fusion.meta_ref, s32[4]{0:T(128)S(1)} %copy-done.3, s32[4,1024]{1,0:T(4,128)S(1)} %copy-done.2, bf16[4,32,4096]{2,1,0:T(8,128)(2,1)S(1)} %copy-done, bf16[4,32,4096]{2,1,0:T(8,128)(2,1)S(1)} %copy-done.1, ...), custom_call_target="tpu_custom_call" | custom-call | flops 37748736 | bytes 294912 | tf_op jit(solution)/shard_map/attend/pallas_call | solution.py:232
  31.6 3.9 %attend.6 = (bf16[128,32,128]{2,1,0:T(8,128)(2,1)}, f32[2,384,512]{2,1,0:T(8,128)S(1)}) custom-call(s32[2]{0:T(128)S(1)} %pad_add_fusion.meta_ref, s32[4]{0:T(128)S(1)} %copy-done.3, s32[4,1024]{1,0:T(4,128)S(1)} %copy-done.2, bf16[2,32,4096]{2,1,0:T(8,128)(2,1)S(1)} %collective-permute-done.6.query_ref.grad_ref, ...), custom_call_target="tpu_custom_call", output_to_operand_aliasing={{1}: (6, {}), {0}: (7, {})} | custom-call | flops 37748736 | bytes 294912 | tf_op jit(solution)/shard_map/attend/pallas_call | solution.py:232
  35.5 2.1 %collective-permute-done.1.query_ref.grad_ref = bf16[2,32,4096]{2,1,0:T(8,128)(2,1)S(1)} collective-permute-done((bf16[2,32,4096]{2,1,0:T(8,128)(2,1)}, bf16[2,32,4096]{2,1,0:T(8,128)(2,1)S(1)}, u32[]{:S(2)}, u32[]{:S(2)}) %collective-permute-start.1) | collective-permute-done | bytes 524320 | tf_op jit(solution)/shard_map/ppermute | solution.py:27
  37.6 3.9 %attend.7 = (bf16[128,32,128]{2,1,0:T(8,128)(2,1)}, f32[2,384,512]{2,1,0:T(8,128)S(1)}) custom-call(s32[2]{0:T(128)S(1)} %pad_add_fusion.meta_ref, s32[4]{0:T(128)S(1)} %copy-done.3, s32[4,1024]{1,0:T(4,128)S(1)} %copy-done.2, bf16[2,32,4096]{2,1,0:T(8,128)(2,1)S(1)} %collective-permute-done.1.query_ref.grad_ref, ...), custom_call_target="tpu_custom_call", output_to_operand_aliasing={{1}: (6, {}), {0}: (7, {})} | custom-call | flops 37748736 | bytes 294912 | tf_op jit(solution)/shard_map/attend/pallas_call | solution.py:232
  41.6 12.9 %collective-permute-done.8.query_ref.grad_ref = bf16[2,32,2048]{2,1,0:T(8,128)(2,1)S(1)} collective-permute-done((bf16[2,32,2048]{2,1,0:T(8,128)(2,1)S(1)}, bf16[2,32,2048]{2,1,0:T(8,128)(2,1)S(1)}, u32[]{:S(2)}, u32[]{:S(2)}) %collective-permute-start.8) | collective-permute-done | bytes 262176 | tf_op jit(solution)/shard_map/ppermute | solution.py:27
  54.5 2.4 %attend.8 = (bf16[128,32,128]{2,1,0:T(8,128)(2,1)}, f32[2,128,256]{2,1,0:T(8,128)S(1)}, bf16[2,128,256]{2,1,0:T(8,128)(2,1)S(1)}, bf16[2,128,256]{2,1,0:T(8,128)(2,1)S(1)}) custom-call(s32[2]{0:T(128)S(1)} %pad_add_fusion.meta_ref, s32[4]{0:T(128)S(1)} %copy-done.3, s32[4,1024]{1,0:T(4,128)S(1)} %copy-done.2, ...), custom_call_target="tpu_custom_call", output_to_operand_aliasing={{0}: (7, {})} | custom-call | flops 18874368 | bytes 147456 | tf_op jit(solution)/shard_map/attend/pallas_call | solution.py:232
  56.8 1.9 %collective-permute-start.9 = (bf16[2,128,256]{2,1,0:T(8,128)(2,1)S(1)}, bf16[2,128,256]{2,1,0:T(8,128)(2,1)S(1)}, u32[]{:S(2)}, u32[]{:S(2)}) collective-permute-start(bf16[2,128,256]{2,1,0:T(8,128)(2,1)S(1)} %get-tuple-element.62), channel_id=1, source_target_pairs={{4,0},{8,4},{12,8},{16,12},{20,16},{24,20},{28,24},{5,1},{9,5},{13... | collective-permute-start | bytes 393224 | tf_op jit(solution)/shard_map/ppermute | solution.py:33
  58.8 1.9 %collective-permute-start.10 = (bf16[2,128,256]{2,1,0:T(8,128)(2,1)S(1)}, bf16[2,128,256]{2,1,0:T(8,128)(2,1)S(1)}, u32[]{:S(2)}, u32[]{:S(2)}) collective-permute-start(bf16[2,128,256]{2,1,0:T(8,128)(2,1)S(1)} %get-tuple-element.63), channel_id=1, source_target_pairs={{8,0},{12,4},{16,8},{20,12},{24,16},{28,20},{9,1},{13,5},{17,9},{2... | collective-permute-start | bytes 393224 | tf_op jit(solution)/shard_map/ppermute | solution.py:33
  60.7 2.4 %attend.9 = (bf16[128,32,128]{2,1,0:T(8,128)(2,1)}, f32[2,128,256]{2,1,0:T(8,128)S(1)}, bf16[2,128,256]{2,1,0:T(8,128)(2,1)S(1)}, bf16[2,128,256]{2,1,0:T(8,128)(2,1)S(1)}) custom-call(s32[2]{0:T(128)S(1)} %pad_add_fusion.meta_ref, s32[4]{0:T(128)S(1)} %copy-done.3, s32[4,1024]{1,0:T(4,128)S(1)} %copy-done.2, ...), custom_call_target="tpu_custom_call", output_to_operand_aliasing={{0}: (7, {})} | custom-call | flops 18874368 | bytes 147456 | tf_op jit(solution)/shard_map/attend/pallas_call | solution.py:232
  63.4 1.6 %collective-permute-done.10 = bf16[2,128,256]{2,1,0:T(8,128)(2,1)S(1)} collective-permute-done((bf16[2,128,256]{2,1,0:T(8,128)(2,1)S(1)}, bf16[2,128,256]{2,1,0:T(8,128)(2,1)S(1)}, u32[]{:S(2)}, u32[]{:S(2)}) %collective-permute-start.10) | collective-permute-done | bytes 131104 | tf_op jit(solution)/shard_map/ppermute | solution.py:33
  65.1 1.9 %collective-permute-start.11 = (bf16[2,128,256]{2,1,0:T(8,128)(2,1)S(1)}, bf16[2,128,256]{2,1,0:T(8,128)(2,1)S(1)}, u32[]{:S(2)}, u32[]{:S(2)}) collective-permute-start(bf16[2,128,256]{2,1,0:T(8,128)(2,1)S(1)} %get-tuple-element.67), channel_id=1, source_target_pairs={{4,0},{8,4},{12,8},{16,12},{20,16},{24,20},{28,24},{5,1},{9,5},{13... | collective-permute-start | bytes 393224 | tf_op jit(solution)/shard_map/ppermute | solution.py:33
  67.0 1.9 %collective-permute-start.12 = (bf16[2,128,256]{2,1,0:T(8,128)(2,1)S(1)}, bf16[2,128,256]{2,1,0:T(8,128)(2,1)S(1)}, u32[]{:S(2)}, u32[]{:S(2)}) collective-permute-start(bf16[2,128,256]{2,1,0:T(8,128)(2,1)S(1)} %get-tuple-element.68), channel_id=1, source_target_pairs={{8,0},{12,4},{16,8},{20,12},{24,16},{28,20},{9,1},{13,5},{17,9},{2... | collective-permute-start | bytes 393224 | tf_op jit(solution)/shard_map/ppermute | solution.py:33
  69.0 3.4 %collective-permute-done.11 = bf16[2,128,256]{2,1,0:T(8,128)(2,1)S(1)} collective-permute-done((bf16[2,128,256]{2,1,0:T(8,128)(2,1)S(1)}, bf16[2,128,256]{2,1,0:T(8,128)(2,1)S(1)}, u32[]{:S(2)}, u32[]{:S(2)}) %collective-permute-start.11) | collective-permute-done | bytes 131104 | tf_op jit(solution)/shard_map/ppermute | solution.py:33
  72.4 2.0 %collective-permute-done.12 = bf16[2,128,256]{2,1,0:T(8,128)(2,1)S(1)} collective-permute-done((bf16[2,128,256]{2,1,0:T(8,128)(2,1)S(1)}, bf16[2,128,256]{2,1,0:T(8,128)(2,1)S(1)}, u32[]{:S(2)}, u32[]{:S(2)}) %collective-permute-start.12) | collective-permute-done | bytes 131104 | tf_op jit(solution)/shard_map/ppermute | solution.py:33
  (30 shorter events, 3.2 us)
Async XLA Ops:
  3.8 23.2 %copy-start = (bf16[4,32,4096]{2,1,0:T(8,128)(2,1)S(1)}, bf16[4,32,4096]{2,1,0:T(8,128)(2,1)}, u32[]{:S(2)}) copy-start(bf16[4,32,4096]{2,1,0:T(8,128)(2,1)} %query_ref.1) | copy-start | bytes 3145732
  3.8 23.2 %copy-start.1 = (bf16[4,32,4096]{2,1,0:T(8,128)(2,1)S(1)}, bf16[4,32,4096]{2,1,0:T(8,128)(2,1)}, u32[]{:S(2)}) copy-start(bf16[4,32,4096]{2,1,0:T(8,128)(2,1)} %grad_ref.1) | copy-start | bytes 3145732
  3.9 23.2 %copy-start.2 = (s32[4,1024]{1,0:T(4,128)S(1)}, s32[4,1024]{1,0:T(4,128)}, u32[]{:S(2)}) copy-start(s32[4,1024]{1,0:T(4,128)} %segment_ref.9) | copy-start | bytes 49156
  3.9 23.2 %copy-start.3 = (s32[4]{0:T(128)S(1)}, s32[4]{0:T(128)}, u32[]{:S(2)}) copy-start(s32[4]{0:T(128)} %assign_ref.11) | copy-start | bytes 52
  3.9 6.4 %collective-permute-start = (bf16[2,32,512]{2,1,0:T(8,128)(2,1)}, bf16[2,32,512]{2,1,0:T(8,128)(2,1)S(1)}, u32[]{:S(2)}, u32[]{:S(2)}) collective-permute-start(bf16[2,32,512]{2,1,0:T(8,128)(2,1)} %get-tuple-element.40), channel_id=1, source_target_pairs={{0,1},{1,2},{2,3},{3,0},{4,5},{5,6},{6,7},{7,4},{8,9},{9,10},{10,1... | collective-permute-start | bytes 196616 | tf_op jit(solution)/shard_map/ppermute | solution.py:27
  6.1 7.5 %collective-permute-start.2 = (bf16[2,32,512]{2,1,0:T(8,128)(2,1)}, bf16[2,32,512]{2,1,0:T(8,128)(2,1)S(1)}, u32[]{:S(2)}, u32[]{:S(2)}) collective-permute-start(bf16[2,32,512]{2,1,0:T(8,128)(2,1)} %get-tuple-element.45), channel_id=1, source_target_pairs={{0,2},{1,3},{2,0},{3,1},{4,6},{5,7},{6,4},{7,5},{8,10},{9,11},{10,... | collective-permute-start | bytes 196616 | tf_op jit(solution)/shard_map/ppermute | solution.py:27
  8.4 5.2 %collective-permute-start.3 = (bf16[2,32,512]{2,1,0:T(8,128)(2,1)}, bf16[2,32,512]{2,1,0:T(8,128)(2,1)S(1)}, u32[]{:S(2)}, u32[]{:S(2)}) collective-permute-start(bf16[2,32,512]{2,1,0:T(8,128)(2,1)} %get-tuple-element.46), channel_id=1, source_target_pairs={{0,3},{1,0},{2,1},{3,2},{4,7},{5,4},{6,5},{7,6},{8,11},{9,8},{10,9... | collective-permute-start | bytes 196616 | tf_op jit(solution)/shard_map/ppermute | solution.py:27
  10.3 21.3 %collective-permute-start.6 = (bf16[2,32,4096]{2,1,0:T(8,128)(2,1)}, bf16[2,32,4096]{2,1,0:T(8,128)(2,1)S(1)}, u32[]{:S(2)}, u32[]{:S(2)}) collective-permute-start(bf16[2,32,4096]{2,1,0:T(8,128)(2,1)} %get-tuple-element.47), channel_id=1, source_target_pairs={{0,1},{1,2},{2,3},{3,0},{4,5},{5,6},{6,7},{7,4},{8,9},{9,10},{10,1... | collective-permute-start | bytes 1572872 | tf_op jit(solution)/shard_map/ppermute | solution.py:27
  13.6 10.8 %collective-permute-start.5 = (bf16[4,2,32,512]{3,2,1,0:T(8,128)(2,1)S(1)}, bf16[4,2,32,512]{3,2,1,0:T(8,128)(2,1)}, u32[]{:S(2)}, u32[]{:S(2)}) collective-permute-start(bf16[4,2,32,512]{3,2,1,0:T(8,128)(2,1)S(1)} %bitcast_dynamic-update-slice_fusion), channel_id=1, source_target_pairs={{0,4},{4,8},{8,12},{12,16},{16,20},{20,24},{24,28},{1,5},{5,9},{9,... | collective-permute-start | bytes 786440 | tf_op jit(solution)/shard_map/ppermute | solution.py:33
  16.0 9.9 %collective-permute-start.4 = (bf16[4,2,32,512]{3,2,1,0:T(8,128)(2,1)S(1)}, bf16[4,2,32,512]{3,2,1,0:T(8,128)(2,1)}, u32[]{:S(2)}, u32[]{:S(2)}) collective-permute-start(bf16[4,2,32,512]{3,2,1,0:T(8,128)(2,1)S(1)} %bitcast_dynamic-update-slice_fusion), channel_id=1, source_target_pairs={{0,8},{4,12},{8,16},{12,20},{16,24},{20,28},{1,9},{5,13},{9,17},{1... | collective-permute-start | bytes 786440 | tf_op jit(solution)/shard_map/ppermute | solution.py:33
  21.1 16.6 %collective-permute-start.1 = (bf16[2,32,4096]{2,1,0:T(8,128)(2,1)}, bf16[2,32,4096]{2,1,0:T(8,128)(2,1)S(1)}, u32[]{:S(2)}, u32[]{:S(2)}) collective-permute-start(bf16[2,32,4096]{2,1,0:T(8,128)(2,1)} %get-tuple-element.42), channel_id=1, source_target_pairs={{0,3},{1,0},{2,1},{3,2},{4,7},{5,4},{6,5},{7,6},{8,11},{9,8},{10,9... | collective-permute-start | bytes 1572872 | tf_op jit(solution)/shard_map/ppermute | solution.py:27
  27.1 3.9 %copy-start.5 = (bf16[2,32,2048]{2,1,0:T(8,128)(2,1)S(1)}, bf16[2,32,2048]{2,1,0:T(8,128)(2,1)}, u32[]{:S(2)}) copy-start(bf16[2,32,2048]{2,1,0:T(8,128)(2,1)} %get-tuple-element.57) | copy-start | bytes 786436
  31.0 23.5 %collective-permute-start.8 = (bf16[2,32,2048]{2,1,0:T(8,128)(2,1)S(1)}, bf16[2,32,2048]{2,1,0:T(8,128)(2,1)S(1)}, u32[]{:S(2)}, u32[]{:S(2)}) collective-permute-start(bf16[2,32,2048]{2,1,0:T(8,128)(2,1)S(1)} %copy-done.5), channel_id=1, source_target_pairs={{0,2},{1,3},{2,0},{3,1},{4,6},{5,7},{6,4},{7,5},{8,10},{9,11},{10,... | collective-permute-start | bytes 786440 | tf_op jit(solution)/shard_map/ppermute | solution.py:27
  37.6 3.9 %copy-start.4 = (bf16[2,32,2048]{2,1,0:T(8,128)(2,1)S(1)}, bf16[2,32,2048]{2,1,0:T(8,128)(2,1)}, u32[]{:S(2)}) copy-start(bf16[2,32,2048]{2,1,0:T(8,128)(2,1)} %get-tuple-element.55) | copy-start | bytes 786436
  41.6 19.1 %collective-permute-start.7 = (bf16[2,32,2048]{2,1,0:T(8,128)(2,1)S(1)}, bf16[2,32,2048]{2,1,0:T(8,128)(2,1)S(1)}, u32[]{:S(2)}, u32[]{:S(2)}) collective-permute-start(bf16[2,32,2048]{2,1,0:T(8,128)(2,1)S(1)} %copy-done.4), channel_id=1, source_target_pairs={{0,2},{1,3},{2,0},{3,1},{4,6},{5,7},{6,4},{7,5},{8,10},{9,11},{10,... | collective-permute-start | bytes 786440 | tf_op jit(solution)/shard_map/ppermute | solution.py:27
  56.8 6.6 %collective-permute-start.9 = (bf16[2,128,256]{2,1,0:T(8,128)(2,1)S(1)}, bf16[2,128,256]{2,1,0:T(8,128)(2,1)S(1)}, u32[]{:S(2)}, u32[]{:S(2)}) collective-permute-start(bf16[2,128,256]{2,1,0:T(8,128)(2,1)S(1)} %get-tuple-element.62), channel_id=1, source_target_pairs={{4,0},{8,4},{12,8},{16,12},{20,16},{24,20},{28,24},{5,1},{9,5},{13... | collective-permute-start | bytes 393224 | tf_op jit(solution)/shard_map/ppermute | solution.py:33
  58.8 6.3 %collective-permute-start.10 = (bf16[2,128,256]{2,1,0:T(8,128)(2,1)S(1)}, bf16[2,128,256]{2,1,0:T(8,128)(2,1)S(1)}, u32[]{:S(2)}, u32[]{:S(2)}) collective-permute-start(bf16[2,128,256]{2,1,0:T(8,128)(2,1)S(1)} %get-tuple-element.63), channel_id=1, source_target_pairs={{8,0},{12,4},{16,8},{20,12},{24,16},{28,20},{9,1},{13,5},{17,9},{2... | collective-permute-start | bytes 393224 | tf_op jit(solution)/shard_map/ppermute | solution.py:33
  65.1 7.3 %collective-permute-start.11 = (bf16[2,128,256]{2,1,0:T(8,128)(2,1)S(1)}, bf16[2,128,256]{2,1,0:T(8,128)(2,1)S(1)}, u32[]{:S(2)}, u32[]{:S(2)}) collective-permute-start(bf16[2,128,256]{2,1,0:T(8,128)(2,1)S(1)} %get-tuple-element.67), channel_id=1, source_target_pairs={{4,0},{8,4},{12,8},{16,12},{20,16},{24,20},{28,24},{5,1},{9,5},{13... | collective-permute-start | bytes 393224 | tf_op jit(solution)/shard_map/ppermute | solution.py:33
  67.0 7.5 %collective-permute-start.12 = (bf16[2,128,256]{2,1,0:T(8,128)(2,1)S(1)}, bf16[2,128,256]{2,1,0:T(8,128)(2,1)S(1)}, u32[]{:S(2)}, u32[]{:S(2)}) collective-permute-start(bf16[2,128,256]{2,1,0:T(8,128)(2,1)S(1)} %get-tuple-element.68), channel_id=1, source_target_pairs={{8,0},{12,4},{16,8},{20,12},{24,16},{28,20},{9,1},{13,5},{17,9},{2... | collective-permute-start | bytes 393224 | tf_op jit(solution)/shard_map/ppermute | solution.py:33

commit v14 on v13

--- a/solution.py
+++ b/solution.py
@@ -112,9 +112,9 @@
     if filled:
         refs.pop(0)
     query_out_ref = refs.pop(0)
-    column_ref, bias_ref = refs[-2 - last], refs[-1 - last]
+    column_ref, bias_ref, turn_ref = refs[-3 - last : len(refs) - last]
     if last:
-        own_ref, halo_refs, acc_ref = refs[0], refs[1:-3], refs[-1]
+        own_ref, halo_refs, acc_ref = refs[0], refs[1:-4], refs[-1]
     else:
         acc_ref = refs[0]
 
@@ -135,7 +135,6 @@
 
     acc_ref[...] = jnp.zeros_like(acc_ref) if first else acc_in_ref[...]
     turned = (((1,), (1,)), ((), ()))
-    grads = []
     for head in range(HEADS_STEP):
         lanes = slice(head * HD, (head + 1) * HD)
 
@@ -166,7 +165,9 @@
         grad_query = lax.dot_general(
             grad_scores, key, (((0,), (0,)), ((), ())), preferred_element_type=jnp.float32
         )
-        grads.append((grad_query * scale).reshape(ratio, rows, HD))
+        grad_query = (grad_query * scale).reshape(ratio, rows, HD)
+        for r in range(ratio):
+            turn_ref[:, head * ratio + r, :] = grad_query[r]
         acc_ref[0, span, lanes] += grad_key
         acc_ref[1, span, lanes] += grad_value
     if last:
@@ -176,7 +177,7 @@
             part = slice(keys - (back + 1) * tok_dev, keys - back * tok_dev)
             halo_ref[0] = (acc_ref[0, part] * scale).astype(jnp.bfloat16)
             halo_ref[1] = acc_ref[1, part].astype(jnp.bfloat16)
-    query_out_ref[...] = jnp.swapaxes(jnp.concatenate(grads, axis=0), 0, 1).astype(jnp.bfloat16)
+    query_out_ref[...] = turn_ref[...].astype(jnp.bfloat16)
 
 
 def attend(step, base, span, reach, heads, meta, assignment, segments, query, grad, kv, acc, full, last):
@@ -227,7 +228,7 @@
         out_shape.append(jax.ShapeDtypeStruct((2, keys, kv_width), jnp.float32))
         out_specs.append(acc_spec)
     pairs = span * ratio * rows * window
-    held = (keys, ratio * rows), (window, ratio * rows)
+    held = (keys, ratio * rows), (window, ratio * rows), (rows, HEADS_STEP * ratio, HD)
     held += ((2, keys, lanes),) * last
     return pl.pallas_call(
         functools.partial(attend_kernel, step, first, filled, last, tok_dev, reach, ratio),
@@ -241,7 +242,9 @@
         ),
         input_output_aliases=aliases,
         compiler_params=pltpu.CompilerParams(
-            dimension_semantics=("arbitrary",), vmem_limit_bytes=VMEM_BYTES
+            dimension_semantics=("arbitrary",),
+            vmem_limit_bytes=VMEM_BYTES,
+            fuse_transposed_lhs_in_matmul=True,
         ),
         cost_estimate=pl.CostEstimate(
             flops=pairs * HD, bytes_accessed=pairs, transcendentals=0
@@ -300,7 +303,7 @@
             final, half * HEADS_STEP, HEADS_STEP, *fixed, query, grad, kv, acc, full, True
         )
         if half:
-            halos, returned = lax.optimization_barrier((halos, returned))
+            halos, returned[0] = lax.optimization_barrier((halos, returned[0]))
         returned = [shifted(halo, ("blk", "uly"), -back) for back, halo in enumerate(halos, 1)]
         for halo in returned:
             total = total + halo.astype(jnp.float32)

time: 75.5 us -> 74.5 us (0.987)
  waiting for transfers between devices: 26.7 us -> 23.9 us
  starting transfers between devices: 25 us -> 26.2 us
    ppermute x6, waiting for transfers between devices: 8.86 us -> 6.38 us  [shifted(): return lax.ppermute(value, axis, pairs)]
    ppermute x6, starting transfers between devices: 15.1 us -> 16.2 us  [shifted(): return lax.ppermute(value, axis, pairs)]
  transfers between devices with their start and end apart: 13 -> 13, of which waited for: 8 -> 7; matrix products, arithmetic and copies ran while one was open for 3% -> 3% of each run, Pallas kernels for 22% -> 23%
where the time goes in v14:
time: 74.5 us; the launch traced here: 74.1 us
  starting transfers between devices  26.2 us (35%)
  waiting for transfers between devices  23.9 us (32%)
  Pallas kernels  20.3 us (27%)
  other arithmetic  2.01 us (3%)
  local copies, waits for them, and re-layouts  0.93 us (1%)
  between operations  0.82 us (1%)
    ppermute x7, waiting for transfers between devices, exchanged(): lax.ppermute(value, axis, [(i, (i + step) % count) for i in range(count)])  17.5 us
    pallas_call x5, Pallas kernels, attend(): pl.pallas_call(functools.partial(attend_kernel, step, first, filled, last...  17.1 us
    ppermute x6, starting transfers between devices, shifted(): return lax.ppermute(value, axis, pairs)  16.2 us
    ppermute x7, starting transfers between devices, exchanged(): lax.ppermute(value, axis, [(i, (i + step) % count) for i in range(count)])  9.91 us
    ppermute x6, waiting for transfers between devices, shifted(): return lax.ppermute(value, axis, pairs)  6.38 us
    pallas_call x1, Pallas kernels, stage(): pl.pallas_call(functools.partial(stage_kernel, count, jobs, len(jobs)), o...  3.19 us
  transfers between devices with their start and end apart: 13, of which 7 were waited for; matrix products, arithmetic and copies ran while one was open for 3% of the time, Pallas kernels for 23%

profile of v14, /device:TPU:1, one launch (start us, length us, event | category | flops | bytes accessed | tf_op | source)
XLA Modules:
  0.0 74.1 jit_solution(13322539777585049988)
XLA Ops:
  0.6 3.2 %stage.1 = (bf16[2,32,512]{2,1,0:T(8,128)(2,1)}, bf16[2,32,512]{2,1,0:T(8,128)(2,1)}, bf16[2,32,512]{2,1,0:T(8,128)(2,1)}, bf16[2,32,512]{2,1,0:T(8,128)(2,1)}, ...) custom-call(s32[4]{0:T(128)} %assign_ref.11, ...), custom_call_target="tpu_custom_call" | custom-call | tf_op jit(solution)/shard_map/stage/pallas_call | solution.py:62
  3.9 2.2 %collective-permute-start = (bf16[2,32,512]{2,1,0:T(8,128)(2,1)}, bf16[2,32,512]{2,1,0:T(8,128)(2,1)S(1)}, u32[]{:S(2)}, u32[]{:S(2)}) collective-permute-start(bf16[2,32,512]{2,1,0:T(8,128)(2,1)} %get-tuple-element.40), channel_id=1, source_target_pairs={{0,1},{1,2},{2,3},{3,0},{4,5},{5,6},{6,7},{7,4},{8,9},{9,10},{10,1... | collective-permute-start | bytes 196616 | tf_op jit(solution)/shard_map/ppermute | solution.py:27
  6.1 2.3 %collective-permute-start.2 = (bf16[2,32,512]{2,1,0:T(8,128)(2,1)}, bf16[2,32,512]{2,1,0:T(8,128)(2,1)S(1)}, u32[]{:S(2)}, u32[]{:S(2)}) collective-permute-start(bf16[2,32,512]{2,1,0:T(8,128)(2,1)} %get-tuple-element.45), channel_id=1, source_target_pairs={{0,2},{1,3},{2,0},{3,1},{4,6},{5,7},{6,4},{7,5},{8,10},{9,11},{10,... | collective-permute-start | bytes 196616 | tf_op jit(solution)/shard_map/ppermute | solution.py:27
  8.4 1.1 %collective-permute-start.3 = (bf16[2,32,512]{2,1,0:T(8,128)(2,1)}, bf16[2,32,512]{2,1,0:T(8,128)(2,1)S(1)}, u32[]{:S(2)}, u32[]{:S(2)}) collective-permute-start(bf16[2,32,512]{2,1,0:T(8,128)(2,1)} %get-tuple-element.46), channel_id=1, source_target_pairs={{0,3},{1,0},{2,1},{3,2},{4,7},{5,4},{6,5},{7,6},{8,11},{9,8},{10,9... | collective-permute-start | bytes 196616 | tf_op jit(solution)/shard_map/ppermute | solution.py:27
  9.5 0.9 %bitcast_dynamic-update-slice_fusion.3 = bf16[4,2,32,512]{3,2,1,0:T(8,128)(2,1)S(1)} fusion(bf16[4,2,32,512]{3,2,1,0:T(8,128)(2,1)S(1)} %broadcast_in_dim.19, s32[]{:T(128)S(6)} %select_n.13, bf16[2,32,512]{2,1,0:T(8,128)(2,1)} %get-tuple-element.43), kind=kLoop, calls=%fused_computation.10 | loop fusion | bytes 131076 | tf_op jit(solution)/shard_map/jit(dynamic_update_index_in_dim)/dynamic_update_slice | solution.py:282
  10.8 2.8 %collective-permute-done.2 = bf16[2,32,512]{2,1,0:T(8,128)(2,1)S(1)} collective-permute-done((bf16[2,32,512]{2,1,0:T(8,128)(2,1)}, bf16[2,32,512]{2,1,0:T(8,128)(2,1)S(1)}, u32[]{:S(2)}, u32[]{:S(2)}) %collective-permute-start.2) | collective-permute-done | bytes 65568 | tf_op jit(solution)/shard_map/ppermute | solution.py:27
  13.6 2.4 %collective-permute-start.5 = (bf16[4,2,32,512]{3,2,1,0:T(8,128)(2,1)S(1)}, bf16[4,2,32,512]{3,2,1,0:T(8,128)(2,1)}, u32[]{:S(2)}, u32[]{:S(2)}) collective-permute-start(bf16[4,2,32,512]{3,2,1,0:T(8,128)(2,1)S(1)} %bitcast_dynamic-update-slice_fusion), channel_id=1, source_target_pairs={{0,4},{4,8},{8,12},{12,16},{16,20},{20,24},{24,28},{1,5},{5,9},{9,... | collective-permute-start | bytes 786440 | tf_op jit(solution)/shard_map/ppermute | solution.py:33
  16.0 5.0 %collective-permute-start.4 = (bf16[4,2,32,512]{3,2,1,0:T(8,128)(2,1)S(1)}, bf16[4,2,32,512]{3,2,1,0:T(8,128)(2,1)}, u32[]{:S(2)}, u32[]{:S(2)}) collective-permute-start(bf16[4,2,32,512]{3,2,1,0:T(8,128)(2,1)S(1)} %bitcast_dynamic-update-slice_fusion), channel_id=1, source_target_pairs={{0,8},{4,12},{8,16},{12,20},{16,24},{20,28},{1,9},{5,13},{9,17},{1... | collective-permute-start | bytes 786440 | tf_op jit(solution)/shard_map/ppermute | solution.py:33
  21.1 3.3 %collective-permute-start.1 = (bf16[2,32,4096]{2,1,0:T(8,128)(2,1)}, bf16[2,32,4096]{2,1,0:T(8,128)(2,1)S(1)}, u32[]{:S(2)}, u32[]{:S(2)}) collective-permute-start(bf16[2,32,4096]{2,1,0:T(8,128)(2,1)} %get-tuple-element.42), channel_id=1, source_target_pairs={{0,3},{1,0},{2,1},{3,2},{4,7},{5,4},{6,5},{7,6},{8,11},{9,8},{10,9... | collective-permute-start | bytes 1572872 | tf_op jit(solution)/shard_map/ppermute | solution.py:27
  24.5 1.4 %collective-permute-done.4 = bf16[4,2,32,512]{3,2,1,0:T(8,128)(2,1)} collective-permute-done((bf16[4,2,32,512]{3,2,1,0:T(8,128)(2,1)S(1)}, bf16[4,2,32,512]{3,2,1,0:T(8,128)(2,1)}, u32[]{:S(2)}, u32[]{:S(2)}) %collective-permute-start.4) | collective-permute-done | bytes 262176 | tf_op jit(solution)/shard_map/ppermute | solution.py:33
  25.9 1.1 %pad_maximum_fusion.kv_ref = bf16[12,2,32,512]{3,2,1,0:T(8,128)(2,1)S(1)} fusion(bf16[4,2,32,512]{3,2,1,0:T(8,128)(2,1)S(1)} %bitcast_dynamic-update-slice_fusion, bf16[4,2,32,512]{3,2,1,0:T(8,128)(2,1)} %collective-permute-done.5, bf16[4,2,32,512]{3,2,1,0:T(8,128)(2,1)} %collective-permute-done.4), kind=kLoop, calls=%fused_computation | loop fusion | flops 786432 | bytes 1572864 | tf_op jit(solution)/shard_map/concatenate | solution.py:286
  27.1 4.0 %attend.5 = (bf16[128,32,128]{2,1,0:T(8,128)(2,1)}, f32[2,384,512]{2,1,0:T(8,128)S(1)}) custom-call(s32[2]{0:T(128)S(1)} %pad_add_fusion.meta_ref, s32[4]{0:T(128)S(1)} %copy-done.3, s32[4,1024]{1,0:T(4,128)S(1)} %copy-done.2, bf16[4,32,4096]{2,1,0:T(8,128)(2,1)S(1)} %copy-done, bf16[4,32,4096]{2,1,0:T(8,128)(2,1)S(1)} %copy-done.1, ...), custom_call_target="tpu_custom_call" | custom-call | flops 37748736 | bytes 294912 | tf_op jit(solution)/shard_map/attend/pallas_call | solution.py:233
  31.7 4.1 %attend.6 = (bf16[128,32,128]{2,1,0:T(8,128)(2,1)}, f32[2,384,512]{2,1,0:T(8,128)S(1)}) custom-call(s32[2]{0:T(128)S(1)} %pad_add_fusion.meta_ref, s32[4]{0:T(128)S(1)} %copy-done.3, s32[4,1024]{1,0:T(4,128)S(1)} %copy-done.2, bf16[2,32,4096]{2,1,0:T(8,128)(2,1)S(1)} %collective-permute-done.6.query_ref.grad_ref, ...), custom_call_target="tpu_custom_call", output_to_operand_aliasing={{1}: (6, {}), {0}: (7, {})} | custom-call | flops 37748736 | bytes 294912 | tf_op jit(solution)/shard_map/attend/pallas_call | solution.py:233
  35.7 1.9 %collective-permute-done.1.query_ref.grad_ref = bf16[2,32,4096]{2,1,0:T(8,128)(2,1)S(1)} collective-permute-done((bf16[2,32,4096]{2,1,0:T(8,128)(2,1)}, bf16[2,32,4096]{2,1,0:T(8,128)(2,1)S(1)}, u32[]{:S(2)}, u32[]{:S(2)}) %collective-permute-start.1) | collective-permute-done | bytes 524320 | tf_op jit(solution)/shard_map/ppermute | solution.py:27
  37.6 4.0 %attend.7 = (bf16[128,32,128]{2,1,0:T(8,128)(2,1)}, f32[2,384,512]{2,1,0:T(8,128)S(1)}) custom-call(s32[2]{0:T(128)S(1)} %pad_add_fusion.meta_ref, s32[4]{0:T(128)S(1)} %copy-done.3, s32[4,1024]{1,0:T(4,128)S(1)} %copy-done.2, bf16[2,32,4096]{2,1,0:T(8,128)(2,1)S(1)} %collective-permute-done.1.query_ref.grad_ref, ...), custom_call_target="tpu_custom_call", output_to_operand_aliasing={{1}: (6, {}), {0}: (7, {})} | custom-call | flops 37748736 | bytes 294912 | tf_op jit(solution)/shard_map/attend/pallas_call | solution.py:233
  41.7 12.8 %collective-permute-done.8.query_ref.grad_ref = bf16[2,32,2048]{2,1,0:T(8,128)(2,1)S(1)} collective-permute-done((bf16[2,32,2048]{2,1,0:T(8,128)(2,1)S(1)}, bf16[2,32,2048]{2,1,0:T(8,128)(2,1)S(1)}, u32[]{:S(2)}, u32[]{:S(2)}) %collective-permute-start.8) | collective-permute-done | bytes 262176 | tf_op jit(solution)/shard_map/ppermute | solution.py:27
  54.5 2.5 %attend.8 = (bf16[128,32,128]{2,1,0:T(8,128)(2,1)}, f32[2,128,256]{2,1,0:T(8,128)S(1)}, bf16[2,128,256]{2,1,0:T(8,128)(2,1)S(1)}, bf16[2,128,256]{2,1,0:T(8,128)(2,1)S(1)}) custom-call(s32[2]{0:T(128)S(1)} %pad_add_fusion.meta_ref, s32[4]{0:T(128)S(1)} %copy-done.3, s32[4,1024]{1,0:T(4,128)S(1)} %copy-done.2, ...), custom_call_target="tpu_custom_call", output_to_operand_aliasing={{0}: (7, {})} | custom-call | flops 18874368 | bytes 147456 | tf_op jit(solution)/shard_map/attend/pallas_call | solution.py:233
  57.0 1.9 %collective-permute-start.9 = (bf16[2,128,256]{2,1,0:T(8,128)(2,1)S(1)}, bf16[2,128,256]{2,1,0:T(8,128)(2,1)S(1)}, u32[]{:S(2)}, u32[]{:S(2)}) collective-permute-start(bf16[2,128,256]{2,1,0:T(8,128)(2,1)S(1)} %get-tuple-element.62), channel_id=1, source_target_pairs={{4,0},{8,4},{12,8},{16,12},{20,16},{24,20},{28,24},{5,1},{9,5},{13... | collective-permute-start | bytes 393224 | tf_op jit(solution)/shard_map/ppermute | solution.py:33
  58.9 1.9 %collective-permute-start.10 = (bf16[2,128,256]{2,1,0:T(8,128)(2,1)S(1)}, bf16[2,128,256]{2,1,0:T(8,128)(2,1)S(1)}, u32[]{:S(2)}, u32[]{:S(2)}) collective-permute-start(bf16[2,128,256]{2,1,0:T(8,128)(2,1)S(1)} %get-tuple-element.63), channel_id=1, source_target_pairs={{8,0},{12,4},{16,8},{20,12},{24,16},{28,20},{9,1},{13,5},{17,9},{2... | collective-permute-start | bytes 393224 | tf_op jit(solution)/shard_map/ppermute | solution.py:33
  60.8 2.5 %attend.9 = (bf16[128,32,128]{2,1,0:T(8,128)(2,1)}, f32[2,128,256]{2,1,0:T(8,128)S(1)}, bf16[2,128,256]{2,1,0:T(8,128)(2,1)S(1)}, bf16[2,128,256]{2,1,0:T(8,128)(2,1)S(1)}) custom-call(s32[2]{0:T(128)S(1)} %pad_add_fusion.meta_ref, s32[4]{0:T(128)S(1)} %copy-done.3, s32[4,1024]{1,0:T(4,128)S(1)} %copy-done.2, ...), custom_call_target="tpu_custom_call", output_to_operand_aliasing={{0}: (7, {})} | custom-call | flops 18874368 | bytes 147456 | tf_op jit(solution)/shard_map/attend/pallas_call | solution.py:233
  63.5 3.1 %collective-permute-start.11 = (bf16[2,128,256]{2,1,0:T(8,128)(2,1)S(1)}, bf16[2,128,256]{2,1,0:T(8,128)(2,1)S(1)}, u32[]{:S(2)}, u32[]{:S(2)}) collective-permute-start(bf16[2,128,256]{2,1,0:T(8,128)(2,1)S(1)} %get-tuple-element.67), channel_id=1, source_target_pairs={{4,0},{8,4},{12,8},{16,12},{20,16},{24,20},{28,24},{5,1},{9,5},{13... | collective-permute-start | bytes 393224 | tf_op jit(solution)/shard_map/ppermute | solution.py:33
  66.6 1.9 %collective-permute-start.12 = (bf16[2,128,256]{2,1,0:T(8,128)(2,1)S(1)}, bf16[2,128,256]{2,1,0:T(8,128)(2,1)S(1)}, u32[]{:S(2)}, u32[]{:S(2)}) collective-permute-start(bf16[2,128,256]{2,1,0:T(8,128)(2,1)S(1)} %get-tuple-element.68), channel_id=1, source_target_pairs={{8,0},{12,4},{16,8},{20,12},{24,16},{28,20},{9,1},{13,5},{17,9},{2... | collective-permute-start | bytes 393224 | tf_op jit(solution)/shard_map/ppermute | solution.py:33
  68.6 1.5 %collective-permute-done.11 = bf16[2,128,256]{2,1,0:T(8,128)(2,1)S(1)} collective-permute-done((bf16[2,128,256]{2,1,0:T(8,128)(2,1)S(1)}, bf16[2,128,256]{2,1,0:T(8,128)(2,1)S(1)}, u32[]{:S(2)}, u32[]{:S(2)}) %collective-permute-start.11) | collective-permute-done | bytes 131104 | tf_op jit(solution)/shard_map/ppermute | solution.py:33
  70.1 3.2 %collective-permute-done.12 = bf16[2,128,256]{2,1,0:T(8,128)(2,1)S(1)} collective-permute-done((bf16[2,128,256]{2,1,0:T(8,128)(2,1)S(1)}, bf16[2,128,256]{2,1,0:T(8,128)(2,1)S(1)}, u32[]{:S(2)}, u32[]{:S(2)}) %collective-permute-start.12) | collective-permute-done | bytes 131104 | tf_op jit(solution)/shard_map/ppermute | solution.py:33
  (30 shorter events, 2.2 us)
Async XLA Ops:
  3.8 23.2 %copy-start = (bf16[4,32,4096]{2,1,0:T(8,128)(2,1)S(1)}, bf16[4,32,4096]{2,1,0:T(8,128)(2,1)}, u32[]{:S(2)}) copy-start(bf16[4,32,4096]{2,1,0:T(8,128)(2,1)} %query_ref.1) | copy-start | bytes 3145732
  3.8 23.2 %copy-start.1 = (bf16[4,32,4096]{2,1,0:T(8,128)(2,1)S(1)}, bf16[4,32,4096]{2,1,0:T(8,128)(2,1)}, u32[]{:S(2)}) copy-start(bf16[4,32,4096]{2,1,0:T(8,128)(2,1)} %grad_ref.1) | copy-start | bytes 3145732
  3.9 23.2 %copy-start.2 = (s32[4,1024]{1,0:T(4,128)S(1)}, s32[4,1024]{1,0:T(4,128)}, u32[]{:S(2)}) copy-start(s32[4,1024]{1,0:T(4,128)} %segment_ref.9) | copy-start | bytes 49156
  3.9 23.2 %copy-start.3 = (s32[4]{0:T(128)S(1)}, s32[4]{0:T(128)}, u32[]{:S(2)}) copy-start(s32[4]{0:T(128)} %assign_ref.11) | copy-start | bytes 52
  3.9 6.4 %collective-permute-start = (bf16[2,32,512]{2,1,0:T(8,128)(2,1)}, bf16[2,32,512]{2,1,0:T(8,128)(2,1)S(1)}, u32[]{:S(2)}, u32[]{:S(2)}) collective-permute-start(bf16[2,32,512]{2,1,0:T(8,128)(2,1)} %get-tuple-element.40), channel_id=1, source_target_pairs={{0,1},{1,2},{2,3},{3,0},{4,5},{5,6},{6,7},{7,4},{8,9},{9,10},{10,1... | collective-permute-start | bytes 196616 | tf_op jit(solution)/shard_map/ppermute | solution.py:27
  6.1 7.5 %collective-permute-start.2 = (bf16[2,32,512]{2,1,0:T(8,128)(2,1)}, bf16[2,32,512]{2,1,0:T(8,128)(2,1)S(1)}, u32[]{:S(2)}, u32[]{:S(2)}) collective-permute-start(bf16[2,32,512]{2,1,0:T(8,128)(2,1)} %get-tuple-element.45), channel_id=1, source_target_pairs={{0,2},{1,3},{2,0},{3,1},{4,6},{5,7},{6,4},{7,5},{8,10},{9,11},{10,... | collective-permute-start | bytes 196616 | tf_op jit(solution)/shard_map/ppermute | solution.py:27
  8.4 5.2 %collective-permute-start.3 = (bf16[2,32,512]{2,1,0:T(8,128)(2,1)}, bf16[2,32,512]{2,1,0:T(8,128)(2,1)S(1)}, u32[]{:S(2)}, u32[]{:S(2)}) collective-permute-start(bf16[2,32,512]{2,1,0:T(8,128)(2,1)} %get-tuple-element.46), channel_id=1, source_target_pairs={{0,3},{1,0},{2,1},{3,2},{4,7},{5,4},{6,5},{7,6},{8,11},{9,8},{10,9... | collective-permute-start | bytes 196616 | tf_op jit(solution)/shard_map/ppermute | solution.py:27
  10.3 21.4 %collective-permute-start.6 = (bf16[2,32,4096]{2,1,0:T(8,128)(2,1)}, bf16[2,32,4096]{2,1,0:T(8,128)(2,1)S(1)}, u32[]{:S(2)}, u32[]{:S(2)}) collective-permute-start(bf16[2,32,4096]{2,1,0:T(8,128)(2,1)} %get-tuple-element.47), channel_id=1, source_target_pairs={{0,1},{1,2},{2,3},{3,0},{4,5},{5,6},{6,7},{7,4},{8,9},{9,10},{10,1... | collective-permute-start | bytes 1572872 | tf_op jit(solution)/shard_map/ppermute | solution.py:27
  13.6 10.8 %collective-permute-start.5 = (bf16[4,2,32,512]{3,2,1,0:T(8,128)(2,1)S(1)}, bf16[4,2,32,512]{3,2,1,0:T(8,128)(2,1)}, u32[]{:S(2)}, u32[]{:S(2)}) collective-permute-start(bf16[4,2,32,512]{3,2,1,0:T(8,128)(2,1)S(1)} %bitcast_dynamic-update-slice_fusion), channel_id=1, source_target_pairs={{0,4},{4,8},{8,12},{12,16},{16,20},{20,24},{24,28},{1,5},{5,9},{9,... | collective-permute-start | bytes 786440 | tf_op jit(solution)/shard_map/ppermute | solution.py:33
  16.0 9.9 %collective-permute-start.4 = (bf16[4,2,32,512]{3,2,1,0:T(8,128)(2,1)S(1)}, bf16[4,2,32,512]{3,2,1,0:T(8,128)(2,1)}, u32[]{:S(2)}, u32[]{:S(2)}) collective-permute-start(bf16[4,2,32,512]{3,2,1,0:T(8,128)(2,1)S(1)} %bitcast_dynamic-update-slice_fusion), channel_id=1, source_target_pairs={{0,8},{4,12},{8,16},{12,20},{16,24},{20,28},{1,9},{5,13},{9,17},{1... | collective-permute-start | bytes 786440 | tf_op jit(solution)/shard_map/ppermute | solution.py:33
  21.1 16.6 %collective-permute-start.1 = (bf16[2,32,4096]{2,1,0:T(8,128)(2,1)}, bf16[2,32,4096]{2,1,0:T(8,128)(2,1)S(1)}, u32[]{:S(2)}, u32[]{:S(2)}) collective-permute-start(bf16[2,32,4096]{2,1,0:T(8,128)(2,1)} %get-tuple-element.42), channel_id=1, source_target_pairs={{0,3},{1,0},{2,1},{3,2},{4,7},{5,4},{6,5},{7,6},{8,11},{9,8},{10,9... | collective-permute-start | bytes 1572872 | tf_op jit(solution)/shard_map/ppermute | solution.py:27
  27.1 4.1 %copy-start.5 = (bf16[2,32,2048]{2,1,0:T(8,128)(2,1)S(1)}, bf16[2,32,2048]{2,1,0:T(8,128)(2,1)}, u32[]{:S(2)}) copy-start(bf16[2,32,2048]{2,1,0:T(8,128)(2,1)} %get-tuple-element.57) | copy-start | bytes 786436
  31.1 23.4 %collective-permute-start.8 = (bf16[2,32,2048]{2,1,0:T(8,128)(2,1)S(1)}, bf16[2,32,2048]{2,1,0:T(8,128)(2,1)S(1)}, u32[]{:S(2)}, u32[]{:S(2)}) collective-permute-start(bf16[2,32,2048]{2,1,0:T(8,128)(2,1)S(1)} %copy-done.5), channel_id=1, source_target_pairs={{0,2},{1,3},{2,0},{3,1},{4,6},{5,7},{6,4},{7,5},{8,10},{9,11},{10,... | collective-permute-start | bytes 786440 | tf_op jit(solution)/shard_map/ppermute | solution.py:27
  37.6 4.1 %copy-start.4 = (bf16[2,32,2048]{2,1,0:T(8,128)(2,1)S(1)}, bf16[2,32,2048]{2,1,0:T(8,128)(2,1)}, u32[]{:S(2)}) copy-start(bf16[2,32,2048]{2,1,0:T(8,128)(2,1)} %get-tuple-element.55) | copy-start | bytes 786436
  41.7 19.1 %collective-permute-start.7 = (bf16[2,32,2048]{2,1,0:T(8,128)(2,1)S(1)}, bf16[2,32,2048]{2,1,0:T(8,128)(2,1)S(1)}, u32[]{:S(2)}, u32[]{:S(2)}) collective-permute-start(bf16[2,32,2048]{2,1,0:T(8,128)(2,1)S(1)} %copy-done.4), channel_id=1, source_target_pairs={{0,2},{1,3},{2,0},{3,1},{4,6},{5,7},{6,4},{7,5},{8,10},{9,11},{10,... | collective-permute-start | bytes 786440 | tf_op jit(solution)/shard_map/ppermute | solution.py:27
  57.0 6.6 %collective-permute-start.9 = (bf16[2,128,256]{2,1,0:T(8,128)(2,1)S(1)}, bf16[2,128,256]{2,1,0:T(8,128)(2,1)S(1)}, u32[]{:S(2)}, u32[]{:S(2)}) collective-permute-start(bf16[2,128,256]{2,1,0:T(8,128)(2,1)S(1)} %get-tuple-element.62), channel_id=1, source_target_pairs={{4,0},{8,4},{12,8},{16,12},{20,16},{24,20},{28,24},{5,1},{9,5},{13... | collective-permute-start | bytes 393224 | tf_op jit(solution)/shard_map/ppermute | solution.py:33
  58.9 9.7 %collective-permute-start.10 = (bf16[2,128,256]{2,1,0:T(8,128)(2,1)S(1)}, bf16[2,128,256]{2,1,0:T(8,128)(2,1)S(1)}, u32[]{:S(2)}, u32[]{:S(2)}) collective-permute-start(bf16[2,128,256]{2,1,0:T(8,128)(2,1)S(1)} %get-tuple-element.63), channel_id=1, source_target_pairs={{8,0},{12,4},{16,8},{20,12},{24,16},{28,20},{9,1},{13,5},{17,9},{2... | collective-permute-start | bytes 393224 | tf_op jit(solution)/shard_map/ppermute | solution.py:33
  63.5 6.6 %collective-permute-start.11 = (bf16[2,128,256]{2,1,0:T(8,128)(2,1)S(1)}, bf16[2,128,256]{2,1,0:T(8,128)(2,1)S(1)}, u32[]{:S(2)}, u32[]{:S(2)}) collective-permute-start(bf16[2,128,256]{2,1,0:T(8,128)(2,1)S(1)} %get-tuple-element.67), channel_id=1, source_target_pairs={{4,0},{8,4},{12,8},{16,12},{20,16},{24,20},{28,24},{5,1},{9,5},{13... | collective-permute-start | bytes 393224 | tf_op jit(solution)/shard_map/ppermute | solution.py:33
  66.6 6.7 %collective-permute-start.12 = (bf16[2,128,256]{2,1,0:T(8,128)(2,1)S(1)}, bf16[2,128,256]{2,1,0:T(8,128)(2,1)S(1)}, u32[]{:S(2)}, u32[]{:S(2)}) collective-permute-start(bf16[2,128,256]{2,1,0:T(8,128)(2,1)S(1)} %get-tuple-element.68), channel_id=1, source_target_pairs={{8,0},{12,4},{16,8},{20,12},{24,16},{28,20},{9,1},{13,5},{17,9},{2... | collective-permute-start | bytes 393224 | tf_op jit(solution)/shard_map/ppermute | solution.py:33

commit v15 on v13

--- a/solution.py
+++ b/solution.py
@@ -12,6 +12,7 @@
 BIG_NEGATIVE = -1e30
 VMEM_BYTES = 32 * 1024 * 1024
 HEADS_STEP = 2
+CALL_COST = 30
 
 
 def target_of(index, step, count):
@@ -227,6 +228,7 @@
         out_shape.append(jax.ShapeDtypeStruct((2, keys, kv_width), jnp.float32))
         out_specs.append(acc_spec)
     pairs = span * ratio * rows * window
+    cost = CALL_COST if step and not last else 1
     held = (keys, ratio * rows), (window, ratio * rows)
     held += ((2, keys, lanes),) * last
     return pl.pallas_call(
@@ -244,7 +246,7 @@
             dimension_semantics=("arbitrary",), vmem_limit_bytes=VMEM_BYTES
         ),
         cost_estimate=pl.CostEstimate(
-            flops=pairs * HD, bytes_accessed=pairs, transcendentals=0
+            flops=pairs * HD * cost, bytes_accessed=pairs * cost, transcendentals=0
         ),
         name="attend",
     )(*operands)
@@ -291,7 +293,7 @@
         query, grad = (both, lambda m, a: 0), (both, lambda m, a: 1)
         full, acc = attend(step, 0, kv_heads, *fixed, query, grad, kv, acc, full, False)
     for rows in held[1:]:
-        rows, acc = lax.optimization_barrier((rows, acc))
+        rows, split[-1], acc = lax.optimization_barrier((rows, split[-1], acc))
         split.append(exchanged(rows, "dp", final))
     totals, returned = [], []
     for half, both in enumerate(split):
@@ -300,7 +302,7 @@
             final, half * HEADS_STEP, HEADS_STEP, *fixed, query, grad, kv, acc, full, True
         )
         if half:
-            halos, returned = lax.optimization_barrier((halos, returned))
+            halos, returned[0] = lax.optimization_barrier((halos, returned[0]))
         returned = [shifted(halo, ("blk", "uly"), -back) for back, halo in enumerate(halos, 1)]
         for halo in returned:
             total = total + halo.astype(jnp.float32)

time: 75.5 us -> 75.9 us (level)
  starting transfers between devices: 25 us -> 31 us
  waiting for transfers between devices: 26.7 us -> 21.1 us
    ppermute x6, starting transfers between devices: 15.1 us -> 21.1 us  [shifted(): return lax.ppermute(value, axis, pairs)]
    ppermute x6, waiting for transfers between devices: 8.86 us -> 5.72 us  [shifted(): return lax.ppermute(value, axis, pairs)]
    ppermute x7, waiting for transfers between devices: 17.9 us -> 15.4 us  [exchanged(): lax.ppermute(value, axis, [(i, (i + step) % count) for i in range(count)])]
  transfers between devices with their start and end apart: 13 -> 13, of which waited for: 8 -> 7; matrix products, arithmetic and copies ran while one was open for 3% -> 3% of each run, Pallas kernels for 22% -> 22%
where the time goes in v15:
time: 75.9 us; the launch traced here: 75.6 us
  starting transfers between devices  31 us (41%)
  waiting for transfers between devices  21.1 us (28%)
  Pallas kernels  19.7 us (26%)
  other arithmetic  2.01 us (3%)
  local copies, waits for them, and re-layouts  0.93 us (1%)
  between operations  0.82 us (1%)
    ppermute x6, starting transfers between devices, shifted(): return lax.ppermute(value, axis, pairs)  21.1 us
    pallas_call x5, Pallas kernels, attend(): pl.pallas_call(functools.partial(attend_kernel, step, first, filled, last...  16.6 us
    ppermute x7, waiting for transfers between devices, exchanged(): lax.ppermute(value, axis, [(i, (i + step) % count) for i in range(count)])  15.4 us
    ppermute x7, starting transfers between devices, exchanged(): lax.ppermute(value, axis, [(i, (i + step) % count) for i in range(count)])  9.91 us
    ppermute x6, waiting for transfers between devices, shifted(): return lax.ppermute(value, axis, pairs)  5.72 us
    pallas_call x1, Pallas kernels, stage(): pl.pallas_call(functools.partial(stage_kernel, count, jobs, len(jobs)), o...  3.19 us
  transfers between devices with their start and end apart: 13, of which 7 were waited for; matrix products, arithmetic and copies ran while one was open for 3% of the time, Pallas kernels for 22%

profile of v15, /device:TPU:1, one launch (start us, length us, event | category | flops | bytes accessed | tf_op | source)
XLA Modules:
  0.0 75.6 jit_solution(6832066734814061811)
XLA Ops:
  0.6 3.2 %stage.1 = (bf16[2,32,512]{2,1,0:T(8,128)(2,1)}, bf16[2,32,512]{2,1,0:T(8,128)(2,1)}, bf16[2,32,512]{2,1,0:T(8,128)(2,1)}, bf16[2,32,512]{2,1,0:T(8,128)(2,1)}, ...) custom-call(s32[4]{0:T(128)} %assign_ref.11, ...), custom_call_target="tpu_custom_call" | custom-call | tf_op jit(solution)/shard_map/stage/pallas_call | solution.py:63
  3.9 2.2 %collective-permute-start = (bf16[2,32,512]{2,1,0:T(8,128)(2,1)}, bf16[2,32,512]{2,1,0:T(8,128)(2,1)S(1)}, u32[]{:S(2)}, u32[]{:S(2)}) collective-permute-start(bf16[2,32,512]{2,1,0:T(8,128)(2,1)} %get-tuple-element.41), channel_id=1, source_target_pairs={{0,1},{1,2},{2,3},{3,0},{4,5},{5,6},{6,7},{7,4},{8,9},{9,10},{10,1... | collective-permute-start | bytes 196616 | tf_op jit(solution)/shard_map/ppermute | solution.py:28
  6.1 2.3 %collective-permute-start.1 = (bf16[2,32,512]{2,1,0:T(8,128)(2,1)}, bf16[2,32,512]{2,1,0:T(8,128)(2,1)S(1)}, u32[]{:S(2)}, u32[]{:S(2)}) collective-permute-start(bf16[2,32,512]{2,1,0:T(8,128)(2,1)} %get-tuple-element.46), channel_id=1, source_target_pairs={{0,2},{1,3},{2,0},{3,1},{4,6},{5,7},{6,4},{7,5},{8,10},{9,11},{10,... | collective-permute-start | bytes 196616 | tf_op jit(solution)/shard_map/ppermute | solution.py:28
  8.4 1.1 %collective-permute-start.2 = (bf16[2,32,512]{2,1,0:T(8,128)(2,1)}, bf16[2,32,512]{2,1,0:T(8,128)(2,1)S(1)}, u32[]{:S(2)}, u32[]{:S(2)}) collective-permute-start(bf16[2,32,512]{2,1,0:T(8,128)(2,1)} %get-tuple-element.47), channel_id=1, source_target_pairs={{0,3},{1,0},{2,1},{3,2},{4,7},{5,4},{6,5},{7,6},{8,11},{9,8},{10,9... | collective-permute-start | bytes 196616 | tf_op jit(solution)/shard_map/ppermute | solution.py:28
  10.8 2.8 %collective-permute-done.1 = bf16[2,32,512]{2,1,0:T(8,128)(2,1)S(1)} collective-permute-done((bf16[2,32,512]{2,1,0:T(8,128)(2,1)}, bf16[2,32,512]{2,1,0:T(8,128)(2,1)S(1)}, u32[]{:S(2)}, u32[]{:S(2)}) %collective-permute-start.1) | collective-permute-done | bytes 65568 | tf_op jit(solution)/shard_map/ppermute | solution.py:28
  13.6 2.4 %collective-permute-start.4 = (bf16[4,2,32,512]{3,2,1,0:T(8,128)(2,1)S(1)}, bf16[4,2,32,512]{3,2,1,0:T(8,128)(2,1)}, u32[]{:S(2)}, u32[]{:S(2)}) collective-permute-start(bf16[4,2,32,512]{3,2,1,0:T(8,128)(2,1)S(1)} %bitcast_dynamic-update-slice_fusion), channel_id=1, source_target_pairs={{0,4},{4,8},{8,12},{12,16},{16,20},{20,24},{24,28},{1,5},{5,9},{9,... | collective-permute-start | bytes 786440 | tf_op jit(solution)/shard_map/ppermute | solution.py:34
  16.0 5.0 %collective-permute-start.3 = (bf16[4,2,32,512]{3,2,1,0:T(8,128)(2,1)S(1)}, bf16[4,2,32,512]{3,2,1,0:T(8,128)(2,1)}, u32[]{:S(2)}, u32[]{:S(2)}) collective-permute-start(bf16[4,2,32,512]{3,2,1,0:T(8,128)(2,1)S(1)} %bitcast_dynamic-update-slice_fusion), channel_id=1, source_target_pairs={{0,8},{4,12},{8,16},{12,20},{16,24},{20,28},{1,9},{5,13},{9,17},{1... | collective-permute-start | bytes 786440 | tf_op jit(solution)/shard_map/ppermute | solution.py:34
  21.1 3.3 %collective-permute-start.6 = (bf16[2,32,4096]{2,1,0:T(8,128)(2,1)}, bf16[2,32,4096]{2,1,0:T(8,128)(2,1)S(1)}, u32[]{:S(2)}, u32[]{:S(2)}) collective-permute-start(bf16[2,32,4096]{2,1,0:T(8,128)(2,1)} %get-tuple-element.50), channel_id=1, source_target_pairs={{0,3},{1,0},{2,1},{3,2},{4,7},{5,4},{6,5},{7,6},{8,11},{9,8},{10,9... | collective-permute-start | bytes 1572872 | tf_op jit(solution)/shard_map/ppermute | solution.py:28
  24.5 1.4 %collective-permute-done.3 = bf16[4,2,32,512]{3,2,1,0:T(8,128)(2,1)} collective-permute-done((bf16[4,2,32,512]{3,2,1,0:T(8,128)(2,1)S(1)}, bf16[4,2,32,512]{3,2,1,0:T(8,128)(2,1)}, u32[]{:S(2)}, u32[]{:S(2)}) %collective-permute-start.3) | collective-permute-done | bytes 262176 | tf_op jit(solution)/shard_map/ppermute | solution.py:34
  25.9 1.1 %pad_maximum_fusion.kv_ref = bf16[12,2,32,512]{3,2,1,0:T(8,128)(2,1)S(1)} fusion(bf16[4,2,32,512]{3,2,1,0:T(8,128)(2,1)S(1)} %bitcast_dynamic-update-slice_fusion, bf16[4,2,32,512]{3,2,1,0:T(8,128)(2,1)} %collective-permute-done.4, bf16[4,2,32,512]{3,2,1,0:T(8,128)(2,1)} %collective-permute-done.3), kind=kLoop, calls=%fused_computation | loop fusion | flops 786432 | bytes 1572864 | tf_op jit(solution)/shard_map/concatenate | solution.py:285
  27.1 3.9 %attend.5 = (bf16[128,32,128]{2,1,0:T(8,128)(2,1)}, f32[2,384,512]{2,1,0:T(8,128)S(1)}) custom-call(s32[2]{0:T(128)S(1)} %pad_add_fusion.meta_ref, s32[4]{0:T(128)S(1)} %copy-done.3, s32[4,1024]{1,0:T(4,128)S(1)} %copy-done.2, bf16[4,32,4096]{2,1,0:T(8,128)(2,1)S(1)} %copy-done, bf16[4,32,4096]{2,1,0:T(8,128)(2,1)S(1)} %copy-done.1, ...), custom_call_target="tpu_custom_call" | custom-call | flops 37748736 | bytes 294912 | tf_op jit(solution)/shard_map/attend/pallas_call | solution.py:234
  31.6 3.9 %attend.6 = (bf16[128,32,128]{2,1,0:T(8,128)(2,1)}, f32[2,384,512]{2,1,0:T(8,128)S(1)}) custom-call(s32[2]{0:T(128)S(1)} %pad_add_fusion.meta_ref, s32[4]{0:T(128)S(1)} %copy-done.3, s32[4,1024]{1,0:T(4,128)S(1)} %copy-done.2, bf16[2,32,4096]{2,1,0:T(8,128)(2,1)S(1)} %collective-permute-done.7.query_ref.grad_ref, ...), custom_call_target="tpu_custom_call", output_to_operand_aliasing={{1}: (6, {}), {0}: (7, {})} | custom-call | flops 1132462080 | bytes 8847360 | tf_op jit(solution)/shard_map/attend/pallas_call | solution.py:234
  35.5 2.1 %collective-permute-done.6.query_ref.grad_ref = bf16[2,32,4096]{2,1,0:T(8,128)(2,1)S(1)} collective-permute-done((bf16[2,32,4096]{2,1,0:T(8,128)(2,1)}, bf16[2,32,4096]{2,1,0:T(8,128)(2,1)S(1)}, u32[]{:S(2)}, u32[]{:S(2)}) %collective-permute-start.6) | collective-permute-done | bytes 524320 | tf_op jit(solution)/shard_map/ppermute | solution.py:28
  37.6 3.9 %attend.7 = (bf16[128,32,128]{2,1,0:T(8,128)(2,1)}, f32[2,384,512]{2,1,0:T(8,128)S(1)}) custom-call(s32[2]{0:T(128)S(1)} %pad_add_fusion.meta_ref, s32[4]{0:T(128)S(1)} %copy-done.3, s32[4,1024]{1,0:T(4,128)S(1)} %copy-done.2, bf16[2,32,4096]{2,1,0:T(8,128)(2,1)S(1)} %collective-permute-done.6.query_ref.grad_ref, ...), custom_call_target="tpu_custom_call", output_to_operand_aliasing={{1}: (6, {}), {0}: (7, {})} | custom-call | flops 1132462080 | bytes 8847360 | tf_op jit(solution)/shard_map/attend/pallas_call | solution.py:234
  41.5 7.3 %collective-permute-done.5.query_ref.grad_ref = bf16[2,32,2048]{2,1,0:T(8,128)(2,1)S(1)} collective-permute-done((bf16[2,32,2048]{2,1,0:T(8,128)(2,1)S(1)}, bf16[2,32,2048]{2,1,0:T(8,128)(2,1)S(1)}, u32[]{:S(2)}, u32[]{:S(2)}) %collective-permute-start.5) | collective-permute-done | bytes 262176 | tf_op jit(solution)/shard_map/ppermute | solution.py:28
  48.9 2.4 %attend.8 = (bf16[128,32,128]{2,1,0:T(8,128)(2,1)}, f32[2,128,256]{2,1,0:T(8,128)S(1)}, bf16[2,128,256]{2,1,0:T(8,128)(2,1)S(1)}, bf16[2,128,256]{2,1,0:T(8,128)(2,1)S(1)}) custom-call(s32[2]{0:T(128)S(1)} %pad_add_fusion.meta_ref, s32[4]{0:T(128)S(1)} %copy-done.3, s32[4,1024]{1,0:T(4,128)S(1)} %copy-done.2, ...), custom_call_target="tpu_custom_call", output_to_operand_aliasing={{0}: (7, {})} | custom-call | flops 18874368 | bytes 147456 | tf_op jit(solution)/shard_map/attend/pallas_call | solution.py:234
  51.2 7.1 %collective-permute-start.9 = (bf16[2,128,256]{2,1,0:T(8,128)(2,1)S(1)}, bf16[2,128,256]{2,1,0:T(8,128)(2,1)S(1)}, u32[]{:S(2)}, u32[]{:S(2)}) collective-permute-start(bf16[2,128,256]{2,1,0:T(8,128)(2,1)S(1)} %get-tuple-element.64), channel_id=1, source_target_pairs={{4,0},{8,4},{12,8},{16,12},{20,16},{24,20},{28,24},{5,1},{9,5},{13... | collective-permute-start | bytes 393224 | tf_op jit(solution)/shard_map/ppermute | solution.py:34
  58.3 1.9 %collective-permute-start.10 = (bf16[2,128,256]{2,1,0:T(8,128)(2,1)S(1)}, bf16[2,128,256]{2,1,0:T(8,128)(2,1)S(1)}, u32[]{:S(2)}, u32[]{:S(2)}) collective-permute-start(bf16[2,128,256]{2,1,0:T(8,128)(2,1)S(1)} %get-tuple-element.65), channel_id=1, source_target_pairs={{8,0},{12,4},{16,8},{20,12},{24,16},{28,20},{9,1},{13,5},{17,9},{2... | collective-permute-start | bytes 393224 | tf_op jit(solution)/shard_map/ppermute | solution.py:34
  60.3 3.1 %collective-permute-done.8.query_ref.grad_ref = bf16[2,32,2048]{2,1,0:T(8,128)(2,1)S(1)} collective-permute-done((bf16[2,32,2048]{2,1,0:T(8,128)(2,1)S(1)}, bf16[2,32,2048]{2,1,0:T(8,128)(2,1)S(1)}, u32[]{:S(2)}, u32[]{:S(2)}) %collective-permute-start.8) | collective-permute-done | bytes 262176 | tf_op jit(solution)/shard_map/ppermute | solution.py:28
  63.4 2.4 %attend.9 = (bf16[128,32,128]{2,1,0:T(8,128)(2,1)}, f32[2,128,256]{2,1,0:T(8,128)S(1)}, bf16[2,128,256]{2,1,0:T(8,128)(2,1)S(1)}, bf16[2,128,256]{2,1,0:T(8,128)(2,1)S(1)}) custom-call(s32[2]{0:T(128)S(1)} %pad_add_fusion.meta_ref, s32[4]{0:T(128)S(1)} %copy-done.3, s32[4,1024]{1,0:T(4,128)S(1)} %copy-done.2, ...), custom_call_target="tpu_custom_call", output_to_operand_aliasing={{0}: (7, {})} | custom-call | flops 18874368 | bytes 147456 | tf_op jit(solution)/shard_map/attend/pallas_call | solution.py:234
  65.7 2.8 %collective-permute-start.11 = (bf16[2,128,256]{2,1,0:T(8,128)(2,1)S(1)}, bf16[2,128,256]{2,1,0:T(8,128)(2,1)S(1)}, u32[]{:S(2)}, u32[]{:S(2)}) collective-permute-start(bf16[2,128,256]{2,1,0:T(8,128)(2,1)S(1)} %get-tuple-element.69), channel_id=1, source_target_pairs={{4,0},{8,4},{12,8},{16,12},{20,16},{24,20},{28,24},{5,1},{9,5},{13... | collective-permute-start | bytes 393224 | tf_op jit(solution)/shard_map/ppermute | solution.py:34
  68.5 1.9 %collective-permute-start.12 = (bf16[2,128,256]{2,1,0:T(8,128)(2,1)S(1)}, bf16[2,128,256]{2,1,0:T(8,128)(2,1)S(1)}, u32[]{:S(2)}, u32[]{:S(2)}) collective-permute-start(bf16[2,128,256]{2,1,0:T(8,128)(2,1)S(1)} %get-tuple-element.70), channel_id=1, source_target_pairs={{8,0},{12,4},{16,8},{20,12},{24,16},{28,20},{9,1},{13,5},{17,9},{2... | collective-permute-start | bytes 393224 | tf_op jit(solution)/shard_map/ppermute | solution.py:34
  70.5 1.4 %collective-permute-done.11 = bf16[2,128,256]{2,1,0:T(8,128)(2,1)S(1)} collective-permute-done((bf16[2,128,256]{2,1,0:T(8,128)(2,1)S(1)}, bf16[2,128,256]{2,1,0:T(8,128)(2,1)S(1)}, u32[]{:S(2)}, u32[]{:S(2)}) %collective-permute-start.11) | collective-permute-done | bytes 131104 | tf_op jit(solution)/shard_map/ppermute | solution.py:34
  71.9 2.9 %collective-permute-done.12 = bf16[2,128,256]{2,1,0:T(8,128)(2,1)S(1)} collective-permute-done((bf16[2,128,256]{2,1,0:T(8,128)(2,1)S(1)}, bf16[2,128,256]{2,1,0:T(8,128)(2,1)S(1)}, u32[]{:S(2)}, u32[]{:S(2)}) %collective-permute-start.12) | collective-permute-done | bytes 131104 | tf_op jit(solution)/shard_map/ppermute | solution.py:34
  (30 shorter events, 2.9 us)
Async XLA Ops:
  3.8 23.2 %copy-start = (bf16[4,32,4096]{2,1,0:T(8,128)(2,1)S(1)}, bf16[4,32,4096]{2,1,0:T(8,128)(2,1)}, u32[]{:S(2)}) copy-start(bf16[4,32,4096]{2,1,0:T(8,128)(2,1)} %query_ref.1) | copy-start | bytes 3145732
  3.8 23.2 %copy-start.1 = (bf16[4,32,4096]{2,1,0:T(8,128)(2,1)S(1)}, bf16[4,32,4096]{2,1,0:T(8,128)(2,1)}, u32[]{:S(2)}) copy-start(bf16[4,32,4096]{2,1,0:T(8,128)(2,1)} %grad_ref.1) | copy-start | bytes 3145732
  3.9 23.2 %copy-start.2 = (s32[4,1024]{1,0:T(4,128)S(1)}, s32[4,1024]{1,0:T(4,128)}, u32[]{:S(2)}) copy-start(s32[4,1024]{1,0:T(4,128)} %segment_ref.9) | copy-start | bytes 49156
  3.9 23.2 %copy-start.3 = (s32[4]{0:T(128)S(1)}, s32[4]{0:T(128)}, u32[]{:S(2)}) copy-start(s32[4]{0:T(128)} %assign_ref.11) | copy-start | bytes 52
  3.9 6.4 %collective-permute-start = (bf16[2,32,512]{2,1,0:T(8,128)(2,1)}, bf16[2,32,512]{2,1,0:T(8,128)(2,1)S(1)}, u32[]{:S(2)}, u32[]{:S(2)}) collective-permute-start(bf16[2,32,512]{2,1,0:T(8,128)(2,1)} %get-tuple-element.41), channel_id=1, source_target_pairs={{0,1},{1,2},{2,3},{3,0},{4,5},{5,6},{6,7},{7,4},{8,9},{9,10},{10,1... | collective-permute-start | bytes 196616 | tf_op jit(solution)/shard_map/ppermute | solution.py:28
  6.1 7.5 %collective-permute-start.1 = (bf16[2,32,512]{2,1,0:T(8,128)(2,1)}, bf16[2,32,512]{2,1,0:T(8,128)(2,1)S(1)}, u32[]{:S(2)}, u32[]{:S(2)}) collective-permute-start(bf16[2,32,512]{2,1,0:T(8,128)(2,1)} %get-tuple-element.46), channel_id=1, source_target_pairs={{0,2},{1,3},{2,0},{3,1},{4,6},{5,7},{6,4},{7,5},{8,10},{9,11},{10,... | collective-permute-start | bytes 196616 | tf_op jit(solution)/shard_map/ppermute | solution.py:28
  8.4 5.2 %collective-permute-start.2 = (bf16[2,32,512]{2,1,0:T(8,128)(2,1)}, bf16[2,32,512]{2,1,0:T(8,128)(2,1)S(1)}, u32[]{:S(2)}, u32[]{:S(2)}) collective-permute-start(bf16[2,32,512]{2,1,0:T(8,128)(2,1)} %get-tuple-element.47), channel_id=1, source_target_pairs={{0,3},{1,0},{2,1},{3,2},{4,7},{5,4},{6,5},{7,6},{8,11},{9,8},{10,9... | collective-permute-start | bytes 196616 | tf_op jit(solution)/shard_map/ppermute | solution.py:28
  10.3 21.3 %collective-permute-start.7 = (bf16[2,32,4096]{2,1,0:T(8,128)(2,1)}, bf16[2,32,4096]{2,1,0:T(8,128)(2,1)S(1)}, u32[]{:S(2)}, u32[]{:S(2)}) collective-permute-start(bf16[2,32,4096]{2,1,0:T(8,128)(2,1)} %get-tuple-element.51), channel_id=1, source_target_pairs={{0,1},{1,2},{2,3},{3,0},{4,5},{5,6},{6,7},{7,4},{8,9},{9,10},{10,1... | collective-permute-start | bytes 1572872 | tf_op jit(solution)/shard_map/ppermute | solution.py:28
  13.6 10.8 %collective-permute-start.4 = (bf16[4,2,32,512]{3,2,1,0:T(8,128)(2,1)S(1)}, bf16[4,2,32,512]{3,2,1,0:T(8,128)(2,1)}, u32[]{:S(2)}, u32[]{:S(2)}) collective-permute-start(bf16[4,2,32,512]{3,2,1,0:T(8,128)(2,1)S(1)} %bitcast_dynamic-update-slice_fusion), channel_id=1, source_target_pairs={{0,4},{4,8},{8,12},{12,16},{16,20},{20,24},{24,28},{1,5},{5,9},{9,... | collective-permute-start | bytes 786440 | tf_op jit(solution)/shard_map/ppermute | solution.py:34
  16.0 9.9 %collective-permute-start.3 = (bf16[4,2,32,512]{3,2,1,0:T(8,128)(2,1)S(1)}, bf16[4,2,32,512]{3,2,1,0:T(8,128)(2,1)}, u32[]{:S(2)}, u32[]{:S(2)}) collective-permute-start(bf16[4,2,32,512]{3,2,1,0:T(8,128)(2,1)S(1)} %bitcast_dynamic-update-slice_fusion), channel_id=1, source_target_pairs={{0,8},{4,12},{8,16},{12,20},{16,24},{20,28},{1,9},{5,13},{9,17},{1... | collective-permute-start | bytes 786440 | tf_op jit(solution)/shard_map/ppermute | solution.py:34
  21.1 16.6 %collective-permute-start.6 = (bf16[2,32,4096]{2,1,0:T(8,128)(2,1)}, bf16[2,32,4096]{2,1,0:T(8,128)(2,1)S(1)}, u32[]{:S(2)}, u32[]{:S(2)}) collective-permute-start(bf16[2,32,4096]{2,1,0:T(8,128)(2,1)} %get-tuple-element.50), channel_id=1, source_target_pairs={{0,3},{1,0},{2,1},{3,2},{4,7},{5,4},{6,5},{7,6},{8,11},{9,8},{10,9... | collective-permute-start | bytes 1572872 | tf_op jit(solution)/shard_map/ppermute | solution.py:28
  27.1 3.9 %copy-start.5 = (bf16[2,32,2048]{2,1,0:T(8,128)(2,1)S(1)}, bf16[2,32,2048]{2,1,0:T(8,128)(2,1)}, u32[]{:S(2)}) copy-start(bf16[2,32,2048]{2,1,0:T(8,128)(2,1)} %get-tuple-element.49) | copy-start | bytes 786436
  31.0 17.9 %collective-permute-start.5 = (bf16[2,32,2048]{2,1,0:T(8,128)(2,1)S(1)}, bf16[2,32,2048]{2,1,0:T(8,128)(2,1)S(1)}, u32[]{:S(2)}, u32[]{:S(2)}) collective-permute-start(bf16[2,32,2048]{2,1,0:T(8,128)(2,1)S(1)} %copy-done.5), channel_id=1, source_target_pairs={{0,2},{1,3},{2,0},{3,1},{4,6},{5,7},{6,4},{7,5},{8,10},{9,11},{10,... | collective-permute-start | bytes 786440 | tf_op jit(solution)/shard_map/ppermute | solution.py:28
  37.6 11.2 %copy-start.4 = (bf16[2,32,2048]{2,1,0:T(8,128)(2,1)S(1)}, bf16[2,32,2048]{2,1,0:T(8,128)(2,1)}, u32[]{:S(2)}) copy-start(bf16[2,32,2048]{2,1,0:T(8,128)(2,1)} %get-tuple-element.57) | copy-start | bytes 786436
  48.9 14.5 %collective-permute-start.8 = (bf16[2,32,2048]{2,1,0:T(8,128)(2,1)S(1)}, bf16[2,32,2048]{2,1,0:T(8,128)(2,1)S(1)}, u32[]{:S(2)}, u32[]{:S(2)}) collective-permute-start(bf16[2,32,2048]{2,1,0:T(8,128)(2,1)S(1)} %copy-done.4), channel_id=1, source_target_pairs={{0,2},{1,3},{2,0},{3,1},{4,6},{5,7},{6,4},{7,5},{8,10},{9,11},{10,... | collective-permute-start | bytes 786440 | tf_op jit(solution)/shard_map/ppermute | solution.py:28
  51.2 14.5 %collective-permute-start.9 = (bf16[2,128,256]{2,1,0:T(8,128)(2,1)S(1)}, bf16[2,128,256]{2,1,0:T(8,128)(2,1)S(1)}, u32[]{:S(2)}, u32[]{:S(2)}) collective-permute-start(bf16[2,128,256]{2,1,0:T(8,128)(2,1)S(1)} %get-tuple-element.64), channel_id=1, source_target_pairs={{4,0},{8,4},{12,8},{16,12},{20,16},{24,20},{28,24},{5,1},{9,5},{13... | collective-permute-start | bytes 393224 | tf_op jit(solution)/shard_map/ppermute | solution.py:34
  58.3 12.1 %collective-permute-start.10 = (bf16[2,128,256]{2,1,0:T(8,128)(2,1)S(1)}, bf16[2,128,256]{2,1,0:T(8,128)(2,1)S(1)}, u32[]{:S(2)}, u32[]{:S(2)}) collective-permute-start(bf16[2,128,256]{2,1,0:T(8,128)(2,1)S(1)} %get-tuple-element.65), channel_id=1, source_target_pairs={{8,0},{12,4},{16,8},{20,12},{24,16},{28,20},{9,1},{13,5},{17,9},{2... | collective-permute-start | bytes 393224 | tf_op jit(solution)/shard_map/ppermute | solution.py:34
  65.7 6.2 %collective-permute-start.11 = (bf16[2,128,256]{2,1,0:T(8,128)(2,1)S(1)}, bf16[2,128,256]{2,1,0:T(8,128)(2,1)S(1)}, u32[]{:S(2)}, u32[]{:S(2)}) collective-permute-start(bf16[2,128,256]{2,1,0:T(8,128)(2,1)S(1)} %get-tuple-element.69), channel_id=1, source_target_pairs={{4,0},{8,4},{12,8},{16,12},{20,16},{24,20},{28,24},{5,1},{9,5},{13... | collective-permute-start | bytes 393224 | tf_op jit(solution)/shard_map/ppermute | solution.py:34
  68.5 6.3 %collective-permute-start.12 = (bf16[2,128,256]{2,1,0:T(8,128)(2,1)S(1)}, bf16[2,128,256]{2,1,0:T(8,128)(2,1)S(1)}, u32[]{:S(2)}, u32[]{:S(2)}) collective-permute-start(bf16[2,128,256]{2,1,0:T(8,128)(2,1)S(1)} %get-tuple-element.70), channel_id=1, source_target_pairs={{8,0},{12,4},{16,8},{20,12},{24,16},{28,20},{9,1},{13,5},{17,9},{2... | collective-permute-start | bytes 393224 | tf_op jit(solution)/shard_map/ppermute | solution.py:34

commit v16 on v13

--- a/solution.py
+++ b/solution.py
@@ -283,13 +283,14 @@
     kv = jnp.concatenate([*halos, kv_own], axis=0)
 
     fixed = (doc_most, heads, meta, assignment, segment_ids)
-    query, grad = (queries, lambda m, a: a[m[0]]), (grad_out, lambda m, a: a[m[0]])
-    full, acc = attend(0, 0, kv_heads, *fixed, query, grad, kv, None, None, False)
-    rows, acc = lax.optimization_barrier((held[0], acc))
-    split = [exchanged(rows, "dp", final)]
-    for step, both in zip(others, arrived):
-        query, grad = (both, lambda m, a: 0), (both, lambda m, a: 1)
+    pairs = [(step, (both, lambda m, a: 0), (both, lambda m, a: 1)) for step, both in zip(others, arrived)]
+    pairs.append((0, (queries, lambda m, a: a[m[0]]), (grad_out, lambda m, a: a[m[0]])))
+    full, acc, split = None, None, []
+    for step, query, grad in pairs:
         full, acc = attend(step, 0, kv_heads, *fixed, query, grad, kv, acc, full, False)
+        if not split:
+            rows, acc = lax.optimization_barrier((held[0], acc))
+            split = [exchanged(rows, "dp", final)]
     for rows in held[1:]:
         rows, acc = lax.optimization_barrier((rows, acc))
         split.append(exchanged(rows, "dp", final))
@@ -300,7 +301,7 @@
             final, half * HEADS_STEP, HEADS_STEP, *fixed, query, grad, kv, acc, full, True
         )
         if half:
-            halos, returned = lax.optimization_barrier((halos, returned))
+            halos, returned[0] = lax.optimization_barrier((halos, returned[0]))
         returned = [shifted(halo, ("blk", "uly"), -back) for back, halo in enumerate(halos, 1)]
         for halo in returned:
             total = total + halo.astype(jnp.float32)

time: 75.5 us -> 80.5 us (1.066)
  starting transfers between devices: 25 us -> 35.4 us
  waiting for transfers between devices: 26.7 us -> 22.4 us
  other arithmetic: 2.01 us -> 0.97 us
    ppermute x6, starting transfers between devices: 15.1 us -> 23.8 us  [shifted(): return lax.ppermute(value, axis, pairs)]
    ppermute x7, waiting for transfers between devices: 17.9 us -> 12.9 us  [exchanged(): lax.ppermute(value, axis, [(i, (i + step) % count) for i in range(count)])]
    ppermute x7, starting transfers between devices: 9.91 us -> 11.6 us  [exchanged(): lax.ppermute(value, axis, [(i, (i + step) % count) for i in range(count)])]
    concatenate x1, other arithmetic: 1.12 us -> 0.09 us  [shards(): kv = jnp.concatenate([*halos, kv_own], axis=0)]
  transfers between devices with their start and end apart: 13 -> 13, of which waited for: 8 -> 7; matrix products, arithmetic and copies ran while one was open for 3% -> 1% of each run, Pallas kernels for 22% -> 21%
where the time goes in v16:
time: 80.5 us; the launch traced here: 80.2 us
  starting transfers between devices  35.4 us (44%)
  waiting for transfers between devices  22.4 us (28%)
  Pallas kernels  19.7 us (24%)
  other arithmetic  0.97 us (1%)
  local copies, waits for them, and re-layouts  0.93 us (1%)
    ppermute x6, starting transfers between devices, shifted(): return lax.ppermute(value, axis, pairs)  23.8 us
    pallas_call x5, Pallas kernels, attend(): pl.pallas_call(functools.partial(attend_kernel, step, first, filled, last...  16.5 us
    ppermute x7, waiting for transfers between devices, exchanged(): lax.ppermute(value, axis, [(i, (i + step) % count) for i in range(count)])  12.9 us
    ppermute x7, starting transfers between devices, exchanged(): lax.ppermute(value, axis, [(i, (i + step) % count) for i in range(count)])  11.6 us
    ppermute x6, waiting for transfers between devices, shifted(): return lax.ppermute(value, axis, pairs)  9.51 us
    pallas_call x1, Pallas kernels, stage(): pl.pallas_call(functools.partial(stage_kernel, count, jobs, len(jobs)), o...  3.19 us
  transfers between devices with their start and end apart: 13, of which 7 were waited for; matrix products, arithmetic and copies ran while one was open for 1% of the time, Pallas kernels for 21%

profile of v16, /device:TPU:1, one launch (start us, length us, event | category | flops | bytes accessed | tf_op | source)
XLA Modules:
  0.0 80.2 jit_solution(3293140521145998998)
XLA Ops:
  0.6 3.2 %stage.1 = (bf16[2,32,512]{2,1,0:T(8,128)(2,1)}, bf16[2,32,512]{2,1,0:T(8,128)(2,1)}, bf16[2,32,512]{2,1,0:T(8,128)(2,1)}, bf16[2,32,512]{2,1,0:T(8,128)(2,1)}, ...) custom-call(s32[4]{0:T(128)} %assign_ref.11, ...), custom_call_target="tpu_custom_call" | custom-call | tf_op jit(solution)/shard_map/stage/pallas_call | solution.py:62
  3.9 2.2 %collective-permute-start = (bf16[2,32,512]{2,1,0:T(8,128)(2,1)}, bf16[2,32,512]{2,1,0:T(8,128)(2,1)S(1)}, u32[]{:S(2)}, u32[]{:S(2)}) collective-permute-start(bf16[2,32,512]{2,1,0:T(8,128)(2,1)} %get-tuple-element.40), channel_id=1, source_target_pairs={{0,1},{1,2},{2,3},{3,0},{4,5},{5,6},{6,7},{7,4},{8,9},{9,10},{10,1... | collective-permute-start | bytes 196616 | tf_op jit(solution)/shard_map/ppermute | solution.py:27
  6.0 2.3 %collective-permute-start.1 = (bf16[2,32,512]{2,1,0:T(8,128)(2,1)}, bf16[2,32,512]{2,1,0:T(8,128)(2,1)S(1)}, u32[]{:S(2)}, u32[]{:S(2)}) collective-permute-start(bf16[2,32,512]{2,1,0:T(8,128)(2,1)} %get-tuple-element.44), channel_id=1, source_target_pairs={{0,2},{1,3},{2,0},{3,1},{4,6},{5,7},{6,4},{7,5},{8,10},{9,11},{10,... | collective-permute-start | bytes 196616 | tf_op jit(solution)/shard_map/ppermute | solution.py:27
  8.3 1.1 %collective-permute-start.2 = (bf16[2,32,512]{2,1,0:T(8,128)(2,1)}, bf16[2,32,512]{2,1,0:T(8,128)(2,1)S(1)}, u32[]{:S(2)}, u32[]{:S(2)}) collective-permute-start(bf16[2,32,512]{2,1,0:T(8,128)(2,1)} %get-tuple-element.45), channel_id=1, source_target_pairs={{0,3},{1,0},{2,1},{3,2},{4,7},{5,4},{6,5},{7,6},{8,11},{9,8},{10,9... | collective-permute-start | bytes 196616 | tf_op jit(solution)/shard_map/ppermute | solution.py:27
  10.3 1.1 %collective-permute-start.5 = (bf16[2,32,4096]{2,1,0:T(8,128)(2,1)}, bf16[2,32,4096]{2,1,0:T(8,128)(2,1)S(1)}, u32[]{:S(2)}, u32[]{:S(2)}) collective-permute-start(bf16[2,32,4096]{2,1,0:T(8,128)(2,1)} %get-tuple-element.46), channel_id=1, source_target_pairs={{0,3},{1,0},{2,1},{3,2},{4,7},{5,4},{6,5},{7,6},{8,11},{9,8},{10,9... | collective-permute-start | bytes 1572872 | tf_op jit(solution)/shard_map/ppermute | solution.py:27
  11.8 1.8 %collective-permute-done.1 = bf16[2,32,512]{2,1,0:T(8,128)(2,1)S(1)} collective-permute-done((bf16[2,32,512]{2,1,0:T(8,128)(2,1)}, bf16[2,32,512]{2,1,0:T(8,128)(2,1)S(1)}, u32[]{:S(2)}, u32[]{:S(2)}) %collective-permute-start.1) | collective-permute-done | bytes 65568 | tf_op jit(solution)/shard_map/ppermute | solution.py:27
  13.6 2.4 %collective-permute-start.4 = (bf16[4,2,32,512]{3,2,1,0:T(8,128)(2,1)S(1)}, bf16[4,2,32,512]{3,2,1,0:T(8,128)(2,1)S(1)}, u32[]{:S(2)}, u32[]{:S(2)}) collective-permute-start(bf16[4,2,32,512]{3,2,1,0:T(8,128)(2,1)S(1)} %bitcast_dynamic-update-slice_fusion), channel_id=1, source_target_pairs={{0,4},{4,8},{8,12},{12,16},{16,20},{20,24},{24,28},{1,5},{5,9},{9,... | collective-permute-start | bytes 786440 | tf_op jit(solution)/shard_map/ppermute | solution.py:33
  16.0 5.3 %collective-permute-start.3 = (bf16[4,2,32,512]{3,2,1,0:T(8,128)(2,1)S(1)}, bf16[4,2,32,512]{3,2,1,0:T(8,128)(2,1)S(1)}, u32[]{:S(2)}, u32[]{:S(2)}) collective-permute-start(bf16[4,2,32,512]{3,2,1,0:T(8,128)(2,1)S(1)} %bitcast_dynamic-update-slice_fusion), channel_id=1, source_target_pairs={{0,8},{4,12},{8,16},{12,20},{16,24},{20,28},{1,9},{5,13},{9,17},{1... | collective-permute-start | bytes 786440 | tf_op jit(solution)/shard_map/ppermute | solution.py:33
  21.5 2.7 %collective-permute-done.4 = bf16[4,2,32,512]{3,2,1,0:T(8,128)(2,1)S(1)} collective-permute-done((bf16[4,2,32,512]{3,2,1,0:T(8,128)(2,1)S(1)}, bf16[4,2,32,512]{3,2,1,0:T(8,128)(2,1)S(1)}, u32[]{:S(2)}, u32[]{:S(2)}) %collective-permute-start.4) | collective-permute-done | bytes 262176 | tf_op jit(solution)/shard_map/ppermute | solution.py:33
  24.2 2.0 %collective-permute-done.3 = bf16[4,2,32,512]{3,2,1,0:T(8,128)(2,1)S(1)} collective-permute-done((bf16[4,2,32,512]{3,2,1,0:T(8,128)(2,1)S(1)}, bf16[4,2,32,512]{3,2,1,0:T(8,128)(2,1)S(1)}, u32[]{:S(2)}, u32[]{:S(2)}) %collective-permute-start.3) | collective-permute-done | bytes 262176 | tf_op jit(solution)/shard_map/ppermute | solution.py:33
  26.3 7.3 %collective-permute-done.6.query_ref.grad_ref = bf16[2,32,4096]{2,1,0:T(8,128)(2,1)S(1)} collective-permute-done((bf16[2,32,4096]{2,1,0:T(8,128)(2,1)}, bf16[2,32,4096]{2,1,0:T(8,128)(2,1)S(1)}, u32[]{:S(2)}, u32[]{:S(2)}) %collective-permute-start.6) | collective-permute-done | bytes 524320 | tf_op jit(solution)/shard_map/ppermute | solution.py:27
  33.6 3.9 %attend.5 = (bf16[128,32,128]{2,1,0:T(8,128)(2,1)}, f32[2,384,512]{2,1,0:T(8,128)S(1)}) custom-call(s32[2]{0:T(128)S(1)} %pad_add_fusion.meta_ref, s32[4]{0:T(128)S(1)} %copy-done.3, s32[4,1024]{1,0:T(4,128)S(1)} %copy-done.2, bf16[2,32,4096]{2,1,0:T(8,128)(2,1)S(1)} %collective-permute-done.6.query_ref.grad_ref, ...), custom_call_target="tpu_custom_call" | custom-call | flops 37748736 | bytes 294912 | tf_op jit(solution)/shard_map/attend/pallas_call | solution.py:232
  37.5 4.5 %collective-permute-start.8 = (bf16[2,32,2048]{2,1,0:T(8,128)(2,1)S(1)}, bf16[2,32,2048]{2,1,0:T(8,128)(2,1)S(1)}, u32[]{:S(2)}, u32[]{:S(2)}) collective-permute-start(bf16[2,32,2048]{2,1,0:T(8,128)(2,1)S(1)} %copy-done.5), channel_id=1, source_target_pairs={{0,2},{1,3},{2,0},{3,1},{4,6},{5,7},{6,4},{7,5},{8,10},{9,11},{10,... | collective-permute-start | bytes 786440 | tf_op jit(solution)/shard_map/ppermute | solution.py:27
  42.0 3.9 %attend.6 = (bf16[128,32,128]{2,1,0:T(8,128)(2,1)}, f32[2,384,512]{2,1,0:T(8,128)S(1)}) custom-call(s32[2]{0:T(128)S(1)} %pad_add_fusion.meta_ref, s32[4]{0:T(128)S(1)} %copy-done.3, s32[4,1024]{1,0:T(4,128)S(1)} %copy-done.2, bf16[2,32,4096]{2,1,0:T(8,128)(2,1)S(1)} %collective-permute-done.5.query_ref.grad_ref, ...), custom_call_target="tpu_custom_call", output_to_operand_aliasing={{1}: (6, {}), {0}: (7, {})} | custom-call | flops 37748736 | bytes 294912 | tf_op jit(solution)/shard_map/attend/pallas_call | solution.py:232
  45.9 4.0 %attend.7 = (bf16[128,32,128]{2,1,0:T(8,128)(2,1)}, f32[2,384,512]{2,1,0:T(8,128)S(1)}) custom-call(s32[2]{0:T(128)S(1)} %pad_add_fusion.meta_ref, s32[4]{0:T(128)S(1)} %copy-done.3, s32[4,1024]{1,0:T(4,128)S(1)} %copy-done.2, bf16[4,32,4096]{2,1,0:T(8,128)(2,1)S(1)} %copy-done, ...), custom_call_target="tpu_custom_call", output_to_operand_aliasing={{1}: (6, {}), {0}: (7, {})} | custom-call | flops 37748736 | bytes 294912 | tf_op jit(solution)/shard_map/attend/pallas_call | solution.py:232
  49.9 3.8 %collective-permute-done.8.query_ref.grad_ref = bf16[2,32,2048]{2,1,0:T(8,128)(2,1)S(1)} collective-permute-done((bf16[2,32,2048]{2,1,0:T(8,128)(2,1)S(1)}, bf16[2,32,2048]{2,1,0:T(8,128)(2,1)S(1)}, u32[]{:S(2)}, u32[]{:S(2)}) %collective-permute-start.8) | collective-permute-done | bytes 262176 | tf_op jit(solution)/shard_map/ppermute | solution.py:27
  53.8 2.4 %attend.8 = (bf16[128,32,128]{2,1,0:T(8,128)(2,1)}, f32[2,128,256]{2,1,0:T(8,128)S(1)}, bf16[2,128,256]{2,1,0:T(8,128)(2,1)S(1)}, bf16[2,128,256]{2,1,0:T(8,128)(2,1)S(1)}) custom-call(s32[2]{0:T(128)S(1)} %pad_add_fusion.meta_ref, s32[4]{0:T(128)S(1)} %copy-done.3, s32[4,1024]{1,0:T(4,128)S(1)} %copy-done.2, ...), custom_call_target="tpu_custom_call", output_to_operand_aliasing={{0}: (7, {})} | custom-call | flops 18874368 | bytes 147456 | tf_op jit(solution)/shard_map/attend/pallas_call | solution.py:232
  56.2 10.1 %collective-permute-start.9 = (bf16[2,128,256]{2,1,0:T(8,128)(2,1)S(1)}, bf16[2,128,256]{2,1,0:T(8,128)(2,1)S(1)}, u32[]{:S(2)}, u32[]{:S(2)}) collective-permute-start(bf16[2,128,256]{2,1,0:T(8,128)(2,1)S(1)} %get-tuple-element.62), channel_id=1, source_target_pairs={{4,0},{8,4},{12,8},{16,12},{20,16},{24,20},{28,24},{5,1},{9,5},{13... | collective-permute-start | bytes 393224 | tf_op jit(solution)/shard_map/ppermute | solution.py:33
  66.3 1.9 %collective-permute-start.10 = (bf16[2,128,256]{2,1,0:T(8,128)(2,1)S(1)}, bf16[2,128,256]{2,1,0:T(8,128)(2,1)S(1)}, u32[]{:S(2)}, u32[]{:S(2)}) collective-permute-start(bf16[2,128,256]{2,1,0:T(8,128)(2,1)S(1)} %get-tuple-element.63), channel_id=1, source_target_pairs={{8,0},{12,4},{16,8},{20,12},{24,16},{28,20},{9,1},{13,5},{17,9},{2... | collective-permute-start | bytes 393224 | tf_op jit(solution)/shard_map/ppermute | solution.py:33
  68.2 2.4 %attend.9 = (bf16[128,32,128]{2,1,0:T(8,128)(2,1)}, f32[2,128,256]{2,1,0:T(8,128)S(1)}, bf16[2,128,256]{2,1,0:T(8,128)(2,1)S(1)}, bf16[2,128,256]{2,1,0:T(8,128)(2,1)S(1)}) custom-call(s32[2]{0:T(128)S(1)} %pad_add_fusion.meta_ref, s32[4]{0:T(128)S(1)} %copy-done.3, s32[4,1024]{1,0:T(4,128)S(1)} %copy-done.2, ...), custom_call_target="tpu_custom_call", output_to_operand_aliasing={{0}: (7, {})} | custom-call | flops 18874368 | bytes 147456 | tf_op jit(solution)/shard_map/attend/pallas_call | solution.py:232
  70.6 2.1 %collective-permute-start.11 = (bf16[2,128,256]{2,1,0:T(8,128)(2,1)S(1)}, bf16[2,128,256]{2,1,0:T(8,128)(2,1)S(1)}, u32[]{:S(2)}, u32[]{:S(2)}) collective-permute-start(bf16[2,128,256]{2,1,0:T(8,128)(2,1)S(1)} %get-tuple-element.67), channel_id=1, source_target_pairs={{4,0},{8,4},{12,8},{16,12},{20,16},{24,20},{28,24},{5,1},{9,5},{13... | collective-permute-start | bytes 393224 | tf_op jit(solution)/shard_map/ppermute | solution.py:33
  72.7 1.9 %collective-permute-start.12 = (bf16[2,128,256]{2,1,0:T(8,128)(2,1)S(1)}, bf16[2,128,256]{2,1,0:T(8,128)(2,1)S(1)}, u32[]{:S(2)}, u32[]{:S(2)}) collective-permute-start(bf16[2,128,256]{2,1,0:T(8,128)(2,1)S(1)} %get-tuple-element.68), channel_id=1, source_target_pairs={{8,0},{12,4},{16,8},{20,12},{24,16},{28,20},{9,1},{13,5},{17,9},{2... | collective-permute-start | bytes 393224 | tf_op jit(solution)/shard_map/ppermute | solution.py:33
  74.7 3.1 %collective-permute-done.11 = bf16[2,128,256]{2,1,0:T(8,128)(2,1)S(1)} collective-permute-done((bf16[2,128,256]{2,1,0:T(8,128)(2,1)S(1)}, bf16[2,128,256]{2,1,0:T(8,128)(2,1)S(1)}, u32[]{:S(2)}, u32[]{:S(2)}) %collective-permute-start.11) | collective-permute-done | bytes 131104 | tf_op jit(solution)/shard_map/ppermute | solution.py:33
  77.8 1.6 %collective-permute-done.12 = bf16[2,128,256]{2,1,0:T(8,128)(2,1)S(1)} collective-permute-done((bf16[2,128,256]{2,1,0:T(8,128)(2,1)S(1)}, bf16[2,128,256]{2,1,0:T(8,128)(2,1)S(1)}, u32[]{:S(2)}, u32[]{:S(2)}) %collective-permute-start.12) | collective-permute-done | bytes 131104 | tf_op jit(solution)/shard_map/ppermute | solution.py:33
  (30 shorter events, 2.4 us)
Async XLA Ops:
  3.8 29.7 %copy-start.2 = (s32[4,1024]{1,0:T(4,128)S(1)}, s32[4,1024]{1,0:T(4,128)}, u32[]{:S(2)}) copy-start(s32[4,1024]{1,0:T(4,128)} %segment_ref.9) | copy-start | bytes 49156
  3.8 29.7 %copy-start.3 = (s32[4]{0:T(128)S(1)}, s32[4]{0:T(128)}, u32[]{:S(2)}) copy-start(s32[4]{0:T(128)} %assign_ref.11) | copy-start | bytes 52
  3.9 6.4 %collective-permute-start = (bf16[2,32,512]{2,1,0:T(8,128)(2,1)}, bf16[2,32,512]{2,1,0:T(8,128)(2,1)S(1)}, u32[]{:S(2)}, u32[]{:S(2)}) collective-permute-start(bf16[2,32,512]{2,1,0:T(8,128)(2,1)} %get-tuple-element.40), channel_id=1, source_target_pairs={{0,1},{1,2},{2,3},{3,0},{4,5},{5,6},{6,7},{7,4},{8,9},{9,10},{10,1... | collective-permute-start | bytes 196616 | tf_op jit(solution)/shard_map/ppermute | solution.py:27
  6.0 7.5 %collective-permute-start.1 = (bf16[2,32,512]{2,1,0:T(8,128)(2,1)}, bf16[2,32,512]{2,1,0:T(8,128)(2,1)S(1)}, u32[]{:S(2)}, u32[]{:S(2)}) collective-permute-start(bf16[2,32,512]{2,1,0:T(8,128)(2,1)} %get-tuple-element.44), channel_id=1, source_target_pairs={{0,2},{1,3},{2,0},{3,1},{4,6},{5,7},{6,4},{7,5},{8,10},{9,11},{10,... | collective-permute-start | bytes 196616 | tf_op jit(solution)/shard_map/ppermute | solution.py:27
  8.3 5.2 %collective-permute-start.2 = (bf16[2,32,512]{2,1,0:T(8,128)(2,1)}, bf16[2,32,512]{2,1,0:T(8,128)(2,1)S(1)}, u32[]{:S(2)}, u32[]{:S(2)}) collective-permute-start(bf16[2,32,512]{2,1,0:T(8,128)(2,1)} %get-tuple-element.45), channel_id=1, source_target_pairs={{0,3},{1,0},{2,1},{3,2},{4,7},{5,4},{6,5},{7,6},{8,11},{9,8},{10,9... | collective-permute-start | bytes 196616 | tf_op jit(solution)/shard_map/ppermute | solution.py:27
  10.3 31.7 %collective-permute-start.5 = (bf16[2,32,4096]{2,1,0:T(8,128)(2,1)}, bf16[2,32,4096]{2,1,0:T(8,128)(2,1)S(1)}, u32[]{:S(2)}, u32[]{:S(2)}) collective-permute-start(bf16[2,32,4096]{2,1,0:T(8,128)(2,1)} %get-tuple-element.46), channel_id=1, source_target_pairs={{0,3},{1,0},{2,1},{3,2},{4,7},{5,4},{6,5},{7,6},{8,11},{9,8},{10,9... | collective-permute-start | bytes 1572872 | tf_op jit(solution)/shard_map/ppermute | solution.py:27
  11.4 22.2 %collective-permute-start.6 = (bf16[2,32,4096]{2,1,0:T(8,128)(2,1)}, bf16[2,32,4096]{2,1,0:T(8,128)(2,1)S(1)}, u32[]{:S(2)}, u32[]{:S(2)}) collective-permute-start(bf16[2,32,4096]{2,1,0:T(8,128)(2,1)} %get-tuple-element.48), channel_id=1, source_target_pairs={{0,1},{1,2},{2,3},{3,0},{4,5},{5,6},{6,7},{7,4},{8,9},{9,10},{10,1... | collective-permute-start | bytes 1572872 | tf_op jit(solution)/shard_map/ppermute | solution.py:27
  13.6 10.6 %collective-permute-start.4 = (bf16[4,2,32,512]{3,2,1,0:T(8,128)(2,1)S(1)}, bf16[4,2,32,512]{3,2,1,0:T(8,128)(2,1)S(1)}, u32[]{:S(2)}, u32[]{:S(2)}) collective-permute-start(bf16[4,2,32,512]{3,2,1,0:T(8,128)(2,1)S(1)} %bitcast_dynamic-update-slice_fusion), channel_id=1, source_target_pairs={{0,4},{4,8},{8,12},{12,16},{16,20},{20,24},{24,28},{1,5},{5,9},{9,... | collective-permute-start | bytes 786440 | tf_op jit(solution)/shard_map/ppermute | solution.py:33
  16.0 10.2 %collective-permute-start.3 = (bf16[4,2,32,512]{3,2,1,0:T(8,128)(2,1)S(1)}, bf16[4,2,32,512]{3,2,1,0:T(8,128)(2,1)S(1)}, u32[]{:S(2)}, u32[]{:S(2)}) collective-permute-start(bf16[4,2,32,512]{3,2,1,0:T(8,128)(2,1)S(1)} %bitcast_dynamic-update-slice_fusion), channel_id=1, source_target_pairs={{0,8},{4,12},{8,16},{12,20},{16,24},{20,28},{1,9},{5,13},{9,17},{1... | collective-permute-start | bytes 786440 | tf_op jit(solution)/shard_map/ppermute | solution.py:33
  21.4 16.0 %copy-start.5 = (bf16[2,32,2048]{2,1,0:T(8,128)(2,1)S(1)}, bf16[2,32,2048]{2,1,0:T(8,128)(2,1)}, u32[]{:S(2)}) copy-start(bf16[2,32,2048]{2,1,0:T(8,128)(2,1)} %get-tuple-element.57) | copy-start | bytes 786436
  37.5 16.3 %collective-permute-start.8 = (bf16[2,32,2048]{2,1,0:T(8,128)(2,1)S(1)}, bf16[2,32,2048]{2,1,0:T(8,128)(2,1)S(1)}, u32[]{:S(2)}, u32[]{:S(2)}) collective-permute-start(bf16[2,32,2048]{2,1,0:T(8,128)(2,1)S(1)} %copy-done.5), channel_id=1, source_target_pairs={{0,2},{1,3},{2,0},{3,1},{4,6},{5,7},{6,4},{7,5},{8,10},{9,11},{10,... | collective-permute-start | bytes 786440 | tf_op jit(solution)/shard_map/ppermute | solution.py:27
  42.0 3.9 %copy-start = (bf16[4,32,4096]{2,1,0:T(8,128)(2,1)S(1)}, bf16[4,32,4096]{2,1,0:T(8,128)(2,1)}, u32[]{:S(2)}) copy-start(bf16[4,32,4096]{2,1,0:T(8,128)(2,1)} %query_ref.1) | copy-start | bytes 3145732
  42.0 3.9 %copy-start.1 = (bf16[4,32,4096]{2,1,0:T(8,128)(2,1)S(1)}, bf16[4,32,4096]{2,1,0:T(8,128)(2,1)}, u32[]{:S(2)}) copy-start(bf16[4,32,4096]{2,1,0:T(8,128)(2,1)} %grad_ref.1) | copy-start | bytes 3145732
  45.9 4.0 %copy-start.4 = (bf16[2,32,2048]{2,1,0:T(8,128)(2,1)S(1)}, bf16[2,32,2048]{2,1,0:T(8,128)(2,1)}, u32[]{:S(2)}) copy-start(bf16[2,32,2048]{2,1,0:T(8,128)(2,1)} %get-tuple-element.55) | copy-start | bytes 786436
  49.9 18.3 %collective-permute-start.7 = (bf16[2,32,2048]{2,1,0:T(8,128)(2,1)S(1)}, bf16[2,32,2048]{2,1,0:T(8,128)(2,1)S(1)}, u32[]{:S(2)}, u32[]{:S(2)}) collective-permute-start(bf16[2,32,2048]{2,1,0:T(8,128)(2,1)S(1)} %copy-done.4), channel_id=1, source_target_pairs={{0,2},{1,3},{2,0},{3,1},{4,6},{5,7},{6,4},{7,5},{8,10},{9,11},{10,... | collective-permute-start | bytes 786440 | tf_op jit(solution)/shard_map/ppermute | solution.py:27
  56.2 14.5 %collective-permute-start.9 = (bf16[2,128,256]{2,1,0:T(8,128)(2,1)S(1)}, bf16[2,128,256]{2,1,0:T(8,128)(2,1)S(1)}, u32[]{:S(2)}, u32[]{:S(2)}) collective-permute-start(bf16[2,128,256]{2,1,0:T(8,128)(2,1)S(1)} %get-tuple-element.62), channel_id=1, source_target_pairs={{4,0},{8,4},{12,8},{16,12},{20,16},{24,20},{28,24},{5,1},{9,5},{13... | collective-permute-start | bytes 393224 | tf_op jit(solution)/shard_map/ppermute | solution.py:33
  66.3 8.3 %collective-permute-start.10 = (bf16[2,128,256]{2,1,0:T(8,128)(2,1)S(1)}, bf16[2,128,256]{2,1,0:T(8,128)(2,1)S(1)}, u32[]{:S(2)}, u32[]{:S(2)}) collective-permute-start(bf16[2,128,256]{2,1,0:T(8,128)(2,1)S(1)} %get-tuple-element.63), channel_id=1, source_target_pairs={{8,0},{12,4},{16,8},{20,12},{24,16},{28,20},{9,1},{13,5},{17,9},{2... | collective-permute-start | bytes 393224 | tf_op jit(solution)/shard_map/ppermute | solution.py:33
  70.6 7.2 %collective-permute-start.11 = (bf16[2,128,256]{2,1,0:T(8,128)(2,1)S(1)}, bf16[2,128,256]{2,1,0:T(8,128)(2,1)S(1)}, u32[]{:S(2)}, u32[]{:S(2)}) collective-permute-start(bf16[2,128,256]{2,1,0:T(8,128)(2,1)S(1)} %get-tuple-element.67), channel_id=1, source_target_pairs={{4,0},{8,4},{12,8},{16,12},{20,16},{24,20},{28,24},{5,1},{9,5},{13... | collective-permute-start | bytes 393224 | tf_op jit(solution)/shard_map/ppermute | solution.py:33
  72.7 6.7 %collective-permute-start.12 = (bf16[2,128,256]{2,1,0:T(8,128)(2,1)S(1)}, bf16[2,128,256]{2,1,0:T(8,128)(2,1)S(1)}, u32[]{:S(2)}, u32[]{:S(2)}) collective-permute-start(bf16[2,128,256]{2,1,0:T(8,128)(2,1)S(1)} %get-tuple-element.68), channel_id=1, source_target_pairs={{8,0},{12,4},{16,8},{20,12},{24,16},{28,20},{9,1},{13,5},{17,9},{2... | collective-permute-start | bytes 393224 | tf_op jit(solution)/shard_map/ppermute | solution.py:33

commit v17 on v15

--- a/solution.py
+++ b/solution.py
@@ -12,7 +12,7 @@
 BIG_NEGATIVE = -1e30
 VMEM_BYTES = 32 * 1024 * 1024
 HEADS_STEP = 2
-CALL_COST = 30
+CALL_COST = (1, 1, 1, 100)
 
 
 def target_of(index, step, count):
@@ -39,9 +39,9 @@
     sources, refs = refs[:4], refs[4:]
     out_refs, held_refs, (in_sems, out_sems) = refs[:outs], refs[outs : 2 * outs], refs[-2:]
     loads, stores = [], []
-    for out, (first, step, start, width) in enumerate(jobs):
+    for out, (first, step, start, width, *_) in enumerate(jobs):
         chosen = assign_ref[target_of(group, step, count)]
-        for which in range(2):
+        for which in range(out_refs[out].shape[0]):
             origin = sources[first + which].at[chosen, :, start : start + width]
             held, slot = held_refs[out].at[which], 2 * out + which
             loads.append(pltpu.make_async_copy(origin, held, in_sems.at[slot]))
@@ -57,7 +57,7 @@
 
 def stage(assignment, arrays, jobs):
     count, rows, _ = arrays[0].shape
-    shapes = [(2, rows, width) for _, _, _, width in jobs]
+    shapes = [(job[4] if len(job) > 4 else 2, rows, job[3]) for job in jobs]
     kind = arrays[0].dtype
     far = pl.BlockSpec(memory_space=pltpu.HBM)
     return pl.pallas_call(
@@ -228,7 +228,7 @@
         out_shape.append(jax.ShapeDtypeStruct((2, keys, kv_width), jnp.float32))
         out_specs.append(acc_spec)
     pairs = span * ratio * rows * window
-    cost = CALL_COST if step and not last else 1
+    cost = CALL_COST[step] if step < len(CALL_COST) and not last else 1
     held = (keys, ratio * rows), (window, ratio * rows)
     held += ((2, keys, lanes),) * last
     return pl.pallas_call(
@@ -269,7 +269,8 @@
     others = [step for step in range(1, count) if step != final]
     jobs = [(2, step, 0, kv_width) for step in range(count)]
     jobs += [(0, step, 0, width) for step in others]
-    jobs += [(0, final, half * part, part) for half in range(halves)]
+    jobs += [(0, final, half * part, part) for half in range(halves - 1)]
+    jobs += [(which, final, (halves - 1) * part, part, 1) for which in range(2)]
     staged = stage(assignment, (queries, grad_out, keys, values), jobs)
     kv_staged, staged = staged[:count], list(staged[count:])
     kv_arrived = [exchanged(kv_staged[step], "dp", step) for step in range(1, count)]
@@ -289,15 +290,18 @@
     full, acc = attend(0, 0, kv_heads, *fixed, query, grad, kv, None, None, False)
     rows, acc = lax.optimization_barrier((held[0], acc))
     split = [exchanged(rows, "dp", final)]
-    for step, both in zip(others, arrived):
+    for at, (step, both) in enumerate(zip(others, arrived)):
         query, grad = (both, lambda m, a: 0), (both, lambda m, a: 1)
         full, acc = attend(step, 0, kv_heads, *fixed, query, grad, kv, acc, full, False)
-    for rows in held[1:]:
-        rows, split[-1], acc = lax.optimization_barrier((rows, split[-1], acc))
-        split.append(exchanged(rows, "dp", final))
+        if not at:
+            rows, acc = lax.optimization_barrier((held[1:], acc))
+            split += [exchanged(piece, "dp", final) for piece in rows]
     totals, returned = [], []
-    for half, both in enumerate(split):
+    for half in range(halves):
+        both = split[half]
         query, grad = (both, lambda m, a: 0), (both, lambda m, a: 1)
+        if half + 1 == halves:
+            grad = (split[half + 1], lambda m, a: 0)
         full, total, *halos = attend(
             final, half * HEADS_STEP, HEADS_STEP, *fixed, query, grad, kv, acc, full, True
         )

time: 75.9 us -> 74.9 us (0.987)
  waiting for transfers between devices: 21.1 us -> 18.4 us
  local copies, waits for them, and re-layouts: 0.93 us -> 3.24 us
  starting transfers between devices: 31 us -> 30.1 us
    ppermute x7 -> x8, waiting for transfers between devices: 15.4 us -> 9.34 us  [exchanged(): lax.ppermute(value, axis, [(i, (i + step) % count) for i in range(count)])]
    ppermute x6, waiting for transfers between devices: 5.72 us -> 9.06 us  [shifted(): return lax.ppermute(value, axis, pairs)]
    ppermute x6, starting transfers between devices: 21.1 us -> 18.9 us  [shifted(): return lax.ppermute(value, axis, pairs)]
    dynamic_update_slice x4, local copies, waits for them, and re-layouts: 0.88 us -> 2.55 us  [shards(): lax.dynamic_update_index_in_dim(kv_own, piece, source_of(group, step, cou...]
    ppermute x7 -> x8, starting transfers between devices: 9.91 us -> 11.2 us  [exchanged(): lax.ppermute(value, axis, [(i, (i + step) % count) for i in range(count)])]
  transfers between devices with their start and end apart: 13 -> 14, of which waited for: 7 -> 5; matrix products, arithmetic and copies ran while one was open for 3% -> 5% of each run, Pallas kernels for 22% -> 22%
where the time goes in v17:
time: 74.9 us; the launch traced here: 74.4 us
  starting transfers between devices  30.1 us (40%)
  Pallas kernels  19.8 us (26%)
  waiting for transfers between devices  18.4 us (25%)
  local copies, waits for them, and re-layouts  3.24 us (4%)
  other arithmetic  2.01 us (3%)
  between operations  0.85 us (1%)
    ppermute x6, starting transfers between devices, shifted(): return lax.ppermute(value, axis, pairs)  18.9 us
    pallas_call x5, Pallas kernels, attend(): pl.pallas_call(functools.partial(attend_kernel, step, first, filled, last...  16.6 us
    ppermute x8, starting transfers between devices, exchanged(): lax.ppermute(value, axis, [(i, (i + step) % count) for i in range(count)])  11.2 us
    ppermute x8, waiting for transfers between devices, exchanged(): lax.ppermute(value, axis, [(i, (i + step) % count) for i in range(count)])  9.34 us
    ppermute x6, waiting for transfers between devices, shifted(): return lax.ppermute(value, axis, pairs)  9.06 us
    pallas_call x1, Pallas kernels, stage(): pl.pallas_call(functools.partial(stage_kernel, count, jobs, len(jobs)), o...  3.23 us
    dynamic_update_slice x4, local copies, waits for them, and re-layouts, shards(): lax.dynamic_update_index_in_dim(kv_own, piece, source_of(group, step, cou...  2.55 us
  transfers between devices with their start and end apart: 14, of which 5 were waited for; matrix products, arithmetic and copies ran while one was open for 5% of the time, Pallas kernels for 22%

profile of v17, /device:TPU:1, one launch (start us, length us, event | category | flops | bytes accessed | tf_op | source)
XLA Modules:
  0.0 74.4 jit_solution(13233654170795407137)
XLA Ops:
  0.6 3.2 %stage.1 = (bf16[2,32,512]{2,1,0:T(8,128)(2,1)}, bf16[2,32,512]{2,1,0:T(8,128)(2,1)}, bf16[2,32,512]{2,1,0:T(8,128)(2,1)}, bf16[2,32,512]{2,1,0:T(8,128)(2,1)}, ...) custom-call(s32[4]{0:T(128)} %assign_ref.11, ...), custom_call_target="tpu_custom_call" | custom-call | tf_op jit(solution)/shard_map/stage/pallas_call | solution.py:63
  3.9 2.2 %collective-permute-start = (bf16[2,32,512]{2,1,0:T(8,128)(2,1)}, bf16[2,32,512]{2,1,0:T(8,128)(2,1)S(1)}, u32[]{:S(2)}, u32[]{:S(2)}) collective-permute-start(bf16[2,32,512]{2,1,0:T(8,128)(2,1)} %get-tuple-element.44), channel_id=1, source_target_pairs={{0,1},{1,2},{2,3},{3,0},{4,5},{5,6},{6,7},{7,4},{8,9},{9,10},{10,1... | collective-permute-start | bytes 196616 | tf_op jit(solution)/shard_map/ppermute | solution.py:28
  6.1 2.3 %collective-permute-start.2 = (bf16[2,32,512]{2,1,0:T(8,128)(2,1)}, bf16[2,32,512]{2,1,0:T(8,128)(2,1)}, u32[]{:S(2)}, u32[]{:S(2)}) collective-permute-start(bf16[2,32,512]{2,1,0:T(8,128)(2,1)} %get-tuple-element.50), channel_id=1, source_target_pairs={{0,2},{1,3},{2,0},{3,1},{4,6},{5,7},{6,4},{7,5},{8,10},{9,11},{10,... | collective-permute-start | bytes 196616 | tf_op jit(solution)/shard_map/ppermute | solution.py:28
  8.4 1.1 %collective-permute-start.3 = (bf16[2,32,512]{2,1,0:T(8,128)(2,1)}, bf16[2,32,512]{2,1,0:T(8,128)(2,1)S(1)}, u32[]{:S(2)}, u32[]{:S(2)}) collective-permute-start(bf16[2,32,512]{2,1,0:T(8,128)(2,1)} %get-tuple-element.51), channel_id=1, source_target_pairs={{0,3},{1,0},{2,1},{3,2},{4,7},{5,4},{6,5},{7,6},{8,11},{9,8},{10,9... | collective-permute-start | bytes 196616 | tf_op jit(solution)/shard_map/ppermute | solution.py:28
  9.5 0.9 %bitcast_dynamic-update-slice_fusion.3 = bf16[4,2,32,512]{3,2,1,0:T(8,128)(2,1)S(1)} fusion(bf16[4,2,32,512]{3,2,1,0:T(8,128)(2,1)S(1)} %broadcast_in_dim.19, s32[]{:T(128)S(6)} %select_n.13, bf16[2,32,512]{2,1,0:T(8,128)(2,1)} %get-tuple-element.48), kind=kLoop, calls=%fused_computation.10 | loop fusion | bytes 131076 | tf_op jit(solution)/shard_map/jit(dynamic_update_index_in_dim)/dynamic_update_slice | solution.py:282
  11.4 2.9 %collective-permute-start.8 = (bf16[2,32,4096]{2,1,0:T(8,128)(2,1)}, bf16[2,32,4096]{2,1,0:T(8,128)(2,1)S(1)}, u32[]{:S(2)}, u32[]{:S(2)}) collective-permute-start(bf16[2,32,4096]{2,1,0:T(8,128)(2,1)} %get-tuple-element.59), channel_id=1, source_target_pairs={{0,3},{1,0},{2,1},{3,2},{4,7},{5,4},{6,5},{7,6},{8,11},{9,8},{10,9... | collective-permute-start | bytes 1572872 | tf_op jit(solution)/shard_map/ppermute | solution.py:28
  16.0 3.1 %collective-permute-start.5 = (bf16[4,2,32,512]{3,2,1,0:T(8,128)(2,1)S(1)}, bf16[4,2,32,512]{3,2,1,0:T(8,128)(2,1)}, u32[]{:S(2)}, u32[]{:S(2)}) collective-permute-start(bf16[4,2,32,512]{3,2,1,0:T(8,128)(2,1)S(1)} %bitcast_dynamic-update-slice_fusion), channel_id=1, source_target_pairs={{0,4},{4,8},{8,12},{12,16},{16,20},{20,24},{24,28},{1,5},{5,9},{9,... | collective-permute-start | bytes 786440 | tf_op jit(solution)/shard_map/ppermute | solution.py:34
  19.1 5.7 %collective-permute-start.4 = (bf16[4,2,32,512]{3,2,1,0:T(8,128)(2,1)S(1)}, bf16[4,2,32,512]{3,2,1,0:T(8,128)(2,1)}, u32[]{:S(2)}, u32[]{:S(2)}) collective-permute-start(bf16[4,2,32,512]{3,2,1,0:T(8,128)(2,1)S(1)} %bitcast_dynamic-update-slice_fusion), channel_id=1, source_target_pairs={{0,8},{4,12},{8,16},{12,20},{16,24},{20,28},{1,9},{5,13},{9,17},{1... | collective-permute-start | bytes 786440 | tf_op jit(solution)/shard_map/ppermute | solution.py:34
  24.9 2.7 %collective-permute-done.5 = bf16[4,2,32,512]{3,2,1,0:T(8,128)(2,1)} collective-permute-done((bf16[4,2,32,512]{3,2,1,0:T(8,128)(2,1)S(1)}, bf16[4,2,32,512]{3,2,1,0:T(8,128)(2,1)}, u32[]{:S(2)}, u32[]{:S(2)}) %collective-permute-start.5) | collective-permute-done | bytes 262176 | tf_op jit(solution)/shard_map/ppermute | solution.py:34
  27.6 2.0 %collective-permute-done.4 = bf16[4,2,32,512]{3,2,1,0:T(8,128)(2,1)} collective-permute-done((bf16[4,2,32,512]{3,2,1,0:T(8,128)(2,1)S(1)}, bf16[4,2,32,512]{3,2,1,0:T(8,128)(2,1)}, u32[]{:S(2)}, u32[]{:S(2)}) %collective-permute-start.4) | collective-permute-done | bytes 262176 | tf_op jit(solution)/shard_map/ppermute | solution.py:34
  29.6 1.1 %pad_maximum_fusion.kv_ref = bf16[12,2,32,512]{3,2,1,0:T(8,128)(2,1)S(1)} fusion(bf16[4,2,32,512]{3,2,1,0:T(8,128)(2,1)S(1)} %bitcast_dynamic-update-slice_fusion, bf16[4,2,32,512]{3,2,1,0:T(8,128)(2,1)} %collective-permute-done.5, bf16[4,2,32,512]{3,2,1,0:T(8,128)(2,1)} %collective-permute-done.4), kind=kLoop, calls=%fused_computation | loop fusion | flops 786432 | bytes 1572864 | tf_op jit(solution)/shard_map/concatenate | solution.py:286
  30.8 3.9 %attend.5 = (bf16[128,32,128]{2,1,0:T(8,128)(2,1)}, f32[2,384,512]{2,1,0:T(8,128)S(1)}) custom-call(s32[2]{0:T(128)S(1)} %pad_add_fusion.meta_ref, s32[4]{0:T(128)S(1)} %copy-done.3, s32[4,1024]{1,0:T(4,128)S(1)} %copy-done.2, bf16[4,32,4096]{2,1,0:T(8,128)(2,1)S(1)} %copy-done, bf16[4,32,4096]{2,1,0:T(8,128)(2,1)S(1)} %copy-done.1, ...), custom_call_target="tpu_custom_call" | custom-call | flops 37748736 | bytes 294912 | tf_op jit(solution)/shard_map/attend/pallas_call | solution.py:234
  34.8 3.9 %attend.6 = (bf16[128,32,128]{2,1,0:T(8,128)(2,1)}, f32[2,384,512]{2,1,0:T(8,128)S(1)}) custom-call(s32[2]{0:T(128)S(1)} %pad_add_fusion.meta_ref, s32[4]{0:T(128)S(1)} %copy-done.3, s32[4,1024]{1,0:T(4,128)S(1)} %copy-done.2, bf16[2,32,4096]{2,1,0:T(8,128)(2,1)S(1)} %collective-permute-done.1.query_ref.grad_ref, ...), custom_call_target="tpu_custom_call", output_to_operand_aliasing={{1}: (6, {}), {0}: (7, {})} | custom-call | flops 37748736 | bytes 294912 | tf_op jit(solution)/shard_map/attend/pallas_call | solution.py:234
  38.7 2.3 %collective-permute-start.6 = (bf16[1,32,2048]{2,1,0:T(8,128)(2,1)S(1)}, bf16[1,32,2048]{2,1,0:T(8,128)(2,1)S(1)}, u32[]{:S(2)}, u32[]{:S(2)}) collective-permute-start(bf16[1,32,2048]{2,1,0:T(8,128)(2,1)S(1)} %copy-done.7), channel_id=1, source_target_pairs={{0,2},{1,3},{2,0},{3,1},{4,6},{5,7},{6,4},{7,5},{8,10},{9,11},{10,... | collective-permute-start | bytes 393224 | tf_op jit(solution)/shard_map/ppermute | solution.py:28
  41.1 3.9 %attend.7 = (bf16[128,32,128]{2,1,0:T(8,128)(2,1)}, f32[2,384,512]{2,1,0:T(8,128)S(1)}) custom-call(s32[2]{0:T(128)S(1)} %pad_add_fusion.meta_ref, s32[4]{0:T(128)S(1)} %copy-done.3, s32[4,1024]{1,0:T(4,128)S(1)} %copy-done.2, bf16[2,32,4096]{2,1,0:T(8,128)(2,1)S(1)} %collective-permute-done.8.query_ref.grad_ref, ...), custom_call_target="tpu_custom_call", output_to_operand_aliasing={{1}: (6, {}), {0}: (7, {})} | custom-call | flops 3774873600 | bytes 29491200 | tf_op jit(solution)/shard_map/attend/pallas_call | solution.py:234
  45.1 9.3 %collective-permute-done.9.query_ref.grad_ref = bf16[2,32,2048]{2,1,0:T(8,128)(2,1)S(1)} collective-permute-done((bf16[2,32,2048]{2,1,0:T(8,128)(2,1)S(1)}, bf16[2,32,2048]{2,1,0:T(8,128)(2,1)S(1)}, u32[]{:S(2)}, u32[]{:S(2)}) %collective-permute-start.9) | collective-permute-done | bytes 262176 | tf_op jit(solution)/shard_map/ppermute | solution.py:28
  54.4 2.4 %attend.8 = (bf16[128,32,128]{2,1,0:T(8,128)(2,1)}, f32[2,128,256]{2,1,0:T(8,128)S(1)}, bf16[2,128,256]{2,1,0:T(8,128)(2,1)S(1)}, bf16[2,128,256]{2,1,0:T(8,128)(2,1)S(1)}) custom-call(s32[2]{0:T(128)S(1)} %pad_add_fusion.meta_ref, s32[4]{0:T(128)S(1)} %copy-done.3, s32[4,1024]{1,0:T(4,128)S(1)} %copy-done.2, ...), custom_call_target="tpu_custom_call", output_to_operand_aliasing={{0}: (7, {})} | custom-call | flops 18874368 | bytes 147456 | tf_op jit(solution)/shard_map/attend/pallas_call | solution.py:234
  56.8 4.3 %collective-permute-start.10 = (bf16[2,128,256]{2,1,0:T(8,128)(2,1)S(1)}, bf16[2,128,256]{2,1,0:T(8,128)(2,1)S(1)}, u32[]{:S(2)}, u32[]{:S(2)}) collective-permute-start(bf16[2,128,256]{2,1,0:T(8,128)(2,1)S(1)} %get-tuple-element.68), channel_id=1, source_target_pairs={{4,0},{8,4},{12,8},{16,12},{20,16},{24,20},{28,24},{5,1},{9,5},{13... | collective-permute-start | bytes 393224 | tf_op jit(solution)/shard_map/ppermute | solution.py:34
  61.1 1.9 %collective-permute-start.11 = (bf16[2,128,256]{2,1,0:T(8,128)(2,1)S(1)}, bf16[2,128,256]{2,1,0:T(8,128)(2,1)S(1)}, u32[]{:S(2)}, u32[]{:S(2)}) collective-permute-start(bf16[2,128,256]{2,1,0:T(8,128)(2,1)S(1)} %get-tuple-element.69), channel_id=1, source_target_pairs={{8,0},{12,4},{16,8},{20,12},{24,16},{28,20},{9,1},{13,5},{17,9},{2... | collective-permute-start | bytes 393224 | tf_op jit(solution)/shard_map/ppermute | solution.py:34
  63.1 2.4 %attend.9 = (bf16[128,32,128]{2,1,0:T(8,128)(2,1)}, f32[2,128,256]{2,1,0:T(8,128)S(1)}, bf16[2,128,256]{2,1,0:T(8,128)(2,1)S(1)}, bf16[2,128,256]{2,1,0:T(8,128)(2,1)S(1)}) custom-call(s32[2]{0:T(128)S(1)} %pad_add_fusion.meta_ref, s32[4]{0:T(128)S(1)} %copy-done.3, s32[4,1024]{1,0:T(4,128)S(1)} %copy-done.2, ...), custom_call_target="tpu_custom_call", output_to_operand_aliasing={{0}: (7, {})} | custom-call | flops 18874368 | bytes 147456 | tf_op jit(solution)/shard_map/attend/pallas_call | solution.py:234
  65.5 1.9 %collective-permute-start.12 = (bf16[2,128,256]{2,1,0:T(8,128)(2,1)S(1)}, bf16[2,128,256]{2,1,0:T(8,128)(2,1)S(1)}, u32[]{:S(2)}, u32[]{:S(2)}) collective-permute-start(bf16[2,128,256]{2,1,0:T(8,128)(2,1)S(1)} %get-tuple-element.73), channel_id=1, source_target_pairs={{4,0},{8,4},{12,8},{16,12},{20,16},{24,20},{28,24},{5,1},{9,5},{13... | collective-permute-start | bytes 393224 | tf_op jit(solution)/shard_map/ppermute | solution.py:34
  67.4 1.9 %collective-permute-start.13 = (bf16[2,128,256]{2,1,0:T(8,128)(2,1)S(1)}, bf16[2,128,256]{2,1,0:T(8,128)(2,1)S(1)}, u32[]{:S(2)}, u32[]{:S(2)}) collective-permute-start(bf16[2,128,256]{2,1,0:T(8,128)(2,1)S(1)} %get-tuple-element.74), channel_id=1, source_target_pairs={{8,0},{12,4},{16,8},{20,12},{24,16},{28,20},{9,1},{13,5},{17,9},{2... | collective-permute-start | bytes 393224 | tf_op jit(solution)/shard_map/ppermute | solution.py:34
  69.4 2.7 %collective-permute-done.12 = bf16[2,128,256]{2,1,0:T(8,128)(2,1)S(1)} collective-permute-done((bf16[2,128,256]{2,1,0:T(8,128)(2,1)S(1)}, bf16[2,128,256]{2,1,0:T(8,128)(2,1)S(1)}, u32[]{:S(2)}, u32[]{:S(2)}) %collective-permute-start.12) | collective-permute-done | bytes 131104 | tf_op jit(solution)/shard_map/ppermute | solution.py:34
  72.1 1.6 %collective-permute-done.13 = bf16[2,128,256]{2,1,0:T(8,128)(2,1)S(1)} collective-permute-done((bf16[2,128,256]{2,1,0:T(8,128)(2,1)S(1)}, bf16[2,128,256]{2,1,0:T(8,128)(2,1)S(1)}, u32[]{:S(2)}, u32[]{:S(2)}) %collective-permute-start.13) | collective-permute-done | bytes 131104 | tf_op jit(solution)/shard_map/ppermute | solution.py:34
  (36 shorter events, 3.8 us)
Async XLA Ops:
  3.9 26.9 %copy-start = (bf16[4,32,4096]{2,1,0:T(8,128)(2,1)S(1)}, bf16[4,32,4096]{2,1,0:T(8,128)(2,1)}, u32[]{:S(2)}) copy-start(bf16[4,32,4096]{2,1,0:T(8,128)(2,1)} %query_ref.1) | copy-start | bytes 3145732
  3.9 26.9 %copy-start.1 = (bf16[4,32,4096]{2,1,0:T(8,128)(2,1)S(1)}, bf16[4,32,4096]{2,1,0:T(8,128)(2,1)}, u32[]{:S(2)}) copy-start(bf16[4,32,4096]{2,1,0:T(8,128)(2,1)} %grad_ref.1) | copy-start | bytes 3145732
  3.9 26.9 %copy-start.2 = (s32[4,1024]{1,0:T(4,128)S(1)}, s32[4,1024]{1,0:T(4,128)}, u32[]{:S(2)}) copy-start(s32[4,1024]{1,0:T(4,128)} %segment_ref.9) | copy-start | bytes 49156
  3.9 26.9 %copy-start.3 = (s32[4]{0:T(128)S(1)}, s32[4]{0:T(128)}, u32[]{:S(2)}) copy-start(s32[4]{0:T(128)} %assign_ref.11) | copy-start | bytes 52
  3.9 6.4 %collective-permute-start = (bf16[2,32,512]{2,1,0:T(8,128)(2,1)}, bf16[2,32,512]{2,1,0:T(8,128)(2,1)S(1)}, u32[]{:S(2)}, u32[]{:S(2)}) collective-permute-start(bf16[2,32,512]{2,1,0:T(8,128)(2,1)} %get-tuple-element.44), channel_id=1, source_target_pairs={{0,1},{1,2},{2,3},{3,0},{4,5},{5,6},{6,7},{7,4},{8,9},{9,10},{10,1... | collective-permute-start | bytes 196616 | tf_op jit(solution)/shard_map/ppermute | solution.py:28
  6.1 9.0 %collective-permute-start.2 = (bf16[2,32,512]{2,1,0:T(8,128)(2,1)}, bf16[2,32,512]{2,1,0:T(8,128)(2,1)}, u32[]{:S(2)}, u32[]{:S(2)}) collective-permute-start(bf16[2,32,512]{2,1,0:T(8,128)(2,1)} %get-tuple-element.50), channel_id=1, source_target_pairs={{0,2},{1,3},{2,0},{3,1},{4,6},{5,7},{6,4},{7,5},{8,10},{9,11},{10,... | collective-permute-start | bytes 196616 | tf_op jit(solution)/shard_map/ppermute | solution.py:28
  8.4 7.5 %collective-permute-start.3 = (bf16[2,32,512]{2,1,0:T(8,128)(2,1)}, bf16[2,32,512]{2,1,0:T(8,128)(2,1)S(1)}, u32[]{:S(2)}, u32[]{:S(2)}) collective-permute-start(bf16[2,32,512]{2,1,0:T(8,128)(2,1)} %get-tuple-element.51), channel_id=1, source_target_pairs={{0,3},{1,0},{2,1},{3,2},{4,7},{5,4},{6,5},{7,6},{8,11},{9,8},{10,9... | collective-permute-start | bytes 196616 | tf_op jit(solution)/shard_map/ppermute | solution.py:28
  10.4 0.6 copy-start.4
  11.0 23.8 %collective-permute-start.1 = (bf16[2,32,4096]{2,1,0:T(8,128)(2,1)}, bf16[2,32,4096]{2,1,0:T(8,128)(2,1)S(1)}, u32[]{:S(2)}, u32[]{:S(2)}) collective-permute-start(bf16[2,32,4096]{2,1,0:T(8,128)(2,1)} %get-tuple-element.47), channel_id=1, source_target_pairs={{0,1},{1,2},{2,3},{3,0},{4,5},{5,6},{6,7},{7,4},{8,9},{9,10},{10,1... | collective-permute-start | bytes 1572872 | tf_op jit(solution)/shard_map/ppermute | solution.py:28
  11.4 29.7 %collective-permute-start.8 = (bf16[2,32,4096]{2,1,0:T(8,128)(2,1)}, bf16[2,32,4096]{2,1,0:T(8,128)(2,1)S(1)}, u32[]{:S(2)}, u32[]{:S(2)}) collective-permute-start(bf16[2,32,4096]{2,1,0:T(8,128)(2,1)} %get-tuple-element.59), channel_id=1, source_target_pairs={{0,3},{1,0},{2,1},{3,2},{4,7},{5,4},{6,5},{7,6},{8,11},{9,8},{10,9... | collective-permute-start | bytes 1572872 | tf_op jit(solution)/shard_map/ppermute | solution.py:28
  16.0 11.7 %collective-permute-start.5 = (bf16[4,2,32,512]{3,2,1,0:T(8,128)(2,1)S(1)}, bf16[4,2,32,512]{3,2,1,0:T(8,128)(2,1)}, u32[]{:S(2)}, u32[]{:S(2)}) collective-permute-start(bf16[4,2,32,512]{3,2,1,0:T(8,128)(2,1)S(1)} %bitcast_dynamic-update-slice_fusion), channel_id=1, source_target_pairs={{0,4},{4,8},{8,12},{12,16},{16,20},{20,24},{24,28},{1,5},{5,9},{9,... | collective-permute-start | bytes 786440 | tf_op jit(solution)/shard_map/ppermute | solution.py:34
  19.1 10.5 %collective-permute-start.4 = (bf16[4,2,32,512]{3,2,1,0:T(8,128)(2,1)S(1)}, bf16[4,2,32,512]{3,2,1,0:T(8,128)(2,1)}, u32[]{:S(2)}, u32[]{:S(2)}) collective-permute-start(bf16[4,2,32,512]{3,2,1,0:T(8,128)(2,1)S(1)} %bitcast_dynamic-update-slice_fusion), channel_id=1, source_target_pairs={{0,8},{4,12},{8,16},{12,20},{16,24},{20,28},{1,9},{5,13},{9,17},{1... | collective-permute-start | bytes 786440 | tf_op jit(solution)/shard_map/ppermute | solution.py:34
  30.8 3.9 %copy-start.5 = (bf16[2,32,2048]{2,1,0:T(8,128)(2,1)S(1)}, bf16[2,32,2048]{2,1,0:T(8,128)(2,1)}, u32[]{:S(2)}) copy-start(bf16[2,32,2048]{2,1,0:T(8,128)(2,1)} %get-tuple-element.63) | copy-start | bytes 786436
  34.7 19.6 %collective-permute-start.9 = (bf16[2,32,2048]{2,1,0:T(8,128)(2,1)S(1)}, bf16[2,32,2048]{2,1,0:T(8,128)(2,1)S(1)}, u32[]{:S(2)}, u32[]{:S(2)}) collective-permute-start(bf16[2,32,2048]{2,1,0:T(8,128)(2,1)S(1)} %copy-done.5), channel_id=1, source_target_pairs={{0,2},{1,3},{2,0},{3,1},{4,6},{5,7},{6,4},{7,5},{8,10},{9,11},{10,... | collective-permute-start | bytes 786440 | tf_op jit(solution)/shard_map/ppermute | solution.py:28
  34.8 4.0 %copy-start.7 = (bf16[1,32,2048]{2,1,0:T(8,128)(2,1)S(1)}, bf16[1,32,2048]{2,1,0:T(8,128)(2,1)}, u32[]{:S(2)}) copy-start(bf16[1,32,2048]{2,1,0:T(8,128)(2,1)} %get-tuple-element.57) | copy-start | bytes 393220
  34.8 6.3 %copy-start.6 = (bf16[1,32,2048]{2,1,0:T(8,128)(2,1)S(1)}, bf16[1,32,2048]{2,1,0:T(8,128)(2,1)}, u32[]{:S(2)}) copy-start(bf16[1,32,2048]{2,1,0:T(8,128)(2,1)} %get-tuple-element.58) | copy-start | bytes 393220
  38.7 24.3 %collective-permute-start.6 = (bf16[1,32,2048]{2,1,0:T(8,128)(2,1)S(1)}, bf16[1,32,2048]{2,1,0:T(8,128)(2,1)S(1)}, u32[]{:S(2)}, u32[]{:S(2)}) collective-permute-start(bf16[1,32,2048]{2,1,0:T(8,128)(2,1)S(1)} %copy-done.7), channel_id=1, source_target_pairs={{0,2},{1,3},{2,0},{3,1},{4,6},{5,7},{6,4},{7,5},{8,10},{9,11},{10,... | collective-permute-start | bytes 393224 | tf_op jit(solution)/shard_map/ppermute | solution.py:28
  41.1 22.0 %collective-permute-start.7 = (bf16[1,32,2048]{2,1,0:T(8,128)(2,1)S(1)}, bf16[1,32,2048]{2,1,0:T(8,128)(2,1)S(1)}, u32[]{:S(2)}, u32[]{:S(2)}) collective-permute-start(bf16[1,32,2048]{2,1,0:T(8,128)(2,1)S(1)} %copy-done.6), channel_id=1, source_target_pairs={{0,2},{1,3},{2,0},{3,1},{4,6},{5,7},{6,4},{7,5},{8,10},{9,11},{10,... | collective-permute-start | bytes 393224 | tf_op jit(solution)/shard_map/ppermute | solution.py:28
  56.8 8.7 %collective-permute-start.10 = (bf16[2,128,256]{2,1,0:T(8,128)(2,1)S(1)}, bf16[2,128,256]{2,1,0:T(8,128)(2,1)S(1)}, u32[]{:S(2)}, u32[]{:S(2)}) collective-permute-start(bf16[2,128,256]{2,1,0:T(8,128)(2,1)S(1)} %get-tuple-element.68), channel_id=1, source_target_pairs={{4,0},{8,4},{12,8},{16,12},{20,16},{24,20},{28,24},{5,1},{9,5},{13... | collective-permute-start | bytes 393224 | tf_op jit(solution)/shard_map/ppermute | solution.py:34
  61.1 8.2 %collective-permute-start.11 = (bf16[2,128,256]{2,1,0:T(8,128)(2,1)S(1)}, bf16[2,128,256]{2,1,0:T(8,128)(2,1)S(1)}, u32[]{:S(2)}, u32[]{:S(2)}) collective-permute-start(bf16[2,128,256]{2,1,0:T(8,128)(2,1)S(1)} %get-tuple-element.69), channel_id=1, source_target_pairs={{8,0},{12,4},{16,8},{20,12},{24,16},{28,20},{9,1},{13,5},{17,9},{2... | collective-permute-start | bytes 393224 | tf_op jit(solution)/shard_map/ppermute | solution.py:34
  65.5 6.7 %collective-permute-start.12 = (bf16[2,128,256]{2,1,0:T(8,128)(2,1)S(1)}, bf16[2,128,256]{2,1,0:T(8,128)(2,1)S(1)}, u32[]{:S(2)}, u32[]{:S(2)}) collective-permute-start(bf16[2,128,256]{2,1,0:T(8,128)(2,1)S(1)} %get-tuple-element.73), channel_id=1, source_target_pairs={{4,0},{8,4},{12,8},{16,12},{20,16},{24,20},{28,24},{5,1},{9,5},{13... | collective-permute-start | bytes 393224 | tf_op jit(solution)/shard_map/ppermute | solution.py:34
  67.4 6.3 %collective-permute-start.13 = (bf16[2,128,256]{2,1,0:T(8,128)(2,1)S(1)}, bf16[2,128,256]{2,1,0:T(8,128)(2,1)S(1)}, u32[]{:S(2)}, u32[]{:S(2)}) collective-permute-start(bf16[2,128,256]{2,1,0:T(8,128)(2,1)S(1)} %get-tuple-element.74), channel_id=1, source_target_pairs={{8,0},{12,4},{16,8},{20,12},{24,16},{28,20},{9,1},{13,5},{17,9},{2... | collective-permute-start | bytes 393224 | tf_op jit(solution)/shard_map/ppermute | solution.py:34

commit v18 on v17

--- a/solution.py
+++ b/solution.py
@@ -104,7 +104,7 @@
 
 
 def attend_kernel(
-    step, first, filled, last, tok_dev, reach, ratio,
+    step, place, first, filled, last, tok_dev, reach, ratio,
     meta_ref, assign_ref, segment_ref, query_ref, grad_ref, kv_ref, *refs,
 ):
     refs = list(refs)
@@ -113,9 +113,9 @@
     if filled:
         refs.pop(0)
     query_out_ref = refs.pop(0)
-    column_ref, bias_ref = refs[-2 - last], refs[-1 - last]
+    column_ref, bias_ref, fetch_sem = refs[-3 - last : len(refs) - last]
     if last:
-        own_ref, halo_refs, acc_ref = refs[0], refs[1:-3], refs[-1]
+        own_ref, halo_refs, acc_ref = refs[0], refs[1:-4], refs[-1]
     else:
         acc_ref = refs[0]
 
@@ -134,42 +134,55 @@
             source, assign_ref[group], meta_ref[1], segment_ref, column_ref, bias_ref, rows, tok_dev, reach
         )
 
-    acc_ref[...] = jnp.zeros_like(acc_ref) if first else acc_in_ref[...]
-    turned = (((1,), (1,)), ((), ()))
+    if first:
+        acc_ref[...] = jnp.zeros_like(acc_ref)
+    else:
+        start = pl.multiple_of((place + pl.program_id(0)) * HEADS_STEP * HD, HEADS_STEP * HD)
+        fetch = pltpu.make_async_copy(
+            acc_in_ref.at[:, :, pl.ds(start, HEADS_STEP * HD)], acc_ref, fetch_sem
+        )
+        fetch.start()
+    turned, across = (((1,), (1,)), ((), ())), (((0,), (0,)), ((), ()))
+    heads = range(HEADS_STEP)
+    lanes = [slice(head * HD, (head + 1) * HD) for head in heads]
+
+    def product(left, right, contract):
+        return lax.dot_general(left, right, contract, preferred_element_type=jnp.float32)
+
+    def stacked(ref, head):
+        start = head * ratio
+        return jnp.concatenate(
+            [ref[:, r * HD : (r + 1) * HD] for r in range(start, start + ratio)], axis=0
+        )
+
+    def windowed(which, head):
+        return kv_ref[pl.ds(block, window // rows), which, :, lanes[head]].reshape(window, HD)
+
+    plain = (((1,), (0,)), ((), ()))
+    query, key = [stacked(query_ref, head) for head in heads], [windowed(0, head) for head in heads]
+    scores = [product(key[head], query[head], turned) for head in heads]
+    grad, value = [stacked(grad_ref, head) for head in heads], [windowed(1, head) for head in heads]
+    grad_probs = [product(value[head], grad[head], turned) for head in heads]
+    probs, grad_scores = [], []
+    for head in heads:
+        score = scores[head] * (scale * LOG2E) + bias_ref[...]
+        weights = jnp.exp2(score - jnp.max(score, axis=0, keepdims=True))
+        probs.append(weights * (1.0 / jnp.sum(weights, axis=0, keepdims=True)))
+    for head in heads:
+        weighted = probs[head] * grad_probs[head]
+        delta = jnp.sum(weighted, axis=0, keepdims=True)
+        grad_scores.append((weighted - probs[head] * delta).astype(jnp.bfloat16))
     grads = []
-    for head in range(HEADS_STEP):
-        lanes = slice(head * HD, (head + 1) * HD)
-
-        def stacked(ref):
-            start = head * ratio
-            return jnp.concatenate(
-                [ref[:, r * HD : (r + 1) * HD] for r in range(start, start + ratio)], axis=0
-            )
-
-        def windowed(which):
-            return kv_ref[pl.ds(block, window // rows), which, :, lanes].reshape(window, HD)
-
-        query, grad = stacked(query_ref), stacked(grad_ref)
-        key, value = windowed(0), windowed(1)
-        scores = lax.dot_general(key, query, turned, preferred_element_type=jnp.float32)
-        scores = scores * (scale * LOG2E) + bias_ref[...]
-        top = jnp.max(scores, axis=0, keepdims=True)
-        weights = jnp.exp2(scores - top)
-        probs = weights * (1.0 / jnp.sum(weights, axis=0, keepdims=True))
-        grad_probs = lax.dot_general(value, grad, turned, preferred_element_type=jnp.float32)
-        product = probs * grad_probs
-        delta = jnp.sum(product, axis=0, keepdims=True)
-        grad_scores = (product - probs * delta).astype(jnp.bfloat16)
-        grad_value = jnp.dot(
-            probs.astype(jnp.bfloat16), grad, preferred_element_type=jnp.float32
-        )
-        grad_key = jnp.dot(grad_scores, query, preferred_element_type=jnp.float32)
-        grad_query = lax.dot_general(
-            grad_scores, key, (((0,), (0,)), ((), ())), preferred_element_type=jnp.float32
-        )
+    for head in heads:
+        grad_query = product(grad_scores[head], key[head], across)
         grads.append((grad_query * scale).reshape(ratio, rows, HD))
-        acc_ref[0, span, lanes] += grad_key
-        acc_ref[1, span, lanes] += grad_value
+    grad_key = [product(grad_scores[head], query[head], plain) for head in heads]
+    grad_value = [product(probs[head].astype(jnp.bfloat16), grad[head], plain) for head in heads]
+    if not first:
+        fetch.wait()
+    for head in heads:
+        acc_ref[0, span, lanes[head]] += grad_key[head]
+        acc_ref[1, span, lanes[head]] += grad_value[head]
     if last:
         own_ref[0] = acc_ref[0, keys - tok_dev :] * scale
         own_ref[1] = acc_ref[1, keys - tok_dev :]
@@ -207,7 +220,7 @@
         if not last:
             aliases[len(operands)] = 1
         operands.append(acc)
-        in_specs.append(acc_spec)
+        in_specs.append(pl.BlockSpec(memory_space=pl.ANY))
     if filled:
         aliases[len(operands)] = 0
         operands.append(full)
@@ -229,17 +242,18 @@
         out_specs.append(acc_spec)
     pairs = span * ratio * rows * window
     cost = CALL_COST[step] if step < len(CALL_COST) and not last else 1
-    held = (keys, ratio * rows), (window, ratio * rows)
-    held += ((2, keys, lanes),) * last
+    held = [pltpu.VMEM((held, ratio * rows), jnp.float32) for held in (keys, window)]
+    held.append(pltpu.SemaphoreType.DMA)
+    held += [pltpu.VMEM((2, keys, lanes), jnp.float32)] * last
     return pl.pallas_call(
-        functools.partial(attend_kernel, step, first, filled, last, tok_dev, reach, ratio),
+        functools.partial(attend_kernel, step, place, first, filled, last, tok_dev, reach, ratio),
         out_shape=out_shape,
         grid_spec=pltpu.PrefetchScalarGridSpec(
             num_scalar_prefetch=2,
             grid=(span // HEADS_STEP,),
             in_specs=in_specs,
             out_specs=out_specs,
-            scratch_shapes=[pltpu.VMEM(shape, jnp.float32) for shape in held],
+            scratch_shapes=held,
         ),
         input_output_aliases=aliases,
         compiler_params=pltpu.CompilerParams(

time: 74.9 us -> 75.4 us (level)
  no operation moved by 1% of the time
where the time goes in v18:
time: 75.4 us; the launch traced here: 75 us
  starting transfers between devices  30.6 us (41%)
  Pallas kernels  19.9 us (26%)
  waiting for transfers between devices  18.3 us (24%)
  local copies, waits for them, and re-layouts  3.24 us (4%)
  other arithmetic  2.01 us (3%)
  between operations  0.92 us (1%)
    ppermute x6, starting transfers between devices, shifted(): return lax.ppermute(value, axis, pairs)  19.2 us
    pallas_call x5, Pallas kernels, attend(): pl.pallas_call(functools.partial(attend_kernel, step, place, first, fille...  16.6 us
    ppermute x8, starting transfers between devices, exchanged(): lax.ppermute(value, axis, [(i, (i + step) % count) for i in range(count)])  11.4 us
    ppermute x8, waiting for transfers between devices, exchanged(): lax.ppermute(value, axis, [(i, (i + step) % count) for i in range(count)])  9.27 us
    ppermute x6, waiting for transfers between devices, shifted(): return lax.ppermute(value, axis, pairs)  9.06 us
    pallas_call x1, Pallas kernels, stage(): pl.pallas_call(functools.partial(stage_kernel, count, jobs, len(jobs)), o...  3.23 us
    dynamic_update_slice x4, local copies, waits for them, and re-layouts, shards(): lax.dynamic_update_index_in_dim(kv_own, piece, source_of(group, step, cou...  2.55 us
  transfers between devices with their start and end apart: 14, of which 5 were waited for; matrix products, arithmetic and copies ran while one was open for 5% of the time, Pallas kernels for 22%

profile of v18, /device:TPU:1, one launch (start us, length us, event | category | flops | bytes accessed | tf_op | source)
XLA Modules:
  0.0 75.0 jit_solution(3426510594182914486)
XLA Ops:
  0.6 3.2 %stage.1 = (bf16[2,32,512]{2,1,0:T(8,128)(2,1)}, bf16[2,32,512]{2,1,0:T(8,128)(2,1)}, bf16[2,32,512]{2,1,0:T(8,128)(2,1)}, bf16[2,32,512]{2,1,0:T(8,128)(2,1)}, ...) custom-call(s32[4]{0:T(128)} %assign_ref.11, ...), custom_call_target="tpu_custom_call" | custom-call | tf_op jit(solution)/shard_map/stage/pallas_call | solution.py:63
  3.9 2.2 %collective-permute-start = (bf16[2,32,512]{2,1,0:T(8,128)(2,1)}, bf16[2,32,512]{2,1,0:T(8,128)(2,1)S(1)}, u32[]{:S(2)}, u32[]{:S(2)}) collective-permute-start(bf16[2,32,512]{2,1,0:T(8,128)(2,1)} %get-tuple-element.44), channel_id=1, source_target_pairs={{0,1},{1,2},{2,3},{3,0},{4,5},{5,6},{6,7},{7,4},{8,9},{9,10},{10,1... | collective-permute-start | bytes 196616 | tf_op jit(solution)/shard_map/ppermute | solution.py:28
  6.1 2.3 %collective-permute-start.2 = (bf16[2,32,512]{2,1,0:T(8,128)(2,1)}, bf16[2,32,512]{2,1,0:T(8,128)(2,1)}, u32[]{:S(2)}, u32[]{:S(2)}) collective-permute-start(bf16[2,32,512]{2,1,0:T(8,128)(2,1)} %get-tuple-element.50), channel_id=1, source_target_pairs={{0,2},{1,3},{2,0},{3,1},{4,6},{5,7},{6,4},{7,5},{8,10},{9,11},{10,... | collective-permute-start | bytes 196616 | tf_op jit(solution)/shard_map/ppermute | solution.py:28
  8.4 1.1 %collective-permute-start.3 = (bf16[2,32,512]{2,1,0:T(8,128)(2,1)}, bf16[2,32,512]{2,1,0:T(8,128)(2,1)S(1)}, u32[]{:S(2)}, u32[]{:S(2)}) collective-permute-start(bf16[2,32,512]{2,1,0:T(8,128)(2,1)} %get-tuple-element.51), channel_id=1, source_target_pairs={{0,3},{1,0},{2,1},{3,2},{4,7},{5,4},{6,5},{7,6},{8,11},{9,8},{10,9... | collective-permute-start | bytes 196616 | tf_op jit(solution)/shard_map/ppermute | solution.py:28
  9.5 0.9 %bitcast_dynamic-update-slice_fusion.3 = bf16[4,2,32,512]{3,2,1,0:T(8,128)(2,1)S(1)} fusion(bf16[4,2,32,512]{3,2,1,0:T(8,128)(2,1)S(1)} %broadcast_in_dim.19, s32[]{:T(128)S(6)} %select_n.13, bf16[2,32,512]{2,1,0:T(8,128)(2,1)} %get-tuple-element.48), kind=kLoop, calls=%fused_computation.10 | loop fusion | bytes 131076 | tf_op jit(solution)/shard_map/jit(dynamic_update_index_in_dim)/dynamic_update_slice | solution.py:296
  11.4 2.9 %collective-permute-start.8 = (bf16[2,32,4096]{2,1,0:T(8,128)(2,1)}, bf16[2,32,4096]{2,1,0:T(8,128)(2,1)S(1)}, u32[]{:S(2)}, u32[]{:S(2)}) collective-permute-start(bf16[2,32,4096]{2,1,0:T(8,128)(2,1)} %get-tuple-element.59), channel_id=1, source_target_pairs={{0,3},{1,0},{2,1},{3,2},{4,7},{5,4},{6,5},{7,6},{8,11},{9,8},{10,9... | collective-permute-start | bytes 1572872 | tf_op jit(solution)/shard_map/ppermute | solution.py:28
  16.0 3.1 %collective-permute-start.5 = (bf16[4,2,32,512]{3,2,1,0:T(8,128)(2,1)S(1)}, bf16[4,2,32,512]{3,2,1,0:T(8,128)(2,1)}, u32[]{:S(2)}, u32[]{:S(2)}) collective-permute-start(bf16[4,2,32,512]{3,2,1,0:T(8,128)(2,1)S(1)} %bitcast_dynamic-update-slice_fusion), channel_id=1, source_target_pairs={{0,4},{4,8},{8,12},{12,16},{16,20},{20,24},{24,28},{1,5},{5,9},{9,... | collective-permute-start | bytes 786440 | tf_op jit(solution)/shard_map/ppermute | solution.py:34
  19.1 5.7 %collective-permute-start.4 = (bf16[4,2,32,512]{3,2,1,0:T(8,128)(2,1)S(1)}, bf16[4,2,32,512]{3,2,1,0:T(8,128)(2,1)}, u32[]{:S(2)}, u32[]{:S(2)}) collective-permute-start(bf16[4,2,32,512]{3,2,1,0:T(8,128)(2,1)S(1)} %bitcast_dynamic-update-slice_fusion), channel_id=1, source_target_pairs={{0,8},{4,12},{8,16},{12,20},{16,24},{20,28},{1,9},{5,13},{9,17},{1... | collective-permute-start | bytes 786440 | tf_op jit(solution)/shard_map/ppermute | solution.py:34
  24.9 2.7 %collective-permute-done.5 = bf16[4,2,32,512]{3,2,1,0:T(8,128)(2,1)} collective-permute-done((bf16[4,2,32,512]{3,2,1,0:T(8,128)(2,1)S(1)}, bf16[4,2,32,512]{3,2,1,0:T(8,128)(2,1)}, u32[]{:S(2)}, u32[]{:S(2)}) %collective-permute-start.5) | collective-permute-done | bytes 262176 | tf_op jit(solution)/shard_map/ppermute | solution.py:34
  27.6 2.0 %collective-permute-done.4 = bf16[4,2,32,512]{3,2,1,0:T(8,128)(2,1)} collective-permute-done((bf16[4,2,32,512]{3,2,1,0:T(8,128)(2,1)S(1)}, bf16[4,2,32,512]{3,2,1,0:T(8,128)(2,1)}, u32[]{:S(2)}, u32[]{:S(2)}) %collective-permute-start.4) | collective-permute-done | bytes 262176 | tf_op jit(solution)/shard_map/ppermute | solution.py:34
  29.6 1.1 %pad_maximum_fusion.kv_ref = bf16[12,2,32,512]{3,2,1,0:T(8,128)(2,1)S(1)} fusion(bf16[4,2,32,512]{3,2,1,0:T(8,128)(2,1)S(1)} %bitcast_dynamic-update-slice_fusion, bf16[4,2,32,512]{3,2,1,0:T(8,128)(2,1)} %collective-permute-done.5, bf16[4,2,32,512]{3,2,1,0:T(8,128)(2,1)} %collective-permute-done.4), kind=kLoop, calls=%fused_computation | loop fusion | flops 786432 | bytes 1572864 | tf_op jit(solution)/shard_map/concatenate | solution.py:300
  30.8 3.6 %attend.5 = (bf16[128,32,128]{2,1,0:T(8,128)(2,1)}, f32[2,384,512]{2,1,0:T(8,128)S(1)}) custom-call(s32[2]{0:T(128)S(1)} %pad_add_fusion.meta_ref, s32[4]{0:T(128)S(1)} %copy-done.3, s32[4,1024]{1,0:T(4,128)S(1)} %copy-done.2, bf16[4,32,4096]{2,1,0:T(8,128)(2,1)S(1)} %copy-done, bf16[4,32,4096]{2,1,0:T(8,128)(2,1)S(1)} %copy-done.1, ...), custom_call_target="tpu_custom_call" | custom-call | flops 37748736 | bytes 294912 | tf_op jit(solution)/shard_map/attend/pallas_call | solution.py:248
  34.6 3.9 %attend.6 = (bf16[128,32,128]{2,1,0:T(8,128)(2,1)}, f32[2,384,512]{2,1,0:T(8,128)S(1)}) custom-call(s32[2]{0:T(128)S(1)} %pad_add_fusion.meta_ref, s32[4]{0:T(128)S(1)} %copy-done.3, s32[4,1024]{1,0:T(4,128)S(1)} %copy-done.2, bf16[2,32,4096]{2,1,0:T(8,128)(2,1)S(1)} %collective-permute-done.1.query_ref.grad_ref, ...), custom_call_target="tpu_custom_call", output_to_operand_aliasing={{1}: (6, {}), {0}: (7, {})} | custom-call | flops 37748736 | bytes 294912 | tf_op jit(solution)/shard_map/attend/pallas_call | solution.py:248
  38.5 2.4 %collective-permute-start.6 = (bf16[1,32,2048]{2,1,0:T(8,128)(2,1)S(1)}, bf16[1,32,2048]{2,1,0:T(8,128)(2,1)S(1)}, u32[]{:S(2)}, u32[]{:S(2)}) collective-permute-start(bf16[1,32,2048]{2,1,0:T(8,128)(2,1)S(1)} %copy-done.7), channel_id=1, source_target_pairs={{0,2},{1,3},{2,0},{3,1},{4,6},{5,7},{6,4},{7,5},{8,10},{9,11},{10,... | collective-permute-start | bytes 393224 | tf_op jit(solution)/shard_map/ppermute | solution.py:28
  41.0 3.9 %attend.7 = (bf16[128,32,128]{2,1,0:T(8,128)(2,1)}, f32[2,384,512]{2,1,0:T(8,128)S(1)}) custom-call(s32[2]{0:T(128)S(1)} %pad_add_fusion.meta_ref, s32[4]{0:T(128)S(1)} %copy-done.3, s32[4,1024]{1,0:T(4,128)S(1)} %copy-done.2, bf16[2,32,4096]{2,1,0:T(8,128)(2,1)S(1)} %collective-permute-done.8.query_ref.grad_ref, ...), custom_call_target="tpu_custom_call", output_to_operand_aliasing={{1}: (6, {}), {0}: (7, {})} | custom-call | flops 3774873600 | bytes 29491200 | tf_op jit(solution)/shard_map/attend/pallas_call | solution.py:248
  44.9 9.3 %collective-permute-done.9.query_ref.grad_ref = bf16[2,32,2048]{2,1,0:T(8,128)(2,1)S(1)} collective-permute-done((bf16[2,32,2048]{2,1,0:T(8,128)(2,1)S(1)}, bf16[2,32,2048]{2,1,0:T(8,128)(2,1)S(1)}, u32[]{:S(2)}, u32[]{:S(2)}) %collective-permute-start.9) | collective-permute-done | bytes 262176 | tf_op jit(solution)/shard_map/ppermute | solution.py:28
  54.2 2.6 %attend.8 = (bf16[128,32,128]{2,1,0:T(8,128)(2,1)}, f32[2,128,256]{2,1,0:T(8,128)S(1)}, bf16[2,128,256]{2,1,0:T(8,128)(2,1)S(1)}, bf16[2,128,256]{2,1,0:T(8,128)(2,1)S(1)}) custom-call(s32[2]{0:T(128)S(1)} %pad_add_fusion.meta_ref, s32[4]{0:T(128)S(1)} %copy-done.3, s32[4,1024]{1,0:T(4,128)S(1)} %copy-done.2, ...), custom_call_target="tpu_custom_call", output_to_operand_aliasing={{0}: (7, {})} | custom-call | flops 18874368 | bytes 147456 | tf_op jit(solution)/shard_map/attend/pallas_call | solution.py:248
  56.8 4.7 %collective-permute-start.10 = (bf16[2,128,256]{2,1,0:T(8,128)(2,1)S(1)}, bf16[2,128,256]{2,1,0:T(8,128)(2,1)S(1)}, u32[]{:S(2)}, u32[]{:S(2)}) collective-permute-start(bf16[2,128,256]{2,1,0:T(8,128)(2,1)S(1)} %get-tuple-element.68), channel_id=1, source_target_pairs={{4,0},{8,4},{12,8},{16,12},{20,16},{24,20},{28,24},{5,1},{9,5},{13... | collective-permute-start | bytes 393224 | tf_op jit(solution)/shard_map/ppermute | solution.py:34
  61.4 1.9 %collective-permute-start.11 = (bf16[2,128,256]{2,1,0:T(8,128)(2,1)S(1)}, bf16[2,128,256]{2,1,0:T(8,128)(2,1)S(1)}, u32[]{:S(2)}, u32[]{:S(2)}) collective-permute-start(bf16[2,128,256]{2,1,0:T(8,128)(2,1)S(1)} %get-tuple-element.69), channel_id=1, source_target_pairs={{8,0},{12,4},{16,8},{20,12},{24,16},{28,20},{9,1},{13,5},{17,9},{2... | collective-permute-start | bytes 393224 | tf_op jit(solution)/shard_map/ppermute | solution.py:34
  63.4 2.6 %attend.9 = (bf16[128,32,128]{2,1,0:T(8,128)(2,1)}, f32[2,128,256]{2,1,0:T(8,128)S(1)}, bf16[2,128,256]{2,1,0:T(8,128)(2,1)S(1)}, bf16[2,128,256]{2,1,0:T(8,128)(2,1)S(1)}) custom-call(s32[2]{0:T(128)S(1)} %pad_add_fusion.meta_ref, s32[4]{0:T(128)S(1)} %copy-done.3, s32[4,1024]{1,0:T(4,128)S(1)} %copy-done.2, ...), custom_call_target="tpu_custom_call", output_to_operand_aliasing={{0}: (7, {})} | custom-call | flops 18874368 | bytes 147456 | tf_op jit(solution)/shard_map/attend/pallas_call | solution.py:248
  66.0 1.9 %collective-permute-start.12 = (bf16[2,128,256]{2,1,0:T(8,128)(2,1)S(1)}, bf16[2,128,256]{2,1,0:T(8,128)(2,1)S(1)}, u32[]{:S(2)}, u32[]{:S(2)}) collective-permute-start(bf16[2,128,256]{2,1,0:T(8,128)(2,1)S(1)} %get-tuple-element.73), channel_id=1, source_target_pairs={{4,0},{8,4},{12,8},{16,12},{20,16},{24,20},{28,24},{5,1},{9,5},{13... | collective-permute-start | bytes 393224 | tf_op jit(solution)/shard_map/ppermute | solution.py:34
  67.9 1.9 %collective-permute-start.13 = (bf16[2,128,256]{2,1,0:T(8,128)(2,1)S(1)}, bf16[2,128,256]{2,1,0:T(8,128)(2,1)S(1)}, u32[]{:S(2)}, u32[]{:S(2)}) collective-permute-start(bf16[2,128,256]{2,1,0:T(8,128)(2,1)S(1)} %get-tuple-element.74), channel_id=1, source_target_pairs={{8,0},{12,4},{16,8},{20,12},{24,16},{28,20},{9,1},{13,5},{17,9},{2... | collective-permute-start | bytes 393224 | tf_op jit(solution)/shard_map/ppermute | solution.py:34
  69.9 2.4 %collective-permute-done.12 = bf16[2,128,256]{2,1,0:T(8,128)(2,1)S(1)} collective-permute-done((bf16[2,128,256]{2,1,0:T(8,128)(2,1)S(1)}, bf16[2,128,256]{2,1,0:T(8,128)(2,1)S(1)}, u32[]{:S(2)}, u32[]{:S(2)}) %collective-permute-start.12) | collective-permute-done | bytes 131104 | tf_op jit(solution)/shard_map/ppermute | solution.py:34
  72.3 1.9 %collective-permute-done.13 = bf16[2,128,256]{2,1,0:T(8,128)(2,1)S(1)} collective-permute-done((bf16[2,128,256]{2,1,0:T(8,128)(2,1)S(1)}, bf16[2,128,256]{2,1,0:T(8,128)(2,1)S(1)}, u32[]{:S(2)}, u32[]{:S(2)}) %collective-permute-start.13) | collective-permute-done | bytes 131104 | tf_op jit(solution)/shard_map/ppermute | solution.py:34
  (36 shorter events, 3.9 us)
Async XLA Ops:
  3.9 26.9 %copy-start = (bf16[4,32,4096]{2,1,0:T(8,128)(2,1)S(1)}, bf16[4,32,4096]{2,1,0:T(8,128)(2,1)}, u32[]{:S(2)}) copy-start(bf16[4,32,4096]{2,1,0:T(8,128)(2,1)} %query_ref.1) | copy-start | bytes 3145732
  3.9 26.9 %copy-start.1 = (bf16[4,32,4096]{2,1,0:T(8,128)(2,1)S(1)}, bf16[4,32,4096]{2,1,0:T(8,128)(2,1)}, u32[]{:S(2)}) copy-start(bf16[4,32,4096]{2,1,0:T(8,128)(2,1)} %grad_ref.1) | copy-start | bytes 3145732
  3.9 26.9 %copy-start.2 = (s32[4,1024]{1,0:T(4,128)S(1)}, s32[4,1024]{1,0:T(4,128)}, u32[]{:S(2)}) copy-start(s32[4,1024]{1,0:T(4,128)} %segment_ref.9) | copy-start | bytes 49156
  3.9 26.9 %copy-start.3 = (s32[4]{0:T(128)S(1)}, s32[4]{0:T(128)}, u32[]{:S(2)}) copy-start(s32[4]{0:T(128)} %assign_ref.11) | copy-start | bytes 52
  3.9 6.4 %collective-permute-start = (bf16[2,32,512]{2,1,0:T(8,128)(2,1)}, bf16[2,32,512]{2,1,0:T(8,128)(2,1)S(1)}, u32[]{:S(2)}, u32[]{:S(2)}) collective-permute-start(bf16[2,32,512]{2,1,0:T(8,128)(2,1)} %get-tuple-element.44), channel_id=1, source_target_pairs={{0,1},{1,2},{2,3},{3,0},{4,5},{5,6},{6,7},{7,4},{8,9},{9,10},{10,1... | collective-permute-start | bytes 196616 | tf_op jit(solution)/shard_map/ppermute | solution.py:28
  6.1 9.0 %collective-permute-start.2 = (bf16[2,32,512]{2,1,0:T(8,128)(2,1)}, bf16[2,32,512]{2,1,0:T(8,128)(2,1)}, u32[]{:S(2)}, u32[]{:S(2)}) collective-permute-start(bf16[2,32,512]{2,1,0:T(8,128)(2,1)} %get-tuple-element.50), channel_id=1, source_target_pairs={{0,2},{1,3},{2,0},{3,1},{4,6},{5,7},{6,4},{7,5},{8,10},{9,11},{10,... | collective-permute-start | bytes 196616 | tf_op jit(solution)/shard_map/ppermute | solution.py:28
  8.4 7.5 %collective-permute-start.3 = (bf16[2,32,512]{2,1,0:T(8,128)(2,1)}, bf16[2,32,512]{2,1,0:T(8,128)(2,1)S(1)}, u32[]{:S(2)}, u32[]{:S(2)}) collective-permute-start(bf16[2,32,512]{2,1,0:T(8,128)(2,1)} %get-tuple-element.51), channel_id=1, source_target_pairs={{0,3},{1,0},{2,1},{3,2},{4,7},{5,4},{6,5},{7,6},{8,11},{9,8},{10,9... | collective-permute-start | bytes 196616 | tf_op jit(solution)/shard_map/ppermute | solution.py:28
  10.4 0.6 copy-start.4
  11.0 23.6 %collective-permute-start.1 = (bf16[2,32,4096]{2,1,0:T(8,128)(2,1)}, bf16[2,32,4096]{2,1,0:T(8,128)(2,1)S(1)}, u32[]{:S(2)}, u32[]{:S(2)}) collective-permute-start(bf16[2,32,4096]{2,1,0:T(8,128)(2,1)} %get-tuple-element.47), channel_id=1, source_target_pairs={{0,1},{1,2},{2,3},{3,0},{4,5},{5,6},{6,7},{7,4},{8,9},{9,10},{10,1... | collective-permute-start | bytes 1572872 | tf_op jit(solution)/shard_map/ppermute | solution.py:28
  11.4 29.6 %collective-permute-start.8 = (bf16[2,32,4096]{2,1,0:T(8,128)(2,1)}, bf16[2,32,4096]{2,1,0:T(8,128)(2,1)S(1)}, u32[]{:S(2)}, u32[]{:S(2)}) collective-permute-start(bf16[2,32,4096]{2,1,0:T(8,128)(2,1)} %get-tuple-element.59), channel_id=1, source_target_pairs={{0,3},{1,0},{2,1},{3,2},{4,7},{5,4},{6,5},{7,6},{8,11},{9,8},{10,9... | collective-permute-start | bytes 1572872 | tf_op jit(solution)/shard_map/ppermute | solution.py:28
  16.0 11.7 %collective-permute-start.5 = (bf16[4,2,32,512]{3,2,1,0:T(8,128)(2,1)S(1)}, bf16[4,2,32,512]{3,2,1,0:T(8,128)(2,1)}, u32[]{:S(2)}, u32[]{:S(2)}) collective-permute-start(bf16[4,2,32,512]{3,2,1,0:T(8,128)(2,1)S(1)} %bitcast_dynamic-update-slice_fusion), channel_id=1, source_target_pairs={{0,4},{4,8},{8,12},{12,16},{16,20},{20,24},{24,28},{1,5},{5,9},{9,... | collective-permute-start | bytes 786440 | tf_op jit(solution)/shard_map/ppermute | solution.py:34
  19.1 10.5 %collective-permute-start.4 = (bf16[4,2,32,512]{3,2,1,0:T(8,128)(2,1)S(1)}, bf16[4,2,32,512]{3,2,1,0:T(8,128)(2,1)}, u32[]{:S(2)}, u32[]{:S(2)}) collective-permute-start(bf16[4,2,32,512]{3,2,1,0:T(8,128)(2,1)S(1)} %bitcast_dynamic-update-slice_fusion), channel_id=1, source_target_pairs={{0,8},{4,12},{8,16},{12,20},{16,24},{20,28},{1,9},{5,13},{9,17},{1... | collective-permute-start | bytes 786440 | tf_op jit(solution)/shard_map/ppermute | solution.py:34
  30.8 3.7 %copy-start.5 = (bf16[2,32,2048]{2,1,0:T(8,128)(2,1)S(1)}, bf16[2,32,2048]{2,1,0:T(8,128)(2,1)}, u32[]{:S(2)}) copy-start(bf16[2,32,2048]{2,1,0:T(8,128)(2,1)} %get-tuple-element.63) | copy-start | bytes 786436
  34.5 19.7 %collective-permute-start.9 = (bf16[2,32,2048]{2,1,0:T(8,128)(2,1)S(1)}, bf16[2,32,2048]{2,1,0:T(8,128)(2,1)S(1)}, u32[]{:S(2)}, u32[]{:S(2)}) collective-permute-start(bf16[2,32,2048]{2,1,0:T(8,128)(2,1)S(1)} %copy-done.5), channel_id=1, source_target_pairs={{0,2},{1,3},{2,0},{3,1},{4,6},{5,7},{6,4},{7,5},{8,10},{9,11},{10,... | collective-permute-start | bytes 786440 | tf_op jit(solution)/shard_map/ppermute | solution.py:28
  34.6 4.0 %copy-start.7 = (bf16[1,32,2048]{2,1,0:T(8,128)(2,1)S(1)}, bf16[1,32,2048]{2,1,0:T(8,128)(2,1)}, u32[]{:S(2)}) copy-start(bf16[1,32,2048]{2,1,0:T(8,128)(2,1)} %get-tuple-element.57) | copy-start | bytes 393220
  34.6 6.3 %copy-start.6 = (bf16[1,32,2048]{2,1,0:T(8,128)(2,1)S(1)}, bf16[1,32,2048]{2,1,0:T(8,128)(2,1)}, u32[]{:S(2)}) copy-start(bf16[1,32,2048]{2,1,0:T(8,128)(2,1)} %get-tuple-element.58) | copy-start | bytes 393220
  38.5 24.8 %collective-permute-start.6 = (bf16[1,32,2048]{2,1,0:T(8,128)(2,1)S(1)}, bf16[1,32,2048]{2,1,0:T(8,128)(2,1)S(1)}, u32[]{:S(2)}, u32[]{:S(2)}) collective-permute-start(bf16[1,32,2048]{2,1,0:T(8,128)(2,1)S(1)} %copy-done.7), channel_id=1, source_target_pairs={{0,2},{1,3},{2,0},{3,1},{4,6},{5,7},{6,4},{7,5},{8,10},{9,11},{10,... | collective-permute-start | bytes 393224 | tf_op jit(solution)/shard_map/ppermute | solution.py:28
  40.9 22.5 %collective-permute-start.7 = (bf16[1,32,2048]{2,1,0:T(8,128)(2,1)S(1)}, bf16[1,32,2048]{2,1,0:T(8,128)(2,1)S(1)}, u32[]{:S(2)}, u32[]{:S(2)}) collective-permute-start(bf16[1,32,2048]{2,1,0:T(8,128)(2,1)S(1)} %copy-done.6), channel_id=1, source_target_pairs={{0,2},{1,3},{2,0},{3,1},{4,6},{5,7},{6,4},{7,5},{8,10},{9,11},{10,... | collective-permute-start | bytes 393224 | tf_op jit(solution)/shard_map/ppermute | solution.py:28
  56.8 9.2 %collective-permute-start.10 = (bf16[2,128,256]{2,1,0:T(8,128)(2,1)S(1)}, bf16[2,128,256]{2,1,0:T(8,128)(2,1)S(1)}, u32[]{:S(2)}, u32[]{:S(2)}) collective-permute-start(bf16[2,128,256]{2,1,0:T(8,128)(2,1)S(1)} %get-tuple-element.68), channel_id=1, source_target_pairs={{4,0},{8,4},{12,8},{16,12},{20,16},{24,20},{28,24},{5,1},{9,5},{13... | collective-permute-start | bytes 393224 | tf_op jit(solution)/shard_map/ppermute | solution.py:34
  61.4 8.4 %collective-permute-start.11 = (bf16[2,128,256]{2,1,0:T(8,128)(2,1)S(1)}, bf16[2,128,256]{2,1,0:T(8,128)(2,1)S(1)}, u32[]{:S(2)}, u32[]{:S(2)}) collective-permute-start(bf16[2,128,256]{2,1,0:T(8,128)(2,1)S(1)} %get-tuple-element.69), channel_id=1, source_target_pairs={{8,0},{12,4},{16,8},{20,12},{24,16},{28,20},{9,1},{13,5},{17,9},{2... | collective-permute-start | bytes 393224 | tf_op jit(solution)/shard_map/ppermute | solution.py:34
  66.0 6.3 %collective-permute-start.12 = (bf16[2,128,256]{2,1,0:T(8,128)(2,1)S(1)}, bf16[2,128,256]{2,1,0:T(8,128)(2,1)S(1)}, u32[]{:S(2)}, u32[]{:S(2)}) collective-permute-start(bf16[2,128,256]{2,1,0:T(8,128)(2,1)S(1)} %get-tuple-element.73), channel_id=1, source_target_pairs={{4,0},{8,4},{12,8},{16,12},{20,16},{24,20},{28,24},{5,1},{9,5},{13... | collective-permute-start | bytes 393224 | tf_op jit(solution)/shard_map/ppermute | solution.py:34
  67.9 6.3 %collective-permute-start.13 = (bf16[2,128,256]{2,1,0:T(8,128)(2,1)S(1)}, bf16[2,128,256]{2,1,0:T(8,128)(2,1)S(1)}, u32[]{:S(2)}, u32[]{:S(2)}) collective-permute-start(bf16[2,128,256]{2,1,0:T(8,128)(2,1)S(1)} %get-tuple-element.74), channel_id=1, source_target_pairs={{8,0},{12,4},{16,8},{20,12},{24,16},{28,20},{9,1},{13,5},{17,9},{2... | collective-permute-start | bytes 393224 | tf_op jit(solution)/shard_map/ppermute | solution.py:34

commit v19 on v18

--- a/solution.py
+++ b/solution.py
@@ -104,7 +104,7 @@
 
 
 def attend_kernel(
-    step, place, first, filled, last, tok_dev, reach, ratio,
+    step, first, filled, last, tok_dev, reach, ratio,
     meta_ref, assign_ref, segment_ref, query_ref, grad_ref, kv_ref, *refs,
 ):
     refs = list(refs)
@@ -113,9 +113,9 @@
     if filled:
         refs.pop(0)
     query_out_ref = refs.pop(0)
-    column_ref, bias_ref, fetch_sem = refs[-3 - last : len(refs) - last]
+    column_ref, bias_ref = refs[-2 - last], refs[-1 - last]
     if last:
-        own_ref, halo_refs, acc_ref = refs[0], refs[1:-4], refs[-1]
+        own_ref, halo_refs, acc_ref = refs[0], refs[1:-3], refs[-1]
     else:
         acc_ref = refs[0]
 
@@ -128,20 +128,17 @@
     block = (keys - tok_dev - reach) // rows + source
     span = pl.ds(pl.multiple_of(block * rows, rows), window)
 
-    @pl.when(pl.program_id(0) == 0)
-    def _():
+    def mask():
         build_bias(
             source, assign_ref[group], meta_ref[1], segment_ref, column_ref, bias_ref, rows, tok_dev, reach
         )
 
-    if first:
-        acc_ref[...] = jnp.zeros_like(acc_ref)
+    if last:
+        mask()
     else:
-        start = pl.multiple_of((place + pl.program_id(0)) * HEADS_STEP * HD, HEADS_STEP * HD)
-        fetch = pltpu.make_async_copy(
-            acc_in_ref.at[:, :, pl.ds(start, HEADS_STEP * HD)], acc_ref, fetch_sem
-        )
-        fetch.start()
+        pl.when(pl.program_id(0) == 0)(mask)
+
+    acc_ref[...] = jnp.zeros_like(acc_ref) if first else acc_in_ref[...]
     turned, across = (((1,), (1,)), ((), ())), (((0,), (0,)), ((), ()))
     heads = range(HEADS_STEP)
     lanes = [slice(head * HD, (head + 1) * HD) for head in heads]
@@ -178,8 +175,6 @@
         grads.append((grad_query * scale).reshape(ratio, rows, HD))
     grad_key = [product(grad_scores[head], query[head], plain) for head in heads]
     grad_value = [product(probs[head].astype(jnp.bfloat16), grad[head], plain) for head in heads]
-    if not first:
-        fetch.wait()
     for head in heads:
         acc_ref[0, span, lanes[head]] += grad_key[head]
         acc_ref[1, span, lanes[head]] += grad_value[head]
@@ -220,7 +215,7 @@
         if not last:
             aliases[len(operands)] = 1
         operands.append(acc)
-        in_specs.append(pl.BlockSpec(memory_space=pl.ANY))
+        in_specs.append(acc_spec)
     if filled:
         aliases[len(operands)] = 0
         operands.append(full)
@@ -242,18 +237,17 @@
         out_specs.append(acc_spec)
     pairs = span * ratio * rows * window
     cost = CALL_COST[step] if step < len(CALL_COST) and not last else 1
-    held = [pltpu.VMEM((held, ratio * rows), jnp.float32) for held in (keys, window)]
-    held.append(pltpu.SemaphoreType.DMA)
-    held += [pltpu.VMEM((2, keys, lanes), jnp.float32)] * last
+    held = (keys, ratio * rows), (window, ratio * rows)
+    held += ((2, keys, lanes),) * last
     return pl.pallas_call(
-        functools.partial(attend_kernel, step, place, first, filled, last, tok_dev, reach, ratio),
+        functools.partial(attend_kernel, step, first, filled, last, tok_dev, reach, ratio),
         out_shape=out_shape,
         grid_spec=pltpu.PrefetchScalarGridSpec(
             num_scalar_prefetch=2,
             grid=(span // HEADS_STEP,),
             in_specs=in_specs,
             out_specs=out_specs,
-            scratch_shapes=held,
+            scratch_shapes=[pltpu.VMEM(shape, jnp.float32) for shape in held],
         ),
         input_output_aliases=aliases,
         compiler_params=pltpu.CompilerParams(

time: 75.4 us -> 74.8 us (level)
  waiting for transfers between devices: 18.3 us -> 19.5 us
  Pallas kernels: 19.9 us -> 18.8 us
    pallas_call x5, Pallas kernels: 16.6 us -> 15.6 us  [attend(): pl.pallas_call(functools.partial(attend_kernel, step, first, filled, last...]
  transfers between devices with their start and end apart: 14 -> 14, of which waited for: 5 -> 5; matrix products, arithmetic and copies ran while one was open for 5% -> 5% of each run, Pallas kernels for 22% -> 21%
where the time goes in v19:
time: 74.8 us; the launch traced here: 74.4 us
  starting transfers between devices  30 us (40%)
  waiting for transfers between devices  19.5 us (26%)
  Pallas kernels  18.8 us (25%)
  local copies, waits for them, and re-layouts  3.24 us (4%)
  other arithmetic  2.01 us (3%)
  between operations  0.85 us (1%)
    ppermute x6, starting transfers between devices, shifted(): return lax.ppermute(value, axis, pairs)  18.8 us
    pallas_call x5, Pallas kernels, attend(): pl.pallas_call(functools.partial(attend_kernel, step, first, filled, last...  15.6 us
    ppermute x8, starting transfers between devices, exchanged(): lax.ppermute(value, axis, [(i, (i + step) % count) for i in range(count)])  11.2 us
    ppermute x8, waiting for transfers between devices, exchanged(): lax.ppermute(value, axis, [(i, (i + step) % count) for i in range(count)])  9.95 us
    ppermute x6, waiting for transfers between devices, shifted(): return lax.ppermute(value, axis, pairs)  9.51 us
    pallas_call x1, Pallas kernels, stage(): pl.pallas_call(functools.partial(stage_kernel, count, jobs, len(jobs)), o...  3.23 us
    dynamic_update_slice x4, local copies, waits for them, and re-layouts, shards(): lax.dynamic_update_index_in_dim(kv_own, piece, source_of(group, step, cou...  2.55 us
  transfers between devices with their start and end apart: 14, of which 5 were waited for; matrix products, arithmetic and copies ran while one was open for 5% of the time, Pallas kernels for 21%

profile of v19, /device:TPU:1, one launch (start us, length us, event | category | flops | bytes accessed | tf_op | source)
XLA Modules:
  0.0 74.4 jit_solution(3431107574123315935)
XLA Ops:
  0.6 3.2 %stage.1 = (bf16[2,32,512]{2,1,0:T(8,128)(2,1)}, bf16[2,32,512]{2,1,0:T(8,128)(2,1)}, bf16[2,32,512]{2,1,0:T(8,128)(2,1)}, bf16[2,32,512]{2,1,0:T(8,128)(2,1)}, ...) custom-call(s32[4]{0:T(128)} %assign_ref.11, ...), custom_call_target="tpu_custom_call" | custom-call | tf_op jit(solution)/shard_map/stage/pallas_call | solution.py:63
  3.9 2.2 %collective-permute-start = (bf16[2,32,512]{2,1,0:T(8,128)(2,1)}, bf16[2,32,512]{2,1,0:T(8,128)(2,1)S(1)}, u32[]{:S(2)}, u32[]{:S(2)}) collective-permute-start(bf16[2,32,512]{2,1,0:T(8,128)(2,1)} %get-tuple-element.44), channel_id=1, source_target_pairs={{0,1},{1,2},{2,3},{3,0},{4,5},{5,6},{6,7},{7,4},{8,9},{9,10},{10,1... | collective-permute-start | bytes 196616 | tf_op jit(solution)/shard_map/ppermute | solution.py:28
  6.1 2.3 %collective-permute-start.2 = (bf16[2,32,512]{2,1,0:T(8,128)(2,1)}, bf16[2,32,512]{2,1,0:T(8,128)(2,1)}, u32[]{:S(2)}, u32[]{:S(2)}) collective-permute-start(bf16[2,32,512]{2,1,0:T(8,128)(2,1)} %get-tuple-element.50), channel_id=1, source_target_pairs={{0,2},{1,3},{2,0},{3,1},{4,6},{5,7},{6,4},{7,5},{8,10},{9,11},{10,... | collective-permute-start | bytes 196616 | tf_op jit(solution)/shard_map/ppermute | solution.py:28
  8.4 1.1 %collective-permute-start.3 = (bf16[2,32,512]{2,1,0:T(8,128)(2,1)}, bf16[2,32,512]{2,1,0:T(8,128)(2,1)S(1)}, u32[]{:S(2)}, u32[]{:S(2)}) collective-permute-start(bf16[2,32,512]{2,1,0:T(8,128)(2,1)} %get-tuple-element.51), channel_id=1, source_target_pairs={{0,3},{1,0},{2,1},{3,2},{4,7},{5,4},{6,5},{7,6},{8,11},{9,8},{10,9... | collective-permute-start | bytes 196616 | tf_op jit(solution)/shard_map/ppermute | solution.py:28
  9.5 0.9 %bitcast_dynamic-update-slice_fusion.3 = bf16[4,2,32,512]{3,2,1,0:T(8,128)(2,1)S(1)} fusion(bf16[4,2,32,512]{3,2,1,0:T(8,128)(2,1)S(1)} %broadcast_in_dim.19, s32[]{:T(128)S(6)} %select_n.13, bf16[2,32,512]{2,1,0:T(8,128)(2,1)} %get-tuple-element.48), kind=kLoop, calls=%fused_computation.10 | loop fusion | bytes 131076 | tf_op jit(solution)/shard_map/jit(dynamic_update_index_in_dim)/dynamic_update_slice | solution.py:290
  11.4 2.9 %collective-permute-start.8 = (bf16[2,32,4096]{2,1,0:T(8,128)(2,1)}, bf16[2,32,4096]{2,1,0:T(8,128)(2,1)S(1)}, u32[]{:S(2)}, u32[]{:S(2)}) collective-permute-start(bf16[2,32,4096]{2,1,0:T(8,128)(2,1)} %get-tuple-element.59), channel_id=1, source_target_pairs={{0,3},{1,0},{2,1},{3,2},{4,7},{5,4},{6,5},{7,6},{8,11},{9,8},{10,9... | collective-permute-start | bytes 1572872 | tf_op jit(solution)/shard_map/ppermute | solution.py:28
  16.0 3.1 %collective-permute-start.5 = (bf16[4,2,32,512]{3,2,1,0:T(8,128)(2,1)S(1)}, bf16[4,2,32,512]{3,2,1,0:T(8,128)(2,1)}, u32[]{:S(2)}, u32[]{:S(2)}) collective-permute-start(bf16[4,2,32,512]{3,2,1,0:T(8,128)(2,1)S(1)} %bitcast_dynamic-update-slice_fusion), channel_id=1, source_target_pairs={{0,4},{4,8},{8,12},{12,16},{16,20},{20,24},{24,28},{1,5},{5,9},{9,... | collective-permute-start | bytes 786440 | tf_op jit(solution)/shard_map/ppermute | solution.py:34
  19.1 5.7 %collective-permute-start.4 = (bf16[4,2,32,512]{3,2,1,0:T(8,128)(2,1)S(1)}, bf16[4,2,32,512]{3,2,1,0:T(8,128)(2,1)}, u32[]{:S(2)}, u32[]{:S(2)}) collective-permute-start(bf16[4,2,32,512]{3,2,1,0:T(8,128)(2,1)S(1)} %bitcast_dynamic-update-slice_fusion), channel_id=1, source_target_pairs={{0,8},{4,12},{8,16},{12,20},{16,24},{20,28},{1,9},{5,13},{9,17},{1... | collective-permute-start | bytes 786440 | tf_op jit(solution)/shard_map/ppermute | solution.py:34
  24.9 2.7 %collective-permute-done.5 = bf16[4,2,32,512]{3,2,1,0:T(8,128)(2,1)} collective-permute-done((bf16[4,2,32,512]{3,2,1,0:T(8,128)(2,1)S(1)}, bf16[4,2,32,512]{3,2,1,0:T(8,128)(2,1)}, u32[]{:S(2)}, u32[]{:S(2)}) %collective-permute-start.5) | collective-permute-done | bytes 262176 | tf_op jit(solution)/shard_map/ppermute | solution.py:34
  27.6 2.0 %collective-permute-done.4 = bf16[4,2,32,512]{3,2,1,0:T(8,128)(2,1)} collective-permute-done((bf16[4,2,32,512]{3,2,1,0:T(8,128)(2,1)S(1)}, bf16[4,2,32,512]{3,2,1,0:T(8,128)(2,1)}, u32[]{:S(2)}, u32[]{:S(2)}) %collective-permute-start.4) | collective-permute-done | bytes 262176 | tf_op jit(solution)/shard_map/ppermute | solution.py:34
  29.6 1.1 %pad_maximum_fusion.kv_ref = bf16[12,2,32,512]{3,2,1,0:T(8,128)(2,1)S(1)} fusion(bf16[4,2,32,512]{3,2,1,0:T(8,128)(2,1)S(1)} %bitcast_dynamic-update-slice_fusion, bf16[4,2,32,512]{3,2,1,0:T(8,128)(2,1)} %collective-permute-done.5, bf16[4,2,32,512]{3,2,1,0:T(8,128)(2,1)} %collective-permute-done.4), kind=kLoop, calls=%fused_computation | loop fusion | flops 786432 | bytes 1572864 | tf_op jit(solution)/shard_map/concatenate | solution.py:294
  30.8 3.6 %attend.5 = (bf16[128,32,128]{2,1,0:T(8,128)(2,1)}, f32[2,384,512]{2,1,0:T(8,128)S(1)}) custom-call(s32[2]{0:T(128)S(1)} %pad_add_fusion.meta_ref, s32[4]{0:T(128)S(1)} %copy-done.3, s32[4,1024]{1,0:T(4,128)S(1)} %copy-done.2, bf16[4,32,4096]{2,1,0:T(8,128)(2,1)S(1)} %copy-done, bf16[4,32,4096]{2,1,0:T(8,128)(2,1)S(1)} %copy-done.1, ...), custom_call_target="tpu_custom_call" | custom-call | flops 37748736 | bytes 294912 | tf_op jit(solution)/shard_map/attend/pallas_call | solution.py:242
  34.5 3.6 %attend.6 = (bf16[128,32,128]{2,1,0:T(8,128)(2,1)}, f32[2,384,512]{2,1,0:T(8,128)S(1)}) custom-call(s32[2]{0:T(128)S(1)} %pad_add_fusion.meta_ref, s32[4]{0:T(128)S(1)} %copy-done.3, s32[4,1024]{1,0:T(4,128)S(1)} %copy-done.2, bf16[2,32,4096]{2,1,0:T(8,128)(2,1)S(1)} %collective-permute-done.1.query_ref.grad_ref, ...), custom_call_target="tpu_custom_call", output_to_operand_aliasing={{1}: (6, {}), {0}: (7, {})} | custom-call | flops 37748736 | bytes 294912 | tf_op jit(solution)/shard_map/attend/pallas_call | solution.py:242
  38.1 2.3 %collective-permute-start.6 = (bf16[1,32,2048]{2,1,0:T(8,128)(2,1)S(1)}, bf16[1,32,2048]{2,1,0:T(8,128)(2,1)S(1)}, u32[]{:S(2)}, u32[]{:S(2)}) collective-permute-start(bf16[1,32,2048]{2,1,0:T(8,128)(2,1)S(1)} %copy-done.7), channel_id=1, source_target_pairs={{0,2},{1,3},{2,0},{3,1},{4,6},{5,7},{6,4},{7,5},{8,10},{9,11},{10,... | collective-permute-start | bytes 393224 | tf_op jit(solution)/shard_map/ppermute | solution.py:28
  40.5 3.6 %attend.7 = (bf16[128,32,128]{2,1,0:T(8,128)(2,1)}, f32[2,384,512]{2,1,0:T(8,128)S(1)}) custom-call(s32[2]{0:T(128)S(1)} %pad_add_fusion.meta_ref, s32[4]{0:T(128)S(1)} %copy-done.3, s32[4,1024]{1,0:T(4,128)S(1)} %copy-done.2, bf16[2,32,4096]{2,1,0:T(8,128)(2,1)S(1)} %collective-permute-done.8.query_ref.grad_ref, ...), custom_call_target="tpu_custom_call", output_to_operand_aliasing={{1}: (6, {}), {0}: (7, {})} | custom-call | flops 3774873600 | bytes 29491200 | tf_op jit(solution)/shard_map/attend/pallas_call | solution.py:242
  44.1 9.9 %collective-permute-done.9.query_ref.grad_ref = bf16[2,32,2048]{2,1,0:T(8,128)(2,1)S(1)} collective-permute-done((bf16[2,32,2048]{2,1,0:T(8,128)(2,1)S(1)}, bf16[2,32,2048]{2,1,0:T(8,128)(2,1)S(1)}, u32[]{:S(2)}, u32[]{:S(2)}) %collective-permute-start.9) | collective-permute-done | bytes 262176 | tf_op jit(solution)/shard_map/ppermute | solution.py:28
  54.1 2.4 %attend.8 = (bf16[128,32,128]{2,1,0:T(8,128)(2,1)}, f32[2,128,256]{2,1,0:T(8,128)S(1)}, bf16[2,128,256]{2,1,0:T(8,128)(2,1)S(1)}, bf16[2,128,256]{2,1,0:T(8,128)(2,1)S(1)}) custom-call(s32[2]{0:T(128)S(1)} %pad_add_fusion.meta_ref, s32[4]{0:T(128)S(1)} %copy-done.3, s32[4,1024]{1,0:T(4,128)S(1)} %copy-done.2, ...), custom_call_target="tpu_custom_call", output_to_operand_aliasing={{0}: (7, {})} | custom-call | flops 18874368 | bytes 147456 | tf_op jit(solution)/shard_map/attend/pallas_call | solution.py:242
  56.4 4.0 %collective-permute-start.10 = (bf16[2,128,256]{2,1,0:T(8,128)(2,1)S(1)}, bf16[2,128,256]{2,1,0:T(8,128)(2,1)S(1)}, u32[]{:S(2)}, u32[]{:S(2)}) collective-permute-start(bf16[2,128,256]{2,1,0:T(8,128)(2,1)S(1)} %get-tuple-element.68), channel_id=1, source_target_pairs={{4,0},{8,4},{12,8},{16,12},{20,16},{24,20},{28,24},{5,1},{9,5},{13... | collective-permute-start | bytes 393224 | tf_op jit(solution)/shard_map/ppermute | solution.py:34
  60.5 1.9 %collective-permute-start.11 = (bf16[2,128,256]{2,1,0:T(8,128)(2,1)S(1)}, bf16[2,128,256]{2,1,0:T(8,128)(2,1)S(1)}, u32[]{:S(2)}, u32[]{:S(2)}) collective-permute-start(bf16[2,128,256]{2,1,0:T(8,128)(2,1)S(1)} %get-tuple-element.69), channel_id=1, source_target_pairs={{8,0},{12,4},{16,8},{20,12},{24,16},{28,20},{9,1},{13,5},{17,9},{2... | collective-permute-start | bytes 393224 | tf_op jit(solution)/shard_map/ppermute | solution.py:34
  62.4 2.4 %attend.9 = (bf16[128,32,128]{2,1,0:T(8,128)(2,1)}, f32[2,128,256]{2,1,0:T(8,128)S(1)}, bf16[2,128,256]{2,1,0:T(8,128)(2,1)S(1)}, bf16[2,128,256]{2,1,0:T(8,128)(2,1)S(1)}) custom-call(s32[2]{0:T(128)S(1)} %pad_add_fusion.meta_ref, s32[4]{0:T(128)S(1)} %copy-done.3, s32[4,1024]{1,0:T(4,128)S(1)} %copy-done.2, ...), custom_call_target="tpu_custom_call", output_to_operand_aliasing={{0}: (7, {})} | custom-call | flops 18874368 | bytes 147456 | tf_op jit(solution)/shard_map/attend/pallas_call | solution.py:242
  64.8 2.1 %collective-permute-start.12 = (bf16[2,128,256]{2,1,0:T(8,128)(2,1)S(1)}, bf16[2,128,256]{2,1,0:T(8,128)(2,1)S(1)}, u32[]{:S(2)}, u32[]{:S(2)}) collective-permute-start(bf16[2,128,256]{2,1,0:T(8,128)(2,1)S(1)} %get-tuple-element.73), channel_id=1, source_target_pairs={{4,0},{8,4},{12,8},{16,12},{20,16},{24,20},{28,24},{5,1},{9,5},{13... | collective-permute-start | bytes 393224 | tf_op jit(solution)/shard_map/ppermute | solution.py:34
  66.9 1.9 %collective-permute-start.13 = (bf16[2,128,256]{2,1,0:T(8,128)(2,1)S(1)}, bf16[2,128,256]{2,1,0:T(8,128)(2,1)S(1)}, u32[]{:S(2)}, u32[]{:S(2)}) collective-permute-start(bf16[2,128,256]{2,1,0:T(8,128)(2,1)S(1)} %get-tuple-element.74), channel_id=1, source_target_pairs={{8,0},{12,4},{16,8},{20,12},{24,16},{28,20},{9,1},{13,5},{17,9},{2... | collective-permute-start | bytes 393224 | tf_op jit(solution)/shard_map/ppermute | solution.py:34
  68.9 3.0 %collective-permute-done.12 = bf16[2,128,256]{2,1,0:T(8,128)(2,1)S(1)} collective-permute-done((bf16[2,128,256]{2,1,0:T(8,128)(2,1)S(1)}, bf16[2,128,256]{2,1,0:T(8,128)(2,1)S(1)}, u32[]{:S(2)}, u32[]{:S(2)}) %collective-permute-start.12) | collective-permute-done | bytes 131104 | tf_op jit(solution)/shard_map/ppermute | solution.py:34
  71.9 1.7 %collective-permute-done.13 = bf16[2,128,256]{2,1,0:T(8,128)(2,1)S(1)} collective-permute-done((bf16[2,128,256]{2,1,0:T(8,128)(2,1)S(1)}, bf16[2,128,256]{2,1,0:T(8,128)(2,1)S(1)}, u32[]{:S(2)}, u32[]{:S(2)}) %collective-permute-start.13) | collective-permute-done | bytes 131104 | tf_op jit(solution)/shard_map/ppermute | solution.py:34
  (36 shorter events, 3.8 us)
Async XLA Ops:
  3.9 26.9 %copy-start = (bf16[4,32,4096]{2,1,0:T(8,128)(2,1)S(1)}, bf16[4,32,4096]{2,1,0:T(8,128)(2,1)}, u32[]{:S(2)}) copy-start(bf16[4,32,4096]{2,1,0:T(8,128)(2,1)} %query_ref.1) | copy-start | bytes 3145732
  3.9 26.9 %copy-start.1 = (bf16[4,32,4096]{2,1,0:T(8,128)(2,1)S(1)}, bf16[4,32,4096]{2,1,0:T(8,128)(2,1)}, u32[]{:S(2)}) copy-start(bf16[4,32,4096]{2,1,0:T(8,128)(2,1)} %grad_ref.1) | copy-start | bytes 3145732
  3.9 26.9 %copy-start.2 = (s32[4,1024]{1,0:T(4,128)S(1)}, s32[4,1024]{1,0:T(4,128)}, u32[]{:S(2)}) copy-start(s32[4,1024]{1,0:T(4,128)} %segment_ref.9) | copy-start | bytes 49156
  3.9 26.9 %copy-start.3 = (s32[4]{0:T(128)S(1)}, s32[4]{0:T(128)}, u32[]{:S(2)}) copy-start(s32[4]{0:T(128)} %assign_ref.11) | copy-start | bytes 52
  3.9 6.4 %collective-permute-start = (bf16[2,32,512]{2,1,0:T(8,128)(2,1)}, bf16[2,32,512]{2,1,0:T(8,128)(2,1)S(1)}, u32[]{:S(2)}, u32[]{:S(2)}) collective-permute-start(bf16[2,32,512]{2,1,0:T(8,128)(2,1)} %get-tuple-element.44), channel_id=1, source_target_pairs={{0,1},{1,2},{2,3},{3,0},{4,5},{5,6},{6,7},{7,4},{8,9},{9,10},{10,1... | collective-permute-start | bytes 196616 | tf_op jit(solution)/shard_map/ppermute | solution.py:28
  6.1 9.0 %collective-permute-start.2 = (bf16[2,32,512]{2,1,0:T(8,128)(2,1)}, bf16[2,32,512]{2,1,0:T(8,128)(2,1)}, u32[]{:S(2)}, u32[]{:S(2)}) collective-permute-start(bf16[2,32,512]{2,1,0:T(8,128)(2,1)} %get-tuple-element.50), channel_id=1, source_target_pairs={{0,2},{1,3},{2,0},{3,1},{4,6},{5,7},{6,4},{7,5},{8,10},{9,11},{10,... | collective-permute-start | bytes 196616 | tf_op jit(solution)/shard_map/ppermute | solution.py:28
  8.4 7.5 %collective-permute-start.3 = (bf16[2,32,512]{2,1,0:T(8,128)(2,1)}, bf16[2,32,512]{2,1,0:T(8,128)(2,1)S(1)}, u32[]{:S(2)}, u32[]{:S(2)}) collective-permute-start(bf16[2,32,512]{2,1,0:T(8,128)(2,1)} %get-tuple-element.51), channel_id=1, source_target_pairs={{0,3},{1,0},{2,1},{3,2},{4,7},{5,4},{6,5},{7,6},{8,11},{9,8},{10,9... | collective-permute-start | bytes 196616 | tf_op jit(solution)/shard_map/ppermute | solution.py:28
  10.4 0.6 copy-start.4
  11.0 23.5 %collective-permute-start.1 = (bf16[2,32,4096]{2,1,0:T(8,128)(2,1)}, bf16[2,32,4096]{2,1,0:T(8,128)(2,1)S(1)}, u32[]{:S(2)}, u32[]{:S(2)}) collective-permute-start(bf16[2,32,4096]{2,1,0:T(8,128)(2,1)} %get-tuple-element.47), channel_id=1, source_target_pairs={{0,1},{1,2},{2,3},{3,0},{4,5},{5,6},{6,7},{7,4},{8,9},{9,10},{10,1... | collective-permute-start | bytes 1572872 | tf_op jit(solution)/shard_map/ppermute | solution.py:28
  11.4 29.1 %collective-permute-start.8 = (bf16[2,32,4096]{2,1,0:T(8,128)(2,1)}, bf16[2,32,4096]{2,1,0:T(8,128)(2,1)S(1)}, u32[]{:S(2)}, u32[]{:S(2)}) collective-permute-start(bf16[2,32,4096]{2,1,0:T(8,128)(2,1)} %get-tuple-element.59), channel_id=1, source_target_pairs={{0,3},{1,0},{2,1},{3,2},{4,7},{5,4},{6,5},{7,6},{8,11},{9,8},{10,9... | collective-permute-start | bytes 1572872 | tf_op jit(solution)/shard_map/ppermute | solution.py:28
  16.0 11.7 %collective-permute-start.5 = (bf16[4,2,32,512]{3,2,1,0:T(8,128)(2,1)S(1)}, bf16[4,2,32,512]{3,2,1,0:T(8,128)(2,1)}, u32[]{:S(2)}, u32[]{:S(2)}) collective-permute-start(bf16[4,2,32,512]{3,2,1,0:T(8,128)(2,1)S(1)} %bitcast_dynamic-update-slice_fusion), channel_id=1, source_target_pairs={{0,4},{4,8},{8,12},{12,16},{16,20},{20,24},{24,28},{1,5},{5,9},{9,... | collective-permute-start | bytes 786440 | tf_op jit(solution)/shard_map/ppermute | solution.py:34
  19.1 10.5 %collective-permute-start.4 = (bf16[4,2,32,512]{3,2,1,0:T(8,128)(2,1)S(1)}, bf16[4,2,32,512]{3,2,1,0:T(8,128)(2,1)}, u32[]{:S(2)}, u32[]{:S(2)}) collective-permute-start(bf16[4,2,32,512]{3,2,1,0:T(8,128)(2,1)S(1)} %bitcast_dynamic-update-slice_fusion), channel_id=1, source_target_pairs={{0,8},{4,12},{8,16},{12,20},{16,24},{20,28},{1,9},{5,13},{9,17},{1... | collective-permute-start | bytes 786440 | tf_op jit(solution)/shard_map/ppermute | solution.py:34
  30.8 3.6 %copy-start.5 = (bf16[2,32,2048]{2,1,0:T(8,128)(2,1)S(1)}, bf16[2,32,2048]{2,1,0:T(8,128)(2,1)}, u32[]{:S(2)}) copy-start(bf16[2,32,2048]{2,1,0:T(8,128)(2,1)} %get-tuple-element.63) | copy-start | bytes 786436
  34.4 19.6 %collective-permute-start.9 = (bf16[2,32,2048]{2,1,0:T(8,128)(2,1)S(1)}, bf16[2,32,2048]{2,1,0:T(8,128)(2,1)S(1)}, u32[]{:S(2)}, u32[]{:S(2)}) collective-permute-start(bf16[2,32,2048]{2,1,0:T(8,128)(2,1)S(1)} %copy-done.5), channel_id=1, source_target_pairs={{0,2},{1,3},{2,0},{3,1},{4,6},{5,7},{6,4},{7,5},{8,10},{9,11},{10,... | collective-permute-start | bytes 786440 | tf_op jit(solution)/shard_map/ppermute | solution.py:28
  34.5 3.6 %copy-start.7 = (bf16[1,32,2048]{2,1,0:T(8,128)(2,1)S(1)}, bf16[1,32,2048]{2,1,0:T(8,128)(2,1)}, u32[]{:S(2)}) copy-start(bf16[1,32,2048]{2,1,0:T(8,128)(2,1)} %get-tuple-element.57) | copy-start | bytes 393220
  34.5 6.0 %copy-start.6 = (bf16[1,32,2048]{2,1,0:T(8,128)(2,1)S(1)}, bf16[1,32,2048]{2,1,0:T(8,128)(2,1)}, u32[]{:S(2)}) copy-start(bf16[1,32,2048]{2,1,0:T(8,128)(2,1)} %get-tuple-element.58) | copy-start | bytes 393220
  38.1 24.3 %collective-permute-start.6 = (bf16[1,32,2048]{2,1,0:T(8,128)(2,1)S(1)}, bf16[1,32,2048]{2,1,0:T(8,128)(2,1)S(1)}, u32[]{:S(2)}, u32[]{:S(2)}) collective-permute-start(bf16[1,32,2048]{2,1,0:T(8,128)(2,1)S(1)} %copy-done.7), channel_id=1, source_target_pairs={{0,2},{1,3},{2,0},{3,1},{4,6},{5,7},{6,4},{7,5},{8,10},{9,11},{10,... | collective-permute-start | bytes 393224 | tf_op jit(solution)/shard_map/ppermute | solution.py:28
  40.4 22.0 %collective-permute-start.7 = (bf16[1,32,2048]{2,1,0:T(8,128)(2,1)S(1)}, bf16[1,32,2048]{2,1,0:T(8,128)(2,1)S(1)}, u32[]{:S(2)}, u32[]{:S(2)}) collective-permute-start(bf16[1,32,2048]{2,1,0:T(8,128)(2,1)S(1)} %copy-done.6), channel_id=1, source_target_pairs={{0,2},{1,3},{2,0},{3,1},{4,6},{5,7},{6,4},{7,5},{8,10},{9,11},{10,... | collective-permute-start | bytes 393224 | tf_op jit(solution)/shard_map/ppermute | solution.py:28
  56.4 8.4 %collective-permute-start.10 = (bf16[2,128,256]{2,1,0:T(8,128)(2,1)S(1)}, bf16[2,128,256]{2,1,0:T(8,128)(2,1)S(1)}, u32[]{:S(2)}, u32[]{:S(2)}) collective-permute-start(bf16[2,128,256]{2,1,0:T(8,128)(2,1)S(1)} %get-tuple-element.68), channel_id=1, source_target_pairs={{4,0},{8,4},{12,8},{16,12},{20,16},{24,20},{28,24},{5,1},{9,5},{13... | collective-permute-start | bytes 393224 | tf_op jit(solution)/shard_map/ppermute | solution.py:34
  60.5 8.4 %collective-permute-start.11 = (bf16[2,128,256]{2,1,0:T(8,128)(2,1)S(1)}, bf16[2,128,256]{2,1,0:T(8,128)(2,1)S(1)}, u32[]{:S(2)}, u32[]{:S(2)}) collective-permute-start(bf16[2,128,256]{2,1,0:T(8,128)(2,1)S(1)} %get-tuple-element.69), channel_id=1, source_target_pairs={{8,0},{12,4},{16,8},{20,12},{24,16},{28,20},{9,1},{13,5},{17,9},{2... | collective-permute-start | bytes 393224 | tf_op jit(solution)/shard_map/ppermute | solution.py:34
  64.8 7.1 %collective-permute-start.12 = (bf16[2,128,256]{2,1,0:T(8,128)(2,1)S(1)}, bf16[2,128,256]{2,1,0:T(8,128)(2,1)S(1)}, u32[]{:S(2)}, u32[]{:S(2)}) collective-permute-start(bf16[2,128,256]{2,1,0:T(8,128)(2,1)S(1)} %get-tuple-element.73), channel_id=1, source_target_pairs={{4,0},{8,4},{12,8},{16,12},{20,16},{24,20},{28,24},{5,1},{9,5},{13... | collective-permute-start | bytes 393224 | tf_op jit(solution)/shard_map/ppermute | solution.py:34
  66.9 6.7 %collective-permute-start.13 = (bf16[2,128,256]{2,1,0:T(8,128)(2,1)S(1)}, bf16[2,128,256]{2,1,0:T(8,128)(2,1)S(1)}, u32[]{:S(2)}, u32[]{:S(2)}) collective-permute-start(bf16[2,128,256]{2,1,0:T(8,128)(2,1)S(1)} %get-tuple-element.74), channel_id=1, source_target_pairs={{8,0},{12,4},{16,8},{20,12},{24,16},{28,20},{9,1},{13,5},{17,9},{2... | collective-permute-start | bytes 393224 | tf_op jit(solution)/shard_map/ppermute | solution.py:34

commit v20 on v19

--- a/solution.py
+++ b/solution.py
@@ -277,8 +277,7 @@
     others = [step for step in range(1, count) if step != final]
     jobs = [(2, step, 0, kv_width) for step in range(count)]
     jobs += [(0, step, 0, width) for step in others]
-    jobs += [(0, final, half * part, part) for half in range(halves - 1)]
-    jobs += [(which, final, (halves - 1) * part, part, 1) for which in range(2)]
+    jobs += [(which, final, half * part, part, 1) for half in range(halves) for which in range(2)]
     staged = stage(assignment, (queries, grad_out, keys, values), jobs)
     kv_staged, staged = staged[:count], list(staged[count:])
     kv_arrived = [exchanged(kv_staged[step], "dp", step) for step in range(1, count)]
@@ -299,17 +298,16 @@
     rows, acc = lax.optimization_barrier((held[0], acc))
     split = [exchanged(rows, "dp", final)]
     for at, (step, both) in enumerate(zip(others, arrived)):
+        if not at:
+            rows, both = lax.optimization_barrier((held[1], both))
+            split.append(exchanged(rows, "dp", final))
         query, grad = (both, lambda m, a: 0), (both, lambda m, a: 1)
         full, acc = attend(step, 0, kv_heads, *fixed, query, grad, kv, acc, full, False)
-        if not at:
-            rows, acc = lax.optimization_barrier((held[1:], acc))
-            split += [exchanged(piece, "dp", final) for piece in rows]
+        rows, acc = lax.optimization_barrier((held[2 + at], acc))
+        split.append(exchanged(rows, "dp", final))
     totals, returned = [], []
     for half in range(halves):
-        both = split[half]
-        query, grad = (both, lambda m, a: 0), (both, lambda m, a: 1)
-        if half + 1 == halves:
-            grad = (split[half + 1], lambda m, a: 0)
+        query, grad = [(rows, lambda m, a: 0) for rows in split[2 * half : 2 * half + 2]]
         full, total, *halos = attend(
             final, half * HEADS_STEP, HEADS_STEP, *fixed, query, grad, kv, acc, full, True
         )

time: 74.8 us -> 74.3 us (level)
  waiting for transfers between devices: 19.5 us -> 15.3 us
  starting transfers between devices: 30 us -> 33.6 us
    ppermute x8 -> x9, waiting for transfers between devices: 9.95 us -> 6.28 us  [exchanged(): lax.ppermute(value, axis, [(i, (i + step) % count) for i in range(count)])]
    ppermute x8 -> x9, starting transfers between devices: 11.2 us -> 13.5 us  [exchanged(): lax.ppermute(value, axis, [(i, (i + step) % count) for i in range(count)])]
    ppermute x6, starting transfers between devices: 18.8 us -> 20.1 us  [shifted(): return lax.ppermute(value, axis, pairs)]
  transfers between devices with their start and end apart: 14 -> 15, of which waited for: 5 -> 6; matrix products, arithmetic and copies ran while one was open for 5% -> 5% of each run, Pallas kernels for 21% -> 21%
where the time goes in v20:
time: 74.3 us; the launch traced here: 73.9 us
  starting transfers between devices  33.6 us (45%)
  Pallas kernels  18.8 us (25%)
  waiting for transfers between devices  15.3 us (21%)
  local copies, waits for them, and re-layouts  3.24 us (4%)
  other arithmetic  2.01 us (3%)
  between operations  0.85 us (1%)
    ppermute x6, starting transfers between devices, shifted(): return lax.ppermute(value, axis, pairs)  20.1 us
    pallas_call x5, Pallas kernels, attend(): pl.pallas_call(functools.partial(attend_kernel, step, first, filled, last...  15.6 us
    ppermute x9, starting transfers between devices, exchanged(): lax.ppermute(value, axis, [(i, (i + step) % count) for i in range(count)])  13.5 us
    ppermute x6, waiting for transfers between devices, shifted(): return lax.ppermute(value, axis, pairs)  9.05 us
    ppermute x9, waiting for transfers between devices, exchanged(): lax.ppermute(value, axis, [(i, (i + step) % count) for i in range(count)])  6.28 us
    pallas_call x1, Pallas kernels, stage(): pl.pallas_call(functools.partial(stage_kernel, count, jobs, len(jobs)), o...  3.27 us
    dynamic_update_slice x4, local copies, waits for them, and re-layouts, shards(): lax.dynamic_update_index_in_dim(kv_own, piece, source_of(group, step, cou...  2.55 us
  transfers between devices with their start and end apart: 15, of which 6 were waited for; matrix products, arithmetic and copies ran while one was open for 5% of the time, Pallas kernels for 21%

profile of v20, /device:TPU:1, one launch (start us, length us, event | category | flops | bytes accessed | tf_op | source)
XLA Modules:
  0.0 73.9 jit_solution(1810955128431006292)
XLA Ops:
  0.6 3.3 %stage.1 = (bf16[2,32,512]{2,1,0:T(8,128)(2,1)}, bf16[2,32,512]{2,1,0:T(8,128)(2,1)}, bf16[2,32,512]{2,1,0:T(8,128)(2,1)}, bf16[2,32,512]{2,1,0:T(8,128)(2,1)}, ...) custom-call(s32[4]{0:T(128)} %assign_ref.11, ...), custom_call_target="tpu_custom_call" | custom-call | tf_op jit(solution)/shard_map/stage/pallas_call | solution.py:63
  4.0 2.2 %collective-permute-start = (bf16[2,32,512]{2,1,0:T(8,128)(2,1)}, bf16[2,32,512]{2,1,0:T(8,128)(2,1)S(1)}, u32[]{:S(2)}, u32[]{:S(2)}) collective-permute-start(bf16[2,32,512]{2,1,0:T(8,128)(2,1)} %get-tuple-element.50), channel_id=1, source_target_pairs={{0,1},{1,2},{2,3},{3,0},{4,5},{5,6},{6,7},{7,4},{8,9},{9,10},{10,1... | collective-permute-start | bytes 196616 | tf_op jit(solution)/shard_map/ppermute | solution.py:28
  6.1 2.3 %collective-permute-start.2 = (bf16[2,32,512]{2,1,0:T(8,128)(2,1)}, bf16[2,32,512]{2,1,0:T(8,128)(2,1)}, u32[]{:S(2)}, u32[]{:S(2)}) collective-permute-start(bf16[2,32,512]{2,1,0:T(8,128)(2,1)} %get-tuple-element.57), channel_id=1, source_target_pairs={{0,2},{1,3},{2,0},{3,1},{4,6},{5,7},{6,4},{7,5},{8,10},{9,11},{10,... | collective-permute-start | bytes 196616 | tf_op jit(solution)/shard_map/ppermute | solution.py:28
  8.4 1.1 %collective-permute-start.3 = (bf16[2,32,512]{2,1,0:T(8,128)(2,1)}, bf16[2,32,512]{2,1,0:T(8,128)(2,1)S(1)}, u32[]{:S(2)}, u32[]{:S(2)}) collective-permute-start(bf16[2,32,512]{2,1,0:T(8,128)(2,1)} %get-tuple-element.58), channel_id=1, source_target_pairs={{0,3},{1,0},{2,1},{3,2},{4,7},{5,4},{6,5},{7,6},{8,11},{9,8},{10,9... | collective-permute-start | bytes 196616 | tf_op jit(solution)/shard_map/ppermute | solution.py:28
  11.4 2.9 %collective-permute-start.7 = (bf16[2,32,4096]{2,1,0:T(8,128)(2,1)}, bf16[2,32,4096]{2,1,0:T(8,128)(2,1)S(1)}, u32[]{:S(2)}, u32[]{:S(2)}) collective-permute-start(bf16[2,32,4096]{2,1,0:T(8,128)(2,1)} %get-tuple-element.66), channel_id=1, source_target_pairs={{0,3},{1,0},{2,1},{3,2},{4,7},{5,4},{6,5},{7,6},{8,11},{9,8},{10,9... | collective-permute-start | bytes 1572872 | tf_op jit(solution)/shard_map/ppermute | solution.py:28
  16.0 3.1 %collective-permute-start.5 = (bf16[4,2,32,512]{3,2,1,0:T(8,128)(2,1)S(1)}, bf16[4,2,32,512]{3,2,1,0:T(8,128)(2,1)}, u32[]{:S(2)}, u32[]{:S(2)}) collective-permute-start(bf16[4,2,32,512]{3,2,1,0:T(8,128)(2,1)S(1)} %bitcast_dynamic-update-slice_fusion), channel_id=1, source_target_pairs={{0,4},{4,8},{8,12},{12,16},{16,20},{20,24},{24,28},{1,5},{5,9},{9,... | collective-permute-start | bytes 786440 | tf_op jit(solution)/shard_map/ppermute | solution.py:34
  19.1 5.7 %collective-permute-start.4 = (bf16[4,2,32,512]{3,2,1,0:T(8,128)(2,1)S(1)}, bf16[4,2,32,512]{3,2,1,0:T(8,128)(2,1)}, u32[]{:S(2)}, u32[]{:S(2)}) collective-permute-start(bf16[4,2,32,512]{3,2,1,0:T(8,128)(2,1)S(1)} %bitcast_dynamic-update-slice_fusion), channel_id=1, source_target_pairs={{0,8},{4,12},{8,16},{12,20},{16,24},{20,28},{1,9},{5,13},{9,17},{1... | collective-permute-start | bytes 786440 | tf_op jit(solution)/shard_map/ppermute | solution.py:34
  24.9 2.7 %collective-permute-done.5 = bf16[4,2,32,512]{3,2,1,0:T(8,128)(2,1)} collective-permute-done((bf16[4,2,32,512]{3,2,1,0:T(8,128)(2,1)S(1)}, bf16[4,2,32,512]{3,2,1,0:T(8,128)(2,1)}, u32[]{:S(2)}, u32[]{:S(2)}) %collective-permute-start.5) | collective-permute-done | bytes 262176 | tf_op jit(solution)/shard_map/ppermute | solution.py:34
  27.6 2.0 %collective-permute-done.4 = bf16[4,2,32,512]{3,2,1,0:T(8,128)(2,1)} collective-permute-done((bf16[4,2,32,512]{3,2,1,0:T(8,128)(2,1)S(1)}, bf16[4,2,32,512]{3,2,1,0:T(8,128)(2,1)}, u32[]{:S(2)}, u32[]{:S(2)}) %collective-permute-start.4) | collective-permute-done | bytes 262176 | tf_op jit(solution)/shard_map/ppermute | solution.py:34
  29.7 1.1 %pad_maximum_fusion.kv_ref = bf16[12,2,32,512]{3,2,1,0:T(8,128)(2,1)S(1)} fusion(bf16[4,2,32,512]{3,2,1,0:T(8,128)(2,1)S(1)} %bitcast_dynamic-update-slice_fusion, bf16[4,2,32,512]{3,2,1,0:T(8,128)(2,1)} %collective-permute-done.5, bf16[4,2,32,512]{3,2,1,0:T(8,128)(2,1)} %collective-permute-done.4), kind=kLoop, calls=%fused_computation | loop fusion | flops 786432 | bytes 1572864 | tf_op jit(solution)/shard_map/concatenate | solution.py:293
  30.9 3.6 %attend.5 = (bf16[128,32,128]{2,1,0:T(8,128)(2,1)}, f32[2,384,512]{2,1,0:T(8,128)S(1)}) custom-call(s32[2]{0:T(128)S(1)} %pad_add_fusion.meta_ref, s32[4]{0:T(128)S(1)} %copy-done.3, s32[4,1024]{1,0:T(4,128)S(1)} %copy-done.2, bf16[4,32,4096]{2,1,0:T(8,128)(2,1)S(1)} %copy-done, bf16[4,32,4096]{2,1,0:T(8,128)(2,1)S(1)} %copy-done.1, ...), custom_call_target="tpu_custom_call" | custom-call | flops 37748736 | bytes 294912 | tf_op jit(solution)/shard_map/attend/pallas_call | solution.py:242
  34.5 2.4 %collective-permute-start.10 = (bf16[1,32,2048]{2,1,0:T(8,128)(2,1)S(1)}, bf16[1,32,2048]{2,1,0:T(8,128)(2,1)S(1)}, u32[]{:S(2)}, u32[]{:S(2)}) collective-permute-start(bf16[1,32,2048]{2,1,0:T(8,128)(2,1)S(1)} %copy-done.7), channel_id=1, source_target_pairs={{0,2},{1,3},{2,0},{3,1},{4,6},{5,7},{6,4},{7,5},{8,10},{9,11},{10,... | collective-permute-start | bytes 393224 | tf_op jit(solution)/shard_map/ppermute | solution.py:28
  36.9 3.6 %attend.6 = (bf16[128,32,128]{2,1,0:T(8,128)(2,1)}, f32[2,384,512]{2,1,0:T(8,128)S(1)}) custom-call(s32[2]{0:T(128)S(1)} %pad_add_fusion.meta_ref, s32[4]{0:T(128)S(1)} %copy-done.3, s32[4,1024]{1,0:T(4,128)S(1)} %copy-done.2, bf16[2,32,4096]{2,1,0:T(8,128)(2,1)S(1)} %collective-permute-done.1.query_ref.grad_ref, ...), custom_call_target="tpu_custom_call", output_to_operand_aliasing={{1}: (6, {}), {0}: (7, {})} | custom-call | flops 37748736 | bytes 294912 | tf_op jit(solution)/shard_map/attend/pallas_call | solution.py:242
  40.6 3.6 %attend.7 = (bf16[128,32,128]{2,1,0:T(8,128)(2,1)}, f32[2,384,512]{2,1,0:T(8,128)S(1)}) custom-call(s32[2]{0:T(128)S(1)} %pad_add_fusion.meta_ref, s32[4]{0:T(128)S(1)} %copy-done.3, s32[4,1024]{1,0:T(4,128)S(1)} %copy-done.2, bf16[2,32,4096]{2,1,0:T(8,128)(2,1)S(1)} %collective-permute-done.7.query_ref.grad_ref, ...), custom_call_target="tpu_custom_call", output_to_operand_aliasing={{1}: (6, {}), {0}: (7, {})} | custom-call | flops 3774873600 | bytes 29491200 | tf_op jit(solution)/shard_map/attend/pallas_call | solution.py:242
  44.2 2.3 %collective-permute-start.8 = (bf16[1,32,2048]{2,1,0:T(8,128)(2,1)S(1)}, bf16[1,32,2048]{2,1,0:T(8,128)(2,1)S(1)}, u32[]{:S(2)}, u32[]{:S(2)}) collective-permute-start(bf16[1,32,2048]{2,1,0:T(8,128)(2,1)S(1)} %copy-done.5), channel_id=1, source_target_pairs={{0,2},{1,3},{2,0},{3,1},{4,6},{5,7},{6,4},{7,5},{8,10},{9,11},{10,... | collective-permute-start | bytes 393224 | tf_op jit(solution)/shard_map/ppermute | solution.py:28
  47.1 5.6 %collective-permute-done.10.grad_ref = bf16[1,32,2048]{2,1,0:T(8,128)(2,1)S(1)} collective-permute-done((bf16[1,32,2048]{2,1,0:T(8,128)(2,1)S(1)}, bf16[1,32,2048]{2,1,0:T(8,128)(2,1)S(1)}, u32[]{:S(2)}, u32[]{:S(2)}) %collective-permute-start.10) | collective-permute-done | bytes 131104 | tf_op jit(solution)/shard_map/ppermute | solution.py:28
  52.7 2.4 %attend.8 = (bf16[128,32,128]{2,1,0:T(8,128)(2,1)}, f32[2,128,256]{2,1,0:T(8,128)S(1)}, bf16[2,128,256]{2,1,0:T(8,128)(2,1)S(1)}, bf16[2,128,256]{2,1,0:T(8,128)(2,1)S(1)}) custom-call(s32[2]{0:T(128)S(1)} %pad_add_fusion.meta_ref, s32[4]{0:T(128)S(1)} %copy-done.3, s32[4,1024]{1,0:T(4,128)S(1)} %copy-done.2, ...), custom_call_target="tpu_custom_call", output_to_operand_aliasing={{0}: (7, {})} | custom-call | flops 18874368 | bytes 147456 | tf_op jit(solution)/shard_map/attend/pallas_call | solution.py:242
  55.1 5.5 %collective-permute-start.11 = (bf16[2,128,256]{2,1,0:T(8,128)(2,1)S(1)}, bf16[2,128,256]{2,1,0:T(8,128)(2,1)S(1)}, u32[]{:S(2)}, u32[]{:S(2)}) collective-permute-start(bf16[2,128,256]{2,1,0:T(8,128)(2,1)S(1)} %get-tuple-element.78), channel_id=1, source_target_pairs={{4,0},{8,4},{12,8},{16,12},{20,16},{24,20},{28,24},{5,1},{9,5},{13... | collective-permute-start | bytes 393224 | tf_op jit(solution)/shard_map/ppermute | solution.py:34
  60.6 1.9 %collective-permute-start.12 = (bf16[2,128,256]{2,1,0:T(8,128)(2,1)S(1)}, bf16[2,128,256]{2,1,0:T(8,128)(2,1)S(1)}, u32[]{:S(2)}, u32[]{:S(2)}) collective-permute-start(bf16[2,128,256]{2,1,0:T(8,128)(2,1)S(1)} %get-tuple-element.79), channel_id=1, source_target_pairs={{8,0},{12,4},{16,8},{20,12},{24,16},{28,20},{9,1},{13,5},{17,9},{2... | collective-permute-start | bytes 393224 | tf_op jit(solution)/shard_map/ppermute | solution.py:34
  62.5 2.4 %attend.9 = (bf16[128,32,128]{2,1,0:T(8,128)(2,1)}, f32[2,128,256]{2,1,0:T(8,128)S(1)}, bf16[2,128,256]{2,1,0:T(8,128)(2,1)S(1)}, bf16[2,128,256]{2,1,0:T(8,128)(2,1)S(1)}) custom-call(s32[2]{0:T(128)S(1)} %pad_add_fusion.meta_ref, s32[4]{0:T(128)S(1)} %copy-done.3, s32[4,1024]{1,0:T(4,128)S(1)} %copy-done.2, ...), custom_call_target="tpu_custom_call", output_to_operand_aliasing={{0}: (7, {})} | custom-call | flops 18874368 | bytes 147456 | tf_op jit(solution)/shard_map/attend/pallas_call | solution.py:242
  64.9 1.9 %collective-permute-start.13 = (bf16[2,128,256]{2,1,0:T(8,128)(2,1)S(1)}, bf16[2,128,256]{2,1,0:T(8,128)(2,1)S(1)}, u32[]{:S(2)}, u32[]{:S(2)}) collective-permute-start(bf16[2,128,256]{2,1,0:T(8,128)(2,1)S(1)} %get-tuple-element.83), channel_id=1, source_target_pairs={{4,0},{8,4},{12,8},{16,12},{20,16},{24,20},{28,24},{5,1},{9,5},{13... | collective-permute-start | bytes 393224 | tf_op jit(solution)/shard_map/ppermute | solution.py:34
  66.8 1.9 %collective-permute-start.14 = (bf16[2,128,256]{2,1,0:T(8,128)(2,1)S(1)}, bf16[2,128,256]{2,1,0:T(8,128)(2,1)S(1)}, u32[]{:S(2)}, u32[]{:S(2)}) collective-permute-start(bf16[2,128,256]{2,1,0:T(8,128)(2,1)S(1)} %get-tuple-element.84), channel_id=1, source_target_pairs={{8,0},{12,4},{16,8},{20,12},{24,16},{28,20},{9,1},{13,5},{17,9},{2... | collective-permute-start | bytes 393224 | tf_op jit(solution)/shard_map/ppermute | solution.py:34
  68.8 2.6 %collective-permute-done.13 = bf16[2,128,256]{2,1,0:T(8,128)(2,1)S(1)} collective-permute-done((bf16[2,128,256]{2,1,0:T(8,128)(2,1)S(1)}, bf16[2,128,256]{2,1,0:T(8,128)(2,1)S(1)}, u32[]{:S(2)}, u32[]{:S(2)}) %collective-permute-start.13) | collective-permute-done | bytes 131104 | tf_op jit(solution)/shard_map/ppermute | solution.py:34
  71.4 1.7 %collective-permute-done.14 = bf16[2,128,256]{2,1,0:T(8,128)(2,1)S(1)} collective-permute-done((bf16[2,128,256]{2,1,0:T(8,128)(2,1)S(1)}, bf16[2,128,256]{2,1,0:T(8,128)(2,1)S(1)}, u32[]{:S(2)}, u32[]{:S(2)}) %collective-permute-start.14) | collective-permute-done | bytes 131104 | tf_op jit(solution)/shard_map/ppermute | solution.py:34
  (40 shorter events, 5.3 us)
Async XLA Ops:
  3.9 26.9 %copy-start = (bf16[4,32,4096]{2,1,0:T(8,128)(2,1)S(1)}, bf16[4,32,4096]{2,1,0:T(8,128)(2,1)}, u32[]{:S(2)}) copy-start(bf16[4,32,4096]{2,1,0:T(8,128)(2,1)} %query_ref.1) | copy-start | bytes 3145732
  3.9 26.9 %copy-start.1 = (bf16[4,32,4096]{2,1,0:T(8,128)(2,1)S(1)}, bf16[4,32,4096]{2,1,0:T(8,128)(2,1)}, u32[]{:S(2)}) copy-start(bf16[4,32,4096]{2,1,0:T(8,128)(2,1)} %grad_ref.1) | copy-start | bytes 3145732
  3.9 26.9 %copy-start.2 = (s32[4,1024]{1,0:T(4,128)S(1)}, s32[4,1024]{1,0:T(4,128)}, u32[]{:S(2)}) copy-start(s32[4,1024]{1,0:T(4,128)} %segment_ref.9) | copy-start | bytes 49156
  3.9 26.9 %copy-start.3 = (s32[4]{0:T(128)S(1)}, s32[4]{0:T(128)}, u32[]{:S(2)}) copy-start(s32[4]{0:T(128)} %assign_ref.11) | copy-start | bytes 52
  4.0 6.4 %collective-permute-start = (bf16[2,32,512]{2,1,0:T(8,128)(2,1)}, bf16[2,32,512]{2,1,0:T(8,128)(2,1)S(1)}, u32[]{:S(2)}, u32[]{:S(2)}) collective-permute-start(bf16[2,32,512]{2,1,0:T(8,128)(2,1)} %get-tuple-element.50), channel_id=1, source_target_pairs={{0,1},{1,2},{2,3},{3,0},{4,5},{5,6},{6,7},{7,4},{8,9},{9,10},{10,1... | collective-permute-start | bytes 196616 | tf_op jit(solution)/shard_map/ppermute | solution.py:28
  6.1 9.0 %collective-permute-start.2 = (bf16[2,32,512]{2,1,0:T(8,128)(2,1)}, bf16[2,32,512]{2,1,0:T(8,128)(2,1)}, u32[]{:S(2)}, u32[]{:S(2)}) collective-permute-start(bf16[2,32,512]{2,1,0:T(8,128)(2,1)} %get-tuple-element.57), channel_id=1, source_target_pairs={{0,2},{1,3},{2,0},{3,1},{4,6},{5,7},{6,4},{7,5},{8,10},{9,11},{10,... | collective-permute-start | bytes 196616 | tf_op jit(solution)/shard_map/ppermute | solution.py:28
  8.4 7.5 %collective-permute-start.3 = (bf16[2,32,512]{2,1,0:T(8,128)(2,1)}, bf16[2,32,512]{2,1,0:T(8,128)(2,1)S(1)}, u32[]{:S(2)}, u32[]{:S(2)}) collective-permute-start(bf16[2,32,512]{2,1,0:T(8,128)(2,1)} %get-tuple-element.58), channel_id=1, source_target_pairs={{0,3},{1,0},{2,1},{3,2},{4,7},{5,4},{6,5},{7,6},{8,11},{9,8},{10,9... | collective-permute-start | bytes 196616 | tf_op jit(solution)/shard_map/ppermute | solution.py:28
  10.4 0.6 copy-start.4
  11.0 23.5 %collective-permute-start.1 = (bf16[2,32,4096]{2,1,0:T(8,128)(2,1)}, bf16[2,32,4096]{2,1,0:T(8,128)(2,1)S(1)}, u32[]{:S(2)}, u32[]{:S(2)}) collective-permute-start(bf16[2,32,4096]{2,1,0:T(8,128)(2,1)} %get-tuple-element.53), channel_id=1, source_target_pairs={{0,1},{1,2},{2,3},{3,0},{4,5},{5,6},{6,7},{7,4},{8,9},{9,10},{10,1... | collective-permute-start | bytes 1572872 | tf_op jit(solution)/shard_map/ppermute | solution.py:28
  11.4 29.1 %collective-permute-start.7 = (bf16[2,32,4096]{2,1,0:T(8,128)(2,1)}, bf16[2,32,4096]{2,1,0:T(8,128)(2,1)S(1)}, u32[]{:S(2)}, u32[]{:S(2)}) collective-permute-start(bf16[2,32,4096]{2,1,0:T(8,128)(2,1)} %get-tuple-element.66), channel_id=1, source_target_pairs={{0,3},{1,0},{2,1},{3,2},{4,7},{5,4},{6,5},{7,6},{8,11},{9,8},{10,9... | collective-permute-start | bytes 1572872 | tf_op jit(solution)/shard_map/ppermute | solution.py:28
  16.0 11.7 %collective-permute-start.5 = (bf16[4,2,32,512]{3,2,1,0:T(8,128)(2,1)S(1)}, bf16[4,2,32,512]{3,2,1,0:T(8,128)(2,1)}, u32[]{:S(2)}, u32[]{:S(2)}) collective-permute-start(bf16[4,2,32,512]{3,2,1,0:T(8,128)(2,1)S(1)} %bitcast_dynamic-update-slice_fusion), channel_id=1, source_target_pairs={{0,4},{4,8},{8,12},{12,16},{16,20},{20,24},{24,28},{1,5},{5,9},{9,... | collective-permute-start | bytes 786440 | tf_op jit(solution)/shard_map/ppermute | solution.py:34
  19.1 10.5 %collective-permute-start.4 = (bf16[4,2,32,512]{3,2,1,0:T(8,128)(2,1)S(1)}, bf16[4,2,32,512]{3,2,1,0:T(8,128)(2,1)}, u32[]{:S(2)}, u32[]{:S(2)}) collective-permute-start(bf16[4,2,32,512]{3,2,1,0:T(8,128)(2,1)S(1)} %bitcast_dynamic-update-slice_fusion), channel_id=1, source_target_pairs={{0,8},{4,12},{8,16},{12,20},{16,24},{20,28},{1,9},{5,13},{9,17},{1... | collective-permute-start | bytes 786440 | tf_op jit(solution)/shard_map/ppermute | solution.py:34
  30.8 3.7 %copy-start.8 = (bf16[1,32,2048]{2,1,0:T(8,128)(2,1)S(1)}, bf16[1,32,2048]{2,1,0:T(8,128)(2,1)}, u32[]{:S(2)}) copy-start(bf16[1,32,2048]{2,1,0:T(8,128)(2,1)} %get-tuple-element.72) | copy-start | bytes 393220
  30.8 3.7 %copy-start.7 = (bf16[1,32,2048]{2,1,0:T(8,128)(2,1)S(1)}, bf16[1,32,2048]{2,1,0:T(8,128)(2,1)}, u32[]{:S(2)}) copy-start(bf16[1,32,2048]{2,1,0:T(8,128)(2,1)} %get-tuple-element.73) | copy-start | bytes 393220
  34.5 12.6 %collective-permute-start.9 = (bf16[1,32,2048]{2,1,0:T(8,128)(2,1)S(1)}, bf16[1,32,2048]{2,1,0:T(8,128)(2,1)S(1)}, u32[]{:S(2)}, u32[]{:S(2)}) collective-permute-start(bf16[1,32,2048]{2,1,0:T(8,128)(2,1)S(1)} %copy-done.8), channel_id=1, source_target_pairs={{0,2},{1,3},{2,0},{3,1},{4,6},{5,7},{6,4},{7,5},{8,10},{9,11},{10,... | collective-permute-start | bytes 393224 | tf_op jit(solution)/shard_map/ppermute | solution.py:28
  34.5 18.2 %collective-permute-start.10 = (bf16[1,32,2048]{2,1,0:T(8,128)(2,1)S(1)}, bf16[1,32,2048]{2,1,0:T(8,128)(2,1)S(1)}, u32[]{:S(2)}, u32[]{:S(2)}) collective-permute-start(bf16[1,32,2048]{2,1,0:T(8,128)(2,1)S(1)} %copy-done.7), channel_id=1, source_target_pairs={{0,2},{1,3},{2,0},{3,1},{4,6},{5,7},{6,4},{7,5},{8,10},{9,11},{10,... | collective-permute-start | bytes 393224 | tf_op jit(solution)/shard_map/ppermute | solution.py:28
  36.9 3.6 %copy-start.6 = (bf16[1,32,2048]{2,1,0:T(8,128)(2,1)S(1)}, bf16[1,32,2048]{2,1,0:T(8,128)(2,1)}, u32[]{:S(2)}) copy-start(bf16[1,32,2048]{2,1,0:T(8,128)(2,1)} %get-tuple-element.64) | copy-start | bytes 393220
  40.5 22.0 %collective-permute-start.6 = (bf16[1,32,2048]{2,1,0:T(8,128)(2,1)S(1)}, bf16[1,32,2048]{2,1,0:T(8,128)(2,1)S(1)}, u32[]{:S(2)}, u32[]{:S(2)}) collective-permute-start(bf16[1,32,2048]{2,1,0:T(8,128)(2,1)S(1)} %copy-done.6), channel_id=1, source_target_pairs={{0,2},{1,3},{2,0},{3,1},{4,6},{5,7},{6,4},{7,5},{8,10},{9,11},{10,... | collective-permute-start | bytes 393224 | tf_op jit(solution)/shard_map/ppermute | solution.py:28
  40.6 3.6 %copy-start.5 = (bf16[1,32,2048]{2,1,0:T(8,128)(2,1)S(1)}, bf16[1,32,2048]{2,1,0:T(8,128)(2,1)}, u32[]{:S(2)}) copy-start(bf16[1,32,2048]{2,1,0:T(8,128)(2,1)} %get-tuple-element.70) | copy-start | bytes 393220
  44.2 18.3 %collective-permute-start.8 = (bf16[1,32,2048]{2,1,0:T(8,128)(2,1)S(1)}, bf16[1,32,2048]{2,1,0:T(8,128)(2,1)S(1)}, u32[]{:S(2)}, u32[]{:S(2)}) collective-permute-start(bf16[1,32,2048]{2,1,0:T(8,128)(2,1)S(1)} %copy-done.5), channel_id=1, source_target_pairs={{0,2},{1,3},{2,0},{3,1},{4,6},{5,7},{6,4},{7,5},{8,10},{9,11},{10,... | collective-permute-start | bytes 393224 | tf_op jit(solution)/shard_map/ppermute | solution.py:28
  55.1 9.8 %collective-permute-start.11 = (bf16[2,128,256]{2,1,0:T(8,128)(2,1)S(1)}, bf16[2,128,256]{2,1,0:T(8,128)(2,1)S(1)}, u32[]{:S(2)}, u32[]{:S(2)}) collective-permute-start(bf16[2,128,256]{2,1,0:T(8,128)(2,1)S(1)} %get-tuple-element.78), channel_id=1, source_target_pairs={{4,0},{8,4},{12,8},{16,12},{20,16},{24,20},{28,24},{5,1},{9,5},{13... | collective-permute-start | bytes 393224 | tf_op jit(solution)/shard_map/ppermute | solution.py:34
  60.6 8.2 %collective-permute-start.12 = (bf16[2,128,256]{2,1,0:T(8,128)(2,1)S(1)}, bf16[2,128,256]{2,1,0:T(8,128)(2,1)S(1)}, u32[]{:S(2)}, u32[]{:S(2)}) collective-permute-start(bf16[2,128,256]{2,1,0:T(8,128)(2,1)S(1)} %get-tuple-element.79), channel_id=1, source_target_pairs={{8,0},{12,4},{16,8},{20,12},{24,16},{28,20},{9,1},{13,5},{17,9},{2... | collective-permute-start | bytes 393224 | tf_op jit(solution)/shard_map/ppermute | solution.py:34
  64.9 6.6 %collective-permute-start.13 = (bf16[2,128,256]{2,1,0:T(8,128)(2,1)S(1)}, bf16[2,128,256]{2,1,0:T(8,128)(2,1)S(1)}, u32[]{:S(2)}, u32[]{:S(2)}) collective-permute-start(bf16[2,128,256]{2,1,0:T(8,128)(2,1)S(1)} %get-tuple-element.83), channel_id=1, source_target_pairs={{4,0},{8,4},{12,8},{16,12},{20,16},{24,20},{28,24},{5,1},{9,5},{13... | collective-permute-start | bytes 393224 | tf_op jit(solution)/shard_map/ppermute | solution.py:34
  66.8 6.3 %collective-permute-start.14 = (bf16[2,128,256]{2,1,0:T(8,128)(2,1)S(1)}, bf16[2,128,256]{2,1,0:T(8,128)(2,1)S(1)}, u32[]{:S(2)}, u32[]{:S(2)}) collective-permute-start(bf16[2,128,256]{2,1,0:T(8,128)(2,1)S(1)} %get-tuple-element.84), channel_id=1, source_target_pairs={{8,0},{12,4},{16,8},{20,12},{24,16},{28,20},{9,1},{13,5},{17,9},{2... | collective-permute-start | bytes 393224 | tf_op jit(solution)/shard_map/ppermute | solution.py:34

commit v21 on v20

--- a/solution.py
+++ b/solution.py
@@ -12,7 +12,7 @@
 BIG_NEGATIVE = -1e30
 VMEM_BYTES = 32 * 1024 * 1024
 HEADS_STEP = 2
-CALL_COST = (1, 1, 1, 100)
+CALL_COST = 1
 
 
 def target_of(index, step, count):
@@ -210,7 +210,7 @@
     in_specs.append(pl.BlockSpec((blocks, 2, rows, lanes), lambda c, m, a: (0, 0, 0, place + c)))
     operands = [meta, assignment, segments, query[0], grad[0], kv]
     aliases = {}
-    acc_spec = pl.BlockSpec((2, keys, lanes), lambda c, m, a: (0, 0, place + c))
+    acc_spec = pl.BlockSpec((2, keys, lanes), lambda c, m, a: (0, 0, c))
     if not first:
         if not last:
             aliases[len(operands)] = 1
@@ -233,10 +233,10 @@
         out_shape += [jax.ShapeDtypeStruct((2, tok_dev, span * HD), jnp.bfloat16)] * (pieces - 1)
         out_specs += [span_spec] * pieces
     else:
-        out_shape.append(jax.ShapeDtypeStruct((2, keys, kv_width), jnp.float32))
+        out_shape.append(jax.ShapeDtypeStruct((2, keys, span * HD), jnp.float32))
         out_specs.append(acc_spec)
     pairs = span * ratio * rows * window
-    cost = CALL_COST[step] if step < len(CALL_COST) and not last else 1
+    cost = CALL_COST if step and not last else 1
     held = (keys, ratio * rows), (window, ratio * rows)
     held += ((2, keys, lanes),) * last
     return pl.pallas_call(
@@ -276,16 +276,18 @@
     part = width // halves
     others = [step for step in range(1, count) if step != final]
     jobs = [(2, step, 0, kv_width) for step in range(count)]
-    jobs += [(0, step, 0, width) for step in others]
-    jobs += [(which, final, half * part, part, 1) for half in range(halves) for which in range(2)]
+    order = [*others[1:], final]
+    jobs.append((0, others[0], 0, width))
+    jobs += [(0, step, half * part, part) for half in range(halves) for step in order]
     staged = stage(assignment, (queries, grad_out, keys, values), jobs)
     kv_staged, staged = staged[:count], list(staged[count:])
     kv_arrived = [exchanged(kv_staged[step], "dp", step) for step in range(1, count)]
-    staged, kv_arrived[0] = lax.optimization_barrier((staged, kv_arrived[0]))
-    arrived = [exchanged(rows, "dp", step) for rows, step in zip(staged, others)]
-    held = staged[len(others) :]
+    staged, mine, kv_arrived[0] = lax.optimization_barrier((staged, kv_staged[0], kv_arrived[0]))
+    whole = exchanged(staged[0], "dp", others[0])
+    arrived = [exchanged(rows, "dp", step) for rows, step in zip(staged[1:], order)]
+    behind = staged[1 + len(order) :]
     kv_own = jnp.zeros((count, *kv_staged[0].shape), keys.dtype)
-    for step, piece in enumerate([kv_staged[0], *kv_arrived]):
+    for step, piece in enumerate([mine, *kv_arrived]):
         kv_own = lax.dynamic_update_index_in_dim(
             kv_own, piece, source_of(group, step, count), 0
         )
@@ -293,27 +295,33 @@
     kv = jnp.concatenate([*halos, kv_own], axis=0)
 
     fixed = (doc_most, heads, meta, assignment, segment_ids)
-    query, grad = (queries, lambda m, a: a[m[0]]), (grad_out, lambda m, a: a[m[0]])
-    full, acc = attend(0, 0, kv_heads, *fixed, query, grad, kv, None, None, False)
-    rows, acc = lax.optimization_barrier((held[0], acc))
-    split = [exchanged(rows, "dp", final)]
-    for at, (step, both) in enumerate(zip(others, arrived)):
-        if not at:
-            rows, both = lax.optimization_barrier((held[1], both))
-            split.append(exchanged(rows, "dp", final))
-        query, grad = (both, lambda m, a: 0), (both, lambda m, a: 1)
-        full, acc = attend(step, 0, kv_heads, *fixed, query, grad, kv, acc, full, False)
-        rows, acc = lax.optimization_barrier((held[2 + at], acc))
-        split.append(exchanged(rows, "dp", final))
-    totals, returned = [], []
+    own = (queries, lambda m, a: a[m[0]]), (grad_out, lambda m, a: a[m[0]])
+    first = (whole, lambda m, a: 0), (whole, lambda m, a: 1)
+    accs, full, totals, returned = [], None, [], []
     for half in range(halves):
-        query, grad = [(rows, lambda m, a: 0) for rows in split[2 * half : 2 * half + 2]]
-        full, total, *halos = attend(
-            final, half * HEADS_STEP, HEADS_STEP, *fixed, query, grad, kv, acc, full, True
-        )
+        full, acc = attend(0, half * HEADS_STEP, HEADS_STEP, *fixed, *own, kv, None, full, False)
+        accs.append(acc)
+    rows, full = lax.optimization_barrier((behind[:-1], full))
+    arrived += [exchanged(piece, "dp", step) for piece, step in zip(rows, order)]
+    for half in range(halves):
+        full, accs[half] = attend(
+            others[0], half * HEADS_STEP, HEADS_STEP, *fixed, *first, kv, accs[half], full, False
+        )
+    for half in range(halves):
+        base = half * HEADS_STEP
+        for at, step in enumerate(order):
+            both = arrived[half * len(order) + at]
+            pair = (both, lambda m, a: 0), (both, lambda m, a: 1)
+            full, accs[half], *halos = attend(
+                step, base, HEADS_STEP, *fixed, *pair, kv, accs[half], full, step == final
+            )
+            if not half and at == len(order) - 2:
+                rows, full = lax.optimization_barrier((behind[-1], full))
+                arrived.append(exchanged(rows, "dp", final))
         if half:
             halos, returned[0] = lax.optimization_barrier((halos, returned[0]))
         returned = [shifted(halo, ("blk", "uly"), -back) for back, halo in enumerate(halos, 1)]
+        total = accs[half]
         for halo in returned:
             total = total + halo.astype(jnp.float32)
         totals.append(total.astype(jnp.bfloat16))

time: 74.3 us -> 80 us (1.077)
  starting transfers between devices: 33.6 us -> 46.6 us
  waiting for transfers between devices: 15.3 us -> 7.63 us
  Pallas kernels: 18.8 us -> 21.8 us
  local copies, waits for them, and re-layouts: 3.24 us -> 0.89 us
    ppermute x9 -> x8, starting transfers between devices: 13.5 us -> 22.1 us  [exchanged(): lax.ppermute(value, axis, [(i, (i + step) % count) for i in range(count)])]
    ppermute x6, waiting for transfers between devices: 9.05 us -> 4.31 us  [shifted(): return lax.ppermute(value, axis, pairs)]
    ppermute x6, starting transfers between devices: 20.1 us -> 24.5 us  [shifted(): return lax.ppermute(value, axis, pairs)]
    pallas_call x5 -> x8, Pallas kernels: 15.6 us -> 18.6 us  [attend(): pl.pallas_call(functools.partial(attend_kernel, step, first, filled, last...]
    ppermute x9 -> x8, waiting for transfers between devices: 6.28 us -> 3.32 us  [exchanged(): lax.ppermute(value, axis, [(i, (i + step) % count) for i in range(count)])]
    dynamic_update_slice x4, local copies, waits for them, and re-layouts: 2.55 us -> 0.04 us  [shards(): lax.dynamic_update_index_in_dim(kv_own, piece, source_of(group, step, cou...]
  transfers between devices with their start and end apart: 15 -> 14, of which waited for: 6 -> 4; matrix products, arithmetic and copies ran while one was open for 5% -> 2% of each run, Pallas kernels for 21% -> 23%
where the time goes in v21:
time: 80 us; the launch traced here: 79.6 us
  starting transfers between devices  46.6 us (58%)
  Pallas kernels  21.8 us (27%)
  waiting for transfers between devices  7.63 us (10%)
  other arithmetic  1.92 us (2%)
  local copies, waits for them, and re-layouts  0.89 us (1%)
  between operations  0.8 us (1%)
    ppermute x6, starting transfers between devices, shifted(): return lax.ppermute(value, axis, pairs)  24.5 us
    ppermute x8, starting transfers between devices, exchanged(): lax.ppermute(value, axis, [(i, (i + step) % count) for i in range(count)])  22.1 us
    pallas_call x8, Pallas kernels, attend(): pl.pallas_call(functools.partial(attend_kernel, step, first, filled, last...  18.6 us
    ppermute x6, waiting for transfers between devices, shifted(): return lax.ppermute(value, axis, pairs)  4.31 us
    ppermute x8, waiting for transfers between devices, exchanged(): lax.ppermute(value, axis, [(i, (i + step) % count) for i in range(count)])  3.32 us
    pallas_call x1, Pallas kernels, stage(): pl.pallas_call(functools.partial(stage_kernel, count, jobs, len(jobs)), o...  3.25 us
  transfers between devices with their start and end apart: 14, of which 4 were waited for; matrix products, arithmetic and copies ran while one was open for 2% of the time, Pallas kernels for 23%

profile of v21, /device:TPU:1, one launch (start us, length us, event | category | flops | bytes accessed | tf_op | source)
XLA Modules:
  0.0 79.6 jit_solution(16274673327053923108)
XLA Ops:
  0.6 3.2 %stage.1 = (bf16[2,32,512]{2,1,0:T(8,128)(2,1)}, bf16[2,32,512]{2,1,0:T(8,128)(2,1)}, bf16[2,32,512]{2,1,0:T(8,128)(2,1)}, bf16[2,32,512]{2,1,0:T(8,128)(2,1)}, ...) custom-call(s32[4]{0:T(128)} %assign_ref.17, ...), custom_call_target="tpu_custom_call" | custom-call | tf_op jit(solution)/shard_map/stage/pallas_call | solution.py:63
  3.9 2.2 %collective-permute-start = (bf16[2,32,512]{2,1,0:T(8,128)(2,1)}, bf16[2,32,512]{2,1,0:T(8,128)(2,1)S(1)}, u32[]{:S(2)}, u32[]{:S(2)}) collective-permute-start(bf16[2,32,512]{2,1,0:T(8,128)(2,1)} %get-tuple-element.51), channel_id=1, source_target_pairs={{0,1},{1,2},{2,3},{3,0},{4,5},{5,6},{6,7},{7,4},{8,9},{9,10},{10,1... | collective-permute-start | bytes 196616 | tf_op jit(solution)/shard_map/ppermute | solution.py:28
  6.1 2.3 %collective-permute-start.2 = (bf16[2,32,512]{2,1,0:T(8,128)(2,1)}, bf16[2,32,512]{2,1,0:T(8,128)(2,1)S(1)}, u32[]{:S(2)}, u32[]{:S(2)}) collective-permute-start(bf16[2,32,512]{2,1,0:T(8,128)(2,1)} %get-tuple-element.56), channel_id=1, source_target_pairs={{0,2},{1,3},{2,0},{3,1},{4,6},{5,7},{6,4},{7,5},{8,10},{9,11},{10,... | collective-permute-start | bytes 196616 | tf_op jit(solution)/shard_map/ppermute | solution.py:28
  8.4 1.1 %collective-permute-start.3 = (bf16[2,32,512]{2,1,0:T(8,128)(2,1)}, bf16[2,32,512]{2,1,0:T(8,128)(2,1)S(1)}, u32[]{:S(2)}, u32[]{:S(2)}) collective-permute-start(bf16[2,32,512]{2,1,0:T(8,128)(2,1)} %get-tuple-element.57), channel_id=1, source_target_pairs={{0,3},{1,0},{2,1},{3,2},{4,7},{5,4},{6,5},{7,6},{8,11},{9,8},{10,9... | collective-permute-start | bytes 196616 | tf_op jit(solution)/shard_map/ppermute | solution.py:28
  10.9 2.7 %collective-permute-done.2 = bf16[2,32,512]{2,1,0:T(8,128)(2,1)S(1)} collective-permute-done((bf16[2,32,512]{2,1,0:T(8,128)(2,1)}, bf16[2,32,512]{2,1,0:T(8,128)(2,1)S(1)}, u32[]{:S(2)}, u32[]{:S(2)}) %collective-permute-start.2) | collective-permute-done | bytes 65568 | tf_op jit(solution)/shard_map/ppermute | solution.py:28
  13.6 2.4 %collective-permute-start.5 = (bf16[4,2,32,512]{3,2,1,0:T(8,128)(2,1)S(1)}, bf16[4,2,32,512]{3,2,1,0:T(8,128)(2,1)S(1)}, u32[]{:S(2)}, u32[]{:S(2)}) collective-permute-start(bf16[4,2,32,512]{3,2,1,0:T(8,128)(2,1)S(1)} %bitcast_dynamic-update-slice_fusion), channel_id=1, source_target_pairs={{0,4},{4,8},{8,12},{12,16},{16,20},{20,24},{24,28},{1,5},{5,9},{9,... | collective-permute-start | bytes 786440 | tf_op jit(solution)/shard_map/ppermute | solution.py:34
  16.1 5.0 %collective-permute-start.4 = (bf16[4,2,32,512]{3,2,1,0:T(8,128)(2,1)S(1)}, bf16[4,2,32,512]{3,2,1,0:T(8,128)(2,1)}, u32[]{:S(2)}, u32[]{:S(2)}) collective-permute-start(bf16[4,2,32,512]{3,2,1,0:T(8,128)(2,1)S(1)} %bitcast_dynamic-update-slice_fusion), channel_id=1, source_target_pairs={{0,8},{4,12},{8,16},{12,20},{16,24},{20,28},{1,9},{5,13},{9,17},{1... | collective-permute-start | bytes 786440 | tf_op jit(solution)/shard_map/ppermute | solution.py:34
  21.1 3.3 %collective-permute-start.1 = (bf16[2,32,2048]{2,1,0:T(8,128)(2,1)}, bf16[2,32,2048]{2,1,0:T(8,128)(2,1)S(1)}, u32[]{:S(2)}, u32[]{:S(2)}) collective-permute-start(bf16[2,32,2048]{2,1,0:T(8,128)(2,1)} %get-tuple-element.53), channel_id=1, source_target_pairs={{0,3},{1,0},{2,1},{3,2},{4,7},{5,4},{6,5},{7,6},{8,11},{9,8},{10,9... | collective-permute-start | bytes 786440 | tf_op jit(solution)/shard_map/ppermute | solution.py:28
  24.5 8.7 %collective-permute-start.9 = (bf16[2,32,2048]{2,1,0:T(8,128)(2,1)}, bf16[2,32,2048]{2,1,0:T(8,128)(2,1)S(1)}, u32[]{:S(2)}, u32[]{:S(2)}) collective-permute-start(bf16[2,32,2048]{2,1,0:T(8,128)(2,1)} %get-tuple-element.72), channel_id=1, source_target_pairs={{0,2},{1,3},{2,0},{3,1},{4,6},{5,7},{6,4},{7,5},{8,10},{9,11},{10,... | collective-permute-start | bytes 786440 | tf_op jit(solution)/shard_map/ppermute | solution.py:28
  33.2 1.0 %pad_maximum_fusion.kv_ref = bf16[12,2,32,512]{3,2,1,0:T(8,128)(2,1)S(1)} fusion(bf16[4,2,32,512]{3,2,1,0:T(8,128)(2,1)S(1)} %bitcast_dynamic-update-slice_fusion, bf16[4,2,32,512]{3,2,1,0:T(8,128)(2,1)S(1)} %collective-permute-done.5, bf16[4,2,32,512]{3,2,1,0:T(8,128)(2,1)} %collective-permute-done.4), kind=kLoop, calls=%fused_computation | loop fusion | flops 786432 | bytes 1572864 | tf_op jit(solution)/shard_map/concatenate | solution.py:295
  34.3 2.2 %attend.8 = (bf16[128,32,128]{2,1,0:T(8,128)(2,1)}, f32[2,384,256]{2,1,0:T(8,128)S(1)}) custom-call(s32[2]{0:T(128)S(1)} %pad_add_fusion.meta_ref, s32[4]{0:T(128)S(1)} %copy-done.3, s32[4,1024]{1,0:T(4,128)S(1)} %copy-done.2, bf16[4,32,4096]{2,1,0:T(8,128)(2,1)S(1)} %copy-done, bf16[4,32,4096]{2,1,0:T(8,128)(2,1)S(1)} %copy-done.1, ...), custom_call_target="tpu_custom_call" | custom-call | flops 18874368 | bytes 147456 | tf_op jit(solution)/shard_map/attend/pallas_call | solution.py:242
  36.5 2.2 %attend.9 = (bf16[128,32,128]{2,1,0:T(8,128)(2,1)}, f32[2,384,256]{2,1,0:T(8,128)S(1)}) custom-call(s32[2]{0:T(128)S(1)} %pad_add_fusion.meta_ref, s32[4]{0:T(128)S(1)} %copy-done.3, s32[4,1024]{1,0:T(4,128)S(1)} %copy-done.2, bf16[4,32,4096]{2,1,0:T(8,128)(2,1)S(1)} %copy-done, bf16[4,32,4096]{2,1,0:T(8,128)(2,1)S(1)} %copy-done.1, ...), custom_call_target="tpu_custom_call", output_to_operand_aliasing={{0}: (6, {})} | custom-call | flops 18874368 | bytes 147456 | tf_op jit(solution)/shard_map/attend/pallas_call | solution.py:242
  39.7 2.3 %attend.10 = (bf16[128,32,128]{2,1,0:T(8,128)(2,1)}, f32[2,384,256]{2,1,0:T(8,128)S(1)}) custom-call(s32[2]{0:T(128)S(1)} %pad_add_fusion.meta_ref, s32[4]{0:T(128)S(1)} %copy-done.3, s32[4,1024]{1,0:T(4,128)S(1)} %copy-done.2, bf16[2,32,4096]{2,1,0:T(8,128)(2,1)S(1)} %collective-permute-done.6.query_ref.grad_ref, ...), custom_call_target="tpu_custom_call", output_to_operand_aliasing={{1}: (6, {}), {0}: (7, {})} | custom-call | flops 18874368 | bytes 147456 | tf_op jit(solution)/shard_map/attend/pallas_call | solution.py:242
  42.0 2.4 %attend.11 = (bf16[128,32,128]{2,1,0:T(8,128)(2,1)}, f32[2,384,256]{2,1,0:T(8,128)S(1)}) custom-call(s32[2]{0:T(128)S(1)} %pad_add_fusion.meta_ref, s32[4]{0:T(128)S(1)} %copy-done.3, s32[4,1024]{1,0:T(4,128)S(1)} %copy-done.2, bf16[2,32,4096]{2,1,0:T(8,128)(2,1)S(1)} %collective-permute-done.6.query_ref.grad_ref, ...), custom_call_target="tpu_custom_call", output_to_operand_aliasing={{1}: (6, {}), {0}: (7, {})} | custom-call | flops 18874368 | bytes 147456 | tf_op jit(solution)/shard_map/attend/pallas_call | solution.py:242
  44.4 2.4 %attend.12 = (bf16[128,32,128]{2,1,0:T(8,128)(2,1)}, f32[2,384,256]{2,1,0:T(8,128)S(1)}) custom-call(s32[2]{0:T(128)S(1)} %pad_add_fusion.meta_ref, s32[4]{0:T(128)S(1)} %copy-done.3, s32[4,1024]{1,0:T(4,128)S(1)} %copy-done.2, bf16[2,32,2048]{2,1,0:T(8,128)(2,1)S(1)} %collective-permute-done.1.query_ref.grad_ref, ...), custom_call_target="tpu_custom_call", output_to_operand_aliasing={{1}: (6, {}), {0}: (7, {})} | custom-call | flops 18874368 | bytes 147456 | tf_op jit(solution)/shard_map/attend/pallas_call | solution.py:242
  46.7 3.6 %collective-permute-start.7 = (bf16[2,32,2048]{2,1,0:T(8,128)(2,1)S(1)}, bf16[2,32,2048]{2,1,0:T(8,128)(2,1)S(1)}, u32[]{:S(2)}, u32[]{:S(2)}) collective-permute-start(bf16[2,32,2048]{2,1,0:T(8,128)(2,1)S(1)} %copy-done.5), channel_id=1, source_target_pairs={{0,2},{1,3},{2,0},{3,1},{4,6},{5,7},{6,4},{7,5},{8,10},{9,11},{10,... | collective-permute-start | bytes 786440 | tf_op jit(solution)/shard_map/ppermute | solution.py:28
  50.3 2.3 %attend.13 = (bf16[128,32,128]{2,1,0:T(8,128)(2,1)}, f32[2,128,256]{2,1,0:T(8,128)S(1)}, bf16[2,128,256]{2,1,0:T(8,128)(2,1)S(1)}, bf16[2,128,256]{2,1,0:T(8,128)(2,1)S(1)}) custom-call(s32[2]{0:T(128)S(1)} %pad_add_fusion.meta_ref, s32[4]{0:T(128)S(1)} %copy-done.3, s32[4,1024]{1,0:T(4,128)S(1)} %copy-done.2, ...), custom_call_target="tpu_custom_call", output_to_operand_aliasing={{0}: (7, {})} | custom-call | flops 18874368 | bytes 147456 | tf_op jit(solution)/shard_map/attend/pallas_call | solution.py:242
  52.7 10.3 %collective-permute-start.10 = (bf16[2,128,256]{2,1,0:T(8,128)(2,1)S(1)}, bf16[2,128,256]{2,1,0:T(8,128)(2,1)S(1)}, u32[]{:S(2)}, u32[]{:S(2)}) collective-permute-start(bf16[2,128,256]{2,1,0:T(8,128)(2,1)S(1)} %get-tuple-element.80), channel_id=1, source_target_pairs={{4,0},{8,4},{12,8},{16,12},{20,16},{24,20},{28,24},{5,1},{9,5},{13... | collective-permute-start | bytes 393224 | tf_op jit(solution)/shard_map/ppermute | solution.py:34
  63.0 1.9 %collective-permute-start.11 = (bf16[2,128,256]{2,1,0:T(8,128)(2,1)S(1)}, bf16[2,128,256]{2,1,0:T(8,128)(2,1)S(1)}, u32[]{:S(2)}, u32[]{:S(2)}) collective-permute-start(bf16[2,128,256]{2,1,0:T(8,128)(2,1)S(1)} %get-tuple-element.81), channel_id=1, source_target_pairs={{8,0},{12,4},{16,8},{20,12},{24,16},{28,20},{9,1},{13,5},{17,9},{2... | collective-permute-start | bytes 393224 | tf_op jit(solution)/shard_map/ppermute | solution.py:34
  64.9 2.4 %attend.14 = (bf16[128,32,128]{2,1,0:T(8,128)(2,1)}, f32[2,384,256]{2,1,0:T(8,128)S(1)}) custom-call(s32[2]{0:T(128)S(1)} %pad_add_fusion.meta_ref, s32[4]{0:T(128)S(1)} %copy-done.3, s32[4,1024]{1,0:T(4,128)S(1)} %copy-done.2, bf16[2,32,2048]{2,1,0:T(8,128)(2,1)S(1)} %collective-permute-done.8.query_ref.grad_ref, ...), custom_call_target="tpu_custom_call", output_to_operand_aliasing={{1}: (6, {}), {0}: (7, {})} | custom-call | flops 18874368 | bytes 147456 | tf_op jit(solution)/shard_map/attend/pallas_call | solution.py:242
  67.3 2.4 %attend.15 = (bf16[128,32,128]{2,1,0:T(8,128)(2,1)}, f32[2,128,256]{2,1,0:T(8,128)S(1)}, bf16[2,128,256]{2,1,0:T(8,128)(2,1)S(1)}, bf16[2,128,256]{2,1,0:T(8,128)(2,1)S(1)}) custom-call(s32[2]{0:T(128)S(1)} %pad_add_fusion.meta_ref, s32[4]{0:T(128)S(1)} %copy-done.3, s32[4,1024]{1,0:T(4,128)S(1)} %copy-done.2, ...), custom_call_target="tpu_custom_call", output_to_operand_aliasing={{0}: (7, {})} | custom-call | flops 18874368 | bytes 147456 | tf_op jit(solution)/shard_map/attend/pallas_call | solution.py:242
  69.7 2.9 %collective-permute-start.12 = (bf16[2,128,256]{2,1,0:T(8,128)(2,1)S(1)}, bf16[2,128,256]{2,1,0:T(8,128)(2,1)S(1)}, u32[]{:S(2)}, u32[]{:S(2)}) collective-permute-start(bf16[2,128,256]{2,1,0:T(8,128)(2,1)S(1)} %get-tuple-element.85), channel_id=1, source_target_pairs={{4,0},{8,4},{12,8},{16,12},{20,16},{24,20},{28,24},{5,1},{9,5},{13... | collective-permute-start | bytes 393224 | tf_op jit(solution)/shard_map/ppermute | solution.py:34
  72.6 1.9 %collective-permute-start.13 = (bf16[2,128,256]{2,1,0:T(8,128)(2,1)S(1)}, bf16[2,128,256]{2,1,0:T(8,128)(2,1)S(1)}, u32[]{:S(2)}, u32[]{:S(2)}) collective-permute-start(bf16[2,128,256]{2,1,0:T(8,128)(2,1)S(1)} %get-tuple-element.86), channel_id=1, source_target_pairs={{8,0},{12,4},{16,8},{20,12},{24,16},{28,20},{9,1},{13,5},{17,9},{2... | collective-permute-start | bytes 393224 | tf_op jit(solution)/shard_map/ppermute | solution.py:34
  75.4 3.5 %collective-permute-done.13 = bf16[2,128,256]{2,1,0:T(8,128)(2,1)S(1)} collective-permute-done((bf16[2,128,256]{2,1,0:T(8,128)(2,1)S(1)}, bf16[2,128,256]{2,1,0:T(8,128)(2,1)S(1)}, u32[]{:S(2)}, u32[]{:S(2)}) %collective-permute-start.13) | collective-permute-done | bytes 131104 | tf_op jit(solution)/shard_map/ppermute | solution.py:34
  (37 shorter events, 4.1 us)
Async XLA Ops:
  3.9 6.1 %collective-permute-start = (bf16[2,32,512]{2,1,0:T(8,128)(2,1)}, bf16[2,32,512]{2,1,0:T(8,128)(2,1)S(1)}, u32[]{:S(2)}, u32[]{:S(2)}) collective-permute-start(bf16[2,32,512]{2,1,0:T(8,128)(2,1)} %get-tuple-element.51), channel_id=1, source_target_pairs={{0,1},{1,2},{2,3},{3,0},{4,5},{5,6},{6,7},{7,4},{8,9},{9,10},{10,1... | collective-permute-start | bytes 196616 | tf_op jit(solution)/shard_map/ppermute | solution.py:28
  6.1 7.5 %collective-permute-start.2 = (bf16[2,32,512]{2,1,0:T(8,128)(2,1)}, bf16[2,32,512]{2,1,0:T(8,128)(2,1)S(1)}, u32[]{:S(2)}, u32[]{:S(2)}) collective-permute-start(bf16[2,32,512]{2,1,0:T(8,128)(2,1)} %get-tuple-element.56), channel_id=1, source_target_pairs={{0,2},{1,3},{2,0},{3,1},{4,6},{5,7},{6,4},{7,5},{8,10},{9,11},{10,... | collective-permute-start | bytes 196616 | tf_op jit(solution)/shard_map/ppermute | solution.py:28
  8.4 5.2 %collective-permute-start.3 = (bf16[2,32,512]{2,1,0:T(8,128)(2,1)}, bf16[2,32,512]{2,1,0:T(8,128)(2,1)S(1)}, u32[]{:S(2)}, u32[]{:S(2)}) collective-permute-start(bf16[2,32,512]{2,1,0:T(8,128)(2,1)} %get-tuple-element.57), channel_id=1, source_target_pairs={{0,3},{1,0},{2,1},{3,2},{4,7},{5,4},{6,5},{7,6},{8,11},{9,8},{10,9... | collective-permute-start | bytes 196616 | tf_op jit(solution)/shard_map/ppermute | solution.py:28
  10.0 0.8 %copy-start.4 = (bf16[2,32,512]{2,1,0:T(8,128)(2,1)S(1)}, bf16[2,32,512]{2,1,0:T(8,128)(2,1)}, u32[]{:S(2)}) copy-start(bf16[2,32,512]{2,1,0:T(8,128)(2,1)} %get-tuple-element.54) | copy-start | bytes 196612
  10.0 29.7 %collective-permute-start.6 = (bf16[2,32,4096]{2,1,0:T(8,128)(2,1)}, bf16[2,32,4096]{2,1,0:T(8,128)(2,1)S(1)}, u32[]{:S(2)}, u32[]{:S(2)}) collective-permute-start(bf16[2,32,4096]{2,1,0:T(8,128)(2,1)} %get-tuple-element.58), channel_id=1, source_target_pairs={{0,1},{1,2},{2,3},{3,0},{4,5},{5,6},{6,7},{7,4},{8,9},{9,10},{10,1... | collective-permute-start | bytes 1572872 | tf_op jit(solution)/shard_map/ppermute | solution.py:28
  10.8 23.4 %copy-start = (bf16[4,32,4096]{2,1,0:T(8,128)(2,1)S(1)}, bf16[4,32,4096]{2,1,0:T(8,128)(2,1)}, u32[]{:S(2)}) copy-start(bf16[4,32,4096]{2,1,0:T(8,128)(2,1)} %query_ref.3) | copy-start | bytes 3145732
  10.8 23.4 %copy-start.1 = (bf16[4,32,4096]{2,1,0:T(8,128)(2,1)S(1)}, bf16[4,32,4096]{2,1,0:T(8,128)(2,1)}, u32[]{:S(2)}) copy-start(bf16[4,32,4096]{2,1,0:T(8,128)(2,1)} %grad_ref.3) | copy-start | bytes 3145732
  13.6 19.5 %collective-permute-start.5 = (bf16[4,2,32,512]{3,2,1,0:T(8,128)(2,1)S(1)}, bf16[4,2,32,512]{3,2,1,0:T(8,128)(2,1)S(1)}, u32[]{:S(2)}, u32[]{:S(2)}) collective-permute-start(bf16[4,2,32,512]{3,2,1,0:T(8,128)(2,1)S(1)} %bitcast_dynamic-update-slice_fusion), channel_id=1, source_target_pairs={{0,4},{4,8},{8,12},{12,16},{16,20},{20,24},{24,28},{1,5},{5,9},{9,... | collective-permute-start | bytes 786440 | tf_op jit(solution)/shard_map/ppermute | solution.py:34
  16.1 17.1 %collective-permute-start.4 = (bf16[4,2,32,512]{3,2,1,0:T(8,128)(2,1)S(1)}, bf16[4,2,32,512]{3,2,1,0:T(8,128)(2,1)}, u32[]{:S(2)}, u32[]{:S(2)}) collective-permute-start(bf16[4,2,32,512]{3,2,1,0:T(8,128)(2,1)S(1)} %bitcast_dynamic-update-slice_fusion), channel_id=1, source_target_pairs={{0,8},{4,12},{8,16},{12,20},{16,24},{20,28},{1,9},{5,13},{9,17},{1... | collective-permute-start | bytes 786440 | tf_op jit(solution)/shard_map/ppermute | solution.py:34
  21.1 23.3 %collective-permute-start.1 = (bf16[2,32,2048]{2,1,0:T(8,128)(2,1)}, bf16[2,32,2048]{2,1,0:T(8,128)(2,1)S(1)}, u32[]{:S(2)}, u32[]{:S(2)}) collective-permute-start(bf16[2,32,2048]{2,1,0:T(8,128)(2,1)} %get-tuple-element.53), channel_id=1, source_target_pairs={{0,3},{1,0},{2,1},{3,2},{4,7},{5,4},{6,5},{7,6},{8,11},{9,8},{10,9... | collective-permute-start | bytes 786440 | tf_op jit(solution)/shard_map/ppermute | solution.py:28
  24.5 9.8 %copy-start.2 = (s32[4,1024]{1,0:T(4,128)S(1)}, s32[4,1024]{1,0:T(4,128)}, u32[]{:S(2)}) copy-start(s32[4,1024]{1,0:T(4,128)} %segment_ref.15) | copy-start | bytes 49156
  24.5 9.8 %copy-start.3 = (s32[4]{0:T(128)S(1)}, s32[4]{0:T(128)}, u32[]{:S(2)}) copy-start(s32[4]{0:T(128)} %assign_ref.17) | copy-start | bytes 52
  24.5 25.8 %collective-permute-start.9 = (bf16[2,32,2048]{2,1,0:T(8,128)(2,1)}, bf16[2,32,2048]{2,1,0:T(8,128)(2,1)S(1)}, u32[]{:S(2)}, u32[]{:S(2)}) collective-permute-start(bf16[2,32,2048]{2,1,0:T(8,128)(2,1)} %get-tuple-element.72), channel_id=1, source_target_pairs={{0,2},{1,3},{2,0},{3,1},{4,6},{5,7},{6,4},{7,5},{8,10},{9,11},{10,... | collective-permute-start | bytes 786440 | tf_op jit(solution)/shard_map/ppermute | solution.py:28
  36.5 2.2 %copy-start.6 = (bf16[2,32,2048]{2,1,0:T(8,128)(2,1)S(1)}, bf16[2,32,2048]{2,1,0:T(8,128)(2,1)}, u32[]{:S(2)}) copy-start(bf16[2,32,2048]{2,1,0:T(8,128)(2,1)} %get-tuple-element.70) | copy-start | bytes 786436
  38.7 26.2 %collective-permute-start.8 = (bf16[2,32,2048]{2,1,0:T(8,128)(2,1)S(1)}, bf16[2,32,2048]{2,1,0:T(8,128)(2,1)S(1)}, u32[]{:S(2)}, u32[]{:S(2)}) collective-permute-start(bf16[2,32,2048]{2,1,0:T(8,128)(2,1)S(1)} %copy-done.6), channel_id=1, source_target_pairs={{0,3},{1,0},{2,1},{3,2},{4,7},{5,4},{6,5},{7,6},{8,11},{9,8},{10,9... | collective-permute-start | bytes 786440 | tf_op jit(solution)/shard_map/ppermute | solution.py:28
  44.4 2.4 %copy-start.5 = (bf16[2,32,2048]{2,1,0:T(8,128)(2,1)S(1)}, bf16[2,32,2048]{2,1,0:T(8,128)(2,1)}, u32[]{:S(2)}) copy-start(bf16[2,32,2048]{2,1,0:T(8,128)(2,1)} %get-tuple-element.69) | copy-start | bytes 786436
  46.7 20.6 %collective-permute-start.7 = (bf16[2,32,2048]{2,1,0:T(8,128)(2,1)S(1)}, bf16[2,32,2048]{2,1,0:T(8,128)(2,1)S(1)}, u32[]{:S(2)}, u32[]{:S(2)}) collective-permute-start(bf16[2,32,2048]{2,1,0:T(8,128)(2,1)S(1)} %copy-done.5), channel_id=1, source_target_pairs={{0,2},{1,3},{2,0},{3,1},{4,6},{5,7},{6,4},{7,5},{8,10},{9,11},{10,... | collective-permute-start | bytes 786440 | tf_op jit(solution)/shard_map/ppermute | solution.py:28
  52.7 17.0 %collective-permute-start.10 = (bf16[2,128,256]{2,1,0:T(8,128)(2,1)S(1)}, bf16[2,128,256]{2,1,0:T(8,128)(2,1)S(1)}, u32[]{:S(2)}, u32[]{:S(2)}) collective-permute-start(bf16[2,128,256]{2,1,0:T(8,128)(2,1)S(1)} %get-tuple-element.80), channel_id=1, source_target_pairs={{4,0},{8,4},{12,8},{16,12},{20,16},{24,20},{28,24},{5,1},{9,5},{13... | collective-permute-start | bytes 393224 | tf_op jit(solution)/shard_map/ppermute | solution.py:34
  63.0 11.5 %collective-permute-start.11 = (bf16[2,128,256]{2,1,0:T(8,128)(2,1)S(1)}, bf16[2,128,256]{2,1,0:T(8,128)(2,1)S(1)}, u32[]{:S(2)}, u32[]{:S(2)}) collective-permute-start(bf16[2,128,256]{2,1,0:T(8,128)(2,1)S(1)} %get-tuple-element.81), channel_id=1, source_target_pairs={{8,0},{12,4},{16,8},{20,12},{24,16},{28,20},{9,1},{13,5},{17,9},{2... | collective-permute-start | bytes 393224 | tf_op jit(solution)/shard_map/ppermute | solution.py:34
  69.7 5.7 %collective-permute-start.12 = (bf16[2,128,256]{2,1,0:T(8,128)(2,1)S(1)}, bf16[2,128,256]{2,1,0:T(8,128)(2,1)S(1)}, u32[]{:S(2)}, u32[]{:S(2)}) collective-permute-start(bf16[2,128,256]{2,1,0:T(8,128)(2,1)S(1)} %get-tuple-element.85), channel_id=1, source_target_pairs={{4,0},{8,4},{12,8},{16,12},{20,16},{24,20},{28,24},{5,1},{9,5},{13... | collective-permute-start | bytes 393224 | tf_op jit(solution)/shard_map/ppermute | solution.py:34
  72.6 6.3 %collective-permute-start.13 = (bf16[2,128,256]{2,1,0:T(8,128)(2,1)S(1)}, bf16[2,128,256]{2,1,0:T(8,128)(2,1)S(1)}, u32[]{:S(2)}, u32[]{:S(2)}) collective-permute-start(bf16[2,128,256]{2,1,0:T(8,128)(2,1)S(1)} %get-tuple-element.86), channel_id=1, source_target_pairs={{8,0},{12,4},{16,8},{20,12},{24,16},{28,20},{9,1},{13,5},{17,9},{2... | collective-permute-start | bytes 393224 | tf_op jit(solution)/shard_map/ppermute | solution.py:34

commit v22 on v20

--- a/solution.py
+++ b/solution.py
@@ -281,11 +281,11 @@
     staged = stage(assignment, (queries, grad_out, keys, values), jobs)
     kv_staged, staged = staged[:count], list(staged[count:])
     kv_arrived = [exchanged(kv_staged[step], "dp", step) for step in range(1, count)]
-    staged, kv_arrived[0] = lax.optimization_barrier((staged, kv_arrived[0]))
+    staged, mine, kv_arrived[0] = lax.optimization_barrier((staged, kv_staged[0], kv_arrived[0]))
     arrived = [exchanged(rows, "dp", step) for rows, step in zip(staged, others)]
     held = staged[len(others) :]
     kv_own = jnp.zeros((count, *kv_staged[0].shape), keys.dtype)
-    for step, piece in enumerate([kv_staged[0], *kv_arrived]):
+    for step, piece in enumerate([mine, *kv_arrived]):
         kv_own = lax.dynamic_update_index_in_dim(
             kv_own, piece, source_of(group, step, count), 0
         )

time: 74.3 us -> 76.1 us (1.024)
  starting transfers between devices: 33.6 us -> 39.6 us
  waiting for transfers between devices: 15.3 us -> 11.1 us
    ppermute x6, starting transfers between devices: 20.1 us -> 26.1 us  [shifted(): return lax.ppermute(value, axis, pairs)]
    ppermute x9, waiting for transfers between devices: 6.28 us -> 0.57 us  [exchanged(): lax.ppermute(value, axis, [(i, (i + step) % count) for i in range(count)])]
    ppermute x6, waiting for transfers between devices: 9.05 us -> 10.6 us  [shifted(): return lax.ppermute(value, axis, pairs)]
  transfers between devices with their start and end apart: 15 -> 15, of which waited for: 6 -> 5; matrix products, arithmetic and copies ran while one was open for 5% -> 5% of each run, Pallas kernels for 21% -> 21%
where the time goes in v22:
time: 76.1 us; the launch traced here: 75.7 us
  starting transfers between devices  39.6 us (52%)
  Pallas kernels  18.9 us (25%)
  waiting for transfers between devices  11.1 us (15%)
  local copies, waits for them, and re-layouts  3.23 us (4%)
  other arithmetic  2.01 us (3%)
  between operations  0.85 us (1%)
    ppermute x6, starting transfers between devices, shifted(): return lax.ppermute(value, axis, pairs)  26.1 us
    pallas_call x5, Pallas kernels, attend(): pl.pallas_call(functools.partial(attend_kernel, step, first, filled, last...  15.6 us
    ppermute x9, starting transfers between devices, exchanged(): lax.ppermute(value, axis, [(i, (i + step) % count) for i in range(count)])  13.5 us
    ppermute x6, waiting for transfers between devices, shifted(): return lax.ppermute(value, axis, pairs)  10.6 us
    pallas_call x1, Pallas kernels, stage(): pl.pallas_call(functools.partial(stage_kernel, count, jobs, len(jobs)), o...  3.27 us
    dynamic_update_slice x4, local copies, waits for them, and re-layouts, shards(): lax.dynamic_update_index_in_dim(kv_own, piece, source_of(group, step, cou...  2.55 us
  transfers between devices with their start and end apart: 15, of which 5 were waited for; matrix products, arithmetic and copies ran while one was open for 5% of the time, Pallas kernels for 21%

profile of v22, /device:TPU:1, one launch (start us, length us, event | category | flops | bytes accessed | tf_op | source)
XLA Modules:
  0.0 75.7 jit_solution(1666988942055605204)
XLA Ops:
  0.6 3.3 %stage.1 = (bf16[2,32,512]{2,1,0:T(8,128)(2,1)}, bf16[2,32,512]{2,1,0:T(8,128)(2,1)}, bf16[2,32,512]{2,1,0:T(8,128)(2,1)}, bf16[2,32,512]{2,1,0:T(8,128)(2,1)}, ...) custom-call(s32[4]{0:T(128)} %assign_ref.11, ...), custom_call_target="tpu_custom_call" | custom-call | tf_op jit(solution)/shard_map/stage/pallas_call | solution.py:63
  4.0 2.2 %collective-permute-start = (bf16[2,32,512]{2,1,0:T(8,128)(2,1)}, bf16[2,32,512]{2,1,0:T(8,128)(2,1)S(1)}, u32[]{:S(2)}, u32[]{:S(2)}) collective-permute-start(bf16[2,32,512]{2,1,0:T(8,128)(2,1)} %get-tuple-element.52), channel_id=1, source_target_pairs={{0,1},{1,2},{2,3},{3,0},{4,5},{5,6},{6,7},{7,4},{8,9},{9,10},{10,1... | collective-permute-start | bytes 196616 | tf_op jit(solution)/shard_map/ppermute | solution.py:28
  6.1 2.3 %collective-permute-start.2 = (bf16[2,32,512]{2,1,0:T(8,128)(2,1)}, bf16[2,32,512]{2,1,0:T(8,128)(2,1)}, u32[]{:S(2)}, u32[]{:S(2)}) collective-permute-start(bf16[2,32,512]{2,1,0:T(8,128)(2,1)} %get-tuple-element.59), channel_id=1, source_target_pairs={{0,2},{1,3},{2,0},{3,1},{4,6},{5,7},{6,4},{7,5},{8,10},{9,11},{10,... | collective-permute-start | bytes 196616 | tf_op jit(solution)/shard_map/ppermute | solution.py:28
  8.4 1.1 %collective-permute-start.3 = (bf16[2,32,512]{2,1,0:T(8,128)(2,1)}, bf16[2,32,512]{2,1,0:T(8,128)(2,1)S(1)}, u32[]{:S(2)}, u32[]{:S(2)}) collective-permute-start(bf16[2,32,512]{2,1,0:T(8,128)(2,1)} %get-tuple-element.60), channel_id=1, source_target_pairs={{0,3},{1,0},{2,1},{3,2},{4,7},{5,4},{6,5},{7,6},{8,11},{9,8},{10,9... | collective-permute-start | bytes 196616 | tf_op jit(solution)/shard_map/ppermute | solution.py:28
  10.7 3.3 %collective-permute-start.7 = (bf16[2,32,4096]{2,1,0:T(8,128)(2,1)}, bf16[2,32,4096]{2,1,0:T(8,128)(2,1)S(1)}, u32[]{:S(2)}, u32[]{:S(2)}) collective-permute-start(bf16[2,32,4096]{2,1,0:T(8,128)(2,1)} %get-tuple-element.68), channel_id=1, source_target_pairs={{0,3},{1,0},{2,1},{3,2},{4,7},{5,4},{6,5},{7,6},{8,11},{9,8},{10,9... | collective-permute-start | bytes 1572872 | tf_op jit(solution)/shard_map/ppermute | solution.py:28
  14.0 0.9 %bitcast_dynamic-update-slice_fusion.3 = bf16[4,2,32,512]{3,2,1,0:T(8,128)(2,1)S(1)} fusion(bf16[4,2,32,512]{3,2,1,0:T(8,128)(2,1)S(1)} %broadcast_in_dim.19, s32[]{:T(128)S(6)} %select_n.13, bf16[2,32,512]{2,1,0:T(8,128)(2,1)} %get-tuple-element.57), kind=kLoop, calls=%fused_computation.10 | loop fusion | bytes 131076 | tf_op jit(solution)/shard_map/jit(dynamic_update_index_in_dim)/dynamic_update_slice | solution.py:289
  16.5 3.1 %collective-permute-start.5 = (bf16[4,2,32,512]{3,2,1,0:T(8,128)(2,1)S(1)}, bf16[4,2,32,512]{3,2,1,0:T(8,128)(2,1)}, u32[]{:S(2)}, u32[]{:S(2)}) collective-permute-start(bf16[4,2,32,512]{3,2,1,0:T(8,128)(2,1)S(1)} %bitcast_dynamic-update-slice_fusion), channel_id=1, source_target_pairs={{0,4},{4,8},{8,12},{12,16},{16,20},{20,24},{24,28},{1,5},{5,9},{9,... | collective-permute-start | bytes 786440 | tf_op jit(solution)/shard_map/ppermute | solution.py:34
  19.7 6.0 %collective-permute-start.4 = (bf16[4,2,32,512]{3,2,1,0:T(8,128)(2,1)S(1)}, bf16[4,2,32,512]{3,2,1,0:T(8,128)(2,1)}, u32[]{:S(2)}, u32[]{:S(2)}) collective-permute-start(bf16[4,2,32,512]{3,2,1,0:T(8,128)(2,1)S(1)} %bitcast_dynamic-update-slice_fusion), channel_id=1, source_target_pairs={{0,8},{4,12},{8,16},{12,20},{16,24},{20,28},{1,9},{5,13},{9,17},{1... | collective-permute-start | bytes 786440 | tf_op jit(solution)/shard_map/ppermute | solution.py:34
  25.8 2.7 %collective-permute-done.5 = bf16[4,2,32,512]{3,2,1,0:T(8,128)(2,1)} collective-permute-done((bf16[4,2,32,512]{3,2,1,0:T(8,128)(2,1)S(1)}, bf16[4,2,32,512]{3,2,1,0:T(8,128)(2,1)}, u32[]{:S(2)}, u32[]{:S(2)}) %collective-permute-start.5) | collective-permute-done | bytes 262176 | tf_op jit(solution)/shard_map/ppermute | solution.py:34
  28.5 2.0 %collective-permute-done.4 = bf16[4,2,32,512]{3,2,1,0:T(8,128)(2,1)} collective-permute-done((bf16[4,2,32,512]{3,2,1,0:T(8,128)(2,1)S(1)}, bf16[4,2,32,512]{3,2,1,0:T(8,128)(2,1)}, u32[]{:S(2)}, u32[]{:S(2)}) %collective-permute-start.4) | collective-permute-done | bytes 262176 | tf_op jit(solution)/shard_map/ppermute | solution.py:34
  30.5 1.1 %pad_maximum_fusion.kv_ref = bf16[12,2,32,512]{3,2,1,0:T(8,128)(2,1)S(1)} fusion(bf16[4,2,32,512]{3,2,1,0:T(8,128)(2,1)S(1)} %bitcast_dynamic-update-slice_fusion, bf16[4,2,32,512]{3,2,1,0:T(8,128)(2,1)} %collective-permute-done.5, bf16[4,2,32,512]{3,2,1,0:T(8,128)(2,1)} %collective-permute-done.4), kind=kLoop, calls=%fused_computation | loop fusion | flops 786432 | bytes 1572864 | tf_op jit(solution)/shard_map/concatenate | solution.py:293
  31.7 3.6 %attend.5 = (bf16[128,32,128]{2,1,0:T(8,128)(2,1)}, f32[2,384,512]{2,1,0:T(8,128)S(1)}) custom-call(s32[2]{0:T(128)S(1)} %pad_add_fusion.meta_ref, s32[4]{0:T(128)S(1)} %copy-done.3, s32[4,1024]{1,0:T(4,128)S(1)} %copy-done.2, bf16[4,32,4096]{2,1,0:T(8,128)(2,1)S(1)} %copy-done, bf16[4,32,4096]{2,1,0:T(8,128)(2,1)S(1)} %copy-done.1, ...), custom_call_target="tpu_custom_call" | custom-call | flops 37748736 | bytes 294912 | tf_op jit(solution)/shard_map/attend/pallas_call | solution.py:242
  35.4 2.4 %collective-permute-start.10 = (bf16[1,32,2048]{2,1,0:T(8,128)(2,1)S(1)}, bf16[1,32,2048]{2,1,0:T(8,128)(2,1)S(1)}, u32[]{:S(2)}, u32[]{:S(2)}) collective-permute-start(bf16[1,32,2048]{2,1,0:T(8,128)(2,1)S(1)} %copy-done.7), channel_id=1, source_target_pairs={{0,2},{1,3},{2,0},{3,1},{4,6},{5,7},{6,4},{7,5},{8,10},{9,11},{10,... | collective-permute-start | bytes 393224 | tf_op jit(solution)/shard_map/ppermute | solution.py:28
  37.7 3.6 %attend.6 = (bf16[128,32,128]{2,1,0:T(8,128)(2,1)}, f32[2,384,512]{2,1,0:T(8,128)S(1)}) custom-call(s32[2]{0:T(128)S(1)} %pad_add_fusion.meta_ref, s32[4]{0:T(128)S(1)} %copy-done.3, s32[4,1024]{1,0:T(4,128)S(1)} %copy-done.2, bf16[2,32,4096]{2,1,0:T(8,128)(2,1)S(1)} %collective-permute-done.1.query_ref.grad_ref, ...), custom_call_target="tpu_custom_call", output_to_operand_aliasing={{1}: (6, {}), {0}: (7, {})} | custom-call | flops 37748736 | bytes 294912 | tf_op jit(solution)/shard_map/attend/pallas_call | solution.py:242
  41.4 3.6 %attend.7 = (bf16[128,32,128]{2,1,0:T(8,128)(2,1)}, f32[2,384,512]{2,1,0:T(8,128)S(1)}) custom-call(s32[2]{0:T(128)S(1)} %pad_add_fusion.meta_ref, s32[4]{0:T(128)S(1)} %copy-done.3, s32[4,1024]{1,0:T(4,128)S(1)} %copy-done.2, bf16[2,32,4096]{2,1,0:T(8,128)(2,1)S(1)} %collective-permute-done.7.query_ref.grad_ref, ...), custom_call_target="tpu_custom_call", output_to_operand_aliasing={{1}: (6, {}), {0}: (7, {})} | custom-call | flops 3774873600 | bytes 29491200 | tf_op jit(solution)/shard_map/attend/pallas_call | solution.py:242
  45.0 2.3 %collective-permute-start.8 = (bf16[1,32,2048]{2,1,0:T(8,128)(2,1)S(1)}, bf16[1,32,2048]{2,1,0:T(8,128)(2,1)S(1)}, u32[]{:S(2)}, u32[]{:S(2)}) collective-permute-start(bf16[1,32,2048]{2,1,0:T(8,128)(2,1)S(1)} %copy-done.5), channel_id=1, source_target_pairs={{0,2},{1,3},{2,0},{3,1},{4,6},{5,7},{6,4},{7,5},{8,10},{9,11},{10,... | collective-permute-start | bytes 393224 | tf_op jit(solution)/shard_map/ppermute | solution.py:28
  47.3 2.4 %attend.8 = (bf16[128,32,128]{2,1,0:T(8,128)(2,1)}, f32[2,128,256]{2,1,0:T(8,128)S(1)}, bf16[2,128,256]{2,1,0:T(8,128)(2,1)S(1)}, bf16[2,128,256]{2,1,0:T(8,128)(2,1)S(1)}) custom-call(s32[2]{0:T(128)S(1)} %pad_add_fusion.meta_ref, s32[4]{0:T(128)S(1)} %copy-done.3, s32[4,1024]{1,0:T(4,128)S(1)} %copy-done.2, ...), custom_call_target="tpu_custom_call", output_to_operand_aliasing={{0}: (7, {})} | custom-call | flops 18874368 | bytes 147456 | tf_op jit(solution)/shard_map/attend/pallas_call | solution.py:242
  49.7 11.1 %collective-permute-start.11 = (bf16[2,128,256]{2,1,0:T(8,128)(2,1)S(1)}, bf16[2,128,256]{2,1,0:T(8,128)(2,1)S(1)}, u32[]{:S(2)}, u32[]{:S(2)}) collective-permute-start(bf16[2,128,256]{2,1,0:T(8,128)(2,1)S(1)} %get-tuple-element.80), channel_id=1, source_target_pairs={{4,0},{8,4},{12,8},{16,12},{20,16},{24,20},{28,24},{5,1},{9,5},{13... | collective-permute-start | bytes 393224 | tf_op jit(solution)/shard_map/ppermute | solution.py:34
  60.8 1.9 %collective-permute-start.12 = (bf16[2,128,256]{2,1,0:T(8,128)(2,1)S(1)}, bf16[2,128,256]{2,1,0:T(8,128)(2,1)S(1)}, u32[]{:S(2)}, u32[]{:S(2)}) collective-permute-start(bf16[2,128,256]{2,1,0:T(8,128)(2,1)S(1)} %get-tuple-element.81), channel_id=1, source_target_pairs={{8,0},{12,4},{16,8},{20,12},{24,16},{28,20},{9,1},{13,5},{17,9},{2... | collective-permute-start | bytes 393224 | tf_op jit(solution)/shard_map/ppermute | solution.py:34
  62.8 2.4 %attend.9 = (bf16[128,32,128]{2,1,0:T(8,128)(2,1)}, f32[2,128,256]{2,1,0:T(8,128)S(1)}, bf16[2,128,256]{2,1,0:T(8,128)(2,1)S(1)}, bf16[2,128,256]{2,1,0:T(8,128)(2,1)S(1)}) custom-call(s32[2]{0:T(128)S(1)} %pad_add_fusion.meta_ref, s32[4]{0:T(128)S(1)} %copy-done.3, s32[4,1024]{1,0:T(4,128)S(1)} %copy-done.2, ...), custom_call_target="tpu_custom_call", output_to_operand_aliasing={{0}: (7, {})} | custom-call | flops 18874368 | bytes 147456 | tf_op jit(solution)/shard_map/attend/pallas_call | solution.py:242
  65.2 1.9 %collective-permute-start.13 = (bf16[2,128,256]{2,1,0:T(8,128)(2,1)S(1)}, bf16[2,128,256]{2,1,0:T(8,128)(2,1)S(1)}, u32[]{:S(2)}, u32[]{:S(2)}) collective-permute-start(bf16[2,128,256]{2,1,0:T(8,128)(2,1)S(1)} %get-tuple-element.85), channel_id=1, source_target_pairs={{4,0},{8,4},{12,8},{16,12},{20,16},{24,20},{28,24},{5,1},{9,5},{13... | collective-permute-start | bytes 393224 | tf_op jit(solution)/shard_map/ppermute | solution.py:34
  67.1 1.9 %collective-permute-start.14 = (bf16[2,128,256]{2,1,0:T(8,128)(2,1)S(1)}, bf16[2,128,256]{2,1,0:T(8,128)(2,1)S(1)}, u32[]{:S(2)}, u32[]{:S(2)}) collective-permute-start(bf16[2,128,256]{2,1,0:T(8,128)(2,1)S(1)} %get-tuple-element.86), channel_id=1, source_target_pairs={{8,0},{12,4},{16,8},{20,12},{24,16},{28,20},{9,1},{13,5},{17,9},{2... | collective-permute-start | bytes 393224 | tf_op jit(solution)/shard_map/ppermute | solution.py:34
  69.1 2.6 %collective-permute-done.13 = bf16[2,128,256]{2,1,0:T(8,128)(2,1)S(1)} collective-permute-done((bf16[2,128,256]{2,1,0:T(8,128)(2,1)S(1)}, bf16[2,128,256]{2,1,0:T(8,128)(2,1)S(1)}, u32[]{:S(2)}, u32[]{:S(2)}) %collective-permute-start.13) | collective-permute-done | bytes 131104 | tf_op jit(solution)/shard_map/ppermute | solution.py:34
  71.7 3.2 %collective-permute-done.14 = bf16[2,128,256]{2,1,0:T(8,128)(2,1)S(1)} collective-permute-done((bf16[2,128,256]{2,1,0:T(8,128)(2,1)S(1)}, bf16[2,128,256]{2,1,0:T(8,128)(2,1)S(1)}, u32[]{:S(2)}, u32[]{:S(2)}) %collective-permute-start.14) | collective-permute-done | bytes 131104 | tf_op jit(solution)/shard_map/ppermute | solution.py:34
  (40 shorter events, 3.9 us)
Async XLA Ops:
  3.9 27.8 %copy-start = (bf16[4,32,4096]{2,1,0:T(8,128)(2,1)S(1)}, bf16[4,32,4096]{2,1,0:T(8,128)(2,1)}, u32[]{:S(2)}) copy-start(bf16[4,32,4096]{2,1,0:T(8,128)(2,1)} %query_ref.1) | copy-start | bytes 3145732
  3.9 27.8 %copy-start.1 = (bf16[4,32,4096]{2,1,0:T(8,128)(2,1)S(1)}, bf16[4,32,4096]{2,1,0:T(8,128)(2,1)}, u32[]{:S(2)}) copy-start(bf16[4,32,4096]{2,1,0:T(8,128)(2,1)} %grad_ref.1) | copy-start | bytes 3145732
  3.9 27.7 %copy-start.2 = (s32[4,1024]{1,0:T(4,128)S(1)}, s32[4,1024]{1,0:T(4,128)}, u32[]{:S(2)}) copy-start(s32[4,1024]{1,0:T(4,128)} %segment_ref.9) | copy-start | bytes 49156
  3.9 27.7 %copy-start.3 = (s32[4]{0:T(128)S(1)}, s32[4]{0:T(128)}, u32[]{:S(2)}) copy-start(s32[4]{0:T(128)} %assign_ref.11) | copy-start | bytes 52
  4.0 6.1 %collective-permute-start = (bf16[2,32,512]{2,1,0:T(8,128)(2,1)}, bf16[2,32,512]{2,1,0:T(8,128)(2,1)S(1)}, u32[]{:S(2)}, u32[]{:S(2)}) collective-permute-start(bf16[2,32,512]{2,1,0:T(8,128)(2,1)} %get-tuple-element.52), channel_id=1, source_target_pairs={{0,1},{1,2},{2,3},{3,0},{4,5},{5,6},{6,7},{7,4},{8,9},{9,10},{10,1... | collective-permute-start | bytes 196616 | tf_op jit(solution)/shard_map/ppermute | solution.py:28
  6.1 9.5 %collective-permute-start.2 = (bf16[2,32,512]{2,1,0:T(8,128)(2,1)}, bf16[2,32,512]{2,1,0:T(8,128)(2,1)}, u32[]{:S(2)}, u32[]{:S(2)}) collective-permute-start(bf16[2,32,512]{2,1,0:T(8,128)(2,1)} %get-tuple-element.59), channel_id=1, source_target_pairs={{0,2},{1,3},{2,0},{3,1},{4,6},{5,7},{6,4},{7,5},{8,10},{9,11},{10,... | collective-permute-start | bytes 196616 | tf_op jit(solution)/shard_map/ppermute | solution.py:28
  8.4 8.1 %collective-permute-start.3 = (bf16[2,32,512]{2,1,0:T(8,128)(2,1)}, bf16[2,32,512]{2,1,0:T(8,128)(2,1)S(1)}, u32[]{:S(2)}, u32[]{:S(2)}) collective-permute-start(bf16[2,32,512]{2,1,0:T(8,128)(2,1)} %get-tuple-element.60), channel_id=1, source_target_pairs={{0,3},{1,0},{2,1},{3,2},{4,7},{5,4},{6,5},{7,6},{8,11},{9,8},{10,9... | collective-permute-start | bytes 196616 | tf_op jit(solution)/shard_map/ppermute | solution.py:28
  10.1 0.6 copy-start.4
  10.7 24.7 %collective-permute-start.1 = (bf16[2,32,4096]{2,1,0:T(8,128)(2,1)}, bf16[2,32,4096]{2,1,0:T(8,128)(2,1)S(1)}, u32[]{:S(2)}, u32[]{:S(2)}) collective-permute-start(bf16[2,32,4096]{2,1,0:T(8,128)(2,1)} %get-tuple-element.55), channel_id=1, source_target_pairs={{0,1},{1,2},{2,3},{3,0},{4,5},{5,6},{6,7},{7,4},{8,9},{9,10},{10,1... | collective-permute-start | bytes 1572872 | tf_op jit(solution)/shard_map/ppermute | solution.py:28
  10.7 30.7 %collective-permute-start.7 = (bf16[2,32,4096]{2,1,0:T(8,128)(2,1)}, bf16[2,32,4096]{2,1,0:T(8,128)(2,1)S(1)}, u32[]{:S(2)}, u32[]{:S(2)}) collective-permute-start(bf16[2,32,4096]{2,1,0:T(8,128)(2,1)} %get-tuple-element.68), channel_id=1, source_target_pairs={{0,3},{1,0},{2,1},{3,2},{4,7},{5,4},{6,5},{7,6},{8,11},{9,8},{10,9... | collective-permute-start | bytes 1572872 | tf_op jit(solution)/shard_map/ppermute | solution.py:28
  16.5 12.0 %collective-permute-start.5 = (bf16[4,2,32,512]{3,2,1,0:T(8,128)(2,1)S(1)}, bf16[4,2,32,512]{3,2,1,0:T(8,128)(2,1)}, u32[]{:S(2)}, u32[]{:S(2)}) collective-permute-start(bf16[4,2,32,512]{3,2,1,0:T(8,128)(2,1)S(1)} %bitcast_dynamic-update-slice_fusion), channel_id=1, source_target_pairs={{0,4},{4,8},{8,12},{12,16},{16,20},{20,24},{24,28},{1,5},{5,9},{9,... | collective-permute-start | bytes 786440 | tf_op jit(solution)/shard_map/ppermute | solution.py:34
  19.7 10.9 %collective-permute-start.4 = (bf16[4,2,32,512]{3,2,1,0:T(8,128)(2,1)S(1)}, bf16[4,2,32,512]{3,2,1,0:T(8,128)(2,1)}, u32[]{:S(2)}, u32[]{:S(2)}) collective-permute-start(bf16[4,2,32,512]{3,2,1,0:T(8,128)(2,1)S(1)} %bitcast_dynamic-update-slice_fusion), channel_id=1, source_target_pairs={{0,8},{4,12},{8,16},{12,20},{16,24},{20,28},{1,9},{5,13},{9,17},{1... | collective-permute-start | bytes 786440 | tf_op jit(solution)/shard_map/ppermute | solution.py:34
  31.7 3.7 %copy-start.8 = (bf16[1,32,2048]{2,1,0:T(8,128)(2,1)S(1)}, bf16[1,32,2048]{2,1,0:T(8,128)(2,1)}, u32[]{:S(2)}) copy-start(bf16[1,32,2048]{2,1,0:T(8,128)(2,1)} %get-tuple-element.74) | copy-start | bytes 393220
  31.7 3.7 %copy-start.7 = (bf16[1,32,2048]{2,1,0:T(8,128)(2,1)S(1)}, bf16[1,32,2048]{2,1,0:T(8,128)(2,1)}, u32[]{:S(2)}) copy-start(bf16[1,32,2048]{2,1,0:T(8,128)(2,1)} %get-tuple-element.75) | copy-start | bytes 393220
  35.4 12.0 %collective-permute-start.9 = (bf16[1,32,2048]{2,1,0:T(8,128)(2,1)S(1)}, bf16[1,32,2048]{2,1,0:T(8,128)(2,1)S(1)}, u32[]{:S(2)}, u32[]{:S(2)}) collective-permute-start(bf16[1,32,2048]{2,1,0:T(8,128)(2,1)S(1)} %copy-done.8), channel_id=1, source_target_pairs={{0,2},{1,3},{2,0},{3,1},{4,6},{5,7},{6,4},{7,5},{8,10},{9,11},{10,... | collective-permute-start | bytes 393224 | tf_op jit(solution)/shard_map/ppermute | solution.py:28
  35.4 12.0 %collective-permute-start.10 = (bf16[1,32,2048]{2,1,0:T(8,128)(2,1)S(1)}, bf16[1,32,2048]{2,1,0:T(8,128)(2,1)S(1)}, u32[]{:S(2)}, u32[]{:S(2)}) collective-permute-start(bf16[1,32,2048]{2,1,0:T(8,128)(2,1)S(1)} %copy-done.7), channel_id=1, source_target_pairs={{0,2},{1,3},{2,0},{3,1},{4,6},{5,7},{6,4},{7,5},{8,10},{9,11},{10,... | collective-permute-start | bytes 393224 | tf_op jit(solution)/shard_map/ppermute | solution.py:28
  37.7 3.6 %copy-start.6 = (bf16[1,32,2048]{2,1,0:T(8,128)(2,1)S(1)}, bf16[1,32,2048]{2,1,0:T(8,128)(2,1)}, u32[]{:S(2)}) copy-start(bf16[1,32,2048]{2,1,0:T(8,128)(2,1)} %get-tuple-element.66) | copy-start | bytes 393220
  41.4 21.4 %collective-permute-start.6 = (bf16[1,32,2048]{2,1,0:T(8,128)(2,1)S(1)}, bf16[1,32,2048]{2,1,0:T(8,128)(2,1)S(1)}, u32[]{:S(2)}, u32[]{:S(2)}) collective-permute-start(bf16[1,32,2048]{2,1,0:T(8,128)(2,1)S(1)} %copy-done.6), channel_id=1, source_target_pairs={{0,2},{1,3},{2,0},{3,1},{4,6},{5,7},{6,4},{7,5},{8,10},{9,11},{10,... | collective-permute-start | bytes 393224 | tf_op jit(solution)/shard_map/ppermute | solution.py:28
  41.4 3.6 %copy-start.5 = (bf16[1,32,2048]{2,1,0:T(8,128)(2,1)S(1)}, bf16[1,32,2048]{2,1,0:T(8,128)(2,1)}, u32[]{:S(2)}) copy-start(bf16[1,32,2048]{2,1,0:T(8,128)(2,1)} %get-tuple-element.72) | copy-start | bytes 393220
  45.0 17.7 %collective-permute-start.8 = (bf16[1,32,2048]{2,1,0:T(8,128)(2,1)S(1)}, bf16[1,32,2048]{2,1,0:T(8,128)(2,1)S(1)}, u32[]{:S(2)}, u32[]{:S(2)}) collective-permute-start(bf16[1,32,2048]{2,1,0:T(8,128)(2,1)S(1)} %copy-done.5), channel_id=1, source_target_pairs={{0,2},{1,3},{2,0},{3,1},{4,6},{5,7},{6,4},{7,5},{8,10},{9,11},{10,... | collective-permute-start | bytes 393224 | tf_op jit(solution)/shard_map/ppermute | solution.py:28
  49.7 15.5 %collective-permute-start.11 = (bf16[2,128,256]{2,1,0:T(8,128)(2,1)S(1)}, bf16[2,128,256]{2,1,0:T(8,128)(2,1)S(1)}, u32[]{:S(2)}, u32[]{:S(2)}) collective-permute-start(bf16[2,128,256]{2,1,0:T(8,128)(2,1)S(1)} %get-tuple-element.80), channel_id=1, source_target_pairs={{4,0},{8,4},{12,8},{16,12},{20,16},{24,20},{28,24},{5,1},{9,5},{13... | collective-permute-start | bytes 393224 | tf_op jit(solution)/shard_map/ppermute | solution.py:34
  60.8 8.2 %collective-permute-start.12 = (bf16[2,128,256]{2,1,0:T(8,128)(2,1)S(1)}, bf16[2,128,256]{2,1,0:T(8,128)(2,1)S(1)}, u32[]{:S(2)}, u32[]{:S(2)}) collective-permute-start(bf16[2,128,256]{2,1,0:T(8,128)(2,1)S(1)} %get-tuple-element.81), channel_id=1, source_target_pairs={{8,0},{12,4},{16,8},{20,12},{24,16},{28,20},{9,1},{13,5},{17,9},{2... | collective-permute-start | bytes 393224 | tf_op jit(solution)/shard_map/ppermute | solution.py:34
  65.2 6.6 %collective-permute-start.13 = (bf16[2,128,256]{2,1,0:T(8,128)(2,1)S(1)}, bf16[2,128,256]{2,1,0:T(8,128)(2,1)S(1)}, u32[]{:S(2)}, u32[]{:S(2)}) collective-permute-start(bf16[2,128,256]{2,1,0:T(8,128)(2,1)S(1)} %get-tuple-element.85), channel_id=1, source_target_pairs={{4,0},{8,4},{12,8},{16,12},{20,16},{24,20},{28,24},{5,1},{9,5},{13... | collective-permute-start | bytes 393224 | tf_op jit(solution)/shard_map/ppermute | solution.py:34
  67.1 7.8 %collective-permute-start.14 = (bf16[2,128,256]{2,1,0:T(8,128)(2,1)S(1)}, bf16[2,128,256]{2,1,0:T(8,128)(2,1)S(1)}, u32[]{:S(2)}, u32[]{:S(2)}) collective-permute-start(bf16[2,128,256]{2,1,0:T(8,128)(2,1)S(1)} %get-tuple-element.86), channel_id=1, source_target_pairs={{8,0},{12,4},{16,8},{20,12},{24,16},{28,20},{9,1},{13,5},{17,9},{2... | collective-permute-start | bytes 393224 | tf_op jit(solution)/shard_map/ppermute | solution.py:34

commit v23 on v19

--- a/solution.py
+++ b/solution.py
@@ -12,7 +12,7 @@
 BIG_NEGATIVE = -1e30
 VMEM_BYTES = 32 * 1024 * 1024
 HEADS_STEP = 2
-CALL_COST = (1, 1, 1, 100)
+CALL_COST = 30
 
 
 def target_of(index, step, count):
@@ -236,7 +236,7 @@
         out_shape.append(jax.ShapeDtypeStruct((2, keys, kv_width), jnp.float32))
         out_specs.append(acc_spec)
     pairs = span * ratio * rows * window
-    cost = CALL_COST[step] if step < len(CALL_COST) and not last else 1
+    cost = CALL_COST if step and not last else 1
     held = (keys, ratio * rows), (window, ratio * rows)
     held += ((2, keys, lanes),) * last
     return pl.pallas_call(
@@ -298,12 +298,11 @@
     full, acc = attend(0, 0, kv_heads, *fixed, query, grad, kv, None, None, False)
     rows, acc = lax.optimization_barrier((held[0], acc))
     split = [exchanged(rows, "dp", final)]
-    for at, (step, both) in enumerate(zip(others, arrived)):
+    for step, both in zip(others, arrived):
         query, grad = (both, lambda m, a: 0), (both, lambda m, a: 1)
         full, acc = attend(step, 0, kv_heads, *fixed, query, grad, kv, acc, full, False)
-        if not at:
-            rows, acc = lax.optimization_barrier((held[1:], acc))
-            split += [exchanged(piece, "dp", final) for piece in rows]
+    rows, acc = lax.optimization_barrier((held[1:], acc))
+    split += [exchanged(piece, "dp", final) for piece in rows]
     totals, returned = [], []
     for half in range(halves):
         both = split[half]

time: 74.8 us -> 74.2 us (level)
  waiting for transfers between devices: 19.5 us -> 23 us
  local copies, waits for them, and re-layouts: 3.24 us -> 0.94 us
  starting transfers between devices: 30 us -> 28.4 us
    ppermute x8, waiting for transfers between devices: 9.95 us -> 16.5 us  [exchanged(): lax.ppermute(value, axis, [(i, (i + step) % count) for i in range(count)])]
    ppermute x6, waiting for transfers between devices: 9.51 us -> 6.51 us  [shifted(): return lax.ppermute(value, axis, pairs)]
    ppermute x6, starting transfers between devices: 18.8 us -> 16.1 us  [shifted(): return lax.ppermute(value, axis, pairs)]
    dynamic_update_slice x4, local copies, waits for them, and re-layouts: 2.55 us -> 0.88 us  [shards(): lax.dynamic_update_index_in_dim(kv_own, piece, source_of(group, step, cou...]
    ppermute x8, starting transfers between devices: 11.2 us -> 12.3 us  [exchanged(): lax.ppermute(value, axis, [(i, (i + step) % count) for i in range(count)])]
  transfers between devices with their start and end apart: 14 -> 14, of which waited for: 5 -> 7; matrix products, arithmetic and copies ran while one was open for 5% -> 3% of each run, Pallas kernels for 21% -> 21%
where the time goes in v23:
time: 74.2 us; the launch traced here: 73.9 us
  starting transfers between devices  28.4 us (38%)
  waiting for transfers between devices  23 us (31%)
  Pallas kernels  18.7 us (25%)
  other arithmetic  2 us (3%)
  local copies, waits for them, and re-layouts  0.94 us (1%)
  between operations  0.84 us (1%)
    ppermute x8, waiting for transfers between devices, exchanged(): lax.ppermute(value, axis, [(i, (i + step) % count) for i in range(count)])  16.5 us
    ppermute x6, starting transfers between devices, shifted(): return lax.ppermute(value, axis, pairs)  16.1 us
    pallas_call x5, Pallas kernels, attend(): pl.pallas_call(functools.partial(attend_kernel, step, first, filled, last...  15.5 us
    ppermute x8, starting transfers between devices, exchanged(): lax.ppermute(value, axis, [(i, (i + step) % count) for i in range(count)])  12.3 us
    ppermute x6, waiting for transfers between devices, shifted(): return lax.ppermute(value, axis, pairs)  6.51 us
    pallas_call x1, Pallas kernels, stage(): pl.pallas_call(functools.partial(stage_kernel, count, jobs, len(jobs)), o...  3.23 us
  transfers between devices with their start and end apart: 14, of which 7 were waited for; matrix products, arithmetic and copies ran while one was open for 3% of the time, Pallas kernels for 21%

profile of v23, /device:TPU:1, one launch (start us, length us, event | category | flops | bytes accessed | tf_op | source)
XLA Modules:
  0.0 73.9 jit_solution(13682280792345209614)
XLA Ops:
  0.6 3.2 %stage.1 = (bf16[2,32,512]{2,1,0:T(8,128)(2,1)}, bf16[2,32,512]{2,1,0:T(8,128)(2,1)}, bf16[2,32,512]{2,1,0:T(8,128)(2,1)}, bf16[2,32,512]{2,1,0:T(8,128)(2,1)}, ...) custom-call(s32[4]{0:T(128)} %assign_ref.11, ...), custom_call_target="tpu_custom_call" | custom-call | tf_op jit(solution)/shard_map/stage/pallas_call | solution.py:63
  3.9 2.2 %collective-permute-start = (bf16[2,32,512]{2,1,0:T(8,128)(2,1)}, bf16[2,32,512]{2,1,0:T(8,128)(2,1)S(1)}, u32[]{:S(2)}, u32[]{:S(2)}) collective-permute-start(bf16[2,32,512]{2,1,0:T(8,128)(2,1)} %get-tuple-element.44), channel_id=1, source_target_pairs={{0,1},{1,2},{2,3},{3,0},{4,5},{5,6},{6,7},{7,4},{8,9},{9,10},{10,1... | collective-permute-start | bytes 196616 | tf_op jit(solution)/shard_map/ppermute | solution.py:28
  6.1 2.3 %collective-permute-start.2 = (bf16[2,32,512]{2,1,0:T(8,128)(2,1)}, bf16[2,32,512]{2,1,0:T(8,128)(2,1)S(1)}, u32[]{:S(2)}, u32[]{:S(2)}) collective-permute-start(bf16[2,32,512]{2,1,0:T(8,128)(2,1)} %get-tuple-element.50), channel_id=1, source_target_pairs={{0,2},{1,3},{2,0},{3,1},{4,6},{5,7},{6,4},{7,5},{8,10},{9,11},{10,... | collective-permute-start | bytes 196616 | tf_op jit(solution)/shard_map/ppermute | solution.py:28
  8.4 1.1 %collective-permute-start.3 = (bf16[2,32,512]{2,1,0:T(8,128)(2,1)}, bf16[2,32,512]{2,1,0:T(8,128)(2,1)S(1)}, u32[]{:S(2)}, u32[]{:S(2)}) collective-permute-start(bf16[2,32,512]{2,1,0:T(8,128)(2,1)} %get-tuple-element.51), channel_id=1, source_target_pairs={{0,3},{1,0},{2,1},{3,2},{4,7},{5,4},{6,5},{7,6},{8,11},{9,8},{10,9... | collective-permute-start | bytes 196616 | tf_op jit(solution)/shard_map/ppermute | solution.py:28
  10.8 2.8 %collective-permute-done.2 = bf16[2,32,512]{2,1,0:T(8,128)(2,1)S(1)} collective-permute-done((bf16[2,32,512]{2,1,0:T(8,128)(2,1)}, bf16[2,32,512]{2,1,0:T(8,128)(2,1)S(1)}, u32[]{:S(2)}, u32[]{:S(2)}) %collective-permute-start.2) | collective-permute-done | bytes 65568 | tf_op jit(solution)/shard_map/ppermute | solution.py:28
  13.7 2.4 %collective-permute-start.5 = (bf16[4,2,32,512]{3,2,1,0:T(8,128)(2,1)S(1)}, bf16[4,2,32,512]{3,2,1,0:T(8,128)(2,1)}, u32[]{:S(2)}, u32[]{:S(2)}) collective-permute-start(bf16[4,2,32,512]{3,2,1,0:T(8,128)(2,1)S(1)} %bitcast_dynamic-update-slice_fusion), channel_id=1, source_target_pairs={{0,4},{4,8},{8,12},{12,16},{16,20},{20,24},{24,28},{1,5},{5,9},{9,... | collective-permute-start | bytes 786440 | tf_op jit(solution)/shard_map/ppermute | solution.py:34
  16.1 5.0 %collective-permute-start.4 = (bf16[4,2,32,512]{3,2,1,0:T(8,128)(2,1)S(1)}, bf16[4,2,32,512]{3,2,1,0:T(8,128)(2,1)}, u32[]{:S(2)}, u32[]{:S(2)}) collective-permute-start(bf16[4,2,32,512]{3,2,1,0:T(8,128)(2,1)S(1)} %bitcast_dynamic-update-slice_fusion), channel_id=1, source_target_pairs={{0,8},{4,12},{8,16},{12,20},{16,24},{20,28},{1,9},{5,13},{9,17},{1... | collective-permute-start | bytes 786440 | tf_op jit(solution)/shard_map/ppermute | solution.py:34
  21.1 3.3 %collective-permute-start.1 = (bf16[2,32,4096]{2,1,0:T(8,128)(2,1)}, bf16[2,32,4096]{2,1,0:T(8,128)(2,1)S(1)}, u32[]{:S(2)}, u32[]{:S(2)}) collective-permute-start(bf16[2,32,4096]{2,1,0:T(8,128)(2,1)} %get-tuple-element.47), channel_id=1, source_target_pairs={{0,3},{1,0},{2,1},{3,2},{4,7},{5,4},{6,5},{7,6},{8,11},{9,8},{10,9... | collective-permute-start | bytes 1572872 | tf_op jit(solution)/shard_map/ppermute | solution.py:28
  24.5 1.4 %collective-permute-done.4 = bf16[4,2,32,512]{3,2,1,0:T(8,128)(2,1)} collective-permute-done((bf16[4,2,32,512]{3,2,1,0:T(8,128)(2,1)S(1)}, bf16[4,2,32,512]{3,2,1,0:T(8,128)(2,1)}, u32[]{:S(2)}, u32[]{:S(2)}) %collective-permute-start.4) | collective-permute-done | bytes 262176 | tf_op jit(solution)/shard_map/ppermute | solution.py:34
  25.9 1.1 %pad_maximum_fusion.kv_ref = bf16[12,2,32,512]{3,2,1,0:T(8,128)(2,1)S(1)} fusion(bf16[4,2,32,512]{3,2,1,0:T(8,128)(2,1)S(1)} %bitcast_dynamic-update-slice_fusion, bf16[4,2,32,512]{3,2,1,0:T(8,128)(2,1)} %collective-permute-done.5, bf16[4,2,32,512]{3,2,1,0:T(8,128)(2,1)} %collective-permute-done.4), kind=kLoop, calls=%fused_computation | loop fusion | flops 786432 | bytes 1572864 | tf_op jit(solution)/shard_map/concatenate | solution.py:294
  27.1 3.6 %attend.5 = (bf16[128,32,128]{2,1,0:T(8,128)(2,1)}, f32[2,384,512]{2,1,0:T(8,128)S(1)}) custom-call(s32[2]{0:T(128)S(1)} %pad_add_fusion.meta_ref, s32[4]{0:T(128)S(1)} %copy-done.3, s32[4,1024]{1,0:T(4,128)S(1)} %copy-done.2, bf16[4,32,4096]{2,1,0:T(8,128)(2,1)S(1)} %copy-done, bf16[4,32,4096]{2,1,0:T(8,128)(2,1)S(1)} %copy-done.1, ...), custom_call_target="tpu_custom_call" | custom-call | flops 37748736 | bytes 294912 | tf_op jit(solution)/shard_map/attend/pallas_call | solution.py:242
  31.3 3.6 %attend.6 = (bf16[128,32,128]{2,1,0:T(8,128)(2,1)}, f32[2,384,512]{2,1,0:T(8,128)S(1)}) custom-call(s32[2]{0:T(128)S(1)} %pad_add_fusion.meta_ref, s32[4]{0:T(128)S(1)} %copy-done.3, s32[4,1024]{1,0:T(4,128)S(1)} %copy-done.2, bf16[2,32,4096]{2,1,0:T(8,128)(2,1)S(1)} %collective-permute-done.6.query_ref.grad_ref, ...), custom_call_target="tpu_custom_call", output_to_operand_aliasing={{1}: (6, {}), {0}: (7, {})} | custom-call | flops 1132462080 | bytes 8847360 | tf_op jit(solution)/shard_map/attend/pallas_call | solution.py:242
  34.9 2.8 %collective-permute-done.1.query_ref.grad_ref = bf16[2,32,4096]{2,1,0:T(8,128)(2,1)S(1)} collective-permute-done((bf16[2,32,4096]{2,1,0:T(8,128)(2,1)}, bf16[2,32,4096]{2,1,0:T(8,128)(2,1)S(1)}, u32[]{:S(2)}, u32[]{:S(2)}) %collective-permute-start.1) | collective-permute-done | bytes 524320 | tf_op jit(solution)/shard_map/ppermute | solution.py:28
  37.7 3.6 %attend.7 = (bf16[128,32,128]{2,1,0:T(8,128)(2,1)}, f32[2,384,512]{2,1,0:T(8,128)S(1)}) custom-call(s32[2]{0:T(128)S(1)} %pad_add_fusion.meta_ref, s32[4]{0:T(128)S(1)} %copy-done.3, s32[4,1024]{1,0:T(4,128)S(1)} %copy-done.2, bf16[2,32,4096]{2,1,0:T(8,128)(2,1)S(1)} %collective-permute-done.1.query_ref.grad_ref, ...), custom_call_target="tpu_custom_call", output_to_operand_aliasing={{1}: (6, {}), {0}: (7, {})} | custom-call | flops 1132462080 | bytes 8847360 | tf_op jit(solution)/shard_map/attend/pallas_call | solution.py:242
  41.3 2.4 %collective-permute-start.8 = (bf16[1,32,2048]{2,1,0:T(8,128)(2,1)S(1)}, bf16[1,32,2048]{2,1,0:T(8,128)(2,1)S(1)}, u32[]{:S(2)}, u32[]{:S(2)}) collective-permute-start(bf16[1,32,2048]{2,1,0:T(8,128)(2,1)S(1)} %copy-done.5), channel_id=1, source_target_pairs={{0,2},{1,3},{2,0},{3,1},{4,6},{5,7},{6,4},{7,5},{8,10},{9,11},{10,... | collective-permute-start | bytes 393224 | tf_op jit(solution)/shard_map/ppermute | solution.py:28
  43.6 10.9 %collective-permute-done.9.query_ref.grad_ref = bf16[2,32,2048]{2,1,0:T(8,128)(2,1)S(1)} collective-permute-done((bf16[2,32,2048]{2,1,0:T(8,128)(2,1)S(1)}, bf16[2,32,2048]{2,1,0:T(8,128)(2,1)S(1)}, u32[]{:S(2)}, u32[]{:S(2)}) %collective-permute-start.9) | collective-permute-done | bytes 262176 | tf_op jit(solution)/shard_map/ppermute | solution.py:28
  54.5 2.4 %attend.8 = (bf16[128,32,128]{2,1,0:T(8,128)(2,1)}, f32[2,128,256]{2,1,0:T(8,128)S(1)}, bf16[2,128,256]{2,1,0:T(8,128)(2,1)S(1)}, bf16[2,128,256]{2,1,0:T(8,128)(2,1)S(1)}) custom-call(s32[2]{0:T(128)S(1)} %pad_add_fusion.meta_ref, s32[4]{0:T(128)S(1)} %copy-done.3, s32[4,1024]{1,0:T(4,128)S(1)} %copy-done.2, ...), custom_call_target="tpu_custom_call", output_to_operand_aliasing={{0}: (7, {})} | custom-call | flops 18874368 | bytes 147456 | tf_op jit(solution)/shard_map/attend/pallas_call | solution.py:242
  56.9 1.9 %collective-permute-start.10 = (bf16[2,128,256]{2,1,0:T(8,128)(2,1)S(1)}, bf16[2,128,256]{2,1,0:T(8,128)(2,1)S(1)}, u32[]{:S(2)}, u32[]{:S(2)}) collective-permute-start(bf16[2,128,256]{2,1,0:T(8,128)(2,1)S(1)} %get-tuple-element.68), channel_id=1, source_target_pairs={{4,0},{8,4},{12,8},{16,12},{20,16},{24,20},{28,24},{5,1},{9,5},{13... | collective-permute-start | bytes 393224 | tf_op jit(solution)/shard_map/ppermute | solution.py:34
  58.8 1.9 %collective-permute-start.11 = (bf16[2,128,256]{2,1,0:T(8,128)(2,1)S(1)}, bf16[2,128,256]{2,1,0:T(8,128)(2,1)S(1)}, u32[]{:S(2)}, u32[]{:S(2)}) collective-permute-start(bf16[2,128,256]{2,1,0:T(8,128)(2,1)S(1)} %get-tuple-element.69), channel_id=1, source_target_pairs={{8,0},{12,4},{16,8},{20,12},{24,16},{28,20},{9,1},{13,5},{17,9},{2... | collective-permute-start | bytes 393224 | tf_op jit(solution)/shard_map/ppermute | solution.py:34
  60.7 2.4 %attend.9 = (bf16[128,32,128]{2,1,0:T(8,128)(2,1)}, f32[2,128,256]{2,1,0:T(8,128)S(1)}, bf16[2,128,256]{2,1,0:T(8,128)(2,1)S(1)}, bf16[2,128,256]{2,1,0:T(8,128)(2,1)S(1)}) custom-call(s32[2]{0:T(128)S(1)} %pad_add_fusion.meta_ref, s32[4]{0:T(128)S(1)} %copy-done.3, s32[4,1024]{1,0:T(4,128)S(1)} %copy-done.2, ...), custom_call_target="tpu_custom_call", output_to_operand_aliasing={{0}: (7, {})} | custom-call | flops 18874368 | bytes 147456 | tf_op jit(solution)/shard_map/attend/pallas_call | solution.py:242
  63.4 2.9 %collective-permute-start.12 = (bf16[2,128,256]{2,1,0:T(8,128)(2,1)S(1)}, bf16[2,128,256]{2,1,0:T(8,128)(2,1)S(1)}, u32[]{:S(2)}, u32[]{:S(2)}) collective-permute-start(bf16[2,128,256]{2,1,0:T(8,128)(2,1)S(1)} %get-tuple-element.73), channel_id=1, source_target_pairs={{4,0},{8,4},{12,8},{16,12},{20,16},{24,20},{28,24},{5,1},{9,5},{13... | collective-permute-start | bytes 393224 | tf_op jit(solution)/shard_map/ppermute | solution.py:34
  66.4 1.9 %collective-permute-start.13 = (bf16[2,128,256]{2,1,0:T(8,128)(2,1)S(1)}, bf16[2,128,256]{2,1,0:T(8,128)(2,1)S(1)}, u32[]{:S(2)}, u32[]{:S(2)}) collective-permute-start(bf16[2,128,256]{2,1,0:T(8,128)(2,1)S(1)} %get-tuple-element.74), channel_id=1, source_target_pairs={{8,0},{12,4},{16,8},{20,12},{24,16},{28,20},{9,1},{13,5},{17,9},{2... | collective-permute-start | bytes 393224 | tf_op jit(solution)/shard_map/ppermute | solution.py:34
  68.4 1.1 %collective-permute-done.12 = bf16[2,128,256]{2,1,0:T(8,128)(2,1)S(1)} collective-permute-done((bf16[2,128,256]{2,1,0:T(8,128)(2,1)S(1)}, bf16[2,128,256]{2,1,0:T(8,128)(2,1)S(1)}, u32[]{:S(2)}, u32[]{:S(2)}) %collective-permute-start.12) | collective-permute-done | bytes 131104 | tf_op jit(solution)/shard_map/ppermute | solution.py:34
  69.5 3.7 %collective-permute-done.13 = bf16[2,128,256]{2,1,0:T(8,128)(2,1)S(1)} collective-permute-done((bf16[2,128,256]{2,1,0:T(8,128)(2,1)S(1)}, bf16[2,128,256]{2,1,0:T(8,128)(2,1)S(1)}, u32[]{:S(2)}, u32[]{:S(2)}) %collective-permute-start.13) | collective-permute-done | bytes 131104 | tf_op jit(solution)/shard_map/ppermute | solution.py:34
  (34 shorter events, 3.2 us)
Async XLA Ops:
  3.9 23.2 %copy-start = (bf16[4,32,4096]{2,1,0:T(8,128)(2,1)S(1)}, bf16[4,32,4096]{2,1,0:T(8,128)(2,1)}, u32[]{:S(2)}) copy-start(bf16[4,32,4096]{2,1,0:T(8,128)(2,1)} %query_ref.1) | copy-start | bytes 3145732
  3.9 23.2 %copy-start.1 = (bf16[4,32,4096]{2,1,0:T(8,128)(2,1)S(1)}, bf16[4,32,4096]{2,1,0:T(8,128)(2,1)}, u32[]{:S(2)}) copy-start(bf16[4,32,4096]{2,1,0:T(8,128)(2,1)} %grad_ref.1) | copy-start | bytes 3145732
  3.9 23.2 %copy-start.2 = (s32[4,1024]{1,0:T(4,128)S(1)}, s32[4,1024]{1,0:T(4,128)}, u32[]{:S(2)}) copy-start(s32[4,1024]{1,0:T(4,128)} %segment_ref.9) | copy-start | bytes 49156
  3.9 23.2 %copy-start.3 = (s32[4]{0:T(128)S(1)}, s32[4]{0:T(128)}, u32[]{:S(2)}) copy-start(s32[4]{0:T(128)} %assign_ref.11) | copy-start | bytes 52
  3.9 6.4 %collective-permute-start = (bf16[2,32,512]{2,1,0:T(8,128)(2,1)}, bf16[2,32,512]{2,1,0:T(8,128)(2,1)S(1)}, u32[]{:S(2)}, u32[]{:S(2)}) collective-permute-start(bf16[2,32,512]{2,1,0:T(8,128)(2,1)} %get-tuple-element.44), channel_id=1, source_target_pairs={{0,1},{1,2},{2,3},{3,0},{4,5},{5,6},{6,7},{7,4},{8,9},{9,10},{10,1... | collective-permute-start | bytes 196616 | tf_op jit(solution)/shard_map/ppermute | solution.py:28
  6.1 7.5 %collective-permute-start.2 = (bf16[2,32,512]{2,1,0:T(8,128)(2,1)}, bf16[2,32,512]{2,1,0:T(8,128)(2,1)S(1)}, u32[]{:S(2)}, u32[]{:S(2)}) collective-permute-start(bf16[2,32,512]{2,1,0:T(8,128)(2,1)} %get-tuple-element.50), channel_id=1, source_target_pairs={{0,2},{1,3},{2,0},{3,1},{4,6},{5,7},{6,4},{7,5},{8,10},{9,11},{10,... | collective-permute-start | bytes 196616 | tf_op jit(solution)/shard_map/ppermute | solution.py:28
  8.4 5.2 %collective-permute-start.3 = (bf16[2,32,512]{2,1,0:T(8,128)(2,1)}, bf16[2,32,512]{2,1,0:T(8,128)(2,1)S(1)}, u32[]{:S(2)}, u32[]{:S(2)}) collective-permute-start(bf16[2,32,512]{2,1,0:T(8,128)(2,1)} %get-tuple-element.51), channel_id=1, source_target_pairs={{0,3},{1,0},{2,1},{3,2},{4,7},{5,4},{6,5},{7,6},{8,11},{9,8},{10,9... | collective-permute-start | bytes 196616 | tf_op jit(solution)/shard_map/ppermute | solution.py:28
  10.4 21.0 %collective-permute-start.6 = (bf16[2,32,4096]{2,1,0:T(8,128)(2,1)}, bf16[2,32,4096]{2,1,0:T(8,128)(2,1)S(1)}, u32[]{:S(2)}, u32[]{:S(2)}) collective-permute-start(bf16[2,32,4096]{2,1,0:T(8,128)(2,1)} %get-tuple-element.52), channel_id=1, source_target_pairs={{0,1},{1,2},{2,3},{3,0},{4,5},{5,6},{6,7},{7,4},{8,9},{9,10},{10,1... | collective-permute-start | bytes 1572872 | tf_op jit(solution)/shard_map/ppermute | solution.py:28
  13.7 10.8 %collective-permute-start.5 = (bf16[4,2,32,512]{3,2,1,0:T(8,128)(2,1)S(1)}, bf16[4,2,32,512]{3,2,1,0:T(8,128)(2,1)}, u32[]{:S(2)}, u32[]{:S(2)}) collective-permute-start(bf16[4,2,32,512]{3,2,1,0:T(8,128)(2,1)S(1)} %bitcast_dynamic-update-slice_fusion), channel_id=1, source_target_pairs={{0,4},{4,8},{8,12},{12,16},{16,20},{20,24},{24,28},{1,5},{5,9},{9,... | collective-permute-start | bytes 786440 | tf_op jit(solution)/shard_map/ppermute | solution.py:34
  16.1 9.9 %collective-permute-start.4 = (bf16[4,2,32,512]{3,2,1,0:T(8,128)(2,1)S(1)}, bf16[4,2,32,512]{3,2,1,0:T(8,128)(2,1)}, u32[]{:S(2)}, u32[]{:S(2)}) collective-permute-start(bf16[4,2,32,512]{3,2,1,0:T(8,128)(2,1)S(1)} %bitcast_dynamic-update-slice_fusion), channel_id=1, source_target_pairs={{0,8},{4,12},{8,16},{12,20},{16,24},{20,28},{1,9},{5,13},{9,17},{1... | collective-permute-start | bytes 786440 | tf_op jit(solution)/shard_map/ppermute | solution.py:34
  21.1 16.6 %collective-permute-start.1 = (bf16[2,32,4096]{2,1,0:T(8,128)(2,1)}, bf16[2,32,4096]{2,1,0:T(8,128)(2,1)S(1)}, u32[]{:S(2)}, u32[]{:S(2)}) collective-permute-start(bf16[2,32,4096]{2,1,0:T(8,128)(2,1)} %get-tuple-element.47), channel_id=1, source_target_pairs={{0,3},{1,0},{2,1},{3,2},{4,7},{5,4},{6,5},{7,6},{8,11},{9,8},{10,9... | collective-permute-start | bytes 1572872 | tf_op jit(solution)/shard_map/ppermute | solution.py:28
  27.1 3.6 %copy-start.4 = (bf16[2,32,2048]{2,1,0:T(8,128)(2,1)S(1)}, bf16[2,32,2048]{2,1,0:T(8,128)(2,1)}, u32[]{:S(2)}) copy-start(bf16[2,32,2048]{2,1,0:T(8,128)(2,1)} %get-tuple-element.63) | copy-start | bytes 786436
  30.7 23.8 %collective-permute-start.9 = (bf16[2,32,2048]{2,1,0:T(8,128)(2,1)S(1)}, bf16[2,32,2048]{2,1,0:T(8,128)(2,1)S(1)}, u32[]{:S(2)}, u32[]{:S(2)}) collective-permute-start(bf16[2,32,2048]{2,1,0:T(8,128)(2,1)S(1)} %copy-done.4), channel_id=1, source_target_pairs={{0,2},{1,3},{2,0},{3,1},{4,6},{5,7},{6,4},{7,5},{8,10},{9,11},{10,... | collective-permute-start | bytes 786440 | tf_op jit(solution)/shard_map/ppermute | solution.py:28
  37.7 3.6 %copy-start.6 = (bf16[1,32,2048]{2,1,0:T(8,128)(2,1)S(1)}, bf16[1,32,2048]{2,1,0:T(8,128)(2,1)}, u32[]{:S(2)}) copy-start(bf16[1,32,2048]{2,1,0:T(8,128)(2,1)} %get-tuple-element.60) | copy-start | bytes 393220
  37.7 3.6 %copy-start.5 = (bf16[1,32,2048]{2,1,0:T(8,128)(2,1)S(1)}, bf16[1,32,2048]{2,1,0:T(8,128)(2,1)}, u32[]{:S(2)}) copy-start(bf16[1,32,2048]{2,1,0:T(8,128)(2,1)} %get-tuple-element.61) | copy-start | bytes 393220
  41.3 19.5 %collective-permute-start.7 = (bf16[1,32,2048]{2,1,0:T(8,128)(2,1)S(1)}, bf16[1,32,2048]{2,1,0:T(8,128)(2,1)S(1)}, u32[]{:S(2)}, u32[]{:S(2)}) collective-permute-start(bf16[1,32,2048]{2,1,0:T(8,128)(2,1)S(1)} %copy-done.6), channel_id=1, source_target_pairs={{0,2},{1,3},{2,0},{3,1},{4,6},{5,7},{6,4},{7,5},{8,10},{9,11},{10,... | collective-permute-start | bytes 393224 | tf_op jit(solution)/shard_map/ppermute | solution.py:28
  41.3 19.5 %collective-permute-start.8 = (bf16[1,32,2048]{2,1,0:T(8,128)(2,1)S(1)}, bf16[1,32,2048]{2,1,0:T(8,128)(2,1)S(1)}, u32[]{:S(2)}, u32[]{:S(2)}) collective-permute-start(bf16[1,32,2048]{2,1,0:T(8,128)(2,1)S(1)} %copy-done.5), channel_id=1, source_target_pairs={{0,2},{1,3},{2,0},{3,1},{4,6},{5,7},{6,4},{7,5},{8,10},{9,11},{10,... | collective-permute-start | bytes 393224 | tf_op jit(solution)/shard_map/ppermute | solution.py:28
  56.9 6.6 %collective-permute-start.10 = (bf16[2,128,256]{2,1,0:T(8,128)(2,1)S(1)}, bf16[2,128,256]{2,1,0:T(8,128)(2,1)S(1)}, u32[]{:S(2)}, u32[]{:S(2)}) collective-permute-start(bf16[2,128,256]{2,1,0:T(8,128)(2,1)S(1)} %get-tuple-element.68), channel_id=1, source_target_pairs={{4,0},{8,4},{12,8},{16,12},{20,16},{24,20},{28,24},{5,1},{9,5},{13... | collective-permute-start | bytes 393224 | tf_op jit(solution)/shard_map/ppermute | solution.py:34
  58.8 9.5 %collective-permute-start.11 = (bf16[2,128,256]{2,1,0:T(8,128)(2,1)S(1)}, bf16[2,128,256]{2,1,0:T(8,128)(2,1)S(1)}, u32[]{:S(2)}, u32[]{:S(2)}) collective-permute-start(bf16[2,128,256]{2,1,0:T(8,128)(2,1)S(1)} %get-tuple-element.69), channel_id=1, source_target_pairs={{8,0},{12,4},{16,8},{20,12},{24,16},{28,20},{9,1},{13,5},{17,9},{2... | collective-permute-start | bytes 393224 | tf_op jit(solution)/shard_map/ppermute | solution.py:34
  63.4 6.0 %collective-permute-start.12 = (bf16[2,128,256]{2,1,0:T(8,128)(2,1)S(1)}, bf16[2,128,256]{2,1,0:T(8,128)(2,1)S(1)}, u32[]{:S(2)}, u32[]{:S(2)}) collective-permute-start(bf16[2,128,256]{2,1,0:T(8,128)(2,1)S(1)} %get-tuple-element.73), channel_id=1, source_target_pairs={{4,0},{8,4},{12,8},{16,12},{20,16},{24,20},{28,24},{5,1},{9,5},{13... | collective-permute-start | bytes 393224 | tf_op jit(solution)/shard_map/ppermute | solution.py:34
  66.4 6.7 %collective-permute-start.13 = (bf16[2,128,256]{2,1,0:T(8,128)(2,1)S(1)}, bf16[2,128,256]{2,1,0:T(8,128)(2,1)S(1)}, u32[]{:S(2)}, u32[]{:S(2)}) collective-permute-start(bf16[2,128,256]{2,1,0:T(8,128)(2,1)S(1)} %get-tuple-element.74), channel_id=1, source_target_pairs={{8,0},{12,4},{16,8},{20,12},{24,16},{28,20},{9,1},{13,5},{17,9},{2... | collective-permute-start | bytes 393224 | tf_op jit(solution)/shard_map/ppermute | solution.py:34

commit v24 on v23

--- a/solution.py
+++ b/solution.py
@@ -293,11 +293,11 @@
     halos = [shifted(kv_own, ("blk", "uly"), back) for back in range(hops, 0, -1)]
     kv = jnp.concatenate([*halos, kv_own], axis=0)
 
+    rows, kv = lax.optimization_barrier((held[0], kv))
+    split = [exchanged(rows, "dp", final)]
     fixed = (doc_most, heads, meta, assignment, segment_ids)
     query, grad = (queries, lambda m, a: a[m[0]]), (grad_out, lambda m, a: a[m[0]])
     full, acc = attend(0, 0, kv_heads, *fixed, query, grad, kv, None, None, False)
-    rows, acc = lax.optimization_barrier((held[0], acc))
-    split = [exchanged(rows, "dp", final)]
     for step, both in zip(others, arrived):
         query, grad = (both, lambda m, a: 0), (both, lambda m, a: 1)
         full, acc = attend(step, 0, kv_heads, *fixed, query, grad, kv, acc, full, False)

time: 74.2 us -> 74.2 us (level)
  no operation moved by 1% of the time
where the time goes in v24:
time: 74.2 us; the launch traced here: 73.9 us
  starting transfers between devices  28.4 us (38%)
  waiting for transfers between devices  23 us (31%)
  Pallas kernels  18.7 us (25%)
  other arithmetic  2 us (3%)
  local copies, waits for them, and re-layouts  0.93 us (1%)
  between operations  0.8 us (1%)
    ppermute x8, waiting for transfers between devices, exchanged(): lax.ppermute(value, axis, [(i, (i + step) % count) for i in range(count)])  16.4 us
    ppermute x6, starting transfers between devices, shifted(): return lax.ppermute(value, axis, pairs)  16.1 us
    pallas_call x5, Pallas kernels, attend(): pl.pallas_call(functools.partial(attend_kernel, step, first, filled, last...  15.5 us
    ppermute x8, starting transfers between devices, exchanged(): lax.ppermute(value, axis, [(i, (i + step) % count) for i in range(count)])  12.3 us
    ppermute x6, waiting for transfers between devices, shifted(): return lax.ppermute(value, axis, pairs)  6.59 us
    pallas_call x1, Pallas kernels, stage(): pl.pallas_call(functools.partial(stage_kernel, count, jobs, len(jobs)), o...  3.23 us
  transfers between devices with their start and end apart: 14, of which 7 were waited for; matrix products, arithmetic and copies ran while one was open for 3% of the time, Pallas kernels for 21%

profile of v24, /device:TPU:1, one launch (start us, length us, event | category | flops | bytes accessed | tf_op | source)
XLA Modules:
  0.0 73.9 jit_solution(65279500444425342)
XLA Ops:
  0.6 3.2 %stage.1 = (bf16[2,32,512]{2,1,0:T(8,128)(2,1)}, bf16[2,32,512]{2,1,0:T(8,128)(2,1)}, bf16[2,32,512]{2,1,0:T(8,128)(2,1)}, bf16[2,32,512]{2,1,0:T(8,128)(2,1)}, ...) custom-call(s32[4]{0:T(128)} %assign_ref.11, ...), custom_call_target="tpu_custom_call" | custom-call | tf_op jit(solution)/shard_map/stage/pallas_call | solution.py:63
  3.9 2.2 %collective-permute-start = (bf16[2,32,512]{2,1,0:T(8,128)(2,1)}, bf16[2,32,512]{2,1,0:T(8,128)(2,1)S(1)}, u32[]{:S(2)}, u32[]{:S(2)}) collective-permute-start(bf16[2,32,512]{2,1,0:T(8,128)(2,1)} %get-tuple-element.44), channel_id=1, source_target_pairs={{0,1},{1,2},{2,3},{3,0},{4,5},{5,6},{6,7},{7,4},{8,9},{9,10},{10,1... | collective-permute-start | bytes 196616 | tf_op jit(solution)/shard_map/ppermute | solution.py:28
  6.1 2.3 %collective-permute-start.2 = (bf16[2,32,512]{2,1,0:T(8,128)(2,1)}, bf16[2,32,512]{2,1,0:T(8,128)(2,1)S(1)}, u32[]{:S(2)}, u32[]{:S(2)}) collective-permute-start(bf16[2,32,512]{2,1,0:T(8,128)(2,1)} %get-tuple-element.51), channel_id=1, source_target_pairs={{0,2},{1,3},{2,0},{3,1},{4,6},{5,7},{6,4},{7,5},{8,10},{9,11},{10,... | collective-permute-start | bytes 196616 | tf_op jit(solution)/shard_map/ppermute | solution.py:28
  8.4 1.1 %collective-permute-start.3 = (bf16[2,32,512]{2,1,0:T(8,128)(2,1)}, bf16[2,32,512]{2,1,0:T(8,128)(2,1)S(1)}, u32[]{:S(2)}, u32[]{:S(2)}) collective-permute-start(bf16[2,32,512]{2,1,0:T(8,128)(2,1)} %get-tuple-element.52), channel_id=1, source_target_pairs={{0,3},{1,0},{2,1},{3,2},{4,7},{5,4},{6,5},{7,6},{8,11},{9,8},{10,9... | collective-permute-start | bytes 196616 | tf_op jit(solution)/shard_map/ppermute | solution.py:28
  10.8 2.8 %collective-permute-done.2 = bf16[2,32,512]{2,1,0:T(8,128)(2,1)S(1)} collective-permute-done((bf16[2,32,512]{2,1,0:T(8,128)(2,1)}, bf16[2,32,512]{2,1,0:T(8,128)(2,1)S(1)}, u32[]{:S(2)}, u32[]{:S(2)}) %collective-permute-start.2) | collective-permute-done | bytes 65568 | tf_op jit(solution)/shard_map/ppermute | solution.py:28
  13.7 2.4 %collective-permute-start.5 = (bf16[4,2,32,512]{3,2,1,0:T(8,128)(2,1)S(1)}, bf16[4,2,32,512]{3,2,1,0:T(8,128)(2,1)}, u32[]{:S(2)}, u32[]{:S(2)}) collective-permute-start(bf16[4,2,32,512]{3,2,1,0:T(8,128)(2,1)S(1)} %bitcast_dynamic-update-slice_fusion), channel_id=1, source_target_pairs={{0,4},{4,8},{8,12},{12,16},{16,20},{20,24},{24,28},{1,5},{5,9},{9,... | collective-permute-start | bytes 786440 | tf_op jit(solution)/shard_map/ppermute | solution.py:34
  16.1 5.0 %collective-permute-start.4 = (bf16[4,2,32,512]{3,2,1,0:T(8,128)(2,1)S(1)}, bf16[4,2,32,512]{3,2,1,0:T(8,128)(2,1)}, u32[]{:S(2)}, u32[]{:S(2)}) collective-permute-start(bf16[4,2,32,512]{3,2,1,0:T(8,128)(2,1)S(1)} %bitcast_dynamic-update-slice_fusion), channel_id=1, source_target_pairs={{0,8},{4,12},{8,16},{12,20},{16,24},{20,28},{1,9},{5,13},{9,17},{1... | collective-permute-start | bytes 786440 | tf_op jit(solution)/shard_map/ppermute | solution.py:34
  21.1 3.3 %collective-permute-start.1 = (bf16[2,32,4096]{2,1,0:T(8,128)(2,1)}, bf16[2,32,4096]{2,1,0:T(8,128)(2,1)S(1)}, u32[]{:S(2)}, u32[]{:S(2)}) collective-permute-start(bf16[2,32,4096]{2,1,0:T(8,128)(2,1)} %get-tuple-element.47), channel_id=1, source_target_pairs={{0,3},{1,0},{2,1},{3,2},{4,7},{5,4},{6,5},{7,6},{8,11},{9,8},{10,9... | collective-permute-start | bytes 1572872 | tf_op jit(solution)/shard_map/ppermute | solution.py:28
  24.4 1.5 %collective-permute-done.4 = bf16[4,2,32,512]{3,2,1,0:T(8,128)(2,1)} collective-permute-done((bf16[4,2,32,512]{3,2,1,0:T(8,128)(2,1)S(1)}, bf16[4,2,32,512]{3,2,1,0:T(8,128)(2,1)}, u32[]{:S(2)}, u32[]{:S(2)}) %collective-permute-start.4) | collective-permute-done | bytes 262176 | tf_op jit(solution)/shard_map/ppermute | solution.py:34
  25.9 1.1 %pad_maximum_fusion.kv_ref = bf16[12,2,32,512]{3,2,1,0:T(8,128)(2,1)S(1)} fusion(bf16[4,2,32,512]{3,2,1,0:T(8,128)(2,1)S(1)} %bitcast_dynamic-update-slice_fusion, bf16[4,2,32,512]{3,2,1,0:T(8,128)(2,1)} %collective-permute-done.5, bf16[4,2,32,512]{3,2,1,0:T(8,128)(2,1)} %collective-permute-done.4), kind=kLoop, calls=%fused_computation | loop fusion | flops 786432 | bytes 1572864 | tf_op jit(solution)/shard_map/concatenate | solution.py:294
  27.8 3.6 %attend.5 = (bf16[128,32,128]{2,1,0:T(8,128)(2,1)}, f32[2,384,512]{2,1,0:T(8,128)S(1)}) custom-call(s32[2]{0:T(128)S(1)} %pad_add_fusion.meta_ref, s32[4]{0:T(128)S(1)} %copy-done.3, s32[4,1024]{1,0:T(4,128)S(1)} %copy-done.2, bf16[4,32,4096]{2,1,0:T(8,128)(2,1)S(1)} %copy-done, bf16[4,32,4096]{2,1,0:T(8,128)(2,1)S(1)} %copy-done.1, ...), custom_call_target="tpu_custom_call" | custom-call | flops 37748736 | bytes 294912 | tf_op jit(solution)/shard_map/attend/pallas_call | solution.py:242
  31.4 3.6 %attend.6 = (bf16[128,32,128]{2,1,0:T(8,128)(2,1)}, f32[2,384,512]{2,1,0:T(8,128)S(1)}) custom-call(s32[2]{0:T(128)S(1)} %pad_add_fusion.meta_ref, s32[4]{0:T(128)S(1)} %copy-done.3, s32[4,1024]{1,0:T(4,128)S(1)} %copy-done.2, bf16[2,32,4096]{2,1,0:T(8,128)(2,1)S(1)} %collective-permute-done.6.query_ref.grad_ref, ...), custom_call_target="tpu_custom_call", output_to_operand_aliasing={{1}: (6, {}), {0}: (7, {})} | custom-call | flops 1132462080 | bytes 8847360 | tf_op jit(solution)/shard_map/attend/pallas_call | solution.py:242
  35.0 2.7 %collective-permute-done.1.query_ref.grad_ref = bf16[2,32,4096]{2,1,0:T(8,128)(2,1)S(1)} collective-permute-done((bf16[2,32,4096]{2,1,0:T(8,128)(2,1)}, bf16[2,32,4096]{2,1,0:T(8,128)(2,1)S(1)}, u32[]{:S(2)}, u32[]{:S(2)}) %collective-permute-start.1) | collective-permute-done | bytes 524320 | tf_op jit(solution)/shard_map/ppermute | solution.py:28
  37.7 3.6 %attend.7 = (bf16[128,32,128]{2,1,0:T(8,128)(2,1)}, f32[2,384,512]{2,1,0:T(8,128)S(1)}) custom-call(s32[2]{0:T(128)S(1)} %pad_add_fusion.meta_ref, s32[4]{0:T(128)S(1)} %copy-done.3, s32[4,1024]{1,0:T(4,128)S(1)} %copy-done.2, bf16[2,32,4096]{2,1,0:T(8,128)(2,1)S(1)} %collective-permute-done.1.query_ref.grad_ref, ...), custom_call_target="tpu_custom_call", output_to_operand_aliasing={{1}: (6, {}), {0}: (7, {})} | custom-call | flops 1132462080 | bytes 8847360 | tf_op jit(solution)/shard_map/attend/pallas_call | solution.py:242
  41.3 2.4 %collective-permute-start.8 = (bf16[1,32,2048]{2,1,0:T(8,128)(2,1)S(1)}, bf16[1,32,2048]{2,1,0:T(8,128)(2,1)S(1)}, u32[]{:S(2)}, u32[]{:S(2)}) collective-permute-start(bf16[1,32,2048]{2,1,0:T(8,128)(2,1)S(1)} %copy-done.4), channel_id=1, source_target_pairs={{0,2},{1,3},{2,0},{3,1},{4,6},{5,7},{6,4},{7,5},{8,10},{9,11},{10,... | collective-permute-start | bytes 393224 | tf_op jit(solution)/shard_map/ppermute | solution.py:28
  43.6 10.9 %collective-permute-done.9.query_ref.grad_ref = bf16[2,32,2048]{2,1,0:T(8,128)(2,1)S(1)} collective-permute-done((bf16[2,32,2048]{2,1,0:T(8,128)(2,1)}, bf16[2,32,2048]{2,1,0:T(8,128)(2,1)S(1)}, u32[]{:S(2)}, u32[]{:S(2)}) %collective-permute-start.9) | collective-permute-done | bytes 262176 | tf_op jit(solution)/shard_map/ppermute | solution.py:28
  54.5 2.4 %attend.8 = (bf16[128,32,128]{2,1,0:T(8,128)(2,1)}, f32[2,128,256]{2,1,0:T(8,128)S(1)}, bf16[2,128,256]{2,1,0:T(8,128)(2,1)S(1)}, bf16[2,128,256]{2,1,0:T(8,128)(2,1)S(1)}) custom-call(s32[2]{0:T(128)S(1)} %pad_add_fusion.meta_ref, s32[4]{0:T(128)S(1)} %copy-done.3, s32[4,1024]{1,0:T(4,128)S(1)} %copy-done.2, ...), custom_call_target="tpu_custom_call", output_to_operand_aliasing={{0}: (7, {})} | custom-call | flops 18874368 | bytes 147456 | tf_op jit(solution)/shard_map/attend/pallas_call | solution.py:242
  56.9 1.9 %collective-permute-start.10 = (bf16[2,128,256]{2,1,0:T(8,128)(2,1)S(1)}, bf16[2,128,256]{2,1,0:T(8,128)(2,1)S(1)}, u32[]{:S(2)}, u32[]{:S(2)}) collective-permute-start(bf16[2,128,256]{2,1,0:T(8,128)(2,1)S(1)} %get-tuple-element.68), channel_id=1, source_target_pairs={{4,0},{8,4},{12,8},{16,12},{20,16},{24,20},{28,24},{5,1},{9,5},{13... | collective-permute-start | bytes 393224 | tf_op jit(solution)/shard_map/ppermute | solution.py:34
  58.8 1.9 %collective-permute-start.11 = (bf16[2,128,256]{2,1,0:T(8,128)(2,1)S(1)}, bf16[2,128,256]{2,1,0:T(8,128)(2,1)S(1)}, u32[]{:S(2)}, u32[]{:S(2)}) collective-permute-start(bf16[2,128,256]{2,1,0:T(8,128)(2,1)S(1)} %get-tuple-element.69), channel_id=1, source_target_pairs={{8,0},{12,4},{16,8},{20,12},{24,16},{28,20},{9,1},{13,5},{17,9},{2... | collective-permute-start | bytes 393224 | tf_op jit(solution)/shard_map/ppermute | solution.py:34
  60.7 2.4 %attend.9 = (bf16[128,32,128]{2,1,0:T(8,128)(2,1)}, f32[2,128,256]{2,1,0:T(8,128)S(1)}, bf16[2,128,256]{2,1,0:T(8,128)(2,1)S(1)}, bf16[2,128,256]{2,1,0:T(8,128)(2,1)S(1)}) custom-call(s32[2]{0:T(128)S(1)} %pad_add_fusion.meta_ref, s32[4]{0:T(128)S(1)} %copy-done.3, s32[4,1024]{1,0:T(4,128)S(1)} %copy-done.2, ...), custom_call_target="tpu_custom_call", output_to_operand_aliasing={{0}: (7, {})} | custom-call | flops 18874368 | bytes 147456 | tf_op jit(solution)/shard_map/attend/pallas_call | solution.py:242
  63.4 2.9 %collective-permute-start.12 = (bf16[2,128,256]{2,1,0:T(8,128)(2,1)S(1)}, bf16[2,128,256]{2,1,0:T(8,128)(2,1)S(1)}, u32[]{:S(2)}, u32[]{:S(2)}) collective-permute-start(bf16[2,128,256]{2,1,0:T(8,128)(2,1)S(1)} %get-tuple-element.73), channel_id=1, source_target_pairs={{4,0},{8,4},{12,8},{16,12},{20,16},{24,20},{28,24},{5,1},{9,5},{13... | collective-permute-start | bytes 393224 | tf_op jit(solution)/shard_map/ppermute | solution.py:34
  66.4 1.9 %collective-permute-start.13 = (bf16[2,128,256]{2,1,0:T(8,128)(2,1)S(1)}, bf16[2,128,256]{2,1,0:T(8,128)(2,1)S(1)}, u32[]{:S(2)}, u32[]{:S(2)}) collective-permute-start(bf16[2,128,256]{2,1,0:T(8,128)(2,1)S(1)} %get-tuple-element.74), channel_id=1, source_target_pairs={{8,0},{12,4},{16,8},{20,12},{24,16},{28,20},{9,1},{13,5},{17,9},{2... | collective-permute-start | bytes 393224 | tf_op jit(solution)/shard_map/ppermute | solution.py:34
  68.4 1.1 %collective-permute-done.12 = bf16[2,128,256]{2,1,0:T(8,128)(2,1)S(1)} collective-permute-done((bf16[2,128,256]{2,1,0:T(8,128)(2,1)S(1)}, bf16[2,128,256]{2,1,0:T(8,128)(2,1)S(1)}, u32[]{:S(2)}, u32[]{:S(2)}) %collective-permute-start.12) | collective-permute-done | bytes 131104 | tf_op jit(solution)/shard_map/ppermute | solution.py:34
  69.5 3.7 %collective-permute-done.13 = bf16[2,128,256]{2,1,0:T(8,128)(2,1)S(1)} collective-permute-done((bf16[2,128,256]{2,1,0:T(8,128)(2,1)S(1)}, bf16[2,128,256]{2,1,0:T(8,128)(2,1)S(1)}, u32[]{:S(2)}, u32[]{:S(2)}) %collective-permute-start.13) | collective-permute-done | bytes 131104 | tf_op jit(solution)/shard_map/ppermute | solution.py:34
  (32 shorter events, 3.2 us)
Async XLA Ops:
  3.9 23.9 %copy-start = (bf16[4,32,4096]{2,1,0:T(8,128)(2,1)S(1)}, bf16[4,32,4096]{2,1,0:T(8,128)(2,1)}, u32[]{:S(2)}) copy-start(bf16[4,32,4096]{2,1,0:T(8,128)(2,1)} %query_ref.1) | copy-start | bytes 3145732
  3.9 23.9 %copy-start.1 = (bf16[4,32,4096]{2,1,0:T(8,128)(2,1)S(1)}, bf16[4,32,4096]{2,1,0:T(8,128)(2,1)}, u32[]{:S(2)}) copy-start(bf16[4,32,4096]{2,1,0:T(8,128)(2,1)} %grad_ref.1) | copy-start | bytes 3145732
  3.9 23.9 %copy-start.2 = (s32[4,1024]{1,0:T(4,128)S(1)}, s32[4,1024]{1,0:T(4,128)}, u32[]{:S(2)}) copy-start(s32[4,1024]{1,0:T(4,128)} %segment_ref.9) | copy-start | bytes 49156
  3.9 23.9 %copy-start.3 = (s32[4]{0:T(128)S(1)}, s32[4]{0:T(128)}, u32[]{:S(2)}) copy-start(s32[4]{0:T(128)} %assign_ref.11) | copy-start | bytes 52
  3.9 6.4 %collective-permute-start = (bf16[2,32,512]{2,1,0:T(8,128)(2,1)}, bf16[2,32,512]{2,1,0:T(8,128)(2,1)S(1)}, u32[]{:S(2)}, u32[]{:S(2)}) collective-permute-start(bf16[2,32,512]{2,1,0:T(8,128)(2,1)} %get-tuple-element.44), channel_id=1, source_target_pairs={{0,1},{1,2},{2,3},{3,0},{4,5},{5,6},{6,7},{7,4},{8,9},{9,10},{10,1... | collective-permute-start | bytes 196616 | tf_op jit(solution)/shard_map/ppermute | solution.py:28
  6.1 7.5 %collective-permute-start.2 = (bf16[2,32,512]{2,1,0:T(8,128)(2,1)}, bf16[2,32,512]{2,1,0:T(8,128)(2,1)S(1)}, u32[]{:S(2)}, u32[]{:S(2)}) collective-permute-start(bf16[2,32,512]{2,1,0:T(8,128)(2,1)} %get-tuple-element.51), channel_id=1, source_target_pairs={{0,2},{1,3},{2,0},{3,1},{4,6},{5,7},{6,4},{7,5},{8,10},{9,11},{10,... | collective-permute-start | bytes 196616 | tf_op jit(solution)/shard_map/ppermute | solution.py:28
  8.4 5.2 %collective-permute-start.3 = (bf16[2,32,512]{2,1,0:T(8,128)(2,1)}, bf16[2,32,512]{2,1,0:T(8,128)(2,1)S(1)}, u32[]{:S(2)}, u32[]{:S(2)}) collective-permute-start(bf16[2,32,512]{2,1,0:T(8,128)(2,1)} %get-tuple-element.52), channel_id=1, source_target_pairs={{0,3},{1,0},{2,1},{3,2},{4,7},{5,4},{6,5},{7,6},{8,11},{9,8},{10,9... | collective-permute-start | bytes 196616 | tf_op jit(solution)/shard_map/ppermute | solution.py:28
  10.4 21.1 %collective-permute-start.6 = (bf16[2,32,4096]{2,1,0:T(8,128)(2,1)}, bf16[2,32,4096]{2,1,0:T(8,128)(2,1)S(1)}, u32[]{:S(2)}, u32[]{:S(2)}) collective-permute-start(bf16[2,32,4096]{2,1,0:T(8,128)(2,1)} %get-tuple-element.54), channel_id=1, source_target_pairs={{0,1},{1,2},{2,3},{3,0},{4,5},{5,6},{6,7},{7,4},{8,9},{9,10},{10,1... | collective-permute-start | bytes 1572872 | tf_op jit(solution)/shard_map/ppermute | solution.py:28
  13.7 10.8 %collective-permute-start.5 = (bf16[4,2,32,512]{3,2,1,0:T(8,128)(2,1)S(1)}, bf16[4,2,32,512]{3,2,1,0:T(8,128)(2,1)}, u32[]{:S(2)}, u32[]{:S(2)}) collective-permute-start(bf16[4,2,32,512]{3,2,1,0:T(8,128)(2,1)S(1)} %bitcast_dynamic-update-slice_fusion), channel_id=1, source_target_pairs={{0,4},{4,8},{8,12},{12,16},{16,20},{20,24},{24,28},{1,5},{5,9},{9,... | collective-permute-start | bytes 786440 | tf_op jit(solution)/shard_map/ppermute | solution.py:34
  16.1 9.9 %collective-permute-start.4 = (bf16[4,2,32,512]{3,2,1,0:T(8,128)(2,1)S(1)}, bf16[4,2,32,512]{3,2,1,0:T(8,128)(2,1)}, u32[]{:S(2)}, u32[]{:S(2)}) collective-permute-start(bf16[4,2,32,512]{3,2,1,0:T(8,128)(2,1)S(1)} %bitcast_dynamic-update-slice_fusion), channel_id=1, source_target_pairs={{0,8},{4,12},{8,16},{12,20},{16,24},{20,28},{1,9},{5,13},{9,17},{1... | collective-permute-start | bytes 786440 | tf_op jit(solution)/shard_map/ppermute | solution.py:34
  21.1 16.6 %collective-permute-start.1 = (bf16[2,32,4096]{2,1,0:T(8,128)(2,1)}, bf16[2,32,4096]{2,1,0:T(8,128)(2,1)S(1)}, u32[]{:S(2)}, u32[]{:S(2)}) collective-permute-start(bf16[2,32,4096]{2,1,0:T(8,128)(2,1)} %get-tuple-element.47), channel_id=1, source_target_pairs={{0,3},{1,0},{2,1},{3,2},{4,7},{5,4},{6,5},{7,6},{8,11},{9,8},{10,9... | collective-permute-start | bytes 1572872 | tf_op jit(solution)/shard_map/ppermute | solution.py:28
  27.1 27.5 %collective-permute-start.9 = (bf16[2,32,2048]{2,1,0:T(8,128)(2,1)}, bf16[2,32,2048]{2,1,0:T(8,128)(2,1)S(1)}, u32[]{:S(2)}, u32[]{:S(2)}) collective-permute-start(bf16[2,32,2048]{2,1,0:T(8,128)(2,1)} %get-tuple-element.63), channel_id=1, source_target_pairs={{0,2},{1,3},{2,0},{3,1},{4,6},{5,7},{6,4},{7,5},{8,10},{9,11},{10,... | collective-permute-start | bytes 786440 | tf_op jit(solution)/shard_map/ppermute | solution.py:28
  37.7 3.6 %copy-start.5 = (bf16[1,32,2048]{2,1,0:T(8,128)(2,1)S(1)}, bf16[1,32,2048]{2,1,0:T(8,128)(2,1)}, u32[]{:S(2)}) copy-start(bf16[1,32,2048]{2,1,0:T(8,128)(2,1)} %get-tuple-element.60) | copy-start | bytes 393220
  37.7 3.6 %copy-start.4 = (bf16[1,32,2048]{2,1,0:T(8,128)(2,1)S(1)}, bf16[1,32,2048]{2,1,0:T(8,128)(2,1)}, u32[]{:S(2)}) copy-start(bf16[1,32,2048]{2,1,0:T(8,128)(2,1)} %get-tuple-element.61) | copy-start | bytes 393220
  41.3 19.5 %collective-permute-start.7 = (bf16[1,32,2048]{2,1,0:T(8,128)(2,1)S(1)}, bf16[1,32,2048]{2,1,0:T(8,128)(2,1)S(1)}, u32[]{:S(2)}, u32[]{:S(2)}) collective-permute-start(bf16[1,32,2048]{2,1,0:T(8,128)(2,1)S(1)} %copy-done.5), channel_id=1, source_target_pairs={{0,2},{1,3},{2,0},{3,1},{4,6},{5,7},{6,4},{7,5},{8,10},{9,11},{10,... | collective-permute-start | bytes 393224 | tf_op jit(solution)/shard_map/ppermute | solution.py:28
  41.3 19.5 %collective-permute-start.8 = (bf16[1,32,2048]{2,1,0:T(8,128)(2,1)S(1)}, bf16[1,32,2048]{2,1,0:T(8,128)(2,1)S(1)}, u32[]{:S(2)}, u32[]{:S(2)}) collective-permute-start(bf16[1,32,2048]{2,1,0:T(8,128)(2,1)S(1)} %copy-done.4), channel_id=1, source_target_pairs={{0,2},{1,3},{2,0},{3,1},{4,6},{5,7},{6,4},{7,5},{8,10},{9,11},{10,... | collective-permute-start | bytes 393224 | tf_op jit(solution)/shard_map/ppermute | solution.py:28
  56.9 6.6 %collective-permute-start.10 = (bf16[2,128,256]{2,1,0:T(8,128)(2,1)S(1)}, bf16[2,128,256]{2,1,0:T(8,128)(2,1)S(1)}, u32[]{:S(2)}, u32[]{:S(2)}) collective-permute-start(bf16[2,128,256]{2,1,0:T(8,128)(2,1)S(1)} %get-tuple-element.68), channel_id=1, source_target_pairs={{4,0},{8,4},{12,8},{16,12},{20,16},{24,20},{28,24},{5,1},{9,5},{13... | collective-permute-start | bytes 393224 | tf_op jit(solution)/shard_map/ppermute | solution.py:34
  58.8 9.5 %collective-permute-start.11 = (bf16[2,128,256]{2,1,0:T(8,128)(2,1)S(1)}, bf16[2,128,256]{2,1,0:T(8,128)(2,1)S(1)}, u32[]{:S(2)}, u32[]{:S(2)}) collective-permute-start(bf16[2,128,256]{2,1,0:T(8,128)(2,1)S(1)} %get-tuple-element.69), channel_id=1, source_target_pairs={{8,0},{12,4},{16,8},{20,12},{24,16},{28,20},{9,1},{13,5},{17,9},{2... | collective-permute-start | bytes 393224 | tf_op jit(solution)/shard_map/ppermute | solution.py:34
  63.4 6.0 %collective-permute-start.12 = (bf16[2,128,256]{2,1,0:T(8,128)(2,1)S(1)}, bf16[2,128,256]{2,1,0:T(8,128)(2,1)S(1)}, u32[]{:S(2)}, u32[]{:S(2)}) collective-permute-start(bf16[2,128,256]{2,1,0:T(8,128)(2,1)S(1)} %get-tuple-element.73), channel_id=1, source_target_pairs={{4,0},{8,4},{12,8},{16,12},{20,16},{24,20},{28,24},{5,1},{9,5},{13... | collective-permute-start | bytes 393224 | tf_op jit(solution)/shard_map/ppermute | solution.py:34
  66.4 6.7 %collective-permute-start.13 = (bf16[2,128,256]{2,1,0:T(8,128)(2,1)S(1)}, bf16[2,128,256]{2,1,0:T(8,128)(2,1)S(1)}, u32[]{:S(2)}, u32[]{:S(2)}) collective-permute-start(bf16[2,128,256]{2,1,0:T(8,128)(2,1)S(1)} %get-tuple-element.74), channel_id=1, source_target_pairs={{8,0},{12,4},{16,8},{20,12},{24,16},{28,20},{9,1},{13,5},{17,9},{2... | collective-permute-start | bytes 393224 | tf_op jit(solution)/shard_map/ppermute | solution.py:34

commit v25 on v24

--- a/solution.py
+++ b/solution.py
@@ -171,6 +171,9 @@
         grad_scores.append((weighted - probs[head] * delta).astype(jnp.bfloat16))
     grads = []
     for head in heads:
+        if last:
+            query_out_ref[head] = grad_scores[head]
+            continue
         grad_query = product(grad_scores[head], key[head], across)
         grads.append((grad_query * scale).reshape(ratio, rows, HD))
     grad_key = [product(grad_scores[head], query[head], plain) for head in heads]
@@ -185,11 +188,13 @@
             part = slice(keys - (back + 1) * tok_dev, keys - back * tok_dev)
             halo_ref[0] = (acc_ref[0, part] * scale).astype(jnp.bfloat16)
             halo_ref[1] = acc_ref[1, part].astype(jnp.bfloat16)
-    query_out_ref[...] = jnp.swapaxes(jnp.concatenate(grads, axis=0), 0, 1).astype(jnp.bfloat16)
+    if not last:
+        turned_grads = jnp.swapaxes(jnp.concatenate(grads, axis=0), 0, 1)
+        query_out_ref[...] = turned_grads.astype(jnp.bfloat16)
 
 
 def attend(step, base, span, reach, heads, meta, assignment, segments, query, grad, kv, acc, full, last):
-    first, filled = acc is None, full is not None
+    first, filled = acc is None, full is not None and not last
     rows, (blocks, _, _, kv_width) = query[0].shape[1], kv.shape
     ratio = heads // (kv_width // HD)
     keys, tok_dev = blocks * rows, query[0].shape[1] * lax.axis_size("dp")
@@ -228,6 +233,9 @@
         )
     ]
     if last:
+        stretch = (HEADS_STEP, window, ratio * rows)
+        out_shape = [jax.ShapeDtypeStruct(stretch, jnp.bfloat16)]
+        out_specs = [pl.BlockSpec(stretch, lambda c, m, a: (0, 0, 0))]
         span_spec = pl.BlockSpec((2, tok_dev, lanes), lambda c, m, a: (0, 0, c))
         out_shape.append(jax.ShapeDtypeStruct((2, tok_dev, span * HD), jnp.float32))
         out_shape += [jax.ShapeDtypeStruct((2, tok_dev, span * HD), jnp.bfloat16)] * (pieces - 1)
@@ -260,6 +268,52 @@
     )(*operands)
 
 
+def turn_kernel(step, tok_dev, reach, meta_ref, scores_ref, key_ref, full_ref, out_ref):
+    rows, blocks = out_ref.shape[0], key_ref.shape[0]
+    window = scores_ref.shape[1]
+    source = source_of(meta_ref[0], step, tok_dev // rows)
+    block = (blocks * rows - tok_dev - reach) // rows + source
+    grads = []
+    for head in range(HEADS_STEP):
+        key = key_ref[pl.ds(block, window // rows), :, head * HD : (head + 1) * HD]
+        grad = lax.dot_general(
+            scores_ref[head],
+            key.reshape(window, HD),
+            (((0,), (0,)), ((), ())),
+            preferred_element_type=jnp.float32,
+        )
+        grads.append((grad * (1.0 / HD**0.5)).reshape(-1, rows, HD))
+    out_ref[...] = jnp.swapaxes(jnp.concatenate(grads, axis=0), 0, 1).astype(jnp.bfloat16)
+
+
+def turn(step, place, reach, meta, scores, kv, full):
+    blocks, _, rows, _ = kv.shape
+    tok_dev, heads, _ = full.shape
+    step_heads = HEADS_STEP * scores.shape[2] // rows
+    return pl.pallas_call(
+        functools.partial(turn_kernel, step, tok_dev, reach),
+        out_shape=jax.ShapeDtypeStruct(full.shape, full.dtype),
+        grid_spec=pltpu.PrefetchScalarGridSpec(
+            num_scalar_prefetch=1,
+            grid=(1,),
+            in_specs=[
+                pl.BlockSpec(scores.shape, lambda c, m: (0, 0, 0)),
+                pl.BlockSpec((blocks, None, rows, HEADS_STEP * HD), lambda c, m: (0, 0, 0, place)),
+                pl.BlockSpec(memory_space=pl.ANY),
+            ],
+            out_specs=pl.BlockSpec(
+                (rows, step_heads, HD),
+                lambda c, m: (source_of(m[0], step, tok_dev // rows), place, 0),
+            ),
+        ),
+        input_output_aliases={3: 0},
+        compiler_params=pltpu.CompilerParams(
+            dimension_semantics=("arbitrary",), vmem_limit_bytes=VMEM_BYTES
+        ),
+        name="turn",
+    )(meta, scores, kv, full)
+
+
 def shards(queries, keys, values, grad_out, segment_ids, assignment):
     count = lax.axis_size("dp")
     uly = lax.axis_size("uly")
@@ -303,21 +357,25 @@
         full, acc = attend(step, 0, kv_heads, *fixed, query, grad, kv, acc, full, False)
     rows, acc = lax.optimization_barrier((held[1:], acc))
     split += [exchanged(piece, "dp", final) for piece in rows]
-    totals, returned = [], []
+    totals, returned, held_scores = [], [], []
     for half in range(halves):
         both = split[half]
         query, grad = (both, lambda m, a: 0), (both, lambda m, a: 1)
         if half + 1 == halves:
             grad = (split[half + 1], lambda m, a: 0)
-        full, total, *halos = attend(
+        scores, total, *halos = attend(
             final, half * HEADS_STEP, HEADS_STEP, *fixed, query, grad, kv, acc, full, True
         )
         if half:
             halos, returned[0] = lax.optimization_barrier((halos, returned[0]))
+            held_scores, total = lax.optimization_barrier((held_scores, total))
+        held_scores.append(scores)
         returned = [shifted(halo, ("blk", "uly"), -back) for back, halo in enumerate(halos, 1)]
         for halo in returned:
             total = total + halo.astype(jnp.float32)
         totals.append(total.astype(jnp.bfloat16))
+    for half, scores in enumerate(held_scores):
+        full = turn(final, half, doc_most, meta, scores, kv, full)
     total = jnp.concatenate(totals, axis=2)
     return full[None], total[0][None], total[1][None]
 

time: 74.2 us -> 72.5 us (0.977)
  waiting for transfers between devices: 23 us -> 20.4 us
  Pallas kernels: 18.7 us -> 20 us
    pallas_call x0 -> x2, Pallas kernels: none -> 3.04 us  [turn(): pl.pallas_call(functools.partial(turn_kernel, step, tok_dev, reach), out_...]
    ppermute x6, waiting for transfers between devices: 6.59 us -> 3.74 us  [shifted(): return lax.ppermute(value, axis, pairs)]
    pallas_call x5, Pallas kernels: 15.5 us -> 13.7 us  [attend(): pl.pallas_call(functools.partial(attend_kernel, step, first, filled, last...]
  transfers between devices with their start and end apart: 14 -> 14, of which waited for: 7 -> 7; matrix products, arithmetic and copies ran while one was open for 3% -> 3% of each run, Pallas kernels for 21% -> 23%
where the time goes in v25:
time: 72.5 us; the launch traced here: 72.2 us
  starting transfers between devices  28 us (39%)
  waiting for transfers between devices  20.4 us (28%)
  Pallas kernels  20 us (28%)
  other arithmetic  2.01 us (3%)
  local copies, waits for them, and re-layouts  0.93 us (1%)
  between operations  0.81 us (1%)
    ppermute x8, waiting for transfers between devices, exchanged(): lax.ppermute(value, axis, [(i, (i + step) % count) for i in range(count)])  16.7 us
    ppermute x6, starting transfers between devices, shifted(): return lax.ppermute(value, axis, pairs)  15.7 us
    pallas_call x5, Pallas kernels, attend(): pl.pallas_call(functools.partial(attend_kernel, step, first, filled, last...  13.7 us
    ppermute x8, starting transfers between devices, exchanged(): lax.ppermute(value, axis, [(i, (i + step) % count) for i in range(count)])  12.3 us
    ppermute x6, waiting for transfers between devices, shifted(): return lax.ppermute(value, axis, pairs)  3.74 us
    pallas_call x1, Pallas kernels, stage(): pl.pallas_call(functools.partial(stage_kernel, count, jobs, len(jobs)), o...  3.23 us
    pallas_call x2, Pallas kernels, turn(): pl.pallas_call(functools.partial(turn_kernel, step, tok_dev, reach), out_...  3.04 us
  transfers between devices with their start and end apart: 14, of which 7 were waited for; matrix products, arithmetic and copies ran while one was open for 3% of the time, Pallas kernels for 23%

profile of v25, /device:TPU:1, one launch (start us, length us, event | category | flops | bytes accessed | tf_op | source)
XLA Modules:
  0.0 72.2 jit_solution(17788891913747266066)
XLA Ops:
  0.6 3.2 %stage.1 = (bf16[2,32,512]{2,1,0:T(8,128)(2,1)}, bf16[2,32,512]{2,1,0:T(8,128)(2,1)}, bf16[2,32,512]{2,1,0:T(8,128)(2,1)}, bf16[2,32,512]{2,1,0:T(8,128)(2,1)}, ...) custom-call(s32[4]{0:T(128)} %assign_ref.11, ...), custom_call_target="tpu_custom_call" | custom-call | tf_op jit(solution)/shard_map/stage/pallas_call | solution.py:63
  3.9 2.2 %collective-permute-start = (bf16[2,32,512]{2,1,0:T(8,128)(2,1)}, bf16[2,32,512]{2,1,0:T(8,128)(2,1)S(1)}, u32[]{:S(2)}, u32[]{:S(2)}) collective-permute-start(bf16[2,32,512]{2,1,0:T(8,128)(2,1)} %get-tuple-element.46), channel_id=1, source_target_pairs={{0,1},{1,2},{2,3},{3,0},{4,5},{5,6},{6,7},{7,4},{8,9},{9,10},{10,1... | collective-permute-start | bytes 196616 | tf_op jit(solution)/shard_map/ppermute | solution.py:28
  6.1 2.3 %collective-permute-start.2 = (bf16[2,32,512]{2,1,0:T(8,128)(2,1)}, bf16[2,32,512]{2,1,0:T(8,128)(2,1)S(1)}, u32[]{:S(2)}, u32[]{:S(2)}) collective-permute-start(bf16[2,32,512]{2,1,0:T(8,128)(2,1)} %get-tuple-element.53), channel_id=1, source_target_pairs={{0,2},{1,3},{2,0},{3,1},{4,6},{5,7},{6,4},{7,5},{8,10},{9,11},{10,... | collective-permute-start | bytes 196616 | tf_op jit(solution)/shard_map/ppermute | solution.py:28
  10.8 2.8 %collective-permute-done.2 = bf16[2,32,512]{2,1,0:T(8,128)(2,1)S(1)} collective-permute-done((bf16[2,32,512]{2,1,0:T(8,128)(2,1)}, bf16[2,32,512]{2,1,0:T(8,128)(2,1)S(1)}, u32[]{:S(2)}, u32[]{:S(2)}) %collective-permute-start.2) | collective-permute-done | bytes 65568 | tf_op jit(solution)/shard_map/ppermute | solution.py:28
  13.7 2.4 %collective-permute-start.5 = (bf16[4,2,32,512]{3,2,1,0:T(8,128)(2,1)S(1)}, bf16[4,2,32,512]{3,2,1,0:T(8,128)(2,1)}, u32[]{:S(2)}, u32[]{:S(2)}) collective-permute-start(bf16[4,2,32,512]{3,2,1,0:T(8,128)(2,1)S(1)} %bitcast_dynamic-update-slice_fusion), channel_id=1, source_target_pairs={{0,4},{4,8},{8,12},{12,16},{16,20},{20,24},{24,28},{1,5},{5,9},{9,... | collective-permute-start | bytes 786440 | tf_op jit(solution)/shard_map/ppermute | solution.py:34
  16.1 5.0 %collective-permute-start.4 = (bf16[4,2,32,512]{3,2,1,0:T(8,128)(2,1)S(1)}, bf16[4,2,32,512]{3,2,1,0:T(8,128)(2,1)}, u32[]{:S(2)}, u32[]{:S(2)}) collective-permute-start(bf16[4,2,32,512]{3,2,1,0:T(8,128)(2,1)S(1)} %bitcast_dynamic-update-slice_fusion), channel_id=1, source_target_pairs={{0,8},{4,12},{8,16},{12,20},{16,24},{20,28},{1,9},{5,13},{9,17},{1... | collective-permute-start | bytes 786440 | tf_op jit(solution)/shard_map/ppermute | solution.py:34
  21.1 3.3 %collective-permute-start.1 = (bf16[2,32,4096]{2,1,0:T(8,128)(2,1)}, bf16[2,32,4096]{2,1,0:T(8,128)(2,1)S(1)}, u32[]{:S(2)}, u32[]{:S(2)}) collective-permute-start(bf16[2,32,4096]{2,1,0:T(8,128)(2,1)} %get-tuple-element.49), channel_id=1, source_target_pairs={{0,3},{1,0},{2,1},{3,2},{4,7},{5,4},{6,5},{7,6},{8,11},{9,8},{10,9... | collective-permute-start | bytes 1572872 | tf_op jit(solution)/shard_map/ppermute | solution.py:28
  24.4 1.5 %collective-permute-done.4 = bf16[4,2,32,512]{3,2,1,0:T(8,128)(2,1)} collective-permute-done((bf16[4,2,32,512]{3,2,1,0:T(8,128)(2,1)S(1)}, bf16[4,2,32,512]{3,2,1,0:T(8,128)(2,1)}, u32[]{:S(2)}, u32[]{:S(2)}) %collective-permute-start.4) | collective-permute-done | bytes 262176 | tf_op jit(solution)/shard_map/ppermute | solution.py:34
  25.9 1.1 %pad_maximum_fusion.kv_ref.key_ref = bf16[12,2,32,512]{3,2,1,0:T(8,128)(2,1)S(1)} fusion(bf16[4,2,32,512]{3,2,1,0:T(8,128)(2,1)S(1)} %bitcast_dynamic-update-slice_fusion, bf16[4,2,32,512]{3,2,1,0:T(8,128)(2,1)} %collective-permute-done.5, bf16[4,2,32,512]{3,2,1,0:T(8,128)(2,1)} %collective-permute-done.4), kind=kLoop, calls=%fused_computation | loop fusion | flops 786432 | bytes 1572864 | tf_op jit(solution)/shard_map/concatenate | solution.py:348
  27.8 3.6 %attend.5 = (bf16[128,32,128]{2,1,0:T(8,128)(2,1)}, f32[2,384,512]{2,1,0:T(8,128)S(1)}) custom-call(s32[2]{0:T(128)S(1)} %pad_add_fusion.meta_ref, s32[4]{0:T(128)S(1)} %copy-done.3, s32[4,1024]{1,0:T(4,128)S(1)} %copy-done.2, bf16[4,32,4096]{2,1,0:T(8,128)(2,1)S(1)} %copy-done, bf16[4,32,4096]{2,1,0:T(8,128)(2,1)S(1)} %copy-done.1, ...), custom_call_target="tpu_custom_call" | custom-call | flops 37748736 | bytes 294912 | tf_op jit(solution)/shard_map/attend/pallas_call | solution.py:250
  31.4 3.6 %attend.6 = (bf16[128,32,128]{2,1,0:T(8,128)(2,1)}, f32[2,384,512]{2,1,0:T(8,128)S(1)}) custom-call(s32[2]{0:T(128)S(1)} %pad_add_fusion.meta_ref, s32[4]{0:T(128)S(1)} %copy-done.3, s32[4,1024]{1,0:T(4,128)S(1)} %copy-done.2, bf16[2,32,4096]{2,1,0:T(8,128)(2,1)S(1)} %collective-permute-done.6.query_ref.grad_ref, ...), custom_call_target="tpu_custom_call", output_to_operand_aliasing={{1}: (6, {}), {0}: (7, {})} | custom-call | flops 1132462080 | bytes 8847360 | tf_op jit(solution)/shard_map/attend/pallas_call | solution.py:250
  35.0 2.7 %collective-permute-done.1.query_ref.grad_ref = bf16[2,32,4096]{2,1,0:T(8,128)(2,1)S(1)} collective-permute-done((bf16[2,32,4096]{2,1,0:T(8,128)(2,1)}, bf16[2,32,4096]{2,1,0:T(8,128)(2,1)S(1)}, u32[]{:S(2)}, u32[]{:S(2)}) %collective-permute-start.1) | collective-permute-done | bytes 524320 | tf_op jit(solution)/shard_map/ppermute | solution.py:28
  37.7 3.6 %attend.7 = (bf16[128,32,128]{2,1,0:T(8,128)(2,1)}, f32[2,384,512]{2,1,0:T(8,128)S(1)}) custom-call(s32[2]{0:T(128)S(1)} %pad_add_fusion.meta_ref, s32[4]{0:T(128)S(1)} %copy-done.3, s32[4,1024]{1,0:T(4,128)S(1)} %copy-done.2, bf16[2,32,4096]{2,1,0:T(8,128)(2,1)S(1)} %collective-permute-done.1.query_ref.grad_ref, ...), custom_call_target="tpu_custom_call", output_to_operand_aliasing={{1}: (6, {}), {0}: (7, {})} | custom-call | flops 1132462080 | bytes 8847360 | tf_op jit(solution)/shard_map/attend/pallas_call | solution.py:250
  41.3 2.4 %collective-permute-start.8 = (bf16[1,32,2048]{2,1,0:T(8,128)(2,1)S(1)}, bf16[1,32,2048]{2,1,0:T(8,128)(2,1)S(1)}, u32[]{:S(2)}, u32[]{:S(2)}) collective-permute-start(bf16[1,32,2048]{2,1,0:T(8,128)(2,1)S(1)} %copy-done.4), channel_id=1, source_target_pairs={{0,2},{1,3},{2,0},{3,1},{4,6},{5,7},{6,4},{7,5},{8,10},{9,11},{10,... | collective-permute-start | bytes 393224 | tf_op jit(solution)/shard_map/ppermute | solution.py:28
  43.6 10.9 %collective-permute-done.9.query_ref.grad_ref = bf16[2,32,2048]{2,1,0:T(8,128)(2,1)S(1)} collective-permute-done((bf16[2,32,2048]{2,1,0:T(8,128)(2,1)}, bf16[2,32,2048]{2,1,0:T(8,128)(2,1)S(1)}, u32[]{:S(2)}, u32[]{:S(2)}) %collective-permute-start.9) | collective-permute-done | bytes 262176 | tf_op jit(solution)/shard_map/ppermute | solution.py:28
  54.5 1.5 %attend.9 = (bf16[2,288,256]{2,1,0:T(8,128)(2,1)S(1)}, f32[2,128,256]{2,1,0:T(8,128)S(1)}, bf16[2,128,256]{2,1,0:T(8,128)(2,1)S(1)}, bf16[2,128,256]{2,1,0:T(8,128)(2,1)S(1)}) custom-call(s32[2]{0:T(128)S(1)} %pad_add_fusion.meta_ref, s32[4]{0:T(128)S(1)} %copy-done.3, s32[4,1024]{1,0:T(4,128)S(1)} %copy-done.2, ...), custom_call_target="tpu_custom_call" | custom-call | flops 18874368 | bytes 147456 | tf_op jit(solution)/shard_map/attend/pallas_call | solution.py:250
  56.0 1.9 %collective-permute-start.10 = (bf16[2,128,256]{2,1,0:T(8,128)(2,1)S(1)}, bf16[2,128,256]{2,1,0:T(8,128)(2,1)S(1)}, u32[]{:S(2)}, u32[]{:S(2)}) collective-permute-start(bf16[2,128,256]{2,1,0:T(8,128)(2,1)S(1)} %get-tuple-element.72), channel_id=1, source_target_pairs={{4,0},{8,4},{12,8},{16,12},{20,16},{24,20},{28,24},{5,1},{9,5},{13... | collective-permute-start | bytes 393224 | tf_op jit(solution)/shard_map/ppermute | solution.py:34
  57.9 1.9 %collective-permute-start.11 = (bf16[2,128,256]{2,1,0:T(8,128)(2,1)S(1)}, bf16[2,128,256]{2,1,0:T(8,128)(2,1)S(1)}, u32[]{:S(2)}, u32[]{:S(2)}) collective-permute-start(bf16[2,128,256]{2,1,0:T(8,128)(2,1)S(1)} %get-tuple-element.73), channel_id=1, source_target_pairs={{8,0},{12,4},{16,8},{20,12},{24,16},{28,20},{9,1},{13,5},{17,9},{2... | collective-permute-start | bytes 393224 | tf_op jit(solution)/shard_map/ppermute | solution.py:34
  60.1 1.5 %attend.8 = (bf16[2,288,256]{2,1,0:T(8,128)(2,1)S(1)}, f32[2,128,256]{2,1,0:T(8,128)S(1)}, bf16[2,128,256]{2,1,0:T(8,128)(2,1)S(1)}, bf16[2,128,256]{2,1,0:T(8,128)(2,1)S(1)}) custom-call(s32[2]{0:T(128)S(1)} %pad_add_fusion.meta_ref, s32[4]{0:T(128)S(1)} %copy-done.3, s32[4,1024]{1,0:T(4,128)S(1)} %copy-done.2, ...), custom_call_target="tpu_custom_call" | custom-call | flops 18874368 | bytes 147456 | tf_op jit(solution)/shard_map/attend/pallas_call | solution.py:250
  62.6 2.5 %collective-permute-start.12 = (bf16[2,128,256]{2,1,0:T(8,128)(2,1)S(1)}, bf16[2,128,256]{2,1,0:T(8,128)(2,1)S(1)}, u32[]{:S(2)}, u32[]{:S(2)}) collective-permute-start(bf16[2,128,256]{2,1,0:T(8,128)(2,1)S(1)} %get-tuple-element.77), channel_id=1, source_target_pairs={{4,0},{8,4},{12,8},{16,12},{20,16},{24,20},{28,24},{5,1},{9,5},{13... | collective-permute-start | bytes 393224 | tf_op jit(solution)/shard_map/ppermute | solution.py:34
  65.0 2.0 %collective-permute-start.13 = (bf16[2,128,256]{2,1,0:T(8,128)(2,1)S(1)}, bf16[2,128,256]{2,1,0:T(8,128)(2,1)S(1)}, u32[]{:S(2)}, u32[]{:S(2)}) collective-permute-start(bf16[2,128,256]{2,1,0:T(8,128)(2,1)S(1)} %get-tuple-element.78), channel_id=1, source_target_pairs={{8,0},{12,4},{16,8},{20,12},{24,16},{28,20},{9,1},{13,5},{17,9},{2... | collective-permute-start | bytes 393224 | tf_op jit(solution)/shard_map/ppermute | solution.py:34
  67.0 1.5 %turn.2.full_ref = bf16[128,32,128]{2,1,0:T(8,128)(2,1)} custom-call(s32[2]{0:T(128)S(1)} %pad_add_fusion.meta_ref, bf16[2,288,256]{2,1,0:T(8,128)(2,1)S(1)} %get-tuple-element.69.scores_ref, bf16[12,2,32,512]{3,2,1,0:T(8,128)(2,1)S(1)} %pad_maximum_fusion.kv_ref.key_ref, ...), custom_call_target="tpu_custom_call", output_to_operand_aliasing={{}: (3, {})} | custom-call | tf_op jit(solution)/shard_map/turn/pallas_call | solution.py:293
  68.5 1.5 %turn.3 = bf16[128,32,128]{2,1,0:T(8,128)(2,1)} custom-call(s32[2]{0:T(128)S(1)} %pad_add_fusion.meta_ref, bf16[2,288,256]{2,1,0:T(8,128)(2,1)S(1)} %get-tuple-element.65.scores_ref, bf16[12,2,32,512]{3,2,1,0:T(8,128)(2,1)S(1)} %pad_maximum_fusion.kv_ref.key_ref, bf16[128,32,128]{2,1,0:T(8,128)(2,1)} %turn.2.full_ref), custom_call_target="tpu_custom_call", output_to_operand_aliasing={{}: (3, {})} | custom-call | tf_op jit(solution)/shard_map/turn/pallas_call | solution.py:293
  70.1 1.3 %collective-permute-done.13 = bf16[2,128,256]{2,1,0:T(8,128)(2,1)S(1)} collective-permute-done((bf16[2,128,256]{2,1,0:T(8,128)(2,1)S(1)}, bf16[2,128,256]{2,1,0:T(8,128)(2,1)S(1)}, u32[]{:S(2)}, u32[]{:S(2)}) %collective-permute-start.13) | collective-permute-done | bytes 131104 | tf_op jit(solution)/shard_map/ppermute | solution.py:34
  (34 shorter events, 5.2 us)
Async XLA Ops:
  3.9 23.9 %copy-start = (bf16[4,32,4096]{2,1,0:T(8,128)(2,1)S(1)}, bf16[4,32,4096]{2,1,0:T(8,128)(2,1)}, u32[]{:S(2)}) copy-start(bf16[4,32,4096]{2,1,0:T(8,128)(2,1)} %query_ref.1) | copy-start | bytes 3145732
  3.9 23.9 %copy-start.1 = (bf16[4,32,4096]{2,1,0:T(8,128)(2,1)S(1)}, bf16[4,32,4096]{2,1,0:T(8,128)(2,1)}, u32[]{:S(2)}) copy-start(bf16[4,32,4096]{2,1,0:T(8,128)(2,1)} %grad_ref.1) | copy-start | bytes 3145732
  3.9 23.9 %copy-start.2 = (s32[4,1024]{1,0:T(4,128)S(1)}, s32[4,1024]{1,0:T(4,128)}, u32[]{:S(2)}) copy-start(s32[4,1024]{1,0:T(4,128)} %segment_ref.9) | copy-start | bytes 49156
  3.9 23.9 %copy-start.3 = (s32[4]{0:T(128)S(1)}, s32[4]{0:T(128)}, u32[]{:S(2)}) copy-start(s32[4]{0:T(128)} %assign_ref.11) | copy-start | bytes 52
  3.9 6.4 %collective-permute-start = (bf16[2,32,512]{2,1,0:T(8,128)(2,1)}, bf16[2,32,512]{2,1,0:T(8,128)(2,1)S(1)}, u32[]{:S(2)}, u32[]{:S(2)}) collective-permute-start(bf16[2,32,512]{2,1,0:T(8,128)(2,1)} %get-tuple-element.46), channel_id=1, source_target_pairs={{0,1},{1,2},{2,3},{3,0},{4,5},{5,6},{6,7},{7,4},{8,9},{9,10},{10,1... | collective-permute-start | bytes 196616 | tf_op jit(solution)/shard_map/ppermute | solution.py:28
  6.1 7.5 %collective-permute-start.2 = (bf16[2,32,512]{2,1,0:T(8,128)(2,1)}, bf16[2,32,512]{2,1,0:T(8,128)(2,1)S(1)}, u32[]{:S(2)}, u32[]{:S(2)}) collective-permute-start(bf16[2,32,512]{2,1,0:T(8,128)(2,1)} %get-tuple-element.53), channel_id=1, source_target_pairs={{0,2},{1,3},{2,0},{3,1},{4,6},{5,7},{6,4},{7,5},{8,10},{9,11},{10,... | collective-permute-start | bytes 196616 | tf_op jit(solution)/shard_map/ppermute | solution.py:28
  8.4 5.2 %collective-permute-start.3 = (bf16[2,32,512]{2,1,0:T(8,128)(2,1)}, bf16[2,32,512]{2,1,0:T(8,128)(2,1)S(1)}, u32[]{:S(2)}, u32[]{:S(2)}) collective-permute-start(bf16[2,32,512]{2,1,0:T(8,128)(2,1)} %get-tuple-element.54), channel_id=1, source_target_pairs={{0,3},{1,0},{2,1},{3,2},{4,7},{5,4},{6,5},{7,6},{8,11},{9,8},{10,9... | collective-permute-start | bytes 196616 | tf_op jit(solution)/shard_map/ppermute | solution.py:28
  10.4 21.1 %collective-permute-start.6 = (bf16[2,32,4096]{2,1,0:T(8,128)(2,1)}, bf16[2,32,4096]{2,1,0:T(8,128)(2,1)S(1)}, u32[]{:S(2)}, u32[]{:S(2)}) collective-permute-start(bf16[2,32,4096]{2,1,0:T(8,128)(2,1)} %get-tuple-element.56), channel_id=1, source_target_pairs={{0,1},{1,2},{2,3},{3,0},{4,5},{5,6},{6,7},{7,4},{8,9},{9,10},{10,1... | collective-permute-start | bytes 1572872 | tf_op jit(solution)/shard_map/ppermute | solution.py:28
  13.7 10.8 %collective-permute-start.5 = (bf16[4,2,32,512]{3,2,1,0:T(8,128)(2,1)S(1)}, bf16[4,2,32,512]{3,2,1,0:T(8,128)(2,1)}, u32[]{:S(2)}, u32[]{:S(2)}) collective-permute-start(bf16[4,2,32,512]{3,2,1,0:T(8,128)(2,1)S(1)} %bitcast_dynamic-update-slice_fusion), channel_id=1, source_target_pairs={{0,4},{4,8},{8,12},{12,16},{16,20},{20,24},{24,28},{1,5},{5,9},{9,... | collective-permute-start | bytes 786440 | tf_op jit(solution)/shard_map/ppermute | solution.py:34
  16.1 9.9 %collective-permute-start.4 = (bf16[4,2,32,512]{3,2,1,0:T(8,128)(2,1)S(1)}, bf16[4,2,32,512]{3,2,1,0:T(8,128)(2,1)}, u32[]{:S(2)}, u32[]{:S(2)}) collective-permute-start(bf16[4,2,32,512]{3,2,1,0:T(8,128)(2,1)S(1)} %bitcast_dynamic-update-slice_fusion), channel_id=1, source_target_pairs={{0,8},{4,12},{8,16},{12,20},{16,24},{20,28},{1,9},{5,13},{9,17},{1... | collective-permute-start | bytes 786440 | tf_op jit(solution)/shard_map/ppermute | solution.py:34
  21.1 16.6 %collective-permute-start.1 = (bf16[2,32,4096]{2,1,0:T(8,128)(2,1)}, bf16[2,32,4096]{2,1,0:T(8,128)(2,1)S(1)}, u32[]{:S(2)}, u32[]{:S(2)}) collective-permute-start(bf16[2,32,4096]{2,1,0:T(8,128)(2,1)} %get-tuple-element.49), channel_id=1, source_target_pairs={{0,3},{1,0},{2,1},{3,2},{4,7},{5,4},{6,5},{7,6},{8,11},{9,8},{10,9... | collective-permute-start | bytes 1572872 | tf_op jit(solution)/shard_map/ppermute | solution.py:28
  27.1 27.5 %collective-permute-start.9 = (bf16[2,32,2048]{2,1,0:T(8,128)(2,1)}, bf16[2,32,2048]{2,1,0:T(8,128)(2,1)S(1)}, u32[]{:S(2)}, u32[]{:S(2)}) collective-permute-start(bf16[2,32,2048]{2,1,0:T(8,128)(2,1)} %get-tuple-element.66), channel_id=1, source_target_pairs={{0,2},{1,3},{2,0},{3,1},{4,6},{5,7},{6,4},{7,5},{8,10},{9,11},{10,... | collective-permute-start | bytes 786440 | tf_op jit(solution)/shard_map/ppermute | solution.py:28
  37.7 3.6 %copy-start.5 = (bf16[1,32,2048]{2,1,0:T(8,128)(2,1)S(1)}, bf16[1,32,2048]{2,1,0:T(8,128)(2,1)}, u32[]{:S(2)}) copy-start(bf16[1,32,2048]{2,1,0:T(8,128)(2,1)} %get-tuple-element.62) | copy-start | bytes 393220
  37.7 3.6 %copy-start.4 = (bf16[1,32,2048]{2,1,0:T(8,128)(2,1)S(1)}, bf16[1,32,2048]{2,1,0:T(8,128)(2,1)}, u32[]{:S(2)}) copy-start(bf16[1,32,2048]{2,1,0:T(8,128)(2,1)} %get-tuple-element.63) | copy-start | bytes 393220
  41.3 18.6 %collective-permute-start.7 = (bf16[1,32,2048]{2,1,0:T(8,128)(2,1)S(1)}, bf16[1,32,2048]{2,1,0:T(8,128)(2,1)S(1)}, u32[]{:S(2)}, u32[]{:S(2)}) collective-permute-start(bf16[1,32,2048]{2,1,0:T(8,128)(2,1)S(1)} %copy-done.5), channel_id=1, source_target_pairs={{0,2},{1,3},{2,0},{3,1},{4,6},{5,7},{6,4},{7,5},{8,10},{9,11},{10,... | collective-permute-start | bytes 393224 | tf_op jit(solution)/shard_map/ppermute | solution.py:28
  41.3 18.9 %collective-permute-start.8 = (bf16[1,32,2048]{2,1,0:T(8,128)(2,1)S(1)}, bf16[1,32,2048]{2,1,0:T(8,128)(2,1)S(1)}, u32[]{:S(2)}, u32[]{:S(2)}) collective-permute-start(bf16[1,32,2048]{2,1,0:T(8,128)(2,1)S(1)} %copy-done.4), channel_id=1, source_target_pairs={{0,2},{1,3},{2,0},{3,1},{4,6},{5,7},{6,4},{7,5},{8,10},{9,11},{10,... | collective-permute-start | bytes 393224 | tf_op jit(solution)/shard_map/ppermute | solution.py:28
  56.0 6.6 %collective-permute-start.10 = (bf16[2,128,256]{2,1,0:T(8,128)(2,1)S(1)}, bf16[2,128,256]{2,1,0:T(8,128)(2,1)S(1)}, u32[]{:S(2)}, u32[]{:S(2)}) collective-permute-start(bf16[2,128,256]{2,1,0:T(8,128)(2,1)S(1)} %get-tuple-element.72), channel_id=1, source_target_pairs={{4,0},{8,4},{12,8},{16,12},{20,16},{24,20},{28,24},{5,1},{9,5},{13... | collective-permute-start | bytes 393224 | tf_op jit(solution)/shard_map/ppermute | solution.py:34
  57.9 12.1 %collective-permute-start.11 = (bf16[2,128,256]{2,1,0:T(8,128)(2,1)S(1)}, bf16[2,128,256]{2,1,0:T(8,128)(2,1)S(1)}, u32[]{:S(2)}, u32[]{:S(2)}) collective-permute-start(bf16[2,128,256]{2,1,0:T(8,128)(2,1)S(1)} %get-tuple-element.73), channel_id=1, source_target_pairs={{8,0},{12,4},{16,8},{20,12},{24,16},{28,20},{9,1},{13,5},{17,9},{2... | collective-permute-start | bytes 393224 | tf_op jit(solution)/shard_map/ppermute | solution.py:34
  62.6 7.5 %collective-permute-start.12 = (bf16[2,128,256]{2,1,0:T(8,128)(2,1)S(1)}, bf16[2,128,256]{2,1,0:T(8,128)(2,1)S(1)}, u32[]{:S(2)}, u32[]{:S(2)}) collective-permute-start(bf16[2,128,256]{2,1,0:T(8,128)(2,1)S(1)} %get-tuple-element.77), channel_id=1, source_target_pairs={{4,0},{8,4},{12,8},{16,12},{20,16},{24,20},{28,24},{5,1},{9,5},{13... | collective-permute-start | bytes 393224 | tf_op jit(solution)/shard_map/ppermute | solution.py:34
  65.0 6.4 %collective-permute-start.13 = (bf16[2,128,256]{2,1,0:T(8,128)(2,1)S(1)}, bf16[2,128,256]{2,1,0:T(8,128)(2,1)S(1)}, u32[]{:S(2)}, u32[]{:S(2)}) collective-permute-start(bf16[2,128,256]{2,1,0:T(8,128)(2,1)S(1)} %get-tuple-element.78), channel_id=1, source_target_pairs={{8,0},{12,4},{16,8},{20,12},{24,16},{28,20},{9,1},{13,5},{17,9},{2... | collective-permute-start | bytes 393224 | tf_op jit(solution)/shard_map/ppermute | solution.py:34

commit v26 on v25

--- a/solution.py
+++ b/solution.py
@@ -268,50 +268,58 @@
     )(*operands)
 
 
-def turn_kernel(step, tok_dev, reach, meta_ref, scores_ref, key_ref, full_ref, out_ref):
+def turn_kernel(step, tok_dev, reach, meta_ref, key_ref, full_ref, *refs):
+    scores_refs, out_ref = refs[:-1], refs[-1]
     rows, blocks = out_ref.shape[0], key_ref.shape[0]
-    window = scores_ref.shape[1]
+    window = scores_refs[0].shape[1]
     source = source_of(meta_ref[0], step, tok_dev // rows)
     block = (blocks * rows - tok_dev - reach) // rows + source
-    grads = []
-    for head in range(HEADS_STEP):
-        key = key_ref[pl.ds(block, window // rows), :, head * HD : (head + 1) * HD]
-        grad = lax.dot_general(
-            scores_ref[head],
-            key.reshape(window, HD),
-            (((0,), (0,)), ((), ())),
-            preferred_element_type=jnp.float32,
-        )
-        grads.append((grad * (1.0 / HD**0.5)).reshape(-1, rows, HD))
-    out_ref[...] = jnp.swapaxes(jnp.concatenate(grads, axis=0), 0, 1).astype(jnp.bfloat16)
-
-
-def turn(step, place, reach, meta, scores, kv, full):
+
+    def one(scores_ref):
+        grads = []
+        for head in range(HEADS_STEP):
+            key = key_ref[pl.ds(block, window // rows), :, head * HD : (head + 1) * HD]
+            grad = lax.dot_general(
+                scores_ref[head],
+                key.reshape(window, HD),
+                (((0,), (0,)), ((), ())),
+                preferred_element_type=jnp.float32,
+            )
+            grads.append((grad * (1.0 / HD**0.5)).reshape(-1, rows, HD))
+        turned = jnp.swapaxes(jnp.concatenate(grads, axis=0), 0, 1)
+        out_ref[...] = turned.astype(jnp.bfloat16)
+
+    for half, scores_ref in enumerate(scores_refs):
+        pl.when(pl.program_id(0) == half)(functools.partial(one, scores_ref))
+
+
+def turn(step, reach, meta, scores, kv, full):
     blocks, _, rows, _ = kv.shape
     tok_dev, heads, _ = full.shape
-    step_heads = HEADS_STEP * scores.shape[2] // rows
+    shape = scores[0].shape
+    step_heads = HEADS_STEP * shape[2] // rows
     return pl.pallas_call(
         functools.partial(turn_kernel, step, tok_dev, reach),
         out_shape=jax.ShapeDtypeStruct(full.shape, full.dtype),
         grid_spec=pltpu.PrefetchScalarGridSpec(
             num_scalar_prefetch=1,
-            grid=(1,),
+            grid=(len(scores),),
             in_specs=[
-                pl.BlockSpec(scores.shape, lambda c, m: (0, 0, 0)),
-                pl.BlockSpec((blocks, None, rows, HEADS_STEP * HD), lambda c, m: (0, 0, 0, place)),
+                pl.BlockSpec((blocks, None, rows, HEADS_STEP * HD), lambda c, m: (0, 0, 0, c)),
                 pl.BlockSpec(memory_space=pl.ANY),
-            ],
+            ]
+            + [pl.BlockSpec(shape, lambda c, m: (0, 0, 0))] * len(scores),
             out_specs=pl.BlockSpec(
                 (rows, step_heads, HD),
-                lambda c, m: (source_of(m[0], step, tok_dev // rows), place, 0),
+                lambda c, m: (source_of(m[0], step, tok_dev // rows), c, 0),
             ),
         ),
-        input_output_aliases={3: 0},
+        input_output_aliases={2: 0},
         compiler_params=pltpu.CompilerParams(
             dimension_semantics=("arbitrary",), vmem_limit_bytes=VMEM_BYTES
         ),
         name="turn",
-    )(meta, scores, kv, full)
+    )(meta, kv, full, *scores)
 
 
 def shards(queries, keys, values, grad_out, segment_ids, assignment):
@@ -374,8 +382,7 @@
         for halo in returned:
             total = total + halo.astype(jnp.float32)
         totals.append(total.astype(jnp.bfloat16))
-    for half, scores in enumerate(held_scores):
-        full = turn(final, half, doc_most, meta, scores, kv, full)
+    full = turn(final, doc_most, meta, held_scores, kv, full)
     total = jnp.concatenate(totals, axis=2)
     return full[None], total[0][None], total[1][None]
 

time: 72.5 us -> 72.5 us (level)
  Pallas kernels: 20 us -> 18.9 us
  waiting for transfers between devices: 20.4 us -> 21.5 us
    ppermute x6, waiting for transfers between devices: 3.74 us -> 4.83 us  [shifted(): return lax.ppermute(value, axis, pairs)]
    pallas_call x2 -> x1, Pallas kernels: 3.04 us -> 1.96 us  [turn(): pl.pallas_call(functools.partial(turn_kernel, step, tok_dev, reach), out_...]
  transfers between devices with their start and end apart: 14 -> 14, of which waited for: 7 -> 7; matrix products, arithmetic and copies ran while one was open for 3% -> 3% of each run, Pallas kernels for 23% -> 22%
where the time goes in v26:
time: 72.5 us; the launch traced here: 72.2 us
  starting transfers between devices  28 us (39%)
  waiting for transfers between devices  21.5 us (30%)
  Pallas kernels  18.9 us (26%)
  other arithmetic  2.01 us (3%)
  local copies, waits for them, and re-layouts  0.93 us (1%)
  between operations  0.81 us (1%)
    ppermute x8, waiting for transfers between devices, exchanged(): lax.ppermute(value, axis, [(i, (i + step) % count) for i in range(count)])  16.7 us
    ppermute x6, starting transfers between devices, shifted(): return lax.ppermute(value, axis, pairs)  15.7 us
    pallas_call x5, Pallas kernels, attend(): pl.pallas_call(functools.partial(attend_kernel, step, first, filled, last...  13.7 us
    ppermute x8, starting transfers between devices, exchanged(): lax.ppermute(value, axis, [(i, (i + step) % count) for i in range(count)])  12.3 us
    ppermute x6, waiting for transfers between devices, shifted(): return lax.ppermute(value, axis, pairs)  4.83 us
    pallas_call x1, Pallas kernels, stage(): pl.pallas_call(functools.partial(stage_kernel, count, jobs, len(jobs)), o...  3.23 us
    pallas_call x1, Pallas kernels, turn(): pl.pallas_call(functools.partial(turn_kernel, step, tok_dev, reach), out_...  1.96 us
  transfers between devices with their start and end apart: 14, of which 7 were waited for; matrix products, arithmetic and copies ran while one was open for 3% of the time, Pallas kernels for 22%

profile of v26, /device:TPU:1, one launch (start us, length us, event | category | flops | bytes accessed | tf_op | source)
XLA Modules:
  0.0 72.2 jit_solution(9319911233547101134)
XLA Ops:
  0.6 3.2 %stage.1 = (bf16[2,32,512]{2,1,0:T(8,128)(2,1)}, bf16[2,32,512]{2,1,0:T(8,128)(2,1)}, bf16[2,32,512]{2,1,0:T(8,128)(2,1)}, bf16[2,32,512]{2,1,0:T(8,128)(2,1)}, ...) custom-call(s32[4]{0:T(128)} %assign_ref.11, ...), custom_call_target="tpu_custom_call" | custom-call | tf_op jit(solution)/shard_map/stage/pallas_call | solution.py:63
  3.9 2.2 %collective-permute-start = (bf16[2,32,512]{2,1,0:T(8,128)(2,1)}, bf16[2,32,512]{2,1,0:T(8,128)(2,1)S(1)}, u32[]{:S(2)}, u32[]{:S(2)}) collective-permute-start(bf16[2,32,512]{2,1,0:T(8,128)(2,1)} %get-tuple-element.46), channel_id=1, source_target_pairs={{0,1},{1,2},{2,3},{3,0},{4,5},{5,6},{6,7},{7,4},{8,9},{9,10},{10,1... | collective-permute-start | bytes 196616 | tf_op jit(solution)/shard_map/ppermute | solution.py:28
  6.1 2.3 %collective-permute-start.1 = (bf16[2,32,512]{2,1,0:T(8,128)(2,1)}, bf16[2,32,512]{2,1,0:T(8,128)(2,1)S(1)}, u32[]{:S(2)}, u32[]{:S(2)}) collective-permute-start(bf16[2,32,512]{2,1,0:T(8,128)(2,1)} %get-tuple-element.50), channel_id=1, source_target_pairs={{0,2},{1,3},{2,0},{3,1},{4,6},{5,7},{6,4},{7,5},{8,10},{9,11},{10,... | collective-permute-start | bytes 196616 | tf_op jit(solution)/shard_map/ppermute | solution.py:28
  8.4 1.1 %collective-permute-start.2 = (bf16[2,32,512]{2,1,0:T(8,128)(2,1)}, bf16[2,32,512]{2,1,0:T(8,128)(2,1)S(1)}, u32[]{:S(2)}, u32[]{:S(2)}) collective-permute-start(bf16[2,32,512]{2,1,0:T(8,128)(2,1)} %get-tuple-element.51), channel_id=1, source_target_pairs={{0,3},{1,0},{2,1},{3,2},{4,7},{5,4},{6,5},{7,6},{8,11},{9,8},{10,9... | collective-permute-start | bytes 196616 | tf_op jit(solution)/shard_map/ppermute | solution.py:28
  10.8 2.8 %collective-permute-done.1 = bf16[2,32,512]{2,1,0:T(8,128)(2,1)S(1)} collective-permute-done((bf16[2,32,512]{2,1,0:T(8,128)(2,1)}, bf16[2,32,512]{2,1,0:T(8,128)(2,1)S(1)}, u32[]{:S(2)}, u32[]{:S(2)}) %collective-permute-start.1) | collective-permute-done | bytes 65568 | tf_op jit(solution)/shard_map/ppermute | solution.py:28
  13.7 2.4 %collective-permute-start.4 = (bf16[4,2,32,512]{3,2,1,0:T(8,128)(2,1)S(1)}, bf16[4,2,32,512]{3,2,1,0:T(8,128)(2,1)}, u32[]{:S(2)}, u32[]{:S(2)}) collective-permute-start(bf16[4,2,32,512]{3,2,1,0:T(8,128)(2,1)S(1)} %bitcast_dynamic-update-slice_fusion), channel_id=1, source_target_pairs={{0,4},{4,8},{8,12},{12,16},{16,20},{20,24},{24,28},{1,5},{5,9},{9,... | collective-permute-start | bytes 786440 | tf_op jit(solution)/shard_map/ppermute | solution.py:34
  16.1 5.0 %collective-permute-start.3 = (bf16[4,2,32,512]{3,2,1,0:T(8,128)(2,1)S(1)}, bf16[4,2,32,512]{3,2,1,0:T(8,128)(2,1)}, u32[]{:S(2)}, u32[]{:S(2)}) collective-permute-start(bf16[4,2,32,512]{3,2,1,0:T(8,128)(2,1)S(1)} %bitcast_dynamic-update-slice_fusion), channel_id=1, source_target_pairs={{0,8},{4,12},{8,16},{12,20},{16,24},{20,28},{1,9},{5,13},{9,17},{1... | collective-permute-start | bytes 786440 | tf_op jit(solution)/shard_map/ppermute | solution.py:34
  21.1 3.3 %collective-permute-start.5 = (bf16[2,32,4096]{2,1,0:T(8,128)(2,1)}, bf16[2,32,4096]{2,1,0:T(8,128)(2,1)S(1)}, u32[]{:S(2)}, u32[]{:S(2)}) collective-permute-start(bf16[2,32,4096]{2,1,0:T(8,128)(2,1)} %get-tuple-element.53), channel_id=1, source_target_pairs={{0,3},{1,0},{2,1},{3,2},{4,7},{5,4},{6,5},{7,6},{8,11},{9,8},{10,9... | collective-permute-start | bytes 1572872 | tf_op jit(solution)/shard_map/ppermute | solution.py:28
  24.4 1.5 %collective-permute-done.3 = bf16[4,2,32,512]{3,2,1,0:T(8,128)(2,1)} collective-permute-done((bf16[4,2,32,512]{3,2,1,0:T(8,128)(2,1)S(1)}, bf16[4,2,32,512]{3,2,1,0:T(8,128)(2,1)}, u32[]{:S(2)}, u32[]{:S(2)}) %collective-permute-start.3) | collective-permute-done | bytes 262176 | tf_op jit(solution)/shard_map/ppermute | solution.py:34
  25.9 1.1 %pad_maximum_fusion.kv_ref.key_ref = bf16[12,2,32,512]{3,2,1,0:T(8,128)(2,1)S(1)} fusion(bf16[4,2,32,512]{3,2,1,0:T(8,128)(2,1)S(1)} %bitcast_dynamic-update-slice_fusion, bf16[4,2,32,512]{3,2,1,0:T(8,128)(2,1)} %collective-permute-done.4, bf16[4,2,32,512]{3,2,1,0:T(8,128)(2,1)} %collective-permute-done.3), kind=kLoop, calls=%fused_computation | loop fusion | flops 786432 | bytes 1572864 | tf_op jit(solution)/shard_map/concatenate | solution.py:356
  27.8 3.6 %attend.5 = (bf16[128,32,128]{2,1,0:T(8,128)(2,1)}, f32[2,384,512]{2,1,0:T(8,128)S(1)}) custom-call(s32[2]{0:T(128)S(1)} %pad_add_fusion.meta_ref, s32[4]{0:T(128)S(1)} %copy-done.3, s32[4,1024]{1,0:T(4,128)S(1)} %copy-done.2, bf16[4,32,4096]{2,1,0:T(8,128)(2,1)S(1)} %copy-done, bf16[4,32,4096]{2,1,0:T(8,128)(2,1)S(1)} %copy-done.1, ...), custom_call_target="tpu_custom_call" | custom-call | flops 37748736 | bytes 294912 | tf_op jit(solution)/shard_map/attend/pallas_call | solution.py:250
  31.4 3.6 %attend.6 = (bf16[128,32,128]{2,1,0:T(8,128)(2,1)}, f32[2,384,512]{2,1,0:T(8,128)S(1)}) custom-call(s32[2]{0:T(128)S(1)} %pad_add_fusion.meta_ref, s32[4]{0:T(128)S(1)} %copy-done.3, s32[4,1024]{1,0:T(4,128)S(1)} %copy-done.2, bf16[2,32,4096]{2,1,0:T(8,128)(2,1)S(1)} %collective-permute-done.6.query_ref.grad_ref, ...), custom_call_target="tpu_custom_call", output_to_operand_aliasing={{1}: (6, {}), {0}: (7, {})} | custom-call | flops 1132462080 | bytes 8847360 | tf_op jit(solution)/shard_map/attend/pallas_call | solution.py:250
  35.0 2.7 %collective-permute-done.5.query_ref.grad_ref = bf16[2,32,4096]{2,1,0:T(8,128)(2,1)S(1)} collective-permute-done((bf16[2,32,4096]{2,1,0:T(8,128)(2,1)}, bf16[2,32,4096]{2,1,0:T(8,128)(2,1)S(1)}, u32[]{:S(2)}, u32[]{:S(2)}) %collective-permute-start.5) | collective-permute-done | bytes 524320 | tf_op jit(solution)/shard_map/ppermute | solution.py:28
  37.7 3.6 %attend.7 = (bf16[128,32,128]{2,1,0:T(8,128)(2,1)}, f32[2,384,512]{2,1,0:T(8,128)S(1)}) custom-call(s32[2]{0:T(128)S(1)} %pad_add_fusion.meta_ref, s32[4]{0:T(128)S(1)} %copy-done.3, s32[4,1024]{1,0:T(4,128)S(1)} %copy-done.2, bf16[2,32,4096]{2,1,0:T(8,128)(2,1)S(1)} %collective-permute-done.5.query_ref.grad_ref, ...), custom_call_target="tpu_custom_call", output_to_operand_aliasing={{1}: (6, {}), {0}: (7, {})} | custom-call | flops 1132462080 | bytes 8847360 | tf_op jit(solution)/shard_map/attend/pallas_call | solution.py:250
  41.3 2.4 %collective-permute-start.9 = (bf16[1,32,2048]{2,1,0:T(8,128)(2,1)S(1)}, bf16[1,32,2048]{2,1,0:T(8,128)(2,1)S(1)}, u32[]{:S(2)}, u32[]{:S(2)}) collective-permute-start(bf16[1,32,2048]{2,1,0:T(8,128)(2,1)S(1)} %copy-done.4), channel_id=1, source_target_pairs={{0,2},{1,3},{2,0},{3,1},{4,6},{5,7},{6,4},{7,5},{8,10},{9,11},{10,... | collective-permute-start | bytes 393224 | tf_op jit(solution)/shard_map/ppermute | solution.py:28
  43.6 10.9 %collective-permute-done.7.query_ref.grad_ref = bf16[2,32,2048]{2,1,0:T(8,128)(2,1)S(1)} collective-permute-done((bf16[2,32,2048]{2,1,0:T(8,128)(2,1)}, bf16[2,32,2048]{2,1,0:T(8,128)(2,1)S(1)}, u32[]{:S(2)}, u32[]{:S(2)}) %collective-permute-start.7) | collective-permute-done | bytes 262176 | tf_op jit(solution)/shard_map/ppermute | solution.py:28
  54.5 1.5 %attend.8 = (bf16[2,288,256]{2,1,0:T(8,128)(2,1)S(1)}, f32[2,128,256]{2,1,0:T(8,128)S(1)}, bf16[2,128,256]{2,1,0:T(8,128)(2,1)S(1)}, bf16[2,128,256]{2,1,0:T(8,128)(2,1)S(1)}) custom-call(s32[2]{0:T(128)S(1)} %pad_add_fusion.meta_ref, s32[4]{0:T(128)S(1)} %copy-done.3, s32[4,1024]{1,0:T(4,128)S(1)} %copy-done.2, ...), custom_call_target="tpu_custom_call" | custom-call | flops 18874368 | bytes 147456 | tf_op jit(solution)/shard_map/attend/pallas_call | solution.py:250
  56.0 1.9 %collective-permute-start.10 = (bf16[2,128,256]{2,1,0:T(8,128)(2,1)S(1)}, bf16[2,128,256]{2,1,0:T(8,128)(2,1)S(1)}, u32[]{:S(2)}, u32[]{:S(2)}) collective-permute-start(bf16[2,128,256]{2,1,0:T(8,128)(2,1)S(1)} %get-tuple-element.72), channel_id=1, source_target_pairs={{4,0},{8,4},{12,8},{16,12},{20,16},{24,20},{28,24},{5,1},{9,5},{13... | collective-permute-start | bytes 393224 | tf_op jit(solution)/shard_map/ppermute | solution.py:34
  57.9 1.9 %collective-permute-start.11 = (bf16[2,128,256]{2,1,0:T(8,128)(2,1)S(1)}, bf16[2,128,256]{2,1,0:T(8,128)(2,1)S(1)}, u32[]{:S(2)}, u32[]{:S(2)}) collective-permute-start(bf16[2,128,256]{2,1,0:T(8,128)(2,1)S(1)} %get-tuple-element.73), channel_id=1, source_target_pairs={{8,0},{12,4},{16,8},{20,12},{24,16},{28,20},{9,1},{13,5},{17,9},{2... | collective-permute-start | bytes 393224 | tf_op jit(solution)/shard_map/ppermute | solution.py:34
  60.1 1.5 %attend.9 = (bf16[2,288,256]{2,1,0:T(8,128)(2,1)S(1)}, f32[2,128,256]{2,1,0:T(8,128)S(1)}, bf16[2,128,256]{2,1,0:T(8,128)(2,1)S(1)}, bf16[2,128,256]{2,1,0:T(8,128)(2,1)S(1)}) custom-call(s32[2]{0:T(128)S(1)} %pad_add_fusion.meta_ref, s32[4]{0:T(128)S(1)} %copy-done.3, s32[4,1024]{1,0:T(4,128)S(1)} %copy-done.2, ...), custom_call_target="tpu_custom_call" | custom-call | flops 18874368 | bytes 147456 | tf_op jit(solution)/shard_map/attend/pallas_call | solution.py:250
  62.6 2.5 %collective-permute-start.12 = (bf16[2,128,256]{2,1,0:T(8,128)(2,1)S(1)}, bf16[2,128,256]{2,1,0:T(8,128)(2,1)S(1)}, u32[]{:S(2)}, u32[]{:S(2)}) collective-permute-start(bf16[2,128,256]{2,1,0:T(8,128)(2,1)S(1)} %get-tuple-element.77), channel_id=1, source_target_pairs={{4,0},{8,4},{12,8},{16,12},{20,16},{24,20},{28,24},{5,1},{9,5},{13... | collective-permute-start | bytes 393224 | tf_op jit(solution)/shard_map/ppermute | solution.py:34
  65.0 2.0 %collective-permute-start.13 = (bf16[2,128,256]{2,1,0:T(8,128)(2,1)S(1)}, bf16[2,128,256]{2,1,0:T(8,128)(2,1)S(1)}, u32[]{:S(2)}, u32[]{:S(2)}) collective-permute-start(bf16[2,128,256]{2,1,0:T(8,128)(2,1)S(1)} %get-tuple-element.78), channel_id=1, source_target_pairs={{8,0},{12,4},{16,8},{20,12},{24,16},{28,20},{9,1},{13,5},{17,9},{2... | collective-permute-start | bytes 393224 | tf_op jit(solution)/shard_map/ppermute | solution.py:34
  67.0 2.0 %turn.1 = bf16[128,32,128]{2,1,0:T(8,128)(2,1)} custom-call(s32[2]{0:T(128)S(1)} %pad_add_fusion.meta_ref, bf16[12,2,32,512]{3,2,1,0:T(8,128)(2,1)S(1)} %pad_maximum_fusion.kv_ref.key_ref, bf16[128,32,128]{2,1,0:T(8,128)(2,1)} %get-tuple-element.59.full_ref, bf16[2,288,256]{2,1,0:T(8,128)(2,1)S(1)} %get-tuple-element.69.refs_0_, ...), custom_call_target="tpu_custom_call", output_to_operand_aliasing={{}: (2, {})} | custom-call | tf_op jit(solution)/shard_map/turn/pallas_call | solution.py:301
  69.0 2.4 %collective-permute-done.13 = bf16[2,128,256]{2,1,0:T(8,128)(2,1)S(1)} collective-permute-done((bf16[2,128,256]{2,1,0:T(8,128)(2,1)S(1)}, bf16[2,128,256]{2,1,0:T(8,128)(2,1)S(1)}, u32[]{:S(2)}, u32[]{:S(2)}) %collective-permute-start.13) | collective-permute-done | bytes 131104 | tf_op jit(solution)/shard_map/ppermute | solution.py:34
  (33 shorter events, 4.2 us)
Async XLA Ops:
  3.9 23.9 %copy-start = (bf16[4,32,4096]{2,1,0:T(8,128)(2,1)S(1)}, bf16[4,32,4096]{2,1,0:T(8,128)(2,1)}, u32[]{:S(2)}) copy-start(bf16[4,32,4096]{2,1,0:T(8,128)(2,1)} %query_ref.1) | copy-start | bytes 3145732
  3.9 23.9 %copy-start.1 = (bf16[4,32,4096]{2,1,0:T(8,128)(2,1)S(1)}, bf16[4,32,4096]{2,1,0:T(8,128)(2,1)}, u32[]{:S(2)}) copy-start(bf16[4,32,4096]{2,1,0:T(8,128)(2,1)} %grad_ref.1) | copy-start | bytes 3145732
  3.9 23.9 %copy-start.2 = (s32[4,1024]{1,0:T(4,128)S(1)}, s32[4,1024]{1,0:T(4,128)}, u32[]{:S(2)}) copy-start(s32[4,1024]{1,0:T(4,128)} %segment_ref.9) | copy-start | bytes 49156
  3.9 23.9 %copy-start.3 = (s32[4]{0:T(128)S(1)}, s32[4]{0:T(128)}, u32[]{:S(2)}) copy-start(s32[4]{0:T(128)} %assign_ref.11) | copy-start | bytes 52
  3.9 6.4 %collective-permute-start = (bf16[2,32,512]{2,1,0:T(8,128)(2,1)}, bf16[2,32,512]{2,1,0:T(8,128)(2,1)S(1)}, u32[]{:S(2)}, u32[]{:S(2)}) collective-permute-start(bf16[2,32,512]{2,1,0:T(8,128)(2,1)} %get-tuple-element.46), channel_id=1, source_target_pairs={{0,1},{1,2},{2,3},{3,0},{4,5},{5,6},{6,7},{7,4},{8,9},{9,10},{10,1... | collective-permute-start | bytes 196616 | tf_op jit(solution)/shard_map/ppermute | solution.py:28
  6.1 7.5 %collective-permute-start.1 = (bf16[2,32,512]{2,1,0:T(8,128)(2,1)}, bf16[2,32,512]{2,1,0:T(8,128)(2,1)S(1)}, u32[]{:S(2)}, u32[]{:S(2)}) collective-permute-start(bf16[2,32,512]{2,1,0:T(8,128)(2,1)} %get-tuple-element.50), channel_id=1, source_target_pairs={{0,2},{1,3},{2,0},{3,1},{4,6},{5,7},{6,4},{7,5},{8,10},{9,11},{10,... | collective-permute-start | bytes 196616 | tf_op jit(solution)/shard_map/ppermute | solution.py:28
  8.4 5.2 %collective-permute-start.2 = (bf16[2,32,512]{2,1,0:T(8,128)(2,1)}, bf16[2,32,512]{2,1,0:T(8,128)(2,1)S(1)}, u32[]{:S(2)}, u32[]{:S(2)}) collective-permute-start(bf16[2,32,512]{2,1,0:T(8,128)(2,1)} %get-tuple-element.51), channel_id=1, source_target_pairs={{0,3},{1,0},{2,1},{3,2},{4,7},{5,4},{6,5},{7,6},{8,11},{9,8},{10,9... | collective-permute-start | bytes 196616 | tf_op jit(solution)/shard_map/ppermute | solution.py:28
  10.4 21.1 %collective-permute-start.6 = (bf16[2,32,4096]{2,1,0:T(8,128)(2,1)}, bf16[2,32,4096]{2,1,0:T(8,128)(2,1)S(1)}, u32[]{:S(2)}, u32[]{:S(2)}) collective-permute-start(bf16[2,32,4096]{2,1,0:T(8,128)(2,1)} %get-tuple-element.54), channel_id=1, source_target_pairs={{0,1},{1,2},{2,3},{3,0},{4,5},{5,6},{6,7},{7,4},{8,9},{9,10},{10,1... | collective-permute-start | bytes 1572872 | tf_op jit(solution)/shard_map/ppermute | solution.py:28
  13.7 10.8 %collective-permute-start.4 = (bf16[4,2,32,512]{3,2,1,0:T(8,128)(2,1)S(1)}, bf16[4,2,32,512]{3,2,1,0:T(8,128)(2,1)}, u32[]{:S(2)}, u32[]{:S(2)}) collective-permute-start(bf16[4,2,32,512]{3,2,1,0:T(8,128)(2,1)S(1)} %bitcast_dynamic-update-slice_fusion), channel_id=1, source_target_pairs={{0,4},{4,8},{8,12},{12,16},{16,20},{20,24},{24,28},{1,5},{5,9},{9,... | collective-permute-start | bytes 786440 | tf_op jit(solution)/shard_map/ppermute | solution.py:34
  16.1 9.9 %collective-permute-start.3 = (bf16[4,2,32,512]{3,2,1,0:T(8,128)(2,1)S(1)}, bf16[4,2,32,512]{3,2,1,0:T(8,128)(2,1)}, u32[]{:S(2)}, u32[]{:S(2)}) collective-permute-start(bf16[4,2,32,512]{3,2,1,0:T(8,128)(2,1)S(1)} %bitcast_dynamic-update-slice_fusion), channel_id=1, source_target_pairs={{0,8},{4,12},{8,16},{12,20},{16,24},{20,28},{1,9},{5,13},{9,17},{1... | collective-permute-start | bytes 786440 | tf_op jit(solution)/shard_map/ppermute | solution.py:34
  21.1 16.6 %collective-permute-start.5 = (bf16[2,32,4096]{2,1,0:T(8,128)(2,1)}, bf16[2,32,4096]{2,1,0:T(8,128)(2,1)S(1)}, u32[]{:S(2)}, u32[]{:S(2)}) collective-permute-start(bf16[2,32,4096]{2,1,0:T(8,128)(2,1)} %get-tuple-element.53), channel_id=1, source_target_pairs={{0,3},{1,0},{2,1},{3,2},{4,7},{5,4},{6,5},{7,6},{8,11},{9,8},{10,9... | collective-permute-start | bytes 1572872 | tf_op jit(solution)/shard_map/ppermute | solution.py:28
  27.1 27.5 %collective-permute-start.7 = (bf16[2,32,2048]{2,1,0:T(8,128)(2,1)}, bf16[2,32,2048]{2,1,0:T(8,128)(2,1)S(1)}, u32[]{:S(2)}, u32[]{:S(2)}) collective-permute-start(bf16[2,32,2048]{2,1,0:T(8,128)(2,1)} %get-tuple-element.60), channel_id=1, source_target_pairs={{0,2},{1,3},{2,0},{3,1},{4,6},{5,7},{6,4},{7,5},{8,10},{9,11},{10,... | collective-permute-start | bytes 786440 | tf_op jit(solution)/shard_map/ppermute | solution.py:28
  37.7 3.6 %copy-start.5 = (bf16[1,32,2048]{2,1,0:T(8,128)(2,1)S(1)}, bf16[1,32,2048]{2,1,0:T(8,128)(2,1)}, u32[]{:S(2)}) copy-start(bf16[1,32,2048]{2,1,0:T(8,128)(2,1)} %get-tuple-element.66) | copy-start | bytes 393220
  37.7 3.6 %copy-start.4 = (bf16[1,32,2048]{2,1,0:T(8,128)(2,1)S(1)}, bf16[1,32,2048]{2,1,0:T(8,128)(2,1)}, u32[]{:S(2)}) copy-start(bf16[1,32,2048]{2,1,0:T(8,128)(2,1)} %get-tuple-element.67) | copy-start | bytes 393220
  41.3 18.6 %collective-permute-start.8 = (bf16[1,32,2048]{2,1,0:T(8,128)(2,1)S(1)}, bf16[1,32,2048]{2,1,0:T(8,128)(2,1)S(1)}, u32[]{:S(2)}, u32[]{:S(2)}) collective-permute-start(bf16[1,32,2048]{2,1,0:T(8,128)(2,1)S(1)} %copy-done.5), channel_id=1, source_target_pairs={{0,2},{1,3},{2,0},{3,1},{4,6},{5,7},{6,4},{7,5},{8,10},{9,11},{10,... | collective-permute-start | bytes 393224 | tf_op jit(solution)/shard_map/ppermute | solution.py:28
  41.3 18.9 %collective-permute-start.9 = (bf16[1,32,2048]{2,1,0:T(8,128)(2,1)S(1)}, bf16[1,32,2048]{2,1,0:T(8,128)(2,1)S(1)}, u32[]{:S(2)}, u32[]{:S(2)}) collective-permute-start(bf16[1,32,2048]{2,1,0:T(8,128)(2,1)S(1)} %copy-done.4), channel_id=1, source_target_pairs={{0,2},{1,3},{2,0},{3,1},{4,6},{5,7},{6,4},{7,5},{8,10},{9,11},{10,... | collective-permute-start | bytes 393224 | tf_op jit(solution)/shard_map/ppermute | solution.py:28
  56.0 6.6 %collective-permute-start.10 = (bf16[2,128,256]{2,1,0:T(8,128)(2,1)S(1)}, bf16[2,128,256]{2,1,0:T(8,128)(2,1)S(1)}, u32[]{:S(2)}, u32[]{:S(2)}) collective-permute-start(bf16[2,128,256]{2,1,0:T(8,128)(2,1)S(1)} %get-tuple-element.72), channel_id=1, source_target_pairs={{4,0},{8,4},{12,8},{16,12},{20,16},{24,20},{28,24},{5,1},{9,5},{13... | collective-permute-start | bytes 393224 | tf_op jit(solution)/shard_map/ppermute | solution.py:34
  57.9 11.0 %collective-permute-start.11 = (bf16[2,128,256]{2,1,0:T(8,128)(2,1)S(1)}, bf16[2,128,256]{2,1,0:T(8,128)(2,1)S(1)}, u32[]{:S(2)}, u32[]{:S(2)}) collective-permute-start(bf16[2,128,256]{2,1,0:T(8,128)(2,1)S(1)} %get-tuple-element.73), channel_id=1, source_target_pairs={{8,0},{12,4},{16,8},{20,12},{24,16},{28,20},{9,1},{13,5},{17,9},{2... | collective-permute-start | bytes 393224 | tf_op jit(solution)/shard_map/ppermute | solution.py:34
  62.6 6.5 %collective-permute-start.12 = (bf16[2,128,256]{2,1,0:T(8,128)(2,1)S(1)}, bf16[2,128,256]{2,1,0:T(8,128)(2,1)S(1)}, u32[]{:S(2)}, u32[]{:S(2)}) collective-permute-start(bf16[2,128,256]{2,1,0:T(8,128)(2,1)S(1)} %get-tuple-element.77), channel_id=1, source_target_pairs={{4,0},{8,4},{12,8},{16,12},{20,16},{24,20},{28,24},{5,1},{9,5},{13... | collective-permute-start | bytes 393224 | tf_op jit(solution)/shard_map/ppermute | solution.py:34
  65.0 6.4 %collective-permute-start.13 = (bf16[2,128,256]{2,1,0:T(8,128)(2,1)S(1)}, bf16[2,128,256]{2,1,0:T(8,128)(2,1)S(1)}, u32[]{:S(2)}, u32[]{:S(2)}) collective-permute-start(bf16[2,128,256]{2,1,0:T(8,128)(2,1)S(1)} %get-tuple-element.78), channel_id=1, source_target_pairs={{8,0},{12,4},{16,8},{20,12},{24,16},{28,20},{9,1},{13,5},{17,9},{2... | collective-permute-start | bytes 393224 | tf_op jit(solution)/shard_map/ppermute | solution.py:34

commit v27 on v26

--- a/solution.py
+++ b/solution.py
@@ -375,7 +375,7 @@
             final, half * HEADS_STEP, HEADS_STEP, *fixed, query, grad, kv, acc, full, True
         )
         if half:
-            halos, returned[0] = lax.optimization_barrier((halos, returned[0]))
+            halos, returned[-1] = lax.optimization_barrier((halos, returned[-1]))
             held_scores, total = lax.optimization_barrier((held_scores, total))
         held_scores.append(scores)
         returned = [shifted(halo, ("blk", "uly"), -back) for back, halo in enumerate(halos, 1)]

time: 72.5 us -> 72.4 us (level)
  no operation moved by 1% of the time
where the time goes in v27:
time: 72.4 us; the launch traced here: 72.1 us
  starting transfers between devices  28.6 us (40%)
  waiting for transfers between devices  20.8 us (29%)
  Pallas kernels  18.9 us (26%)
  other arithmetic  2.01 us (3%)
  local copies, waits for them, and re-layouts  0.93 us (1%)
  between operations  0.81 us (1%)
    ppermute x8, waiting for transfers between devices, exchanged(): lax.ppermute(value, axis, [(i, (i + step) % count) for i in range(count)])  16.4 us
    ppermute x6, starting transfers between devices, shifted(): return lax.ppermute(value, axis, pairs)  16.3 us
    pallas_call x5, Pallas kernels, attend(): pl.pallas_call(functools.partial(attend_kernel, step, first, filled, last...  13.7 us
    ppermute x8, starting transfers between devices, exchanged(): lax.ppermute(value, axis, [(i, (i + step) % count) for i in range(count)])  12.3 us
    ppermute x6, waiting for transfers between devices, shifted(): return lax.ppermute(value, axis, pairs)  4.4 us
    pallas_call x1, Pallas kernels, stage(): pl.pallas_call(functools.partial(stage_kernel, count, jobs, len(jobs)), o...  3.23 us
    pallas_call x1, Pallas kernels, turn(): pl.pallas_call(functools.partial(turn_kernel, step, tok_dev, reach), out_...  1.96 us
  transfers between devices with their start and end apart: 14, of which 7 were waited for; matrix products, arithmetic and copies ran while one was open for 3% of the time, Pallas kernels for 22%

profile of v27, /device:TPU:1, one launch (start us, length us, event | category | flops | bytes accessed | tf_op | source)
XLA Modules:
  0.0 72.1 jit_solution(5435714374807007739)
XLA Ops:
  0.6 3.2 %stage.1 = (bf16[2,32,512]{2,1,0:T(8,128)(2,1)}, bf16[2,32,512]{2,1,0:T(8,128)(2,1)}, bf16[2,32,512]{2,1,0:T(8,128)(2,1)}, bf16[2,32,512]{2,1,0:T(8,128)(2,1)}, ...) custom-call(s32[4]{0:T(128)} %assign_ref.11, ...), custom_call_target="tpu_custom_call" | custom-call | tf_op jit(solution)/shard_map/stage/pallas_call | solution.py:63
  3.9 2.2 %collective-permute-start = (bf16[2,32,512]{2,1,0:T(8,128)(2,1)}, bf16[2,32,512]{2,1,0:T(8,128)(2,1)S(1)}, u32[]{:S(2)}, u32[]{:S(2)}) collective-permute-start(bf16[2,32,512]{2,1,0:T(8,128)(2,1)} %get-tuple-element.46), channel_id=1, source_target_pairs={{0,1},{1,2},{2,3},{3,0},{4,5},{5,6},{6,7},{7,4},{8,9},{9,10},{10,1... | collective-permute-start | bytes 196616 | tf_op jit(solution)/shard_map/ppermute | solution.py:28
  6.1 2.3 %collective-permute-start.1 = (bf16[2,32,512]{2,1,0:T(8,128)(2,1)}, bf16[2,32,512]{2,1,0:T(8,128)(2,1)S(1)}, u32[]{:S(2)}, u32[]{:S(2)}) collective-permute-start(bf16[2,32,512]{2,1,0:T(8,128)(2,1)} %get-tuple-element.50), channel_id=1, source_target_pairs={{0,2},{1,3},{2,0},{3,1},{4,6},{5,7},{6,4},{7,5},{8,10},{9,11},{10,... | collective-permute-start | bytes 196616 | tf_op jit(solution)/shard_map/ppermute | solution.py:28
  8.4 1.1 %collective-permute-start.2 = (bf16[2,32,512]{2,1,0:T(8,128)(2,1)}, bf16[2,32,512]{2,1,0:T(8,128)(2,1)S(1)}, u32[]{:S(2)}, u32[]{:S(2)}) collective-permute-start(bf16[2,32,512]{2,1,0:T(8,128)(2,1)} %get-tuple-element.51), channel_id=1, source_target_pairs={{0,3},{1,0},{2,1},{3,2},{4,7},{5,4},{6,5},{7,6},{8,11},{9,8},{10,9... | collective-permute-start | bytes 196616 | tf_op jit(solution)/shard_map/ppermute | solution.py:28
  10.8 2.8 %collective-permute-done.1 = bf16[2,32,512]{2,1,0:T(8,128)(2,1)S(1)} collective-permute-done((bf16[2,32,512]{2,1,0:T(8,128)(2,1)}, bf16[2,32,512]{2,1,0:T(8,128)(2,1)S(1)}, u32[]{:S(2)}, u32[]{:S(2)}) %collective-permute-start.1) | collective-permute-done | bytes 65568 | tf_op jit(solution)/shard_map/ppermute | solution.py:28
  13.7 2.4 %collective-permute-start.4 = (bf16[4,2,32,512]{3,2,1,0:T(8,128)(2,1)S(1)}, bf16[4,2,32,512]{3,2,1,0:T(8,128)(2,1)}, u32[]{:S(2)}, u32[]{:S(2)}) collective-permute-start(bf16[4,2,32,512]{3,2,1,0:T(8,128)(2,1)S(1)} %bitcast_dynamic-update-slice_fusion), channel_id=1, source_target_pairs={{0,4},{4,8},{8,12},{12,16},{16,20},{20,24},{24,28},{1,5},{5,9},{9,... | collective-permute-start | bytes 786440 | tf_op jit(solution)/shard_map/ppermute | solution.py:34
  16.1 5.0 %collective-permute-start.3 = (bf16[4,2,32,512]{3,2,1,0:T(8,128)(2,1)S(1)}, bf16[4,2,32,512]{3,2,1,0:T(8,128)(2,1)}, u32[]{:S(2)}, u32[]{:S(2)}) collective-permute-start(bf16[4,2,32,512]{3,2,1,0:T(8,128)(2,1)S(1)} %bitcast_dynamic-update-slice_fusion), channel_id=1, source_target_pairs={{0,8},{4,12},{8,16},{12,20},{16,24},{20,28},{1,9},{5,13},{9,17},{1... | collective-permute-start | bytes 786440 | tf_op jit(solution)/shard_map/ppermute | solution.py:34
  21.1 3.3 %collective-permute-start.5 = (bf16[2,32,4096]{2,1,0:T(8,128)(2,1)}, bf16[2,32,4096]{2,1,0:T(8,128)(2,1)S(1)}, u32[]{:S(2)}, u32[]{:S(2)}) collective-permute-start(bf16[2,32,4096]{2,1,0:T(8,128)(2,1)} %get-tuple-element.53), channel_id=1, source_target_pairs={{0,3},{1,0},{2,1},{3,2},{4,7},{5,4},{6,5},{7,6},{8,11},{9,8},{10,9... | collective-permute-start | bytes 1572872 | tf_op jit(solution)/shard_map/ppermute | solution.py:28
  24.4 1.5 %collective-permute-done.3 = bf16[4,2,32,512]{3,2,1,0:T(8,128)(2,1)} collective-permute-done((bf16[4,2,32,512]{3,2,1,0:T(8,128)(2,1)S(1)}, bf16[4,2,32,512]{3,2,1,0:T(8,128)(2,1)}, u32[]{:S(2)}, u32[]{:S(2)}) %collective-permute-start.3) | collective-permute-done | bytes 262176 | tf_op jit(solution)/shard_map/ppermute | solution.py:34
  25.9 1.1 %pad_maximum_fusion.kv_ref.key_ref = bf16[12,2,32,512]{3,2,1,0:T(8,128)(2,1)S(1)} fusion(bf16[4,2,32,512]{3,2,1,0:T(8,128)(2,1)S(1)} %bitcast_dynamic-update-slice_fusion, bf16[4,2,32,512]{3,2,1,0:T(8,128)(2,1)} %collective-permute-done.4, bf16[4,2,32,512]{3,2,1,0:T(8,128)(2,1)} %collective-permute-done.3), kind=kLoop, calls=%fused_computation | loop fusion | flops 786432 | bytes 1572864 | tf_op jit(solution)/shard_map/concatenate | solution.py:356
  27.8 3.6 %attend.5 = (bf16[128,32,128]{2,1,0:T(8,128)(2,1)}, f32[2,384,512]{2,1,0:T(8,128)S(1)}) custom-call(s32[2]{0:T(128)S(1)} %pad_add_fusion.meta_ref, s32[4]{0:T(128)S(1)} %copy-done.3, s32[4,1024]{1,0:T(4,128)S(1)} %copy-done.2, bf16[4,32,4096]{2,1,0:T(8,128)(2,1)S(1)} %copy-done, bf16[4,32,4096]{2,1,0:T(8,128)(2,1)S(1)} %copy-done.1, ...), custom_call_target="tpu_custom_call" | custom-call | flops 37748736 | bytes 294912 | tf_op jit(solution)/shard_map/attend/pallas_call | solution.py:250
  31.4 3.6 %attend.6 = (bf16[128,32,128]{2,1,0:T(8,128)(2,1)}, f32[2,384,512]{2,1,0:T(8,128)S(1)}) custom-call(s32[2]{0:T(128)S(1)} %pad_add_fusion.meta_ref, s32[4]{0:T(128)S(1)} %copy-done.3, s32[4,1024]{1,0:T(4,128)S(1)} %copy-done.2, bf16[2,32,4096]{2,1,0:T(8,128)(2,1)S(1)} %collective-permute-done.6.query_ref.grad_ref, ...), custom_call_target="tpu_custom_call", output_to_operand_aliasing={{1}: (6, {}), {0}: (7, {})} | custom-call | flops 1132462080 | bytes 8847360 | tf_op jit(solution)/shard_map/attend/pallas_call | solution.py:250
  35.0 2.7 %collective-permute-done.5.query_ref.grad_ref = bf16[2,32,4096]{2,1,0:T(8,128)(2,1)S(1)} collective-permute-done((bf16[2,32,4096]{2,1,0:T(8,128)(2,1)}, bf16[2,32,4096]{2,1,0:T(8,128)(2,1)S(1)}, u32[]{:S(2)}, u32[]{:S(2)}) %collective-permute-start.5) | collective-permute-done | bytes 524320 | tf_op jit(solution)/shard_map/ppermute | solution.py:28
  37.7 3.6 %attend.7 = (bf16[128,32,128]{2,1,0:T(8,128)(2,1)}, f32[2,384,512]{2,1,0:T(8,128)S(1)}) custom-call(s32[2]{0:T(128)S(1)} %pad_add_fusion.meta_ref, s32[4]{0:T(128)S(1)} %copy-done.3, s32[4,1024]{1,0:T(4,128)S(1)} %copy-done.2, bf16[2,32,4096]{2,1,0:T(8,128)(2,1)S(1)} %collective-permute-done.5.query_ref.grad_ref, ...), custom_call_target="tpu_custom_call", output_to_operand_aliasing={{1}: (6, {}), {0}: (7, {})} | custom-call | flops 1132462080 | bytes 8847360 | tf_op jit(solution)/shard_map/attend/pallas_call | solution.py:250
  41.3 2.4 %collective-permute-start.9 = (bf16[1,32,2048]{2,1,0:T(8,128)(2,1)S(1)}, bf16[1,32,2048]{2,1,0:T(8,128)(2,1)S(1)}, u32[]{:S(2)}, u32[]{:S(2)}) collective-permute-start(bf16[1,32,2048]{2,1,0:T(8,128)(2,1)S(1)} %copy-done.4), channel_id=1, source_target_pairs={{0,2},{1,3},{2,0},{3,1},{4,6},{5,7},{6,4},{7,5},{8,10},{9,11},{10,... | collective-permute-start | bytes 393224 | tf_op jit(solution)/shard_map/ppermute | solution.py:28
  43.6 10.9 %collective-permute-done.7.query_ref.grad_ref = bf16[2,32,2048]{2,1,0:T(8,128)(2,1)S(1)} collective-permute-done((bf16[2,32,2048]{2,1,0:T(8,128)(2,1)}, bf16[2,32,2048]{2,1,0:T(8,128)(2,1)S(1)}, u32[]{:S(2)}, u32[]{:S(2)}) %collective-permute-start.7) | collective-permute-done | bytes 262176 | tf_op jit(solution)/shard_map/ppermute | solution.py:28
  54.5 1.5 %attend.8 = (bf16[2,288,256]{2,1,0:T(8,128)(2,1)S(1)}, f32[2,128,256]{2,1,0:T(8,128)S(1)}, bf16[2,128,256]{2,1,0:T(8,128)(2,1)S(1)}, bf16[2,128,256]{2,1,0:T(8,128)(2,1)S(1)}) custom-call(s32[2]{0:T(128)S(1)} %pad_add_fusion.meta_ref, s32[4]{0:T(128)S(1)} %copy-done.3, s32[4,1024]{1,0:T(4,128)S(1)} %copy-done.2, ...), custom_call_target="tpu_custom_call" | custom-call | flops 18874368 | bytes 147456 | tf_op jit(solution)/shard_map/attend/pallas_call | solution.py:250
  56.0 2.3 %collective-permute-start.11 = (bf16[2,128,256]{2,1,0:T(8,128)(2,1)S(1)}, bf16[2,128,256]{2,1,0:T(8,128)(2,1)S(1)}, u32[]{:S(2)}, u32[]{:S(2)}) collective-permute-start(bf16[2,128,256]{2,1,0:T(8,128)(2,1)S(1)} %get-tuple-element.73), channel_id=1, source_target_pairs={{8,0},{12,4},{16,8},{20,12},{24,16},{28,20},{9,1},{13,5},{17,9},{2... | collective-permute-start | bytes 393224 | tf_op jit(solution)/shard_map/ppermute | solution.py:34
  58.3 1.9 %collective-permute-start.10 = (bf16[2,128,256]{2,1,0:T(8,128)(2,1)S(1)}, bf16[2,128,256]{2,1,0:T(8,128)(2,1)S(1)}, u32[]{:S(2)}, u32[]{:S(2)}) collective-permute-start(bf16[2,128,256]{2,1,0:T(8,128)(2,1)S(1)} %get-tuple-element.72), channel_id=1, source_target_pairs={{4,0},{8,4},{12,8},{16,12},{20,16},{24,20},{28,24},{5,1},{9,5},{13... | collective-permute-start | bytes 393224 | tf_op jit(solution)/shard_map/ppermute | solution.py:34
  60.2 1.5 %attend.9 = (bf16[2,288,256]{2,1,0:T(8,128)(2,1)S(1)}, f32[2,128,256]{2,1,0:T(8,128)S(1)}, bf16[2,128,256]{2,1,0:T(8,128)(2,1)S(1)}, bf16[2,128,256]{2,1,0:T(8,128)(2,1)S(1)}) custom-call(s32[2]{0:T(128)S(1)} %pad_add_fusion.meta_ref, s32[4]{0:T(128)S(1)} %copy-done.3, s32[4,1024]{1,0:T(4,128)S(1)} %copy-done.2, ...), custom_call_target="tpu_custom_call" | custom-call | flops 18874368 | bytes 147456 | tf_op jit(solution)/shard_map/attend/pallas_call | solution.py:250
  62.3 2.8 %collective-permute-start.12 = (bf16[2,128,256]{2,1,0:T(8,128)(2,1)S(1)}, bf16[2,128,256]{2,1,0:T(8,128)(2,1)S(1)}, u32[]{:S(2)}, u32[]{:S(2)}) collective-permute-start(bf16[2,128,256]{2,1,0:T(8,128)(2,1)S(1)} %get-tuple-element.77), channel_id=1, source_target_pairs={{4,0},{8,4},{12,8},{16,12},{20,16},{24,20},{28,24},{5,1},{9,5},{13... | collective-permute-start | bytes 393224 | tf_op jit(solution)/shard_map/ppermute | solution.py:34
  65.0 1.9 %collective-permute-start.13 = (bf16[2,128,256]{2,1,0:T(8,128)(2,1)S(1)}, bf16[2,128,256]{2,1,0:T(8,128)(2,1)S(1)}, u32[]{:S(2)}, u32[]{:S(2)}) collective-permute-start(bf16[2,128,256]{2,1,0:T(8,128)(2,1)S(1)} %get-tuple-element.78), channel_id=1, source_target_pairs={{8,0},{12,4},{16,8},{20,12},{24,16},{28,20},{9,1},{13,5},{17,9},{2... | collective-permute-start | bytes 393224 | tf_op jit(solution)/shard_map/ppermute | solution.py:34
  67.0 2.0 %turn.1 = bf16[128,32,128]{2,1,0:T(8,128)(2,1)} custom-call(s32[2]{0:T(128)S(1)} %pad_add_fusion.meta_ref, bf16[12,2,32,512]{3,2,1,0:T(8,128)(2,1)S(1)} %pad_maximum_fusion.kv_ref.key_ref, bf16[128,32,128]{2,1,0:T(8,128)(2,1)} %get-tuple-element.59.full_ref, bf16[2,288,256]{2,1,0:T(8,128)(2,1)S(1)} %get-tuple-element.69.refs_0_, ...), custom_call_target="tpu_custom_call", output_to_operand_aliasing={{}: (2, {})} | custom-call | tf_op jit(solution)/shard_map/turn/pallas_call | solution.py:301
  69.5 1.9 %collective-permute-done.13 = bf16[2,128,256]{2,1,0:T(8,128)(2,1)S(1)} collective-permute-done((bf16[2,128,256]{2,1,0:T(8,128)(2,1)S(1)}, bf16[2,128,256]{2,1,0:T(8,128)(2,1)S(1)}, u32[]{:S(2)}, u32[]{:S(2)}) %collective-permute-start.13) | collective-permute-done | bytes 131104 | tf_op jit(solution)/shard_map/ppermute | solution.py:34
  (33 shorter events, 4.0 us)
Async XLA Ops:
  3.9 23.9 %copy-start = (bf16[4,32,4096]{2,1,0:T(8,128)(2,1)S(1)}, bf16[4,32,4096]{2,1,0:T(8,128)(2,1)}, u32[]{:S(2)}) copy-start(bf16[4,32,4096]{2,1,0:T(8,128)(2,1)} %query_ref.1) | copy-start | bytes 3145732
  3.9 23.9 %copy-start.1 = (bf16[4,32,4096]{2,1,0:T(8,128)(2,1)S(1)}, bf16[4,32,4096]{2,1,0:T(8,128)(2,1)}, u32[]{:S(2)}) copy-start(bf16[4,32,4096]{2,1,0:T(8,128)(2,1)} %grad_ref.1) | copy-start | bytes 3145732
  3.9 23.9 %copy-start.2 = (s32[4,1024]{1,0:T(4,128)S(1)}, s32[4,1024]{1,0:T(4,128)}, u32[]{:S(2)}) copy-start(s32[4,1024]{1,0:T(4,128)} %segment_ref.9) | copy-start | bytes 49156
  3.9 23.9 %copy-start.3 = (s32[4]{0:T(128)S(1)}, s32[4]{0:T(128)}, u32[]{:S(2)}) copy-start(s32[4]{0:T(128)} %assign_ref.11) | copy-start | bytes 52
  3.9 6.4 %collective-permute-start = (bf16[2,32,512]{2,1,0:T(8,128)(2,1)}, bf16[2,32,512]{2,1,0:T(8,128)(2,1)S(1)}, u32[]{:S(2)}, u32[]{:S(2)}) collective-permute-start(bf16[2,32,512]{2,1,0:T(8,128)(2,1)} %get-tuple-element.46), channel_id=1, source_target_pairs={{0,1},{1,2},{2,3},{3,0},{4,5},{5,6},{6,7},{7,4},{8,9},{9,10},{10,1... | collective-permute-start | bytes 196616 | tf_op jit(solution)/shard_map/ppermute | solution.py:28
  6.1 7.5 %collective-permute-start.1 = (bf16[2,32,512]{2,1,0:T(8,128)(2,1)}, bf16[2,32,512]{2,1,0:T(8,128)(2,1)S(1)}, u32[]{:S(2)}, u32[]{:S(2)}) collective-permute-start(bf16[2,32,512]{2,1,0:T(8,128)(2,1)} %get-tuple-element.50), channel_id=1, source_target_pairs={{0,2},{1,3},{2,0},{3,1},{4,6},{5,7},{6,4},{7,5},{8,10},{9,11},{10,... | collective-permute-start | bytes 196616 | tf_op jit(solution)/shard_map/ppermute | solution.py:28
  8.4 5.2 %collective-permute-start.2 = (bf16[2,32,512]{2,1,0:T(8,128)(2,1)}, bf16[2,32,512]{2,1,0:T(8,128)(2,1)S(1)}, u32[]{:S(2)}, u32[]{:S(2)}) collective-permute-start(bf16[2,32,512]{2,1,0:T(8,128)(2,1)} %get-tuple-element.51), channel_id=1, source_target_pairs={{0,3},{1,0},{2,1},{3,2},{4,7},{5,4},{6,5},{7,6},{8,11},{9,8},{10,9... | collective-permute-start | bytes 196616 | tf_op jit(solution)/shard_map/ppermute | solution.py:28
  10.4 21.1 %collective-permute-start.6 = (bf16[2,32,4096]{2,1,0:T(8,128)(2,1)}, bf16[2,32,4096]{2,1,0:T(8,128)(2,1)S(1)}, u32[]{:S(2)}, u32[]{:S(2)}) collective-permute-start(bf16[2,32,4096]{2,1,0:T(8,128)(2,1)} %get-tuple-element.54), channel_id=1, source_target_pairs={{0,1},{1,2},{2,3},{3,0},{4,5},{5,6},{6,7},{7,4},{8,9},{9,10},{10,1... | collective-permute-start | bytes 1572872 | tf_op jit(solution)/shard_map/ppermute | solution.py:28
  13.7 10.8 %collective-permute-start.4 = (bf16[4,2,32,512]{3,2,1,0:T(8,128)(2,1)S(1)}, bf16[4,2,32,512]{3,2,1,0:T(8,128)(2,1)}, u32[]{:S(2)}, u32[]{:S(2)}) collective-permute-start(bf16[4,2,32,512]{3,2,1,0:T(8,128)(2,1)S(1)} %bitcast_dynamic-update-slice_fusion), channel_id=1, source_target_pairs={{0,4},{4,8},{8,12},{12,16},{16,20},{20,24},{24,28},{1,5},{5,9},{9,... | collective-permute-start | bytes 786440 | tf_op jit(solution)/shard_map/ppermute | solution.py:34
  16.1 9.9 %collective-permute-start.3 = (bf16[4,2,32,512]{3,2,1,0:T(8,128)(2,1)S(1)}, bf16[4,2,32,512]{3,2,1,0:T(8,128)(2,1)}, u32[]{:S(2)}, u32[]{:S(2)}) collective-permute-start(bf16[4,2,32,512]{3,2,1,0:T(8,128)(2,1)S(1)} %bitcast_dynamic-update-slice_fusion), channel_id=1, source_target_pairs={{0,8},{4,12},{8,16},{12,20},{16,24},{20,28},{1,9},{5,13},{9,17},{1... | collective-permute-start | bytes 786440 | tf_op jit(solution)/shard_map/ppermute | solution.py:34
  21.1 16.6 %collective-permute-start.5 = (bf16[2,32,4096]{2,1,0:T(8,128)(2,1)}, bf16[2,32,4096]{2,1,0:T(8,128)(2,1)S(1)}, u32[]{:S(2)}, u32[]{:S(2)}) collective-permute-start(bf16[2,32,4096]{2,1,0:T(8,128)(2,1)} %get-tuple-element.53), channel_id=1, source_target_pairs={{0,3},{1,0},{2,1},{3,2},{4,7},{5,4},{6,5},{7,6},{8,11},{9,8},{10,9... | collective-permute-start | bytes 1572872 | tf_op jit(solution)/shard_map/ppermute | solution.py:28
  27.1 27.5 %collective-permute-start.7 = (bf16[2,32,2048]{2,1,0:T(8,128)(2,1)}, bf16[2,32,2048]{2,1,0:T(8,128)(2,1)S(1)}, u32[]{:S(2)}, u32[]{:S(2)}) collective-permute-start(bf16[2,32,2048]{2,1,0:T(8,128)(2,1)} %get-tuple-element.60), channel_id=1, source_target_pairs={{0,2},{1,3},{2,0},{3,1},{4,6},{5,7},{6,4},{7,5},{8,10},{9,11},{10,... | collective-permute-start | bytes 786440 | tf_op jit(solution)/shard_map/ppermute | solution.py:28
  37.7 3.6 %copy-start.5 = (bf16[1,32,2048]{2,1,0:T(8,128)(2,1)S(1)}, bf16[1,32,2048]{2,1,0:T(8,128)(2,1)}, u32[]{:S(2)}) copy-start(bf16[1,32,2048]{2,1,0:T(8,128)(2,1)} %get-tuple-element.66) | copy-start | bytes 393220
  37.7 3.6 %copy-start.4 = (bf16[1,32,2048]{2,1,0:T(8,128)(2,1)S(1)}, bf16[1,32,2048]{2,1,0:T(8,128)(2,1)}, u32[]{:S(2)}) copy-start(bf16[1,32,2048]{2,1,0:T(8,128)(2,1)} %get-tuple-element.67) | copy-start | bytes 393220
  41.3 19.0 %collective-permute-start.8 = (bf16[1,32,2048]{2,1,0:T(8,128)(2,1)S(1)}, bf16[1,32,2048]{2,1,0:T(8,128)(2,1)S(1)}, u32[]{:S(2)}, u32[]{:S(2)}) collective-permute-start(bf16[1,32,2048]{2,1,0:T(8,128)(2,1)S(1)} %copy-done.5), channel_id=1, source_target_pairs={{0,2},{1,3},{2,0},{3,1},{4,6},{5,7},{6,4},{7,5},{8,10},{9,11},{10,... | collective-permute-start | bytes 393224 | tf_op jit(solution)/shard_map/ppermute | solution.py:28
  41.3 19.0 %collective-permute-start.9 = (bf16[1,32,2048]{2,1,0:T(8,128)(2,1)S(1)}, bf16[1,32,2048]{2,1,0:T(8,128)(2,1)S(1)}, u32[]{:S(2)}, u32[]{:S(2)}) collective-permute-start(bf16[1,32,2048]{2,1,0:T(8,128)(2,1)S(1)} %copy-done.4), channel_id=1, source_target_pairs={{0,2},{1,3},{2,0},{3,1},{4,6},{5,7},{6,4},{7,5},{8,10},{9,11},{10,... | collective-permute-start | bytes 393224 | tf_op jit(solution)/shard_map/ppermute | solution.py:28
  56.0 6.3 %collective-permute-start.11 = (bf16[2,128,256]{2,1,0:T(8,128)(2,1)S(1)}, bf16[2,128,256]{2,1,0:T(8,128)(2,1)S(1)}, u32[]{:S(2)}, u32[]{:S(2)}) collective-permute-start(bf16[2,128,256]{2,1,0:T(8,128)(2,1)S(1)} %get-tuple-element.73), channel_id=1, source_target_pairs={{8,0},{12,4},{16,8},{20,12},{24,16},{28,20},{9,1},{13,5},{17,9},{2... | collective-permute-start | bytes 393224 | tf_op jit(solution)/shard_map/ppermute | solution.py:34
  58.3 10.6 %collective-permute-start.10 = (bf16[2,128,256]{2,1,0:T(8,128)(2,1)S(1)}, bf16[2,128,256]{2,1,0:T(8,128)(2,1)S(1)}, u32[]{:S(2)}, u32[]{:S(2)}) collective-permute-start(bf16[2,128,256]{2,1,0:T(8,128)(2,1)S(1)} %get-tuple-element.72), channel_id=1, source_target_pairs={{4,0},{8,4},{12,8},{16,12},{20,16},{24,20},{28,24},{5,1},{9,5},{13... | collective-permute-start | bytes 393224 | tf_op jit(solution)/shard_map/ppermute | solution.py:34
  62.3 7.2 %collective-permute-start.12 = (bf16[2,128,256]{2,1,0:T(8,128)(2,1)S(1)}, bf16[2,128,256]{2,1,0:T(8,128)(2,1)S(1)}, u32[]{:S(2)}, u32[]{:S(2)}) collective-permute-start(bf16[2,128,256]{2,1,0:T(8,128)(2,1)S(1)} %get-tuple-element.77), channel_id=1, source_target_pairs={{4,0},{8,4},{12,8},{16,12},{20,16},{24,20},{28,24},{5,1},{9,5},{13... | collective-permute-start | bytes 393224 | tf_op jit(solution)/shard_map/ppermute | solution.py:34
  65.0 6.3 %collective-permute-start.13 = (bf16[2,128,256]{2,1,0:T(8,128)(2,1)S(1)}, bf16[2,128,256]{2,1,0:T(8,128)(2,1)S(1)}, u32[]{:S(2)}, u32[]{:S(2)}) collective-permute-start(bf16[2,128,256]{2,1,0:T(8,128)(2,1)S(1)} %get-tuple-element.78), channel_id=1, source_target_pairs={{8,0},{12,4},{16,8},{20,12},{24,16},{28,20},{9,1},{13,5},{17,9},{2... | collective-permute-start | bytes 393224 | tf_op jit(solution)/shard_map/ppermute | solution.py:34

commit v28 on v27

--- a/solution.py
+++ b/solution.py
@@ -375,7 +375,7 @@
             final, half * HEADS_STEP, HEADS_STEP, *fixed, query, grad, kv, acc, full, True
         )
         if half:
-            halos, returned[-1] = lax.optimization_barrier((halos, returned[-1]))
+            held_scores, halos = lax.optimization_barrier((held_scores, halos))
             held_scores, total = lax.optimization_barrier((held_scores, total))
         held_scores.append(scores)
         returned = [shifted(halo, ("blk", "uly"), -back) for back, halo in enumerate(halos, 1)]

time: 72.4 us -> 72.5 us (level)
  no operation moved by 1% of the time
where the time goes in v28:
time: 72.5 us; the launch traced here: 72.2 us
  starting transfers between devices  28.9 us (40%)
  waiting for transfers between devices  20.6 us (28%)
  Pallas kernels  18.9 us (26%)
  other arithmetic  2.01 us (3%)
  local copies, waits for them, and re-layouts  0.93 us (1%)
  between operations  0.8 us (1%)
    ppermute x8, waiting for transfers between devices, exchanged(): lax.ppermute(value, axis, [(i, (i + step) % count) for i in range(count)])  16.7 us
    ppermute x6, starting transfers between devices, shifted(): return lax.ppermute(value, axis, pairs)  16.6 us
    pallas_call x5, Pallas kernels, attend(): pl.pallas_call(functools.partial(attend_kernel, step, first, filled, last...  13.7 us
    ppermute x8, starting transfers between devices, exchanged(): lax.ppermute(value, axis, [(i, (i + step) % count) for i in range(count)])  12.3 us
    ppermute x6, waiting for transfers between devices, shifted(): return lax.ppermute(value, axis, pairs)  3.92 us
    pallas_call x1, Pallas kernels, stage(): pl.pallas_call(functools.partial(stage_kernel, count, jobs, len(jobs)), o...  3.23 us
    pallas_call x1, Pallas kernels, turn(): pl.pallas_call(functools.partial(turn_kernel, step, tok_dev, reach), out_...  1.96 us
  transfers between devices with their start and end apart: 14, of which 7 were waited for; matrix products, arithmetic and copies ran while one was open for 3% of the time, Pallas kernels for 22%

profile of v28, /device:TPU:1, one launch (start us, length us, event | category | flops | bytes accessed | tf_op | source)
XLA Modules:
  0.0 72.2 jit_solution(5206551934543881472)
XLA Ops:
  0.6 3.2 %stage.1 = (bf16[2,32,512]{2,1,0:T(8,128)(2,1)}, bf16[2,32,512]{2,1,0:T(8,128)(2,1)}, bf16[2,32,512]{2,1,0:T(8,128)(2,1)}, bf16[2,32,512]{2,1,0:T(8,128)(2,1)}, ...) custom-call(s32[4]{0:T(128)} %assign_ref.11, ...), custom_call_target="tpu_custom_call" | custom-call | tf_op jit(solution)/shard_map/stage/pallas_call | solution.py:63
  3.9 2.2 %collective-permute-start = (bf16[2,32,512]{2,1,0:T(8,128)(2,1)}, bf16[2,32,512]{2,1,0:T(8,128)(2,1)S(1)}, u32[]{:S(2)}, u32[]{:S(2)}) collective-permute-start(bf16[2,32,512]{2,1,0:T(8,128)(2,1)} %get-tuple-element.47), channel_id=1, source_target_pairs={{0,1},{1,2},{2,3},{3,0},{4,5},{5,6},{6,7},{7,4},{8,9},{9,10},{10,1... | collective-permute-start | bytes 196616 | tf_op jit(solution)/shard_map/ppermute | solution.py:28
  6.1 2.3 %collective-permute-start.1 = (bf16[2,32,512]{2,1,0:T(8,128)(2,1)}, bf16[2,32,512]{2,1,0:T(8,128)(2,1)S(1)}, u32[]{:S(2)}, u32[]{:S(2)}) collective-permute-start(bf16[2,32,512]{2,1,0:T(8,128)(2,1)} %get-tuple-element.51), channel_id=1, source_target_pairs={{0,2},{1,3},{2,0},{3,1},{4,6},{5,7},{6,4},{7,5},{8,10},{9,11},{10,... | collective-permute-start | bytes 196616 | tf_op jit(solution)/shard_map/ppermute | solution.py:28
  8.4 1.1 %collective-permute-start.2 = (bf16[2,32,512]{2,1,0:T(8,128)(2,1)}, bf16[2,32,512]{2,1,0:T(8,128)(2,1)S(1)}, u32[]{:S(2)}, u32[]{:S(2)}) collective-permute-start(bf16[2,32,512]{2,1,0:T(8,128)(2,1)} %get-tuple-element.52), channel_id=1, source_target_pairs={{0,3},{1,0},{2,1},{3,2},{4,7},{5,4},{6,5},{7,6},{8,11},{9,8},{10,9... | collective-permute-start | bytes 196616 | tf_op jit(solution)/shard_map/ppermute | solution.py:28
  10.8 2.8 %collective-permute-done.1 = bf16[2,32,512]{2,1,0:T(8,128)(2,1)S(1)} collective-permute-done((bf16[2,32,512]{2,1,0:T(8,128)(2,1)}, bf16[2,32,512]{2,1,0:T(8,128)(2,1)S(1)}, u32[]{:S(2)}, u32[]{:S(2)}) %collective-permute-start.1) | collective-permute-done | bytes 65568 | tf_op jit(solution)/shard_map/ppermute | solution.py:28
  13.7 2.4 %collective-permute-start.4 = (bf16[4,2,32,512]{3,2,1,0:T(8,128)(2,1)S(1)}, bf16[4,2,32,512]{3,2,1,0:T(8,128)(2,1)}, u32[]{:S(2)}, u32[]{:S(2)}) collective-permute-start(bf16[4,2,32,512]{3,2,1,0:T(8,128)(2,1)S(1)} %bitcast_dynamic-update-slice_fusion), channel_id=1, source_target_pairs={{0,4},{4,8},{8,12},{12,16},{16,20},{20,24},{24,28},{1,5},{5,9},{9,... | collective-permute-start | bytes 786440 | tf_op jit(solution)/shard_map/ppermute | solution.py:34
  16.1 5.0 %collective-permute-start.3 = (bf16[4,2,32,512]{3,2,1,0:T(8,128)(2,1)S(1)}, bf16[4,2,32,512]{3,2,1,0:T(8,128)(2,1)}, u32[]{:S(2)}, u32[]{:S(2)}) collective-permute-start(bf16[4,2,32,512]{3,2,1,0:T(8,128)(2,1)S(1)} %bitcast_dynamic-update-slice_fusion), channel_id=1, source_target_pairs={{0,8},{4,12},{8,16},{12,20},{16,24},{20,28},{1,9},{5,13},{9,17},{1... | collective-permute-start | bytes 786440 | tf_op jit(solution)/shard_map/ppermute | solution.py:34
  21.1 3.3 %collective-permute-start.5 = (bf16[2,32,4096]{2,1,0:T(8,128)(2,1)}, bf16[2,32,4096]{2,1,0:T(8,128)(2,1)S(1)}, u32[]{:S(2)}, u32[]{:S(2)}) collective-permute-start(bf16[2,32,4096]{2,1,0:T(8,128)(2,1)} %get-tuple-element.54), channel_id=1, source_target_pairs={{0,3},{1,0},{2,1},{3,2},{4,7},{5,4},{6,5},{7,6},{8,11},{9,8},{10,9... | collective-permute-start | bytes 1572872 | tf_op jit(solution)/shard_map/ppermute | solution.py:28
  24.4 1.5 %collective-permute-done.3 = bf16[4,2,32,512]{3,2,1,0:T(8,128)(2,1)} collective-permute-done((bf16[4,2,32,512]{3,2,1,0:T(8,128)(2,1)S(1)}, bf16[4,2,32,512]{3,2,1,0:T(8,128)(2,1)}, u32[]{:S(2)}, u32[]{:S(2)}) %collective-permute-start.3) | collective-permute-done | bytes 262176 | tf_op jit(solution)/shard_map/ppermute | solution.py:34
  25.9 1.1 %pad_maximum_fusion.kv_ref.key_ref = bf16[12,2,32,512]{3,2,1,0:T(8,128)(2,1)S(1)} fusion(bf16[4,2,32,512]{3,2,1,0:T(8,128)(2,1)S(1)} %bitcast_dynamic-update-slice_fusion, bf16[4,2,32,512]{3,2,1,0:T(8,128)(2,1)} %collective-permute-done.4, bf16[4,2,32,512]{3,2,1,0:T(8,128)(2,1)} %collective-permute-done.3), kind=kLoop, calls=%fused_computation | loop fusion | flops 786432 | bytes 1572864 | tf_op jit(solution)/shard_map/concatenate | solution.py:356
  27.8 3.6 %attend.5 = (bf16[128,32,128]{2,1,0:T(8,128)(2,1)}, f32[2,384,512]{2,1,0:T(8,128)S(1)}) custom-call(s32[2]{0:T(128)S(1)} %pad_add_fusion.meta_ref, s32[4]{0:T(128)S(1)} %copy-done.3, s32[4,1024]{1,0:T(4,128)S(1)} %copy-done.2, bf16[4,32,4096]{2,1,0:T(8,128)(2,1)S(1)} %copy-done, bf16[4,32,4096]{2,1,0:T(8,128)(2,1)S(1)} %copy-done.1, ...), custom_call_target="tpu_custom_call" | custom-call | flops 37748736 | bytes 294912 | tf_op jit(solution)/shard_map/attend/pallas_call | solution.py:250
  31.4 3.6 %attend.6 = (bf16[128,32,128]{2,1,0:T(8,128)(2,1)}, f32[2,384,512]{2,1,0:T(8,128)S(1)}) custom-call(s32[2]{0:T(128)S(1)} %pad_add_fusion.meta_ref, s32[4]{0:T(128)S(1)} %copy-done.3, s32[4,1024]{1,0:T(4,128)S(1)} %copy-done.2, bf16[2,32,4096]{2,1,0:T(8,128)(2,1)S(1)} %collective-permute-done.6.query_ref.grad_ref, ...), custom_call_target="tpu_custom_call", output_to_operand_aliasing={{1}: (6, {}), {0}: (7, {})} | custom-call | flops 1132462080 | bytes 8847360 | tf_op jit(solution)/shard_map/attend/pallas_call | solution.py:250
  35.0 2.7 %collective-permute-done.5.query_ref.grad_ref = bf16[2,32,4096]{2,1,0:T(8,128)(2,1)S(1)} collective-permute-done((bf16[2,32,4096]{2,1,0:T(8,128)(2,1)}, bf16[2,32,4096]{2,1,0:T(8,128)(2,1)S(1)}, u32[]{:S(2)}, u32[]{:S(2)}) %collective-permute-start.5) | collective-permute-done | bytes 524320 | tf_op jit(solution)/shard_map/ppermute | solution.py:28
  37.7 3.6 %attend.7 = (bf16[128,32,128]{2,1,0:T(8,128)(2,1)}, f32[2,384,512]{2,1,0:T(8,128)S(1)}) custom-call(s32[2]{0:T(128)S(1)} %pad_add_fusion.meta_ref, s32[4]{0:T(128)S(1)} %copy-done.3, s32[4,1024]{1,0:T(4,128)S(1)} %copy-done.2, bf16[2,32,4096]{2,1,0:T(8,128)(2,1)S(1)} %collective-permute-done.5.query_ref.grad_ref, ...), custom_call_target="tpu_custom_call", output_to_operand_aliasing={{1}: (6, {}), {0}: (7, {})} | custom-call | flops 1132462080 | bytes 8847360 | tf_op jit(solution)/shard_map/attend/pallas_call | solution.py:250
  41.3 2.4 %collective-permute-start.9 = (bf16[1,32,2048]{2,1,0:T(8,128)(2,1)S(1)}, bf16[1,32,2048]{2,1,0:T(8,128)(2,1)S(1)}, u32[]{:S(2)}, u32[]{:S(2)}) collective-permute-start(bf16[1,32,2048]{2,1,0:T(8,128)(2,1)S(1)} %copy-done.4), channel_id=1, source_target_pairs={{0,2},{1,3},{2,0},{3,1},{4,6},{5,7},{6,4},{7,5},{8,10},{9,11},{10,... | collective-permute-start | bytes 393224 | tf_op jit(solution)/shard_map/ppermute | solution.py:28
  43.6 10.9 %collective-permute-done.7.query_ref.grad_ref = bf16[2,32,2048]{2,1,0:T(8,128)(2,1)S(1)} collective-permute-done((bf16[2,32,2048]{2,1,0:T(8,128)(2,1)}, bf16[2,32,2048]{2,1,0:T(8,128)(2,1)S(1)}, u32[]{:S(2)}, u32[]{:S(2)}) %collective-permute-start.7) | collective-permute-done | bytes 262176 | tf_op jit(solution)/shard_map/ppermute | solution.py:28
  54.5 1.5 %attend.8 = (bf16[2,288,256]{2,1,0:T(8,128)(2,1)S(1)}, f32[2,128,256]{2,1,0:T(8,128)S(1)}, bf16[2,128,256]{2,1,0:T(8,128)(2,1)S(1)}, bf16[2,128,256]{2,1,0:T(8,128)(2,1)S(1)}) custom-call(s32[2]{0:T(128)S(1)} %pad_add_fusion.meta_ref, s32[4]{0:T(128)S(1)} %copy-done.3, s32[4,1024]{1,0:T(4,128)S(1)} %copy-done.2, ...), custom_call_target="tpu_custom_call" | custom-call | flops 18874368 | bytes 147456 | tf_op jit(solution)/shard_map/attend/pallas_call | solution.py:250
  56.0 1.9 %collective-permute-start.10 = (bf16[2,128,256]{2,1,0:T(8,128)(2,1)S(1)}, bf16[2,128,256]{2,1,0:T(8,128)(2,1)S(1)}, u32[]{:S(2)}, u32[]{:S(2)}) collective-permute-start(bf16[2,128,256]{2,1,0:T(8,128)(2,1)S(1)} %get-tuple-element.76), channel_id=1, source_target_pairs={{4,0},{8,4},{12,8},{16,12},{20,16},{24,20},{28,24},{5,1},{9,5},{13... | collective-permute-start | bytes 393224 | tf_op jit(solution)/shard_map/ppermute | solution.py:34
  57.9 1.9 %collective-permute-start.11 = (bf16[2,128,256]{2,1,0:T(8,128)(2,1)S(1)}, bf16[2,128,256]{2,1,0:T(8,128)(2,1)S(1)}, u32[]{:S(2)}, u32[]{:S(2)}) collective-permute-start(bf16[2,128,256]{2,1,0:T(8,128)(2,1)S(1)} %get-tuple-element.77), channel_id=1, source_target_pairs={{8,0},{12,4},{16,8},{20,12},{24,16},{28,20},{9,1},{13,5},{17,9},{2... | collective-permute-start | bytes 393224 | tf_op jit(solution)/shard_map/ppermute | solution.py:34
  60.1 1.5 %attend.9 = (bf16[2,288,256]{2,1,0:T(8,128)(2,1)S(1)}, f32[2,128,256]{2,1,0:T(8,128)S(1)}, bf16[2,128,256]{2,1,0:T(8,128)(2,1)S(1)}, bf16[2,128,256]{2,1,0:T(8,128)(2,1)S(1)}) custom-call(s32[2]{0:T(128)S(1)} %pad_add_fusion.meta_ref, s32[4]{0:T(128)S(1)} %copy-done.3, s32[4,1024]{1,0:T(4,128)S(1)} %copy-done.2, ...), custom_call_target="tpu_custom_call" | custom-call | flops 18874368 | bytes 147456 | tf_op jit(solution)/shard_map/attend/pallas_call | solution.py:250
  61.6 3.4 %collective-permute-start.12 = (bf16[2,128,256]{2,1,0:T(8,128)(2,1)S(1)}, bf16[2,128,256]{2,1,0:T(8,128)(2,1)S(1)}, u32[]{:S(2)}, u32[]{:S(2)}) collective-permute-start(bf16[2,128,256]{2,1,0:T(8,128)(2,1)S(1)} %get-tuple-element.79), channel_id=1, source_target_pairs={{4,0},{8,4},{12,8},{16,12},{20,16},{24,20},{28,24},{5,1},{9,5},{13... | collective-permute-start | bytes 393224 | tf_op jit(solution)/shard_map/ppermute | solution.py:34
  65.0 1.9 %collective-permute-start.13 = (bf16[2,128,256]{2,1,0:T(8,128)(2,1)S(1)}, bf16[2,128,256]{2,1,0:T(8,128)(2,1)S(1)}, u32[]{:S(2)}, u32[]{:S(2)}) collective-permute-start(bf16[2,128,256]{2,1,0:T(8,128)(2,1)S(1)} %get-tuple-element.80), channel_id=1, source_target_pairs={{8,0},{12,4},{16,8},{20,12},{24,16},{28,20},{9,1},{13,5},{17,9},{2... | collective-permute-start | bytes 393224 | tf_op jit(solution)/shard_map/ppermute | solution.py:34
  66.9 2.0 %turn.1 = bf16[128,32,128]{2,1,0:T(8,128)(2,1)} custom-call(s32[2]{0:T(128)S(1)} %pad_add_fusion.meta_ref, bf16[12,2,32,512]{3,2,1,0:T(8,128)(2,1)S(1)} %pad_maximum_fusion.kv_ref.key_ref, bf16[128,32,128]{2,1,0:T(8,128)(2,1)} %get-tuple-element.60.full_ref, bf16[2,288,256]{2,1,0:T(8,128)(2,1)S(1)} %get-tuple-element.73.refs_0_, ...), custom_call_target="tpu_custom_call", output_to_operand_aliasing={{}: (2, {})} | custom-call | tf_op jit(solution)/shard_map/turn/pallas_call | solution.py:301
  69.0 2.4 %collective-permute-done.13 = bf16[2,128,256]{2,1,0:T(8,128)(2,1)S(1)} collective-permute-done((bf16[2,128,256]{2,1,0:T(8,128)(2,1)S(1)}, bf16[2,128,256]{2,1,0:T(8,128)(2,1)S(1)}, u32[]{:S(2)}, u32[]{:S(2)}) %collective-permute-start.13) | collective-permute-done | bytes 131104 | tf_op jit(solution)/shard_map/ppermute | solution.py:34
  (33 shorter events, 3.3 us)
Async XLA Ops:
  3.9 23.9 %copy-start = (bf16[4,32,4096]{2,1,0:T(8,128)(2,1)S(1)}, bf16[4,32,4096]{2,1,0:T(8,128)(2,1)}, u32[]{:S(2)}) copy-start(bf16[4,32,4096]{2,1,0:T(8,128)(2,1)} %query_ref.1) | copy-start | bytes 3145732
  3.9 23.9 %copy-start.1 = (bf16[4,32,4096]{2,1,0:T(8,128)(2,1)S(1)}, bf16[4,32,4096]{2,1,0:T(8,128)(2,1)}, u32[]{:S(2)}) copy-start(bf16[4,32,4096]{2,1,0:T(8,128)(2,1)} %grad_ref.1) | copy-start | bytes 3145732
  3.9 23.9 %copy-start.2 = (s32[4,1024]{1,0:T(4,128)S(1)}, s32[4,1024]{1,0:T(4,128)}, u32[]{:S(2)}) copy-start(s32[4,1024]{1,0:T(4,128)} %segment_ref.9) | copy-start | bytes 49156
  3.9 23.9 %copy-start.3 = (s32[4]{0:T(128)S(1)}, s32[4]{0:T(128)}, u32[]{:S(2)}) copy-start(s32[4]{0:T(128)} %assign_ref.11) | copy-start | bytes 52
  3.9 6.4 %collective-permute-start = (bf16[2,32,512]{2,1,0:T(8,128)(2,1)}, bf16[2,32,512]{2,1,0:T(8,128)(2,1)S(1)}, u32[]{:S(2)}, u32[]{:S(2)}) collective-permute-start(bf16[2,32,512]{2,1,0:T(8,128)(2,1)} %get-tuple-element.47), channel_id=1, source_target_pairs={{0,1},{1,2},{2,3},{3,0},{4,5},{5,6},{6,7},{7,4},{8,9},{9,10},{10,1... | collective-permute-start | bytes 196616 | tf_op jit(solution)/shard_map/ppermute | solution.py:28
  6.1 7.5 %collective-permute-start.1 = (bf16[2,32,512]{2,1,0:T(8,128)(2,1)}, bf16[2,32,512]{2,1,0:T(8,128)(2,1)S(1)}, u32[]{:S(2)}, u32[]{:S(2)}) collective-permute-start(bf16[2,32,512]{2,1,0:T(8,128)(2,1)} %get-tuple-element.51), channel_id=1, source_target_pairs={{0,2},{1,3},{2,0},{3,1},{4,6},{5,7},{6,4},{7,5},{8,10},{9,11},{10,... | collective-permute-start | bytes 196616 | tf_op jit(solution)/shard_map/ppermute | solution.py:28
  8.4 5.2 %collective-permute-start.2 = (bf16[2,32,512]{2,1,0:T(8,128)(2,1)}, bf16[2,32,512]{2,1,0:T(8,128)(2,1)S(1)}, u32[]{:S(2)}, u32[]{:S(2)}) collective-permute-start(bf16[2,32,512]{2,1,0:T(8,128)(2,1)} %get-tuple-element.52), channel_id=1, source_target_pairs={{0,3},{1,0},{2,1},{3,2},{4,7},{5,4},{6,5},{7,6},{8,11},{9,8},{10,9... | collective-permute-start | bytes 196616 | tf_op jit(solution)/shard_map/ppermute | solution.py:28
  10.4 21.1 %collective-permute-start.6 = (bf16[2,32,4096]{2,1,0:T(8,128)(2,1)}, bf16[2,32,4096]{2,1,0:T(8,128)(2,1)S(1)}, u32[]{:S(2)}, u32[]{:S(2)}) collective-permute-start(bf16[2,32,4096]{2,1,0:T(8,128)(2,1)} %get-tuple-element.55), channel_id=1, source_target_pairs={{0,1},{1,2},{2,3},{3,0},{4,5},{5,6},{6,7},{7,4},{8,9},{9,10},{10,1... | collective-permute-start | bytes 1572872 | tf_op jit(solution)/shard_map/ppermute | solution.py:28
  13.7 10.8 %collective-permute-start.4 = (bf16[4,2,32,512]{3,2,1,0:T(8,128)(2,1)S(1)}, bf16[4,2,32,512]{3,2,1,0:T(8,128)(2,1)}, u32[]{:S(2)}, u32[]{:S(2)}) collective-permute-start(bf16[4,2,32,512]{3,2,1,0:T(8,128)(2,1)S(1)} %bitcast_dynamic-update-slice_fusion), channel_id=1, source_target_pairs={{0,4},{4,8},{8,12},{12,16},{16,20},{20,24},{24,28},{1,5},{5,9},{9,... | collective-permute-start | bytes 786440 | tf_op jit(solution)/shard_map/ppermute | solution.py:34
  16.1 9.9 %collective-permute-start.3 = (bf16[4,2,32,512]{3,2,1,0:T(8,128)(2,1)S(1)}, bf16[4,2,32,512]{3,2,1,0:T(8,128)(2,1)}, u32[]{:S(2)}, u32[]{:S(2)}) collective-permute-start(bf16[4,2,32,512]{3,2,1,0:T(8,128)(2,1)S(1)} %bitcast_dynamic-update-slice_fusion), channel_id=1, source_target_pairs={{0,8},{4,12},{8,16},{12,20},{16,24},{20,28},{1,9},{5,13},{9,17},{1... | collective-permute-start | bytes 786440 | tf_op jit(solution)/shard_map/ppermute | solution.py:34
  21.1 16.6 %collective-permute-start.5 = (bf16[2,32,4096]{2,1,0:T(8,128)(2,1)}, bf16[2,32,4096]{2,1,0:T(8,128)(2,1)S(1)}, u32[]{:S(2)}, u32[]{:S(2)}) collective-permute-start(bf16[2,32,4096]{2,1,0:T(8,128)(2,1)} %get-tuple-element.54), channel_id=1, source_target_pairs={{0,3},{1,0},{2,1},{3,2},{4,7},{5,4},{6,5},{7,6},{8,11},{9,8},{10,9... | collective-permute-start | bytes 1572872 | tf_op jit(solution)/shard_map/ppermute | solution.py:28
  27.1 27.5 %collective-permute-start.7 = (bf16[2,32,2048]{2,1,0:T(8,128)(2,1)}, bf16[2,32,2048]{2,1,0:T(8,128)(2,1)S(1)}, u32[]{:S(2)}, u32[]{:S(2)}) collective-permute-start(bf16[2,32,2048]{2,1,0:T(8,128)(2,1)} %get-tuple-element.61), channel_id=1, source_target_pairs={{0,2},{1,3},{2,0},{3,1},{4,6},{5,7},{6,4},{7,5},{8,10},{9,11},{10,... | collective-permute-start | bytes 786440 | tf_op jit(solution)/shard_map/ppermute | solution.py:28
  37.7 3.6 %copy-start.5 = (bf16[1,32,2048]{2,1,0:T(8,128)(2,1)S(1)}, bf16[1,32,2048]{2,1,0:T(8,128)(2,1)}, u32[]{:S(2)}) copy-start(bf16[1,32,2048]{2,1,0:T(8,128)(2,1)} %get-tuple-element.67) | copy-start | bytes 393220
  37.7 3.6 %copy-start.4 = (bf16[1,32,2048]{2,1,0:T(8,128)(2,1)S(1)}, bf16[1,32,2048]{2,1,0:T(8,128)(2,1)}, u32[]{:S(2)}) copy-start(bf16[1,32,2048]{2,1,0:T(8,128)(2,1)} %get-tuple-element.68) | copy-start | bytes 393220
  41.3 18.6 %collective-permute-start.8 = (bf16[1,32,2048]{2,1,0:T(8,128)(2,1)S(1)}, bf16[1,32,2048]{2,1,0:T(8,128)(2,1)S(1)}, u32[]{:S(2)}, u32[]{:S(2)}) collective-permute-start(bf16[1,32,2048]{2,1,0:T(8,128)(2,1)S(1)} %copy-done.5), channel_id=1, source_target_pairs={{0,2},{1,3},{2,0},{3,1},{4,6},{5,7},{6,4},{7,5},{8,10},{9,11},{10,... | collective-permute-start | bytes 393224 | tf_op jit(solution)/shard_map/ppermute | solution.py:28
  41.3 18.9 %collective-permute-start.9 = (bf16[1,32,2048]{2,1,0:T(8,128)(2,1)S(1)}, bf16[1,32,2048]{2,1,0:T(8,128)(2,1)S(1)}, u32[]{:S(2)}, u32[]{:S(2)}) collective-permute-start(bf16[1,32,2048]{2,1,0:T(8,128)(2,1)S(1)} %copy-done.4), channel_id=1, source_target_pairs={{0,2},{1,3},{2,0},{3,1},{4,6},{5,7},{6,4},{7,5},{8,10},{9,11},{10,... | collective-permute-start | bytes 393224 | tf_op jit(solution)/shard_map/ppermute | solution.py:28
  56.0 12.9 %collective-permute-start.10 = (bf16[2,128,256]{2,1,0:T(8,128)(2,1)S(1)}, bf16[2,128,256]{2,1,0:T(8,128)(2,1)S(1)}, u32[]{:S(2)}, u32[]{:S(2)}) collective-permute-start(bf16[2,128,256]{2,1,0:T(8,128)(2,1)S(1)} %get-tuple-element.76), channel_id=1, source_target_pairs={{4,0},{8,4},{12,8},{16,12},{20,16},{24,20},{28,24},{5,1},{9,5},{13... | collective-permute-start | bytes 393224 | tf_op jit(solution)/shard_map/ppermute | solution.py:34
  57.9 11.0 %collective-permute-start.11 = (bf16[2,128,256]{2,1,0:T(8,128)(2,1)S(1)}, bf16[2,128,256]{2,1,0:T(8,128)(2,1)S(1)}, u32[]{:S(2)}, u32[]{:S(2)}) collective-permute-start(bf16[2,128,256]{2,1,0:T(8,128)(2,1)S(1)} %get-tuple-element.77), channel_id=1, source_target_pairs={{8,0},{12,4},{16,8},{20,12},{24,16},{28,20},{9,1},{13,5},{17,9},{2... | collective-permute-start | bytes 393224 | tf_op jit(solution)/shard_map/ppermute | solution.py:34
  61.6 7.4 %collective-permute-start.12 = (bf16[2,128,256]{2,1,0:T(8,128)(2,1)S(1)}, bf16[2,128,256]{2,1,0:T(8,128)(2,1)S(1)}, u32[]{:S(2)}, u32[]{:S(2)}) collective-permute-start(bf16[2,128,256]{2,1,0:T(8,128)(2,1)S(1)} %get-tuple-element.79), channel_id=1, source_target_pairs={{4,0},{8,4},{12,8},{16,12},{20,16},{24,20},{28,24},{5,1},{9,5},{13... | collective-permute-start | bytes 393224 | tf_op jit(solution)/shard_map/ppermute | solution.py:34
  65.0 6.4 %collective-permute-start.13 = (bf16[2,128,256]{2,1,0:T(8,128)(2,1)S(1)}, bf16[2,128,256]{2,1,0:T(8,128)(2,1)S(1)}, u32[]{:S(2)}, u32[]{:S(2)}) collective-permute-start(bf16[2,128,256]{2,1,0:T(8,128)(2,1)S(1)} %get-tuple-element.80), channel_id=1, source_target_pairs={{8,0},{12,4},{16,8},{20,12},{24,16},{28,20},{9,1},{13,5},{17,9},{2... | collective-permute-start | bytes 393224 | tf_op jit(solution)/shard_map/ppermute | solution.py:34
